TPU v7x, 32 devices: a whole 2x2x4 slice. The times are simulated.
32 devices in a mesh: seq: 4 (over z), fsdp: 8 (over y, x, core).
Axes of the slice: x: 2, y: 2, z: 4, core: 2. Of those that a mesh axis runs over, the one named last changes fastest.
Arguments:
- tokens: bfloat16 [4096, 1536], P(('seq', 'fsdp')), may hold values from -6 to 6
- teacher: bfloat16 [4096, 1536], P(('seq', 'fsdp')), may hold values from -6 to 6
- valid: int32 [4096], P(('seq', 'fsdp')), may hold values from 0 to 1
- routes: int32 [4096, 2], P(('seq', 'fsdp')), may hold values from 0 to 3, as said below
- slots: int32 [4096, 2], P(('seq', 'fsdp')), may hold values from 0 to 127, as said below
- gain_attn: bfloat16 [1536], P('fsdp'), may hold values from 0.5 to 1.5
- w_query: bfloat16 [1536, 1536], P('fsdp'), may hold values from -0.15625 to 0.15625
- w_keyval: bfloat16 [1536, 1024], P('fsdp'), may hold values from -0.15625 to 0.15625
- w_out: bfloat16 [1536, 1536], P(None, 'fsdp'), may hold values from -6 to 6
- gain_ffn: bfloat16 [1536], P('fsdp'), may hold values from 0.5 to 1.5
- w_router: bfloat16 [1536, 4], P('fsdp'), may hold values from -0.3125 to 0.3125
- w_gate_up: bfloat16 [4, 1536, 2048], P(None, 'fsdp'), may hold values from -0.15625 to 0.15625
- w_down: bfloat16 [4, 1024, 1536], P(None, None, 'fsdp'), may hold values from -0.1875 to 0.1875
Outputs:
- mixed: bfloat16 [4096, 1536], P(('seq', 'fsdp'))
- loss: float32 [], replicated
- grad_tokens: float32 [4096, 1536], P(('seq', 'fsdp'))
- grad_gain_attn: float32 [1536], P('fsdp')
- grad_query: float32 [1536, 1536], P('fsdp')
- grad_keyval: float32 [1536, 1024], P('fsdp')
- grad_out: float32 [1536, 1536], P(None, 'fsdp')
- grad_gain_ffn: float32 [1536], P('fsdp')
- grad_router: float32 [1536, 4], P('fsdp')
- grad_gate_up: float32 [4, 1536, 2048], P(None, 'fsdp')
- grad_down: float32 [4, 1024, 1536], P(None, None, 'fsdp')
Inputs may be any that keep to these rules, and one draw needn't show every extreme that they name: `routes`: each row names 2 different experts. In each aligned block of 128 rows (the rows of one device) some expert is named by every row. In each aligned block of 128 rows, the rows that name an expert carry the slots 0, 1, ... up to their number - 1 for it, each once.
All inputs are finite; a program needn't handle non-finite values.
Results may differ from a plain program's by a relative error of at most 0.018.
Values may be sent and summed in bfloat16 or wider, within the bound.
No kernel may reach another device: no remote copies, remote signals or barrier semaphores. Data moves between devices by JAX's collectives and lax.ppermute only.
A program may use at most 256 MiB of HBM per device.

v0:
```python
import math

import jax
import jax.numpy as jnp
from jax import lax
from jax.sharding import PartitionSpec as P

HEADS = 24
KVH = 8
HD = 64
CAP = 96


EPSILON = 1e-06
FLOOR_SCORE = -1e30
PRECISE = lax.Precision.HIGHEST


def rms_norm(values, gain_row):
    factor = lax.rsqrt(jnp.mean(values * values, axis=-1, keepdims=True) + EPSILON)
    return (values * factor * gain_row, factor)


def norm_back(values, factor, gain_row, grad_norm):
    scaled = grad_norm * gain_row
    inner_mean = jnp.mean(scaled * values, axis=-1, keepdims=True)
    grad_values = factor * scaled - values * factor * factor * factor * inner_mean
    grad_gain = jnp.sum(grad_norm * values * factor, axis=0)
    return (grad_values, grad_gain)


def token_place(row_index, rows_tok, shard_count, local_rows):
    owner_shard = row_index // local_rows
    within = row_index % local_rows
    return (within // rows_tok * shard_count + owner_shard) * rows_tok + within % rows_tok


def score_block(queries, key_rows, query_place, key_place, key_valid, score_scale):
    scores = (
        jnp.einsum("rkgd,jkd->rkgj", queries, key_rows, preferred_element_type=jnp.float32)
        * score_scale
    )
    causal = key_place[None, :] <= query_place[:, None]
    usable = (key_valid[None, :] > 0) | (key_place[None, :] == query_place[:, None])
    visible = (causal & usable)[:, None, None, :]
    return (jnp.where(visible, scores, FLOOR_SCORE), visible)


def local(
    tokens,
    teacher,
    valid,
    routes,
    slots,
    gain_attn,
    w_query,
    w_keyval,
    w_out,
    gain_ffn,
    w_router,
    w_gate_up,
    w_down,
):
    seq_count = lax.axis_size("seq")
    shard_count = lax.axis_size("fsdp")
    rows_tok = tokens.shape[0]
    model_width = tokens.shape[1]
    head_count = HEADS
    kv_heads = KVH
    head_size = HD
    groups = head_count // kv_heads
    local_kv = kv_heads // seq_count
    local_rows = rows_tok * seq_count
    seq_len = local_rows * shard_count
    experts = w_gate_up.shape[0]
    hidden_units = w_down.shape[1]
    capacity = CAP
    score_scale = head_size ** (-0.5)
    shard_index = lax.axis_index("fsdp")
    gathered = (
        lax.all_gather(gain_attn, "fsdp", axis=0, tiled=True),
        lax.all_gather(w_query, "fsdp", axis=0, tiled=True),
        lax.all_gather(w_keyval, "fsdp", axis=0, tiled=True),
        lax.all_gather(w_out, "fsdp", axis=1, tiled=True),
        lax.all_gather(gain_ffn, "fsdp", axis=0, tiled=True),
        lax.all_gather(w_router, "fsdp", axis=0, tiled=True),
        lax.all_gather(w_gate_up, "fsdp", axis=1, tiled=True),
        lax.all_gather(w_down, "fsdp", axis=2, tiled=True),
    )
    gain_one, query_full, keyval_full, out_full, gain_two, router_full, gate_up_full, down_full = (
        gathered
    )
    inputs = tokens.astype(jnp.float32)
    normed, factor_one = rms_norm(inputs, gain_one.astype(jnp.float32))
    normed_low = normed.astype(jnp.bfloat16)
    queries = jnp.dot(normed_low, query_full, preferred_element_type=jnp.float32).astype(
        jnp.bfloat16
    )
    queries = queries.reshape(rows_tok, kv_heads, groups * head_size)
    keyvals = jnp.dot(normed_low, keyval_full, preferred_element_type=jnp.float32).astype(
        jnp.bfloat16
    )
    keyvals = keyvals.reshape(rows_tok, kv_heads, 2 * head_size)
    valid_wide = jnp.broadcast_to(valid.astype(jnp.bfloat16)[:, None], (rows_tok, kv_heads))
    head_q, head_kv, head_valid = (
        lax.all_to_all(queries, "seq", split_axis=1, concat_axis=0, tiled=True),
        lax.all_to_all(keyvals, "seq", split_axis=1, concat_axis=0, tiled=True),
        lax.all_to_all(valid_wide, "seq", split_axis=1, concat_axis=0, tiled=True),
    )
    head_queries = head_q.reshape(local_rows, local_kv, groups, head_size)
    query_place = token_place(
        shard_index * local_rows + jnp.arange(local_rows, dtype=jnp.int32),
        rows_tok,
        shard_count,
        local_rows,
    )
    start_state = (
        jnp.full((local_rows, local_kv, groups), FLOOR_SCORE, jnp.float32),
        jnp.zeros((local_rows, local_kv, groups), jnp.float32),
        jnp.zeros((local_rows, local_kv, groups, head_size), jnp.float32),
    )
    running = start_state
    kv_piece = lax.all_gather(head_kv, "fsdp", axis=0, tiled=True)
    valid_piece = lax.all_gather(head_valid, "fsdp", axis=0, tiled=True)
    piece_rows = kv_piece.shape[0]
    fold_block_rows = math.gcd(piece_rows, 1024)
    number = piece_rows // fold_block_rows
    kv_blocks = kv_piece.reshape(number, fold_block_rows, local_kv, 2 * head_size)
    valid_blocks = valid_piece[:, 0].reshape(number, fold_block_rows)
    starts = jnp.arange(number, dtype=jnp.int32) * fold_block_rows

    def advance(running_state, inputs_block):
        kv_block, valid_block, first_row = inputs_block
        row_max, denominator, summed = running_state
        key_place = token_place(
            first_row + jnp.arange(fold_block_rows, dtype=jnp.int32),
            rows_tok,
            shard_count,
            local_rows,
        )
        masked, visible = score_block(
            head_queries,
            kv_block[..., :head_size],
            query_place,
            key_place,
            valid_block,
            score_scale,
        )
        new_max = jnp.maximum(row_max, jnp.max(masked, axis=-1))
        exp_terms = jnp.where(visible, jnp.exp(masked - new_max[..., None]), 0.0)
        factor = jnp.exp(row_max - new_max)
        denominator = denominator * factor + jnp.sum(exp_terms, axis=-1)
        summed = summed * factor[..., None] + jnp.einsum(
            "rkgj,jkd->rkgd",
            exp_terms.astype(jnp.bfloat16),
            kv_block[..., head_size:],
            preferred_element_type=jnp.float32,
        )
        return ((new_max, denominator, summed), None)

    running, unused = lax.scan(advance, running, (kv_blocks, valid_blocks, starts))
    row_max, denominator, summed = running
    attended_exact = summed / denominator[..., None]
    attended_low = attended_exact.astype(jnp.bfloat16).reshape(
        local_rows, local_kv, groups * head_size
    )
    token_attended = lax.all_to_all(attended_low, "seq", split_axis=0, concat_axis=1, tiled=True)
    attn_rows = token_attended.reshape(rows_tok, head_count * head_size)
    residual = inputs + jnp.dot(attn_rows, out_full, preferred_element_type=jnp.float32)
    normed_two, factor_two = rms_norm(residual, gain_two.astype(jnp.float32))
    normed_two_low = normed_two.astype(jnp.bfloat16)
    logits = jnp.dot(normed_two_low, router_full, preferred_element_type=jnp.float32)
    expert_ids = jnp.arange(experts, dtype=jnp.int32)
    picked = (routes[:, :, None] == expert_ids).astype(jnp.float32)
    chosen = jnp.sum(picked * logits[:, None, :], axis=-1)
    gating = jax.nn.softmax(chosen, axis=-1)
    slot_hot = (slots[:, :, None] == jnp.arange(capacity, dtype=jnp.int32)).astype(jnp.float32)
    placed = (picked[:, :, :, None] * slot_hot[:, :, None, :]).reshape(
        rows_tok, routes.shape[1], experts * capacity
    )
    placed_low = placed.astype(jnp.bfloat16)
    dispatch = jnp.sum(placed, axis=1).astype(jnp.bfloat16)
    expert_rows = jnp.einsum(
        "ts,td->sd", dispatch, normed_two_low, preferred_element_type=jnp.float32
    ).astype(jnp.bfloat16)
    expert_rows = expert_rows.reshape(experts, capacity, model_width)
    gate_up = jnp.einsum(
        "ecd,edf->ecf", expert_rows, gate_up_full, preferred_element_type=jnp.float32
    )
    gate_part = gate_up[..., :hidden_units]
    up_part = gate_up[..., hidden_units:]
    hidden = (jax.nn.silu(gate_part) * up_part).astype(jnp.bfloat16)
    expert_out = jnp.einsum(
        "ecf,efd->ecd", hidden, down_full, preferred_element_type=jnp.float32
    ).astype(jnp.bfloat16)
    expert_out = expert_out.reshape(experts * capacity, model_width)
    selected = jnp.einsum("tks,sd->tkd", placed_low, expert_out, preferred_element_type=jnp.float32)
    mixed_exact = residual + jnp.sum(gating[:, :, None] * selected, axis=1)
    valid_rows = valid.astype(jnp.float32)
    errors = (mixed_exact - teacher.astype(jnp.float32)) * valid_rows[:, None]
    valid_count, squares = lax.psum(
        (jnp.sum(valid_rows), jnp.sum(errors * errors)), ("seq", "fsdp")
    )
    loss_value = squares / (model_width * valid_count)
    loss_scale = model_width * seq_len // 8
    grad_mixed = errors * (2.0 * loss_scale / (model_width * valid_count))
    gathered_back = (
        lax.all_gather(gain_attn, "fsdp", axis=0, tiled=True),
        lax.all_gather(w_query, "fsdp", axis=0, tiled=True),
        lax.all_gather(w_keyval, "fsdp", axis=0, tiled=True),
        lax.all_gather(w_out, "fsdp", axis=1, tiled=True),
        lax.all_gather(gain_ffn, "fsdp", axis=0, tiled=True),
        lax.all_gather(w_router, "fsdp", axis=0, tiled=True),
        lax.all_gather(w_gate_up, "fsdp", axis=1, tiled=True),
        lax.all_gather(w_down, "fsdp", axis=2, tiled=True),
    )
    (
        gain_one_b,
        query_back,
        keyval_back,
        out_back,
        gain_two_b,
        router_back,
        gate_up_back,
        down_back,
    ) = gathered_back
    grad_gating = jnp.sum(selected * grad_mixed[:, None, :], axis=-1)
    grad_chosen = gating * (grad_gating - jnp.sum(gating * grad_gating, axis=-1, keepdims=True))
    grad_logits = jnp.sum(grad_chosen[:, :, None] * picked, axis=1)
    weighted = gating[:, :, None] * grad_mixed[:, None, :]
    grad_expert_out = jnp.einsum("tks,tkd->sd", placed, weighted, precision=PRECISE).astype(
        jnp.bfloat16
    )
    grad_expert_out = grad_expert_out.reshape(experts, capacity, model_width)
    grad_down_local = jnp.einsum(
        "ecf,ecd->efd", hidden, grad_expert_out, preferred_element_type=jnp.float32
    )
    grad_hidden = jnp.einsum(
        "ecd,efd->ecf", grad_expert_out, down_back, preferred_element_type=jnp.float32
    )
    sigmoid_gate = jax.nn.sigmoid(gate_part)
    grad_gate = grad_hidden * up_part * sigmoid_gate * (1.0 + gate_part * (1.0 - sigmoid_gate))
    grad_up = grad_hidden * gate_part * sigmoid_gate
    grad_gate_up_rows = jnp.concatenate([grad_gate, grad_up], axis=-1).astype(jnp.bfloat16)
    grad_gate_up_local = jnp.einsum(
        "ecd,ecf->edf", expert_rows, grad_gate_up_rows, preferred_element_type=jnp.float32
    )
    grad_rows = jnp.einsum(
        "ecf,edf->ecd", grad_gate_up_rows, gate_up_back, preferred_element_type=jnp.float32
    ).astype(jnp.bfloat16)
    grad_rows = grad_rows.reshape(experts * capacity, model_width)
    grad_normed_two = jnp.einsum(
        "ts,sd->td", dispatch, grad_rows, preferred_element_type=jnp.float32
    )
    grad_normed_two = grad_normed_two + jnp.dot(
        grad_logits, router_back.astype(jnp.float32).T, precision=PRECISE
    )
    grad_router_local = jnp.dot(
        normed_two_low.astype(jnp.float32).T, grad_logits, precision=PRECISE
    )
    grad_resid_norm, grad_gain_two = norm_back(
        residual, factor_two, gain_two_b.astype(jnp.float32), grad_normed_two
    )
    grad_residual = grad_mixed + grad_resid_norm
    grad_branch = grad_residual.astype(jnp.bfloat16)
    grad_out_local = jnp.einsum(
        "tc,td->cd", attn_rows, grad_branch, preferred_element_type=jnp.float32
    )
    grad_attended = jnp.einsum(
        "td,cd->tc", grad_branch, out_back, preferred_element_type=jnp.float32
    ).astype(jnp.bfloat16)
    grad_attended = grad_attended.reshape(rows_tok, kv_heads, groups * head_size)
    head_grad = lax.all_to_all(grad_attended, "seq", split_axis=1, concat_axis=0, tiled=True)
    head_grad = head_grad.reshape(local_rows, local_kv, groups, head_size).astype(jnp.float32)
    grad_summed = (head_grad / denominator[..., None]).astype(jnp.bfloat16)
    shift_term = -jnp.sum(head_grad * attended_exact, axis=-1) / denominator
    all_kv, all_valid = (
        lax.all_gather(head_kv, "fsdp", axis=0, tiled=True),
        lax.all_gather(head_valid, "fsdp", axis=0, tiled=True),
    )
    block_rows = math.gcd(seq_len, 1024)
    number = seq_len // block_rows
    kv_blocks = all_kv.reshape(number, block_rows, local_kv, 2 * head_size)
    valid_blocks = all_valid[:, 0].reshape(number, block_rows)
    starts = jnp.arange(number, dtype=jnp.int32) * block_rows

    def backward_block(grad_q, inputs_block):
        kv_block, valid_block, first_row = inputs_block
        key_rows = kv_block[..., :head_size]
        value_rows = kv_block[..., head_size:]
        key_place = token_place(
            first_row + jnp.arange(block_rows, dtype=jnp.int32), rows_tok, shard_count, local_rows
        )
        masked, visible = score_block(
            head_queries, key_rows, query_place, key_place, valid_block, score_scale
        )
        exp_terms = jnp.where(visible, jnp.exp(masked - row_max[..., None]), 0.0)
        weights = exp_terms.astype(jnp.bfloat16)
        products = jnp.einsum(
            "rkgd,jkd->rkgj", grad_summed, value_rows, preferred_element_type=jnp.float32
        )
        grad_scores = (exp_terms * (products + shift_term[..., None])).astype(jnp.bfloat16)
        grad_q = (
            grad_q
            + jnp.einsum(
                "rkgj,jkd->rkgd", grad_scores, key_rows, preferred_element_type=jnp.float32
            )
            * score_scale
        )
        grad_keys = (
            jnp.einsum(
                "rkgj,rkgd->jkd", grad_scores, head_queries, preferred_element_type=jnp.float32
            )
            * score_scale
        )
        grad_values = jnp.einsum(
            "rkgj,rkgd->jkd", weights, grad_summed, preferred_element_type=jnp.float32
        )
        return (grad_q, jnp.concatenate([grad_keys, grad_values], axis=-1))

    grad_q_total, grad_kv_blocks = lax.scan(
        backward_block,
        jnp.zeros((local_rows, local_kv, groups, head_size), jnp.float32),
        (kv_blocks, valid_blocks, starts),
    )
    grad_kv_all = grad_kv_blocks.reshape(seq_len, local_kv, 2 * head_size)
    grad_kv_own = lax.psum_scatter(
        grad_kv_all.astype(jnp.bfloat16), "fsdp", scatter_dimension=0, tiled=True
    )
    grad_q_low = grad_q_total.astype(jnp.bfloat16).reshape(local_rows, local_kv, groups * head_size)
    token_grad_q, token_grad_kv = (
        lax.all_to_all(grad_q_low, "seq", split_axis=0, concat_axis=1, tiled=True),
        lax.all_to_all(grad_kv_own, "seq", split_axis=0, concat_axis=1, tiled=True),
    )
    grad_queries = token_grad_q.reshape(rows_tok, head_count * head_size)
    grad_keyvals = token_grad_kv.reshape(rows_tok, 2 * kv_heads * head_size)
    grad_query_local = jnp.einsum(
        "td,tc->dc", normed_low, grad_queries, preferred_element_type=jnp.float32
    )
    grad_keyval_local = jnp.einsum(
        "td,tc->dc", normed_low, grad_keyvals, preferred_element_type=jnp.float32
    )
    grad_normed = jnp.einsum(
        "tc,dc->td", grad_queries, query_back, preferred_element_type=jnp.float32
    )
    grad_normed = grad_normed + jnp.einsum(
        "tc,dc->td", grad_keyvals, keyval_back, preferred_element_type=jnp.float32
    )
    grad_input_norm, grad_gain_one = norm_back(
        inputs, factor_one, gain_one_b.astype(jnp.float32), grad_normed
    )
    grad_tokens = grad_residual + grad_input_norm
    shard_grads = (
        lax.psum_scatter(
            grad_gain_one.astype(jnp.bfloat16), "fsdp", scatter_dimension=0, tiled=True
        ).astype(jnp.float32),
        lax.psum_scatter(
            grad_query_local.astype(jnp.bfloat16), "fsdp", scatter_dimension=0, tiled=True
        ).astype(jnp.float32),
        lax.psum_scatter(
            grad_keyval_local.astype(jnp.bfloat16), "fsdp", scatter_dimension=0, tiled=True
        ).astype(jnp.float32),
        lax.psum_scatter(
            grad_out_local.astype(jnp.bfloat16), "fsdp", scatter_dimension=1, tiled=True
        ).astype(jnp.float32),
        lax.psum_scatter(
            grad_gain_two.astype(jnp.bfloat16), "fsdp", scatter_dimension=0, tiled=True
        ).astype(jnp.float32),
        lax.psum_scatter(
            grad_router_local.astype(jnp.bfloat16), "fsdp", scatter_dimension=0, tiled=True
        ).astype(jnp.float32),
        lax.psum_scatter(
            grad_gate_up_local.astype(jnp.bfloat16), "fsdp", scatter_dimension=1, tiled=True
        ).astype(jnp.float32),
        lax.psum_scatter(
            grad_down_local.astype(jnp.bfloat16), "fsdp", scatter_dimension=2, tiled=True
        ).astype(jnp.float32),
    )
    part_one, part_two, part_three, part_four, part_five, part_six, part_seven, part_eight = (
        shard_grads
    )
    results = (
        lax.psum(part_one.astype(jnp.bfloat16), "seq").astype(jnp.float32),
        lax.psum(part_two.astype(jnp.bfloat16), "seq").astype(jnp.float32),
        lax.psum(part_three.astype(jnp.bfloat16), "seq").astype(jnp.float32),
        lax.psum(part_four.astype(jnp.bfloat16), "seq").astype(jnp.float32),
        lax.psum(part_five.astype(jnp.bfloat16), "seq").astype(jnp.float32),
        lax.psum(part_six.astype(jnp.bfloat16), "seq").astype(jnp.float32),
        lax.psum(part_seven.astype(jnp.bfloat16), "seq").astype(jnp.float32),
        lax.psum(part_eight.astype(jnp.bfloat16), "seq").astype(jnp.float32),
    )
    return (
        mixed_exact.astype(jnp.bfloat16),
        loss_value,
        grad_tokens,
        results[0],
        results[1],
        results[2],
        results[3],
        results[4],
        results[5],
        results[6],
        results[7],
    )


def solution(mesh):
    return jax.shard_map(
        local,
        mesh=mesh,
        in_specs=(
            P(("seq", "fsdp"), None),
            P(("seq", "fsdp"), None),
            P(("seq", "fsdp")),
            P(("seq", "fsdp"), None),
            P(("seq", "fsdp"), None),
            P("fsdp"),
            P("fsdp", None),
            P("fsdp", None),
            P(None, "fsdp"),
            P("fsdp"),
            P("fsdp", None),
            P(None, "fsdp", None),
            P(None, None, "fsdp"),
        ),
        out_specs=(
            P(("seq", "fsdp"), None),
            P(),
            P(("seq", "fsdp"), None),
            P("fsdp"),
            P("fsdp", None),
            P("fsdp", None),
            P(None, "fsdp"),
            P("fsdp"),
            P("fsdp", None),
            P(None, "fsdp", None),
            P(None, None, "fsdp"),
        ),
        check_vma=False,
    )
```

profile of v0, /device:TPU:12, one launch (start us, length us, event | category | flops | bytes accessed | tf_op | source)
XLA Modules:
  0.0 1282.3 jit_solution(5250928610438677902)
XLA Ops:
  12.4 13.2 %all-reduce.5 = (bf16[1536]{0:T(1024)(128)(2,1)S(1)}, bf16[1536]{0:T(1024)(128)(2,1)S(1)}) all-reduce(bf16[1536]{0:T(1024)(128)(2,1)S(1)} %dynamic-update-slice, bf16[1536]{0:T(1024)(128)(2,1)S(1)} %dynamic-update-slice.1), channel_id=1, replica_groups=mesh['seq'=4,'fsdp'=8] {'fsdp'}, use_global_device_ids=true, to_apply=%add | all-reduce | flops 3072 | bytes 12288
  26.9 16.5 %all-gather.8.cloned.1.call-done = bf16[1536,1024]{1,0:T(8,128)(2,1)} async-done(((bf16[192,1024]{1,0:T(8,128)(2,1)}), bf16[1536,1024]{1,0:T(8,128)(2,1)}) %all-gather.8.cloned.1.call-update) | async-done | bytes 3145744 | tf_op jit(solution)/shard_map/all_gather | solution.py:83
  46.1 12.4 all_to_all.103
  67.1 17.0 %all-gather.12.cloned.1.call-done = bf16[1536,1536]{1,0:T(8,128)(2,1)} async-done(((bf16[192,1536]{1,0:T(8,128)(2,1)}), bf16[1536,1536]{1,0:T(8,128)(2,1)}) %all-gather.12.cloned.1.call-update) | async-done | bytes 4718608 | tf_op jit(solution)/shard_map/all_gather | solution.py:82
  88.2 5.1 all-to-all-start.2
  94.0 40.8 %psum.71 = f32[]{:T(128)} all-reduce(f32[]{:T(128)} %convert_reduce_fusion), channel_id=1, replica_groups=mesh['seq'=4,'fsdp'=8] {'seq','fsdp'}, use_global_device_ids=true, to_apply=%region_14.15 | all-reduce | flops 1 | bytes 8 | tf_op jit(solution)/shard_map/psum | solution.py:201
  134.8 9.1 all-gather
  144.7 7.8 all_gather.40
  156.0 95.0 %while.34 = (s32[]{:T(128)}, f32[512,2,3]{0,2,1:T(4,128)S(1)}, f32[512,2,3]{0,2,1:T(4,128)S(1)}, f32[512,2,3,64]{0,3,2,1:T(8,128)}, s32[4]{0:T(128)S(1)}, /*inde...) while((s32[]{:T(128)}, f32[512,2,3]{0,2,1:T(4,128)S(1)}, ...), condition=%wide.region_4.5_spmd.clone, body=%wide.region_1.4_spmd.clone.sunk | while | flops 848972288 | bytes 98132216 | solution.py:161
  158.3 6.7 fusion.187
  165.0 9.7 fusion.188
  182.4 6.6 fusion.187
  189.1 7.5 fusion.188
  204.7 6.7 fusion.187
  211.5 10.2 fusion.188
  230.9 6.6 fusion.187
  237.5 7.6 fusion.188
  261.2 9.5 all-to-all-done.3
  282.6 10.7 fusion.120
  294.7 62.2 %all-gather.18.cloned.1.call-done = bf16[4,1024,1536]{1,2,0:T(8,128)(2,1)} async-done(((bf16[4,1024,192]{1,2,0:T(8,128)(2,1)}), bf16[4,1024,1536]{1,2,0:T(8,128)(2,1)}) %all-gather.18.cloned.1.call-update) | async-done | bytes 12582928 | tf_op jit(solution)/shard_map/all_gather | solution.py:88
  356.9 11.2 multiply_reduce_fusion.1
  374.5 8.6 multiply_convert_fusion.1
  383.0 22.2 %convolution_bitcast_fusion.3 = f32[128,1536]{1,0:T(8,128)} fusion(bf16[128,4,96]{0,2,1:T(8,128)(2,1)} %get-tuple-element.576, bf16[4,1536,2048]{2,1,0:T(8,128)(2,1)} %all-gather.16.cloned.1.call-done, bf16[4,96,1024]{2,1,0:T(8,128)(2,1)} %get-tuple-element.571, bf16[4,96,1024]{2,1,0:T(8,128)(2,1)} %get-tuple-element.570), kind=kOutput, calls=%fused_computation.162 | convolution fusion | flops 2570649600 | bytes 27623424 | tf_op jit(solution)/shard_map/ts,sd->td/dot_general | solution.py:252
  413.4 5.1 all-to-all-start.4
  418.6 9.5 all-to-all-done.4
  431.8 103.1 %while.35 = (s32[]{:T(128)}, f32[512,2,3,64]{0,3,2,1:T(8,128)S(1)}, bf16[4,1024,2,128]{3,1,0,2:T(8,128)(2,1)}, bf16[4,1024,2,128]{1,3,2,0:T(8,128)(2,1)}, s32[4]...) while((s32[]{:T(128)}, f32[512,2,3,64]{0,3,2,1:T(8,128)S(1)}, ...), condition=%wide.region_21.22_spmd.clone, body=%wide.region_20.21_spmd.clone.sunk | while | flops 2055081472 | bytes 137720208 | solution.py:321
  437.2 6.4 fusion.201
  447.8 6.6 fusion.203
  462.9 6.4 fusion.201
  473.6 6.6 fusion.203
  488.7 6.4 fusion.201
  499.3 6.6 fusion.203
  514.4 6.4 fusion.201
  525.1 6.6 fusion.203
  540.5 17.3 %all_to_all.104 = bf16[512,2,192]{2,1,0:T(2,128)(2,1)S(1)} all-to-all(bf16[512,2,192]{2,1,0:T(2,128)(2,1)S(1)} %copy.95), channel_id=1, replica_groups=mesh['seq'=4,'fsdp'=8] {'seq'}, dimensions={0} | all-to-all | bytes 786432 | tf_op jit(solution)/shard_map/all_to_all | solution.py:332
  562.6 14.4 %reduce-scatter.10.cloned.1.call-done = bf16[512,2,128]{2,0,1:T(8,128)(2,1)} async-done(((bf16[4096,2,128]{2,0,1:T(8,128)(2,1)}), bf16[512,2,128]{2,0,1:T(8,128)(2,1)}) %reduce-scatter.10.cloned.1.call-update) | async-done | bytes 262160 | tf_op jit(solution)/shard_map/reduce_scatter | solution.py:327
  578.2 12.0 all_to_all.105
  593.2 6.5 convolution_convert_fusion.1
  601.2 13.1 %convolution_convert_fusion = bf16[4,1536,2048]{2,1,0:T(8,128)(2,1)} fusion(bf16[4,96,1536]{2,1,0:T(8,128)(2,1)S(1)} %bitcast.251, bf16[4,96,1024]{2,1,0:T(8,128)(2,1)} %get-tuple-element.571, bf16[4,96,1024]{2,1,0:T(8,128)(2,1)S(1)} %copy-done.24), kind=kOutput, calls=%fused_computation.147 | convolution fusion | flops 2431647744 | bytes 27918336 | tf_op jit(solution)/shard_map/ecd,ecf->edf/dot_general | solution.py:245
  616.6 18.1 %reduce-scatter.16.cloned.1.call-done = bf16[1536,192]{0,1:T(8,128)(2,1)} async-done(((bf16[1536,1536]{0,1:T(8,128)(2,1)}), bf16[1536,192]{0,1:T(8,128)(2,1)}) %reduce-scatter.16.cloned.1.call-update) | async-done | bytes 589840 | tf_op jit(solution)/shard_map/reduce_scatter | solution.py:363
  634.7 58.0 %reduce-scatter.12.cloned.1.call-done = bf16[192,1536]{1,0:T(8,128)(2,1)} async-done(((bf16[1536,1536]{1,0:T(8,128)(2,1)}), bf16[192,1536]{1,0:T(8,128)(2,1)}) %reduce-scatter.12.cloned.1.call-update) | async-done | bytes 589840 | tf_op jit(solution)/shard_map/reduce_scatter | solution.py:357
  692.6 50.5 %reduce-scatter.14.cloned.1.call-done = bf16[192,1024]{1,0:T(8,128)(2,1)} async-done(((bf16[1536,1024]{1,0:T(8,128)(2,1)}), bf16[192,1024]{1,0:T(8,128)(2,1)}) %reduce-scatter.14.cloned.1.call-update) | async-done | bytes 393232 | tf_op jit(solution)/shard_map/reduce_scatter | solution.py:360
  743.1 95.8 %reduce-scatter.20.cloned.1.call-done = bf16[4,1024,192]{1,2,0:T(8,128)(2,1)} async-done(((bf16[4,1024,1536]{1,2,0:T(8,128)(2,1)}), bf16[4,1024,192]{1,2,0:T(8,128)(2,1)}) %reduce-scatter.20.cloned.1.call-update) | async-done | bytes 1572880 | tf_op jit(solution)/shard_map/reduce_scatter | solution.py:375
  838.9 160.4 %reduce-scatter.18.cloned.1.call-done = bf16[4,192,2048]{2,1,0:T(8,128)(2,1)} async-done(((bf16[4,1536,2048]{2,1,0:T(8,128)(2,1)}), bf16[4,192,2048]{2,1,0:T(8,128)(2,1)}) %reduce-scatter.18.cloned.1.call-update) | async-done | bytes 3145744 | tf_op jit(solution)/shard_map/reduce_scatter | solution.py:372
  1000.0 40.9 %psum.70 = f32[]{:T(128)} all-reduce(f32[]{:T(128)} %get-tuple-element.513), channel_id=1, replica_groups=mesh['seq'=4,'fsdp'=8] {'seq','fsdp'}, use_global_device_ids=true, to_apply=%region_12.13 | all-reduce | flops 1 | bytes 8 | tf_op jit(solution)/shard_map/psum | solution.py:201
  1050.0 13.1 %all-reduce.4 = (bf16[1536]{0:T(1024)(128)(2,1)S(1)}, bf16[1536]{0:T(1024)(128)(2,1)S(1)}) all-reduce(bf16[1536]{0:T(1024)(128)(2,1)S(1)} %get-tuple-element.511, bf16[1536]{0:T(1024)(128)(2,1)S(1)} %copy-done.43), channel_id=3, replica_groups=mesh['seq'=4,'fsdp'=8] {'fsdp'}, use_global_device_ids=true, to_apply=%region_25.26.clone | all-reduce | flops 3072 | bytes 12288
  1063.2 9.4 all-reduce.6
  1075.5 186.6 %all-reduce.10.cloned.1.call-done = (bf16[192,1536]{1,0:T(8,128)(2,1)}, bf16[192,1024]{1,0:T(8,128)(2,1)}, bf16[1536,192]{0,1:T(8,128)(2,1)}, bf16[4,192,2048]{2,1,0:T(8,128)(2,1)}, bf16[4,1024,192]{1,2,0:T(8,128)(2,1)}) async-done(((bf16[192,1536]{1,0:T(8,128)(2,1)}, bf16[192,1024]{1,0:T(8,128)(2,1)}, bf16[1536,192]{0,1:T(8,128)(2,1)}, bf16[4,192,2048]{2,1,0:T(8,128)(2,1)}, ...) | async-done | bytes 6291472 | tf_op jit(solution)/shard_map/psum | solution.py:384
  (390 shorter events, 192.2 us)
Async XLA Ops:
  7.2 36.2 %all-gather.8.cloned.1.call-start = ((), (), s32[]{:S(2)}) async-start(), calls=%async_computation.14 | async-start | bytes 3538944 | tf_op jit(solution)/shard_map/all_gather | solution.py:83
  7.9 76.2 %all-gather.12.cloned.1.call-start = ((), (), s32[]{:S(2)}) async-start(), calls=%async_computation.16 | async-start | bytes 5308416 | tf_op jit(solution)/shard_map/all_gather | solution.py:82
  8.7 144.3 %all-gather.10.cloned.1.call-start = ((), (), s32[]{:S(2)}) async-start(), calls=%async_computation.15 | async-start | bytes 2359296 | tf_op jit(solution)/shard_map/all_gather | solution.py:123
  25.7 58.5 %copy-start.29 = (f32[1536]{0:T(1024)}, f32[1536]{0:T(1024)S(1)}, u32[]{:S(2)}) copy-start(f32[1536]{0:T(1024)S(1)} %convert_element_type.198) | copy-start | bytes 18436
  26.8 57.3 %copy-start.40 = (f32[128]{0:T(128)}, f32[128]{0:T(128)S(1)}, u32[]{:S(2)}) copy-start(f32[128]{0:T(128)S(1)} %add_rsqrt_fusion.1) | copy-start | bytes 1540
  58.5 25.7 %copy-start.3 = (bf16[128,1536]{1,0:T(8,128)(2,1)S(1)}, bf16[128,1536]{1,0:T(8,128)(2,1)}, u32[]{:S(2)}) copy-start(bf16[128,1536]{1,0:T(8,128)(2,1)} %param.17) | copy-start | bytes 1179652
  59.2 214.0 %all-gather.14.cloned.1.call-start = ((), (), s32[]{:S(2)}) async-start(), calls=%async_computation.17 | async-start | bytes 5308416 | tf_op jit(solution)/shard_map/all_gather | solution.py:84
  59.8 222.8 %all-gather.16.cloned.1.call-start = ((), (), s32[]{:S(2)}) async-start(), calls=%async_computation.18 | async-start | bytes 28311552 | tf_op jit(solution)/shard_map/all_gather | solution.py:87
  60.4 296.5 %all-gather.18.cloned.1.call-start = ((), (), s32[]{:S(2)}) async-start(), calls=%async_computation.19 | async-start | bytes 14155776 | tf_op jit(solution)/shard_map/all_gather | solution.py:88
  62.1 26.1 %all-to-all-start = ((bf16[128,4,2]{0,2,1:T(2,128)(2,1)}), bf16[128,4,2]{0,2,1:T(2,128)(2,1)S(1)}, u32[]{:S(2)}, u32[]{:S(2)}) async-start(bf16[128,4,2]{0,2,1:T(2,128)(2,1)} %broadcast_in_dim.125), calls=%async_computation | async-start | bytes 4096 | tf_op jit(solution)/shard_map/all_to_all | solution.py:108
  67.1 67.7 %copy-start.52 = (bf16[192,4]{0,1:T(4,128)(2,1)S(1)}, bf16[192,4]{0,1:T(4,128)(2,1)}, u32[]{:S(2)}) copy-start(bf16[192,4]{0,1:T(4,128)(2,1)} %param.27) | copy-start | bytes 4612
  88.2 64.3 %all-to-all-start.2 = ((bf16[128,8,192]{0,2,1:T(8,128)(2,1)}), bf16[128,8,192]{0,2,1:T(8,128)(2,1)S(1)}, u32[]{:S(2)}, u32[]{:S(2)}) async-start(bf16[128,8,192]{0,2,1:T(8,128)(2,1)} %bitcast.7), calls=%async_computation.2 | async-start | bytes 786432 | tf_op jit(solution)/shard_map/all_to_all | solution.py:106
  134.8 142.7 %copy-start.34 = (f32[1536]{0:T(1024)}, f32[1536]{0:T(1024)S(1)}, u32[]{:S(2)}) copy-start(f32[1536]{0:T(1024)S(1)} %convert_element_type.203) | copy-start | bytes 18436
  143.9 134.6 %copy-start.36 = (bf16[1536,4]{0,1:T(4,128)(2,1)}, bf16[1536,4]{0,1:T(4,128)(2,1)S(1)}, u32[]{:S(2)}) copy-start(bf16[1536,4]{0,1:T(4,128)(2,1)S(1)} %reshape.463) | copy-start | bytes 36868
  165.0 11.0 copy-start
  165.0 11.0 copy-start.9
  211.4 12.0 copy-start
  211.5 12.0 copy-start.9
  251.0 26.4 %copy-start.5 = (bf16[4,1024,2,128]{1,3,2,0:T(8,128)(2,1)}, bf16[4,1024,2,128]{1,3,2,0:T(8,128)(2,1)S(1)}, u32[]{:S(2)}) copy-start(bf16[4,1024,2,128]{1,3,2,0:T(8,128)(2,1)S(1)} %get-tuple-element.822) | copy-start | bytes 6291460
  251.0 26.4 %copy-start.26 = (f32[512,2,3]{0,2,1:T(4,128)}, f32[512,2,3]{0,2,1:T(4,128)S(1)}, u32[]{:S(2)}) copy-start(f32[512,2,3]{0,2,1:T(4,128)S(1)} %get-tuple-element.353) | copy-start | bytes 36868
  251.0 26.4 %copy-start.32 = (bf16[4,1024]{1,0:T(4,128)(2,1)}, bf16[4,1024]{1,0:T(4,128)(2,1)S(1)}, u32[]{:S(2)}) copy-start(bf16[4,1024]{1,0:T(4,128)(2,1)S(1)} %get-tuple-element.868) | copy-start | bytes 24580
  251.0 26.4 %copy-start.55 = (s32[4]{0:T(128)}, s32[4]{0:T(128)S(1)}, u32[]{:S(2)}) copy-start(s32[4]{0:T(128)S(1)} %get-tuple-element.872) | copy-start | bytes 52
  254.1 16.5 %all-to-all-start.3 = ((bf16[512,2,192]{2,1,0:T(2,128)(2,1)}), bf16[512,2,192]{2,1,0:T(2,128)(2,1)S(1)}, u32[]{:S(2)}, u32[]{:S(2)}) async-start(bf16[512,2,192]{2,1,0:T(2,128)(2,1)} %copy.88), calls=%async_computation.3 | async-start | bytes 1048576 | tf_op jit(solution)/shard_map/all_to_all | solution.py:167
  259.0 18.4 %copy-start.37 = (f32[128,2,4]{0,2,1:T(4,128)}, f32[128,2,4]{0,2,1:T(4,128)S(1)}, u32[]{:S(2)}) copy-start(f32[128,2,4]{0,2,1:T(4,128)S(1)} %fusion.107) | copy-start | bytes 12292
  373.5 9.6 copy-start.15
  383.0 22.2 %copy-start.7 = (f32[128,1536]{1,0:T(8,128)S(1)}, f32[128,1536]{1,0:T(8,128)}, u32[]{:S(2)}) copy-start(f32[128,1536]{1,0:T(8,128)} %copy-done.6) | copy-start | bytes 2359300
  383.0 22.2 %copy-start.17 = (f32[128,1536]{1,0:T(8,128)S(1)}, f32[128,1536]{1,0:T(8,128)}, u32[]{:S(2)}) copy-start(f32[128,1536]{1,0:T(8,128)} %get-tuple-element.583) | copy-start | bytes 2359300
  413.4 14.6 %all-to-all-start.4 = ((bf16[128,8,192]{0,2,1:T(8,128)(2,1)}), bf16[128,8,192]{0,2,1:T(8,128)(2,1)S(1)}, u32[]{:S(2)}, u32[]{:S(2)}) async-start(bf16[128,8,192]{0,2,1:T(8,128)(2,1)} %bitcast.24), calls=%async_computation.4 | async-start | bytes 786432 | tf_op jit(solution)/shard_map/all_to_all | solution.py:273
  418.5 158.4 %reduce-scatter.10.cloned.1.call-start = ((), (), s32[]{:S(2)}) async-start(), calls=%async_computation.20 | async-start | bytes 2359296 | tf_op jit(solution)/shard_map/reduce_scatter | solution.py:327
  431.8 103.4 %copy-start.22 = (bf16[128,4,2,192]{0,3,2,1:T(8,128)(2,1)S(1)}, bf16[128,4,2,192]{0,3,2,1:T(8,128)(2,1)}, u32[]{:S(2)}) copy-start(bf16[128,4,2,192]{0,3,2,1:T(8,128)(2,1)} %copy-done.21) | copy-start | bytes 1179652
  434.8 8.8 copy-start.1
  443.6 10.8 slice-start
  460.5 8.8 copy-start.1
  469.3 10.8 slice-start
  486.3 8.8 copy-start.1
  495.1 10.8 slice-start
  520.8 10.8 slice-start
  534.9 99.8 %reduce-scatter.16.cloned.1.call-start = ((), (), s32[]{:S(2)}) async-start(), calls=%async_computation.23 | async-start | bytes 5308416 | tf_op jit(solution)/shard_map/reduce_scatter | solution.py:363
  539.9 18.9 %copy-start.4 = (bf16[128,1536]{1,0:T(8,128)(2,1)S(1)}, bf16[128,1536]{1,0:T(8,128)(2,1)}, u32[]{:S(2)}) copy-start(bf16[128,1536]{1,0:T(8,128)(2,1)} %param.17) | copy-start | bytes 1179652
  539.9 18.9 %copy-start.30 = (f32[1536]{0:T(1024)S(1)}, f32[1536]{0:T(1024)}, u32[]{:S(2)}) copy-start(f32[1536]{0:T(1024)} %copy-done.29) | copy-start | bytes 18436
  539.9 18.9 %copy-start.41 = (f32[128]{0:T(128)S(1)}, f32[128]{0:T(128)}, u32[]{:S(2)}) copy-start(f32[128]{0:T(128)} %copy-done.40) | copy-start | bytes 1540
  539.9 152.7 %reduce-scatter.12.cloned.1.call-start = ((), (), s32[]{:S(2)}) async-start(), calls=%async_computation.21 | async-start | bytes 5308416 | tf_op jit(solution)/shard_map/reduce_scatter | solution.py:357
  562.5 180.6 %reduce-scatter.14.cloned.1.call-start = ((), (), s32[]{:S(2)}) async-start(), calls=%async_computation.22 | async-start | bytes 3538944 | tf_op jit(solution)/shard_map/reduce_scatter | solution.py:360
  593.2 245.7 %reduce-scatter.20.cloned.1.call-start = ((), (), s32[]{:S(2)}) async-start(), calls=%async_computation.25 | async-start | bytes 14155776 | tf_op jit(solution)/shard_map/reduce_scatter | solution.py:375
  599.7 399.6 %reduce-scatter.18.cloned.1.call-start = ((), (), s32[]{:S(2)}) async-start(), calls=%async_computation.24 | async-start | bytes 28311552 | tf_op jit(solution)/shard_map/reduce_scatter | solution.py:372
  614.3 427.3 %reduce-scatter.22.cloned.1.call-start = ((), (), s32[]{:S(2)}) async-start(), calls=%async_computation.26 | async-start | bytes 442368
  616.5 645.6 %all-reduce.10.cloned.1.call-start = ((), (), s32[]{:S(2)}) async-start(), calls=%async_computation.27 | async-start | bytes 12582912 | tf_op jit(solution)/shard_map/psum | solution.py:384
  1046.5 27.8 %copy-start.11 = (f32[128,1536]{1,0:T(8,128)S(1)}, f32[128,1536]{1,0:T(8,128)}, u32[]{:S(2)}) copy-start(f32[128,1536]{1,0:T(8,128)} %copy-done.10) | copy-start | bytes 2359300
  (56 other events, 250.2 us)
Sparse Core Ops, SparseCore 0:
  9.9 33.4 all-gather.7
  45.2 38.8 all-gather.11
  86.6 28.4 all-gather.9
  116.8 39.4 all-gather.13
  158.0 124.5 all-gather.15
  284.4 72.4 all-gather.17
  535.0 41.8 reduce-scatter.9
  580.8 53.8 reduce-scatter.15
  638.7 53.8 reduce-scatter.11
  696.8 46.2 reduce-scatter.13
  746.6 92.2 reduce-scatter.19
  842.4 156.9 reduce-scatter.17
  1003.0 33.9 reduce-scatter.21
  1039.6 222.4 all-reduce.9
where the time goes:
time: 1300 us; the launch traced here: 1280 us
  waiting for transfers between devices  703 us (54%)
  matrix products  243 us (19%)
  blocking collectives  176 us (14%)
  other arithmetic  77 us (6%)
  local copies, waits for them, and re-layouts  42 us (3%)
  starting transfers between devices  21 us (2%)
  between operations  18.9 us (1%)
    psum x1, waiting for transfers between devices, local(): lax.psum(part_two.astype(jnp.bfloat16), 'seq').astype(jnp.float32)  187 us
    reduce_scatter x1, waiting for transfers between devices, local(): lax.psum_scatter(grad_gate_up_local.astype(jnp.bfloat16), 'fsdp', scatter...  160 us
    reduce_scatter x1, waiting for transfers between devices, local(): lax.psum_scatter(grad_down_local.astype(jnp.bfloat16), 'fsdp', scatter_di...  95.8 us
    psum x2, blocking collectives, local(): lax.psum((jnp.sum(valid_rows), jnp.sum(errors * errors)), ('seq', 'fsdp'))  81.7 us
    all_gather x1, waiting for transfers between devices, local(): lax.all_gather(w_down, 'fsdp', axis=2, tiled=True)  62.2 us
    reduce_scatter x1, waiting for transfers between devices, local(): lax.psum_scatter(grad_query_local.astype(jnp.bfloat16), 'fsdp', scatter_d...  58 us
    reduce_scatter x1, waiting for transfers between devices, local(): lax.psum_scatter(grad_keyval_local.astype(jnp.bfloat16), 'fsdp', scatter_...  50.5 us
    reduce_sum x4, other arithmetic, advance(): denominator = denominator * factor + jnp.sum(exp_terms, axis=-1)  35 us
  transfers between devices with their start and end apart: 18, of which 13 were waited for; matrix products, arithmetic and copies ran while one was open for 14% of the time, Pallas kernels for 0%

commit v1 on v0

v1 whole, which is shorter than its diff:
```python
import math

import jax
import jax.numpy as jnp
from jax import lax
from jax.sharding import PartitionSpec as P

HEADS = 24
KVH = 8
HD = 64
CAP = 96
EPSILON = 1e-06
FLOOR_SCORE = -1e30
BF = jnp.bfloat16
F32 = jnp.float32


def token_place(row_index, rows_tok, shard_count, local_rows):
    owner_shard = row_index // local_rows
    within = row_index % local_rows
    return (within // rows_tok * shard_count + owner_shard) * rows_tok + within % rows_tok


def score_block(queries, key_rows, query_place, key_place, key_valid, score_scale):
    scores = (
        jnp.einsum("rkgd,jkd->rkgj", queries, key_rows, preferred_element_type=jnp.float32)
        * score_scale
    )
    causal = key_place[None, :] <= query_place[:, None]
    usable = (key_valid[None, :] > 0) | (key_place[None, :] == query_place[:, None])
    visible = (causal & usable)[:, None, None, :]
    return (jnp.where(visible, scores, FLOOR_SCORE), visible)


def attend_forward(head_queries, kv_piece, valid_row, query_place, place):
    local_rows, local_kv, groups, head_size = head_queries.shape
    score_scale = head_size ** (-0.5)
    fold = math.gcd(kv_piece.shape[0], 1024)
    number = kv_piece.shape[0] // fold
    kv_blocks = kv_piece.reshape(number, fold, local_kv, 2 * head_size)
    valid_blocks = valid_row.reshape(number, fold)
    starts = jnp.arange(number, dtype=jnp.int32) * fold

    def advance(state, block):
        kv_block, valid_block, first_row = block
        row_max, denominator, summed = state
        key_place = place(first_row + jnp.arange(fold, dtype=jnp.int32))
        masked, visible = score_block(
            head_queries,
            kv_block[..., :head_size],
            query_place,
            key_place,
            valid_block,
            score_scale,
        )
        new_max = jnp.maximum(row_max, jnp.max(masked, axis=-1))
        exp_terms = jnp.where(visible, jnp.exp(masked - new_max[..., None]), 0.0)
        factor = jnp.exp(row_max - new_max)
        denominator = denominator * factor + jnp.sum(exp_terms, axis=-1)
        summed = summed * factor[..., None] + jnp.einsum(
            "rkgj,jkd->rkgd",
            exp_terms.astype(BF),
            kv_block[..., head_size:],
            preferred_element_type=F32,
        )
        return ((new_max, denominator, summed), None)

    start = (
        jnp.full((local_rows, local_kv, groups), FLOOR_SCORE, F32),
        jnp.zeros((local_rows, local_kv, groups), F32),
        jnp.zeros((local_rows, local_kv, groups, head_size), F32),
    )
    (row_max, denominator, summed), unused = lax.scan(
        advance, start, (kv_blocks, valid_blocks, starts)
    )
    return row_max, denominator, summed / denominator[..., None]


def attend_backward(
    head_queries, kv_piece, valid_row, query_place, place, row_max, denominator, exact, head_grad
):
    local_rows, local_kv, groups, head_size = head_queries.shape
    score_scale = head_size ** (-0.5)
    grad_summed = (head_grad / denominator[..., None]).astype(BF)
    shift_term = -jnp.sum(head_grad * exact, axis=-1) / denominator
    total = kv_piece.shape[0]
    fold = math.gcd(total, 1024)
    number = total // fold
    kv_blocks = kv_piece.reshape(number, fold, local_kv, 2 * head_size)
    valid_blocks = valid_row.reshape(number, fold)
    starts = jnp.arange(number, dtype=jnp.int32) * fold

    def step(grad_q, block):
        kv_block, valid_block, first_row = block
        key_rows = kv_block[..., :head_size]
        value_rows = kv_block[..., head_size:]
        key_place = place(first_row + jnp.arange(fold, dtype=jnp.int32))
        masked, visible = score_block(
            head_queries, key_rows, query_place, key_place, valid_block, score_scale
        )
        exp_terms = jnp.where(visible, jnp.exp(masked - row_max[..., None]), 0.0)
        weights = exp_terms.astype(BF)
        products = jnp.einsum(
            "rkgd,jkd->rkgj", grad_summed, value_rows, preferred_element_type=F32
        )
        grad_scores = (exp_terms * (products + shift_term[..., None])).astype(BF)
        grad_q = (
            grad_q
            + jnp.einsum("rkgj,jkd->rkgd", grad_scores, key_rows, preferred_element_type=F32)
            * score_scale
        )
        grad_keys = (
            jnp.einsum("rkgj,rkgd->jkd", grad_scores, head_queries, preferred_element_type=F32)
            * score_scale
        )
        grad_values = jnp.einsum(
            "rkgj,rkgd->jkd", weights, grad_summed, preferred_element_type=F32
        )
        return (grad_q, jnp.concatenate([grad_keys, grad_values], axis=-1))

    grad_q, grad_kv = lax.scan(
        step,
        jnp.zeros((local_rows, local_kv, groups, head_size), F32),
        (kv_blocks, valid_blocks, starts),
    )
    return grad_q, grad_kv.reshape(total, local_kv * 2 * head_size)


def shift(block, count, step):
    return lax.ppermute(block, "seq", [(i, (i + step) % count) for i in range(count)])


def send_out(blocks, count):
    return [blocks[0]] + [shift(blocks[s], count, s) for s in range(1, count)]


def send_back(blocks, count):
    return [blocks[0]] + [shift(blocks[s], count, count - s) for s in range(1, count)]


def from_relative(blocks, place):
    count = len(blocks)
    rising = jnp.stack([blocks[-s % count] for s in range(count)])
    return lax.dynamic_slice_in_dim(
        jnp.concatenate([rising, rising]), count - place, count, 0
    )


def dot(a, b):
    return jnp.dot(a, b, preferred_element_type=F32)


def dot_nt(a, b):
    return lax.dot_general(a, b, (((1,), (1,)), ((), ())), preferred_element_type=F32)


def dot_tn(a, b):
    return lax.dot_general(a, b, (((0,), (0,)), ((), ())), preferred_element_type=F32)


def root(values):
    return lax.rsqrt(jnp.mean(values * values, axis=-1, keepdims=True) + EPSILON)


def root_back(values, factor, grad_scaled):
    inner = jnp.mean(grad_scaled * values, axis=-1, keepdims=True)
    return factor * grad_scaled - values * (factor * factor * factor * inner)


def local(
    tokens,
    teacher,
    valid,
    routes,
    slots,
    gain_attn,
    w_query,
    w_keyval,
    w_out,
    gain_ffn,
    w_router,
    w_gate_up,
    w_down,
):
    seqs = lax.axis_size("seq")
    shards = lax.axis_size("fsdp")
    z = lax.axis_index("seq")
    shard = lax.axis_index("fsdp")
    rows, width = tokens.shape
    groups = HEADS // KVH
    local_kv = KVH // seqs
    q_cols = local_kv * groups * HD
    kv_cols = local_kv * 2 * HD
    local_rows = rows * seqs
    seq_len = local_rows * shards
    experts, part, both = w_gate_up.shape
    units = both // 2
    split = seqs // experts
    piece = units // split
    expert = z // split
    fraction = z % split

    gain_one = gain_attn.astype(F32)[:, None]
    gain_two = gain_ffn.astype(F32)[:, None]
    query_scaled = (w_query.astype(F32) * gain_one).astype(BF)
    keyval_scaled = (w_keyval.astype(F32) * gain_one).astype(BF)
    heads_shard = jnp.concatenate(
        [
            lax.dynamic_slice_in_dim(query_scaled, z * q_cols, q_cols, 1),
            lax.dynamic_slice_in_dim(keyval_scaled, z * kv_cols, kv_cols, 1),
        ],
        axis=1,
    )
    heads_full = lax.all_gather(heads_shard, "fsdp", axis=0, tiled=True)
    out_full = lax.all_gather(w_out, "fsdp", axis=1, tiled=True)
    router_full = lax.all_gather(
        (w_router.astype(F32) * gain_two).astype(BF), "fsdp", axis=0, tiled=True
    )
    gate_up_shard = lax.dynamic_slice(
        w_gate_up.reshape(experts, part, 2, split, piece),
        (expert, 0, 0, fraction, 0),
        (1, part, 2, 1, piece),
    ).reshape(part, 2 * piece)
    gate_up_full = lax.all_gather(
        (gate_up_shard.astype(F32) * gain_two).astype(BF), "fsdp", axis=0, tiled=True
    )
    down_shard = lax.dynamic_slice(
        w_down, (expert, fraction * piece, 0), (1, piece, part)
    ).reshape(piece, part)
    down_full = lax.all_gather(down_shard, "fsdp", axis=1, tiled=True)
    query_full = lax.all_gather(query_scaled, "fsdp", axis=0, tiled=True)
    keyval_full = lax.all_gather(keyval_scaled, "fsdp", axis=0, tiled=True)

    valid_low = valid.astype(BF).reshape(1, rows)
    valid_local = lax.all_gather(valid_low, "seq", axis=0, tiled=True)
    valid_all = lax.all_gather(valid_local, "fsdp", axis=0, tiled=True).reshape(seq_len)
    valid_count = jnp.sum(valid_all.astype(F32))

    token_blocks = send_out([tokens] * seqs, seqs)
    projected = []
    for block in token_blocks:
        values = block.astype(F32)
        projected.append((dot(block, heads_full) * root(values)).astype(BF))
    projected = from_relative(projected, z).reshape(local_rows, q_cols + kv_cols)
    tokens_local = from_relative(token_blocks, z).reshape(local_rows, width)
    head_queries = projected[:, :q_cols].reshape(local_rows, local_kv, groups, HD)
    head_kv = projected[:, q_cols:]
    kv_all = lax.all_gather(head_kv, "fsdp", axis=0, tiled=True)

    def place(index):
        return token_place(index, rows, shards, local_rows)

    query_place = place(shard * local_rows + jnp.arange(local_rows, dtype=jnp.int32))
    row_max, denominator, exact = attend_forward(
        head_queries, kv_all, valid_all, query_place, place
    )
    attended = lax.all_to_all(
        exact.astype(BF).reshape(local_rows, q_cols), "seq", split_axis=0, concat_axis=1, tiled=True
    )

    inputs = tokens.astype(F32)
    residual = inputs + dot(attended, out_full)
    factor_two = root(residual)
    normed_two = (residual * factor_two).astype(BF)
    logits = dot(normed_two, router_full)
    expert_ids = jnp.arange(experts, dtype=jnp.int32)
    picked = (routes[:, :, None] == expert_ids).astype(F32)
    chosen = jnp.sum(picked * logits[:, None, :], axis=-1)
    gating = jax.nn.softmax(chosen, axis=-1)
    owners = ((jnp.arange(seqs, dtype=jnp.int32) + z) % seqs) // split
    to_owner = routes[:, :, None] == owners
    slot_hot = slots[:, :, None] == jnp.arange(CAP, dtype=jnp.int32)
    placed = (to_owner[:, :, :, None] & slot_hot[:, :, None, :]).astype(BF)
    placed = placed.reshape(rows, 2, seqs * CAP)
    dispatch = placed[:, 0] + placed[:, 1]
    placed_pairs = jnp.concatenate([placed[:, 0], placed[:, 1]], axis=0)
    sent_rows = dot_tn(dispatch, normed_two).astype(BF).reshape(seqs, CAP, width)
    expert_rows = jnp.concatenate(send_out([sent_rows[s] for s in range(seqs)], seqs))
    gate_up = dot(expert_rows, gate_up_full)
    gate_part = gate_up[:, :piece]
    up_part = gate_up[:, piece:]
    sigmoid_gate = jax.nn.sigmoid(gate_part)
    hidden = (gate_part * sigmoid_gate * up_part).astype(BF)
    expert_out = dot(hidden, down_full).astype(BF).reshape(seqs, CAP, width)
    returned = jnp.concatenate(send_back([expert_out[s] for s in range(seqs)], seqs))
    selected = dot(placed_pairs, returned).reshape(2, rows, width)
    mixed_exact = residual + gating[:, :1] * selected[0] + gating[:, 1:] * selected[1]
    valid_rows = valid.astype(F32)
    errors = (mixed_exact - teacher.astype(F32)) * valid_rows[:, None]
    squares = lax.psum(jnp.sum(errors * errors), ("seq", "fsdp"))
    loss_value = squares / (width * valid_count)
    loss_scale = width * seq_len // 8
    grad_mixed = errors * (2.0 * loss_scale / (width * valid_count))

    grad_gating = jnp.stack(
        [jnp.sum(selected[0] * grad_mixed, axis=-1), jnp.sum(selected[1] * grad_mixed, axis=-1)],
        axis=1,
    )
    grad_chosen = gating * (grad_gating - jnp.sum(gating * grad_gating, axis=-1, keepdims=True))
    grad_logits = jnp.sum(grad_chosen[:, :, None] * picked, axis=1).astype(BF)
    weighted = jnp.concatenate(
        [(gating[:, :1] * grad_mixed).astype(BF), (gating[:, 1:] * grad_mixed).astype(BF)], axis=0
    )
    sent_grads = dot_tn(placed_pairs, weighted).astype(BF).reshape(seqs, CAP, width)
    grad_expert_out = jnp.concatenate(send_out([sent_grads[s] for s in range(seqs)], seqs))
    grad_down_local = dot_tn(hidden, grad_expert_out).astype(BF)
    grad_hidden = dot_nt(grad_expert_out, down_full)
    grad_gate = grad_hidden * up_part * sigmoid_gate * (1.0 + gate_part * (1.0 - sigmoid_gate))
    grad_up = grad_hidden * gate_part * sigmoid_gate
    grad_gate_up_rows = jnp.concatenate([grad_gate, grad_up], axis=-1).astype(BF)
    grad_rows = dot_nt(grad_gate_up_rows, gate_up_full).astype(BF).reshape(seqs, CAP, width)
    grad_gate_up_local = dot_tn(expert_rows, grad_gate_up_rows).astype(BF)
    grad_returned = jnp.concatenate(send_back([grad_rows[s] for s in range(seqs)], seqs))
    grad_down_shard = lax.psum_scatter(
        grad_down_local, "fsdp", scatter_dimension=1, tiled=True
    )
    grad_gate_up_shard = lax.psum_scatter(
        grad_gate_up_local, "fsdp", scatter_dimension=0, tiled=True
    )
    grad_down = lax.all_gather(grad_down_shard, "seq", axis=0, tiled=False)
    grad_gate_up = lax.all_gather(grad_gate_up_shard, "seq", axis=0, tiled=False)

    grad_normed_two = dot(dispatch, grad_returned) + dot_nt(grad_logits, router_full)
    grad_residual = grad_mixed + root_back(residual, factor_two, grad_normed_two)
    grad_branch = grad_residual.astype(BF)
    grad_attended = dot_nt(grad_branch, out_full).astype(BF)
    head_grad = lax.all_to_all(grad_attended, "seq", split_axis=1, concat_axis=0, tiled=True)
    head_grad = head_grad.reshape(local_rows, local_kv, groups, HD).astype(F32)

    grad_out_local = jnp.concatenate(
        [dot_tn(attended, grad_branch), dot_tn(grad_logits, normed_two)], axis=0
    ).astype(BF)
    grad_out_shard = lax.psum_scatter(grad_out_local, "fsdp", scatter_dimension=1, tiled=True)
    grad_out_sum = lax.psum(grad_out_shard, "seq").astype(F32)
    grad_out = grad_out_sum[: HEADS * HD]
    grad_router_base = grad_out_sum[HEADS * HD :].T

    grad_q, grad_kv = attend_backward(
        head_queries, kv_all, valid_all, query_place, place, row_max, denominator, exact, head_grad
    )
    grad_q = grad_q.reshape(local_rows, q_cols)
    grad_kv_own = lax.psum_scatter(grad_kv.astype(BF), "fsdp", scatter_dimension=0, tiled=True)
    token_grad_q = lax.all_to_all(
        grad_q.astype(BF), "seq", split_axis=0, concat_axis=1, tiled=True
    )
    token_grad_kv = lax.all_to_all(grad_kv_own, "seq", split_axis=0, concat_axis=1, tiled=True)
    factor_local = root(tokens_local.astype(F32))
    grad_heads = jnp.concatenate([grad_q, grad_kv_own.astype(F32)], axis=1) * factor_local
    grad_heads_local = dot_tn(tokens_local, grad_heads.astype(BF)).astype(BF)
    grad_heads_shard = lax.psum_scatter(
        grad_heads_local, "fsdp", scatter_dimension=0, tiled=True
    )
    grad_heads_all = lax.all_gather(grad_heads_shard, "seq", axis=0, tiled=False).astype(F32)
    grad_query_base = jnp.concatenate([grad_heads_all[s, :, :q_cols] for s in range(seqs)], axis=1)
    grad_keyval_base = jnp.concatenate([grad_heads_all[s, :, q_cols:] for s in range(seqs)], axis=1)
    grad_normed = dot_nt(token_grad_q, query_full) + dot_nt(token_grad_kv, keyval_full)
    grad_tokens = grad_residual + root_back(inputs, root(inputs), grad_normed)

    grad_gain_attn = jnp.sum(w_query.astype(F32) * grad_query_base, axis=1) + jnp.sum(
        w_keyval.astype(F32) * grad_keyval_base, axis=1
    )
    grad_down = grad_down.reshape(experts, units, part).astype(F32)
    grad_gate_up = (
        grad_gate_up.reshape(experts, split, part, 2, piece)
        .transpose(0, 2, 3, 1, 4)
        .reshape(experts, part, both)
        .astype(F32)
    )
    grad_gain_ffn = jnp.sum(w_gate_up.astype(F32) * grad_gate_up, axis=(0, 2)) + jnp.sum(
        w_router.astype(F32) * grad_router_base, axis=1
    )
    return (
        mixed_exact.astype(BF),
        loss_value,
        grad_tokens,
        grad_gain_attn,
        grad_query_base * gain_one,
        grad_keyval_base * gain_one,
        grad_out,
        grad_gain_ffn,
        grad_router_base * gain_two,
        grad_gate_up * gain_two,
        grad_down,
    )


def solution(mesh):
    return jax.shard_map(
        local,
        mesh=mesh,
        in_specs=(
            P(("seq", "fsdp"), None),
            P(("seq", "fsdp"), None),
            P(("seq", "fsdp")),
            P(("seq", "fsdp"), None),
            P(("seq", "fsdp"), None),
            P("fsdp"),
            P("fsdp", None),
            P("fsdp", None),
            P(None, "fsdp"),
            P("fsdp"),
            P("fsdp", None),
            P(None, "fsdp", None),
            P(None, None, "fsdp"),
        ),
        out_specs=(
            P(("seq", "fsdp"), None),
            P(),
            P(("seq", "fsdp"), None),
            P("fsdp"),
            P("fsdp", None),
            P("fsdp", None),
            P(None, "fsdp"),
            P("fsdp"),
            P("fsdp", None),
            P(None, "fsdp", None),
            P(None, None, "fsdp"),
        ),
        check_vma=False,
    )
```

time: 1300 us -> 993 us (0.76)
  waiting for transfers between devices: 703 us -> 491 us
  blocking collectives: 176 us -> 98.5 us
  matrix products: 243 us -> 176 us
  local copies, waits for them, and re-layouts: 42 us -> 76 us
  starting transfers between devices: 21 us -> 46 us
    reduce_scatter x6 -> x4, waiting for transfers between devices: 397 us -> 162 us  [the longest x1 63.4 us: local(): lax.psum_scatter(grad_gate_up_local, 'fsdp', scatter_dimension=0, tiled=T...]
    psum x1, waiting for transfers between devices: 187 us -> 41.4 us  [local(): grad_out_sum = lax.psum(grad_out_shard, 'seq').astype(F32)]
    ppermute x0 -> x15, waiting for transfers between devices: none -> 121 us  [shift(): lax.ppermute(block, 'seq', [(i, (i + step) % count) for i in range(count)])]
    dot_general x40 -> x43, matrix products: 209 us -> 141 us  [the longest x4 26.4 us: step(): jnp.einsum('rkgj,rkgd->jkd', weights, grad_summed, preferred_element_type...]
    unnamed x15 -> x16, waiting for transfers between devices: 3.12 us -> 61.4 us
    psum x3 -> x1, blocking collectives: 91.1 us -> 40.9 us  [local(): squares = lax.psum(jnp.sum(errors * errors), ('seq', 'fsdp'))]
    all_to_all x3 -> x0, blocking collectives: 41.6 us -> none  [the longest x1 17.3 us: local(): lax.all_to_all(grad_q_low, 'seq', split_axis=0, concat_axis=1, tiled=True)]
    all_gather x2 -> x4, blocking collectives: 16.8 us -> 57.6 us  [the longest x1 31.2 us: local(): lax.all_gather(grad_heads_shard, 'seq', axis=0, tiled=False).astype(F32)]
  transfers between devices with their start and end apart: 18 -> 34, of which waited for: 13 -> 24; matrix products, arithmetic and copies ran while one was open for 14% -> 18% of each run, Pallas kernels for 0% -> 0%
where the time goes in v1:
time: 993 us; the launch traced here: 982 us
  waiting for transfers between devices  491 us (49%)
  matrix products  176 us (18%)
  blocking collectives  98.5 us (10%)
  other arithmetic  76.5 us (8%)
  local copies, waits for them, and re-layouts  76 us (8%)
  starting transfers between devices  46 us (5%)
  between operations  17.8 us (2%)
    ppermute x15, waiting for transfers between devices, shift(): lax.ppermute(block, 'seq', [(i, (i + step) % count) for i in range(count)])  121 us
    reduce_scatter x1, waiting for transfers between devices, local(): lax.psum_scatter(grad_gate_up_local, 'fsdp', scatter_dimension=0, tiled=T...  63.4 us
    unnamed x16, waiting for transfers between devices  61.4 us
    all_gather x1, waiting for transfers between devices, local(): lax.all_gather(grad_gate_up_shard, 'seq', axis=0, tiled=False)  58.9 us
    reduce_scatter x1, waiting for transfers between devices, local(): lax.psum_scatter(grad_down_local, 'fsdp', scatter_dimension=1, tiled=True)  45.3 us
    psum x1, waiting for transfers between devices, local(): grad_out_sum = lax.psum(grad_out_shard, 'seq').astype(F32)  41.4 us
    psum x1, blocking collectives, local(): squares = lax.psum(jnp.sum(errors * errors), ('seq', 'fsdp'))  40.9 us
    reduce_scatter x1, waiting for transfers between devices, local(): lax.psum_scatter(grad_heads_local, 'fsdp', scatter_dimension=0, tiled=True)  39.8 us
  transfers between devices with their start and end apart: 34, of which 24 were waited for; matrix products, arithmetic and copies ran while one was open for 18% of the time, Pallas kernels for 0%

profile of v1, /device:TPU:12, one launch (start us, length us, event | category | flops | bytes accessed | tf_op | source)
XLA Modules:
  0.0 982.3 jit_solution(11369002140688120662)
XLA Ops:
  17.3 23.2 %collective-permute-done = bf16[128,1536]{1,0:T(8,128)(2,1)S(1)} collective-permute-done((bf16[128,1536]{1,0:T(8,128)(2,1)S(1)}, bf16[128,1536]{1,0:T(8,128)(2,1)S(1)}, u32[]{:S(2)}, u32[]{:S(2)}) %collective-permute-start) | collective-permute-done | bytes 393248 | tf_op jit(solution)/shard_map/ppermute | solution.py:130
  40.8 7.3 collective-permute-done.2
  53.8 6.1 reshape.530
  64.3 9.1 all-gather.5
  73.4 8.9 all-gather.6
  82.9 8.5 all-gather.7
  96.5 6.2 copy.99
  102.7 89.5 %while.34 = (s32[]{:T(128)}, f32[512,2,3]{0,2,1:T(4,128)S(1)}, f32[512,2,3]{0,2,1:T(4,128)S(1)}, f32[512,2,3,64]{0,3,2,1:T(8,128)S(1)}, s32[4]{0:T(128)S(1)}, /*...) while((s32[]{:T(128)}, f32[512,2,3]{0,2,1:T(4,128)S(1)}, ...), condition=%wide.region_7.8_spmd.clone, body=%wide.region_4.7_spmd.clone.sunk | while | flops 848972288 | bytes 93937848 | solution.py:73
  106.0 6.7 fusion.229
  112.7 6.9 fusion.230
  128.2 7.1 fusion.229
  135.4 6.9 fusion.230
  150.9 6.7 fusion.229
  157.6 7.0 fusion.230
  173.2 6.7 fusion.229
  179.9 7.1 fusion.230
  197.9 9.1 all-to-all-done
  217.9 16.7 %collective-permute-done.5 = bf16[96,1536]{1,0:T(8,128)(2,1)S(1)} collective-permute-done((bf16[96,1536]{1,0:T(8,128)(2,1)S(1)}, bf16[96,1536]{1,0:T(8,128)(2,1)S(1)}, u32[]{:S(2)}, u32[]{:S(2)}) %collective-permute-start.5) | collective-permute-done | bytes 294944 | tf_op jit(solution)/shard_map/ppermute | solution.py:130
  254.5 18.5 %collective-permute-done.8 = bf16[96,1536]{1,0:T(8,128)(2,1)S(1)} collective-permute-done((bf16[96,1536]{1,0:T(8,128)(2,1)S(1)}, bf16[96,1536]{1,0:T(8,128)(2,1)S(1)}, u32[]{:S(2)}, u32[]{:S(2)}) %collective-permute-start.8) | collective-permute-done | bytes 294944 | tf_op jit(solution)/shard_map/ppermute | solution.py:130
  287.4 17.1 %collective-permute-done.11 = bf16[96,1536]{1,0:T(8,128)(2,1)S(1)} collective-permute-done((bf16[96,1536]{1,0:T(8,128)(2,1)S(1)}, bf16[96,1536]{1,0:T(8,128)(2,1)S(1)}, u32[]{:S(2)}, u32[]{:S(2)}) %collective-permute-start.11) | collective-permute-done | bytes 294944 | tf_op jit(solution)/shard_map/ppermute | solution.py:130
  318.9 16.7 %collective-permute-done.14 = bf16[96,1536]{1,0:T(8,128)(2,1)S(1)} collective-permute-done((bf16[96,1536]{1,0:T(8,128)(2,1)S(1)}, bf16[96,1536]{1,0:T(8,128)(2,1)S(1)}, u32[]{:S(2)}, u32[]{:S(2)}) %collective-permute-start.14) | collective-permute-done | bytes 294944 | tf_op jit(solution)/shard_map/ppermute | solution.py:130
  349.2 8.1 all-to-all-done.1
  362.0 101.7 %while.35 = (s32[]{:T(128)}, f32[512,2,3,64]{0,3,2,1:T(8,128)S(1)}, bf16[4,1024,2,128]{1,3,2,0:T(8,128)(2,1)}, bf16[4,1024,2,128]{1,3,2,0:T(8,128)(2,1)}, s32[4]...) while((s32[]{:T(128)}, f32[512,2,3,64]{0,3,2,1:T(8,128)S(1)}, ...), condition=%wide.region_22.23_spmd.clone, body=%wide.region_21.22_spmd.clone.sunk | while | flops 2055081472 | bytes 137163056 | solution.py:121
  367.3 6.4 fusion.243
  378.0 6.6 fusion.245
  392.7 6.4 fusion.243
  403.4 6.6 fusion.245
  418.1 6.4 fusion.243
  428.8 6.6 fusion.245
  443.6 6.4 fusion.243
  454.2 6.6 fusion.245
  463.7 6.2 copy.109
  482.8 7.5 copy.126
  491.6 7.5 convolution_convert_fusion
  502.3 13.9 %reduce-scatter.8.cloned.1.call-done = bf16[512,256]{1,0:T(8,128)(2,1)} async-done(((bf16[4096,256]{1,0:T(8,128)(2,1)}), bf16[512,256]{1,0:T(8,128)(2,1)}) %reduce-scatter.8.cloned.1.call-update) | async-done | bytes 262160 | tf_op jit(solution)/shard_map/reduce_scatter | solution.py:342
  521.5 45.3 %reduce-scatter.14.cloned.1.call-done = bf16[1024,192]{0,1:T(8,128)(2,1)} async-done(((bf16[1024,1536]{0,1:T(8,128)(2,1)}), bf16[1024,192]{0,1:T(8,128)(2,1)}) %reduce-scatter.14.cloned.1.call-update) | async-done | bytes 393232 | tf_op jit(solution)/shard_map/reduce_scatter | solution.py:314
  566.8 59.3 %reduce-scatter.16.cloned.1.call-done = bf16[192,1540]{1,0:T(8,128)(2,1)} async-done(((bf16[1536,1540]{1,0:T(8,128)(2,1)}), bf16[192,1540]{1,0:T(8,128)(2,1)}) %reduce-scatter.16.cloned.1.call-update) | async-done | bytes 591376
  628.4 63.4 %reduce-scatter.12.cloned.1.call-done = bf16[192,2048]{1,0:T(8,128)(2,1)} async-done(((bf16[1536,2048]{1,0:T(8,128)(2,1)}), bf16[192,2048]{1,0:T(8,128)(2,1)}) %reduce-scatter.12.cloned.1.call-update) | async-done | bytes 786448 | tf_op jit(solution)/shard_map/reduce_scatter | solution.py:317
  698.8 8.3 all-to-all-done.2
  707.1 5.9 all-to-all-start.3
  713.0 40.9 %psum.14 = f32[]{:T(128)} all-reduce(f32[]{:T(128)} %get-tuple-element.566), channel_id=1, replica_groups=mesh['seq'=4,'fsdp'=8] {'seq','fsdp'}, use_global_device_ids=true, to_apply=%region_13.14 | all-reduce | flops 1 | bytes 8 | tf_op jit(solution)/shard_map/psum | solution.py:290
  759.2 8.8 all-gather.28.cloned.1.call-done
  772.2 39.8 %reduce-scatter.10.cloned.1.call-done = bf16[192,640]{1,0:T(8,128)(2,1)} async-done(((bf16[1536,640]{1,0:T(8,128)(2,1)}), bf16[192,640]{1,0:T(8,128)(2,1)}) %reduce-scatter.10.cloned.1.call-update) | async-done | bytes 245776 | tf_op jit(solution)/shard_map/reduce_scatter | solution.py:350
  812.0 31.2 %all-gather.2 = bf16[768,640]{1,0:T(8,128)(2,1)S(1)} all-gather(bf16[192,640]{1,0:T(8,128)(2,1)} %reduce-scatter.10.cloned.1.call-done), channel_id=4, replica_groups=mesh['seq'=4,'fsdp'=8] {'seq'}, dimensions={0}, use_global_device_ids=true | all-gather | bytes 1228800 | tf_op jit(solution)/shard_map/all_gather | solution.py:353
  847.2 11.7 %all-gather.34.cloned.1.call-done = bf16[4096,192]{0,1:T(8,128)(2,1)} async-done(((bf16[1024,192]{0,1:T(8,128)(2,1)}), bf16[4096,192]{0,1:T(8,128)(2,1)}) %all-gather.34.cloned.1.call-update) | async-done | bytes 1572880 | tf_op jit(solution)/shard_map/all_gather | solution.py:320
  862.6 41.4 %all-reduce.2.cloned.1.call-done = bf16[1540,192]{1,0:T(8,128)(2,1)} async-done(((bf16[1540,192]{1,0:T(8,128)(2,1)}), bf16[1540,192]{1,0:T(8,128)(2,1)}) %all-reduce.2.cloned.1.call-update) | async-done | bytes 591376 | tf_op jit(solution)/shard_map/psum | solution.py:334
  907.6 58.9 %all-gather.32.cloned.1.call-done = bf16[768,2048]{1,0:T(8,128)(2,1)} async-done(((bf16[192,2048]{1,0:T(8,128)(2,1)}), bf16[768,2048]{1,0:T(8,128)(2,1)}) %all-gather.32.cloned.1.call-update) | async-done | bytes 3145744 | tf_op jit(solution)/shard_map/all_gather | solution.py:321
  966.5 7.4 convert_multiply_fusion
  (453 shorter events, 244.0 us)
Async XLA Ops:
  7.2 56.2 %copy-start = (bf16[4,1024,192]{1,2,0:T(8,128)(2,1)S(1)}, bf16[4,1024,192]{1,2,0:T(8,128)(2,1)}, u32[]{:S(2)}) copy-start(bf16[4,1024,192]{1,2,0:T(8,128)(2,1)} %param.29) | copy-start | bytes 4718596
  7.2 41.1 %all-gather.18.cloned.1.call-start = ((), (), s32[]{:S(2)}) async-start(), calls=%async_computation.9 | async-start | bytes 2211840 | tf_op jit(solution)/shard_map/all_gather | solution.py:214
  11.5 80.9 %all-gather.20.cloned.1.call-start = ((), (), s32[]{:S(2)}) async-start(), calls=%async_computation.10 | async-start | bytes 2359296 | tf_op jit(solution)/shard_map/all_gather | solution.py:248
  11.6 28.9 %collective-permute-start = (bf16[128,1536]{1,0:T(8,128)(2,1)S(1)}, bf16[128,1536]{1,0:T(8,128)(2,1)S(1)}, u32[]{:S(2)}, u32[]{:S(2)}) collective-permute-start(bf16[128,1536]{1,0:T(8,128)(2,1)S(1)} %copy-done.5), channel_id=1, source_target_pairs={{0,24},{8,0},{16,8},{24,16},{1,25},{9,1},{17,9},{25,17},{2,26},{10... | collective-permute-start | bytes 1179656 | tf_op jit(solution)/shard_map/ppermute | solution.py:130
  12.1 28.6 %collective-permute-start.1 = (bf16[128,1536]{1,0:T(8,128)(2,1)S(1)}, bf16[128,1536]{1,0:T(8,128)(2,1)S(1)}, u32[]{:S(2)}, u32[]{:S(2)}) collective-permute-start(bf16[128,1536]{1,0:T(8,128)(2,1)S(1)} %copy-done.5), channel_id=1, source_target_pairs={{0,16},{8,24},{16,0},{24,8},{1,17},{9,25},{17,1},{25,9},{2,18},{10... | collective-permute-start | bytes 1179656 | tf_op jit(solution)/shard_map/ppermute | solution.py:130
  14.7 33.4 %collective-permute-start.2 = (bf16[128,1536]{1,0:T(8,128)(2,1)S(1)}, bf16[128,1536]{1,0:T(8,128)(2,1)S(1)}, u32[]{:S(2)}, u32[]{:S(2)}) collective-permute-start(bf16[128,1536]{1,0:T(8,128)(2,1)S(1)} %copy-done.5), channel_id=1, source_target_pairs={{0,8},{8,16},{16,24},{24,0},{1,9},{9,17},{17,25},{25,1},{2,10},{10... | collective-permute-start | bytes 1179656 | tf_op jit(solution)/shard_map/ppermute | solution.py:130
  17.3 33.7 %copy-start.48 = (f32[128]{0:T(128)}, f32[128]{0:T(128)S(1)}, u32[]{:S(2)}) copy-start(f32[128]{0:T(128)S(1)} %fusion.120) | copy-start | bytes 1540
  17.3 33.7 %copy-start.45 = (f32[128]{0:T(128)}, f32[128]{0:T(128)S(1)}, u32[]{:S(2)}) copy-start(f32[128]{0:T(128)S(1)} %add_rsqrt_fusion.4) | copy-start | bytes 1540
  53.0 154.0 %all-gather.22.cloned.1.call-start = ((), (), s32[]{:S(2)}) async-start(), calls=%async_computation.11 | async-start | bytes 5308416 | tf_op jit(solution)/shard_map/all_gather | solution.py:215
  53.7 185.8 %all-gather.24.cloned.1.call-start = ((), (), s32[]{:S(2)}) async-start(), calls=%async_computation.12 | async-start | bytes 7077888 | tf_op jit(solution)/shard_map/all_gather | solution.py:224
  53.8 29.1 %copy-start.40 = (f32[192]{0:T(256)}, f32[192]{0:T(256)S(1)}, u32[]{:S(2)}) copy-start(f32[192]{0:T(256)S(1)} %convert_element_type.236) | copy-start | bytes 2308
  62.3 29.2 %copy-start.47 = (s32[128,2]{0,1:T(2,128)S(1)}, s32[128,2]{0,1:T(2,128)}, u32[]{:S(2)}) copy-start(s32[128,2]{0,1:T(2,128)} %param.21) | copy-start | bytes 3076
  63.4 183.2 %all-gather.30.cloned.1.call-start = ((), (), s32[]{:S(2)}) async-start(), calls=%async_computation.20 | async-start | bytes 3538944 | tf_op jit(solution)/shard_map/all_gather | solution.py:230
  193.2 13.8 %all-to-all-start = ((bf16[4,128,384]{1,2,0:T(8,128)(2,1)}), bf16[4,128,384]{1,2,0:T(8,128)(2,1)S(1)}, u32[]{:S(2)}, u32[]{:S(2)}) async-start(bf16[4,128,384]{1,2,0:T(8,128)(2,1)} %copy.100), calls=%async_computation | async-start | bytes 786432 | tf_op jit(solution)/shard_map/all_to_all | solution.py:257
  197.9 80.5 %copy-start.35 = (bf16[128,384]{0,1:T(8,128)(2,1)}, bf16[128,384]{0,1:T(8,128)(2,1)S(1)}, u32[]{:S(2)}) copy-start(bf16[128,384]{0,1:T(8,128)(2,1)S(1)} %get-tuple-element.653) | copy-start | bytes 294916
  211.4 33.0 %copy-start.8 = (bf16[128,1536]{1,0:T(8,128)(2,1)}, bf16[128,1536]{1,0:T(8,128)(2,1)S(1)}, u32[]{:S(2)}) copy-start(bf16[128,1536]{1,0:T(8,128)(2,1)S(1)} %multiply_convert_fusion.6) | copy-start | bytes 1179652
  211.9 32.4 %copy-start.31 = (bf16[96,1536]{1,0:T(8,128)(2,1)}, bf16[96,1536]{1,0:T(8,128)(2,1)S(1)}, u32[]{:S(2)}) copy-start(bf16[96,1536]{1,0:T(8,128)(2,1)S(1)} %get-tuple-element.644) | copy-start | bytes 884740
  211.9 22.6 %collective-permute-start.5 = (bf16[96,1536]{1,0:T(8,128)(2,1)S(1)}, bf16[96,1536]{1,0:T(8,128)(2,1)S(1)}, u32[]{:S(2)}, u32[]{:S(2)}) collective-permute-start(bf16[96,1536]{1,0:T(8,128)(2,1)S(1)} %get-tuple-element.645), channel_id=1, source_target_pairs={{0,24},{8,0},{16,8},{24,16},{1,25},{9,1},{17,9},{25,17},{2,26},{10... | collective-permute-start | bytes 884744 | tf_op jit(solution)/shard_map/ppermute | solution.py:130
  214.5 20.1 %collective-permute-start.4 = (bf16[96,1536]{1,0:T(8,128)(2,1)S(1)}, bf16[96,1536]{1,0:T(8,128)(2,1)}, u32[]{:S(2)}, u32[]{:S(2)}) collective-permute-start(bf16[96,1536]{1,0:T(8,128)(2,1)S(1)} %get-tuple-element.646), channel_id=1, source_target_pairs={{0,16},{8,24},{16,0},{24,8},{1,17},{9,25},{17,1},{25,9},{2,18},{10... | collective-permute-start | bytes 884744 | tf_op jit(solution)/shard_map/ppermute | solution.py:130
  214.6 24.9 %collective-permute-start.3 = (bf16[96,1536]{1,0:T(8,128)(2,1)S(1)}, bf16[96,1536]{1,0:T(8,128)(2,1)}, u32[]{:S(2)}, u32[]{:S(2)}) collective-permute-start(bf16[96,1536]{1,0:T(8,128)(2,1)S(1)} %get-tuple-element.647), channel_id=1, source_target_pairs={{0,8},{8,16},{16,24},{24,0},{1,9},{9,17},{17,25},{25,1},{2,10},{10... | collective-permute-start | bytes 884744 | tf_op jit(solution)/shard_map/ppermute | solution.py:130
  250.2 28.2 %copy-start.37 = (bf16[128,384]{0,1:T(8,128)(2,1)S(1)}, bf16[128,384]{0,1:T(8,128)(2,1)}, u32[]{:S(2)}) copy-start(bf16[128,384]{0,1:T(8,128)(2,1)} %get-tuple-element.654) | copy-start | bytes 294916
  250.3 22.7 %collective-permute-start.8 = (bf16[96,1536]{1,0:T(8,128)(2,1)S(1)}, bf16[96,1536]{1,0:T(8,128)(2,1)S(1)}, u32[]{:S(2)}, u32[]{:S(2)}) collective-permute-start(bf16[96,1536]{1,0:T(8,128)(2,1)S(1)} %get-tuple-element.641), channel_id=1, source_target_pairs={{0,8},{8,16},{16,24},{24,0},{1,9},{9,17},{17,25},{25,1},{2,10},{10... | collective-permute-start | bytes 884744 | tf_op jit(solution)/shard_map/ppermute | solution.py:130
  252.9 24.5 %collective-permute-start.7 = (bf16[96,1536]{1,0:T(8,128)(2,1)S(1)}, bf16[96,1536]{1,0:T(8,128)(2,1)S(1)}, u32[]{:S(2)}, u32[]{:S(2)}) collective-permute-start(bf16[96,1536]{1,0:T(8,128)(2,1)S(1)} %get-tuple-element.642), channel_id=1, source_target_pairs={{0,16},{8,24},{16,0},{24,8},{1,17},{9,25},{17,1},{25,9},{2,18},{10... | collective-permute-start | bytes 884744 | tf_op jit(solution)/shard_map/ppermute | solution.py:130
  254.0 24.4 %collective-permute-start.6 = (bf16[96,1536]{1,0:T(8,128)(2,1)S(1)}, bf16[96,1536]{1,0:T(8,128)(2,1)S(1)}, u32[]{:S(2)}, u32[]{:S(2)}) collective-permute-start(bf16[96,1536]{1,0:T(8,128)(2,1)S(1)} %get-tuple-element.643), channel_id=1, source_target_pairs={{0,24},{8,0},{16,8},{24,16},{1,25},{9,1},{17,9},{25,17},{2,26},{10... | collective-permute-start | bytes 884744 | tf_op jit(solution)/shard_map/ppermute | solution.py:130
  280.5 27.7 %copy-start.50 = (bf16[1,1024,1536]{1,2,0:T(8,128)(2,1)S(1)}, bf16[1,1024,1536]{1,2,0:T(8,128)(2,1)}, u32[]{:S(2)}) copy-start(bf16[1,1024,1536]{1,2,0:T(8,128)(2,1)} %all-gather.30.cloned.1.call-done) | copy-start | bytes 9437188
  281.9 28.3 %slice-start.4 = ((s8[6291456]{0:T(1024)(128)(4,1)}), s8[4194304]{0:T(1024)(128)(4,1)S(1)}, s32[]{:S(2)}) async-start(s8[6291456]{0:T(1024)(128)(4,1)} %bitcast.361), calls=%async_computation.28 | async-start | bytes 8388608
  282.0 28.1 %copy-start.33 = (bf16[96,1536]{1,0:T(8,128)(2,1)}, bf16[96,1536]{1,0:T(8,128)(2,1)S(1)}, u32[]{:S(2)}) copy-start(bf16[96,1536]{1,0:T(8,128)(2,1)S(1)} %get-tuple-element.636) | copy-start | bytes 884740
  282.0 22.6 %collective-permute-start.11 = (bf16[96,1536]{1,0:T(8,128)(2,1)S(1)}, bf16[96,1536]{1,0:T(8,128)(2,1)S(1)}, u32[]{:S(2)}, u32[]{:S(2)}) collective-permute-start(bf16[96,1536]{1,0:T(8,128)(2,1)S(1)} %get-tuple-element.637), channel_id=1, source_target_pairs={{0,24},{8,0},{16,8},{24,16},{1,25},{9,1},{17,9},{25,17},{2,26},{10... | collective-permute-start | bytes 884744 | tf_op jit(solution)/shard_map/ppermute | solution.py:130
  282.1 22.5 %collective-permute-start.10 = (bf16[96,1536]{1,0:T(8,128)(2,1)S(1)}, bf16[96,1536]{1,0:T(8,128)(2,1)S(1)}, u32[]{:S(2)}, u32[]{:S(2)}) collective-permute-start(bf16[96,1536]{1,0:T(8,128)(2,1)S(1)} %get-tuple-element.638), channel_id=1, source_target_pairs={{0,16},{8,24},{16,0},{24,8},{1,17},{9,25},{17,1},{25,9},{2,18},{10... | collective-permute-start | bytes 884744 | tf_op jit(solution)/shard_map/ppermute | solution.py:130
  284.6 23.7 %collective-permute-start.9 = (bf16[96,1536]{1,0:T(8,128)(2,1)S(1)}, bf16[96,1536]{1,0:T(8,128)(2,1)S(1)}, u32[]{:S(2)}, u32[]{:S(2)}) collective-permute-start(bf16[96,1536]{1,0:T(8,128)(2,1)S(1)} %get-tuple-element.639), channel_id=1, source_target_pairs={{0,8},{8,16},{16,24},{24,0},{1,9},{9,17},{17,25},{25,1},{2,10},{10... | collective-permute-start | bytes 884744 | tf_op jit(solution)/shard_map/ppermute | solution.py:130
  312.9 30.7 %slice-start.2 = ((s8[4718592]{0:T(1024)(128)(4,1)}), s8[4194304]{0:T(1024)(128)(4,1)S(1)}, s32[]{:S(2)}) async-start(s8[4718592]{0:T(1024)(128)(4,1)} %bitcast.333), calls=%async_computation.26 | async-start | bytes 8388608
  313.0 22.6 %collective-permute-start.14 = (bf16[96,1536]{1,0:T(8,128)(2,1)S(1)}, bf16[96,1536]{1,0:T(8,128)(2,1)S(1)}, u32[]{:S(2)}, u32[]{:S(2)}) collective-permute-start(bf16[96,1536]{1,0:T(8,128)(2,1)S(1)} %get-tuple-element.633), channel_id=1, source_target_pairs={{0,8},{8,16},{16,24},{24,0},{1,9},{9,17},{17,25},{25,1},{2,10},{10... | collective-permute-start | bytes 884744 | tf_op jit(solution)/shard_map/ppermute | solution.py:130
  315.5 24.5 %collective-permute-start.13 = (bf16[96,1536]{1,0:T(8,128)(2,1)S(1)}, bf16[96,1536]{1,0:T(8,128)(2,1)S(1)}, u32[]{:S(2)}, u32[]{:S(2)}) collective-permute-start(bf16[96,1536]{1,0:T(8,128)(2,1)S(1)} %get-tuple-element.634), channel_id=1, source_target_pairs={{0,16},{8,24},{16,0},{24,8},{1,17},{9,25},{17,1},{25,9},{2,18},{10... | collective-permute-start | bytes 884744 | tf_op jit(solution)/shard_map/ppermute | solution.py:130
  318.6 24.2 %collective-permute-start.12 = (bf16[96,1536]{1,0:T(8,128)(2,1)S(1)}, bf16[96,1536]{1,0:T(8,128)(2,1)S(1)}, u32[]{:S(2)}, u32[]{:S(2)}) collective-permute-start(bf16[96,1536]{1,0:T(8,128)(2,1)S(1)} %get-tuple-element.635), channel_id=1, source_target_pairs={{0,24},{8,0},{16,8},{24,16},{1,25},{9,1},{17,9},{25,17},{2,26},{10... | collective-permute-start | bytes 884744 | tf_op jit(solution)/shard_map/ppermute | solution.py:130
  345.5 11.8 %all-to-all-start.1 = ((bf16[128,4,384]{2,0,1:T(8,128)(2,1)}), bf16[128,4,384]{2,0,1:T(8,128)(2,1)S(1)}, u32[]{:S(2)}, u32[]{:S(2)}) async-start(bf16[128,4,384]{2,0,1:T(8,128)(2,1)} %bitcast.270), calls=%async_computation.1 | async-start | bytes 786432 | tf_op jit(solution)/shard_map/all_to_all | solution.py:327
  348.9 167.2 %reduce-scatter.8.cloned.1.call-start = ((), (), s32[]{:S(2)}) async-start(), calls=%async_computation.14 | async-start | bytes 2359296 | tf_op jit(solution)/shard_map/reduce_scatter | solution.py:342
  473.2 93.6 %reduce-scatter.14.cloned.1.call-start = ((), (), s32[]{:S(2)}) async-start(), calls=%async_computation.19 | async-start | bytes 3538944 | tf_op jit(solution)/shard_map/reduce_scatter | solution.py:314
  477.8 148.3 %reduce-scatter.16.cloned.1.call-start = ((), (), s32[]{:S(2)}) async-start(), calls=%async_computation.23 | async-start | bytes 5750784
  490.3 201.5 %reduce-scatter.12.cloned.1.call-start = ((), (), s32[]{:S(2)}) async-start(), calls=%async_computation.18 | async-start | bytes 7077888 | tf_op jit(solution)/shard_map/reduce_scatter | solution.py:317
  499.1 255.5 %all-gather.26.cloned.1.call-start = ((), (), s32[]{:S(2)}) async-start(), calls=%async_computation.13 | async-start | bytes 5308416 | tf_op jit(solution)/shard_map/all_gather | solution.py:231
  499.7 268.2 %all-gather.28.cloned.1.call-start = ((), (), s32[]{:S(2)}) async-start(), calls=%async_computation.15 | async-start | bytes 3538944 | tf_op jit(solution)/shard_map/all_gather | solution.py:232
  500.5 311.5 %reduce-scatter.10.cloned.1.call-start = ((), (), s32[]{:S(2)}) async-start(), calls=%async_computation.16 | async-start | bytes 2211840 | tf_op jit(solution)/shard_map/reduce_scatter | solution.py:350
  521.4 337.6 %all-gather.34.cloned.1.call-start = ((), (), s32[]{:S(2)}) async-start(), calls=%async_computation.22 | async-start | bytes 1966080 | tf_op jit(solution)/shard_map/all_gather | solution.py:320
  566.8 337.3 %all-reduce.2.cloned.1.call-start = ((), (), s32[]{:S(2)}) async-start(), calls=%async_computation.17 | async-start | bytes 1581056 | tf_op jit(solution)/shard_map/psum | solution.py:334
  628.4 69.6 %copy-start.25 = (bf16[512,256]{1,0:T(8,128)(2,1)S(1)}, bf16[512,256]{1,0:T(8,128)(2,1)}, u32[]{:S(2)}) copy-start(bf16[512,256]{1,0:T(8,128)(2,1)} %reduce-scatter.8.cloned.1.call-done) | copy-start | bytes 786436
  628.4 338.1 %all-gather.32.cloned.1.call-start = ((), (), s32[]{:S(2)}) async-start(), calls=%async_computation.21 | async-start | bytes 3932160 | tf_op jit(solution)/shard_map/all_gather | solution.py:321
  692.8 14.3 %all-to-all-start.2 = ((bf16[4,128,384]{1,2,0:T(8,128)(2,1)}), bf16[4,128,384]{1,2,0:T(8,128)(2,1)S(1)}, u32[]{:S(2)}, u32[]{:S(2)}) async-start(bf16[4,128,384]{1,2,0:T(8,128)(2,1)} %copy.108), calls=%async_computation.2 | async-start | bytes 786432 | tf_op jit(solution)/shard_map/all_to_all | solution.py:343
  707.1 60.8 %all-to-all-start.3 = ((bf16[4,128,256]{1,2,0:T(8,128)(2,1)}), bf16[4,128,256]{1,2,0:T(8,128)(2,1)S(1)}, u32[]{:S(2)}, u32[]{:S(2)}) async-start(bf16[4,128,256]{1,2,0:T(8,128)(2,1)} %copy.110), calls=%async_computation.4 | async-start | bytes 524288 | tf_op jit(solution)/shard_map/all_to_all | solution.py:346
  (73 other events, 376.1 us)
Sparse Core Ops, SparseCore 0:
  11.6 28.3 all-gather.17
  53.1 28.8 all-gather.19
  83.9 38.8 all-gather.21
  125.1 45.4 all-gather.23
  172.9 32.4 all-gather.29
  473.3 42.7 reduce-scatter.7
  520.5 46.2 reduce-scatter.13
  570.3 55.7 reduce-scatter.15
  630.1 61.7 reduce-scatter.11
  693.7 39.4 all-gather.25
  735.3 32.5 all-gather.27
  771.6 40.3 reduce-scatter.9
  813.5 45.3 all-gather.33
  861.8 42.2 all-reduce.1
  905.5 60.9 all-gather.31

commit v2 on v1

v2 whole, which is shorter than its diff:
```python
import functools

import jax
import jax.numpy as jnp
from jax import lax
from jax.experimental import pallas as pl
from jax.experimental.pallas import tpu as pltpu
from jax.sharding import PartitionSpec as P

HEADS = 24
KVH = 8
HD = 64
CAP = 96
EPSILON = 1e-06
FLOOR_SCORE = -1e30
BF = jnp.bfloat16
F32 = jnp.float32


def dot(a, b):
    return jnp.dot(a, b, preferred_element_type=F32)


def dot_nt(a, b):
    return lax.dot_general(a, b, (((1,), (1,)), ((), ())), preferred_element_type=F32)


def dot_tn(a, b):
    return lax.dot_general(a, b, (((0,), (0,)), ((), ())), preferred_element_type=F32)


def own_mask(valid_row, rows):
    i = lax.broadcasted_iota(jnp.int32, (rows, rows), 0)
    j = lax.broadcasted_iota(jnp.int32, (rows, rows), 1)
    return jnp.where(j == i, 0.0, jnp.where(j < i, valid_row, FLOOR_SCORE))


def key_chunk(kv_refs, zk, rows, g):
    return jnp.concatenate(
        [ref[pl.ds(zk * rows, rows), pl.ds(g * 2 * HD, 2 * HD)] for ref in kv_refs], axis=0
    )


def forward_kernel(shards, seqs, rows, local_kv, groups, *refs):
    kv_refs = refs[:shards]
    q_ref, bias_ref, low_ref, exact_ref, lse_ref, acc_ref, max_ref = refs[shards:]
    zq = pl.program_id(0)
    stack = groups * rows
    zeros = jnp.zeros((rows, HD), BF)
    half = lax.broadcasted_iota(jnp.int32, (1, 2 * HD), 1) < HD

    def queries(g):
        parts = []
        for h in range(groups):
            start = (g * groups + h) * HD
            parts.append(jnp.concatenate([q_ref[:, start : start + HD], zeros], axis=1))
        return jnp.concatenate(parts, axis=0)

    def chunk(g, zk, scores):
        first = scores is None
        keys = key_chunk(kv_refs, zk, rows, g)
        raw = dot_nt(queries(g), keys)
        if first:
            row = bias_ref[seqs + zk]
            mask = own_mask(row[:, :rows], rows)
            mask = jnp.concatenate([mask] * groups, axis=0)
            masked = jnp.concatenate([raw[:, :rows] + mask, raw[:, rows:] + row[:, rows:]], axis=1)
            new_max = jnp.max(masked, axis=1, keepdims=True)
        else:
            masked = raw + bias_ref[zk]
            new_max = jnp.maximum(max_ref[g][:, :1], jnp.max(masked, axis=1, keepdims=True))
        terms = jnp.exp(masked - new_max).astype(BF)
        ones_values = jnp.where(half, jnp.ones_like(keys), keys)
        part = dot(terms, ones_values)
        if first:
            acc_ref[g] = part
        else:
            acc_ref[g] = acc_ref[g] * jnp.exp(max_ref[g][:, :1] - new_max) + part
        max_ref[g] = jnp.broadcast_to(new_max, (stack, 2 * HD))

    for g in range(local_kv):
        chunk(g, zq, None)

    @pl.loop(0, zq)
    def _(zk):
        for g in range(local_kv):
            chunk(g, zk, True)

    exact_parts, lse_parts = [], []
    for g in range(local_kv):
        acc = acc_ref[g]
        total = acc[:, :HD]
        exact = acc[:, HD:] / total
        lse = max_ref[g][:, :HD] + jnp.log(total)
        for h in range(groups):
            exact_parts.append(exact[h * rows : (h + 1) * rows])
            lse_parts.append(lse[h * rows : (h + 1) * rows])
    exact = jnp.concatenate(exact_parts, axis=1)
    exact_ref[...] = exact
    low_ref[...] = exact.astype(BF)
    lse_ref[...] = jnp.concatenate(lse_parts, axis=1)


def flash_forward(q, kv_blocks, bias, seqs, rows, local_kv, groups):
    shards = len(kv_blocks)
    q_cols = q.shape[1]
    kv_spec = pl.BlockSpec(kv_blocks[0].shape, lambda i: (0, 0))
    q_spec = pl.BlockSpec((rows, q_cols), lambda i: (i, 0))
    stack = groups * rows
    out = jax.ShapeDtypeStruct((seqs * rows, q_cols), F32)
    return pl.pallas_call(
        functools.partial(forward_kernel, shards, seqs, rows, local_kv, groups),
        grid=(seqs,),
        in_specs=[kv_spec] * shards + [q_spec, pl.BlockSpec(bias.shape, lambda i: (0, 0, 0))],
        out_specs=[q_spec] * 3,
        out_shape=[jax.ShapeDtypeStruct((seqs * rows, q_cols), BF), out, out],
        scratch_shapes=[
            pltpu.VMEM((local_kv, stack, 2 * HD), F32),
            pltpu.VMEM((local_kv, stack, 2 * HD), F32),
        ],
        compiler_params=pltpu.CompilerParams(vmem_limit_bytes=40 * 1024 * 1024),
        cost_estimate=pl.CostEstimate(
            flops=8 * seqs * seqs * shards * rows * rows * local_kv * groups * HD,
            bytes_accessed=8 * 1024 * 1024,
            transcendentals=seqs * seqs * shards * rows * rows * local_kv * groups // 2,
        ),
    )(*kv_blocks, q, bias)


def backward_kernel(shards, seqs, rows, local_kv, groups, *refs):
    kv_refs = refs[:shards]
    (q_ref, bias_ref, grad_ref, exact_ref, lse_ref, grad_q_ref, near_ref, far_ref,
     pair_ref, pair_t_ref, lse_wide, delta_wide, acc_q, acc_kv) = refs[shards:]
    zk = pl.program_id(0)
    stack = groups * rows
    zeros = jnp.zeros((rows, HD), BF)

    @pl.when(zk == 0)
    def _():
        acc_q[...] = jnp.zeros_like(acc_q)

        @pl.loop(0, seqs)
        def _(zq):
            here = pl.ds(zq * rows, rows)
            for g in range(local_kv):
                tops, bottoms = [], []
                for h in range(groups):
                    cols = slice((g * groups + h) * HD, (g * groups + h + 1) * HD)
                    grad = grad_ref[here, cols]
                    tops.append(jnp.concatenate([q_ref[here, cols], zeros], axis=1))
                    bottoms.append(jnp.concatenate([zeros, grad], axis=1))
                    delta = jnp.sum(grad.astype(F32) * exact_ref[here, cols], axis=1, keepdims=True)
                    part = slice(h * rows, (h + 1) * rows)
                    delta_wide[zq, g, part] = jnp.broadcast_to(delta, (rows, 2 * HD))
                    lse_wide[zq, g, part] = jnp.broadcast_to(
                        lse_ref[here, cols][:, :1], (rows, 2 * HD)
                    )
                pair = jnp.concatenate(tops + bottoms, axis=0)
                pair_ref[zq, g] = pair
                pair_t_ref[zq, g] = pair.astype(F32).T.astype(BF)

    def chunk(g, zq, first):
        keys = key_chunk(kv_refs, zk, rows, g)
        both = dot_nt(pair_ref[zq, g], keys)
        raw, products = both[:stack], both[stack:]
        if first:
            row = bias_ref[seqs + zk]
            mask = own_mask(row[:, :rows], rows)
            mask = jnp.concatenate([mask] * groups, axis=0)
            masked = jnp.concatenate([raw[:, :rows] + mask, raw[:, rows:] + row[:, rows:]], axis=1)
        else:
            masked = raw + bias_ref[zk]
        weights = jnp.exp(masked - lse_wide[zq, g][:, :1])
        grads = (weights * (products - delta_wide[zq, g][:, :1])).astype(BF)
        acc_q[zq, g] += dot(grads, keys)
        part = dot(pair_t_ref[zq, g], jnp.concatenate([grads, weights.astype(BF)], axis=0))
        if first:
            acc_kv[g] = part
        else:
            acc_kv[g] += part

    for g in range(local_kv):
        chunk(g, zk, True)

    @pl.loop(zk + 1, seqs)
    def _(zq):
        for g in range(local_kv):
            chunk(g, zq, False)

    for p in range(shards):
        target = near_ref if p < shards // 2 else far_ref
        block = jnp.concatenate(
            [acc_kv[g, :, p * rows : (p + 1) * rows].T for g in range(local_kv)], axis=1
        )
        target[p % (shards // 2)] = block.astype(BF)

    @pl.when(zk == seqs - 1)
    def _():
        @pl.loop(0, seqs)
        def _(zq):
            parts = []
            for g in range(local_kv):
                total = acc_q[zq, g]
                for h in range(groups):
                    parts.append(total[h * rows : (h + 1) * rows, :HD])
            grad_q_ref[pl.ds(zq * rows, rows), :] = jnp.concatenate(parts, axis=1)


def flash_backward(q, kv_blocks, bias, grad, exact, lse, seqs, rows, local_kv, groups):
    shards = len(kv_blocks)
    q_cols = q.shape[1]
    stack = groups * rows
    kv_cols = 2 * HD * local_kv
    kv_spec = pl.BlockSpec(kv_blocks[0].shape, lambda i: (0, 0))
    whole = pl.BlockSpec((seqs * rows, q_cols), lambda i: (0, 0))
    out_spec = pl.BlockSpec((shards // 2, rows, kv_cols), lambda i: (0, i, 0))
    out = jax.ShapeDtypeStruct((shards // 2, seqs * rows, kv_cols), BF)
    return pl.pallas_call(
        functools.partial(backward_kernel, shards, seqs, rows, local_kv, groups),
        grid=(seqs,),
        in_specs=[kv_spec] * shards
        + [whole, pl.BlockSpec(bias.shape, lambda i: (0, 0, 0)), whole, whole, whole],
        out_specs=[whole, out_spec, out_spec],
        out_shape=[jax.ShapeDtypeStruct((seqs * rows, q_cols), F32), out, out],
        scratch_shapes=[
            pltpu.VMEM((seqs, local_kv, 2 * stack, 2 * HD), BF),
            pltpu.VMEM((seqs, local_kv, 2 * HD, 2 * stack), BF),
            pltpu.VMEM((seqs, local_kv, stack, 2 * HD), F32),
            pltpu.VMEM((seqs, local_kv, stack, 2 * HD), F32),
            pltpu.VMEM((seqs, local_kv, stack, 2 * HD), F32),
            pltpu.VMEM((local_kv, 2 * HD, shards * rows), F32),
        ],
        compiler_params=pltpu.CompilerParams(vmem_limit_bytes=48 * 1024 * 1024),
        cost_estimate=pl.CostEstimate(
            flops=20 * seqs * seqs * shards * rows * rows * local_kv * groups * HD,
            bytes_accessed=12 * 1024 * 1024,
            transcendentals=seqs * seqs * shards * rows * rows * local_kv * groups // 2,
        ),
    )(*kv_blocks, q, bias, grad, exact, lse)


def shift(block, count, step):
    return lax.ppermute(block, "seq", [(i, (i + step) % count) for i in range(count)])


def send_out(blocks, count):
    return [blocks[0]] + [shift(blocks[s], count, s) for s in range(1, count)]


def send_back(blocks, count):
    return [blocks[0]] + [shift(blocks[s], count, count - s) for s in range(1, count)]


def from_relative(blocks, place):
    count = len(blocks)
    rising = jnp.stack([blocks[-s % count] for s in range(count)])
    return lax.dynamic_slice_in_dim(jnp.concatenate([rising, rising]), count - place, count, 0)


def hop(block, count, mask):
    return lax.ppermute(block, "fsdp", [(i, i ^ mask) for i in range(count)])


def gather_shards(block, count):
    near = [block] + [hop(block, count, 2 * m) for m in range(1, count // 2)]
    return near + [hop(each, count, 1) for each in near]


def sum_chips(parts, count):
    total = parts(0)
    for m in range(1, count // 2):
        total = total + hop(parts(m).astype(BF), count, 2 * m).astype(F32)
    return total


def take(array, index, axis):
    return lax.dynamic_index_in_dim(array, index, axis, keepdims=False)


def split_columns(lhs, shard, count):
    tokens, width = lhs.shape
    cut = lhs.reshape(tokens, count // 2, 2, width // count)
    core = shard % 2
    far = take(cut, 1 - core, 2).reshape(tokens, width // 2)
    near = take(cut, core, 2).reshape(tokens, width // 2)
    return far, near


def sum_product(columns, rhs, shard, count):
    far, near = columns
    return sum_parts(dot_tn(far, rhs).astype(BF), dot_tn(near, rhs).astype(BF), shard, count)


def sum_parts(far, near, shard, count):
    there = hop(far, count, 1).reshape(count // 2, -1, far.shape[1])
    here = near.reshape(count // 2, -1, far.shape[1])
    chip = shard // 2

    def parts(m):
        return take(here, chip ^ m, 0).astype(F32) + take(there, chip ^ m, 0).astype(F32)

    return sum_chips(parts, count)


def spread_scalar(value, core, rows):
    high = value.astype(BF)
    low = (value - high.astype(F32)).astype(BF)
    pair = jnp.stack([high, low])
    none = jnp.zeros_like(pair)
    row = jnp.where(core == 0, jnp.concatenate([pair, none]), jnp.concatenate([none, pair]))
    return jnp.broadcast_to(row[None, :], (rows, 4))


def root(values):
    return lax.rsqrt(jnp.mean(values * values, axis=-1, keepdims=True) + EPSILON)


def root_back(values, factor, grad_scaled):
    inner = jnp.mean(grad_scaled * values, axis=-1, keepdims=True)
    return factor * grad_scaled - values * (factor * factor * factor * inner)


def local(
    tokens,
    teacher,
    valid,
    routes,
    slots,
    gain_attn,
    w_query,
    w_keyval,
    w_out,
    gain_ffn,
    w_router,
    w_gate_up,
    w_down,
):
    seqs = lax.axis_size("seq")
    shards = lax.axis_size("fsdp")
    z = lax.axis_index("seq")
    shard = lax.axis_index("fsdp")
    rows, width = tokens.shape
    groups = HEADS // KVH
    local_kv = KVH // seqs
    q_cols = local_kv * groups * HD
    kv_cols = local_kv * 2 * HD
    local_rows = rows * seqs
    seq_len = local_rows * shards
    experts, part, both = w_gate_up.shape
    units = both // 2
    split = seqs // experts
    piece = units // split
    expert = z // split
    fraction = z % split
    scale = HD ** (-0.5)

    gain_one = gain_attn.astype(F32)[:, None]
    gain_two = gain_ffn.astype(F32)[:, None]
    query_scaled = (w_query.astype(F32) * gain_one).astype(BF)
    keyval_scaled = (w_keyval.astype(F32) * gain_one).astype(BF)
    heads_shard = jnp.concatenate(
        [
            lax.dynamic_slice_in_dim(query_scaled, z * q_cols, q_cols, 1),
            lax.dynamic_slice_in_dim(keyval_scaled, z * kv_cols, kv_cols, 1),
        ],
        axis=1,
    )
    heads_full = lax.all_gather(heads_shard, "fsdp", axis=0, tiled=True)
    out_full = lax.all_gather(w_out, "fsdp", axis=1, tiled=True)
    router_full = lax.all_gather(
        (w_router.astype(F32) * gain_two).astype(BF), "fsdp", axis=0, tiled=True
    )
    own_expert = take(w_gate_up, expert, 0)
    gate_shard = lax.dynamic_slice_in_dim(own_expert, fraction * piece, piece, 1)
    up_shard = lax.dynamic_slice_in_dim(own_expert, units + fraction * piece, piece, 1)
    down_shard = lax.dynamic_slice_in_dim(
        take(w_down, expert, 0), fraction * piece, piece, 0
    ).T
    expert_shard = jnp.concatenate(
        [
            (gate_shard.astype(F32) * gain_two).astype(BF),
            (up_shard.astype(F32) * gain_two).astype(BF),
            down_shard,
        ],
        axis=1,
    )
    expert_full = lax.all_gather(expert_shard, "fsdp", axis=0, tiled=True)
    gate_up_full = expert_full[:, : 2 * piece]
    down_full = expert_full[:, 2 * piece :]
    attn_full = lax.all_gather(
        jnp.concatenate([query_scaled, keyval_scaled], axis=1), "fsdp", axis=0, tiled=True
    )

    valid_low = valid.astype(BF).reshape(1, rows)
    token_blocks = send_out([tokens] * seqs, seqs)
    valid_local = from_relative(send_out([valid_low] * seqs, seqs), z)
    projected = []
    for block in token_blocks:
        projected.append(dot(block, heads_full) * root(block.astype(F32)))
    projected = from_relative([each.astype(BF) for each in projected], z)
    projected = projected.reshape(local_rows, q_cols + kv_cols)
    tokens_local = from_relative(token_blocks, z).reshape(local_rows, width)
    factor_local = root(tokens_local.astype(F32))
    head_queries = projected[:, :q_cols] * jnp.asarray(scale, BF)

    valid_rows_kv = local_rows // kv_cols
    payload = jnp.concatenate(
        [
            projected[:, q_cols:],
            valid_local.reshape(valid_rows_kv, kv_cols),
            jnp.zeros((16 - valid_rows_kv, kv_cols), BF),
        ],
        axis=0,
    )
    kv_blocks = gather_shards(payload, shards)
    order = jnp.asarray(
        [2 * m for m in range(shards // 2)] + [2 * m + 1 for m in range(shards // 2)], jnp.int32
    )
    valid_all = jnp.stack(
        [
            each[local_rows : local_rows + valid_rows_kv].reshape(seqs, rows)
            for each in kv_blocks
        ],
        axis=1,
    ).astype(F32)
    valid_count = jnp.sum(valid_all)
    bias = jnp.where(valid_all > 0, 0.0, FLOOR_SCORE)
    earlier = ((order ^ shard) < shard) | (order == 0)
    bias_same = jnp.where(earlier[None, :, None], bias, FLOOR_SCORE)
    bias = jnp.concatenate([bias, bias_same]).reshape(2 * seqs, 1, shards * rows)
    attended_low, exact, lse = flash_forward(
        head_queries, kv_blocks, bias, seqs, rows, local_kv, groups
    )
    attended = lax.all_to_all(attended_low, "seq", split_axis=0, concat_axis=1, tiled=True)

    inputs = tokens.astype(F32)
    residual = inputs + dot(attended, out_full)
    factor_two = root(residual)
    normed_two = (residual * factor_two).astype(BF)
    logits = dot(normed_two, router_full)
    expert_ids = jnp.arange(experts, dtype=jnp.int32)
    picked = (routes[:, :, None] == expert_ids).astype(F32)
    chosen = jnp.sum(picked * logits[:, None, :], axis=-1)
    gating = jax.nn.softmax(chosen, axis=-1)
    owners = ((jnp.arange(seqs, dtype=jnp.int32) + z) % seqs) // split
    to_owner = routes[:, :, None] == owners
    slot_hot = slots[:, :, None] == jnp.arange(CAP, dtype=jnp.int32)
    placed = (to_owner[:, :, :, None] & slot_hot[:, :, None, :]).astype(BF)
    placed = placed.reshape(rows, 2, seqs * CAP)
    dispatch = placed[:, 0] + placed[:, 1]
    placed_pairs = jnp.concatenate([placed[:, 0], placed[:, 1]], axis=0)
    sent_rows = dot_tn(dispatch, normed_two).astype(BF).reshape(seqs, CAP, width)
    expert_rows = jnp.concatenate(send_out([sent_rows[s] for s in range(seqs)], seqs))
    gate_up = dot(expert_rows, gate_up_full)
    gate_part = gate_up[:, :piece]
    up_part = gate_up[:, piece:]
    sigmoid_gate = jax.nn.sigmoid(gate_part)
    hidden = (gate_part * sigmoid_gate * up_part).astype(BF)
    expert_out = dot_nt(hidden, down_full).astype(BF).reshape(seqs, CAP, width)
    returned = jnp.concatenate(send_back([expert_out[s] for s in range(seqs)], seqs))
    selected = dot(placed_pairs, returned).reshape(2, rows, width)
    mixed_exact = residual + gating[:, :1] * selected[0] + gating[:, 1:] * selected[1]
    valid_rows = valid.astype(F32)
    errors = (mixed_exact - teacher.astype(F32)) * valid_rows[:, None]
    squares = jnp.sum(errors * errors)
    loss_scale = width * seq_len // 8
    grad_mixed = errors * (2.0 * loss_scale / (width * valid_count))

    grad_gating = jnp.stack(
        [jnp.sum(selected[0] * grad_mixed, axis=-1), jnp.sum(selected[1] * grad_mixed, axis=-1)],
        axis=1,
    )
    grad_chosen = gating * (grad_gating - jnp.sum(gating * grad_gating, axis=-1, keepdims=True))
    grad_logits = jnp.sum(grad_chosen[:, :, None] * picked, axis=1).astype(BF)
    weighted = jnp.concatenate(
        [(gating[:, :1] * grad_mixed).astype(BF), (gating[:, 1:] * grad_mixed).astype(BF)], axis=0
    )
    sent_grads = dot_tn(placed_pairs, weighted).astype(BF).reshape(seqs, CAP, width)
    grad_expert_out = jnp.concatenate(send_out([sent_grads[s] for s in range(seqs)], seqs))
    grad_hidden = dot(grad_expert_out, down_full)
    grad_gate = grad_hidden * up_part * sigmoid_gate * (1.0 + gate_part * (1.0 - sigmoid_gate))
    grad_up = grad_hidden * gate_part * sigmoid_gate
    grad_gate_up_rows = jnp.concatenate([grad_gate, grad_up], axis=-1).astype(BF)
    grad_rows = dot_nt(grad_gate_up_rows, gate_up_full).astype(BF).reshape(seqs, CAP, width)
    grad_returned = jnp.concatenate(send_back([grad_rows[s] for s in range(seqs)], seqs))
    grad_down_shard = sum_product(
        split_columns(grad_expert_out, shard, shards), hidden, shard, shards
    )
    grad_down = lax.all_gather(grad_down_shard.astype(BF), "seq", axis=0, tiled=False)
    grad_gate_up_shard = sum_product(
        split_columns(expert_rows, shard, shards), grad_gate_up_rows, shard, shards
    )
    grad_gate_up = lax.all_gather(grad_gate_up_shard.astype(BF), "seq", axis=0, tiled=False)

    grad_normed_two = dot(dispatch, grad_returned) + dot_nt(grad_logits, router_full)
    grad_residual = grad_mixed + root_back(residual, factor_two, grad_normed_two)
    grad_branch = grad_residual.astype(BF)
    grad_attended = dot_nt(grad_branch, out_full).astype(BF)
    head_grad = lax.all_to_all(grad_attended, "seq", split_axis=1, concat_axis=0, tiled=True)

    grad_out_part = sum_product(split_columns(grad_branch, shard, shards), attended, shard, shards)
    cut = grad_out_part.astype(BF).reshape(part, seqs, q_cols)
    grad_out_own = jnp.zeros((part, q_cols), F32)
    for each in send_out([take(cut, (z + s) % seqs, 1) for s in range(seqs)], seqs):
        grad_out_own = grad_out_own + each.astype(F32)
    grad_out = from_relative(send_out([grad_out_own.astype(BF)] * seqs, seqs), z)
    grad_out = grad_out.transpose(0, 2, 1).reshape(HEADS * HD, part).astype(F32)

    grad_q, near_kv, far_kv = flash_backward(
        head_queries, kv_blocks, bias, head_grad, exact, lse, seqs, rows, local_kv, groups
    )
    grad_q = grad_q * scale
    there_kv = hop(far_kv, shards, 1)
    grad_kv = sum_chips(lambda m: near_kv[m].astype(F32) + there_kv[m].astype(F32), shards)
    token_grad_q = lax.all_to_all(
        grad_q.astype(BF), "seq", split_axis=0, concat_axis=1, tiled=True
    )
    token_grad_kv = lax.all_to_all(
        grad_kv.astype(BF), "seq", split_axis=0, concat_axis=1, tiled=True
    )
    grad_normed = dot_nt(token_grad_q, attn_full[:, : HEADS * HD]) + dot_nt(
        token_grad_kv, attn_full[:, HEADS * HD :]
    )
    grad_tokens = grad_residual + root_back(inputs, root(inputs), grad_normed)

    token_columns = split_columns(tokens_local, shard, shards)
    normed_columns = split_columns(normed_two, shard, shards)
    query_rhs = (grad_q * factor_local).astype(BF)
    marks = spread_scalar(squares, shard % 2, width // 2)
    grad_query_part = sum_parts(
        *[
            jnp.concatenate(
                [dot_tn(columns, query_rhs).astype(BF), dot_tn(others, grad_logits).astype(BF), marks],
                axis=1,
            )
            for columns, others in zip(token_columns, normed_columns)
        ],
        shard,
        shards,
    )
    grad_keyval_part = sum_product(
        token_columns, (grad_kv * factor_local).astype(BF), shard, shards
    )
    base_cols = q_cols + experts
    plane_squares = jnp.sum(grad_query_part[:, base_cols:], axis=1, keepdims=True)
    plane_high = plane_squares.astype(BF)
    plane_low = (plane_squares - plane_high.astype(F32)).astype(BF)
    grad_query_base = from_relative(
        send_out(
            [jnp.concatenate([grad_query_part[:, :base_cols].astype(BF), plane_high, plane_low], axis=1)]
            * seqs,
            seqs,
        ),
        z,
    ).astype(F32)
    loss_value = jnp.sum(grad_query_base[:, 0, base_cols:]) / (width * valid_count)
    grad_router_base = jnp.sum(grad_query_base[:, :, q_cols:base_cols], axis=0)
    grad_query_base = grad_query_base[:, :, :q_cols].transpose(1, 0, 2).reshape(part, HEADS * HD)
    grad_keyval_base = (
        from_relative(send_out([grad_keyval_part.astype(BF)] * seqs, seqs), z)
        .astype(F32)
        .transpose(1, 0, 2)
        .reshape(part, 2 * KVH * HD)
    )

    grad_gain_attn = jnp.sum(w_query.astype(F32) * grad_query_base, axis=1) + jnp.sum(
        w_keyval.astype(F32) * grad_keyval_base, axis=1
    )
    grad_down = (
        grad_down.reshape(experts, split, part, piece)
        .transpose(0, 1, 3, 2)
        .reshape(experts, units, part)
        .astype(F32)
    )
    grad_gate_up = grad_gate_up.astype(F32)
    if split > 1:
        grad_gate_up = (
            grad_gate_up.reshape(experts, split, part, 2, piece)
            .transpose(0, 2, 3, 1, 4)
            .reshape(experts, part, both)
        )
    grad_gain_ffn = jnp.sum(w_gate_up.astype(F32) * grad_gate_up, axis=(0, 2)) + jnp.sum(
        w_router.astype(F32) * grad_router_base, axis=1
    )
    return (
        mixed_exact.astype(BF),
        loss_value,
        grad_tokens,
        grad_gain_attn,
        grad_query_base * gain_one,
        grad_keyval_base * gain_one,
        grad_out,
        grad_gain_ffn,
        grad_router_base * gain_two,
        grad_gate_up * gain_two,
        grad_down,
    )


def solution(mesh):
    return jax.shard_map(
        local,
        mesh=mesh,
        in_specs=(
            P(("seq", "fsdp"), None),
            P(("seq", "fsdp"), None),
            P(("seq", "fsdp")),
            P(("seq", "fsdp"), None),
            P(("seq", "fsdp"), None),
            P("fsdp"),
            P("fsdp", None),
            P("fsdp", None),
            P(None, "fsdp"),
            P("fsdp"),
            P("fsdp", None),
            P(None, "fsdp", None),
            P(None, None, "fsdp"),
        ),
        out_specs=(
            P(("seq", "fsdp"), None),
            P(),
            P(("seq", "fsdp"), None),
            P("fsdp"),
            P("fsdp", None),
            P("fsdp", None),
            P(None, "fsdp"),
            P("fsdp"),
            P("fsdp", None),
            P(None, "fsdp", None),
            P(None, None, "fsdp"),
        ),
        check_vma=False,
    )
```

time: 993 us -> 617 us (0.62)
  the two profiles are of different devices: /device:TPU:12 before, /device:TPU:0 now
where the time goes in v2:
time: 617 us; the launch traced here: 608 us
  waiting for transfers between devices  247 us (40%)
  starting transfers between devices  82.6 us (13%)
  local copies, waits for them, and re-layouts  72.8 us (12%)
  other arithmetic  71.3 us (12%)
  matrix products  63.4 us (10%)
  Pallas kernels  42.7 us (7%)
  between operations  19.6 us (3%)
  blocking collectives  8.92 us (1%)
    ppermute x30, waiting for transfers between devices, shift(): lax.ppermute(block, 'seq', [(i, (i + step) % count) for i in range(count)])  144 us
    ppermute x31, waiting for transfers between devices, hop(): return lax.ppermute(block, 'fsdp', [(i, i ^ mask) for i in range(count)])  73.6 us
    ppermute x30, starting transfers between devices, shift(): lax.ppermute(block, 'seq', [(i, (i + step) % count) for i in range(count)])  41.3 us
    pallas_call x1, Pallas kernels, flash_backward(): pl.pallas_call(functools.partial(backward_kernel, shards, seqs, rows, loc...  24.3 us
    ppermute x31, starting transfers between devices, hop(): return lax.ppermute(block, 'fsdp', [(i, i ^ mask) for i in range(count)])  24.1 us
    dot_general x10, matrix products, dot(): return jnp.dot(a, b, preferred_element_type=F32)  22.5 us
    dot_general x14, matrix products, dot_tn(): lax.dot_general(a, b, (((0,), (0,)), ((), ())), preferred_element_type=F32)  21.9 us
    unnamed x180, local copies, waits for them, and re-layouts  20.4 us
  transfers between devices with their start and end apart: 71, of which 30 were waited for; matrix products, arithmetic and copies ran while one was open for 31% of the time, Pallas kernels for 7%

profile of v2, /device:TPU:0, one launch (start us, length us, event | category | flops | bytes accessed | tf_op | source)
XLA Modules:
  0.0 608.2 jit_solution(8834419316379995562)
XLA Ops:
  15.1 5.0 collective-permute-start.3
  28.3 8.9 %all-gather.2 = bf16[8,192,4]{1,2,0:T(4,128)(2,1)S(1)} all-gather(bf16[1,192,4]{1,2,0:T(4,128)(2,1)S(1)} %copy.277), channel_id=1, replica_groups=mesh['seq'=4,'fsdp'=8] {'fsdp'}, dimensions={0}, use_global_device_ids=true | all-gather | bytes 13824 | tf_op jit(solution)/shard_map/all_gather | solution.py:370
  38.8 19.6 %collective-permute-done.1 = bf16[128,1536]{1,0:T(8,128)(2,1)S(1)} collective-permute-done((bf16[128,1536]{1,0:T(8,128)(2,1)S(1)}, bf16[128,1536]{1,0:T(8,128)(2,1)S(1)}, u32[]{:S(2)}, u32[]{:S(2)}) %collective-permute-start.1) | collective-permute-done | bytes 393248 | tf_op jit(solution)/shard_map/ppermute | solution.py:243
  71.1 11.5 %collective-permute-done.6.refs_1_ = bf16[528,256]{1,0:T(8,128)(2,1)S(1)} collective-permute-done((bf16[528,256]{1,0:T(8,128)(2,1)S(1)}, bf16[528,256]{1,0:T(8,128)(2,1)S(1)}, u32[]{:S(2)}, u32[]{:S(2)}) %collective-permute-start.6) | collective-permute-done | bytes 270368 | tf_op jit(solution)/shard_map/ppermute | solution.py:261
  84.5 8.5 %collective-permute-done.8.refs_3_ = bf16[528,256]{1,0:T(8,128)(2,1)S(1)} collective-permute-done((bf16[528,256]{1,0:T(8,128)(2,1)S(1)}, bf16[528,256]{1,0:T(8,128)(2,1)S(1)}, u32[]{:S(2)}, u32[]{:S(2)}) %collective-permute-start.8) | collective-permute-done | bytes 270368 | tf_op jit(solution)/shard_map/ppermute | solution.py:261
  94.4 3.8 copy.282
  98.2 3.6 reshape_reshape.3
  103.8 18.4 %shard_map.221 = (bf16[512,384]{1,0:T(8,128)(2,1)S(1)}, f32[512,384]{1,0:T(8,128)S(1)}, f32[512,384]{1,0:T(8,128)S(1)}) custom-call(bf16[528,256]{1,0:T(8,128)(2,1)S(1)} %maximum_maximum_fusion.2.refs_0_, bf16[528,256]{1,0:T(8,128)(2,1)S(1)} %collective-permute-done.6.refs_1_, bf16[528,256]{1,0:T(8,128)(2,1)S(1)} %collective-permute-done.7.refs_2_, ...), custom_call_target="tpu_custom_call" | custom-call | flops 6442450944 | bytes 8388608 | tf_op jit(solution)/shard_map/pallas_call | solution.py:111
  125.0 4.1 all-to-all-start
  132.4 9.1 %all-to-all-done = bf16[4,128,384]{1,2,0:T(8,128)(2,1)S(1)} async-done(((bf16[4,128,384]{1,2,0:T(8,128)(2,1)}), bf16[4,128,384]{1,2,0:T(8,128)(2,1)S(1)}, u32[]{:S(2)}, u32[]{:S(2)}) %all-to-all-start) | async-done | bytes 393248 | tf_op jit(solution)/shard_map/all_to_all | solution.py:434
  142.3 4.2 multiply_reduce_fusion.5
  156.2 5.3 collective-permute-done.15
  161.6 16.8 %collective-permute-done.14 = bf16[96,1536]{1,0:T(8,128)(2,1)} collective-permute-done((bf16[96,1536]{1,0:T(8,128)(2,1)}, bf16[96,1536]{1,0:T(8,128)(2,1)}, u32[]{:S(2)}, u32[]{:S(2)}) %collective-permute-start.14) | collective-permute-done | bytes 294944 | tf_op jit(solution)/shard_map/ppermute | solution.py:243
  178.4 6.0 fusion.3
  186.0 3.6 convolution_convert_fusion.6
  203.5 3.1 pad_maximum_fusion.2
  206.6 7.0 %collective-permute-done.17 = bf16[96,1536]{1,0:T(8,128)(2,1)} collective-permute-done((bf16[96,1536]{1,0:T(8,128)(2,1)}, bf16[96,1536]{1,0:T(8,128)(2,1)}, u32[]{:S(2)}, u32[]{:S(2)}) %collective-permute-start.17) | collective-permute-done | bytes 294944 | tf_op jit(solution)/shard_map/ppermute | solution.py:243
  218.9 8.4 %collective-permute-start.21 = (bf16[96,1536]{1,0:T(8,128)(2,1)}, bf16[96,1536]{1,0:T(8,128)(2,1)}, u32[]{:S(2)}, u32[]{:S(2)}) collective-permute-start(bf16[96,1536]{1,0:T(8,128)(2,1)} %get-tuple-element.99), channel_id=1, source_target_pairs={{0,24},{8,0},{16,8},{24,16},{1,25},{9,1},{17,9},{25,17},{2,26},{10... | collective-permute-start | bytes 884744 | tf_op jit(solution)/shard_map/ppermute | solution.py:243
  235.1 18.2 %collective-permute-done.20 = bf16[96,1536]{1,0:T(8,128)(2,1)} collective-permute-done((bf16[96,1536]{1,0:T(8,128)(2,1)}, bf16[96,1536]{1,0:T(8,128)(2,1)}, u32[]{:S(2)}, u32[]{:S(2)}) %collective-permute-start.20) | collective-permute-done | bytes 294944 | tf_op jit(solution)/shard_map/ppermute | solution.py:243
  253.4 4.9 multiply_convert_fusion.1
  263.0 3.0 collective-permute-start.22
  277.0 3.5 convolution_convert_fusion
  283.2 3.5 convolution_convert_fusion.1
  289.9 3.1 convolution_convert_fusion.7
  293.8 6.1 %all-to-all-start.1 = ((bf16[128,4,384]{2,0,1:T(8,128)(2,1)}), bf16[128,4,384]{2,0,1:T(8,128)(2,1)S(1)}, u32[]{:S(2)}, u32[]{:S(2)}) async-start(bf16[128,4,384]{2,0,1:T(8,128)(2,1)} %bitcast.328), calls=%async_computation.1 | async-start | bytes 786432 | tf_op jit(solution)/shard_map/all_to_all | solution.py:499
  301.1 9.6 %all-to-all-done.1 = bf16[128,4,384]{2,0,1:T(8,128)(2,1)S(1)} async-done(((bf16[128,4,384]{2,0,1:T(8,128)(2,1)}), bf16[128,4,384]{2,0,1:T(8,128)(2,1)S(1)}, u32[]{:S(2)}, u32[]{:S(2)}) %all-to-all-start.1) | async-done | bytes 393248 | tf_op jit(solution)/shard_map/all_to_all | solution.py:499
  313.9 24.3 %shard_map.222 = (f32[512,384]{1,0:T(8,128)S(1)}, bf16[4,512,256]{2,1,0:T(8,128)(2,1)}, bf16[4,512,256]{2,1,0:T(8,128)(2,1)}) custom-call(bf16[528,256]{1,0:T(8,128)(2,1)S(1)} %maximum_maximum_fusion.2.refs_0_, bf16[528,256]{1,0:T(8,128)(2,1)S(1)} %collective-permute-done.6.refs_1_, bf16[528,256]{1,0:T(8,128)(2,1)S(1)} %collective-permute-done.7.refs_2_, ...), custom_call_target="tpu_custom_call" | custom-call | flops 16106127360 | bytes 12582912 | tf_op jit(solution)/shard_map/pallas_call | solution.py:218
  357.9 3.5 all-to-all-start.2
  370.2 3.8 all-to-all-done.2
  374.0 5.0 fusion.5
  382.9 11.4 %collective-permute-done.30 = bf16[192,390]{1,0:T(8,128)(2,1)S(1)} collective-permute-done((bf16[192,390]{1,0:T(8,128)(2,1)S(1)}, bf16[192,390]{1,0:T(8,128)(2,1)S(1)}, u32[]{:S(2)}, u32[]{:S(2)}) %collective-permute-start.30) | collective-permute-done | bytes 149792 | tf_op jit(solution)/shard_map/ppermute | solution.py:243
  408.8 5.3 collective-permute-done.35
  415.0 3.6 collective-permute-done.34
  423.9 3.4 all-to-all-start.3
  429.6 6.2 %collective-permute-done.59 = bf16[192,1024]{1,0:T(8,128)(2,1)} collective-permute-done((bf16[192,1024]{1,0:T(8,128)(2,1)}, bf16[192,1024]{1,0:T(8,128)(2,1)}, u32[]{:S(2)}, u32[]{:S(2)}) %collective-permute-start.59) | collective-permute-done | bytes 393248 | tf_op jit(solution)/shard_map/ppermute | solution.py:261
  445.5 3.5 fusion.66
  461.6 6.2 %collective-permute-done.40 = bf16[192,256]{1,0:T(8,128)(2,1)S(1)} collective-permute-done((bf16[192,256]{1,0:T(8,128)(2,1)S(1)}, bf16[192,256]{1,0:T(8,128)(2,1)S(1)}, u32[]{:S(2)}, u32[]{:S(2)}) %collective-permute-start.40) | collective-permute-done | bytes 98336 | tf_op jit(solution)/shard_map/ppermute | solution.py:243
  469.8 3.3 collective-permute-done.56
  473.6 16.4 %collective-permute-done.55 = bf16[192,2048]{1,0:T(8,128)(2,1)S(1)} collective-permute-done((bf16[192,2048]{1,0:T(8,128)(2,1)S(1)}, bf16[192,2048]{1,0:T(8,128)(2,1)S(1)}, u32[]{:S(2)}, u32[]{:S(2)}) %collective-permute-start.55) | collective-permute-done | bytes 786464 | tf_op jit(solution)/shard_map/ppermute | solution.py:261
  492.7 4.6 collective-permute-done.41
  502.7 10.5 %collective-permute-done.45 = bf16[192,1536]{1,0:T(8,128)(2,1)} collective-permute-done((bf16[192,1536]{1,0:T(8,128)(2,1)}, bf16[192,1536]{1,0:T(8,128)(2,1)}, u32[]{:S(2)}, u32[]{:S(2)}) %collective-permute-start.45) | collective-permute-done | bytes 589856 | tf_op jit(solution)/shard_map/ppermute | solution.py:261
  521.8 9.1 %collective-permute-done.49 = bf16[192,384]{1,0:T(8,128)(2,1)S(1)} collective-permute-done((bf16[192,384]{1,0:T(8,128)(2,1)S(1)}, bf16[192,384]{1,0:T(8,128)(2,1)S(1)}, u32[]{:S(2)}, u32[]{:S(2)}) %collective-permute-start.49) | collective-permute-done | bytes 147488 | tf_op jit(solution)/shard_map/ppermute | solution.py:243
  530.9 19.2 %collective-permute-done.48 = bf16[192,384]{1,0:T(8,128)(2,1)S(1)} collective-permute-done((bf16[192,384]{1,0:T(8,128)(2,1)S(1)}, bf16[192,384]{1,0:T(8,128)(2,1)S(1)}, u32[]{:S(2)}, u32[]{:S(2)}) %collective-permute-start.48) | collective-permute-done | bytes 147488 | tf_op jit(solution)/shard_map/ppermute | solution.py:243
  556.7 5.8 collective-permute-done.50
  562.5 18.9 %collective-permute-done.51 = bf16[192,384]{1,0:T(8,128)(2,1)S(1)} collective-permute-done((bf16[192,384]{1,0:T(8,128)(2,1)S(1)}, bf16[192,384]{1,0:T(8,128)(2,1)S(1)}, u32[]{:S(2)}, u32[]{:S(2)}) %collective-permute-start.51) | collective-permute-done | bytes 147488 | tf_op jit(solution)/shard_map/ppermute | solution.py:243
  582.9 3.5 convert_bitcast_fusion
  586.4 5.7 all-gather.18.cloned.1.call-done
  592.1 7.4 %convert_multiply_fusion = (f32[4,192,2048]{2,1,0:T(8,128)}, f32[192]{0:T(256)S(1)}) fusion(bf16[4,192,2048]{2,1,0:T(8,128)(2,1)} %bitcast.351, f32[192]{0:T(256)S(1)} %convert_element_type.686, bf16[4,192,2048]{2,1,0:T(8,128)(2,1)} %param.25), kind=kLoop, calls=%fused_computation | loop fusion | flops 7864128 | bytes 12584448 | tf_op jit(solution)/shard_map/mul | solution.py:595
  (476 shorter events, 209.1 us)
Async XLA Ops:
  7.2 56.2 %all-gather.10.cloned.1.call-start = ((), (), s32[]{:S(2)}) async-start(), calls=%async_computation.4 | async-start | bytes 2211840 | tf_op jit(solution)/shard_map/all_gather | solution.py:368
  11.2 130.3 %all-gather.12.cloned.1.call-start = ((), (), s32[]{:S(2)}) async-start(), calls=%async_computation.5 | async-start | bytes 5308416 | tf_op jit(solution)/shard_map/all_gather | solution.py:369
  12.0 166.4 %all-gather.14.cloned.1.call-start = ((), (), s32[]{:S(2)}) async-start(), calls=%async_computation.6 | async-start | bytes 10616832 | tf_op jit(solution)/shard_map/all_gather | solution.py:387
  14.5 355.7 %all-gather.16.cloned.1.call-start = ((), (), s32[]{:S(2)}) async-start(), calls=%async_computation.7 | async-start | bytes 8847360 | tf_op jit(solution)/shard_map/all_gather | solution.py:390
  15.1 23.2 %collective-permute-start.3 = (bf16[1,128]{1,0:T(2,128)(2,1)S(1)}, bf16[1,128]{1,0:T(2,128)(2,1)S(1)}, u32[]{:S(2)}, u32[]{:S(2)}) collective-permute-start(bf16[1,128]{1,0:T(2,128)(2,1)S(1)} %get-tuple-element.135), channel_id=1, source_target_pairs={{0,24},{8,0},{16,8},{24,16},{1,25},{9,1},{17,9},{25,17},{2,26},{10... | collective-permute-start | bytes 776 | tf_op jit(solution)/shard_map/ppermute | solution.py:243
  20.2 18.3 %collective-permute-start.4 = (bf16[1,128]{1,0:T(2,128)(2,1)S(1)}, bf16[1,128]{1,0:T(2,128)(2,1)S(1)}, u32[]{:S(2)}, u32[]{:S(2)}) collective-permute-start(bf16[1,128]{1,0:T(2,128)(2,1)S(1)} %get-tuple-element.135), channel_id=1, source_target_pairs={{0,16},{8,24},{16,0},{24,8},{1,17},{9,25},{17,1},{25,9},{2,18},{10... | collective-permute-start | bytes 776 | tf_op jit(solution)/shard_map/ppermute | solution.py:243
  20.2 18.3 %collective-permute-start.5 = (bf16[1,128]{1,0:T(2,128)(2,1)S(1)}, bf16[1,128]{1,0:T(2,128)(2,1)S(1)}, u32[]{:S(2)}, u32[]{:S(2)}) collective-permute-start(bf16[1,128]{1,0:T(2,128)(2,1)S(1)} %get-tuple-element.135), channel_id=1, source_target_pairs={{0,8},{8,16},{16,24},{24,0},{1,9},{9,17},{17,25},{25,1},{2,10},{10... | collective-permute-start | bytes 776 | tf_op jit(solution)/shard_map/ppermute | solution.py:243
  21.2 17.4 %collective-permute-start = (bf16[128,1536]{1,0:T(8,128)(2,1)S(1)}, bf16[128,1536]{1,0:T(8,128)(2,1)S(1)}, u32[]{:S(2)}, u32[]{:S(2)}) collective-permute-start(bf16[128,1536]{1,0:T(8,128)(2,1)S(1)} %copy-done.9), channel_id=1, source_target_pairs={{0,24},{8,0},{16,8},{24,16},{1,25},{9,1},{17,9},{25,17},{2,26},{10... | collective-permute-start | bytes 1179656 | tf_op jit(solution)/shard_map/ppermute | solution.py:243
  24.0 34.4 %collective-permute-start.1 = (bf16[128,1536]{1,0:T(8,128)(2,1)S(1)}, bf16[128,1536]{1,0:T(8,128)(2,1)S(1)}, u32[]{:S(2)}, u32[]{:S(2)}) collective-permute-start(bf16[128,1536]{1,0:T(8,128)(2,1)S(1)} %copy-done.9), channel_id=1, source_target_pairs={{0,16},{8,24},{16,0},{24,8},{1,17},{9,25},{17,1},{25,9},{2,18},{10... | collective-permute-start | bytes 1179656 | tf_op jit(solution)/shard_map/ppermute | solution.py:243
  38.3 20.2 %collective-permute-start.2 = (bf16[128,1536]{1,0:T(8,128)(2,1)S(1)}, bf16[128,1536]{1,0:T(8,128)(2,1)S(1)}, u32[]{:S(2)}, u32[]{:S(2)}) collective-permute-start(bf16[128,1536]{1,0:T(8,128)(2,1)S(1)} %copy-done.9), channel_id=1, source_target_pairs={{0,8},{8,16},{16,24},{24,0},{1,9},{9,17},{17,25},{25,1},{2,10},{10... | collective-permute-start | bytes 1179656 | tf_op jit(solution)/shard_map/ppermute | solution.py:243
  69.0 15.5 %collective-permute-start.7 = (bf16[528,256]{1,0:T(8,128)(2,1)S(1)}, bf16[528,256]{1,0:T(8,128)(2,1)S(1)}, u32[]{:S(2)}, u32[]{:S(2)}) collective-permute-start(bf16[528,256]{1,0:T(8,128)(2,1)S(1)} %maximum_maximum_fusion.2.refs_0_), channel_id=1, source_target_pairs={{0,4},{1,5},{2,6},{3,7},{4,0},{5,1},{6,2},{7,3},{8,12},{9,13},{10,... | collective-permute-start | bytes 811016 | tf_op jit(solution)/shard_map/ppermute | solution.py:261
  70.5 22.4 %collective-permute-start.8 = (bf16[528,256]{1,0:T(8,128)(2,1)S(1)}, bf16[528,256]{1,0:T(8,128)(2,1)S(1)}, u32[]{:S(2)}, u32[]{:S(2)}) collective-permute-start(bf16[528,256]{1,0:T(8,128)(2,1)S(1)} %maximum_maximum_fusion.2.refs_0_), channel_id=1, source_target_pairs={{0,6},{1,7},{2,4},{3,5},{4,2},{5,3},{6,0},{7,1},{8,14},{9,15},{10,... | collective-permute-start | bytes 811016 | tf_op jit(solution)/shard_map/ppermute | solution.py:261
  71.1 31.9 %collective-permute-start.9 = (bf16[528,256]{1,0:T(8,128)(2,1)S(1)}, bf16[528,256]{1,0:T(8,128)(2,1)S(1)}, u32[]{:S(2)}, u32[]{:S(2)}) collective-permute-start(bf16[528,256]{1,0:T(8,128)(2,1)S(1)} %maximum_maximum_fusion.2.refs_0_), channel_id=1, source_target_pairs={{0,1},{1,0},{2,3},{3,2},{4,5},{5,4},{6,7},{7,6},{8,9},{9,8},{10,11... | collective-permute-start | bytes 811016 | tf_op jit(solution)/shard_map/ppermute | solution.py:261
  82.6 20.4 %collective-permute-start.10 = (bf16[528,256]{1,0:T(8,128)(2,1)S(1)}, bf16[528,256]{1,0:T(8,128)(2,1)S(1)}, u32[]{:S(2)}, u32[]{:S(2)}) collective-permute-start(bf16[528,256]{1,0:T(8,128)(2,1)S(1)} %collective-permute-done.6.refs_1_), channel_id=1, source_target_pairs={{0,1},{1,0},{2,3},{3,2},{4,5},{5,4},{6,7},{7,6},{8,9},{9,8},{10,11... | collective-permute-start | bytes 811016 | tf_op jit(solution)/shard_map/ppermute | solution.py:261
  84.5 18.6 %collective-permute-start.11 = (bf16[528,256]{1,0:T(8,128)(2,1)S(1)}, bf16[528,256]{1,0:T(8,128)(2,1)S(1)}, u32[]{:S(2)}, u32[]{:S(2)}) collective-permute-start(bf16[528,256]{1,0:T(8,128)(2,1)S(1)} %collective-permute-done.7.refs_2_), channel_id=1, source_target_pairs={{0,1},{1,0},{2,3},{3,2},{4,5},{5,4},{6,7},{7,6},{8,9},{9,8},{10,11... | collective-permute-start | bytes 811016 | tf_op jit(solution)/shard_map/ppermute | solution.py:261
  125.0 16.5 %all-to-all-start = ((bf16[4,128,384]{1,2,0:T(8,128)(2,1)}), bf16[4,128,384]{1,2,0:T(8,128)(2,1)S(1)}, u32[]{:S(2)}, u32[]{:S(2)}) async-start(bf16[4,128,384]{1,2,0:T(8,128)(2,1)} %copy.274), calls=%async_computation | async-start | bytes 786432 | tf_op jit(solution)/shard_map/all_to_all | solution.py:434
  153.2 25.2 %collective-permute-start.14 = (bf16[96,1536]{1,0:T(8,128)(2,1)}, bf16[96,1536]{1,0:T(8,128)(2,1)}, u32[]{:S(2)}, u32[]{:S(2)}) collective-permute-start(bf16[96,1536]{1,0:T(8,128)(2,1)} %get-tuple-element.108), channel_id=1, source_target_pairs={{0,16},{8,24},{16,0},{24,8},{1,17},{9,25},{17,1},{25,9},{2,18},{10... | collective-permute-start | bytes 884744 | tf_op jit(solution)/shard_map/ppermute | solution.py:243
  153.2 25.2 %collective-permute-start.13 = (bf16[96,1536]{1,0:T(8,128)(2,1)}, bf16[96,1536]{1,0:T(8,128)(2,1)}, u32[]{:S(2)}, u32[]{:S(2)}) collective-permute-start(bf16[96,1536]{1,0:T(8,128)(2,1)} %get-tuple-element.109), channel_id=1, source_target_pairs={{0,8},{8,16},{16,24},{24,0},{1,9},{9,17},{17,25},{25,1},{2,10},{10... | collective-permute-start | bytes 884744 | tf_op jit(solution)/shard_map/ppermute | solution.py:243
  190.7 15.9 %collective-permute-start.18 = (bf16[96,1536]{1,0:T(8,128)(2,1)}, bf16[96,1536]{1,0:T(8,128)(2,1)}, u32[]{:S(2)}, u32[]{:S(2)}) collective-permute-start(bf16[96,1536]{1,0:T(8,128)(2,1)} %get-tuple-element.103), channel_id=1, source_target_pairs={{0,8},{8,16},{16,24},{24,0},{1,9},{9,17},{17,25},{25,1},{2,10},{10... | collective-permute-start | bytes 884744 | tf_op jit(solution)/shard_map/ppermute | solution.py:243
  191.9 21.7 %collective-permute-start.17 = (bf16[96,1536]{1,0:T(8,128)(2,1)}, bf16[96,1536]{1,0:T(8,128)(2,1)}, u32[]{:S(2)}, u32[]{:S(2)}) collective-permute-start(bf16[96,1536]{1,0:T(8,128)(2,1)} %get-tuple-element.104), channel_id=1, source_target_pairs={{0,16},{8,24},{16,0},{24,8},{1,17},{9,25},{17,1},{25,9},{2,18},{10... | collective-permute-start | bytes 884744 | tf_op jit(solution)/shard_map/ppermute | solution.py:243
  193.3 20.3 %collective-permute-start.16 = (bf16[96,1536]{1,0:T(8,128)(2,1)}, bf16[96,1536]{1,0:T(8,128)(2,1)}, u32[]{:S(2)}, u32[]{:S(2)}) collective-permute-start(bf16[96,1536]{1,0:T(8,128)(2,1)} %get-tuple-element.105), channel_id=1, source_target_pairs={{0,24},{8,0},{16,8},{24,16},{1,25},{9,1},{17,9},{25,17},{2,26},{10... | collective-permute-start | bytes 884744 | tf_op jit(solution)/shard_map/ppermute | solution.py:243
  218.9 16.2 %collective-permute-start.21 = (bf16[96,1536]{1,0:T(8,128)(2,1)}, bf16[96,1536]{1,0:T(8,128)(2,1)}, u32[]{:S(2)}, u32[]{:S(2)}) collective-permute-start(bf16[96,1536]{1,0:T(8,128)(2,1)} %get-tuple-element.99), channel_id=1, source_target_pairs={{0,24},{8,0},{16,8},{24,16},{1,25},{9,1},{17,9},{25,17},{2,26},{10... | collective-permute-start | bytes 884744 | tf_op jit(solution)/shard_map/ppermute | solution.py:243
  227.3 26.0 %collective-permute-start.20 = (bf16[96,1536]{1,0:T(8,128)(2,1)}, bf16[96,1536]{1,0:T(8,128)(2,1)}, u32[]{:S(2)}, u32[]{:S(2)}) collective-permute-start(bf16[96,1536]{1,0:T(8,128)(2,1)} %get-tuple-element.100), channel_id=1, source_target_pairs={{0,16},{8,24},{16,0},{24,8},{1,17},{9,25},{17,1},{25,9},{2,18},{10... | collective-permute-start | bytes 884744 | tf_op jit(solution)/shard_map/ppermute | solution.py:243
  227.3 26.0 %collective-permute-start.19 = (bf16[96,1536]{1,0:T(8,128)(2,1)}, bf16[96,1536]{1,0:T(8,128)(2,1)}, u32[]{:S(2)}, u32[]{:S(2)}) collective-permute-start(bf16[96,1536]{1,0:T(8,128)(2,1)} %get-tuple-element.101), channel_id=1, source_target_pairs={{0,8},{8,16},{16,24},{24,0},{1,9},{9,17},{17,25},{25,1},{2,10},{10... | collective-permute-start | bytes 884744 | tf_op jit(solution)/shard_map/ppermute | solution.py:243
  262.1 24.5 %collective-permute-start.24 = (bf16[96,1536]{1,0:T(8,128)(2,1)}, bf16[96,1536]{1,0:T(8,128)(2,1)}, u32[]{:S(2)}, u32[]{:S(2)}) collective-permute-start(bf16[96,1536]{1,0:T(8,128)(2,1)} %get-tuple-element.95), channel_id=1, source_target_pairs={{0,8},{8,16},{16,24},{24,0},{1,9},{9,17},{17,25},{25,1},{2,10},{10... | collective-permute-start | bytes 884744 | tf_op jit(solution)/shard_map/ppermute | solution.py:243
  262.2 24.5 %collective-permute-start.23 = (bf16[96,1536]{1,0:T(8,128)(2,1)}, bf16[96,1536]{1,0:T(8,128)(2,1)}, u32[]{:S(2)}, u32[]{:S(2)}) collective-permute-start(bf16[96,1536]{1,0:T(8,128)(2,1)} %get-tuple-element.96), channel_id=1, source_target_pairs={{0,16},{8,24},{16,0},{24,8},{1,17},{9,25},{17,1},{25,9},{2,18},{10... | collective-permute-start | bytes 884744 | tf_op jit(solution)/shard_map/ppermute | solution.py:243
  263.0 23.7 %collective-permute-start.22 = (bf16[96,1536]{1,0:T(8,128)(2,1)}, bf16[96,1536]{1,0:T(8,128)(2,1)}, u32[]{:S(2)}, u32[]{:S(2)}) collective-permute-start(bf16[96,1536]{1,0:T(8,128)(2,1)} %get-tuple-element.97), channel_id=1, source_target_pairs={{0,24},{8,0},{16,8},{24,16},{1,25},{9,1},{17,9},{25,17},{2,26},{10... | collective-permute-start | bytes 884744 | tf_op jit(solution)/shard_map/ppermute | solution.py:243
  280.5 168.5 %collective-permute-start.53 = (bf16[768,2048]{1,0:T(8,128)(2,1)}, bf16[768,2048]{1,0:T(8,128)(2,1)}, u32[]{:S(2)}, u32[]{:S(2)}) collective-permute-start(bf16[768,2048]{1,0:T(8,128)(2,1)} %convolution_convert_fusion), channel_id=1, source_target_pairs={{0,1},{1,0},{2,3},{3,2},{4,5},{5,4},{6,7},{7,6},{8,9},{9,8},{10,11... | collective-permute-start | bytes 9437192 | tf_op jit(solution)/shard_map/ppermute | solution.py:261
  282.7 96.3 %collective-permute-start.57 = (bf16[768,1024]{1,0:T(8,128)(2,1)}, bf16[768,1024]{1,0:T(8,128)(2,1)}, u32[]{:S(2)}, u32[]{:S(2)}) collective-permute-start(bf16[768,1024]{1,0:T(8,128)(2,1)} %convolution_convert_fusion.8), channel_id=1, source_target_pairs={{0,1},{1,0},{2,3},{3,2},{4,5},{5,4},{6,7},{7,6},{8,9},{9,8},{10,11... | collective-permute-start | bytes 4718600 | tf_op jit(solution)/shard_map/ppermute | solution.py:261
  293.8 16.9 %all-to-all-start.1 = ((bf16[128,4,384]{2,0,1:T(8,128)(2,1)}), bf16[128,4,384]{2,0,1:T(8,128)(2,1)S(1)}, u32[]{:S(2)}, u32[]{:S(2)}) async-start(bf16[128,4,384]{2,0,1:T(8,128)(2,1)} %bitcast.328), calls=%async_computation.1 | async-start | bytes 786432 | tf_op jit(solution)/shard_map/all_to_all | solution.py:499
  357.9 16.1 %all-to-all-start.2 = ((bf16[4,128,384]{1,2,0:T(8,128)(2,1)}), bf16[4,128,384]{1,2,0:T(8,128)(2,1)S(1)}, u32[]{:S(2)}, u32[]{:S(2)}) async-start(bf16[4,128,384]{1,2,0:T(8,128)(2,1)} %copy.295), calls=%async_computation.2 | async-start | bytes 786432 | tf_op jit(solution)/shard_map/all_to_all | solution.py:515
  362.4 95.6 %collective-permute-start.43 = (bf16[768,1536]{1,0:T(8,128)(2,1)}, bf16[768,1536]{1,0:T(8,128)(2,1)}, u32[]{:S(2)}, u32[]{:S(2)}) collective-permute-start(bf16[768,1536]{1,0:T(8,128)(2,1)} %convolution_convert_fusion.2), channel_id=1, source_target_pairs={{0,1},{1,0},{2,3},{3,2},{4,5},{5,4},{6,7},{7,6},{8,9},{9,8},{10,11... | collective-permute-start | bytes 7077896 | tf_op jit(solution)/shard_map/ppermute | solution.py:261
  365.1 37.3 %collective-permute-start.32 = (bf16[4,512,256]{2,1,0:T(8,128)(2,1)}, bf16[4,512,256]{2,1,0:T(8,128)(2,1)}, u32[]{:S(2)}, u32[]{:S(2)}) collective-permute-start(bf16[4,512,256]{2,1,0:T(8,128)(2,1)} %get-tuple-element.22), channel_id=1, source_target_pairs={{0,1},{1,0},{2,3},{3,2},{4,5},{5,4},{6,7},{7,6},{8,9},{9,8},{10,11... | collective-permute-start | bytes 3145736 | tf_op jit(solution)/shard_map/ppermute | solution.py:261
  418.6 17.2 %collective-permute-start.59 = (bf16[192,1024]{1,0:T(8,128)(2,1)}, bf16[192,1024]{1,0:T(8,128)(2,1)}, u32[]{:S(2)}, u32[]{:S(2)}) collective-permute-start(bf16[192,1024]{1,0:T(8,128)(2,1)} %get-tuple-element.77), channel_id=1, source_target_pairs={{0,4},{1,5},{2,6},{3,7},{4,0},{5,1},{6,2},{7,3},{8,12},{9,13},{10,... | collective-permute-start | bytes 1179656 | tf_op jit(solution)/shard_map/ppermute | solution.py:261
  420.2 15.6 %collective-permute-start.58 = (bf16[192,1024]{1,0:T(8,128)(2,1)}, bf16[192,1024]{1,0:T(8,128)(2,1)}, u32[]{:S(2)}, u32[]{:S(2)}) collective-permute-start(bf16[192,1024]{1,0:T(8,128)(2,1)} %get-tuple-element.75), channel_id=1, source_target_pairs={{0,2},{1,3},{2,0},{3,1},{4,6},{5,7},{6,4},{7,5},{8,10},{9,11},{10,... | collective-permute-start | bytes 1179656 | tf_op jit(solution)/shard_map/ppermute | solution.py:261
  423.9 21.6 %all-to-all-start.3 = ((bf16[4,128,256]{1,2,0:T(8,128)(2,1)}), bf16[4,128,256]{1,2,0:T(8,128)(2,1)S(1)}, u32[]{:S(2)}, u32[]{:S(2)}) async-start(bf16[4,128,256]{1,2,0:T(8,128)(2,1)} %copy.296), calls=%async_computation.3 | async-start | bytes 524288 | tf_op jit(solution)/shard_map/all_to_all | solution.py:518
  427.3 155.6 %all-gather.20.cloned.1.call-start = ((), (), s32[]{:S(2)}) async-start(), calls=%async_computation.9 | async-start | bytes 1966080 | tf_op jit(solution)/shard_map/all_gather | solution.py:489
  438.4 153.7 %all-gather.18.cloned.1.call-start = ((), (), s32[]{:S(2)}) async-start(), calls=%async_computation.8 | async-start | bytes 3932160 | tf_op jit(solution)/shard_map/all_gather | solution.py:493
  451.6 21.4 %collective-permute-start.56 = (bf16[192,2048]{1,0:T(8,128)(2,1)S(1)}, bf16[192,2048]{1,0:T(8,128)(2,1)S(1)}, u32[]{:S(2)}, u32[]{:S(2)}) collective-permute-start(bf16[192,2048]{1,0:T(8,128)(2,1)S(1)} %get-tuple-element.66), channel_id=1, source_target_pairs={{0,6},{1,7},{2,4},{3,5},{4,2},{5,3},{6,0},{7,1},{8,14},{9,15},{10,... | collective-permute-start | bytes 2359304 | tf_op jit(solution)/shard_map/ppermute | solution.py:261
  452.5 37.5 %collective-permute-start.55 = (bf16[192,2048]{1,0:T(8,128)(2,1)S(1)}, bf16[192,2048]{1,0:T(8,128)(2,1)S(1)}, u32[]{:S(2)}, u32[]{:S(2)}) collective-permute-start(bf16[192,2048]{1,0:T(8,128)(2,1)S(1)} %get-tuple-element.67), channel_id=1, source_target_pairs={{0,4},{1,5},{2,6},{3,7},{4,0},{5,1},{6,2},{7,3},{8,12},{9,13},{10,... | collective-permute-start | bytes 2359304 | tf_op jit(solution)/shard_map/ppermute | solution.py:261
  453.7 36.4 %collective-permute-start.54 = (bf16[192,2048]{1,0:T(8,128)(2,1)S(1)}, bf16[192,2048]{1,0:T(8,128)(2,1)S(1)}, u32[]{:S(2)}, u32[]{:S(2)}) collective-permute-start(bf16[192,2048]{1,0:T(8,128)(2,1)S(1)} %get-tuple-element.65), channel_id=1, source_target_pairs={{0,2},{1,3},{2,0},{3,1},{4,6},{5,7},{6,4},{7,5},{8,10},{9,11},{10,... | collective-permute-start | bytes 2359304 | tf_op jit(solution)/shard_map/ppermute | solution.py:261
  460.9 41.9 %collective-permute-start.46 = (bf16[192,1536]{1,0:T(8,128)(2,1)}, bf16[192,1536]{1,0:T(8,128)(2,1)}, u32[]{:S(2)}, u32[]{:S(2)}) collective-permute-start(bf16[192,1536]{1,0:T(8,128)(2,1)} %get-tuple-element.69), channel_id=1, source_target_pairs={{0,6},{1,7},{2,4},{3,5},{4,2},{5,3},{6,0},{7,1},{8,14},{9,15},{10,... | collective-permute-start | bytes 1769480 | tf_op jit(solution)/shard_map/ppermute | solution.py:261
  467.9 45.4 %collective-permute-start.45 = (bf16[192,1536]{1,0:T(8,128)(2,1)}, bf16[192,1536]{1,0:T(8,128)(2,1)}, u32[]{:S(2)}, u32[]{:S(2)}) collective-permute-start(bf16[192,1536]{1,0:T(8,128)(2,1)} %get-tuple-element.70), channel_id=1, source_target_pairs={{0,4},{1,5},{2,6},{3,7},{4,0},{5,1},{6,2},{7,3},{8,12},{9,13},{10,... | collective-permute-start | bytes 1769480 | tf_op jit(solution)/shard_map/ppermute | solution.py:261
  473.1 40.2 %collective-permute-start.44 = (bf16[192,1536]{1,0:T(8,128)(2,1)S(1)}, bf16[192,1536]{1,0:T(8,128)(2,1)}, u32[]{:S(2)}, u32[]{:S(2)}) collective-permute-start(bf16[192,1536]{1,0:T(8,128)(2,1)S(1)} %get-tuple-element.68), channel_id=1, source_target_pairs={{0,2},{1,3},{2,0},{3,1},{4,6},{5,7},{6,4},{7,5},{8,10},{9,11},{10,... | collective-permute-start | bytes 1769480 | tf_op jit(solution)/shard_map/ppermute | solution.py:261
  518.9 31.1 %collective-permute-start.48 = (bf16[192,384]{1,0:T(8,128)(2,1)S(1)}, bf16[192,384]{1,0:T(8,128)(2,1)S(1)}, u32[]{:S(2)}, u32[]{:S(2)}) collective-permute-start(bf16[192,384]{1,0:T(8,128)(2,1)S(1)} %bitcast.380), channel_id=1, source_target_pairs={{0,16},{8,24},{16,0},{24,8},{1,17},{9,25},{17,1},{25,9},{2,18},{10... | collective-permute-start | bytes 442376 | tf_op jit(solution)/shard_map/ppermute | solution.py:243
  519.5 30.5 %collective-permute-start.47 = (bf16[192,384]{1,0:T(8,128)(2,1)S(1)}, bf16[192,384]{1,0:T(8,128)(2,1)S(1)}, u32[]{:S(2)}, u32[]{:S(2)}) collective-permute-start(bf16[192,384]{1,0:T(8,128)(2,1)S(1)} %bitcast.381), channel_id=1, source_target_pairs={{0,8},{8,16},{16,24},{24,0},{1,9},{9,17},{17,25},{25,1},{2,10},{10... | collective-permute-start | bytes 442376 | tf_op jit(solution)/shard_map/ppermute | solution.py:243
  551.9 29.6 %collective-permute-start.51 = (bf16[192,384]{1,0:T(8,128)(2,1)S(1)}, bf16[192,384]{1,0:T(8,128)(2,1)S(1)}, u32[]{:S(2)}, u32[]{:S(2)}) collective-permute-start(bf16[192,384]{1,0:T(8,128)(2,1)S(1)} %get-tuple-element.49), channel_id=1, source_target_pairs={{0,16},{8,24},{16,0},{24,8},{1,17},{9,25},{17,1},{25,9},{2,18},{10... | collective-permute-start | bytes 442376 | tf_op jit(solution)/shard_map/ppermute | solution.py:243
  554.7 26.8 %collective-permute-start.52 = (bf16[192,384]{1,0:T(8,128)(2,1)S(1)}, bf16[192,384]{1,0:T(8,128)(2,1)S(1)}, u32[]{:S(2)}, u32[]{:S(2)}) collective-permute-start(bf16[192,384]{1,0:T(8,128)(2,1)S(1)} %get-tuple-element.49), channel_id=1, source_target_pairs={{0,8},{8,16},{16,24},{24,0},{1,9},{9,17},{17,25},{25,1},{2,10},{10... | collective-permute-start | bytes 442376 | tf_op jit(solution)/shard_map/ppermute | solution.py:243
  (93 other events, 703.6 us)
Sparse Core Ops, SparseCore 0:
  11.3 30.0 all-gather.9
  43.3 49.7 all-gather.11
  95.6 59.4 all-gather.13
  156.9 52.1 all-gather.15
  438.5 36.8 all-gather.19
  492.8 99.1 all-gather.17

commit v3 on v2

--- a/solution.py
+++ b/solution.py
@@ -127,10 +127,12 @@
     )(*kv_blocks, q, bias)
 
 
-def backward_kernel(shards, seqs, rows, local_kv, groups, *refs):
+def backward_kernel(shards, seqs, rows, g, groups, *refs):
     kv_refs = refs[:shards]
-    (q_ref, bias_ref, grad_ref, exact_ref, lse_ref, grad_q_ref, near_ref, far_ref,
-     pair_ref, pair_t_ref, lse_wide, delta_wide, acc_q, acc_kv) = refs[shards:]
+    (
+        q_ref, bias_ref, grad_ref, exact_ref, lse_ref, grad_q_ref, near_ref, far_ref,
+        pair_ref, pair_t_ref, lse_wide, delta_wide, acc_q, acc_kv,
+    ) = refs[shards:]
     zk = pl.program_id(0)
     stack = groups * rows
     zeros = jnp.zeros((rows, HD), BF)
@@ -142,26 +144,23 @@
         @pl.loop(0, seqs)
         def _(zq):
             here = pl.ds(zq * rows, rows)
-            for g in range(local_kv):
-                tops, bottoms = [], []
-                for h in range(groups):
-                    cols = slice((g * groups + h) * HD, (g * groups + h + 1) * HD)
-                    grad = grad_ref[here, cols]
-                    tops.append(jnp.concatenate([q_ref[here, cols], zeros], axis=1))
-                    bottoms.append(jnp.concatenate([zeros, grad], axis=1))
-                    delta = jnp.sum(grad.astype(F32) * exact_ref[here, cols], axis=1, keepdims=True)
-                    part = slice(h * rows, (h + 1) * rows)
-                    delta_wide[zq, g, part] = jnp.broadcast_to(delta, (rows, 2 * HD))
-                    lse_wide[zq, g, part] = jnp.broadcast_to(
-                        lse_ref[here, cols][:, :1], (rows, 2 * HD)
-                    )
-                pair = jnp.concatenate(tops + bottoms, axis=0)
-                pair_ref[zq, g] = pair
-                pair_t_ref[zq, g] = pair.astype(F32).T.astype(BF)
-
-    def chunk(g, zq, first):
+            tops, bottoms = [], []
+            for h in range(groups):
+                cols = slice((g * groups + h) * HD, (g * groups + h + 1) * HD)
+                grad = grad_ref[here, cols]
+                tops.append(jnp.concatenate([q_ref[here, cols], zeros], axis=1))
+                bottoms.append(jnp.concatenate([zeros, grad], axis=1))
+                delta = jnp.sum(grad.astype(F32) * exact_ref[here, cols], axis=1, keepdims=True)
+                part = slice(h * rows, (h + 1) * rows)
+                delta_wide[zq, part] = jnp.broadcast_to(delta, (rows, 2 * HD))
+                lse_wide[zq, part] = jnp.broadcast_to(lse_ref[here, cols][:, :1], (rows, 2 * HD))
+            pair = jnp.concatenate(tops + bottoms, axis=0)
+            pair_ref[zq] = pair
+            pair_t_ref[zq] = pair.astype(F32).T.astype(BF)
+
+    def chunk(zq, first):
         keys = key_chunk(kv_refs, zk, rows, g)
-        both = dot_nt(pair_ref[zq, g], keys)
+        both = dot_nt(pair_ref[zq], keys)
         raw, products = both[:stack], both[stack:]
         if first:
             row = bias_ref[seqs + zk]
@@ -170,71 +169,63 @@
             masked = jnp.concatenate([raw[:, :rows] + mask, raw[:, rows:] + row[:, rows:]], axis=1)
         else:
             masked = raw + bias_ref[zk]
-        weights = jnp.exp(masked - lse_wide[zq, g][:, :1])
-        grads = (weights * (products - delta_wide[zq, g][:, :1])).astype(BF)
-        acc_q[zq, g] += dot(grads, keys)
-        part = dot(pair_t_ref[zq, g], jnp.concatenate([grads, weights.astype(BF)], axis=0))
+        weights = jnp.exp(masked - lse_wide[zq][:, :1])
+        grads = (weights * (products - delta_wide[zq][:, :1])).astype(BF)
+        acc_q[zq] += dot(grads, keys)
+        part = dot(pair_t_ref[zq], jnp.concatenate([grads, weights.astype(BF)], axis=0))
         if first:
-            acc_kv[g] = part
+            acc_kv[...] = part
         else:
-            acc_kv[g] += part
-
-    for g in range(local_kv):
-        chunk(g, zk, True)
+            acc_kv[...] += part
+
+    chunk(zk, True)
 
     @pl.loop(zk + 1, seqs)
     def _(zq):
-        for g in range(local_kv):
-            chunk(g, zq, False)
+        chunk(zq, False)
 
     for p in range(shards):
         target = near_ref if p < shards // 2 else far_ref
-        block = jnp.concatenate(
-            [acc_kv[g, :, p * rows : (p + 1) * rows].T for g in range(local_kv)], axis=1
-        )
-        target[p % (shards // 2)] = block.astype(BF)
+        target[p % (shards // 2)] = acc_kv[:, p * rows : (p + 1) * rows].T.astype(BF)
 
     @pl.when(zk == seqs - 1)
     def _():
         @pl.loop(0, seqs)
         def _(zq):
-            parts = []
-            for g in range(local_kv):
-                total = acc_q[zq, g]
-                for h in range(groups):
-                    parts.append(total[h * rows : (h + 1) * rows, :HD])
+            total = acc_q[zq]
+            parts = [total[h * rows : (h + 1) * rows, :HD] for h in range(groups)]
             grad_q_ref[pl.ds(zq * rows, rows), :] = jnp.concatenate(parts, axis=1)
 
 
-def flash_backward(q, kv_blocks, bias, grad, exact, lse, seqs, rows, local_kv, groups):
+def flash_backward(q, kv_blocks, bias, grad, exact, lse, seqs, rows, g, groups):
     shards = len(kv_blocks)
     q_cols = q.shape[1]
     stack = groups * rows
-    kv_cols = 2 * HD * local_kv
     kv_spec = pl.BlockSpec(kv_blocks[0].shape, lambda i: (0, 0))
     whole = pl.BlockSpec((seqs * rows, q_cols), lambda i: (0, 0))
-    out_spec = pl.BlockSpec((shards // 2, rows, kv_cols), lambda i: (0, i, 0))
-    out = jax.ShapeDtypeStruct((shards // 2, seqs * rows, kv_cols), BF)
+    grad_q_shape = (seqs * rows, groups * HD)
+    out_spec = pl.BlockSpec((shards // 2, rows, 2 * HD), lambda i: (0, i, 0))
+    out = jax.ShapeDtypeStruct((shards // 2, seqs * rows, 2 * HD), BF)
     return pl.pallas_call(
-        functools.partial(backward_kernel, shards, seqs, rows, local_kv, groups),
+        functools.partial(backward_kernel, shards, seqs, rows, g, groups),
         grid=(seqs,),
         in_specs=[kv_spec] * shards
         + [whole, pl.BlockSpec(bias.shape, lambda i: (0, 0, 0)), whole, whole, whole],
-        out_specs=[whole, out_spec, out_spec],
-        out_shape=[jax.ShapeDtypeStruct((seqs * rows, q_cols), F32), out, out],
+        out_specs=[pl.BlockSpec(grad_q_shape, lambda i: (0, 0)), out_spec, out_spec],
+        out_shape=[jax.ShapeDtypeStruct(grad_q_shape, F32), out, out],
         scratch_shapes=[
-            pltpu.VMEM((seqs, local_kv, 2 * stack, 2 * HD), BF),
-            pltpu.VMEM((seqs, local_kv, 2 * HD, 2 * stack), BF),
-            pltpu.VMEM((seqs, local_kv, stack, 2 * HD), F32),
-            pltpu.VMEM((seqs, local_kv, stack, 2 * HD), F32),
-            pltpu.VMEM((seqs, local_kv, stack, 2 * HD), F32),
-            pltpu.VMEM((local_kv, 2 * HD, shards * rows), F32),
+            pltpu.VMEM((seqs, 2 * stack, 2 * HD), BF),
+            pltpu.VMEM((seqs, 2 * HD, 2 * stack), BF),
+            pltpu.VMEM((seqs, stack, 2 * HD), F32),
+            pltpu.VMEM((seqs, stack, 2 * HD), F32),
+            pltpu.VMEM((seqs, stack, 2 * HD), F32),
+            pltpu.VMEM((2 * HD, shards * rows), F32),
         ],
-        compiler_params=pltpu.CompilerParams(vmem_limit_bytes=48 * 1024 * 1024),
+        compiler_params=pltpu.CompilerParams(vmem_limit_bytes=40 * 1024 * 1024),
         cost_estimate=pl.CostEstimate(
-            flops=20 * seqs * seqs * shards * rows * rows * local_kv * groups * HD,
-            bytes_accessed=12 * 1024 * 1024,
-            transcendentals=seqs * seqs * shards * rows * rows * local_kv * groups // 2,
+            flops=40 * seqs * seqs * shards * rows * rows * groups * HD,
+            bytes_accessed=8 * 1024 * 1024,
+            transcendentals=seqs * seqs * shards * rows * rows * groups // 2,
         ),
     )(*kv_blocks, q, bias, grad, exact, lse)
 
@@ -266,10 +257,14 @@
     return near + [hop(each, count, 1) for each in near]
 
 
-def sum_chips(parts, count):
-    total = parts(0)
-    for m in range(1, count // 2):
-        total = total + hop(parts(m).astype(BF), count, 2 * m).astype(F32)
+def send_chips(parts, count):
+    return [parts[0]] + [hop(parts[m], count, 2 * m) for m in range(1, count // 2)]
+
+
+def total_of(blocks):
+    total = blocks[0].astype(F32)
+    for each in blocks[1:]:
+        total = total + each.astype(F32)
     return total
 
 
@@ -277,29 +272,25 @@
     return lax.dynamic_index_in_dim(array, index, axis, keepdims=False)
 
 
-def split_columns(lhs, shard, count):
-    tokens, width = lhs.shape
-    cut = lhs.reshape(tokens, count // 2, 2, width // count)
+def pair_halves(product, shard, count):
+    width, cols = product.shape
+    cut = product.reshape(count // 2, 2, width // count, cols)
     core = shard % 2
-    far = take(cut, 1 - core, 2).reshape(tokens, width // 2)
-    near = take(cut, core, 2).reshape(tokens, width // 2)
-    return far, near
-
-
-def sum_product(columns, rhs, shard, count):
-    far, near = columns
-    return sum_parts(dot_tn(far, rhs).astype(BF), dot_tn(near, rhs).astype(BF), shard, count)
-
-
-def sum_parts(far, near, shard, count):
-    there = hop(far, count, 1).reshape(count // 2, -1, far.shape[1])
-    here = near.reshape(count // 2, -1, far.shape[1])
+    return take(cut, core, 1), hop(take(cut, 1 - core, 1), count, 1)
+
+
+def pair_sums(halves, shard):
+    here, there = halves
     chip = shard // 2
-
-    def parts(m):
-        return take(here, chip ^ m, 0).astype(F32) + take(there, chip ^ m, 0).astype(F32)
-
-    return sum_chips(parts, count)
+    sums = []
+    for m in range(here.shape[0]):
+        each = take(here, chip ^ m, 0).astype(F32) + take(there, chip ^ m, 0).astype(F32)
+        sums.append(each if m == 0 else each.astype(BF))
+    return sums
+
+
+def sum_rows(product, shard, count):
+    return total_of(send_chips(pair_sums(pair_halves(product, shard, count), shard), count))
 
 
 def spread_scalar(value, core, rows):
@@ -309,6 +300,10 @@
     none = jnp.zeros_like(pair)
     row = jnp.where(core == 0, jnp.concatenate([pair, none]), jnp.concatenate([none, pair]))
     return jnp.broadcast_to(row[None, :], (rows, 4))
+
+
+def after(values, *others):
+    return lax.optimization_barrier((values, others))[0]
 
 
 def root(values):
@@ -356,25 +351,26 @@
 
     gain_one = gain_attn.astype(F32)[:, None]
     gain_two = gain_ffn.astype(F32)[:, None]
-    query_scaled = (w_query.astype(F32) * gain_one).astype(BF)
-    keyval_scaled = (w_keyval.astype(F32) * gain_one).astype(BF)
     heads_shard = jnp.concatenate(
         [
-            lax.dynamic_slice_in_dim(query_scaled, z * q_cols, q_cols, 1),
-            lax.dynamic_slice_in_dim(keyval_scaled, z * kv_cols, kv_cols, 1),
+            lax.dynamic_slice_in_dim(w_query, z * q_cols, q_cols, 1),
+            lax.dynamic_slice_in_dim(w_keyval, z * kv_cols, kv_cols, 1),
         ],
         axis=1,
     )
+    heads_shard = (heads_shard.astype(F32) * gain_one).astype(BF)
     heads_full = lax.all_gather(heads_shard, "fsdp", axis=0, tiled=True)
+    token_blocks = send_out([tokens] * seqs, seqs)
+    late_gate_up, late_down, late_valid = after((w_gate_up, w_down, valid), token_blocks[1])
     out_full = lax.all_gather(w_out, "fsdp", axis=1, tiled=True)
     router_full = lax.all_gather(
         (w_router.astype(F32) * gain_two).astype(BF), "fsdp", axis=0, tiled=True
     )
-    own_expert = take(w_gate_up, expert, 0)
+    own_expert = take(late_gate_up, expert, 0)
     gate_shard = lax.dynamic_slice_in_dim(own_expert, fraction * piece, piece, 1)
     up_shard = lax.dynamic_slice_in_dim(own_expert, units + fraction * piece, piece, 1)
     down_shard = lax.dynamic_slice_in_dim(
-        take(w_down, expert, 0), fraction * piece, piece, 0
+        take(late_down, expert, 0), fraction * piece, piece, 0
     ).T
     expert_shard = jnp.concatenate(
         [
@@ -387,20 +383,13 @@
     expert_full = lax.all_gather(expert_shard, "fsdp", axis=0, tiled=True)
     gate_up_full = expert_full[:, : 2 * piece]
     down_full = expert_full[:, 2 * piece :]
-    attn_full = lax.all_gather(
-        jnp.concatenate([query_scaled, keyval_scaled], axis=1), "fsdp", axis=0, tiled=True
-    )
-
-    valid_low = valid.astype(BF).reshape(1, rows)
-    token_blocks = send_out([tokens] * seqs, seqs)
+    valid_low = late_valid.astype(BF).reshape(1, rows)
     valid_local = from_relative(send_out([valid_low] * seqs, seqs), z)
     projected = []
     for block in token_blocks:
         projected.append(dot(block, heads_full) * root(block.astype(F32)))
     projected = from_relative([each.astype(BF) for each in projected], z)
     projected = projected.reshape(local_rows, q_cols + kv_cols)
-    tokens_local = from_relative(token_blocks, z).reshape(local_rows, width)
-    factor_local = root(tokens_local.astype(F32))
     head_queries = projected[:, :q_cols] * jnp.asarray(scale, BF)
 
     valid_rows_kv = local_rows // kv_cols
@@ -433,6 +422,11 @@
     )
     attended = lax.all_to_all(attended_low, "seq", split_axis=0, concat_axis=1, tiled=True)
 
+    late_query, late_keyval = after((w_query, w_keyval), attended)
+    attn_shard = jnp.concatenate([late_query, late_keyval], axis=1)
+    attn_full = lax.all_gather(
+        (attn_shard.astype(F32) * gain_one).astype(BF), "fsdp", axis=0, tiled=True
+    )
     inputs = tokens.astype(F32)
     residual = inputs + dot(attended, out_full)
     factor_two = root(residual)
@@ -477,70 +471,90 @@
     )
     sent_grads = dot_tn(placed_pairs, weighted).astype(BF).reshape(seqs, CAP, width)
     grad_expert_out = jnp.concatenate(send_out([sent_grads[s] for s in range(seqs)], seqs))
+    grad_expert_out = after(grad_expert_out, attn_full)
     grad_hidden = dot(grad_expert_out, down_full)
     grad_gate = grad_hidden * up_part * sigmoid_gate * (1.0 + gate_part * (1.0 - sigmoid_gate))
     grad_up = grad_hidden * gate_part * sigmoid_gate
     grad_gate_up_rows = jnp.concatenate([grad_gate, grad_up], axis=-1).astype(BF)
     grad_rows = dot_nt(grad_gate_up_rows, gate_up_full).astype(BF).reshape(seqs, CAP, width)
     grad_returned = jnp.concatenate(send_back([grad_rows[s] for s in range(seqs)], seqs))
-    grad_down_shard = sum_product(
-        split_columns(grad_expert_out, shard, shards), hidden, shard, shards
-    )
-    grad_down = lax.all_gather(grad_down_shard.astype(BF), "seq", axis=0, tiled=False)
-    grad_gate_up_shard = sum_product(
-        split_columns(expert_rows, shard, shards), grad_gate_up_rows, shard, shards
-    )
-    grad_gate_up = lax.all_gather(grad_gate_up_shard.astype(BF), "seq", axis=0, tiled=False)
+    held_out, held_hidden = after((grad_expert_out, hidden), grad_rows)
+    grad_down_sums = pair_sums(
+        pair_halves(dot_tn(held_out, held_hidden).astype(BF), shard, shards), shard
+    )
+    held_rows, held_gate_up = after((expert_rows, grad_gate_up_rows), grad_rows)
+    grad_gate_up_halves = pair_halves(
+        dot_tn(held_rows, held_gate_up).astype(BF), shard, shards
+    )
+    grad_returned = after(grad_returned, grad_down_sums)
+    late_blocks = after(token_blocks, sent_grads)
+    tokens_local = from_relative(late_blocks, z).reshape(local_rows, width)
+    factor_local = root(tokens_local.astype(F32))
 
     grad_normed_two = dot(dispatch, grad_returned) + dot_nt(grad_logits, router_full)
     grad_residual = grad_mixed + root_back(residual, factor_two, grad_normed_two)
     grad_branch = grad_residual.astype(BF)
     grad_attended = dot_nt(grad_branch, out_full).astype(BF)
     head_grad = lax.all_to_all(grad_attended, "seq", split_axis=1, concat_axis=0, tiled=True)
-
-    grad_out_part = sum_product(split_columns(grad_branch, shard, shards), attended, shard, shards)
+    grad_down_shard = total_of(send_chips(grad_down_sums, shards)).astype(BF)
+    grad_down = lax.all_gather(grad_down_shard, "seq", axis=0, tiled=False)
+    grad_gate_up_sums = pair_sums(after(grad_gate_up_halves, grad_attended), shard)
+    grad_gate_up_blocks = send_chips(grad_gate_up_sums, shards)
+
+    grad_out_halves = pair_halves(dot_tn(grad_branch, attended).astype(BF), shard, shards)
+
+    grad_q, near, far = [], [], []
+    held = after(head_grad, grad_down_shard, grad_gate_up_sums, grad_out_halves)
+    for g in range(local_kv):
+        part_q, near_kv, far_kv = flash_backward(
+            head_queries, kv_blocks, bias, held, exact, lse, seqs, rows, g, groups
+        )
+        grad_q.append(part_q * scale)
+        near.append(near_kv)
+        far.append(far_kv)
+        if g == 0:
+            grad_gate_up_shard = total_of(after(grad_gate_up_blocks, part_q)).astype(BF)
+            grad_out_sums = pair_sums(after(grad_out_halves, part_q), shard)
+            held = after(head_grad, grad_gate_up_shard, grad_out_sums)
+    grad_gate_up = lax.all_gather(grad_gate_up_shard, "seq", axis=0, tiled=False)
+    near = jnp.concatenate(near, axis=2)
+    there = hop(jnp.concatenate(far, axis=2), shards, 1)
+    pairs = [near[m].astype(F32) + there[m].astype(F32) for m in range(shards // 2)]
+    pairs = [pairs[0]] + [each.astype(BF) for each in pairs[1:]]
+    grad_q = jnp.concatenate(grad_q, axis=1)
+    grad_kv = total_of(send_chips(pairs, shards))
+    token_grad_q = lax.all_to_all(
+        grad_q.astype(BF), "seq", split_axis=0, concat_axis=1, tiled=True
+    )
+    token_grad_kv = lax.all_to_all(
+        grad_kv.astype(BF), "seq", split_axis=0, concat_axis=1, tiled=True
+    )
+    grad_out_part = total_of(after(send_chips(grad_out_sums, shards), pairs))
     cut = grad_out_part.astype(BF).reshape(part, seqs, q_cols)
     grad_out_own = jnp.zeros((part, q_cols), F32)
-    for each in send_out([take(cut, (z + s) % seqs, 1) for s in range(seqs)], seqs):
+    out_parts = send_out([take(cut, (z + s) % seqs, 1) for s in range(seqs)], seqs)
+    for each in after(out_parts, grad_kv):
         grad_out_own = grad_out_own + each.astype(F32)
     grad_out = from_relative(send_out([grad_out_own.astype(BF)] * seqs, seqs), z)
     grad_out = grad_out.transpose(0, 2, 1).reshape(HEADS * HD, part).astype(F32)
-
-    grad_q, near_kv, far_kv = flash_backward(
-        head_queries, kv_blocks, bias, head_grad, exact, lse, seqs, rows, local_kv, groups
-    )
-    grad_q = grad_q * scale
-    there_kv = hop(far_kv, shards, 1)
-    grad_kv = sum_chips(lambda m: near_kv[m].astype(F32) + there_kv[m].astype(F32), shards)
-    token_grad_q = lax.all_to_all(
-        grad_q.astype(BF), "seq", split_axis=0, concat_axis=1, tiled=True
-    )
-    token_grad_kv = lax.all_to_all(
-        grad_kv.astype(BF), "seq", split_axis=0, concat_axis=1, tiled=True
-    )
     grad_normed = dot_nt(token_grad_q, attn_full[:, : HEADS * HD]) + dot_nt(
         token_grad_kv, attn_full[:, HEADS * HD :]
     )
     grad_tokens = grad_residual + root_back(inputs, root(inputs), grad_normed)
 
-    token_columns = split_columns(tokens_local, shard, shards)
-    normed_columns = split_columns(normed_two, shard, shards)
     query_rhs = (grad_q * factor_local).astype(BF)
-    marks = spread_scalar(squares, shard % 2, width // 2)
-    grad_query_part = sum_parts(
-        *[
-            jnp.concatenate(
-                [dot_tn(columns, query_rhs).astype(BF), dot_tn(others, grad_logits).astype(BF), marks],
-                axis=1,
-            )
-            for columns, others in zip(token_columns, normed_columns)
+    marks = spread_scalar(squares, shard % 2, width)
+    query_product = jnp.concatenate(
+        [
+            dot_tn(tokens_local, query_rhs).astype(BF),
+            dot_tn(normed_two, grad_logits).astype(BF),
+            marks,
         ],
-        shard,
-        shards,
-    )
-    grad_keyval_part = sum_product(
-        token_columns, (grad_kv * factor_local).astype(BF), shard, shards
-    )
+        axis=1,
+    )
+    grad_query_part = sum_rows(after(query_product, pairs), shard, shards)
+    keyval_rhs = (grad_kv * factor_local).astype(BF)
+    grad_keyval_part = sum_rows(dot_tn(tokens_local, keyval_rhs).astype(BF), shard, shards)
     base_cols = q_cols + experts
     plane_squares = jnp.sum(grad_query_part[:, base_cols:], axis=1, keepdims=True)
     plane_high = plane_squares.astype(BF)

time: 617 us -> 551 us (0.89)
  waiting for transfers between devices: 247 us -> 186 us
  blocking collectives: 8.92 us -> 26 us
  local copies, waits for them, and re-layouts: 72.8 us -> 59.2 us
  matrix products: 63.4 us -> 53.1 us
  other arithmetic: 71.3 us -> 65 us
    ppermute x31, waiting for transfers between devices: 73.6 us -> 29.9 us  [hop(): return lax.ppermute(block, 'fsdp', [(i, i ^ mask) for i in range(count)])]
    concatenate x17 -> x4, local copies, waits for them, and re-layouts: 19.4 us -> 1.23 us  [the longest x1 0.83 us: local(): near = jnp.concatenate(near, axis=2)]
    ppermute x30, waiting for transfers between devices: 144 us -> 127 us  [shift(): lax.ppermute(block, 'seq', [(i, (i + step) % count) for i in range(count)])]
    all_to_all x0 -> x1, blocking collectives: none -> 16 us  [local(): lax.all_to_all(attended_low, 'seq', split_axis=0, concat_axis=1, tiled=True)]
    all_to_all x1, waiting for transfers between devices: 3.79 us -> 16.2 us  [local(): lax.all_to_all(grad_q.astype(BF), 'seq', split_axis=0, concat_axis=1, til...]
    dot_general x14 -> x8, matrix products: 21.9 us -> 10.6 us  [dot_tn(): lax.dot_general(a, b, (((0,), (0,)), ((), ())), preferred_element_type=F32)]
    unnamed x180 -> x228, local copies, waits for them, and re-layouts: 20.4 us -> 31.3 us
    ppermute x30, starting transfers between devices: 41.3 us -> 51.3 us  [shift(): lax.ppermute(block, 'seq', [(i, (i + step) % count) for i in range(count)])]
  transfers between devices with their start and end apart: 71 -> 70, of which waited for: 30 -> 26; matrix products, arithmetic and copies ran while one was open for 31% -> 24% of each run, Pallas kernels for 7% -> 8%
where the time goes in v3:
time: 551 us; the launch traced here: 541 us
  waiting for transfers between devices  186 us (34%)
  starting transfers between devices  86.9 us (16%)
  other arithmetic  65 us (12%)
  local copies, waits for them, and re-layouts  59.2 us (11%)
  matrix products  53.1 us (10%)
  Pallas kernels  44.1 us (8%)
  blocking collectives  26 us (5%)
  between operations  20.4 us (4%)
    ppermute x30, waiting for transfers between devices, shift(): lax.ppermute(block, 'seq', [(i, (i + step) % count) for i in range(count)])  127 us
    ppermute x30, starting transfers between devices, shift(): lax.ppermute(block, 'seq', [(i, (i + step) % count) for i in range(count)])  51.3 us
    unnamed x228, local copies, waits for them, and re-layouts  31.3 us
    ppermute x31, waiting for transfers between devices, hop(): return lax.ppermute(block, 'fsdp', [(i, i ^ mask) for i in range(count)])  29.9 us
    pallas_call x2, Pallas kernels, flash_backward(): pl.pallas_call(functools.partial(backward_kernel, shards, seqs, rows, g,...  25.9 us
    ppermute x31, starting transfers between devices, hop(): return lax.ppermute(block, 'fsdp', [(i, i ^ mask) for i in range(count)])  23.4 us
    dot_general x6, matrix products, dot_nt(): lax.dot_general(a, b, (((1,), (1,)), ((), ())), preferred_element_type=F32)  21.5 us
    dot_general x10, matrix products, dot(): return jnp.dot(a, b, preferred_element_type=F32)  21 us
  transfers between devices with their start and end apart: 70, of which 26 were waited for; matrix products, arithmetic and copies ran while one was open for 24% of the time, Pallas kernels for 8%

profile of v3, /device:TPU:0, one launch (start us, length us, event | category | flops | bytes accessed | tf_op | source)
XLA Modules:
  0.0 540.9 jit_solution(10569363861328469985)
XLA Ops:
  11.5 3.1 collective-permute-start.2
  14.6 11.1 %collective-permute-done.2 = bf16[128,1536]{1,0:T(8,128)(2,1)S(1)} collective-permute-done((bf16[128,1536]{1,0:T(8,128)(2,1)S(1)}, bf16[128,1536]{1,0:T(8,128)(2,1)S(1)}, u32[]{:S(2)}, u32[]{:S(2)}) %collective-permute-start.2) | collective-permute-done | bytes 393248 | tf_op jit(solution)/shard_map/ppermute | solution.py:234
  35.6 11.5 %collective-permute-done.1 = bf16[128,1536]{1,0:T(8,128)(2,1)S(1)} collective-permute-done((bf16[128,1536]{1,0:T(8,128)(2,1)S(1)}, bf16[128,1536]{1,0:T(8,128)(2,1)S(1)}, u32[]{:S(2)}, u32[]{:S(2)}) %collective-permute-start.1) | collective-permute-done | bytes 393248 | tf_op jit(solution)/shard_map/ppermute | solution.py:234
  47.6 7.8 %collective-permute-done.4 = bf16[1,128]{1,0:T(2,128)(2,1)S(1)} collective-permute-done((bf16[1,128]{1,0:T(2,128)(2,1)S(1)}, bf16[1,128]{1,0:T(2,128)(2,1)S(1)}, u32[]{:S(2)}, u32[]{:S(2)}) %collective-permute-start.4) | collective-permute-done | bytes 288 | tf_op jit(solution)/shard_map/ppermute | solution.py:234
  63.4 9.4 %collective-permute-done.8.refs_3_ = bf16[528,256]{1,0:T(8,128)(2,1)S(1)} collective-permute-done((bf16[528,256]{1,0:T(8,128)(2,1)S(1)}, bf16[528,256]{1,0:T(8,128)(2,1)S(1)}, u32[]{:S(2)}, u32[]{:S(2)}) %collective-permute-start.8) | collective-permute-done | bytes 270368 | tf_op jit(solution)/shard_map/ppermute | solution.py:252
  72.8 7.6 %collective-permute-done.7.refs_2_ = bf16[528,256]{1,0:T(8,128)(2,1)S(1)} collective-permute-done((bf16[528,256]{1,0:T(8,128)(2,1)S(1)}, bf16[528,256]{1,0:T(8,128)(2,1)S(1)}, u32[]{:S(2)}, u32[]{:S(2)}) %collective-permute-start.7) | collective-permute-done | bytes 270368 | tf_op jit(solution)/shard_map/ppermute | solution.py:252
  87.2 18.3 %shard_map.221 = (bf16[512,384]{1,0:T(8,128)(2,1)S(1)}, f32[512,384]{1,0:T(8,128)S(1)}, f32[512,384]{1,0:T(8,128)S(1)}) custom-call(bf16[528,256]{1,0:T(8,128)(2,1)S(1)} %maximum_maximum_fusion.1.refs_0_, bf16[528,256]{1,0:T(8,128)(2,1)S(1)} %collective-permute-done.6.refs_1_, bf16[528,256]{1,0:T(8,128)(2,1)S(1)} %collective-permute-done.7.refs_2_, ...), custom_call_target="tpu_custom_call" | custom-call | flops 6442450944 | bytes 8388608 | tf_op jit(solution)/shard_map/pallas_call | solution.py:111
  107.6 16.0 %all_to_all.73 = bf16[4,128,384]{1,2,0:T(8,128)(2,1)} all-to-all(bf16[4,128,384]{1,2,0:T(8,128)(2,1)S(1)} %copy.213), channel_id=1, replica_groups=mesh['seq'=4,'fsdp'=8] {'seq'}, dimensions={0} | all-to-all | bytes 786432 | tf_op jit(solution)/shard_map/all_to_all | solution.py:423
  126.2 10.0 %all-gather.2 = bf16[8,192,4]{1,2,0:T(4,128)(2,1)S(1)} all-gather(bf16[1,192,4]{1,2,0:T(4,128)(2,1)S(1)} %copy.216), channel_id=1, replica_groups=mesh['seq'=4,'fsdp'=8] {'fsdp'}, dimensions={0}, use_global_device_ids=true | all-gather | bytes 13824 | tf_op jit(solution)/shard_map/all_gather | solution.py:366
  139.1 4.3 multiply_reduce_fusion.7
  147.6 7.1 %collective-permute-done.15 = bf16[96,1536]{1,0:T(8,128)(2,1)S(1)} collective-permute-done((bf16[96,1536]{1,0:T(8,128)(2,1)}, bf16[96,1536]{1,0:T(8,128)(2,1)S(1)}, u32[]{:S(2)}, u32[]{:S(2)}) %collective-permute-start.15) | collective-permute-done | bytes 294944 | tf_op jit(solution)/shard_map/ppermute | solution.py:234
  154.7 18.4 %collective-permute-done.14 = bf16[96,1536]{1,0:T(8,128)(2,1)} collective-permute-done((bf16[96,1536]{1,0:T(8,128)(2,1)}, bf16[96,1536]{1,0:T(8,128)(2,1)}, u32[]{:S(2)}, u32[]{:S(2)}) %collective-permute-start.14) | collective-permute-done | bytes 294944 | tf_op jit(solution)/shard_map/ppermute | solution.py:234
  173.0 5.7 %fusion.3 = f32[384,2048]{1,0:T(8,128)S(1)} fusion(bf16[1536,3072]{1,0:T(8,128)(2,1)} %all-gather.14.cloned.1.call-done, bf16[96,1536]{1,0:T(8,128)(2,1)S(1)} %collective-permute-done.15, bf16[96,1536]{1,0:T(8,128)(2,1)} %collective-permute-done.14, bf16[96,1536]{1,0:T(8,128)(2,1)} %collective-permute-done.13, bf16[96,1536]{1,0:T(8,128)(2,1)S(1)} %get-tuple-element.184), kind=kOutput, calls=%fused_computation.7 | convolution fusion | flops 2420637696 | bytes 10616832 | tf_op jit(solution)/shard_map/dot_general | solution.py:21
  180.6 3.9 convolution_convert_fusion.6
  189.6 6.9 %collective-permute-done.18 = bf16[96,1536]{1,0:T(8,128)(2,1)S(1)} collective-permute-done((bf16[96,1536]{1,0:T(8,128)(2,1)S(1)}, bf16[96,1536]{1,0:T(8,128)(2,1)S(1)}, u32[]{:S(2)}, u32[]{:S(2)}) %collective-permute-start.18) | collective-permute-done | bytes 294944 | tf_op jit(solution)/shard_map/ppermute | solution.py:234
  196.5 11.3 %collective-permute-done.17 = bf16[96,1536]{1,0:T(8,128)(2,1)S(1)} collective-permute-done((bf16[96,1536]{1,0:T(8,128)(2,1)S(1)}, bf16[96,1536]{1,0:T(8,128)(2,1)S(1)}, u32[]{:S(2)}, u32[]{:S(2)}) %collective-permute-start.17) | collective-permute-done | bytes 294944 | tf_op jit(solution)/shard_map/ppermute | solution.py:234
  211.4 7.2 %collective-permute-start.21 = (bf16[96,1536]{1,0:T(8,128)(2,1)S(1)}, bf16[96,1536]{1,0:T(8,128)(2,1)S(1)}, u32[]{:S(2)}, u32[]{:S(2)}) collective-permute-start(bf16[96,1536]{1,0:T(8,128)(2,1)S(1)} %get-tuple-element.177), channel_id=1, source_target_pairs={{0,24},{8,0},{16,8},{24,16},{1,25},{9,1},{17,9},{25,17},{2,26},{10... | collective-permute-start | bytes 884744 | tf_op jit(solution)/shard_map/ppermute | solution.py:234
  221.4 4.7 collective-permute-done.21
  226.1 17.7 %collective-permute-done.20 = bf16[96,1536]{1,0:T(8,128)(2,1)S(1)} collective-permute-done((bf16[96,1536]{1,0:T(8,128)(2,1)S(1)}, bf16[96,1536]{1,0:T(8,128)(2,1)S(1)}, u32[]{:S(2)}, u32[]{:S(2)}) %collective-permute-start.20) | collective-permute-done | bytes 294944 | tf_op jit(solution)/shard_map/ppermute | solution.py:234
  244.8 4.9 multiply_convert_fusion.2
  249.8 5.6 %fusion.9 = bf16[384,1536]{1,0:T(8,128)(2,1)S(1)} fusion(bf16[1536,3072]{1,0:T(8,128)(2,1)} %all-gather.14.cloned.1.call-done, bf16[384,1024]{1,0:T(8,128)(2,1)S(1)} %get-tuple-element.155, bf16[384,1024]{1,0:T(8,128)(2,1)S(1)} %get-tuple-element.154), kind=kOutput, calls=%fused_computation.20 | convolution fusion | flops 2419654656 | bytes 9043968 | tf_op jit(solution)/shard_map/dot_general | solution.py:25
  259.3 3.2 collective-permute-start.22
  262.5 3.7 convolution_convert_fusion
  270.3 3.3 dynamic-slice_bitcast_fusion
  273.6 7.7 %collective-permute-done.23 = bf16[96,1536]{1,0:T(8,128)(2,1)S(1)} collective-permute-done((bf16[96,1536]{1,0:T(8,128)(2,1)S(1)}, bf16[96,1536]{1,0:T(8,128)(2,1)S(1)}, u32[]{:S(2)}, u32[]{:S(2)}) %collective-permute-start.23) | collective-permute-done | bytes 294944 | tf_op jit(solution)/shard_map/ppermute | solution.py:234
  282.4 3.3 collective-permute-done.28
  301.7 3.1 convolution_convert_fusion.8
  305.6 4.6 all-to-all-start.1
  310.7 5.7 %fusion.40 = (bf16[192,2048]{1,0:T(8,128)(2,1)}, bf16[192,2048]{1,0:T(8,128)(2,1)}, bf16[192,2048]{1,0:T(8,128)(2,1)}, f32[192,2048]{1,0:T(8,128)}) fusion(bf16[4,192,2048]{2,1,0:T(8,128)(2,1)} %collective-permute-done.29, s32[]{:T(128)S(6)} %select_n.238, bf16[4,192,2048]{2,1,0:T(8,128)(2,1)} %get-tuple-element.70, s32[]{:T(128)S(6)} %select_n.236, ...), kind=kLoop, calls=%fused_computation.89 | loop fusion | flops 5898240 | bytes 10223632 | tf_op jit(solution)/shard_map/convert_element_type | solution.py:288
  319.9 12.8 %all-to-all-done.1 = bf16[128,4,384]{2,0,1:T(8,128)(2,1)S(1)} async-done(((bf16[128,4,384]{2,0,1:T(8,128)(2,1)}), bf16[128,4,384]{2,0,1:T(8,128)(2,1)S(1)}, u32[]{:S(2)}, u32[]{:S(2)}) %all-to-all-start.1) | async-done | bytes 393248 | tf_op jit(solution)/shard_map/all_to_all | solution.py:498
  340.7 12.9 %shard_map.222 = (f32[512,192]{1,0:T(8,128)S(1)}, bf16[4,512,128]{2,1,0:T(8,128)(2,1)S(1)}, bf16[4,512,128]{2,1,0:T(8,128)(2,1)S(1)}) custom-call(bf16[528,256]{1,0:T(8,128)(2,1)S(1)} %maximum_maximum_fusion.1.refs_0_, bf16[528,256]{1,0:T(8,128)(2,1)S(1)} %copy-done.10, bf16[528,256]{1,0:T(8,128)(2,1)S(1)} %copy-done.7, ...), custom_call_target="tpu_custom_call" | custom-call | flops 16106127360 | bytes 8388608 | tf_op jit(solution)/shard_map/pallas_call | solution.py:209
  353.6 3.6 convert_bitcast_fusion
  357.2 3.0 add_convert_fusion
  360.4 4.4 fusion.52
  368.5 13.0 %shard_map.223 = (f32[512,192]{1,0:T(8,128)S(1)}, bf16[4,512,128]{2,1,0:T(8,128)(2,1)S(1)}, bf16[4,512,128]{2,1,0:T(8,128)(2,1)S(1)}) custom-call(bf16[528,256]{1,0:T(8,128)(2,1)S(1)} %copy-done.3, bf16[528,256]{1,0:T(8,128)(2,1)S(1)} %copy-done.11, bf16[528,256]{1,0:T(8,128)(2,1)S(1)} %copy-done.8, bf16[528,256]{1,0:T(8,128)(2,1)S(1)} %copy-done.5, ...), custom_call_target="tpu_custom_call" | custom-call | flops 16106127360 | bytes 8388608 | tf_op jit(solution)/shard_map/pallas_call | solution.py:209
  383.7 3.8 all-to-all-start.2
  392.2 16.2 %all-to-all-done.2 = bf16[4,128,384]{1,2,0:T(8,128)(2,1)S(1)} async-done(((bf16[4,128,384]{1,2,0:T(8,128)(2,1)}), bf16[4,128,384]{1,2,0:T(8,128)(2,1)S(1)}, u32[]{:S(2)}, u32[]{:S(2)}) %all-to-all-start.2) | async-done | bytes 393248 | tf_op jit(solution)/shard_map/all_to_all | solution.py:526
  408.4 5.0 fusion.5
  425.3 3.4 collective-permute-start.56
  431.6 3.8 copy.223
  441.5 3.5 collective-permute-done.57
  453.2 3.4 all-to-all-start.3
  469.9 3.5 fusion.35
  486.0 5.0 collective-permute-start.49
  491.8 3.2 collective-permute-start.39
  495.6 3.8 collective-permute-start.50
  499.3 17.3 %collective-permute-done.50 = bf16[192,256]{1,0:T(8,128)(2,1)S(1)} collective-permute-done((bf16[192,256]{1,0:T(8,128)(2,1)S(1)}, bf16[192,256]{1,0:T(8,128)(2,1)S(1)}, u32[]{:S(2)}, u32[]{:S(2)}) %collective-permute-start.50) | collective-permute-done | bytes 98336 | tf_op jit(solution)/shard_map/ppermute | solution.py:234
  524.5 7.4 %convert_multiply_fusion = (f32[4,192,2048]{2,1,0:T(8,128)}, f32[192]{0:T(256)S(1)}) fusion(bf16[4,192,2048]{2,1,0:T(8,128)(2,1)} %bitcast.343, f32[192]{0:T(256)S(1)} %copy-done.77, bf16[4,192,2048]{2,1,0:T(8,128)(2,1)} %param.25), kind=kLoop, calls=%fused_computation | loop fusion | flops 7864128 | bytes 12584448 | tf_op jit(solution)/shard_map/mul | solution.py:609
  (504 shorter events, 164.6 us)
Async XLA Ops:
  7.2 48.3 %all-gather.10.cloned.1.call-start = ((), (), s32[]{:S(2)}) async-start(), calls=%async_computation.4 | async-start | bytes 2211840 | tf_op jit(solution)/shard_map/all_gather | solution.py:362
  10.7 128.4 %all-gather.12.cloned.1.call-start = ((), (), s32[]{:S(2)}) async-start(), calls=%async_computation.5 | async-start | bytes 5308416 | tf_op jit(solution)/shard_map/all_gather | solution.py:365
  11.5 161.5 %all-gather.14.cloned.1.call-start = ((), (), s32[]{:S(2)}) async-start(), calls=%async_computation.6 | async-start | bytes 10616832 | tf_op jit(solution)/shard_map/all_gather | solution.py:383
  28.3 216.5 %all-gather.16.cloned.1.call-start = ((), (), s32[]{:S(2)}) async-start(), calls=%async_computation.7 | async-start | bytes 8847360 | tf_op jit(solution)/shard_map/all_gather | solution.py:427
  28.4 18.7 %collective-permute-start.1 = (bf16[128,1536]{1,0:T(8,128)(2,1)S(1)}, bf16[128,1536]{1,0:T(8,128)(2,1)S(1)}, u32[]{:S(2)}, u32[]{:S(2)}) collective-permute-start(bf16[128,1536]{1,0:T(8,128)(2,1)S(1)} %copy-done.32), channel_id=1, source_target_pairs={{0,16},{8,24},{16,0},{24,8},{1,17},{9,25},{17,1},{25,9},{2,18},{10... | collective-permute-start | bytes 1179656 | tf_op jit(solution)/shard_map/ppermute | solution.py:234
  29.2 18.1 %collective-permute-start = (bf16[128,1536]{1,0:T(8,128)(2,1)S(1)}, bf16[128,1536]{1,0:T(8,128)(2,1)S(1)}, u32[]{:S(2)}, u32[]{:S(2)}) collective-permute-start(bf16[128,1536]{1,0:T(8,128)(2,1)S(1)} %copy-done.32), channel_id=1, source_target_pairs={{0,24},{8,0},{16,8},{24,16},{1,25},{9,1},{17,9},{25,17},{2,26},{10... | collective-permute-start | bytes 1179656 | tf_op jit(solution)/shard_map/ppermute | solution.py:234
  30.8 24.6 %collective-permute-start.5 = (bf16[1,128]{1,0:T(2,128)(2,1)S(1)}, bf16[1,128]{1,0:T(2,128)(2,1)S(1)}, u32[]{:S(2)}, u32[]{:S(2)}) collective-permute-start(bf16[1,128]{1,0:T(2,128)(2,1)S(1)} %convert_bitcast_fusion.4), channel_id=1, source_target_pairs={{0,8},{8,16},{16,24},{24,0},{1,9},{9,17},{17,25},{25,1},{2,10},{10... | collective-permute-start | bytes 776 | tf_op jit(solution)/shard_map/ppermute | solution.py:234
  31.5 23.9 %collective-permute-start.4 = (bf16[1,128]{1,0:T(2,128)(2,1)S(1)}, bf16[1,128]{1,0:T(2,128)(2,1)S(1)}, u32[]{:S(2)}, u32[]{:S(2)}) collective-permute-start(bf16[1,128]{1,0:T(2,128)(2,1)S(1)} %convert_bitcast_fusion.4), channel_id=1, source_target_pairs={{0,16},{8,24},{16,0},{24,8},{1,17},{9,25},{17,1},{25,9},{2,18},{10... | collective-permute-start | bytes 776 | tf_op jit(solution)/shard_map/ppermute | solution.py:234
  62.2 18.2 %collective-permute-start.7 = (bf16[528,256]{1,0:T(8,128)(2,1)S(1)}, bf16[528,256]{1,0:T(8,128)(2,1)S(1)}, u32[]{:S(2)}, u32[]{:S(2)}) collective-permute-start(bf16[528,256]{1,0:T(8,128)(2,1)S(1)} %maximum_maximum_fusion.1.refs_0_), channel_id=1, source_target_pairs={{0,4},{1,5},{2,6},{3,7},{4,0},{5,1},{6,2},{7,3},{8,12},{9,13},{10,... | collective-permute-start | bytes 811016 | tf_op jit(solution)/shard_map/ppermute | solution.py:252
  62.7 20.6 %collective-permute-start.6 = (bf16[528,256]{1,0:T(8,128)(2,1)S(1)}, bf16[528,256]{1,0:T(8,128)(2,1)S(1)}, u32[]{:S(2)}, u32[]{:S(2)}) collective-permute-start(bf16[528,256]{1,0:T(8,128)(2,1)S(1)} %maximum_maximum_fusion.1.refs_0_), channel_id=1, source_target_pairs={{0,2},{1,3},{2,0},{3,1},{4,6},{5,7},{6,4},{7,5},{8,10},{9,11},{10,... | collective-permute-start | bytes 811016 | tf_op jit(solution)/shard_map/ppermute | solution.py:252
  63.4 21.1 %collective-permute-start.9 = (bf16[528,256]{1,0:T(8,128)(2,1)S(1)}, bf16[528,256]{1,0:T(8,128)(2,1)S(1)}, u32[]{:S(2)}, u32[]{:S(2)}) collective-permute-start(bf16[528,256]{1,0:T(8,128)(2,1)S(1)} %maximum_maximum_fusion.1.refs_0_), channel_id=1, source_target_pairs={{0,1},{1,0},{2,3},{3,2},{4,5},{5,4},{6,7},{7,6},{8,9},{9,8},{10,11... | collective-permute-start | bytes 811016 | tf_op jit(solution)/shard_map/ppermute | solution.py:252
  124.9 228.7 %all-gather.20.cloned.1.call-start = ((), (), s32[]{:S(2)}) async-start(), calls=%async_computation.9 | async-start | bytes 1966080 | tf_op jit(solution)/shard_map/all_gather | solution.py:500
  146.3 26.7 %collective-permute-start.14 = (bf16[96,1536]{1,0:T(8,128)(2,1)}, bf16[96,1536]{1,0:T(8,128)(2,1)}, u32[]{:S(2)}, u32[]{:S(2)}) collective-permute-start(bf16[96,1536]{1,0:T(8,128)(2,1)} %get-tuple-element.186), channel_id=1, source_target_pairs={{0,16},{8,24},{16,0},{24,8},{1,17},{9,25},{17,1},{25,9},{2,18},{10... | collective-permute-start | bytes 884744 | tf_op jit(solution)/shard_map/ppermute | solution.py:234
  146.5 26.5 %collective-permute-start.13 = (bf16[96,1536]{1,0:T(8,128)(2,1)}, bf16[96,1536]{1,0:T(8,128)(2,1)}, u32[]{:S(2)}, u32[]{:S(2)}) collective-permute-start(bf16[96,1536]{1,0:T(8,128)(2,1)} %get-tuple-element.187), channel_id=1, source_target_pairs={{0,8},{8,16},{16,24},{24,0},{1,9},{9,17},{17,25},{25,1},{2,10},{10... | collective-permute-start | bytes 884744 | tf_op jit(solution)/shard_map/ppermute | solution.py:234
  184.9 22.9 %collective-permute-start.17 = (bf16[96,1536]{1,0:T(8,128)(2,1)S(1)}, bf16[96,1536]{1,0:T(8,128)(2,1)S(1)}, u32[]{:S(2)}, u32[]{:S(2)}) collective-permute-start(bf16[96,1536]{1,0:T(8,128)(2,1)S(1)} %get-tuple-element.182), channel_id=1, source_target_pairs={{0,16},{8,24},{16,0},{24,8},{1,17},{9,25},{17,1},{25,9},{2,18},{10... | collective-permute-start | bytes 884744 | tf_op jit(solution)/shard_map/ppermute | solution.py:234
  186.7 21.0 %collective-permute-start.16 = (bf16[96,1536]{1,0:T(8,128)(2,1)S(1)}, bf16[96,1536]{1,0:T(8,128)(2,1)S(1)}, u32[]{:S(2)}, u32[]{:S(2)}) collective-permute-start(bf16[96,1536]{1,0:T(8,128)(2,1)S(1)} %get-tuple-element.183), channel_id=1, source_target_pairs={{0,24},{8,0},{16,8},{24,16},{1,25},{9,1},{17,9},{25,17},{2,26},{10... | collective-permute-start | bytes 884744 | tf_op jit(solution)/shard_map/ppermute | solution.py:234
  218.6 25.2 %collective-permute-start.20 = (bf16[96,1536]{1,0:T(8,128)(2,1)S(1)}, bf16[96,1536]{1,0:T(8,128)(2,1)S(1)}, u32[]{:S(2)}, u32[]{:S(2)}) collective-permute-start(bf16[96,1536]{1,0:T(8,128)(2,1)S(1)} %get-tuple-element.178), channel_id=1, source_target_pairs={{0,16},{8,24},{16,0},{24,8},{1,17},{9,25},{17,1},{25,9},{2,18},{10... | collective-permute-start | bytes 884744 | tf_op jit(solution)/shard_map/ppermute | solution.py:234
  218.8 25.0 %collective-permute-start.19 = (bf16[96,1536]{1,0:T(8,128)(2,1)S(1)}, bf16[96,1536]{1,0:T(8,128)(2,1)S(1)}, u32[]{:S(2)}, u32[]{:S(2)}) collective-permute-start(bf16[96,1536]{1,0:T(8,128)(2,1)S(1)} %get-tuple-element.179), channel_id=1, source_target_pairs={{0,8},{8,16},{16,24},{24,0},{1,9},{9,17},{17,25},{25,1},{2,10},{10... | collective-permute-start | bytes 884744 | tf_op jit(solution)/shard_map/ppermute | solution.py:234
  257.9 23.5 %collective-permute-start.23 = (bf16[96,1536]{1,0:T(8,128)(2,1)S(1)}, bf16[96,1536]{1,0:T(8,128)(2,1)S(1)}, u32[]{:S(2)}, u32[]{:S(2)}) collective-permute-start(bf16[96,1536]{1,0:T(8,128)(2,1)S(1)} %get-tuple-element.174), channel_id=1, source_target_pairs={{0,16},{8,24},{16,0},{24,8},{1,17},{9,25},{17,1},{25,9},{2,18},{10... | collective-permute-start | bytes 884744 | tf_op jit(solution)/shard_map/ppermute | solution.py:234
  259.3 22.0 %collective-permute-start.22 = (bf16[96,1536]{1,0:T(8,128)(2,1)S(1)}, bf16[96,1536]{1,0:T(8,128)(2,1)S(1)}, u32[]{:S(2)}, u32[]{:S(2)}) collective-permute-start(bf16[96,1536]{1,0:T(8,128)(2,1)S(1)} %get-tuple-element.175), channel_id=1, source_target_pairs={{0,24},{8,0},{16,8},{24,16},{1,25},{9,1},{17,9},{25,17},{2,26},{10... | collective-permute-start | bytes 884744 | tf_op jit(solution)/shard_map/ppermute | solution.py:234
  266.7 15.7 %collective-permute-start.26 = (bf16[192,1024]{1,0:T(8,128)(2,1)S(1)}, bf16[192,1024]{1,0:T(8,128)(2,1)S(1)}, u32[]{:S(2)}, u32[]{:S(2)}) collective-permute-start(bf16[192,1024]{1,0:T(8,128)(2,1)S(1)} %get-tuple-element.151), channel_id=1, source_target_pairs={{0,2},{1,3},{2,0},{3,1},{4,6},{5,7},{6,4},{7,5},{8,10},{9,11},{10,... | collective-permute-start | bytes 1179656 | tf_op jit(solution)/shard_map/ppermute | solution.py:252
  266.8 18.9 %collective-permute-start.28 = (bf16[192,1024]{1,0:T(8,128)(2,1)S(1)}, bf16[192,1024]{1,0:T(8,128)(2,1)S(1)}, u32[]{:S(2)}, u32[]{:S(2)}) collective-permute-start(bf16[192,1024]{1,0:T(8,128)(2,1)S(1)} %get-tuple-element.152), channel_id=1, source_target_pairs={{0,6},{1,7},{2,4},{3,5},{4,2},{5,3},{6,0},{7,1},{8,14},{9,15},{10,... | collective-permute-start | bytes 1179656 | tf_op jit(solution)/shard_map/ppermute | solution.py:252
  269.6 18.7 %collective-permute-start.27 = (bf16[192,1024]{1,0:T(8,128)(2,1)S(1)}, bf16[192,1024]{1,0:T(8,128)(2,1)S(1)}, u32[]{:S(2)}, u32[]{:S(2)}) collective-permute-start(bf16[192,1024]{1,0:T(8,128)(2,1)S(1)} %get-tuple-element.153), channel_id=1, source_target_pairs={{0,4},{1,5},{2,6},{3,7},{4,0},{5,1},{6,2},{7,3},{8,12},{9,13},{10,... | collective-permute-start | bytes 1179656 | tf_op jit(solution)/shard_map/ppermute | solution.py:252
  281.3 29.4 %collective-permute-start.29 = (bf16[4,192,2048]{2,1,0:T(8,128)(2,1)}, bf16[4,192,2048]{2,1,0:T(8,128)(2,1)}, u32[]{:S(2)}, u32[]{:S(2)}) collective-permute-start(bf16[4,192,2048]{2,1,0:T(8,128)(2,1)} %get-tuple-element.143), channel_id=1, source_target_pairs={{0,1},{1,0},{2,3},{3,2},{4,5},{5,4},{6,7},{7,6},{8,9},{9,8},{10,11... | collective-permute-start | bytes 9437192 | tf_op jit(solution)/shard_map/ppermute | solution.py:252
  297.5 35.2 %collective-permute-start.30 = (bf16[4,192,1536]{2,1,0:T(8,128)(2,1)}, bf16[4,192,1536]{2,1,0:T(8,128)(2,1)}, u32[]{:S(2)}, u32[]{:S(2)}) collective-permute-start(bf16[4,192,1536]{2,1,0:T(8,128)(2,1)} %get-tuple-element.149), channel_id=1, source_target_pairs={{0,1},{1,0},{2,3},{3,2},{4,5},{5,4},{6,7},{7,6},{8,9},{9,8},{10,11... | collective-permute-start | bytes 7077896 | tf_op jit(solution)/shard_map/ppermute | solution.py:252
  305.6 27.1 %all-to-all-start.1 = ((bf16[128,4,384]{2,0,1:T(8,128)(2,1)}), bf16[128,4,384]{2,0,1:T(8,128)(2,1)S(1)}, u32[]{:S(2)}, u32[]{:S(2)}) async-start(bf16[128,4,384]{2,0,1:T(8,128)(2,1)} %bitcast.326), calls=%async_computation.1 | async-start | bytes 786432 | tf_op jit(solution)/shard_map/all_to_all | solution.py:498
  310.2 214.3 %all-gather.18.cloned.1.call-start = ((), (), s32[]{:S(2)}) async-start(), calls=%async_computation.8 | async-start | bytes 3932160 | tf_op jit(solution)/shard_map/all_gather | solution.py:519
  316.4 40.8 %collective-permute-start.33 = (bf16[192,2048]{1,0:T(8,128)(2,1)}, bf16[192,2048]{1,0:T(8,128)(2,1)}, u32[]{:S(2)}, u32[]{:S(2)}) collective-permute-start(bf16[192,2048]{1,0:T(8,128)(2,1)} %get-tuple-element.139), channel_id=1, source_target_pairs={{0,6},{1,7},{2,4},{3,5},{4,2},{5,3},{6,0},{7,1},{8,14},{9,15},{10,... | collective-permute-start | bytes 2359304 | tf_op jit(solution)/shard_map/ppermute | solution.py:252
  317.2 40.0 %collective-permute-start.32 = (bf16[192,2048]{1,0:T(8,128)(2,1)}, bf16[192,2048]{1,0:T(8,128)(2,1)}, u32[]{:S(2)}, u32[]{:S(2)}) collective-permute-start(bf16[192,2048]{1,0:T(8,128)(2,1)} %get-tuple-element.140), channel_id=1, source_target_pairs={{0,4},{1,5},{2,6},{3,7},{4,0},{5,1},{6,2},{7,3},{8,12},{9,13},{10,... | collective-permute-start | bytes 2359304 | tf_op jit(solution)/shard_map/ppermute | solution.py:252
  317.9 39.3 %collective-permute-start.31 = (bf16[192,2048]{1,0:T(8,128)(2,1)}, bf16[192,2048]{1,0:T(8,128)(2,1)}, u32[]{:S(2)}, u32[]{:S(2)}) collective-permute-start(bf16[192,2048]{1,0:T(8,128)(2,1)} %get-tuple-element.141), channel_id=1, source_target_pairs={{0,2},{1,3},{2,0},{3,1},{4,6},{5,7},{6,4},{7,5},{8,10},{9,11},{10,... | collective-permute-start | bytes 2359304 | tf_op jit(solution)/shard_map/ppermute | solution.py:252
  364.9 53.2 %collective-permute-start.54 = (bf16[192,1536]{1,0:T(8,128)(2,1)}, bf16[192,1536]{1,0:T(8,128)(2,1)}, u32[]{:S(2)}, u32[]{:S(2)}) collective-permute-start(bf16[192,1536]{1,0:T(8,128)(2,1)} %get-tuple-element.145), channel_id=1, source_target_pairs={{0,6},{1,7},{2,4},{3,5},{4,2},{5,3},{6,0},{7,1},{8,14},{9,15},{10,... | collective-permute-start | bytes 1769480 | tf_op jit(solution)/shard_map/ppermute | solution.py:252
  365.5 53.8 %collective-permute-start.53 = (bf16[192,1536]{1,0:T(8,128)(2,1)}, bf16[192,1536]{1,0:T(8,128)(2,1)}, u32[]{:S(2)}, u32[]{:S(2)}) collective-permute-start(bf16[192,1536]{1,0:T(8,128)(2,1)} %get-tuple-element.146), channel_id=1, source_target_pairs={{0,4},{1,5},{2,6},{3,7},{4,0},{5,1},{6,2},{7,3},{8,12},{9,13},{10,... | collective-permute-start | bytes 1769480 | tf_op jit(solution)/shard_map/ppermute | solution.py:252
  366.3 53.0 %collective-permute-start.52 = (bf16[192,1536]{1,0:T(8,128)(2,1)}, bf16[192,1536]{1,0:T(8,128)(2,1)}, u32[]{:S(2)}, u32[]{:S(2)}) collective-permute-start(bf16[192,1536]{1,0:T(8,128)(2,1)} %get-tuple-element.147), channel_id=1, source_target_pairs={{0,2},{1,3},{2,0},{3,1},{4,6},{5,7},{6,4},{7,5},{8,10},{9,11},{10,... | collective-permute-start | bytes 1769480 | tf_op jit(solution)/shard_map/ppermute | solution.py:252
  383.7 24.7 %all-to-all-start.2 = ((bf16[4,128,384]{1,2,0:T(8,128)(2,1)}), bf16[4,128,384]{1,2,0:T(8,128)(2,1)S(1)}, u32[]{:S(2)}, u32[]{:S(2)}) async-start(bf16[4,128,384]{1,2,0:T(8,128)(2,1)} %pad_maximum_fusion.6), calls=%async_computation.2 | async-start | bytes 786432 | tf_op jit(solution)/shard_map/all_to_all | solution.py:526
  388.6 24.7 %collective-permute-start.34 = (bf16[4,512,256]{2,1,0:T(8,128)(2,1)}, bf16[4,512,256]{2,1,0:T(8,128)(2,1)}, u32[]{:S(2)}, u32[]{:S(2)}) collective-permute-start(bf16[4,512,256]{2,1,0:T(8,128)(2,1)} %pad_maximum_fusion.5), channel_id=1, source_target_pairs={{0,1},{1,0},{2,3},{3,2},{4,5},{5,4},{6,7},{7,6},{8,9},{9,8},{10,11... | collective-permute-start | bytes 3145736 | tf_op jit(solution)/shard_map/ppermute | solution.py:252
  415.8 23.9 %collective-permute-start.44 = (bf16[512,256]{1,0:T(8,128)(2,1)}, bf16[512,256]{1,0:T(8,128)(2,1)}, u32[]{:S(2)}, u32[]{:S(2)}) collective-permute-start(bf16[512,256]{1,0:T(8,128)(2,1)} %get-tuple-element.160), channel_id=1, source_target_pairs={{0,6},{1,7},{2,4},{3,5},{4,2},{5,3},{6,0},{7,1},{8,14},{9,15},{10,... | collective-permute-start | bytes 786440 | tf_op jit(solution)/shard_map/ppermute | solution.py:252
  417.5 22.3 %collective-permute-start.43 = (bf16[512,256]{1,0:T(8,128)(2,1)}, bf16[512,256]{1,0:T(8,128)(2,1)}, u32[]{:S(2)}, u32[]{:S(2)}) collective-permute-start(bf16[512,256]{1,0:T(8,128)(2,1)} %get-tuple-element.161), channel_id=1, source_target_pairs={{0,4},{1,5},{2,6},{3,7},{4,0},{5,1},{6,2},{7,3},{8,12},{9,13},{10,... | collective-permute-start | bytes 786440 | tf_op jit(solution)/shard_map/ppermute | solution.py:252
  418.1 21.8 %collective-permute-start.42 = (bf16[512,256]{1,0:T(8,128)(2,1)}, bf16[512,256]{1,0:T(8,128)(2,1)}, u32[]{:S(2)}, u32[]{:S(2)}) collective-permute-start(bf16[512,256]{1,0:T(8,128)(2,1)} %get-tuple-element.162), channel_id=1, source_target_pairs={{0,2},{1,3},{2,0},{3,1},{4,6},{5,7},{6,4},{7,5},{8,10},{9,11},{10,... | collective-permute-start | bytes 786440 | tf_op jit(solution)/shard_map/ppermute | solution.py:252
  424.5 17.0 %collective-permute-start.55 = (bf16[192,384]{1,0:T(8,128)(2,1)}, bf16[192,384]{1,0:T(8,128)(2,1)}, u32[]{:S(2)}, u32[]{:S(2)}) collective-permute-start(bf16[192,384]{1,0:T(8,128)(2,1)} %bitcast.329), channel_id=1, source_target_pairs={{0,8},{8,16},{16,24},{24,0},{1,9},{9,17},{17,25},{25,1},{2,10},{10... | collective-permute-start | bytes 442376 | tf_op jit(solution)/shard_map/ppermute | solution.py:234
  425.3 16.2 %collective-permute-start.56 = (bf16[192,384]{1,0:T(8,128)(2,1)}, bf16[192,384]{1,0:T(8,128)(2,1)}, u32[]{:S(2)}, u32[]{:S(2)}) collective-permute-start(bf16[192,384]{1,0:T(8,128)(2,1)} %bitcast.328), channel_id=1, source_target_pairs={{0,16},{8,24},{16,0},{24,8},{1,17},{9,25},{17,1},{25,9},{2,18},{10... | collective-permute-start | bytes 442376 | tf_op jit(solution)/shard_map/ppermute | solution.py:234
  439.8 25.6 %collective-permute-start.35 = (bf16[4,192,392]{2,1,0:T(8,128)(2,1)}, bf16[4,192,392]{2,1,0:T(8,128)(2,1)S(1)}, u32[]{:S(2)}, u32[]{:S(2)}) collective-permute-start(bf16[4,192,392]{2,1,0:T(8,128)(2,1)} %bitcast.361), channel_id=1, source_target_pairs={{0,1},{1,0},{2,3},{3,2},{4,5},{5,4},{6,7},{7,6},{8,9},{9,8},{10,11... | collective-permute-start | bytes 1806344 | tf_op jit(solution)/shard_map/ppermute | solution.py:252
  453.2 16.7 %all-to-all-start.3 = ((bf16[4,128,256]{1,2,0:T(8,128)(2,1)}), bf16[4,128,256]{1,2,0:T(8,128)(2,1)S(1)}, u32[]{:S(2)}, u32[]{:S(2)}) async-start(bf16[4,128,256]{1,2,0:T(8,128)(2,1)} %copy.231), calls=%async_computation.3 | async-start | bytes 524288 | tf_op jit(solution)/shard_map/all_to_all | solution.py:529
  458.4 15.0 %collective-permute-start.45 = (bf16[4,192,256]{2,1,0:T(8,128)(2,1)}, bf16[4,192,256]{2,1,0:T(8,128)(2,1)S(1)}, u32[]{:S(2)}, u32[]{:S(2)}) collective-permute-start(bf16[4,192,256]{2,1,0:T(8,128)(2,1)} %dynamic-slice_bitcast_fusion.5), channel_id=1, source_target_pairs={{0,1},{1,0},{2,3},{3,2},{4,5},{5,4},{6,7},{7,6},{8,9},{9,8},{10,11... | collective-permute-start | bytes 1179656 | tf_op jit(solution)/shard_map/ppermute | solution.py:252
  491.1 27.8 %collective-permute-start.41 = (bf16[192,390]{1,0:T(8,128)(2,1)S(1)}, bf16[192,390]{1,0:T(8,128)(2,1)S(1)}, u32[]{:S(2)}, u32[]{:S(2)}) collective-permute-start(bf16[192,390]{1,0:T(8,128)(2,1)S(1)} %get-tuple-element.129), channel_id=1, source_target_pairs={{0,8},{8,16},{16,24},{24,0},{1,9},{9,17},{17,25},{25,1},{2,10},{10... | collective-permute-start | bytes 449288 | tf_op jit(solution)/shard_map/ppermute | solution.py:234
  491.2 27.7 %collective-permute-start.40 = (bf16[192,390]{1,0:T(8,128)(2,1)S(1)}, bf16[192,390]{1,0:T(8,128)(2,1)S(1)}, u32[]{:S(2)}, u32[]{:S(2)}) collective-permute-start(bf16[192,390]{1,0:T(8,128)(2,1)S(1)} %get-tuple-element.129), channel_id=1, source_target_pairs={{0,16},{8,24},{16,0},{24,8},{1,17},{9,25},{17,1},{25,9},{2,18},{10... | collective-permute-start | bytes 449288 | tf_op jit(solution)/shard_map/ppermute | solution.py:234
  491.8 27.1 %collective-permute-start.39 = (bf16[192,390]{1,0:T(8,128)(2,1)S(1)}, bf16[192,390]{1,0:T(8,128)(2,1)S(1)}, u32[]{:S(2)}, u32[]{:S(2)}) collective-permute-start(bf16[192,390]{1,0:T(8,128)(2,1)S(1)} %get-tuple-element.129), channel_id=1, source_target_pairs={{0,24},{8,0},{16,8},{24,16},{1,25},{9,1},{17,9},{25,17},{2,26},{10... | collective-permute-start | bytes 449288 | tf_op jit(solution)/shard_map/ppermute | solution.py:234
  495.0 21.7 %collective-permute-start.51 = (bf16[192,256]{1,0:T(8,128)(2,1)S(1)}, bf16[192,256]{1,0:T(8,128)(2,1)S(1)}, u32[]{:S(2)}, u32[]{:S(2)}) collective-permute-start(bf16[192,256]{1,0:T(8,128)(2,1)S(1)} %get-tuple-element.125), channel_id=1, source_target_pairs={{0,8},{8,16},{16,24},{24,0},{1,9},{9,17},{17,25},{25,1},{2,10},{10... | collective-permute-start | bytes 294920 | tf_op jit(solution)/shard_map/ppermute | solution.py:234
  495.6 21.1 %collective-permute-start.50 = (bf16[192,256]{1,0:T(8,128)(2,1)S(1)}, bf16[192,256]{1,0:T(8,128)(2,1)S(1)}, u32[]{:S(2)}, u32[]{:S(2)}) collective-permute-start(bf16[192,256]{1,0:T(8,128)(2,1)S(1)} %get-tuple-element.125), channel_id=1, source_target_pairs={{0,16},{8,24},{16,0},{24,8},{1,17},{9,25},{17,1},{25,9},{2,18},{10... | collective-permute-start | bytes 294920 | tf_op jit(solution)/shard_map/ppermute | solution.py:234
  (113 other events, 1611.7 us)
Sparse Core Ops, SparseCore 0:
  10.8 30.0 all-gather.9
  42.8 46.1 all-gather.11
  91.5 59.3 all-gather.13
  152.6 52.2 all-gather.15
  301.8 45.5 all-gather.19
  360.4 80.1 all-gather.17

commit v4 on v3

--- a/solution.py
+++ b/solution.py
@@ -11,6 +11,7 @@
 KVH = 8
 HD = 64
 CAP = 96
+LANES = 128
 EPSILON = 1e-06
 FLOOR_SCORE = -1e30
 BF = jnp.bfloat16
@@ -118,7 +119,7 @@
             pltpu.VMEM((local_kv, stack, 2 * HD), F32),
             pltpu.VMEM((local_kv, stack, 2 * HD), F32),
         ],
-        compiler_params=pltpu.CompilerParams(vmem_limit_bytes=40 * 1024 * 1024),
+        compiler_params=pltpu.CompilerParams(vmem_limit_bytes=60 * 1024 * 1024),
         cost_estimate=pl.CostEstimate(
             flops=8 * seqs * seqs * shards * rows * rows * local_kv * groups * HD,
             bytes_accessed=8 * 1024 * 1024,
@@ -221,7 +222,7 @@
             pltpu.VMEM((seqs, stack, 2 * HD), F32),
             pltpu.VMEM((2 * HD, shards * rows), F32),
         ],
-        compiler_params=pltpu.CompilerParams(vmem_limit_bytes=40 * 1024 * 1024),
+        compiler_params=pltpu.CompilerParams(vmem_limit_bytes=60 * 1024 * 1024),
         cost_estimate=pl.CostEstimate(
             flops=40 * seqs * seqs * shards * rows * rows * groups * HD,
             bytes_accessed=8 * 1024 * 1024,
@@ -242,6 +243,21 @@
     return [blocks[0]] + [shift(blocks[s], count, count - s) for s in range(1, count)]
 
 
+def relay_step(blocks, count):
+    up, down = blocks
+    return (
+        lax.ppermute(up, "seq", [(i, i + 1) for i in range(count - 1)]),
+        lax.ppermute(down, "seq", [(i + 1, i) for i in range(count - 1)]),
+    )
+
+
+def relay_blocks(steps, place):
+    count = len(steps)
+    return [steps[0][0]] + [
+        jnp.where(place >= s, steps[s][0], steps[count - s][1]) for s in range(1, count)
+    ]
+
+
 def from_relative(blocks, place):
     count = len(blocks)
     rising = jnp.stack([blocks[-s % count] for s in range(count)])
@@ -258,7 +274,7 @@
 
 
 def send_chips(parts, count):
-    return [parts[0]] + [hop(parts[m], count, 2 * m) for m in range(1, count // 2)]
+    return list(parts[0]) + [hop(parts[m], count, 2 * m) for m in range(1, count // 2)]
 
 
 def total_of(blocks):
@@ -275,17 +291,16 @@
 def pair_halves(product, shard, count):
     width, cols = product.shape
     cut = product.reshape(count // 2, 2, width // count, cols)
-    core = shard % 2
-    return take(cut, core, 1), hop(take(cut, 1 - core, 1), count, 1)
+    there = hop(take(cut, 1 - shard % 2, 1), count, 1)
+    return product.reshape(count, width // count, cols), there
 
 
 def pair_sums(halves, shard):
     here, there = halves
-    chip = shard // 2
-    sums = []
-    for m in range(here.shape[0]):
-        each = take(here, chip ^ m, 0).astype(F32) + take(there, chip ^ m, 0).astype(F32)
-        sums.append(each if m == 0 else each.astype(BF))
+    sums = [(take(here, shard, 0), take(there, shard // 2, 0))]
+    for m in range(1, there.shape[0]):
+        each = take(here, shard ^ (2 * m), 0).astype(F32)
+        sums.append((each + take(there, (shard // 2) ^ m, 0).astype(F32)).astype(BF))
     return sums
 
 
@@ -293,13 +308,9 @@
     return total_of(send_chips(pair_sums(pair_halves(product, shard, count), shard), count))
 
 
-def spread_scalar(value, core, rows):
+def two_parts(value):
     high = value.astype(BF)
-    low = (value - high.astype(F32)).astype(BF)
-    pair = jnp.stack([high, low])
-    none = jnp.zeros_like(pair)
-    row = jnp.where(core == 0, jnp.concatenate([pair, none]), jnp.concatenate([none, pair]))
-    return jnp.broadcast_to(row[None, :], (rows, 4))
+    return high, (value - high.astype(F32)).astype(BF)
 
 
 def after(values, *others):
@@ -313,6 +324,46 @@
 def root_back(values, factor, grad_scaled):
     inner = jnp.mean(grad_scaled * values, axis=-1, keepdims=True)
     return factor * grad_scaled - values * (factor * factor * factor * inner)
+
+
+def place_gate_up(blocks, weight, gain, place, *wait):
+    experts, part, both = weight.shape
+    count = len(blocks)
+    split = count // experts
+    if split > 1:
+        base = (
+            from_relative(blocks, place)
+            .reshape(experts, split, part, 2, both // (2 * split))
+            .transpose(0, 2, 3, 1, 4)
+            .reshape(experts, part, both)
+            .astype(F32)
+        )
+        return base * gain, jnp.sum(weight.astype(F32) * base, axis=(0, 2))
+    result = jnp.zeros((experts, part, both), F32)
+    blocks = [after(blocks[0], *wait)] + blocks[1:]
+    sums = jnp.zeros((part,), F32)
+    for s in range(count):
+        expert = (place - s) % count
+        base = blocks[s].astype(F32)
+        result = lax.dynamic_update_index_in_dim(result, base * gain, expert, 0)
+        sums = sums + jnp.sum(take(weight, expert, 0).astype(F32) * base, axis=1)
+    return result, sums
+
+
+def place_columns(blocks, place, finish):
+    count = len(blocks)
+    rows, cols = blocks[0].shape
+    result = jnp.zeros((rows, count * cols), F32)
+    for s in range(count):
+        column = (place - s) % count * cols
+        result = lax.dynamic_update_slice(
+            result, finish(blocks[s].astype(F32), column), (0, column)
+        )
+    return result
+
+
+def columns_of(array, column, cols):
+    return lax.dynamic_slice_in_dim(array, column, cols, 1).astype(F32)
 
 
 def local(
@@ -360,31 +411,15 @@
     )
     heads_shard = (heads_shard.astype(F32) * gain_one).astype(BF)
     heads_full = lax.all_gather(heads_shard, "fsdp", axis=0, tiled=True)
-    token_blocks = send_out([tokens] * seqs, seqs)
-    late_gate_up, late_down, late_valid = after((w_gate_up, w_down, valid), token_blocks[1])
-    out_full = lax.all_gather(w_out, "fsdp", axis=1, tiled=True)
-    router_full = lax.all_gather(
-        (w_router.astype(F32) * gain_two).astype(BF), "fsdp", axis=0, tiled=True
-    )
-    own_expert = take(late_gate_up, expert, 0)
-    gate_shard = lax.dynamic_slice_in_dim(own_expert, fraction * piece, piece, 1)
-    up_shard = lax.dynamic_slice_in_dim(own_expert, units + fraction * piece, piece, 1)
-    down_shard = lax.dynamic_slice_in_dim(
-        take(late_down, expert, 0), fraction * piece, piece, 0
-    ).T
-    expert_shard = jnp.concatenate(
-        [
-            (gate_shard.astype(F32) * gain_two).astype(BF),
-            (up_shard.astype(F32) * gain_two).astype(BF),
-            down_shard,
-        ],
-        axis=1,
-    )
-    expert_full = lax.all_gather(expert_shard, "fsdp", axis=0, tiled=True)
-    gate_up_full = expert_full[:, : 2 * piece]
-    down_full = expert_full[:, 2 * piece :]
-    valid_low = late_valid.astype(BF).reshape(1, rows)
-    valid_local = from_relative(send_out([valid_low] * seqs, seqs), z)
+    valid_row = jnp.pad(valid.astype(BF).reshape(1, rows), ((0, 7), (0, width - rows)))
+    steps = [(jnp.concatenate([tokens, valid_row], axis=0),) * 2]
+    for unused in range(seqs - 1):
+        steps.append(relay_step(steps[-1], seqs))
+    midway = steps[seqs // 2]
+    token_blocks = relay_blocks(steps, z)
+
+    valid_local = from_relative([each[rows : rows + 1, :rows] for each in token_blocks], z)
+    token_blocks = [each[:rows] for each in token_blocks]
     projected = []
     for block in token_blocks:
         projected.append(dot(block, heads_full) * root(block.astype(F32)))
@@ -402,6 +437,32 @@
         axis=0,
     )
     kv_blocks = gather_shards(payload, shards)
+    late_query, late_keyval, late_out, late_router, late_gate_up, late_down = after(
+        (w_query, w_keyval, w_out, w_router, w_gate_up, w_down), midway
+    )
+    out_full = lax.all_gather(w_out, "fsdp", axis=1, tiled=True)
+    own_expert = take(late_gate_up, expert, 0)
+    gate_shard = lax.dynamic_slice_in_dim(own_expert, fraction * piece, piece, 1)
+    up_shard = lax.dynamic_slice_in_dim(own_expert, units + fraction * piece, piece, 1)
+    down_shard = lax.dynamic_slice_in_dim(take(late_down, expert, 0), fraction * piece, piece, 0).T
+    router_shard = jnp.pad((late_router.astype(F32) * gain_two).astype(BF), ((0, 0), (0, LANES - experts)))
+    expert_shard = jnp.concatenate(
+        [
+            (gate_shard.astype(F32) * gain_two).astype(BF),
+            (up_shard.astype(F32) * gain_two).astype(BF),
+            down_shard,
+            router_shard,
+        ],
+        axis=1,
+    )
+    expert_full = lax.all_gather(expert_shard, "fsdp", axis=0, tiled=True)
+    gate_up_full = expert_full[:, : 2 * piece]
+    down_full = expert_full[:, 2 * piece : 3 * piece]
+    router_full = expert_full[:, 3 * piece :]
+    attn_shard = jnp.concatenate([late_query, late_keyval], axis=1)
+    attn_full = lax.all_gather(
+        (attn_shard.astype(F32) * gain_one).astype(BF), "fsdp", axis=0, tiled=True
+    )
     order = jnp.asarray(
         [2 * m for m in range(shards // 2)] + [2 * m + 1 for m in range(shards // 2)], jnp.int32
     )
@@ -422,16 +483,11 @@
     )
     attended = lax.all_to_all(attended_low, "seq", split_axis=0, concat_axis=1, tiled=True)
 
-    late_query, late_keyval = after((w_query, w_keyval), attended)
-    attn_shard = jnp.concatenate([late_query, late_keyval], axis=1)
-    attn_full = lax.all_gather(
-        (attn_shard.astype(F32) * gain_one).astype(BF), "fsdp", axis=0, tiled=True
-    )
     inputs = tokens.astype(F32)
     residual = inputs + dot(attended, out_full)
     factor_two = root(residual)
     normed_two = (residual * factor_two).astype(BF)
-    logits = dot(normed_two, router_full)
+    logits = dot(normed_two, router_full)[:, :experts]
     expert_ids = jnp.arange(experts, dtype=jnp.int32)
     picked = (routes[:, :, None] == expert_ids).astype(F32)
     chosen = jnp.sum(picked * logits[:, None, :], axis=-1)
@@ -466,6 +522,7 @@
     )
     grad_chosen = gating * (grad_gating - jnp.sum(gating * grad_gating, axis=-1, keepdims=True))
     grad_logits = jnp.sum(grad_chosen[:, :, None] * picked, axis=1).astype(BF)
+    grad_logits = jnp.pad(grad_logits, ((0, 0), (0, LANES - experts)))
     weighted = jnp.concatenate(
         [(gating[:, :1] * grad_mixed).astype(BF), (gating[:, 1:] * grad_mixed).astype(BF)], axis=0
     )
@@ -486,9 +543,9 @@
     grad_gate_up_halves = pair_halves(
         dot_tn(held_rows, held_gate_up).astype(BF), shard, shards
     )
-    grad_returned = after(grad_returned, grad_down_sums)
-    late_blocks = after(token_blocks, sent_grads)
-    tokens_local = from_relative(late_blocks, z).reshape(local_rows, width)
+    grad_gate_up_sums = pair_sums(grad_gate_up_halves, shard)
+    grad_returned = after(grad_returned, grad_down_sums, grad_gate_up_sums)
+    tokens_local = from_relative(after(token_blocks, grad_rows), z).reshape(local_rows, width)
     factor_local = root(tokens_local.astype(F32))
 
     grad_normed_two = dot(dispatch, grad_returned) + dot_nt(grad_logits, router_full)
@@ -496,15 +553,19 @@
     grad_branch = grad_residual.astype(BF)
     grad_attended = dot_nt(grad_branch, out_full).astype(BF)
     head_grad = lax.all_to_all(grad_attended, "seq", split_axis=1, concat_axis=0, tiled=True)
-    grad_down_shard = total_of(send_chips(grad_down_sums, shards)).astype(BF)
+    grad_down_blocks = after(send_chips(grad_down_sums, shards), grad_attended)
+    grad_down_shard = total_of(grad_down_blocks).astype(BF)
     grad_down = lax.all_gather(grad_down_shard, "seq", axis=0, tiled=False)
-    grad_gate_up_sums = pair_sums(after(grad_gate_up_halves, grad_attended), shard)
-    grad_gate_up_blocks = send_chips(grad_gate_up_sums, shards)
-
-    grad_out_halves = pair_halves(dot_tn(grad_branch, attended).astype(BF), shard, shards)
+    grad_gate_up_blocks = after(send_chips(grad_gate_up_sums, shards), grad_attended)
+    grad_gate_up_steps = [(total_of(grad_gate_up_blocks).astype(BF),) * 2]
+    grad_gate_up_steps.append(relay_step(grad_gate_up_steps[0], seqs))
+
+    late_branch = after(grad_branch, grad_attended)
+    grad_out_halves = pair_halves(dot_tn(late_branch, attended).astype(BF), shard, shards)
+    grad_out_sums = pair_sums(grad_out_halves, shard)
 
     grad_q, near, far = [], [], []
-    held = after(head_grad, grad_down_shard, grad_gate_up_sums, grad_out_halves)
+    held = after(head_grad, grad_down_shard, grad_gate_up_steps[0], grad_out_sums)
     for g in range(local_kv):
         part_q, near_kv, far_kv = flash_backward(
             head_queries, kv_blocks, bias, held, exact, lse, seqs, rows, g, groups
@@ -512,101 +573,116 @@
         grad_q.append(part_q * scale)
         near.append(near_kv)
         far.append(far_kv)
-        if g == 0:
-            grad_gate_up_shard = total_of(after(grad_gate_up_blocks, part_q)).astype(BF)
-            grad_out_sums = pair_sums(after(grad_out_halves, part_q), shard)
-            held = after(head_grad, grad_gate_up_shard, grad_out_sums)
-    grad_gate_up = lax.all_gather(grad_gate_up_shard, "seq", axis=0, tiled=False)
+        held = after(head_grad, part_q)
+    grad_gate_up_steps[-1] = after(grad_gate_up_steps[-1], part_q)
+    grad_gate_up_steps.append(relay_step(grad_gate_up_steps[-1], seqs))
+    grad_out_blocks = after(send_chips(grad_out_sums, shards), part_q)
     near = jnp.concatenate(near, axis=2)
     there = hop(jnp.concatenate(far, axis=2), shards, 1)
     pairs = [near[m].astype(F32) + there[m].astype(F32) for m in range(shards // 2)]
-    pairs = [pairs[0]] + [each.astype(BF) for each in pairs[1:]]
+    pairs = [(near[0], there[0])] + [each.astype(BF) for each in pairs[1:]]
     grad_q = jnp.concatenate(grad_q, axis=1)
-    grad_kv = total_of(send_chips(pairs, shards))
     token_grad_q = lax.all_to_all(
         grad_q.astype(BF), "seq", split_axis=0, concat_axis=1, tiled=True
     )
+    query_rhs = (grad_q * factor_local).astype(BF)
+    high, low = two_parts(squares)
+    lane = jnp.arange(LANES, dtype=jnp.int32)[None, :]
+    marks = jnp.where(lane == experts + 2 * (shard % 2), high, 0) + jnp.where(
+        lane == experts + 1 + 2 * (shard % 2), low, 0
+    )
+    router_product = dot_tn(normed_two, grad_logits).astype(BF) + marks.astype(BF)
+    query_product = jnp.concatenate(
+        [dot_tn(tokens_local, query_rhs).astype(BF), router_product], axis=1
+    )
+    grad_query_sums = pair_sums(pair_halves(after(query_product, pairs), shard, shards), shard)
+    grad_kv = total_of(after(send_chips(pairs, shards), grad_query_sums))
+    while len(grad_gate_up_steps) < seqs:
+        grad_gate_up_steps[-1] = after(grad_gate_up_steps[-1], grad_kv)
+        grad_gate_up_steps.append(relay_step(grad_gate_up_steps[-1], seqs))
     token_grad_kv = lax.all_to_all(
         grad_kv.astype(BF), "seq", split_axis=0, concat_axis=1, tiled=True
     )
-    grad_out_part = total_of(after(send_chips(grad_out_sums, shards), pairs))
-    cut = grad_out_part.astype(BF).reshape(part, seqs, q_cols)
+    keyval_rhs = (grad_kv * factor_local).astype(BF)
+    grad_keyval_sums = pair_sums(
+        pair_halves(dot_tn(tokens_local, keyval_rhs).astype(BF), shard, shards), shard
+    )
+    grad_query_part = total_of(after(send_chips(grad_query_sums, shards), grad_keyval_sums))
+    base_cols = q_cols + experts
+    plane_high, plane_low = two_parts(
+        jnp.sum(grad_query_part[:1, base_cols : base_cols + 4], axis=1, keepdims=True)
+    )
+    lanes = lax.broadcasted_iota(jnp.int32, grad_query_part.shape, 1)
+    grad_query_part = jnp.where(
+        lanes == base_cols,
+        plane_high.astype(F32),
+        jnp.where(lanes == base_cols + 1, plane_low.astype(F32), grad_query_part),
+    )
+    grad_query_blocks = send_out([grad_query_part.astype(BF)] * seqs, seqs)
+    grad_out_part = total_of(after(grad_out_blocks, pairs))
+    cut = grad_out_part.astype(BF)
     grad_out_own = jnp.zeros((part, q_cols), F32)
-    out_parts = send_out([take(cut, (z + s) % seqs, 1) for s in range(seqs)], seqs)
+    out_parts = send_out(
+        [
+            lax.dynamic_slice_in_dim(cut, (z + s) % seqs * q_cols, q_cols, 1)
+            for s in range(seqs)
+        ],
+        seqs,
+    )
     for each in after(out_parts, grad_kv):
         grad_out_own = grad_out_own + each.astype(F32)
-    grad_out = from_relative(send_out([grad_out_own.astype(BF)] * seqs, seqs), z)
-    grad_out = grad_out.transpose(0, 2, 1).reshape(HEADS * HD, part).astype(F32)
-    grad_normed = dot_nt(token_grad_q, attn_full[:, : HEADS * HD]) + dot_nt(
+    grad_out = place_columns(
+        send_out([grad_out_own.astype(BF)] * seqs, seqs), z, lambda block, column: block
+    ).T
+    grad_normed = dot_nt(after(token_grad_q, grad_kv), attn_full[:, : HEADS * HD]) + dot_nt(
         token_grad_kv, attn_full[:, HEADS * HD :]
     )
     grad_tokens = grad_residual + root_back(inputs, root(inputs), grad_normed)
 
-    query_rhs = (grad_q * factor_local).astype(BF)
-    marks = spread_scalar(squares, shard % 2, width)
-    query_product = jnp.concatenate(
-        [
-            dot_tn(tokens_local, query_rhs).astype(BF),
-            dot_tn(normed_two, grad_logits).astype(BF),
-            marks,
-        ],
-        axis=1,
-    )
-    grad_query_part = sum_rows(after(query_product, pairs), shard, shards)
-    keyval_rhs = (grad_kv * factor_local).astype(BF)
-    grad_keyval_part = sum_rows(dot_tn(tokens_local, keyval_rhs).astype(BF), shard, shards)
-    base_cols = q_cols + experts
-    plane_squares = jnp.sum(grad_query_part[:, base_cols:], axis=1, keepdims=True)
-    plane_high = plane_squares.astype(BF)
-    plane_low = (plane_squares - plane_high.astype(F32)).astype(BF)
-    grad_query_base = from_relative(
-        send_out(
-            [jnp.concatenate([grad_query_part[:, :base_cols].astype(BF), plane_high, plane_low], axis=1)]
-            * seqs,
-            seqs,
-        ),
-        z,
-    ).astype(F32)
-    loss_value = jnp.sum(grad_query_base[:, 0, base_cols:]) / (width * valid_count)
-    grad_router_base = jnp.sum(grad_query_base[:, :, q_cols:base_cols], axis=0)
-    grad_query_base = grad_query_base[:, :, :q_cols].transpose(1, 0, 2).reshape(part, HEADS * HD)
-    grad_keyval_base = (
-        from_relative(send_out([grad_keyval_part.astype(BF)] * seqs, seqs), z)
-        .astype(F32)
-        .transpose(1, 0, 2)
-        .reshape(part, 2 * KVH * HD)
-    )
-
-    grad_gain_attn = jnp.sum(w_query.astype(F32) * grad_query_base, axis=1) + jnp.sum(
-        w_keyval.astype(F32) * grad_keyval_base, axis=1
-    )
+    grad_keyval_part = total_of(after(send_chips(grad_keyval_sums, shards), grad_query_part))
+    grad_keyval_blocks = send_out([grad_keyval_part.astype(BF)] * seqs, seqs)
+    grad_gate_up, grad_gain_ffn = place_gate_up(
+        relay_blocks(grad_gate_up_steps, z), w_gate_up, gain_two, z, grad_kv
+    )
+    grad_keyval_blocks = after(grad_keyval_blocks, grad_gate_up)
+    sums = sum(
+        jnp.sum(each[:, q_cols : q_cols + LANES].astype(F32).reshape(part, 1, LANES), axis=1)
+        for each in grad_query_blocks
+    )
+    loss_value = jnp.sum(sums[0, experts : experts + 2]) / (width * valid_count)
+    grad_router_base = sums[:, :experts]
+
+    gain_parts = []
+
+    def end_query(block, column):
+        gain_parts.append(jnp.sum(columns_of(w_query, column, q_cols) * block, axis=1))
+        return block * gain_one
+
+    def end_keyval(block, column):
+        gain_parts.append(jnp.sum(columns_of(w_keyval, column, kv_cols) * block, axis=1))
+        return block * gain_one
+
+    grad_query = place_columns([each[:, :q_cols] for each in grad_query_blocks], z, end_query)
+    grad_keyval = place_columns(grad_keyval_blocks, z, end_keyval)
+    grad_gain_attn = sum(gain_parts)
     grad_down = (
-        grad_down.reshape(experts, split, part, piece)
+        after(grad_down, grad_kv).reshape(experts, split, part, piece)
         .transpose(0, 1, 3, 2)
         .reshape(experts, units, part)
         .astype(F32)
     )
-    grad_gate_up = grad_gate_up.astype(F32)
-    if split > 1:
-        grad_gate_up = (
-            grad_gate_up.reshape(experts, split, part, 2, piece)
-            .transpose(0, 2, 3, 1, 4)
-            .reshape(experts, part, both)
-        )
-    grad_gain_ffn = jnp.sum(w_gate_up.astype(F32) * grad_gate_up, axis=(0, 2)) + jnp.sum(
-        w_router.astype(F32) * grad_router_base, axis=1
-    )
+    grad_gain_ffn = grad_gain_ffn + jnp.sum(w_router.astype(F32) * grad_router_base, axis=1)
     return (
         mixed_exact.astype(BF),
         loss_value,
         grad_tokens,
         grad_gain_attn,
-        grad_query_base * gain_one,
-        grad_keyval_base * gain_one,
+        grad_query,
+        grad_keyval,
         grad_out,
         grad_gain_ffn,
         grad_router_base * gain_two,
-        grad_gate_up * gain_two,
+        grad_gate_up,
         grad_down,
     )
 

time: 551 us -> 615 us (1.12)
  starting transfers between devices: 86.9 us -> 138 us
  blocking collectives: 26 us -> 0 us
  other arithmetic: 65 us -> 77 us
  local copies, waits for them, and re-layouts: 59.2 us -> 69 us
  Pallas kernels: 44.1 us -> 53.8 us
    ppermute x30 -> x24, waiting for transfers between devices: 127 us -> 91.3 us  [shift(): lax.ppermute(block, 'seq', [(i, (i + step) % count) for i in range(count)])]
    ppermute x0 -> x12, starting transfers between devices: none -> 34.1 us  [the longest x6 25.8 us: relay_step(): lax.ppermute(up, 'seq', [(i, i + 1) for i in range(count - 1)])]
    ppermute x31, waiting for transfers between devices: 29.9 us -> 59.2 us  [hop(): return lax.ppermute(block, 'fsdp', [(i, i ^ mask) for i in range(count)])]
    ppermute x0 -> x12, waiting for transfers between devices: none -> 27.2 us  [the longest x6 18.2 us: relay_step(): lax.ppermute(up, 'seq', [(i, i + 1) for i in range(count - 1)])]
    all_to_all x1, waiting for transfers between devices: 16.2 us -> 0.01 us  [local(): lax.all_to_all(grad_q.astype(BF), 'seq', split_axis=0, concat_axis=1, til...]
    all_to_all x1 -> x0, blocking collectives: 16 us -> none  [local(): lax.all_to_all(attended_low, 'seq', split_axis=0, concat_axis=1, tiled=True)]
    dynamic_update_slice x0 -> x11, other arithmetic: none -> 14.9 us  [the longest x4 8.05 us: place_gate_up(): result = lax.dynamic_update_index_in_dim(result, base * gain, expert, 0)]
    ppermute x30 -> x24, starting transfers between devices: 51.3 us -> 64.7 us  [shift(): lax.ppermute(block, 'seq', [(i, (i + step) % count) for i in range(count)])]
  transfers between devices with their start and end apart: 70 -> 76, of which waited for: 26 -> 26; matrix products, arithmetic and copies ran while one was open for 24% -> 26% of each run, Pallas kernels for 8% -> 9%
where the time goes in v4:
time: 615 us; the launch traced here: 605 us
  waiting for transfers between devices  191 us (31%)
  starting transfers between devices  138 us (22%)
  other arithmetic  77 us (13%)
  local copies, waits for them, and re-layouts  69 us (11%)
  matrix products  55 us (9%)
  Pallas kernels  53.8 us (9%)
  between operations  21.1 us (3%)
    ppermute x24, waiting for transfers between devices, shift(): lax.ppermute(block, 'seq', [(i, (i + step) % count) for i in range(count)])  91.3 us
    ppermute x24, starting transfers between devices, shift(): lax.ppermute(block, 'seq', [(i, (i + step) % count) for i in range(count)])  64.7 us
    ppermute x31, waiting for transfers between devices, hop(): return lax.ppermute(block, 'fsdp', [(i, i ^ mask) for i in range(count)])  59.2 us
    pallas_call x2, Pallas kernels, flash_backward(): pl.pallas_call(functools.partial(backward_kernel, shards, seqs, rows, g,...  32.7 us
    ppermute x6, starting transfers between devices, relay_step(): lax.ppermute(up, 'seq', [(i, i + 1) for i in range(count - 1)])  25.8 us
    ppermute x31, starting transfers between devices, hop(): return lax.ppermute(block, 'fsdp', [(i, i ^ mask) for i in range(count)])  23.3 us
    dot_general x10, matrix products, dot(): return jnp.dot(a, b, preferred_element_type=F32)  21.8 us
    pallas_call x1, Pallas kernels, flash_forward(): pl.pallas_call(functools.partial(forward_kernel, shards, seqs, rows, loca...  21.1 us
  transfers between devices with their start and end apart: 76, of which 26 were waited for; matrix products, arithmetic and copies ran while one was open for 26% of the time, Pallas kernels for 9%

profile of v4, /device:TPU:0, one launch (start us, length us, event | category | flops | bytes accessed | tf_op | source)
XLA Modules:
  0.0 604.6 jit_solution(17798605579942165105)
XLA Ops:
  12.0 5.0 collective-permute-start
  18.3 7.6 %collective-permute-done = bf16[136,1536]{1,0:T(8,128)(2,1)S(1)} collective-permute-done((bf16[136,1536]{1,0:T(8,128)(2,1)S(1)}, bf16[136,1536]{1,0:T(8,128)(2,1)S(1)}, u32[]{:S(2)}, u32[]{:S(2)}) %collective-permute-start) | collective-permute-done | bytes 417824 | tf_op jit(solution)/shard_map/ppermute | solution.py:249
  25.9 5.2 collective-permute-start.1
  32.3 6.0 collective-permute-done.1
  38.4 5.0 collective-permute-done.4
  53.1 4.7 collective-permute-done.2
  57.9 4.0 collective-permute-done.5
  70.8 11.7 %collective-permute-done.6.refs_1_ = bf16[528,256]{1,0:T(8,128)(2,1)S(1)} collective-permute-done((bf16[528,256]{1,0:T(8,128)(2,1)}, bf16[528,256]{1,0:T(8,128)(2,1)S(1)}, u32[]{:S(2)}, u32[]{:S(2)}) %collective-permute-start.6) | collective-permute-done | bytes 270368 | tf_op jit(solution)/shard_map/ppermute | solution.py:268
  85.7 6.3 %collective-permute-done.8.refs_3_ = bf16[528,256]{1,0:T(8,128)(2,1)} collective-permute-done((bf16[528,256]{1,0:T(8,128)(2,1)}, bf16[528,256]{1,0:T(8,128)(2,1)}, u32[]{:S(2)}, u32[]{:S(2)}) %collective-permute-start.8) | collective-permute-done | bytes 270368 | tf_op jit(solution)/shard_map/ppermute | solution.py:268
  101.9 21.1 %shard_map.221 = (bf16[512,384]{1,0:T(8,128)(2,1)}, f32[512,384]{1,0:T(8,128)}, f32[512,384]{1,0:T(8,128)}) custom-call(bf16[528,256]{1,0:T(8,128)(2,1)} %maximum_maximum_fusion.refs_0_, bf16[528,256]{1,0:T(8,128)(2,1)} %copy-done.90, bf16[528,256]{1,0:T(8,128)(2,1)} %collective-permute-done.7.refs_2_, bf16[528,256]{1,0:T(8,128)(2,1)} %collective-permute-done.8.refs_3_, ...), custom_call_target="tpu_custom_call" | custom-call | flops 6442450944 | bytes 8388608 | tf_op jit(solution)/shard_map/pallas_call | solution.py:112
  128.6 12.3 %all-to-all-done = bf16[4,128,384]{1,2,0:T(8,128)(2,1)S(1)} async-done(((bf16[4,128,384]{1,2,0:T(8,128)(2,1)}), bf16[4,128,384]{1,2,0:T(8,128)(2,1)S(1)}, u32[]{:S(2)}, u32[]{:S(2)}) %all-to-all-start) | async-done | bytes 393248 | tf_op jit(solution)/shard_map/all_to_all | solution.py:484
  140.9 4.2 multiply_reduce_fusion.5
  154.5 4.3 collective-permute-done.13
  158.8 11.3 %collective-permute-done.14 = bf16[96,1536]{1,0:T(8,128)(2,1)} collective-permute-done((bf16[96,1536]{1,0:T(8,128)(2,1)}, bf16[96,1536]{1,0:T(8,128)(2,1)}, u32[]{:S(2)}, u32[]{:S(2)}) %collective-permute-start.14) | collective-permute-done | bytes 294944 | tf_op jit(solution)/shard_map/ppermute | solution.py:235
  172.3 5.7 fusion.2
  179.7 3.6 convolution_convert_fusion.6
  184.2 4.7 collective-permute-start.16
  188.9 3.5 collective-permute-start.17
  197.0 19.7 %collective-permute-done.17 = bf16[96,1536]{1,0:T(8,128)(2,1)S(1)} collective-permute-done((bf16[96,1536]{1,0:T(8,128)(2,1)}, bf16[96,1536]{1,0:T(8,128)(2,1)S(1)}, u32[]{:S(2)}, u32[]{:S(2)}) %collective-permute-start.17) | collective-permute-done | bytes 294944 | tf_op jit(solution)/shard_map/ppermute | solution.py:235
  221.9 4.0 collective-permute-start.21
  228.3 5.7 collective-permute-done.19
  234.0 9.1 %collective-permute-done.20 = bf16[96,1536]{1,0:T(8,128)(2,1)} collective-permute-done((bf16[96,1536]{1,0:T(8,128)(2,1)}, bf16[96,1536]{1,0:T(8,128)(2,1)}, u32[]{:S(2)}, u32[]{:S(2)}) %collective-permute-start.20) | collective-permute-done | bytes 294944 | tf_op jit(solution)/shard_map/ppermute | solution.py:235
  245.4 4.9 multiply_convert_fusion.2
  250.5 5.5 fusion.8
  257.3 3.7 convolution_convert_fusion
  264.5 7.7 %collective-permute-start.22 = (bf16[96,1536]{1,0:T(8,128)(2,1)S(1)}, bf16[96,1536]{1,0:T(8,128)(2,1)S(1)}, u32[]{:S(2)}, u32[]{:S(2)}) collective-permute-start(bf16[96,1536]{1,0:T(8,128)(2,1)S(1)} %get-tuple-element.239), channel_id=1, source_target_pairs={{0,24},{8,0},{16,8},{24,16},{1,25},{9,1},{17,9},{25,17},{2,26},{10... | collective-permute-start | bytes 884744 | tf_op jit(solution)/shard_map/ppermute | solution.py:235
  273.4 6.2 %collective-permute-done.22 = bf16[96,1536]{1,0:T(8,128)(2,1)S(1)} collective-permute-done((bf16[96,1536]{1,0:T(8,128)(2,1)S(1)}, bf16[96,1536]{1,0:T(8,128)(2,1)S(1)}, u32[]{:S(2)}, u32[]{:S(2)}) %collective-permute-start.22) | collective-permute-done | bytes 294944 | tf_op jit(solution)/shard_map/ppermute | solution.py:235
  279.6 18.6 %collective-permute-done.23 = bf16[96,1536]{1,0:T(8,128)(2,1)S(1)} collective-permute-done((bf16[96,1536]{1,0:T(8,128)(2,1)S(1)}, bf16[96,1536]{1,0:T(8,128)(2,1)S(1)}, u32[]{:S(2)}, u32[]{:S(2)}) %collective-permute-start.23) | collective-permute-done | bytes 294944 | tf_op jit(solution)/shard_map/ppermute | solution.py:235
  315.6 6.9 %collective-permute-done.27 = bf16[192,1024]{1,0:T(8,128)(2,1)S(1)} collective-permute-done((bf16[192,1024]{1,0:T(8,128)(2,1)S(1)}, bf16[192,1024]{1,0:T(8,128)(2,1)S(1)}, u32[]{:S(2)}, u32[]{:S(2)}) %collective-permute-start.27) | collective-permute-done | bytes 393248 | tf_op jit(solution)/shard_map/ppermute | solution.py:268
  323.6 8.5 %collective-permute-done.28 = bf16[192,1024]{1,0:T(8,128)(2,1)S(1)} collective-permute-done((bf16[192,1024]{1,0:T(8,128)(2,1)S(1)}, bf16[192,1024]{1,0:T(8,128)(2,1)S(1)}, u32[]{:S(2)}, u32[]{:S(2)}) %collective-permute-start.28) | collective-permute-done | bytes 393248 | tf_op jit(solution)/shard_map/ppermute | solution.py:268
  334.5 4.1 all-to-all-start.1
  343.0 4.8 collective-permute-done.30
  347.8 17.7 %collective-permute-done.31 = bf16[192,2048]{1,0:T(8,128)(2,1)} collective-permute-done((bf16[192,2048]{1,0:T(8,128)(2,1)}, bf16[192,2048]{1,0:T(8,128)(2,1)}, u32[]{:S(2)}, u32[]{:S(2)}) %collective-permute-start.31) | collective-permute-done | bytes 786464 | tf_op jit(solution)/shard_map/ppermute | solution.py:268
  380.4 16.2 %shard_map.222 = (f32[512,192]{1,0:T(8,128)}, bf16[4,512,128]{2,1,0:T(8,128)(2,1)}, bf16[4,512,128]{2,1,0:T(8,128)(2,1)}) custom-call(bf16[528,256]{1,0:T(8,128)(2,1)} %maximum_maximum_fusion.refs_0_, bf16[528,256]{1,0:T(8,128)(2,1)} %copy-done.90, bf16[528,256]{1,0:T(8,128)(2,1)} %collective-permute-done.7.refs_2_, ...), custom_call_target="tpu_custom_call" | custom-call | flops 16106127360 | bytes 8388608 | tf_op jit(solution)/shard_map/pallas_call | solution.py:210
  396.6 16.4 %shard_map.223 = (f32[512,192]{1,0:T(8,128)}, bf16[4,512,128]{2,1,0:T(8,128)(2,1)}, bf16[4,512,128]{2,1,0:T(8,128)(2,1)}) custom-call(bf16[528,256]{1,0:T(8,128)(2,1)} %maximum_maximum_fusion.refs_0_, bf16[528,256]{1,0:T(8,128)(2,1)} %copy-done.90, bf16[528,256]{1,0:T(8,128)(2,1)} %collective-permute-done.7.refs_2_, ...), custom_call_target="tpu_custom_call" | custom-call | flops 16106127360 | bytes 8388608 | tf_op jit(solution)/shard_map/pallas_call | solution.py:210
  416.5 5.9 collective-permute-start.54
  426.8 4.1 all-to-all-start.2
  463.5 3.7 collective-permute-start.62
  472.9 4.7 collective-permute-done.62
  491.6 4.0 all-to-all-start.3
  495.6 3.5 broadcast_in_dim.121
  500.4 5.2 fusion.4
  506.3 3.8 collective-permute-start.66
  515.4 4.6 collective-permute-start.57
  530.9 3.5 fusion.50
  542.6 4.4 collective-permute-done.43
  547.0 9.4 %collective-permute-start.49 = (bf16[192,256]{1,0:T(8,128)(2,1)}, bf16[192,256]{1,0:T(8,128)(2,1)}, u32[]{:S(2)}, u32[]{:S(2)}) collective-permute-start(bf16[192,256]{1,0:T(8,128)(2,1)} %add_convert_fusion.19), channel_id=1, source_target_pairs={{0,8},{8,16},{16,24},{24,0},{1,9},{9,17},{17,25},{25,1},{2,10},{10... | collective-permute-start | bytes 294920 | tf_op jit(solution)/shard_map/ppermute | solution.py:235
  558.5 8.8 %collective-permute-start.51 = (bf16[192,256]{1,0:T(8,128)(2,1)}, bf16[192,256]{1,0:T(8,128)(2,1)}, u32[]{:S(2)}, u32[]{:S(2)}) collective-permute-start(bf16[192,256]{1,0:T(8,128)(2,1)} %add_convert_fusion.19), channel_id=1, source_target_pairs={{0,24},{8,0},{16,8},{24,16},{1,25},{9,1},{17,9},{25,17},{2,26},{10... | collective-permute-start | bytes 294920 | tf_op jit(solution)/shard_map/ppermute | solution.py:235
  (526 shorter events, 232.2 us)
Async XLA Ops:
  7.2 55.1 %all-gather.7.cloned.1.call-start = ((), (), s32[]{:S(2)}) async-start(), calls=%async_computation.4 | async-start | bytes 2211840 | tf_op jit(solution)/shard_map/all_gather | solution.py:413
  11.2 129.7 %all-gather.9.cloned.1.call-start = ((), (), s32[]{:S(2)}) async-start(), calls=%async_computation.5 | async-start | bytes 5308416 | tf_op jit(solution)/shard_map/all_gather | solution.py:443
  11.9 160.4 %all-gather.11.cloned.1.call-start = ((), (), s32[]{:S(2)}) async-start(), calls=%async_computation.6 | async-start | bytes 11059200 | tf_op jit(solution)/shard_map/all_gather | solution.py:458
  46.1 199.3 %all-gather.13.cloned.1.call-start = ((), (), s32[]{:S(2)}) async-start(), calls=%async_computation.7 | async-start | bytes 8847360 | tf_op jit(solution)/shard_map/all_gather | solution.py:463
  70.2 21.9 %collective-permute-start.8 = (bf16[528,256]{1,0:T(8,128)(2,1)}, bf16[528,256]{1,0:T(8,128)(2,1)}, u32[]{:S(2)}, u32[]{:S(2)}) collective-permute-start(bf16[528,256]{1,0:T(8,128)(2,1)} %maximum_maximum_fusion.refs_0_), channel_id=1, source_target_pairs={{0,6},{1,7},{2,4},{3,5},{4,2},{5,3},{6,0},{7,1},{8,14},{9,15},{10,... | collective-permute-start | bytes 811016 | tf_op jit(solution)/shard_map/ppermute | solution.py:268
  70.7 27.0 %collective-permute-start.9 = (bf16[528,256]{1,0:T(8,128)(2,1)}, bf16[528,256]{1,0:T(8,128)(2,1)}, u32[]{:S(2)}, u32[]{:S(2)}) collective-permute-start(bf16[528,256]{1,0:T(8,128)(2,1)} %maximum_maximum_fusion.refs_0_), channel_id=1, source_target_pairs={{0,1},{1,0},{2,3},{3,2},{4,5},{5,4},{6,7},{7,6},{8,9},{9,8},{10,11... | collective-permute-start | bytes 811016 | tf_op jit(solution)/shard_map/ppermute | solution.py:268
  146.7 23.4 %collective-permute-start.14 = (bf16[96,1536]{1,0:T(8,128)(2,1)}, bf16[96,1536]{1,0:T(8,128)(2,1)}, u32[]{:S(2)}, u32[]{:S(2)}) collective-permute-start(bf16[96,1536]{1,0:T(8,128)(2,1)} %get-tuple-element.250), channel_id=1, source_target_pairs={{0,16},{8,24},{16,0},{24,8},{1,17},{9,25},{17,1},{25,9},{2,18},{10... | collective-permute-start | bytes 884744 | tf_op jit(solution)/shard_map/ppermute | solution.py:235
  148.7 21.4 %collective-permute-start.15 = (bf16[96,1536]{1,0:T(8,128)(2,1)}, bf16[96,1536]{1,0:T(8,128)(2,1)}, u32[]{:S(2)}, u32[]{:S(2)}) collective-permute-start(bf16[96,1536]{1,0:T(8,128)(2,1)} %get-tuple-element.249), channel_id=1, source_target_pairs={{0,24},{8,0},{16,8},{24,16},{1,25},{9,1},{17,9},{25,17},{2,26},{10... | collective-permute-start | bytes 884744 | tf_op jit(solution)/shard_map/ppermute | solution.py:235
  188.9 27.8 %collective-permute-start.17 = (bf16[96,1536]{1,0:T(8,128)(2,1)}, bf16[96,1536]{1,0:T(8,128)(2,1)S(1)}, u32[]{:S(2)}, u32[]{:S(2)}) collective-permute-start(bf16[96,1536]{1,0:T(8,128)(2,1)} %get-tuple-element.246), channel_id=1, source_target_pairs={{0,16},{8,24},{16,0},{24,8},{1,17},{9,25},{17,1},{25,9},{2,18},{10... | collective-permute-start | bytes 884744 | tf_op jit(solution)/shard_map/ppermute | solution.py:235
  192.4 24.3 %collective-permute-start.18 = (bf16[96,1536]{1,0:T(8,128)(2,1)S(1)}, bf16[96,1536]{1,0:T(8,128)(2,1)}, u32[]{:S(2)}, u32[]{:S(2)}) collective-permute-start(bf16[96,1536]{1,0:T(8,128)(2,1)S(1)} %get-tuple-element.245), channel_id=1, source_target_pairs={{0,8},{8,16},{16,24},{24,0},{1,9},{9,17},{17,25},{25,1},{2,10},{10... | collective-permute-start | bytes 884744 | tf_op jit(solution)/shard_map/ppermute | solution.py:235
  221.9 21.2 %collective-permute-start.20 = (bf16[96,1536]{1,0:T(8,128)(2,1)}, bf16[96,1536]{1,0:T(8,128)(2,1)}, u32[]{:S(2)}, u32[]{:S(2)}) collective-permute-start(bf16[96,1536]{1,0:T(8,128)(2,1)} %get-tuple-element.242), channel_id=1, source_target_pairs={{0,16},{8,24},{16,0},{24,8},{1,17},{9,25},{17,1},{25,9},{2,18},{10... | collective-permute-start | bytes 884744 | tf_op jit(solution)/shard_map/ppermute | solution.py:235
  221.9 21.2 %collective-permute-start.21 = (bf16[96,1536]{1,0:T(8,128)(2,1)S(1)}, bf16[96,1536]{1,0:T(8,128)(2,1)}, u32[]{:S(2)}, u32[]{:S(2)}) collective-permute-start(bf16[96,1536]{1,0:T(8,128)(2,1)S(1)} %get-tuple-element.241), channel_id=1, source_target_pairs={{0,24},{8,0},{16,8},{24,16},{1,25},{9,1},{17,9},{25,17},{2,26},{10... | collective-permute-start | bytes 884744 | tf_op jit(solution)/shard_map/ppermute | solution.py:235
  261.4 37.5 %collective-permute-start.26 = (bf16[4,192,2048]{2,1,0:T(8,128)(2,1)S(1)}, bf16[4,192,2048]{2,1,0:T(8,128)(2,1)S(1)}, u32[]{:S(2)}, u32[]{:S(2)}) collective-permute-start(bf16[4,192,2048]{2,1,0:T(8,128)(2,1)S(1)} %dynamic-slice_bitcast_fusion), channel_id=1, source_target_pairs={{0,1},{1,0},{2,3},{3,2},{4,5},{5,4},{6,7},{7,6},{8,9},{9,8},{10,11... | collective-permute-start | bytes 9437192 | tf_op jit(solution)/shard_map/ppermute | solution.py:268
  264.4 33.9 %collective-permute-start.25 = (bf16[4,192,1024]{2,1,0:T(8,128)(2,1)S(1)}, bf16[4,192,1024]{2,1,0:T(8,128)(2,1)S(1)}, u32[]{:S(2)}, u32[]{:S(2)}) collective-permute-start(bf16[4,192,1024]{2,1,0:T(8,128)(2,1)S(1)} %dynamic-slice_bitcast_fusion.2), channel_id=1, source_target_pairs={{0,1},{1,0},{2,3},{3,2},{4,5},{5,4},{6,7},{7,6},{8,9},{9,8},{10,11... | collective-permute-start | bytes 4718600 | tf_op jit(solution)/shard_map/ppermute | solution.py:268
  272.2 26.1 %collective-permute-start.23 = (bf16[96,1536]{1,0:T(8,128)(2,1)S(1)}, bf16[96,1536]{1,0:T(8,128)(2,1)S(1)}, u32[]{:S(2)}, u32[]{:S(2)}) collective-permute-start(bf16[96,1536]{1,0:T(8,128)(2,1)S(1)} %get-tuple-element.238), channel_id=1, source_target_pairs={{0,16},{8,24},{16,0},{24,8},{1,17},{9,25},{17,1},{25,9},{2,18},{10... | collective-permute-start | bytes 884744 | tf_op jit(solution)/shard_map/ppermute | solution.py:235
  272.2 26.1 %collective-permute-start.24 = (bf16[96,1536]{1,0:T(8,128)(2,1)S(1)}, bf16[96,1536]{1,0:T(8,128)(2,1)S(1)}, u32[]{:S(2)}, u32[]{:S(2)}) collective-permute-start(bf16[96,1536]{1,0:T(8,128)(2,1)S(1)} %get-tuple-element.237), channel_id=1, source_target_pairs={{0,8},{8,16},{16,24},{24,0},{1,9},{9,17},{17,25},{25,1},{2,10},{10... | collective-permute-start | bytes 884744 | tf_op jit(solution)/shard_map/ppermute | solution.py:235
  310.4 61.1 %collective-permute-start.33 = (bf16[4,192,1536]{2,1,0:T(8,128)(2,1)}, bf16[4,192,1536]{2,1,0:T(8,128)(2,1)}, u32[]{:S(2)}, u32[]{:S(2)}) collective-permute-start(bf16[4,192,1536]{2,1,0:T(8,128)(2,1)} %dynamic-slice_bitcast_fusion.1), channel_id=1, source_target_pairs={{0,1},{1,0},{2,3},{3,2},{4,5},{5,4},{6,7},{7,6},{8,9},{9,8},{10,11... | collective-permute-start | bytes 7077896 | tf_op jit(solution)/shard_map/ppermute | solution.py:268
  312.0 20.1 %collective-permute-start.28 = (bf16[192,1024]{1,0:T(8,128)(2,1)S(1)}, bf16[192,1024]{1,0:T(8,128)(2,1)S(1)}, u32[]{:S(2)}, u32[]{:S(2)}) collective-permute-start(bf16[192,1024]{1,0:T(8,128)(2,1)S(1)} %get-tuple-element.220), channel_id=1, source_target_pairs={{0,4},{1,5},{2,6},{3,7},{4,0},{5,1},{6,2},{7,3},{8,12},{9,13},{10,... | collective-permute-start | bytes 1179656 | tf_op jit(solution)/shard_map/ppermute | solution.py:268
  313.1 20.4 %collective-permute-start.29 = (bf16[192,1024]{1,0:T(8,128)(2,1)S(1)}, bf16[192,1024]{1,0:T(8,128)(2,1)S(1)}, u32[]{:S(2)}, u32[]{:S(2)}) collective-permute-start(bf16[192,1024]{1,0:T(8,128)(2,1)S(1)} %get-tuple-element.219), channel_id=1, source_target_pairs={{0,6},{1,7},{2,4},{3,5},{4,2},{5,3},{6,0},{7,1},{8,14},{9,15},{10,... | collective-permute-start | bytes 1179656 | tf_op jit(solution)/shard_map/ppermute | solution.py:268
  314.1 33.7 %collective-permute-start.30 = (bf16[192,2048]{1,0:T(8,128)(2,1)}, bf16[192,2048]{1,0:T(8,128)(2,1)S(1)}, u32[]{:S(2)}, u32[]{:S(2)}) collective-permute-start(bf16[192,2048]{1,0:T(8,128)(2,1)} %get-tuple-element.215), channel_id=1, source_target_pairs={{0,2},{1,3},{2,0},{3,1},{4,6},{5,7},{6,4},{7,5},{8,10},{9,11},{10,... | collective-permute-start | bytes 2359304 | tf_op jit(solution)/shard_map/ppermute | solution.py:268
  322.5 43.0 %collective-permute-start.31 = (bf16[192,2048]{1,0:T(8,128)(2,1)}, bf16[192,2048]{1,0:T(8,128)(2,1)}, u32[]{:S(2)}, u32[]{:S(2)}) collective-permute-start(bf16[192,2048]{1,0:T(8,128)(2,1)} %get-tuple-element.214), channel_id=1, source_target_pairs={{0,4},{1,5},{2,6},{3,7},{4,0},{5,1},{6,2},{7,3},{8,12},{9,13},{10,... | collective-permute-start | bytes 2359304 | tf_op jit(solution)/shard_map/ppermute | solution.py:268
  332.1 33.4 %collective-permute-start.32 = (bf16[192,2048]{1,0:T(8,128)(2,1)}, bf16[192,2048]{1,0:T(8,128)(2,1)}, u32[]{:S(2)}, u32[]{:S(2)}) collective-permute-start(bf16[192,2048]{1,0:T(8,128)(2,1)} %get-tuple-element.213), channel_id=1, source_target_pairs={{0,6},{1,7},{2,4},{3,5},{4,2},{5,3},{6,0},{7,1},{8,14},{9,15},{10,... | collective-permute-start | bytes 2359304 | tf_op jit(solution)/shard_map/ppermute | solution.py:268
  334.5 45.9 %all-to-all-start.1 = ((bf16[128,4,384]{2,0,1:T(8,128)(2,1)}), bf16[128,4,384]{2,0,1:T(8,128)(2,1)}, u32[]{:S(2)}, u32[]{:S(2)}) async-start(bf16[128,4,384]{2,0,1:T(8,128)(2,1)} %bitcast.250), calls=%async_computation.1 | async-start | bytes 786432 | tf_op jit(solution)/shard_map/all_to_all | solution.py:555
  338.6 131.4 %all-gather.15.cloned.1.call-start = ((), (), s32[]{:S(2)}) async-start(), calls=%async_computation.8 | async-start | bytes 1966080 | tf_op jit(solution)/shard_map/all_gather | solution.py:558
  367.5 49.0 %collective-permute-start.52 = (bf16[192,2048]{1,0:T(8,128)(2,1)S(1)}, bf16[192,2048]{1,0:T(8,128)(2,1)S(1)}, u32[]{:S(2)}, u32[]{:S(2)}) collective-permute-start(bf16[192,2048]{1,0:T(8,128)(2,1)S(1)} %add_convert_fusion), channel_id=1, source_target_pairs={{0,8},{8,16},{16,24},{1,9},{9,17},{17,25},{2,10},{10,18},{18,26},{... | collective-permute-start | bytes 2359304 | tf_op jit(solution)/shard_map/ppermute | solution.py:249
  369.9 46.6 %collective-permute-start.53 = (bf16[192,2048]{1,0:T(8,128)(2,1)S(1)}, bf16[192,2048]{1,0:T(8,128)(2,1)}, u32[]{:S(2)}, u32[]{:S(2)}) collective-permute-start(bf16[192,2048]{1,0:T(8,128)(2,1)S(1)} %add_convert_fusion), channel_id=1, source_target_pairs={{8,0},{16,8},{24,16},{9,1},{17,9},{25,17},{10,2},{18,10},{26,18},{... | collective-permute-start | bytes 2359304 | tf_op jit(solution)/shard_map/ppermute | solution.py:250
  375.0 58.7 %collective-permute-start.58 = (bf16[192,1536]{1,0:T(8,128)(2,1)}, bf16[192,1536]{1,0:T(8,128)(2,1)}, u32[]{:S(2)}, u32[]{:S(2)}) collective-permute-start(bf16[192,1536]{1,0:T(8,128)(2,1)} %get-tuple-element.218), channel_id=1, source_target_pairs={{0,2},{1,3},{2,0},{3,1},{4,6},{5,7},{6,4},{7,5},{8,10},{9,11},{10,... | collective-permute-start | bytes 1769480 | tf_op jit(solution)/shard_map/ppermute | solution.py:268
  375.5 59.6 %collective-permute-start.59 = (bf16[192,1536]{1,0:T(8,128)(2,1)}, bf16[192,1536]{1,0:T(8,128)(2,1)}, u32[]{:S(2)}, u32[]{:S(2)}) collective-permute-start(bf16[192,1536]{1,0:T(8,128)(2,1)} %get-tuple-element.217), channel_id=1, source_target_pairs={{0,4},{1,5},{2,6},{3,7},{4,0},{5,1},{6,2},{7,3},{8,12},{9,13},{10,... | collective-permute-start | bytes 1769480 | tf_op jit(solution)/shard_map/ppermute | solution.py:268
  376.8 58.4 %collective-permute-start.60 = (bf16[192,1536]{1,0:T(8,128)(2,1)}, bf16[192,1536]{1,0:T(8,128)(2,1)}, u32[]{:S(2)}, u32[]{:S(2)}) collective-permute-start(bf16[192,1536]{1,0:T(8,128)(2,1)} %get-tuple-element.216), channel_id=1, source_target_pairs={{0,6},{1,7},{2,4},{3,5},{4,2},{5,3},{6,0},{7,1},{8,14},{9,15},{10,... | collective-permute-start | bytes 1769480 | tf_op jit(solution)/shard_map/ppermute | solution.py:268
  416.5 18.7 %collective-permute-start.34 = (bf16[4,512,256]{2,1,0:T(8,128)(2,1)}, bf16[4,512,256]{2,1,0:T(8,128)(2,1)}, u32[]{:S(2)}, u32[]{:S(2)}) collective-permute-start(bf16[4,512,256]{2,1,0:T(8,128)(2,1)} %pad_maximum_fusion.5), channel_id=1, source_target_pairs={{0,1},{1,0},{2,3},{3,2},{4,5},{5,4},{6,7},{7,6},{8,9},{9,8},{10,11... | collective-permute-start | bytes 3145736 | tf_op jit(solution)/shard_map/ppermute | solution.py:268
  416.5 64.9 %collective-permute-start.54 = (bf16[192,2048]{1,0:T(8,128)(2,1)S(1)}, bf16[192,2048]{1,0:T(8,128)(2,1)}, u32[]{:S(2)}, u32[]{:S(2)}) collective-permute-start(bf16[192,2048]{1,0:T(8,128)(2,1)S(1)} %collective-permute-done.52), channel_id=1, source_target_pairs={{0,8},{8,16},{16,24},{1,9},{9,17},{17,25},{2,10},{10,18},{18,26},{... | collective-permute-start | bytes 2359304 | tf_op jit(solution)/shard_map/ppermute | solution.py:249
  426.8 63.9 %all-to-all-start.2 = ((bf16[4,128,384]{1,2,0:T(8,128)(2,1)}), bf16[4,128,384]{1,2,0:T(8,128)(2,1)}, u32[]{:S(2)}, u32[]{:S(2)}) async-start(bf16[4,128,384]{1,2,0:T(8,128)(2,1)} %pad_maximum_fusion.6), calls=%async_computation.2 | async-start | bytes 786432 | tf_op jit(solution)/shard_map/all_to_all | solution.py:585
  433.8 51.3 %collective-permute-start.55 = (bf16[192,2048]{1,0:T(8,128)(2,1)}, bf16[192,2048]{1,0:T(8,128)(2,1)}, u32[]{:S(2)}, u32[]{:S(2)}) collective-permute-start(bf16[192,2048]{1,0:T(8,128)(2,1)} %collective-permute-done.53), channel_id=1, source_target_pairs={{8,0},{16,8},{24,16},{9,1},{17,9},{25,17},{10,2},{18,10},{26,18},{... | collective-permute-start | bytes 2359304 | tf_op jit(solution)/shard_map/ppermute | solution.py:250
  437.4 23.5 %collective-permute-start.39 = (bf16[512,256]{1,0:T(8,128)(2,1)}, bf16[512,256]{1,0:T(8,128)(2,1)}, u32[]{:S(2)}, u32[]{:S(2)}) collective-permute-start(bf16[512,256]{1,0:T(8,128)(2,1)} %get-tuple-element.228), channel_id=1, source_target_pairs={{0,2},{1,3},{2,0},{3,1},{4,6},{5,7},{6,4},{7,5},{8,10},{9,11},{10,... | collective-permute-start | bytes 786440 | tf_op jit(solution)/shard_map/ppermute | solution.py:268
  437.9 25.6 %collective-permute-start.40 = (bf16[512,256]{1,0:T(8,128)(2,1)}, bf16[512,256]{1,0:T(8,128)(2,1)}, u32[]{:S(2)}, u32[]{:S(2)}) collective-permute-start(bf16[512,256]{1,0:T(8,128)(2,1)} %get-tuple-element.227), channel_id=1, source_target_pairs={{0,4},{1,5},{2,6},{3,7},{4,0},{5,1},{6,2},{7,3},{8,12},{9,13},{10,... | collective-permute-start | bytes 786440 | tf_op jit(solution)/shard_map/ppermute | solution.py:268
  471.7 49.7 %collective-permute-start.38 = (bf16[192,512]{0,1:T(8,128)(2,1)}, bf16[192,512]{0,1:T(8,128)(2,1)}, u32[]{:S(2)}, u32[]{:S(2)}) collective-permute-start(bf16[192,512]{0,1:T(8,128)(2,1)} %fusion.83), channel_id=1, source_target_pairs={{0,6},{1,7},{2,4},{3,5},{4,2},{5,3},{6,0},{7,1},{8,14},{9,15},{10,... | collective-permute-start | bytes 589832 | tf_op jit(solution)/shard_map/ppermute | solution.py:268
  477.7 44.6 %collective-permute-start.37 = (bf16[192,512]{0,1:T(8,128)(2,1)}, bf16[192,512]{0,1:T(8,128)(2,1)}, u32[]{:S(2)}, u32[]{:S(2)}) collective-permute-start(bf16[192,512]{0,1:T(8,128)(2,1)} %fusion.82), channel_id=1, source_target_pairs={{0,4},{1,5},{2,6},{3,7},{4,0},{5,1},{6,2},{7,3},{8,12},{9,13},{10,... | collective-permute-start | bytes 589832 | tf_op jit(solution)/shard_map/ppermute | solution.py:268
  478.2 45.6 %collective-permute-start.36 = (bf16[192,512]{0,1:T(8,128)(2,1)}, bf16[192,512]{0,1:T(8,128)(2,1)}, u32[]{:S(2)}, u32[]{:S(2)}) collective-permute-start(bf16[192,512]{0,1:T(8,128)(2,1)} %fusion.81), channel_id=1, source_target_pairs={{0,2},{1,3},{2,0},{3,1},{4,6},{5,7},{6,4},{7,5},{8,10},{9,11},{10,... | collective-permute-start | bytes 589832 | tf_op jit(solution)/shard_map/ppermute | solution.py:268
  482.4 23.9 %collective-permute-start.64 = (bf16[192,384]{1,0:T(8,128)(2,1)}, bf16[192,384]{1,0:T(8,128)(2,1)}, u32[]{:S(2)}, u32[]{:S(2)}) collective-permute-start(bf16[192,384]{1,0:T(8,128)(2,1)} %get-tuple-element.201), channel_id=1, source_target_pairs={{0,8},{8,16},{16,24},{24,0},{1,9},{9,17},{17,25},{25,1},{2,10},{10... | collective-permute-start | bytes 442376 | tf_op jit(solution)/shard_map/ppermute | solution.py:235
  485.0 26.0 %collective-permute-start.65 = (bf16[192,384]{1,0:T(8,128)(2,1)}, bf16[192,384]{1,0:T(8,128)(2,1)}, u32[]{:S(2)}, u32[]{:S(2)}) collective-permute-start(bf16[192,384]{1,0:T(8,128)(2,1)} %get-tuple-element.201), channel_id=1, source_target_pairs={{0,16},{8,24},{16,0},{24,8},{1,17},{9,25},{17,1},{25,9},{2,18},{10... | collective-permute-start | bytes 442376 | tf_op jit(solution)/shard_map/ppermute | solution.py:235
  491.6 39.3 %all-to-all-start.3 = ((bf16[4,128,256]{1,2,0:T(8,128)(2,1)}), bf16[4,128,256]{1,2,0:T(8,128)(2,1)}, u32[]{:S(2)}, u32[]{:S(2)}) async-start(bf16[4,128,256]{1,2,0:T(8,128)(2,1)} %copy.149), calls=%async_computation.3 | async-start | bytes 524288 | tf_op jit(solution)/shard_map/all_to_all | solution.py:603
  513.1 68.2 %collective-permute-start.56 = (bf16[192,2048]{1,0:T(8,128)(2,1)}, bf16[192,2048]{1,0:T(8,128)(2,1)S(1)}, u32[]{:S(2)}, u32[]{:S(2)}) collective-permute-start(bf16[192,2048]{1,0:T(8,128)(2,1)} %collective-permute-done.55), channel_id=1, source_target_pairs={{8,0},{16,8},{24,16},{9,1},{17,9},{25,17},{10,2},{18,10},{26,18},{... | collective-permute-start | bytes 2359304 | tf_op jit(solution)/shard_map/ppermute | solution.py:250
  515.4 69.7 %collective-permute-start.57 = (bf16[192,2048]{1,0:T(8,128)(2,1)}, bf16[192,2048]{1,0:T(8,128)(2,1)S(1)}, u32[]{:S(2)}, u32[]{:S(2)}) collective-permute-start(bf16[192,2048]{1,0:T(8,128)(2,1)} %collective-permute-done.54), channel_id=1, source_target_pairs={{0,8},{8,16},{16,24},{1,9},{9,17},{17,25},{2,10},{10,18},{18,26},{... | collective-permute-start | bytes 2359304 | tf_op jit(solution)/shard_map/ppermute | solution.py:249
  536.4 21.1 %collective-permute-start.44 = (bf16[192,512]{0,1:T(8,128)(2,1)S(1)}, bf16[192,512]{0,1:T(8,128)(2,1)S(1)}, u32[]{:S(2)}, u32[]{:S(2)}) collective-permute-start(bf16[192,512]{0,1:T(8,128)(2,1)S(1)} %select_select_fusion), channel_id=1, source_target_pairs={{0,16},{8,24},{16,0},{24,8},{1,17},{9,25},{17,1},{25,9},{2,18},{10... | collective-permute-start | bytes 589832 | tf_op jit(solution)/shard_map/ppermute | solution.py:235
  538.1 20.5 %collective-permute-start.45 = (bf16[192,512]{0,1:T(8,128)(2,1)S(1)}, bf16[192,512]{0,1:T(8,128)(2,1)S(1)}, u32[]{:S(2)}, u32[]{:S(2)}) collective-permute-start(bf16[192,512]{0,1:T(8,128)(2,1)S(1)} %select_select_fusion), channel_id=1, source_target_pairs={{0,24},{8,0},{16,8},{24,16},{1,25},{9,1},{17,9},{25,17},{2,26},{10... | collective-permute-start | bytes 589832 | tf_op jit(solution)/shard_map/ppermute | solution.py:235
  547.0 41.0 %collective-permute-start.49 = (bf16[192,256]{1,0:T(8,128)(2,1)}, bf16[192,256]{1,0:T(8,128)(2,1)}, u32[]{:S(2)}, u32[]{:S(2)}) collective-permute-start(bf16[192,256]{1,0:T(8,128)(2,1)} %add_convert_fusion.19), channel_id=1, source_target_pairs={{0,8},{8,16},{16,24},{24,0},{1,9},{9,17},{17,25},{25,1},{2,10},{10... | collective-permute-start | bytes 294920 | tf_op jit(solution)/shard_map/ppermute | solution.py:235
  557.6 30.5 %collective-permute-start.50 = (bf16[192,256]{1,0:T(8,128)(2,1)}, bf16[192,256]{1,0:T(8,128)(2,1)}, u32[]{:S(2)}, u32[]{:S(2)}) collective-permute-start(bf16[192,256]{1,0:T(8,128)(2,1)} %add_convert_fusion.19), channel_id=1, source_target_pairs={{0,16},{8,24},{16,0},{24,8},{1,17},{9,25},{17,1},{25,9},{2,18},{10... | collective-permute-start | bytes 294920 | tf_op jit(solution)/shard_map/ppermute | solution.py:235
  558.5 29.5 %collective-permute-start.51 = (bf16[192,256]{1,0:T(8,128)(2,1)}, bf16[192,256]{1,0:T(8,128)(2,1)}, u32[]{:S(2)}, u32[]{:S(2)}) collective-permute-start(bf16[192,256]{1,0:T(8,128)(2,1)} %add_convert_fusion.19), channel_id=1, source_target_pairs={{0,24},{8,0},{16,8},{24,16},{1,25},{9,1},{17,9},{25,17},{2,26},{10... | collective-permute-start | bytes 294920 | tf_op jit(solution)/shard_map/ppermute | solution.py:235
  (123 other events, 1096.0 us)
Sparse Core Ops, SparseCore 0:
  11.3 30.0 all-gather.6
  43.2 50.5 all-gather.8
  96.3 58.9 all-gather.10
  157.6 52.1 all-gather.12
  341.2 42.2 all-gather.14

commit v5 on v4

--- a/solution.py
+++ b/solution.py
@@ -4,6 +4,7 @@
 import jax.numpy as jnp
 from jax import lax
 from jax.experimental import pallas as pl
+from jax.experimental.layout import Layout, with_layout_constraint
 from jax.experimental.pallas import tpu as pltpu
 from jax.sharding import PartitionSpec as P
 
@@ -119,7 +120,7 @@
             pltpu.VMEM((local_kv, stack, 2 * HD), F32),
             pltpu.VMEM((local_kv, stack, 2 * HD), F32),
         ],
-        compiler_params=pltpu.CompilerParams(vmem_limit_bytes=60 * 1024 * 1024),
+        compiler_params=pltpu.CompilerParams(vmem_limit_bytes=24 * 1024 * 1024),
         cost_estimate=pl.CostEstimate(
             flops=8 * seqs * seqs * shards * rows * rows * local_kv * groups * HD,
             bytes_accessed=8 * 1024 * 1024,
@@ -129,11 +130,11 @@
 
 
 def backward_kernel(shards, seqs, rows, g, groups, *refs):
-    kv_refs = refs[:shards]
+    kv_refs = [refs[0].at[p] for p in range(shards)]
     (
         q_ref, bias_ref, grad_ref, exact_ref, lse_ref, grad_q_ref, near_ref, far_ref,
         pair_ref, pair_t_ref, lse_wide, delta_wide, acc_q, acc_kv,
-    ) = refs[shards:]
+    ) = refs[1:]
     zk = pl.program_id(0)
     stack = groups * rows
     zeros = jnp.zeros((rows, HD), BF)
@@ -198,11 +199,11 @@
             grad_q_ref[pl.ds(zq * rows, rows), :] = jnp.concatenate(parts, axis=1)
 
 
-def flash_backward(q, kv_blocks, bias, grad, exact, lse, seqs, rows, g, groups):
-    shards = len(kv_blocks)
+def flash_backward(q, kv_all, bias, grad, exact, lse, seqs, rows, g, groups):
+    shards = kv_all.shape[0]
     q_cols = q.shape[1]
     stack = groups * rows
-    kv_spec = pl.BlockSpec(kv_blocks[0].shape, lambda i: (0, 0))
+    kv_spec = pl.BlockSpec(kv_all.shape, lambda i: (0, 0, 0))
     whole = pl.BlockSpec((seqs * rows, q_cols), lambda i: (0, 0))
     grad_q_shape = (seqs * rows, groups * HD)
     out_spec = pl.BlockSpec((shards // 2, rows, 2 * HD), lambda i: (0, i, 0))
@@ -210,7 +211,7 @@
     return pl.pallas_call(
         functools.partial(backward_kernel, shards, seqs, rows, g, groups),
         grid=(seqs,),
-        in_specs=[kv_spec] * shards
+        in_specs=[kv_spec]
         + [whole, pl.BlockSpec(bias.shape, lambda i: (0, 0, 0)), whole, whole, whole],
         out_specs=[pl.BlockSpec(grad_q_shape, lambda i: (0, 0)), out_spec, out_spec],
         out_shape=[jax.ShapeDtypeStruct(grad_q_shape, F32), out, out],
@@ -222,13 +223,13 @@
             pltpu.VMEM((seqs, stack, 2 * HD), F32),
             pltpu.VMEM((2 * HD, shards * rows), F32),
         ],
-        compiler_params=pltpu.CompilerParams(vmem_limit_bytes=60 * 1024 * 1024),
+        compiler_params=pltpu.CompilerParams(vmem_limit_bytes=28 * 1024 * 1024),
         cost_estimate=pl.CostEstimate(
             flops=40 * seqs * seqs * shards * rows * rows * groups * HD,
             bytes_accessed=8 * 1024 * 1024,
             transcendentals=seqs * seqs * shards * rows * rows * groups // 2,
         ),
-    )(*kv_blocks, q, bias, grad, exact, lse)
+    )(kv_all, q, bias, grad, exact, lse)
 
 
 def shift(block, count, step):
@@ -241,21 +242,6 @@
 
 def send_back(blocks, count):
     return [blocks[0]] + [shift(blocks[s], count, count - s) for s in range(1, count)]
-
-
-def relay_step(blocks, count):
-    up, down = blocks
-    return (
-        lax.ppermute(up, "seq", [(i, i + 1) for i in range(count - 1)]),
-        lax.ppermute(down, "seq", [(i + 1, i) for i in range(count - 1)]),
-    )
-
-
-def relay_blocks(steps, place):
-    count = len(steps)
-    return [steps[0][0]] + [
-        jnp.where(place >= s, steps[s][0], steps[count - s][1]) for s in range(1, count)
-    ]
 
 
 def from_relative(blocks, place):
@@ -313,6 +299,10 @@
     return high, (value - high.astype(F32)).astype(BF)
 
 
+def by_rows(array):
+    return with_layout_constraint(array, Layout(major_to_minor=tuple(range(array.ndim))))
+
+
 def after(values, *others):
     return lax.optimization_barrier((values, others))[0]
 
@@ -326,28 +316,17 @@
     return factor * grad_scaled - values * (factor * factor * factor * inner)
 
 
-def place_gate_up(blocks, weight, gain, place, *wait):
+def place_gate_up(base, weight, gain):
     experts, part, both = weight.shape
-    count = len(blocks)
-    split = count // experts
+    split = base.shape[0] // experts
+    base = base.astype(F32)
     if split > 1:
         base = (
-            from_relative(blocks, place)
-            .reshape(experts, split, part, 2, both // (2 * split))
+            base.reshape(experts, split, part, 2, both // (2 * split))
             .transpose(0, 2, 3, 1, 4)
             .reshape(experts, part, both)
-            .astype(F32)
         )
-        return base * gain, jnp.sum(weight.astype(F32) * base, axis=(0, 2))
-    result = jnp.zeros((experts, part, both), F32)
-    blocks = [after(blocks[0], *wait)] + blocks[1:]
-    sums = jnp.zeros((part,), F32)
-    for s in range(count):
-        expert = (place - s) % count
-        base = blocks[s].astype(F32)
-        result = lax.dynamic_update_index_in_dim(result, base * gain, expert, 0)
-        sums = sums + jnp.sum(take(weight, expert, 0).astype(F32) * base, axis=1)
-    return result, sums
+    return base * gain, jnp.sum(weight.astype(F32) * base, axis=(0, 2))
 
 
 def place_columns(blocks, place, finish):
@@ -412,11 +391,7 @@
     heads_shard = (heads_shard.astype(F32) * gain_one).astype(BF)
     heads_full = lax.all_gather(heads_shard, "fsdp", axis=0, tiled=True)
     valid_row = jnp.pad(valid.astype(BF).reshape(1, rows), ((0, 7), (0, width - rows)))
-    steps = [(jnp.concatenate([tokens, valid_row], axis=0),) * 2]
-    for unused in range(seqs - 1):
-        steps.append(relay_step(steps[-1], seqs))
-    midway = steps[seqs // 2]
-    token_blocks = relay_blocks(steps, z)
+    token_blocks = send_out([jnp.concatenate([tokens, valid_row], axis=0)] * seqs, seqs)
 
     valid_local = from_relative([each[rows : rows + 1, :rows] for each in token_blocks], z)
     token_blocks = [each[:rows] for each in token_blocks]
@@ -437,8 +412,8 @@
         axis=0,
     )
     kv_blocks = gather_shards(payload, shards)
-    late_query, late_keyval, late_out, late_router, late_gate_up, late_down = after(
-        (w_query, w_keyval, w_out, w_router, w_gate_up, w_down), midway
+    late_router, late_gate_up, late_down = after(
+        (w_router, w_gate_up, w_down), kv_blocks[: shards // 2]
     )
     out_full = lax.all_gather(w_out, "fsdp", axis=1, tiled=True)
     own_expert = take(late_gate_up, expert, 0)
@@ -459,10 +434,6 @@
     gate_up_full = expert_full[:, : 2 * piece]
     down_full = expert_full[:, 2 * piece : 3 * piece]
     router_full = expert_full[:, 3 * piece :]
-    attn_shard = jnp.concatenate([late_query, late_keyval], axis=1)
-    attn_full = lax.all_gather(
-        (attn_shard.astype(F32) * gain_one).astype(BF), "fsdp", axis=0, tiled=True
-    )
     order = jnp.asarray(
         [2 * m for m in range(shards // 2)] + [2 * m + 1 for m in range(shards // 2)], jnp.int32
     )
@@ -500,6 +471,11 @@
     dispatch = placed[:, 0] + placed[:, 1]
     placed_pairs = jnp.concatenate([placed[:, 0], placed[:, 1]], axis=0)
     sent_rows = dot_tn(dispatch, normed_two).astype(BF).reshape(seqs, CAP, width)
+    late_query, late_keyval = after((w_query, w_keyval), sent_rows)
+    attn_shard = jnp.concatenate([late_query, late_keyval], axis=1)
+    attn_full = lax.all_gather(
+        (attn_shard.astype(F32) * gain_one).astype(BF), "fsdp", axis=0, tiled=True
+    )
     expert_rows = jnp.concatenate(send_out([sent_rows[s] for s in range(seqs)], seqs))
     gate_up = dot(expert_rows, gate_up_full)
     gate_part = gate_up[:, :piece]
@@ -543,39 +519,41 @@
     grad_gate_up_halves = pair_halves(
         dot_tn(held_rows, held_gate_up).astype(BF), shard, shards
     )
-    grad_gate_up_sums = pair_sums(grad_gate_up_halves, shard)
-    grad_returned = after(grad_returned, grad_down_sums, grad_gate_up_sums)
+    grad_returned = after(grad_returned, grad_down_sums)
+    kv_all = jnp.stack(after(kv_blocks, grad_rows))
     tokens_local = from_relative(after(token_blocks, grad_rows), z).reshape(local_rows, width)
     factor_local = root(tokens_local.astype(F32))
+    ride_rows = jnp.concatenate([normed_two, jnp.ones((16, width), BF)], axis=0)
+    product_rows = jnp.concatenate([tokens_local, ride_rows], axis=0)
 
     grad_normed_two = dot(dispatch, grad_returned) + dot_nt(grad_logits, router_full)
     grad_residual = grad_mixed + root_back(residual, factor_two, grad_normed_two)
     grad_branch = grad_residual.astype(BF)
     grad_attended = dot_nt(grad_branch, out_full).astype(BF)
     head_grad = lax.all_to_all(grad_attended, "seq", split_axis=1, concat_axis=0, tiled=True)
-    grad_down_blocks = after(send_chips(grad_down_sums, shards), grad_attended)
+    grad_gate_up_sums = pair_sums(after(grad_gate_up_halves, grad_attended), shard)
+    grad_gate_up_blocks = send_chips(grad_gate_up_sums, shards)
+    grad_down_blocks = after(send_chips(grad_down_sums, shards), head_grad)
     grad_down_shard = total_of(grad_down_blocks).astype(BF)
     grad_down = lax.all_gather(grad_down_shard, "seq", axis=0, tiled=False)
-    grad_gate_up_blocks = after(send_chips(grad_gate_up_sums, shards), grad_attended)
-    grad_gate_up_steps = [(total_of(grad_gate_up_blocks).astype(BF),) * 2]
-    grad_gate_up_steps.append(relay_step(grad_gate_up_steps[0], seqs))
-
-    late_branch = after(grad_branch, grad_attended)
+
+    late_branch = after(grad_branch, head_grad)
     grad_out_halves = pair_halves(dot_tn(late_branch, attended).astype(BF), shard, shards)
-    grad_out_sums = pair_sums(grad_out_halves, shard)
 
     grad_q, near, far = [], [], []
-    held = after(head_grad, grad_down_shard, grad_gate_up_steps[0], grad_out_sums)
+    held = after(head_grad, grad_down_shard, grad_gate_up_sums, grad_out_halves)
     for g in range(local_kv):
         part_q, near_kv, far_kv = flash_backward(
-            head_queries, kv_blocks, bias, held, exact, lse, seqs, rows, g, groups
+            head_queries, kv_all, bias, held, exact, lse, seqs, rows, g, groups
         )
         grad_q.append(part_q * scale)
         near.append(near_kv)
         far.append(far_kv)
-        held = after(head_grad, part_q)
-    grad_gate_up_steps[-1] = after(grad_gate_up_steps[-1], part_q)
-    grad_gate_up_steps.append(relay_step(grad_gate_up_steps[-1], seqs))
+        if g == 0:
+            grad_gate_up_shard = total_of(after(grad_gate_up_blocks, part_q)).astype(BF)
+            grad_out_sums = pair_sums(after(grad_out_halves, part_q), shard)
+            held = after(head_grad, grad_gate_up_shard, grad_out_sums)
+    grad_gate_up_all = lax.all_gather(grad_gate_up_shard, "seq", axis=0, tiled=False)
     grad_out_blocks = after(send_chips(grad_out_sums, shards), part_q)
     near = jnp.concatenate(near, axis=2)
     there = hop(jnp.concatenate(far, axis=2), shards, 1)
@@ -591,15 +569,23 @@
     marks = jnp.where(lane == experts + 2 * (shard % 2), high, 0) + jnp.where(
         lane == experts + 1 + 2 * (shard % 2), low, 0
     )
-    router_product = dot_tn(normed_two, grad_logits).astype(BF) + marks.astype(BF)
-    query_product = jnp.concatenate(
-        [dot_tn(tokens_local, query_rhs).astype(BF), router_product], axis=1
-    )
+    ride_columns = jnp.concatenate(
+        [grad_logits, marks.astype(BF), jnp.zeros((15, LANES), BF)], axis=0
+    )
+    product_columns = jnp.concatenate(
+        [
+            jnp.pad(query_rhs, ((0, 0), (0, LANES))),
+            jnp.pad(ride_columns, ((0, 0), (q_cols, 0))),
+        ],
+        axis=0,
+    )
+    query_product = dot_tn(product_rows, product_columns).astype(BF)
     grad_query_sums = pair_sums(pair_halves(after(query_product, pairs), shard, shards), shard)
+    grad_query_sums = [
+        tuple(by_rows(part) for part in each) if isinstance(each, tuple) else by_rows(each)
+        for each in grad_query_sums
+    ]
     grad_kv = total_of(after(send_chips(pairs, shards), grad_query_sums))
-    while len(grad_gate_up_steps) < seqs:
-        grad_gate_up_steps[-1] = after(grad_gate_up_steps[-1], grad_kv)
-        grad_gate_up_steps.append(relay_step(grad_gate_up_steps[-1], seqs))
     token_grad_kv = lax.all_to_all(
         grad_kv.astype(BF), "seq", split_axis=0, concat_axis=1, tiled=True
     )
@@ -618,7 +604,8 @@
         plane_high.astype(F32),
         jnp.where(lanes == base_cols + 1, plane_low.astype(F32), grad_query_part),
     )
-    grad_query_blocks = send_out([grad_query_part.astype(BF)] * seqs, seqs)
+    grad_query_blocks = send_out([by_rows(grad_query_part.astype(BF))] * seqs, seqs)
+    grad_query_blocks = [by_rows(each) for each in grad_query_blocks]
     grad_out_part = total_of(after(grad_out_blocks, pairs))
     cut = grad_out_part.astype(BF)
     grad_out_own = jnp.zeros((part, q_cols), F32)
@@ -641,9 +628,7 @@
 
     grad_keyval_part = total_of(after(send_chips(grad_keyval_sums, shards), grad_query_part))
     grad_keyval_blocks = send_out([grad_keyval_part.astype(BF)] * seqs, seqs)
-    grad_gate_up, grad_gain_ffn = place_gate_up(
-        relay_blocks(grad_gate_up_steps, z), w_gate_up, gain_two, z, grad_kv
-    )
+    grad_gate_up, grad_gain_ffn = place_gate_up(grad_gate_up_all, w_gate_up, gain_two)
     grad_keyval_blocks = after(grad_keyval_blocks, grad_gate_up)
     sums = sum(
         jnp.sum(each[:, q_cols : q_cols + LANES].astype(F32).reshape(part, 1, LANES), axis=1)

time: 615 us -> 555 us (0.902)
  the two profiles are of different devices: /device:TPU:0 before, /device:TPU:12 now
where the time goes in v5:
time: 555 us; the launch traced here: 545 us
  waiting for transfers between devices  215 us (39%)
  starting transfers between devices  88 us (16%)
  other arithmetic  69.5 us (13%)
  matrix products  55.1 us (10%)
  local copies, waits for them, and re-layouts  51.7 us (9%)
  Pallas kernels  43.9 us (8%)
  between operations  21.3 us (4%)
    ppermute x27, waiting for transfers between devices, shift(): lax.ppermute(block, 'seq', [(i, (i + step) % count) for i in range(count)])  155 us
    ppermute x31, waiting for transfers between devices, hop(): return lax.ppermute(block, 'fsdp', [(i, i ^ mask) for i in range(count)])  44.5 us
    ppermute x27, starting transfers between devices, shift(): lax.ppermute(block, 'seq', [(i, (i + step) % count) for i in range(count)])  37.1 us
    ppermute x31, starting transfers between devices, hop(): return lax.ppermute(block, 'fsdp', [(i, i ^ mask) for i in range(count)])  25.9 us
    pallas_call x2, Pallas kernels, flash_backward(): pl.pallas_call(functools.partial(backward_kernel, shards, seqs, rows, g,...  25.5 us
    dot_general x10, matrix products, dot(): return jnp.dot(a, b, preferred_element_type=F32)  23.9 us
    unnamed x206, local copies, waits for them, and re-layouts  22.6 us
    dot_general x6, matrix products, dot_nt(): lax.dot_general(a, b, (((1,), (1,)), ((), ())), preferred_element_type=F32)  20.1 us
  transfers between devices with their start and end apart: 68, of which 27 were waited for; matrix products, arithmetic and copies ran while one was open for 26% of the time, Pallas kernels for 8%

profile of v5, /device:TPU:12, one launch (start us, length us, event | category | flops | bytes accessed | tf_op | source)
XLA Modules:
  0.0 544.9 jit_solution(9483685209871455582)
XLA Ops:
  14.0 2.6 collective-permute-start.1
  19.4 24.9 %collective-permute-done = bf16[136,1536]{1,0:T(8,128)(2,1)S(1)} collective-permute-done((bf16[136,1536]{1,0:T(8,128)(2,1)}, bf16[136,1536]{1,0:T(8,128)(2,1)S(1)}, u32[]{:S(2)}, u32[]{:S(2)}) %collective-permute-start) | collective-permute-done | bytes 417824 | tf_op jit(solution)/shard_map/ppermute | solution.py:236
  44.4 8.1 %collective-permute-done.2 = bf16[136,1536]{1,0:T(8,128)(2,1)S(1)} collective-permute-done((bf16[136,1536]{1,0:T(8,128)(2,1)}, bf16[136,1536]{1,0:T(8,128)(2,1)S(1)}, u32[]{:S(2)}, u32[]{:S(2)}) %collective-permute-start.2) | collective-permute-done | bytes 417824 | tf_op jit(solution)/shard_map/ppermute | solution.py:236
  60.8 5.9 %collective-permute-done.3.refs_1_ = bf16[528,256]{1,0:T(8,128)(2,1)S(1)} collective-permute-done((bf16[528,256]{1,0:T(8,128)(2,1)S(1)}, bf16[528,256]{1,0:T(8,128)(2,1)S(1)}, u32[]{:S(2)}, u32[]{:S(2)}) %collective-permute-start.3) | collective-permute-done | bytes 270368 | tf_op jit(solution)/shard_map/ppermute | solution.py:254
  66.7 7.4 %collective-permute-done.4.refs_2_ = bf16[528,256]{1,0:T(8,128)(2,1)S(1)} collective-permute-done((bf16[528,256]{1,0:T(8,128)(2,1)S(1)}, bf16[528,256]{1,0:T(8,128)(2,1)S(1)}, u32[]{:S(2)}, u32[]{:S(2)}) %collective-permute-start.4) | collective-permute-done | bytes 270368 | tf_op jit(solution)/shard_map/ppermute | solution.py:254
  83.6 18.4 %shard_map.221 = (bf16[512,384]{1,0:T(8,128)(2,1)S(1)}, f32[512,384]{1,0:T(8,128)S(1)}, f32[512,384]{1,0:T(8,128)S(1)}) custom-call(bf16[528,256]{1,0:T(8,128)(2,1)S(1)} %maximum_maximum_fusion.refs_0_, bf16[528,256]{1,0:T(8,128)(2,1)S(1)} %collective-permute-done.3.refs_1_, bf16[528,256]{1,0:T(8,128)(2,1)S(1)} %collective-permute-done.4.refs_2_, ...), custom_call_target="tpu_custom_call" | custom-call | flops 6442450944 | bytes 8388608 | tf_op jit(solution)/shard_map/pallas_call | solution.py:113
  104.7 5.2 all-to-all-start
  110.7 8.5 %all-to-all-done = bf16[4,128,384]{1,2,0:T(8,128)(2,1)S(1)} async-done(((bf16[4,128,384]{1,2,0:T(8,128)(2,1)}), bf16[4,128,384]{1,2,0:T(8,128)(2,1)S(1)}, u32[]{:S(2)}, u32[]{:S(2)}) %all-to-all-start) | async-done | bytes 393248 | tf_op jit(solution)/shard_map/all_to_all | solution.py:455
  119.3 5.3 multiply_reduce_fusion.5
  128.1 2.9 collective-permute-start.11
  135.5 12.0 %collective-permute-done.10 = bf16[96,1536]{1,0:T(8,128)(2,1)} collective-permute-done((bf16[96,1536]{1,0:T(8,128)(2,1)}, bf16[96,1536]{1,0:T(8,128)(2,1)}, u32[]{:S(2)}, u32[]{:S(2)}) %collective-permute-start.10) | collective-permute-done | bytes 294944 | tf_op jit(solution)/shard_map/ppermute | solution.py:236
  147.5 4.1 collective-permute-done.11
  151.6 3.9 collective-permute-done.12
  157.9 6.5 %fusion.3 = f32[384,2048]{1,0:T(8,128)S(1)} fusion(bf16[1536,3200]{1,0:T(8,128)(2,1)} %all-gather.13.cloned.1.call-done, bf16[96,1536]{1,0:T(8,128)(2,1)} %collective-permute-done.12, bf16[96,1536]{1,0:T(8,128)(2,1)} %collective-permute-done.11, bf16[96,1536]{1,0:T(8,128)(2,1)} %collective-permute-done.10, bf16[96,1536]{1,0:T(8,128)(2,1)} %get-tuple-element.284), kind=kOutput, calls=%fused_computation.7 | convolution fusion | flops 2420637696 | bytes 10616832 | tf_op jit(solution)/shard_map/dot_general | solution.py:23
  166.0 3.6 convolution_convert_fusion.6
  174.1 19.5 %collective-permute-done.13 = bf16[96,1536]{1,0:T(8,128)(2,1)} collective-permute-done((bf16[96,1536]{1,0:T(8,128)(2,1)}, bf16[96,1536]{1,0:T(8,128)(2,1)}, u32[]{:S(2)}, u32[]{:S(2)}) %collective-permute-start.13) | collective-permute-done | bytes 294944 | tf_op jit(solution)/shard_map/ppermute | solution.py:236
  199.8 3.1 collective-permute-start.16
  202.9 4.3 collective-permute-start.17
  209.7 13.7 %collective-permute-done.16 = bf16[96,1536]{1,0:T(8,128)(2,1)} collective-permute-done((bf16[96,1536]{1,0:T(8,128)(2,1)}, bf16[96,1536]{1,0:T(8,128)(2,1)}, u32[]{:S(2)}, u32[]{:S(2)}) %collective-permute-start.16) | collective-permute-done | bytes 294944 | tf_op jit(solution)/shard_map/ppermute | solution.py:236
  223.4 4.7 collective-permute-done.17
  232.8 4.9 multiply_convert_fusion.2
  237.8 5.5 %fusion.9 = bf16[384,1536]{1,0:T(8,128)(2,1)S(1)} fusion(bf16[1536,3200]{1,0:T(8,128)(2,1)} %all-gather.13.cloned.1.call-done, bf16[384,1024]{1,0:T(8,128)(2,1)S(1)} %get-tuple-element.258, bf16[384,1024]{1,0:T(8,128)(2,1)S(1)} %get-tuple-element.257), kind=kOutput, calls=%fused_computation.19 | convolution fusion | flops 2419654656 | bytes 9043968 | tf_op jit(solution)/shard_map/dot_general | solution.py:27
  248.0 2.8 collective-permute-start.21
  250.8 3.7 convolution_convert_fusion
  261.4 8.1 %collective-permute-done.19 = bf16[96,1536]{1,0:T(8,128)(2,1)S(1)} collective-permute-done((bf16[96,1536]{1,0:T(8,128)(2,1)S(1)}, bf16[96,1536]{1,0:T(8,128)(2,1)S(1)}, u32[]{:S(2)}, u32[]{:S(2)}) %collective-permute-start.19) | collective-permute-done | bytes 294944 | tf_op jit(solution)/shard_map/ppermute | solution.py:236
  269.4 4.4 collective-permute-done.21
  280.7 6.4 %all-to-all-start.1 = ((bf16[128,4,384]{2,0,1:T(8,128)(2,1)}), bf16[128,4,384]{2,0,1:T(8,128)(2,1)S(1)}, u32[]{:S(2)}, u32[]{:S(2)}) async-start(bf16[128,4,384]{2,0,1:T(8,128)(2,1)} %bitcast.268), calls=%async_computation.1 | async-start | bytes 786432 | tf_op jit(solution)/shard_map/all_to_all | solution.py:533
  289.8 6.6 %all-to-all-done.1 = bf16[128,4,384]{2,0,1:T(8,128)(2,1)S(1)} async-done(((bf16[128,4,384]{2,0,1:T(8,128)(2,1)}), bf16[128,4,384]{2,0,1:T(8,128)(2,1)S(1)}, u32[]{:S(2)}, u32[]{:S(2)}) %all-to-all-start.1) | async-done | bytes 393248 | tf_op jit(solution)/shard_map/all_to_all | solution.py:533
  311.5 7.8 %collective-permute-done.23 = bf16[192,1024]{1,0:T(8,128)(2,1)S(1)} collective-permute-done((bf16[192,1024]{1,0:T(8,128)(2,1)S(1)}, bf16[192,1024]{1,0:T(8,128)(2,1)S(1)}, u32[]{:S(2)}, u32[]{:S(2)}) %collective-permute-start.23) | collective-permute-done | bytes 393248 | tf_op jit(solution)/shard_map/ppermute | solution.py:254
  319.3 8.6 %collective-permute-done.24 = bf16[192,1024]{1,0:T(8,128)(2,1)S(1)} collective-permute-done((bf16[192,1024]{1,0:T(8,128)(2,1)S(1)}, bf16[192,1024]{1,0:T(8,128)(2,1)S(1)}, u32[]{:S(2)}, u32[]{:S(2)}) %collective-permute-start.24) | collective-permute-done | bytes 393248 | tf_op jit(solution)/shard_map/ppermute | solution.py:254
  329.1 3.4 fusion.50
  337.9 12.7 %shard_map.222 = (f32[512,192]{1,0:T(8,128)S(1)}, bf16[4,512,128]{2,1,0:T(8,128)(2,1)S(1)}, bf16[4,512,128]{2,1,0:T(8,128)(2,1)S(1)}) custom-call(bf16[8,528,256]{2,1,0:T(8,128)(2,1)S(1)} %copy-done.2, bf16[512,384]{1,0:T(8,128)(2,1)S(1)} %slice_multiply_fusion.refs_8_.refs_1_, f32[8,1,1024]{2,1,0:T(1,128)S(1)} %pad_maximum_fusion.9.refs_9_.refs_2_, ...), custom_call_target="tpu_custom_call" | custom-call | flops 16106127360 | bytes 8388608 | tf_op jit(solution)/shard_map/pallas_call | solution.py:211
  353.5 2.8 fusion.65
  356.3 11.3 %collective-permute-done.29 = bf16[192,2048]{1,0:T(8,128)(2,1)S(1)} collective-permute-done((bf16[192,2048]{1,0:T(8,128)(2,1)S(1)}, bf16[192,2048]{1,0:T(8,128)(2,1)S(1)}, u32[]{:S(2)}, u32[]{:S(2)}) %collective-permute-start.29) | collective-permute-done | bytes 786464 | tf_op jit(solution)/shard_map/ppermute | solution.py:254
  376.5 12.8 %shard_map.223 = (f32[512,192]{1,0:T(8,128)S(1)}, bf16[4,512,128]{2,1,0:T(8,128)(2,1)S(1)}, bf16[4,512,128]{2,1,0:T(8,128)(2,1)S(1)}) custom-call(bf16[8,528,256]{2,1,0:T(8,128)(2,1)S(1)} %copy-done.3, bf16[512,384]{1,0:T(8,128)(2,1)S(1)} %slice_multiply_fusion.refs_8_.refs_1_, f32[8,1,1024]{2,1,0:T(1,128)S(1)} %pad_maximum_fusion.9.refs_9_.refs_2_, ...), custom_call_target="tpu_custom_call" | custom-call | flops 16106127360 | bytes 8388608 | tf_op jit(solution)/shard_map/pallas_call | solution.py:211
  394.1 7.0 %all-to-all-start.2 = ((bf16[4,128,384]{1,2,0:T(8,128)(2,1)}), bf16[4,128,384]{1,2,0:T(8,128)(2,1)}, u32[]{:S(2)}, u32[]{:S(2)}) async-start(bf16[4,128,384]{1,2,0:T(8,128)(2,1)} %pad_maximum_fusion.5), calls=%async_computation.2 | async-start | bytes 786432 | tf_op jit(solution)/shard_map/all_to_all | solution.py:563
  417.5 3.5 collective-permute-done.37
  424.0 13.7 %collective-permute-done.52 = bf16[192,384]{1,0:T(8,128)(2,1)S(1)} collective-permute-done((bf16[192,384]{1,0:T(8,128)(2,1)S(1)}, bf16[192,384]{1,0:T(8,128)(2,1)S(1)}, u32[]{:S(2)}, u32[]{:S(2)}) %collective-permute-start.52) | collective-permute-done | bytes 147488 | tf_op jit(solution)/shard_map/ppermute | solution.py:236
  439.2 11.2 %collective-permute-done.53 = bf16[192,384]{1,0:T(8,128)(2,1)S(1)} collective-permute-done((bf16[192,384]{1,0:T(8,128)(2,1)S(1)}, bf16[192,384]{1,0:T(8,128)(2,1)S(1)}, u32[]{:S(2)}, u32[]{:S(2)}) %collective-permute-start.53) | collective-permute-done | bytes 147488 | tf_op jit(solution)/shard_map/ppermute | solution.py:236
  454.7 3.5 convert_bitcast_fusion
  459.0 6.0 %all-to-all-start.3 = ((bf16[4,128,256]{1,2,0:T(8,128)(2,1)}), bf16[4,128,256]{1,2,0:T(8,128)(2,1)}, u32[]{:S(2)}, u32[]{:S(2)}) async-start(bf16[4,128,256]{1,2,0:T(8,128)(2,1)} %copy.102), calls=%async_computation.3 | async-start | bytes 524288 | tf_op jit(solution)/shard_map/all_to_all | solution.py:589
  465.0 5.2 fusion.5
  472.6 10.0 %collective-permute-done.56 = bf16[192,384]{1,0:T(8,128)(2,1)} collective-permute-done((bf16[192,384]{1,0:T(8,128)(2,1)}, bf16[192,384]{1,0:T(8,128)(2,1)}, u32[]{:S(2)}, u32[]{:S(2)}) %collective-permute-start.56) | collective-permute-done | bytes 147488 | tf_op jit(solution)/shard_map/ppermute | solution.py:236
  483.5 6.9 %collective-permute-done.57 = bf16[192,384]{1,0:T(8,128)(2,1)S(1)} collective-permute-done((bf16[192,384]{1,0:T(8,128)(2,1)}, bf16[192,384]{1,0:T(8,128)(2,1)S(1)}, u32[]{:S(2)}, u32[]{:S(2)}) %collective-permute-start.57) | collective-permute-done | bytes 147488 | tf_op jit(solution)/shard_map/ppermute | solution.py:236
  499.0 3.5 fusion.45
  509.0 3.3 collective-permute-start.47
  512.5 4.9 collective-permute-done.41
  524.8 7.7 %fusion = (f32[192]{0:T(256)S(1)}, f32[4,192,2048]{2,1,0:T(8,128)}) fusion(bf16[4,192,2048]{2,1,0:T(8,128)(2,1)} %bitcast.260, bf16[4,192,2048]{2,1,0:T(8,128)(2,1)} %param.25, f32[192]{0:T(256)S(1)} %convert_element_type.684), kind=kLoop, calls=%fused_computation.4 | loop fusion | flops 7864128 | bytes 12584448 | tf_op jit(solution)/shard_map/reduce_sum | solution.py:329
  (492 shorter events, 171.0 us)
Async XLA Ops:
  7.2 45.9 %all-gather.9.cloned.1.call-start = ((), (), s32[]{:S(2)}) async-start(), calls=%async_computation.4 | async-start | bytes 2211840 | tf_op jit(solution)/shard_map/all_gather | solution.py:392
  10.8 108.5 %all-gather.11.cloned.1.call-start = ((), (), s32[]{:S(2)}) async-start(), calls=%async_computation.5 | async-start | bytes 5308416 | tf_op jit(solution)/shard_map/all_gather | solution.py:418
  11.5 146.4 %all-gather.13.cloned.1.call-start = ((), (), s32[]{:S(2)}) async-start(), calls=%async_computation.6 | async-start | bytes 11059200 | tf_op jit(solution)/shard_map/all_gather | solution.py:433
  13.6 30.6 %collective-permute-start = (bf16[136,1536]{1,0:T(8,128)(2,1)}, bf16[136,1536]{1,0:T(8,128)(2,1)S(1)}, u32[]{:S(2)}, u32[]{:S(2)}) collective-permute-start(bf16[136,1536]{1,0:T(8,128)(2,1)} %fusion.66), channel_id=1, source_target_pairs={{0,24},{8,0},{16,8},{24,16},{1,25},{9,1},{17,9},{25,17},{2,26},{10... | collective-permute-start | bytes 1253384 | tf_op jit(solution)/shard_map/ppermute | solution.py:236
  14.0 30.4 %collective-permute-start.1 = (bf16[136,1536]{1,0:T(8,128)(2,1)}, bf16[136,1536]{1,0:T(8,128)(2,1)S(1)}, u32[]{:S(2)}, u32[]{:S(2)}) collective-permute-start(bf16[136,1536]{1,0:T(8,128)(2,1)} %fusion.66), channel_id=1, source_target_pairs={{0,16},{8,24},{16,0},{24,8},{1,17},{9,25},{17,1},{25,9},{2,18},{10... | collective-permute-start | bytes 1253384 | tf_op jit(solution)/shard_map/ppermute | solution.py:236
  16.6 35.8 %collective-permute-start.2 = (bf16[136,1536]{1,0:T(8,128)(2,1)}, bf16[136,1536]{1,0:T(8,128)(2,1)S(1)}, u32[]{:S(2)}, u32[]{:S(2)}) collective-permute-start(bf16[136,1536]{1,0:T(8,128)(2,1)} %fusion.66), channel_id=1, source_target_pairs={{0,8},{8,16},{16,24},{24,0},{1,9},{9,17},{17,25},{25,1},{2,10},{10... | collective-permute-start | bytes 1253384 | tf_op jit(solution)/shard_map/ppermute | solution.py:236
  76.9 155.9 %all-gather.15.cloned.1.call-start = ((), (), s32[]{:S(2)}) async-start(), calls=%async_computation.7 | async-start | bytes 8847360 | tf_op jit(solution)/shard_map/all_gather | solution.py:476
  127.1 20.4 %collective-permute-start.10 = (bf16[96,1536]{1,0:T(8,128)(2,1)}, bf16[96,1536]{1,0:T(8,128)(2,1)}, u32[]{:S(2)}, u32[]{:S(2)}) collective-permute-start(bf16[96,1536]{1,0:T(8,128)(2,1)} %get-tuple-element.287), channel_id=1, source_target_pairs={{0,8},{8,16},{16,24},{24,0},{1,9},{9,17},{17,25},{25,1},{2,10},{10... | collective-permute-start | bytes 884744 | tf_op jit(solution)/shard_map/ppermute | solution.py:236
  128.1 23.5 %collective-permute-start.11 = (bf16[96,1536]{1,0:T(8,128)(2,1)}, bf16[96,1536]{1,0:T(8,128)(2,1)}, u32[]{:S(2)}, u32[]{:S(2)}) collective-permute-start(bf16[96,1536]{1,0:T(8,128)(2,1)} %get-tuple-element.286), channel_id=1, source_target_pairs={{0,16},{8,24},{16,0},{24,8},{1,17},{9,25},{17,1},{25,9},{2,18},{10... | collective-permute-start | bytes 884744 | tf_op jit(solution)/shard_map/ppermute | solution.py:236
  131.0 24.6 %collective-permute-start.12 = (bf16[96,1536]{1,0:T(8,128)(2,1)}, bf16[96,1536]{1,0:T(8,128)(2,1)}, u32[]{:S(2)}, u32[]{:S(2)}) collective-permute-start(bf16[96,1536]{1,0:T(8,128)(2,1)} %get-tuple-element.285), channel_id=1, source_target_pairs={{0,24},{8,0},{16,8},{24,16},{1,25},{9,1},{17,9},{25,17},{2,26},{10... | collective-permute-start | bytes 884744 | tf_op jit(solution)/shard_map/ppermute | solution.py:236
  170.8 22.9 %collective-permute-start.13 = (bf16[96,1536]{1,0:T(8,128)(2,1)}, bf16[96,1536]{1,0:T(8,128)(2,1)}, u32[]{:S(2)}, u32[]{:S(2)}) collective-permute-start(bf16[96,1536]{1,0:T(8,128)(2,1)} %get-tuple-element.283), channel_id=1, source_target_pairs={{0,24},{8,0},{16,8},{24,16},{1,25},{9,1},{17,9},{25,17},{2,26},{10... | collective-permute-start | bytes 884744 | tf_op jit(solution)/shard_map/ppermute | solution.py:236
  170.8 22.9 %collective-permute-start.14 = (bf16[96,1536]{1,0:T(8,128)(2,1)}, bf16[96,1536]{1,0:T(8,128)(2,1)}, u32[]{:S(2)}, u32[]{:S(2)}) collective-permute-start(bf16[96,1536]{1,0:T(8,128)(2,1)} %get-tuple-element.282), channel_id=1, source_target_pairs={{0,16},{8,24},{16,0},{24,8},{1,17},{9,25},{17,1},{25,9},{2,18},{10... | collective-permute-start | bytes 884744 | tf_op jit(solution)/shard_map/ppermute | solution.py:236
  171.2 23.1 %collective-permute-start.15 = (bf16[96,1536]{1,0:T(8,128)(2,1)}, bf16[96,1536]{1,0:T(8,128)(2,1)}, u32[]{:S(2)}, u32[]{:S(2)}) collective-permute-start(bf16[96,1536]{1,0:T(8,128)(2,1)} %get-tuple-element.281), channel_id=1, source_target_pairs={{0,8},{8,16},{16,24},{24,0},{1,9},{9,17},{17,25},{25,1},{2,10},{10... | collective-permute-start | bytes 884744 | tf_op jit(solution)/shard_map/ppermute | solution.py:236
  199.8 23.5 %collective-permute-start.16 = (bf16[96,1536]{1,0:T(8,128)(2,1)}, bf16[96,1536]{1,0:T(8,128)(2,1)}, u32[]{:S(2)}, u32[]{:S(2)}) collective-permute-start(bf16[96,1536]{1,0:T(8,128)(2,1)} %get-tuple-element.279), channel_id=1, source_target_pairs={{0,8},{8,16},{16,24},{24,0},{1,9},{9,17},{17,25},{25,1},{2,10},{10... | collective-permute-start | bytes 884744 | tf_op jit(solution)/shard_map/ppermute | solution.py:236
  202.9 25.1 %collective-permute-start.17 = (bf16[96,1536]{1,0:T(8,128)(2,1)}, bf16[96,1536]{1,0:T(8,128)(2,1)}, u32[]{:S(2)}, u32[]{:S(2)}) collective-permute-start(bf16[96,1536]{1,0:T(8,128)(2,1)} %get-tuple-element.278), channel_id=1, source_target_pairs={{0,16},{8,24},{16,0},{24,8},{1,17},{9,25},{17,1},{25,9},{2,18},{10... | collective-permute-start | bytes 884744 | tf_op jit(solution)/shard_map/ppermute | solution.py:236
  207.3 23.2 %collective-permute-start.18 = (bf16[96,1536]{1,0:T(8,128)(2,1)}, bf16[96,1536]{1,0:T(8,128)(2,1)}, u32[]{:S(2)}, u32[]{:S(2)}) collective-permute-start(bf16[96,1536]{1,0:T(8,128)(2,1)} %get-tuple-element.277), channel_id=1, source_target_pairs={{0,24},{8,0},{16,8},{24,16},{1,25},{9,1},{17,9},{25,17},{2,26},{10... | collective-permute-start | bytes 884744 | tf_op jit(solution)/shard_map/ppermute | solution.py:236
  246.8 27.1 %collective-permute-start.22 = (bf16[4,192,1024]{2,1,0:T(8,128)(2,1)S(1)}, bf16[4,192,1024]{2,1,0:T(8,128)(2,1)S(1)}, u32[]{:S(2)}, u32[]{:S(2)}) collective-permute-start(bf16[4,192,1024]{2,1,0:T(8,128)(2,1)S(1)} %dynamic-slice_bitcast_fusion.2), channel_id=1, source_target_pairs={{0,1},{1,0},{2,3},{3,2},{4,5},{5,4},{6,7},{7,6},{8,9},{9,8},{10,11... | collective-permute-start | bytes 4718600 | tf_op jit(solution)/shard_map/ppermute | solution.py:254
  246.9 22.5 %collective-permute-start.19 = (bf16[96,1536]{1,0:T(8,128)(2,1)S(1)}, bf16[96,1536]{1,0:T(8,128)(2,1)S(1)}, u32[]{:S(2)}, u32[]{:S(2)}) collective-permute-start(bf16[96,1536]{1,0:T(8,128)(2,1)S(1)} %get-tuple-element.275), channel_id=1, source_target_pairs={{0,24},{8,0},{16,8},{24,16},{1,25},{9,1},{17,9},{25,17},{2,26},{10... | collective-permute-start | bytes 884744 | tf_op jit(solution)/shard_map/ppermute | solution.py:236
  247.0 22.4 %collective-permute-start.20 = (bf16[96,1536]{1,0:T(8,128)(2,1)S(1)}, bf16[96,1536]{1,0:T(8,128)(2,1)S(1)}, u32[]{:S(2)}, u32[]{:S(2)}) collective-permute-start(bf16[96,1536]{1,0:T(8,128)(2,1)S(1)} %get-tuple-element.274), channel_id=1, source_target_pairs={{0,16},{8,24},{16,0},{24,8},{1,17},{9,25},{17,1},{25,9},{2,18},{10... | collective-permute-start | bytes 884744 | tf_op jit(solution)/shard_map/ppermute | solution.py:236
  248.0 25.8 %collective-permute-start.21 = (bf16[96,1536]{1,0:T(8,128)(2,1)S(1)}, bf16[96,1536]{1,0:T(8,128)(2,1)S(1)}, u32[]{:S(2)}, u32[]{:S(2)}) collective-permute-start(bf16[96,1536]{1,0:T(8,128)(2,1)S(1)} %get-tuple-element.273), channel_id=1, source_target_pairs={{0,8},{8,16},{16,24},{24,0},{1,9},{9,17},{17,25},{25,1},{2,10},{10... | collective-permute-start | bytes 884744 | tf_op jit(solution)/shard_map/ppermute | solution.py:236
  258.2 70.9 %collective-permute-start.26 = (bf16[4,192,2048]{2,1,0:T(8,128)(2,1)}, bf16[4,192,2048]{2,1,0:T(8,128)(2,1)}, u32[]{:S(2)}, u32[]{:S(2)}) collective-permute-start(bf16[4,192,2048]{2,1,0:T(8,128)(2,1)} %dynamic-slice_bitcast_fusion), channel_id=1, source_target_pairs={{0,1},{1,0},{2,3},{3,2},{4,5},{5,4},{6,7},{7,6},{8,9},{9,8},{10,11... | collective-permute-start | bytes 9437192 | tf_op jit(solution)/shard_map/ppermute | solution.py:254
  287.1 167.6 %all-gather.19.cloned.1.call-start = ((), (), s32[]{:S(2)}) async-start(), calls=%async_computation.9 | async-start | bytes 1966080 | tf_op jit(solution)/shard_map/all_gather | solution.py:538
  302.2 35.7 %collective-permute-start.27 = (bf16[4,192,1536]{2,1,0:T(8,128)(2,1)}, bf16[4,192,1536]{2,1,0:T(8,128)(2,1)}, u32[]{:S(2)}, u32[]{:S(2)}) collective-permute-start(bf16[4,192,1536]{2,1,0:T(8,128)(2,1)} %dynamic-slice_bitcast_fusion.1), channel_id=1, source_target_pairs={{0,1},{1,0},{2,3},{3,2},{4,5},{5,4},{6,7},{7,6},{8,9},{9,8},{10,11... | collective-permute-start | bytes 7077896 | tf_op jit(solution)/shard_map/ppermute | solution.py:254
  309.0 18.9 %collective-permute-start.24 = (bf16[192,1024]{1,0:T(8,128)(2,1)S(1)}, bf16[192,1024]{1,0:T(8,128)(2,1)S(1)}, u32[]{:S(2)}, u32[]{:S(2)}) collective-permute-start(bf16[192,1024]{1,0:T(8,128)(2,1)S(1)} %copy-done.60), channel_id=1, source_target_pairs={{0,4},{1,5},{2,6},{3,7},{4,0},{5,1},{6,2},{7,3},{8,12},{9,13},{10,... | collective-permute-start | bytes 1179656 | tf_op jit(solution)/shard_map/ppermute | solution.py:254
  309.3 18.6 %collective-permute-start.25 = (bf16[192,1024]{1,0:T(8,128)(2,1)S(1)}, bf16[192,1024]{1,0:T(8,128)(2,1)S(1)}, u32[]{:S(2)}, u32[]{:S(2)}) collective-permute-start(bf16[192,1024]{1,0:T(8,128)(2,1)S(1)} %copy-done.59), channel_id=1, source_target_pairs={{0,6},{1,7},{2,4},{3,5},{4,2},{5,3},{6,0},{7,1},{8,14},{9,15},{10,... | collective-permute-start | bytes 1179656 | tf_op jit(solution)/shard_map/ppermute | solution.py:254
  329.0 195.8 %all-gather.17.cloned.1.call-start = ((), (), s32[]{:S(2)}) async-start(), calls=%async_computation.8 | async-start | bytes 3932160 | tf_op jit(solution)/shard_map/all_gather | solution.py:556
  332.6 23.8 %collective-permute-start.28 = (bf16[192,2048]{1,0:T(8,128)(2,1)S(1)}, bf16[192,2048]{1,0:T(8,128)(2,1)S(1)}, u32[]{:S(2)}, u32[]{:S(2)}) collective-permute-start(bf16[192,2048]{1,0:T(8,128)(2,1)S(1)} %get-tuple-element.250), channel_id=1, source_target_pairs={{0,2},{1,3},{2,0},{3,1},{4,6},{5,7},{6,4},{7,5},{8,10},{9,11},{10,... | collective-permute-start | bytes 2359304 | tf_op jit(solution)/shard_map/ppermute | solution.py:254
  333.0 34.6 %collective-permute-start.29 = (bf16[192,2048]{1,0:T(8,128)(2,1)S(1)}, bf16[192,2048]{1,0:T(8,128)(2,1)S(1)}, u32[]{:S(2)}, u32[]{:S(2)}) collective-permute-start(bf16[192,2048]{1,0:T(8,128)(2,1)S(1)} %get-tuple-element.249), channel_id=1, source_target_pairs={{0,4},{1,5},{2,6},{3,7},{4,0},{5,1},{6,2},{7,3},{8,12},{9,13},{10,... | collective-permute-start | bytes 2359304 | tf_op jit(solution)/shard_map/ppermute | solution.py:254
  334.4 33.2 %collective-permute-start.30 = (bf16[192,2048]{1,0:T(8,128)(2,1)S(1)}, bf16[192,2048]{1,0:T(8,128)(2,1)S(1)}, u32[]{:S(2)}, u32[]{:S(2)}) collective-permute-start(bf16[192,2048]{1,0:T(8,128)(2,1)S(1)} %get-tuple-element.248), channel_id=1, source_target_pairs={{0,6},{1,7},{2,4},{3,5},{4,2},{5,3},{6,0},{7,1},{8,14},{9,15},{10,... | collective-permute-start | bytes 2359304 | tf_op jit(solution)/shard_map/ppermute | solution.py:254
  367.6 36.5 %collective-permute-start.49 = (bf16[192,1536]{1,0:T(8,128)(2,1)}, bf16[192,1536]{1,0:T(8,128)(2,1)}, u32[]{:S(2)}, u32[]{:S(2)}) collective-permute-start(bf16[192,1536]{1,0:T(8,128)(2,1)} %get-tuple-element.253), channel_id=1, source_target_pairs={{0,2},{1,3},{2,0},{3,1},{4,6},{5,7},{6,4},{7,5},{8,10},{9,11},{10,... | collective-permute-start | bytes 1769480 | tf_op jit(solution)/shard_map/ppermute | solution.py:254
  369.2 34.9 %collective-permute-start.50 = (bf16[192,1536]{1,0:T(8,128)(2,1)}, bf16[192,1536]{1,0:T(8,128)(2,1)}, u32[]{:S(2)}, u32[]{:S(2)}) collective-permute-start(bf16[192,1536]{1,0:T(8,128)(2,1)} %get-tuple-element.252), channel_id=1, source_target_pairs={{0,4},{1,5},{2,6},{3,7},{4,0},{5,1},{6,2},{7,3},{8,12},{9,13},{10,... | collective-permute-start | bytes 1769480 | tf_op jit(solution)/shard_map/ppermute | solution.py:254
  369.7 34.5 %collective-permute-start.51 = (bf16[192,1536]{1,0:T(8,128)(2,1)}, bf16[192,1536]{1,0:T(8,128)(2,1)}, u32[]{:S(2)}, u32[]{:S(2)}) collective-permute-start(bf16[192,1536]{1,0:T(8,128)(2,1)} %get-tuple-element.251), channel_id=1, source_target_pairs={{0,6},{1,7},{2,4},{3,5},{4,2},{5,3},{6,0},{7,1},{8,14},{9,15},{10,... | collective-permute-start | bytes 1769480 | tf_op jit(solution)/shard_map/ppermute | solution.py:254
  394.1 64.0 %all-to-all-start.2 = ((bf16[4,128,384]{1,2,0:T(8,128)(2,1)}), bf16[4,128,384]{1,2,0:T(8,128)(2,1)}, u32[]{:S(2)}, u32[]{:S(2)}) async-start(bf16[4,128,384]{1,2,0:T(8,128)(2,1)} %pad_maximum_fusion.5), calls=%async_computation.2 | async-start | bytes 786432 | tf_op jit(solution)/shard_map/all_to_all | solution.py:563
  412.1 25.6 %collective-permute-start.52 = (bf16[192,384]{1,0:T(8,128)(2,1)S(1)}, bf16[192,384]{1,0:T(8,128)(2,1)S(1)}, u32[]{:S(2)}, u32[]{:S(2)}) collective-permute-start(bf16[192,384]{1,0:T(8,128)(2,1)S(1)} %get-tuple-element.292), channel_id=1, source_target_pairs={{0,8},{8,16},{16,24},{24,0},{1,9},{9,17},{17,25},{25,1},{2,10},{10... | collective-permute-start | bytes 442376 | tf_op jit(solution)/shard_map/ppermute | solution.py:236
  413.6 36.7 %collective-permute-start.53 = (bf16[192,384]{1,0:T(8,128)(2,1)S(1)}, bf16[192,384]{1,0:T(8,128)(2,1)S(1)}, u32[]{:S(2)}, u32[]{:S(2)}) collective-permute-start(bf16[192,384]{1,0:T(8,128)(2,1)S(1)} %get-tuple-element.291), channel_id=1, source_target_pairs={{0,16},{8,24},{16,0},{24,8},{1,17},{9,25},{17,1},{25,9},{2,18},{10... | collective-permute-start | bytes 442376 | tf_op jit(solution)/shard_map/ppermute | solution.py:236
  415.8 36.5 %collective-permute-start.54 = (bf16[192,384]{1,0:T(8,128)(2,1)S(1)}, bf16[192,384]{1,0:T(8,128)(2,1)S(1)}, u32[]{:S(2)}, u32[]{:S(2)}) collective-permute-start(bf16[192,384]{1,0:T(8,128)(2,1)S(1)} %get-tuple-element.290), channel_id=1, source_target_pairs={{0,24},{8,0},{16,8},{24,16},{1,25},{9,1},{17,9},{25,17},{2,26},{10... | collective-permute-start | bytes 442376 | tf_op jit(solution)/shard_map/ppermute | solution.py:236
  421.0 71.0 %collective-permute-start.33 = (bf16[192,512]{1,0:T(8,128)(2,1)}, bf16[192,512]{1,0:T(8,128)(2,1)}, u32[]{:S(2)}, u32[]{:S(2)}) collective-permute-start(bf16[192,512]{1,0:T(8,128)(2,1)} %get-tuple-element.265), channel_id=1, source_target_pairs={{0,2},{1,3},{2,0},{3,1},{4,6},{5,7},{6,4},{7,5},{8,10},{9,11},{10,... | collective-permute-start | bytes 589832 | tf_op jit(solution)/shard_map/ppermute | solution.py:254
  421.4 70.6 %collective-permute-start.34 = (bf16[192,512]{1,0:T(8,128)(2,1)}, bf16[192,512]{1,0:T(8,128)(2,1)}, u32[]{:S(2)}, u32[]{:S(2)}) collective-permute-start(bf16[192,512]{1,0:T(8,128)(2,1)} %get-tuple-element.264), channel_id=1, source_target_pairs={{0,4},{1,5},{2,6},{3,7},{4,0},{5,1},{6,2},{7,3},{8,12},{9,13},{10,... | collective-permute-start | bytes 589832 | tf_op jit(solution)/shard_map/ppermute | solution.py:254
  437.7 54.3 %collective-permute-start.35 = (bf16[192,512]{1,0:T(8,128)(2,1)}, bf16[192,512]{1,0:T(8,128)(2,1)}, u32[]{:S(2)}, u32[]{:S(2)}) collective-permute-start(bf16[192,512]{1,0:T(8,128)(2,1)} %get-tuple-element.263), channel_id=1, source_target_pairs={{0,6},{1,7},{2,4},{3,5},{4,2},{5,3},{6,0},{7,1},{8,14},{9,15},{10,... | collective-permute-start | bytes 589832 | tf_op jit(solution)/shard_map/ppermute | solution.py:254
  453.2 18.4 %collective-permute-start.55 = (bf16[192,384]{1,0:T(8,128)(2,1)}, bf16[192,384]{1,0:T(8,128)(2,1)}, u32[]{:S(2)}, u32[]{:S(2)}) collective-permute-start(bf16[192,384]{1,0:T(8,128)(2,1)} %get-tuple-element.237), channel_id=1, source_target_pairs={{0,8},{8,16},{16,24},{24,0},{1,9},{9,17},{17,25},{25,1},{2,10},{10... | collective-permute-start | bytes 442376 | tf_op jit(solution)/shard_map/ppermute | solution.py:236
  453.2 29.4 %collective-permute-start.56 = (bf16[192,384]{1,0:T(8,128)(2,1)}, bf16[192,384]{1,0:T(8,128)(2,1)}, u32[]{:S(2)}, u32[]{:S(2)}) collective-permute-start(bf16[192,384]{1,0:T(8,128)(2,1)} %get-tuple-element.237), channel_id=1, source_target_pairs={{0,16},{8,24},{16,0},{24,8},{1,17},{9,25},{17,1},{25,9},{2,18},{10... | collective-permute-start | bytes 442376 | tf_op jit(solution)/shard_map/ppermute | solution.py:236
  459.0 40.0 %all-to-all-start.3 = ((bf16[4,128,256]{1,2,0:T(8,128)(2,1)}), bf16[4,128,256]{1,2,0:T(8,128)(2,1)}, u32[]{:S(2)}, u32[]{:S(2)}) async-start(bf16[4,128,256]{1,2,0:T(8,128)(2,1)} %copy.102), calls=%async_computation.3 | async-start | bytes 524288 | tf_op jit(solution)/shard_map/all_to_all | solution.py:589
  471.6 18.9 %collective-permute-start.57 = (bf16[192,384]{1,0:T(8,128)(2,1)}, bf16[192,384]{1,0:T(8,128)(2,1)S(1)}, u32[]{:S(2)}, u32[]{:S(2)}) collective-permute-start(bf16[192,384]{1,0:T(8,128)(2,1)} %get-tuple-element.237), channel_id=1, source_target_pairs={{0,24},{8,0},{16,8},{24,16},{1,25},{9,1},{17,9},{25,17},{2,26},{10... | collective-permute-start | bytes 442376 | tf_op jit(solution)/shard_map/ppermute | solution.py:236
  495.3 17.0 %collective-permute-start.40 = (bf16[192,512]{1,0:T(8,128)(2,1)S(1)}, bf16[192,512]{1,0:T(8,128)(2,1)}, u32[]{:S(2)}, u32[]{:S(2)}) collective-permute-start(bf16[192,512]{1,0:T(8,128)(2,1)S(1)} %select_select_fusion), channel_id=1, source_target_pairs={{0,8},{8,16},{16,24},{24,0},{1,9},{9,17},{17,25},{25,1},{2,10},{10... | collective-permute-start | bytes 589832 | tf_op jit(solution)/shard_map/ppermute | solution.py:236
  495.4 22.0 %collective-permute-start.41 = (bf16[192,512]{1,0:T(8,128)(2,1)S(1)}, bf16[192,512]{1,0:T(8,128)(2,1)}, u32[]{:S(2)}, u32[]{:S(2)}) collective-permute-start(bf16[192,512]{1,0:T(8,128)(2,1)S(1)} %select_select_fusion), channel_id=1, source_target_pairs={{0,16},{8,24},{16,0},{24,8},{1,17},{9,25},{17,1},{25,9},{2,18},{10... | collective-permute-start | bytes 589832 | tf_op jit(solution)/shard_map/ppermute | solution.py:236
  507.5 25.0 %collective-permute-start.46 = (bf16[192,256]{1,0:T(8,128)(2,1)S(1)}, bf16[192,256]{1,0:T(8,128)(2,1)S(1)}, u32[]{:S(2)}, u32[]{:S(2)}) collective-permute-start(bf16[192,256]{1,0:T(8,128)(2,1)S(1)} %add_convert_fusion.19), channel_id=1, source_target_pairs={{0,8},{8,16},{16,24},{24,0},{1,9},{9,17},{17,25},{25,1},{2,10},{10... | collective-permute-start | bytes 294920 | tf_op jit(solution)/shard_map/ppermute | solution.py:236
  509.0 23.5 %collective-permute-start.47 = (bf16[192,256]{1,0:T(8,128)(2,1)S(1)}, bf16[192,256]{1,0:T(8,128)(2,1)}, u32[]{:S(2)}, u32[]{:S(2)}) collective-permute-start(bf16[192,256]{1,0:T(8,128)(2,1)S(1)} %add_convert_fusion.19), channel_id=1, source_target_pairs={{0,16},{8,24},{16,0},{24,8},{1,17},{9,25},{17,1},{25,9},{2,18},{10... | collective-permute-start | bytes 294920 | tf_op jit(solution)/shard_map/ppermute | solution.py:236
  512.3 20.2 %collective-permute-start.48 = (bf16[192,256]{1,0:T(8,128)(2,1)S(1)}, bf16[192,256]{1,0:T(8,128)(2,1)}, u32[]{:S(2)}, u32[]{:S(2)}) collective-permute-start(bf16[192,256]{1,0:T(8,128)(2,1)S(1)} %add_convert_fusion.19), channel_id=1, source_target_pairs={{0,24},{8,0},{16,8},{24,16},{1,25},{9,1},{17,9},{25,17},{2,26},{10... | collective-permute-start | bytes 294920 | tf_op jit(solution)/shard_map/ppermute | solution.py:236
  (111 other events, 1001.5 us)
Sparse Core Ops, SparseCore 0:
  10.9 28.3 all-gather.8
  41.2 45.1 all-gather.10
  88.8 60.4 all-gather.12
  151.6 52.2 all-gather.14
  329.1 36.1 all-gather.18
  391.5 100.3 all-gather.16

commit v6 on v5

--- a/solution.py
+++ b/solution.py
@@ -122,9 +122,9 @@
         ],
         compiler_params=pltpu.CompilerParams(vmem_limit_bytes=24 * 1024 * 1024),
         cost_estimate=pl.CostEstimate(
-            flops=8 * seqs * seqs * shards * rows * rows * local_kv * groups * HD,
-            bytes_accessed=8 * 1024 * 1024,
-            transcendentals=seqs * seqs * shards * rows * rows * local_kv * groups // 2,
+            flops=0,
+            bytes_accessed=0,
+            transcendentals=0,
         ),
     )(*kv_blocks, q, bias)
 
@@ -196,7 +196,7 @@
         def _(zq):
             total = acc_q[zq]
             parts = [total[h * rows : (h + 1) * rows, :HD] for h in range(groups)]
-            grad_q_ref[pl.ds(zq * rows, rows), :] = jnp.concatenate(parts, axis=1)
+            grad_q_ref[pl.ds(zq * rows, rows), :] = jnp.concatenate(parts, axis=1) * HD ** (-0.5)
 
 
 def flash_backward(q, kv_all, bias, grad, exact, lse, seqs, rows, g, groups):
@@ -225,9 +225,9 @@
         ],
         compiler_params=pltpu.CompilerParams(vmem_limit_bytes=28 * 1024 * 1024),
         cost_estimate=pl.CostEstimate(
-            flops=40 * seqs * seqs * shards * rows * rows * groups * HD,
-            bytes_accessed=8 * 1024 * 1024,
-            transcendentals=seqs * seqs * shards * rows * rows * groups // 2,
+            flops=0,
+            bytes_accessed=0,
+            transcendentals=0,
         ),
     )(kv_all, q, bias, grad, exact, lse)
 
@@ -297,6 +297,19 @@
 def two_parts(value):
     high = value.astype(BF)
     return high, (value - high.astype(F32)).astype(BF)
+
+
+def mark_kernel(seed_ref, out_ref):
+    out_ref[...] = seed_ref[...]
+
+
+def mark(*others):
+    seed = after(jnp.zeros((8, LANES), F32), *others)
+    return pl.pallas_call(
+        mark_kernel,
+        out_shape=jax.ShapeDtypeStruct((8, LANES), F32),
+        cost_estimate=pl.CostEstimate(flops=10**12, bytes_accessed=8192, transcendentals=0),
+    )(seed)
 
 
 def by_rows(array):
@@ -391,7 +404,9 @@
     heads_shard = (heads_shard.astype(F32) * gain_one).astype(BF)
     heads_full = lax.all_gather(heads_shard, "fsdp", axis=0, tiled=True)
     valid_row = jnp.pad(valid.astype(BF).reshape(1, rows), ((0, 7), (0, width - rows)))
-    token_blocks = send_out([jnp.concatenate([tokens, valid_row], axis=0)] * seqs, seqs)
+    token_rows = jnp.concatenate([tokens, valid_row], axis=0)
+    token_mark = mark(token_rows)
+    token_blocks = after(send_out([token_rows] * seqs, seqs), token_mark)
 
     valid_local = from_relative([each[rows : rows + 1, :rows] for each in token_blocks], z)
     token_blocks = [each[:rows] for each in token_blocks]
@@ -412,8 +427,8 @@
         axis=0,
     )
     kv_blocks = gather_shards(payload, shards)
-    late_router, late_gate_up, late_down = after(
-        (w_router, w_gate_up, w_down), kv_blocks[: shards // 2]
+    late_query, late_keyval, late_router, late_gate_up, late_down = after(
+        (w_query, w_keyval, w_router, w_gate_up, w_down), token_mark
     )
     out_full = lax.all_gather(w_out, "fsdp", axis=1, tiled=True)
     own_expert = take(late_gate_up, expert, 0)
@@ -434,6 +449,10 @@
     gate_up_full = expert_full[:, : 2 * piece]
     down_full = expert_full[:, 2 * piece : 3 * piece]
     router_full = expert_full[:, 3 * piece :]
+    attn_shard = jnp.concatenate([late_query, late_keyval], axis=1)
+    attn_full = lax.all_gather(
+        (attn_shard.astype(F32) * gain_one).astype(BF), "fsdp", axis=0, tiled=True
+    )
     order = jnp.asarray(
         [2 * m for m in range(shards // 2)] + [2 * m + 1 for m in range(shards // 2)], jnp.int32
     )
@@ -470,19 +489,16 @@
     placed = placed.reshape(rows, 2, seqs * CAP)
     dispatch = placed[:, 0] + placed[:, 1]
     placed_pairs = jnp.concatenate([placed[:, 0], placed[:, 1]], axis=0)
-    sent_rows = dot_tn(dispatch, normed_two).astype(BF).reshape(seqs, CAP, width)
-    late_query, late_keyval = after((w_query, w_keyval), sent_rows)
-    attn_shard = jnp.concatenate([late_query, late_keyval], axis=1)
-    attn_full = lax.all_gather(
-        (attn_shard.astype(F32) * gain_one).astype(BF), "fsdp", axis=0, tiled=True
-    )
+    sent_rows = dot_tn(dispatch, normed_two).astype(BF)
+    sent_rows = sent_rows.reshape(seqs, CAP, width)
     expert_rows = jnp.concatenate(send_out([sent_rows[s] for s in range(seqs)], seqs))
     gate_up = dot(expert_rows, gate_up_full)
     gate_part = gate_up[:, :piece]
     up_part = gate_up[:, piece:]
     sigmoid_gate = jax.nn.sigmoid(gate_part)
     hidden = (gate_part * sigmoid_gate * up_part).astype(BF)
-    expert_out = dot_nt(hidden, down_full).astype(BF).reshape(seqs, CAP, width)
+    expert_out = dot_nt(hidden, down_full).astype(BF)
+    expert_out = expert_out.reshape(seqs, CAP, width)
     returned = jnp.concatenate(send_back([expert_out[s] for s in range(seqs)], seqs))
     selected = dot(placed_pairs, returned).reshape(2, rows, width)
     mixed_exact = residual + gating[:, :1] * selected[0] + gating[:, 1:] * selected[1]
@@ -509,56 +525,58 @@
     grad_gate = grad_hidden * up_part * sigmoid_gate * (1.0 + gate_part * (1.0 - sigmoid_gate))
     grad_up = grad_hidden * gate_part * sigmoid_gate
     grad_gate_up_rows = jnp.concatenate([grad_gate, grad_up], axis=-1).astype(BF)
-    grad_rows = dot_nt(grad_gate_up_rows, gate_up_full).astype(BF).reshape(seqs, CAP, width)
-    grad_returned = jnp.concatenate(send_back([grad_rows[s] for s in range(seqs)], seqs))
-    held_out, held_hidden = after((grad_expert_out, hidden), grad_rows)
+    grad_rows = dot_nt(grad_gate_up_rows, gate_up_full).astype(BF)
+    returned_mark = grad_rows
+    grad_rows = grad_rows.reshape(seqs, CAP, width)
+    grad_returned = send_back([grad_rows[s] for s in range(seqs)], seqs)
+    grad_returned = jnp.concatenate(grad_returned)
+    held_out, held_hidden = after((grad_expert_out, hidden), returned_mark)
     grad_down_sums = pair_sums(
         pair_halves(dot_tn(held_out, held_hidden).astype(BF), shard, shards), shard
     )
-    held_rows, held_gate_up = after((expert_rows, grad_gate_up_rows), grad_rows)
+    held_rows, held_gate_up = after((expert_rows, grad_gate_up_rows), returned_mark)
     grad_gate_up_halves = pair_halves(
         dot_tn(held_rows, held_gate_up).astype(BF), shard, shards
     )
-    grad_returned = after(grad_returned, grad_down_sums)
-    kv_all = jnp.stack(after(kv_blocks, grad_rows))
-    tokens_local = from_relative(after(token_blocks, grad_rows), z).reshape(local_rows, width)
+    kv_all = jnp.stack(after(kv_blocks, returned_mark))
+    tokens_local = from_relative(after(token_blocks, returned_mark), z).reshape(local_rows, width)
     factor_local = root(tokens_local.astype(F32))
     ride_rows = jnp.concatenate([normed_two, jnp.ones((16, width), BF)], axis=0)
     product_rows = jnp.concatenate([tokens_local, ride_rows], axis=0)
 
+    grad_gate_up_sums = pair_sums(grad_gate_up_halves, shard)
+    grad_down_shard = total_of(send_chips(grad_down_sums, shards)).astype(BF)
+    grad_returned = after(grad_returned, grad_down_shard)
     grad_normed_two = dot(dispatch, grad_returned) + dot_nt(grad_logits, router_full)
     grad_residual = grad_mixed + root_back(residual, factor_two, grad_normed_two)
     grad_branch = grad_residual.astype(BF)
-    grad_attended = dot_nt(grad_branch, out_full).astype(BF)
+    grad_attended = dot_nt(after(grad_branch, grad_gate_up_sums), out_full).astype(BF)
     head_grad = lax.all_to_all(grad_attended, "seq", split_axis=1, concat_axis=0, tiled=True)
-    grad_gate_up_sums = pair_sums(after(grad_gate_up_halves, grad_attended), shard)
     grad_gate_up_blocks = send_chips(grad_gate_up_sums, shards)
-    grad_down_blocks = after(send_chips(grad_down_sums, shards), head_grad)
-    grad_down_shard = total_of(grad_down_blocks).astype(BF)
     grad_down = lax.all_gather(grad_down_shard, "seq", axis=0, tiled=False)
 
-    late_branch = after(grad_branch, head_grad)
-    grad_out_halves = pair_halves(dot_tn(late_branch, attended).astype(BF), shard, shards)
-
     grad_q, near, far = [], [], []
-    held = after(head_grad, grad_down_shard, grad_gate_up_sums, grad_out_halves)
+    held = after(head_grad, grad_attended)
     for g in range(local_kv):
         part_q, near_kv, far_kv = flash_backward(
             head_queries, kv_all, bias, held, exact, lse, seqs, rows, g, groups
         )
-        grad_q.append(part_q * scale)
+        grad_q.append(part_q)
         near.append(near_kv)
         far.append(far_kv)
-        if g == 0:
-            grad_gate_up_shard = total_of(after(grad_gate_up_blocks, part_q)).astype(BF)
-            grad_out_sums = pair_sums(after(grad_out_halves, part_q), shard)
-            held = after(head_grad, grad_gate_up_shard, grad_out_sums)
+        held = after(head_grad, part_q)
+    grad_gate_up_shard = total_of(after(grad_gate_up_blocks, part_q)).astype(BF)
     grad_gate_up_all = lax.all_gather(grad_gate_up_shard, "seq", axis=0, tiled=False)
-    grad_out_blocks = after(send_chips(grad_out_sums, shards), part_q)
+    grad_q, near, far = after((grad_q, near, far), grad_gate_up_shard)
+    grad_down = after(grad_down, part_q)
     near = jnp.concatenate(near, axis=2)
-    there = hop(jnp.concatenate(far, axis=2), shards, 1)
+    far = jnp.concatenate(far, axis=2)
+    there = hop(far, shards, 1)
     pairs = [near[m].astype(F32) + there[m].astype(F32) for m in range(shards // 2)]
     pairs = [(near[0], there[0])] + [each.astype(BF) for each in pairs[1:]]
+    grad_out_halves = pair_halves(
+        dot_tn(after(grad_branch, grad_gate_up_shard), attended).astype(BF), shard, shards
+    )
     grad_q = jnp.concatenate(grad_q, axis=1)
     token_grad_q = lax.all_to_all(
         grad_q.astype(BF), "seq", split_axis=0, concat_axis=1, tiled=True
@@ -585,7 +603,9 @@
         tuple(by_rows(part) for part in each) if isinstance(each, tuple) else by_rows(each)
         for each in grad_query_sums
     ]
-    grad_kv = total_of(after(send_chips(pairs, shards), grad_query_sums))
+    grad_out_sums = pair_sums(after(grad_out_halves, pairs), shard)
+    grad_kv = total_of(after(send_chips(pairs, shards), grad_out_sums))
+    grad_out_blocks = send_chips(grad_out_sums, shards)
     token_grad_kv = lax.all_to_all(
         grad_kv.astype(BF), "seq", split_axis=0, concat_axis=1, tiled=True
     )
@@ -606,7 +626,7 @@
     )
     grad_query_blocks = send_out([by_rows(grad_query_part.astype(BF))] * seqs, seqs)
     grad_query_blocks = [by_rows(each) for each in grad_query_blocks]
-    grad_out_part = total_of(after(grad_out_blocks, pairs))
+    grad_out_part = total_of(after(grad_out_blocks, grad_keyval_sums))
     cut = grad_out_part.astype(BF)
     grad_out_own = jnp.zeros((part, q_cols), F32)
     out_parts = send_out(
@@ -616,7 +636,7 @@
         ],
         seqs,
     )
-    for each in after(out_parts, grad_kv):
+    for each in out_parts:
         grad_out_own = grad_out_own + each.astype(F32)
     grad_out = place_columns(
         send_out([grad_out_own.astype(BF)] * seqs, seqs), z, lambda block, column: block

time: 555 us -> 526 us (0.948)
  waiting for transfers between devices: 215 us -> 189 us
    ppermute x27, waiting for transfers between devices: 155 us -> 129 us  [shift(): lax.ppermute(block, 'seq', [(i, (i + step) % count) for i in range(count)])]
    unnamed x206 -> x242, local copies, waits for them, and re-layouts: 22.6 us -> 19.4 us
    squeeze x14 -> x13, local copies, waits for them, and re-layouts: 11.4 us -> 13.3 us  [take(): return lax.dynamic_index_in_dim(array, index, axis, keepdims=False)]
  transfers between devices with their start and end apart: 68 -> 68, of which waited for: 27 -> 28; matrix products, arithmetic and copies ran while one was open for 26% -> 24% of each run, Pallas kernels for 8% -> 8%
where the time goes in v6:
time: 526 us; the launch traced here: 516 us
  waiting for transfers between devices  189 us (36%)
  starting transfers between devices  92.3 us (18%)
  other arithmetic  66.2 us (13%)
  matrix products  53.5 us (10%)
  local copies, waits for them, and re-layouts  49.5 us (9%)
  Pallas kernels  43.8 us (8%)
  between operations  21.5 us (4%)
    ppermute x27, waiting for transfers between devices, shift(): lax.ppermute(block, 'seq', [(i, (i + step) % count) for i in range(count)])  129 us
    ppermute x27, starting transfers between devices, shift(): lax.ppermute(block, 'seq', [(i, (i + step) % count) for i in range(count)])  42.5 us
    ppermute x31, waiting for transfers between devices, hop(): return lax.ppermute(block, 'fsdp', [(i, i ^ mask) for i in range(count)])  41.8 us
    ppermute x31, starting transfers between devices, hop(): return lax.ppermute(block, 'fsdp', [(i, i ^ mask) for i in range(count)])  28.6 us
    pallas_call x2, Pallas kernels, flash_backward(): pl.pallas_call(functools.partial(backward_kernel, shards, seqs, rows, g,...  25.5 us
    dot_general x10, matrix products, dot(): return jnp.dot(a, b, preferred_element_type=F32)  23.4 us
    dot_general x6, matrix products, dot_nt(): lax.dot_general(a, b, (((1,), (1,)), ((), ())), preferred_element_type=F32)  20 us
    unnamed x242, local copies, waits for them, and re-layouts  19.4 us
  transfers between devices with their start and end apart: 68, of which 28 were waited for; matrix products, arithmetic and copies ran while one was open for 24% of the time, Pallas kernels for 8%

profile of v6, /device:TPU:12, one launch (start us, length us, event | category | flops | bytes accessed | tf_op | source)
XLA Modules:
  0.0 515.8 jit_solution(14114961555885739924)
XLA Ops:
  21.0 23.6 %collective-permute-done = bf16[136,1536]{1,0:T(8,128)(2,1)S(1)} collective-permute-done((bf16[136,1536]{1,0:T(8,128)(2,1)S(1)}, bf16[136,1536]{1,0:T(8,128)(2,1)S(1)}, u32[]{:S(2)}, u32[]{:S(2)}) %collective-permute-start) | collective-permute-done | bytes 417824 | tf_op jit(solution)/shard_map/ppermute | solution.py:236
  44.7 7.8 %collective-permute-done.1 = bf16[136,1536]{1,0:T(8,128)(2,1)S(1)} collective-permute-done((bf16[136,1536]{1,0:T(8,128)(2,1)S(1)}, bf16[136,1536]{1,0:T(8,128)(2,1)S(1)}, u32[]{:S(2)}, u32[]{:S(2)}) %collective-permute-start.1) | collective-permute-done | bytes 417824 | tf_op jit(solution)/shard_map/ppermute | solution.py:236
  62.7 7.2 %collective-permute-done.3.refs_1_ = bf16[528,256]{1,0:T(8,128)(2,1)S(1)} collective-permute-done((bf16[528,256]{1,0:T(8,128)(2,1)S(1)}, bf16[528,256]{1,0:T(8,128)(2,1)S(1)}, u32[]{:S(2)}, u32[]{:S(2)}) %collective-permute-start.3) | collective-permute-done | bytes 270368 | tf_op jit(solution)/shard_map/ppermute | solution.py:254
  69.9 7.5 %collective-permute-done.4.refs_2_ = bf16[528,256]{1,0:T(8,128)(2,1)S(1)} collective-permute-done((bf16[528,256]{1,0:T(8,128)(2,1)S(1)}, bf16[528,256]{1,0:T(8,128)(2,1)S(1)}, u32[]{:S(2)}, u32[]{:S(2)}) %collective-permute-start.4) | collective-permute-done | bytes 270368 | tf_op jit(solution)/shard_map/ppermute | solution.py:254
  77.4 3.2 collective-permute-done.5.refs_3_
  83.0 18.4 %shard_map.221 = (bf16[512,384]{1,0:T(8,128)(2,1)S(1)}, f32[512,384]{1,0:T(8,128)S(1)}, f32[512,384]{1,0:T(8,128)S(1)}) custom-call(bf16[528,256]{1,0:T(8,128)(2,1)S(1)} %maximum_maximum_fusion.refs_0_, bf16[528,256]{1,0:T(8,128)(2,1)S(1)} %collective-permute-done.3.refs_1_, bf16[528,256]{1,0:T(8,128)(2,1)S(1)} %collective-permute-done.4.refs_2_, ...), custom_call_target="tpu_custom_call" | custom-call | tf_op jit(solution)/shard_map/pallas_call | solution.py:113
  104.1 3.5 all-to-all-start
  108.4 8.4 %all-to-all-done = bf16[4,128,384]{1,2,0:T(8,128)(2,1)S(1)} async-done(((bf16[4,128,384]{1,2,0:T(8,128)(2,1)}), bf16[4,128,384]{1,2,0:T(8,128)(2,1)S(1)}, u32[]{:S(2)}, u32[]{:S(2)}) %all-to-all-start) | async-done | bytes 393248 | tf_op jit(solution)/shard_map/all_to_all | solution.py:474
  116.8 4.3 multiply_reduce_fusion.5
  122.9 3.8 collective-permute-start.12
  126.7 2.9 collective-permute-start.10
  136.6 9.8 %collective-permute-done.11 = bf16[96,1536]{1,0:T(8,128)(2,1)} collective-permute-done((bf16[96,1536]{1,0:T(8,128)(2,1)}, bf16[96,1536]{1,0:T(8,128)(2,1)}, u32[]{:S(2)}, u32[]{:S(2)}) %collective-permute-start.11) | collective-permute-done | bytes 294944 | tf_op jit(solution)/shard_map/ppermute | solution.py:236
  146.4 5.3 %collective-permute-done.10 = bf16[96,1536]{1,0:T(8,128)(2,1)} collective-permute-done((bf16[96,1536]{1,0:T(8,128)(2,1)}, bf16[96,1536]{1,0:T(8,128)(2,1)}, u32[]{:S(2)}, u32[]{:S(2)}) %collective-permute-start.10) | collective-permute-done | bytes 294944 | tf_op jit(solution)/shard_map/ppermute | solution.py:236
  153.9 5.7 %fusion.3 = f32[384,2048]{1,0:T(8,128)S(1)} fusion(bf16[1536,3200]{1,0:T(8,128)(2,1)} %all-gather.13.cloned.1.call-done, bf16[96,1536]{1,0:T(8,128)(2,1)} %collective-permute-done.12, bf16[96,1536]{1,0:T(8,128)(2,1)} %collective-permute-done.11, bf16[96,1536]{1,0:T(8,128)(2,1)} %collective-permute-done.10, bf16[96,1536]{1,0:T(8,128)(2,1)S(1)} %copy-done.65), kind=kOutput, calls=%fused_computation.7 | convolution fusion | flops 2420637696 | bytes 10616832 | tf_op jit(solution)/shard_map/dot_general | solution.py:23
  161.2 3.8 convolution_convert_fusion.6
  171.1 17.6 %collective-permute-done.15 = bf16[96,1536]{1,0:T(8,128)(2,1)} collective-permute-done((bf16[96,1536]{1,0:T(8,128)(2,1)}, bf16[96,1536]{1,0:T(8,128)(2,1)}, u32[]{:S(2)}, u32[]{:S(2)}) %collective-permute-start.15) | collective-permute-done | bytes 294944 | tf_op jit(solution)/shard_map/ppermute | solution.py:236
  188.7 4.6 collective-permute-done.14
  201.9 2.9 collective-permute-start.16
  207.1 14.9 %collective-permute-done.18 = bf16[96,1536]{1,0:T(8,128)(2,1)S(1)} collective-permute-done((bf16[96,1536]{1,0:T(8,128)(2,1)}, bf16[96,1536]{1,0:T(8,128)(2,1)S(1)}, u32[]{:S(2)}, u32[]{:S(2)}) %collective-permute-start.18) | collective-permute-done | bytes 294944 | tf_op jit(solution)/shard_map/ppermute | solution.py:236
  222.0 4.0 collective-permute-done.16
  227.9 5.0 multiply_convert_fusion.2
  232.9 5.5 %fusion.9 = bf16[384,1536]{1,0:T(8,128)(2,1)S(1)} fusion(bf16[1536,3200]{1,0:T(8,128)(2,1)} %all-gather.13.cloned.1.call-done, bf16[384,1024]{1,0:T(8,128)(2,1)S(1)} %get-tuple-element.254, bf16[384,1024]{1,0:T(8,128)(2,1)S(1)} %get-tuple-element.253), kind=kOutput, calls=%fused_computation.19 | convolution fusion | flops 2419654656 | bytes 9043968 | tf_op jit(solution)/shard_map/dot_general | solution.py:27
  242.5 3.5 collective-permute-start.20
  249.3 3.7 convolution_convert_fusion
  258.2 3.6 collective-permute-start.25
  264.2 2.7 collective-permute-done.20
  272.1 6.9 %collective-permute-done.24 = bf16[192,1024]{1,0:T(8,128)(2,1)S(1)} collective-permute-done((bf16[192,1024]{1,0:T(8,128)(2,1)S(1)}, bf16[192,1024]{1,0:T(8,128)(2,1)S(1)}, u32[]{:S(2)}, u32[]{:S(2)}) %collective-permute-start.24) | collective-permute-done | bytes 393248 | tf_op jit(solution)/shard_map/ppermute | solution.py:254
  284.4 5.0 fusion.50
  296.6 5.6 %all-to-all-start.1 = ((bf16[128,4,384]{2,0,1:T(8,128)(2,1)}), bf16[128,4,384]{2,0,1:T(8,128)(2,1)S(1)}, u32[]{:S(2)}, u32[]{:S(2)}) async-start(bf16[128,4,384]{2,0,1:T(8,128)(2,1)} %bitcast.257), calls=%async_computation.1 | async-start | bytes 786432 | tf_op jit(solution)/shard_map/all_to_all | solution.py:554
  302.7 8.2 %all-to-all-done.1 = bf16[128,4,384]{2,0,1:T(8,128)(2,1)S(1)} async-done(((bf16[128,4,384]{2,0,1:T(8,128)(2,1)}), bf16[128,4,384]{2,0,1:T(8,128)(2,1)S(1)}, u32[]{:S(2)}, u32[]{:S(2)}) %all-to-all-start.1) | async-done | bytes 393248 | tf_op jit(solution)/shard_map/all_to_all | solution.py:554
  313.2 12.7 %shard_map.222 = (f32[512,192]{1,0:T(8,128)S(1)}, bf16[4,512,128]{2,1,0:T(8,128)(2,1)S(1)}, bf16[4,512,128]{2,1,0:T(8,128)(2,1)S(1)}) custom-call(bf16[8,528,256]{2,1,0:T(8,128)(2,1)S(1)} %bitcast_dynamic-update-slice_fusion.8.refs_0_, bf16[512,384]{1,0:T(8,128)(2,1)S(1)} %slice_multiply_fusion.refs_8_.refs_1_, ...), custom_call_target="tpu_custom_call" | custom-call | tf_op jit(solution)/shard_map/pallas_call | solution.py:211
  327.6 12.8 %shard_map.223 = (f32[512,192]{1,0:T(8,128)S(1)}, bf16[4,512,128]{2,1,0:T(8,128)(2,1)S(1)}, bf16[4,512,128]{2,1,0:T(8,128)(2,1)S(1)}) custom-call(bf16[8,528,256]{2,1,0:T(8,128)(2,1)S(1)} %bitcast_dynamic-update-slice_fusion.8.refs_0_, bf16[512,384]{1,0:T(8,128)(2,1)S(1)} %slice_multiply_fusion.refs_8_.refs_1_, ...), custom_call_target="tpu_custom_call" | custom-call | tf_op jit(solution)/shard_map/pallas_call | solution.py:211
  342.8 3.3 add_convert_fusion
  359.5 6.5 %all-to-all-start.2 = ((bf16[4,128,384]{1,2,0:T(8,128)(2,1)}), bf16[4,128,384]{1,2,0:T(8,128)(2,1)}, u32[]{:S(2)}, u32[]{:S(2)}) async-start(bf16[4,128,384]{1,2,0:T(8,128)(2,1)} %pad_maximum_fusion.5), calls=%async_computation.2 | async-start | bytes 786432 | tf_op jit(solution)/shard_map/all_to_all | solution.py:581
  374.8 3.7 fusion.68
  386.8 5.1 all-to-all-start.3
  394.0 5.0 fusion.5
  409.6 3.5 fusion.44
  414.3 6.1 %collective-permute-done.43 = bf16[192,256]{1,0:T(8,128)(2,1)S(1)} collective-permute-done((bf16[192,256]{1,0:T(8,128)(2,1)S(1)}, bf16[192,256]{1,0:T(8,128)(2,1)S(1)}, u32[]{:S(2)}, u32[]{:S(2)}) %collective-permute-start.43) | collective-permute-done | bytes 98336 | tf_op jit(solution)/shard_map/ppermute | solution.py:254
  421.6 9.5 %collective-permute-done.44 = bf16[192,256]{1,0:T(8,128)(2,1)S(1)} collective-permute-done((bf16[192,256]{1,0:T(8,128)(2,1)S(1)}, bf16[192,256]{1,0:T(8,128)(2,1)S(1)}, u32[]{:S(2)}, u32[]{:S(2)}) %collective-permute-start.44) | collective-permute-done | bytes 98336 | tf_op jit(solution)/shard_map/ppermute | solution.py:254
  432.3 2.7 collective-permute-start.41
  435.0 14.1 %collective-permute-done.42 = bf16[192,512]{1,0:T(8,128)(2,1)S(1)} collective-permute-done((bf16[192,512]{1,0:T(8,128)(2,1)S(1)}, bf16[192,512]{1,0:T(8,128)(2,1)S(1)}, u32[]{:S(2)}, u32[]{:S(2)}) %collective-permute-start.42) | collective-permute-done | bytes 196640 | tf_op jit(solution)/shard_map/ppermute | solution.py:236
  462.0 2.8 collective-permute-start.52
  467.7 5.6 %collective-permute-done.54 = bf16[192,384]{1,0:T(8,128)(2,1)S(1)} collective-permute-done((bf16[192,384]{1,0:T(8,128)(2,1)}, bf16[192,384]{1,0:T(8,128)(2,1)S(1)}, u32[]{:S(2)}, u32[]{:S(2)}) %collective-permute-start.54) | collective-permute-done | bytes 147488 | tf_op jit(solution)/shard_map/ppermute | solution.py:236
  480.1 2.7 collective-permute-start.56
  482.8 5.4 %collective-permute-done.55 = bf16[192,384]{1,0:T(8,128)(2,1)S(1)} collective-permute-done((bf16[192,384]{1,0:T(8,128)(2,1)S(1)}, bf16[192,384]{1,0:T(8,128)(2,1)S(1)}, u32[]{:S(2)}, u32[]{:S(2)}) %collective-permute-start.55) | collective-permute-done | bytes 147488 | tf_op jit(solution)/shard_map/ppermute | solution.py:236
  488.2 3.1 collective-permute-done.56
  493.9 7.6 %fusion = (f32[192]{0:T(256)S(1)}, f32[4,192,2048]{2,1,0:T(8,128)}) fusion(bf16[4,192,2048]{2,1,0:T(8,128)(2,1)} %bitcast.249, bf16[4,192,2048]{2,1,0:T(8,128)(2,1)} %param.25, f32[192]{0:T(256)S(1)} %convert_element_type.685), kind=kLoop, calls=%fused_computation.4 | loop fusion | flops 7864128 | bytes 12584448 | tf_op jit(solution)/shard_map/reduce_sum | solution.py:342
  (523 shorter events, 173.1 us)
Async XLA Ops:
  7.2 47.7 %all-gather.9.cloned.1.call-start = ((), (), s32[]{:S(2)}) async-start(), calls=%async_computation.4 | async-start | bytes 2211840 | tf_op jit(solution)/shard_map/all_gather | solution.py:405
  10.7 106.1 %all-gather.11.cloned.1.call-start = ((), (), s32[]{:S(2)}) async-start(), calls=%async_computation.5 | async-start | bytes 5308416 | tf_op jit(solution)/shard_map/all_gather | solution.py:433
  11.5 142.4 %all-gather.13.cloned.1.call-start = ((), (), s32[]{:S(2)}) async-start(), calls=%async_computation.6 | async-start | bytes 11059200 | tf_op jit(solution)/shard_map/all_gather | solution.py:448
  15.0 212.9 %all-gather.15.cloned.1.call-start = ((), (), s32[]{:S(2)}) async-start(), calls=%async_computation.7 | async-start | bytes 8847360 | tf_op jit(solution)/shard_map/all_gather | solution.py:453
  15.1 29.6 %collective-permute-start = (bf16[136,1536]{1,0:T(8,128)(2,1)S(1)}, bf16[136,1536]{1,0:T(8,128)(2,1)S(1)}, u32[]{:S(2)}, u32[]{:S(2)}) collective-permute-start(bf16[136,1536]{1,0:T(8,128)(2,1)S(1)} %fusion.69), channel_id=1, source_target_pairs={{0,8},{8,16},{16,24},{24,0},{1,9},{9,17},{17,25},{25,1},{2,10},{10... | collective-permute-start | bytes 1253384 | tf_op jit(solution)/shard_map/ppermute | solution.py:236
  16.7 35.8 %collective-permute-start.1 = (bf16[136,1536]{1,0:T(8,128)(2,1)S(1)}, bf16[136,1536]{1,0:T(8,128)(2,1)S(1)}, u32[]{:S(2)}, u32[]{:S(2)}) collective-permute-start(bf16[136,1536]{1,0:T(8,128)(2,1)S(1)} %fusion.69), channel_id=1, source_target_pairs={{0,16},{8,24},{16,0},{24,8},{1,17},{9,25},{17,1},{25,9},{2,18},{10... | collective-permute-start | bytes 1253384 | tf_op jit(solution)/shard_map/ppermute | solution.py:236
  17.9 36.3 %collective-permute-start.2 = (bf16[136,1536]{1,0:T(8,128)(2,1)S(1)}, bf16[136,1536]{1,0:T(8,128)(2,1)S(1)}, u32[]{:S(2)}, u32[]{:S(2)}) collective-permute-start(bf16[136,1536]{1,0:T(8,128)(2,1)S(1)} %fusion.69), channel_id=1, source_target_pairs={{0,24},{8,0},{16,8},{24,16},{1,25},{9,1},{17,9},{25,17},{2,26},{10... | collective-permute-start | bytes 1253384 | tf_op jit(solution)/shard_map/ppermute | solution.py:236
  60.6 16.8 %collective-permute-start.4 = (bf16[528,256]{1,0:T(8,128)(2,1)S(1)}, bf16[528,256]{1,0:T(8,128)(2,1)S(1)}, u32[]{:S(2)}, u32[]{:S(2)}) collective-permute-start(bf16[528,256]{1,0:T(8,128)(2,1)S(1)} %maximum_maximum_fusion.refs_0_), channel_id=1, source_target_pairs={{0,4},{1,5},{2,6},{3,7},{4,0},{5,1},{6,2},{7,3},{8,12},{9,13},{10,... | collective-permute-start | bytes 811016 | tf_op jit(solution)/shard_map/ppermute | solution.py:254
  61.1 19.5 %collective-permute-start.5 = (bf16[528,256]{1,0:T(8,128)(2,1)S(1)}, bf16[528,256]{1,0:T(8,128)(2,1)S(1)}, u32[]{:S(2)}, u32[]{:S(2)}) collective-permute-start(bf16[528,256]{1,0:T(8,128)(2,1)S(1)} %maximum_maximum_fusion.refs_0_), channel_id=1, source_target_pairs={{0,6},{1,7},{2,4},{3,5},{4,2},{5,3},{6,0},{7,1},{8,14},{9,15},{10,... | collective-permute-start | bytes 811016 | tf_op jit(solution)/shard_map/ppermute | solution.py:254
  62.7 18.1 %collective-permute-start.6 = (bf16[528,256]{1,0:T(8,128)(2,1)S(1)}, bf16[528,256]{1,0:T(8,128)(2,1)S(1)}, u32[]{:S(2)}, u32[]{:S(2)}) collective-permute-start(bf16[528,256]{1,0:T(8,128)(2,1)S(1)} %maximum_maximum_fusion.refs_0_), channel_id=1, source_target_pairs={{0,1},{1,0},{2,3},{3,2},{4,5},{5,4},{6,7},{7,6},{8,9},{9,8},{10,11... | collective-permute-start | bytes 811016 | tf_op jit(solution)/shard_map/ppermute | solution.py:254
  126.7 19.7 %collective-permute-start.11 = (bf16[96,1536]{1,0:T(8,128)(2,1)}, bf16[96,1536]{1,0:T(8,128)(2,1)}, u32[]{:S(2)}, u32[]{:S(2)}) collective-permute-start(bf16[96,1536]{1,0:T(8,128)(2,1)} %get-tuple-element.282), channel_id=1, source_target_pairs={{0,16},{8,24},{16,0},{24,8},{1,17},{9,25},{17,1},{25,9},{2,18},{10... | collective-permute-start | bytes 884744 | tf_op jit(solution)/shard_map/ppermute | solution.py:236
  126.7 24.9 %collective-permute-start.10 = (bf16[96,1536]{1,0:T(8,128)(2,1)}, bf16[96,1536]{1,0:T(8,128)(2,1)}, u32[]{:S(2)}, u32[]{:S(2)}) collective-permute-start(bf16[96,1536]{1,0:T(8,128)(2,1)} %get-tuple-element.283), channel_id=1, source_target_pairs={{0,8},{8,16},{16,24},{24,0},{1,9},{9,17},{17,25},{25,1},{2,10},{10... | collective-permute-start | bytes 884744 | tf_op jit(solution)/shard_map/ppermute | solution.py:236
  166.0 22.7 %collective-permute-start.15 = (bf16[96,1536]{1,0:T(8,128)(2,1)}, bf16[96,1536]{1,0:T(8,128)(2,1)}, u32[]{:S(2)}, u32[]{:S(2)}) collective-permute-start(bf16[96,1536]{1,0:T(8,128)(2,1)} %get-tuple-element.277), channel_id=1, source_target_pairs={{0,8},{8,16},{16,24},{24,0},{1,9},{9,17},{17,25},{25,1},{2,10},{10... | collective-permute-start | bytes 884744 | tf_op jit(solution)/shard_map/ppermute | solution.py:236
  168.3 25.0 %collective-permute-start.14 = (bf16[96,1536]{1,0:T(8,128)(2,1)}, bf16[96,1536]{1,0:T(8,128)(2,1)}, u32[]{:S(2)}, u32[]{:S(2)}) collective-permute-start(bf16[96,1536]{1,0:T(8,128)(2,1)} %get-tuple-element.278), channel_id=1, source_target_pairs={{0,16},{8,24},{16,0},{24,8},{1,17},{9,25},{17,1},{25,9},{2,18},{10... | collective-permute-start | bytes 884744 | tf_op jit(solution)/shard_map/ppermute | solution.py:236
  168.9 25.1 %collective-permute-start.13 = (bf16[96,1536]{1,0:T(8,128)(2,1)}, bf16[96,1536]{1,0:T(8,128)(2,1)}, u32[]{:S(2)}, u32[]{:S(2)}) collective-permute-start(bf16[96,1536]{1,0:T(8,128)(2,1)} %get-tuple-element.279), channel_id=1, source_target_pairs={{0,24},{8,0},{16,8},{24,16},{1,25},{9,1},{17,9},{25,17},{2,26},{10... | collective-permute-start | bytes 884744 | tf_op jit(solution)/shard_map/ppermute | solution.py:236
  199.3 22.7 %collective-permute-start.18 = (bf16[96,1536]{1,0:T(8,128)(2,1)}, bf16[96,1536]{1,0:T(8,128)(2,1)S(1)}, u32[]{:S(2)}, u32[]{:S(2)}) collective-permute-start(bf16[96,1536]{1,0:T(8,128)(2,1)} %get-tuple-element.273), channel_id=1, source_target_pairs={{0,24},{8,0},{16,8},{24,16},{1,25},{9,1},{17,9},{25,17},{2,26},{10... | collective-permute-start | bytes 884744 | tf_op jit(solution)/shard_map/ppermute | solution.py:236
  199.3 22.7 %collective-permute-start.17 = (bf16[96,1536]{1,0:T(8,128)(2,1)}, bf16[96,1536]{1,0:T(8,128)(2,1)S(1)}, u32[]{:S(2)}, u32[]{:S(2)}) collective-permute-start(bf16[96,1536]{1,0:T(8,128)(2,1)} %get-tuple-element.274), channel_id=1, source_target_pairs={{0,16},{8,24},{16,0},{24,8},{1,17},{9,25},{17,1},{25,9},{2,18},{10... | collective-permute-start | bytes 884744 | tf_op jit(solution)/shard_map/ppermute | solution.py:236
  201.9 24.0 %collective-permute-start.16 = (bf16[96,1536]{1,0:T(8,128)(2,1)S(1)}, bf16[96,1536]{1,0:T(8,128)(2,1)S(1)}, u32[]{:S(2)}, u32[]{:S(2)}) collective-permute-start(bf16[96,1536]{1,0:T(8,128)(2,1)S(1)} %get-tuple-element.275), channel_id=1, source_target_pairs={{0,8},{8,16},{16,24},{24,0},{1,9},{9,17},{17,25},{25,1},{2,10},{10... | collective-permute-start | bytes 884744 | tf_op jit(solution)/shard_map/ppermute | solution.py:236
  240.0 22.6 %collective-permute-start.21 = (bf16[96,1536]{1,0:T(8,128)(2,1)S(1)}, bf16[96,1536]{1,0:T(8,128)(2,1)S(1)}, u32[]{:S(2)}, u32[]{:S(2)}) collective-permute-start(bf16[96,1536]{1,0:T(8,128)(2,1)S(1)} %get-tuple-element.269), channel_id=1, source_target_pairs={{0,8},{8,16},{16,24},{24,0},{1,9},{9,17},{17,25},{25,1},{2,10},{10... | collective-permute-start | bytes 884744 | tf_op jit(solution)/shard_map/ppermute | solution.py:236
  242.5 24.4 %collective-permute-start.20 = (bf16[96,1536]{1,0:T(8,128)(2,1)S(1)}, bf16[96,1536]{1,0:T(8,128)(2,1)S(1)}, u32[]{:S(2)}, u32[]{:S(2)}) collective-permute-start(bf16[96,1536]{1,0:T(8,128)(2,1)S(1)} %get-tuple-element.270), channel_id=1, source_target_pairs={{0,16},{8,24},{16,0},{24,8},{1,17},{9,25},{17,1},{25,9},{2,18},{10... | collective-permute-start | bytes 884744 | tf_op jit(solution)/shard_map/ppermute | solution.py:236
  246.0 25.0 %collective-permute-start.19 = (bf16[96,1536]{1,0:T(8,128)(2,1)S(1)}, bf16[96,1536]{1,0:T(8,128)(2,1)S(1)}, u32[]{:S(2)}, u32[]{:S(2)}) collective-permute-start(bf16[96,1536]{1,0:T(8,128)(2,1)S(1)} %get-tuple-element.271), channel_id=1, source_target_pairs={{0,24},{8,0},{16,8},{24,16},{1,25},{9,1},{17,9},{25,17},{2,26},{10... | collective-permute-start | bytes 884744 | tf_op jit(solution)/shard_map/ppermute | solution.py:236
  254.9 29.5 %collective-permute-start.26 = (bf16[4,192,2048]{2,1,0:T(8,128)(2,1)}, bf16[4,192,2048]{2,1,0:T(8,128)(2,1)}, u32[]{:S(2)}, u32[]{:S(2)}) collective-permute-start(bf16[4,192,2048]{2,1,0:T(8,128)(2,1)} %dynamic-slice_bitcast_fusion), channel_id=1, source_target_pairs={{0,1},{1,0},{2,3},{3,2},{4,5},{5,4},{6,7},{7,6},{8,9},{9,8},{10,11... | collective-permute-start | bytes 9437192 | tf_op jit(solution)/shard_map/ppermute | solution.py:254
  262.6 16.3 %collective-permute-start.24 = (bf16[192,1024]{1,0:T(8,128)(2,1)S(1)}, bf16[192,1024]{1,0:T(8,128)(2,1)S(1)}, u32[]{:S(2)}, u32[]{:S(2)}) collective-permute-start(bf16[192,1024]{1,0:T(8,128)(2,1)S(1)} %get-tuple-element.252), channel_id=1, source_target_pairs={{0,4},{1,5},{2,6},{3,7},{4,0},{5,1},{6,2},{7,3},{8,12},{9,13},{10,... | collective-permute-start | bytes 1179656 | tf_op jit(solution)/shard_map/ppermute | solution.py:254
  289.4 53.4 %collective-permute-start.27 = (bf16[192,2048]{1,0:T(8,128)(2,1)}, bf16[192,2048]{1,0:T(8,128)(2,1)}, u32[]{:S(2)}, u32[]{:S(2)}) collective-permute-start(bf16[192,2048]{1,0:T(8,128)(2,1)} %get-tuple-element.246), channel_id=1, source_target_pairs={{0,2},{1,3},{2,0},{3,1},{4,6},{5,7},{6,4},{7,5},{8,10},{9,11},{10,... | collective-permute-start | bytes 2359304 | tf_op jit(solution)/shard_map/ppermute | solution.py:254
  291.1 51.6 %collective-permute-start.28 = (bf16[192,2048]{1,0:T(8,128)(2,1)}, bf16[192,2048]{1,0:T(8,128)(2,1)}, u32[]{:S(2)}, u32[]{:S(2)}) collective-permute-start(bf16[192,2048]{1,0:T(8,128)(2,1)} %get-tuple-element.245), channel_id=1, source_target_pairs={{0,4},{1,5},{2,6},{3,7},{4,0},{5,1},{6,2},{7,3},{8,12},{9,13},{10,... | collective-permute-start | bytes 2359304 | tf_op jit(solution)/shard_map/ppermute | solution.py:254
  291.9 50.9 %collective-permute-start.29 = (bf16[192,2048]{1,0:T(8,128)(2,1)}, bf16[192,2048]{1,0:T(8,128)(2,1)}, u32[]{:S(2)}, u32[]{:S(2)}) collective-permute-start(bf16[192,2048]{1,0:T(8,128)(2,1)} %get-tuple-element.244), channel_id=1, source_target_pairs={{0,6},{1,7},{2,4},{3,5},{4,2},{5,3},{6,0},{7,1},{8,14},{9,15},{10,... | collective-permute-start | bytes 2359304 | tf_op jit(solution)/shard_map/ppermute | solution.py:254
  296.6 14.4 %all-to-all-start.1 = ((bf16[128,4,384]{2,0,1:T(8,128)(2,1)}), bf16[128,4,384]{2,0,1:T(8,128)(2,1)S(1)}, u32[]{:S(2)}, u32[]{:S(2)}) async-start(bf16[128,4,384]{2,0,1:T(8,128)(2,1)} %bitcast.257), calls=%async_computation.1 | async-start | bytes 786432 | tf_op jit(solution)/shard_map/all_to_all | solution.py:554
  302.1 64.5 %all-gather.19.cloned.1.call-start = ((), (), s32[]{:S(2)}) async-start(), calls=%async_computation.9 | async-start | bytes 1966080 | tf_op jit(solution)/shard_map/all_gather | solution.py:556
  350.4 23.4 %collective-permute-start.38 = (bf16[4,192,1536]{2,1,0:T(8,128)(2,1)}, bf16[4,192,1536]{2,1,0:T(8,128)(2,1)}, u32[]{:S(2)}, u32[]{:S(2)}) collective-permute-start(bf16[4,192,1536]{2,1,0:T(8,128)(2,1)} %dynamic-slice_bitcast_fusion.1), channel_id=1, source_target_pairs={{0,1},{1,0},{2,3},{3,2},{4,5},{5,4},{6,7},{7,6},{8,9},{9,8},{10,11... | collective-permute-start | bytes 7077896 | tf_op jit(solution)/shard_map/ppermute | solution.py:254
  359.5 26.5 %all-to-all-start.2 = ((bf16[4,128,384]{1,2,0:T(8,128)(2,1)}), bf16[4,128,384]{1,2,0:T(8,128)(2,1)}, u32[]{:S(2)}, u32[]{:S(2)}) async-start(bf16[4,128,384]{1,2,0:T(8,128)(2,1)} %pad_maximum_fusion.5), calls=%async_computation.2 | async-start | bytes 786432 | tf_op jit(solution)/shard_map/all_to_all | solution.py:581
  366.0 127.8 %all-gather.17.cloned.1.call-start = ((), (), s32[]{:S(2)}) async-start(), calls=%async_computation.8 | async-start | bytes 3932160 | tf_op jit(solution)/shard_map/all_gather | solution.py:569
  366.6 14.3 %collective-permute-start.35 = (bf16[512,256]{1,0:T(8,128)(2,1)}, bf16[512,256]{1,0:T(8,128)(2,1)S(1)}, u32[]{:S(2)}, u32[]{:S(2)}) collective-permute-start(bf16[512,256]{1,0:T(8,128)(2,1)} %get-tuple-element.264), channel_id=1, source_target_pairs={{0,2},{1,3},{2,0},{3,1},{4,6},{5,7},{6,4},{7,5},{8,10},{9,11},{10,... | collective-permute-start | bytes 786440 | tf_op jit(solution)/shard_map/ppermute | solution.py:254
  367.3 15.5 %collective-permute-start.36 = (bf16[512,256]{1,0:T(8,128)(2,1)}, bf16[512,256]{1,0:T(8,128)(2,1)S(1)}, u32[]{:S(2)}, u32[]{:S(2)}) collective-permute-start(bf16[512,256]{1,0:T(8,128)(2,1)} %get-tuple-element.263), channel_id=1, source_target_pairs={{0,4},{1,5},{2,6},{3,7},{4,0},{5,1},{6,2},{7,3},{8,12},{9,13},{10,... | collective-permute-start | bytes 786440 | tf_op jit(solution)/shard_map/ppermute | solution.py:254
  368.3 15.1 %collective-permute-start.37 = (bf16[512,256]{1,0:T(8,128)(2,1)S(1)}, bf16[512,256]{1,0:T(8,128)(2,1)S(1)}, u32[]{:S(2)}, u32[]{:S(2)}) collective-permute-start(bf16[512,256]{1,0:T(8,128)(2,1)S(1)} %copy-done.87), channel_id=1, source_target_pairs={{0,6},{1,7},{2,4},{3,5},{4,2},{5,3},{6,0},{7,1},{8,14},{9,15},{10,... | collective-permute-start | bytes 786440 | tf_op jit(solution)/shard_map/ppermute | solution.py:254
  372.2 30.6 %collective-permute-start.32 = (bf16[192,512]{1,0:T(8,128)(2,1)}, bf16[192,512]{1,0:T(8,128)(2,1)}, u32[]{:S(2)}, u32[]{:S(2)}) collective-permute-start(bf16[192,512]{1,0:T(8,128)(2,1)} %get-tuple-element.261), channel_id=1, source_target_pairs={{0,2},{1,3},{2,0},{3,1},{4,6},{5,7},{6,4},{7,5},{8,10},{9,11},{10,... | collective-permute-start | bytes 589832 | tf_op jit(solution)/shard_map/ppermute | solution.py:254
  373.8 30.9 %collective-permute-start.33 = (bf16[192,512]{1,0:T(8,128)(2,1)}, bf16[192,512]{1,0:T(8,128)(2,1)}, u32[]{:S(2)}, u32[]{:S(2)}) collective-permute-start(bf16[192,512]{1,0:T(8,128)(2,1)} %get-tuple-element.260), channel_id=1, source_target_pairs={{0,4},{1,5},{2,6},{3,7},{4,0},{5,1},{6,2},{7,3},{8,12},{9,13},{10,... | collective-permute-start | bytes 589832 | tf_op jit(solution)/shard_map/ppermute | solution.py:254
  380.9 24.5 %collective-permute-start.34 = (bf16[192,512]{1,0:T(8,128)(2,1)}, bf16[192,512]{1,0:T(8,128)(2,1)}, u32[]{:S(2)}, u32[]{:S(2)}) collective-permute-start(bf16[192,512]{1,0:T(8,128)(2,1)} %get-tuple-element.259), channel_id=1, source_target_pairs={{0,6},{1,7},{2,4},{3,5},{4,2},{5,3},{6,0},{7,1},{8,14},{9,15},{10,... | collective-permute-start | bytes 589832 | tf_op jit(solution)/shard_map/ppermute | solution.py:254
  382.8 75.1 %collective-permute-start.49 = (bf16[192,1536]{1,0:T(8,128)(2,1)}, bf16[192,1536]{1,0:T(8,128)(2,1)}, u32[]{:S(2)}, u32[]{:S(2)}) collective-permute-start(bf16[192,1536]{1,0:T(8,128)(2,1)} %get-tuple-element.249), channel_id=1, source_target_pairs={{0,2},{1,3},{2,0},{3,1},{4,6},{5,7},{6,4},{7,5},{8,10},{9,11},{10,... | collective-permute-start | bytes 1769480 | tf_op jit(solution)/shard_map/ppermute | solution.py:254
  386.8 22.8 %all-to-all-start.3 = ((bf16[4,128,256]{1,2,0:T(8,128)(2,1)}), bf16[4,128,256]{1,2,0:T(8,128)(2,1)}, u32[]{:S(2)}, u32[]{:S(2)}) async-start(bf16[4,128,256]{1,2,0:T(8,128)(2,1)} %copy.102), calls=%async_computation.3 | async-start | bytes 524288 | tf_op jit(solution)/shard_map/all_to_all | solution.py:609
  399.0 58.9 %collective-permute-start.50 = (bf16[192,1536]{1,0:T(8,128)(2,1)}, bf16[192,1536]{1,0:T(8,128)(2,1)}, u32[]{:S(2)}, u32[]{:S(2)}) collective-permute-start(bf16[192,1536]{1,0:T(8,128)(2,1)} %get-tuple-element.248), channel_id=1, source_target_pairs={{0,4},{1,5},{2,6},{3,7},{4,0},{5,1},{6,2},{7,3},{8,12},{9,13},{10,... | collective-permute-start | bytes 1769480 | tf_op jit(solution)/shard_map/ppermute | solution.py:254
  402.8 55.1 %collective-permute-start.51 = (bf16[192,1536]{1,0:T(8,128)(2,1)}, bf16[192,1536]{1,0:T(8,128)(2,1)}, u32[]{:S(2)}, u32[]{:S(2)}) collective-permute-start(bf16[192,1536]{1,0:T(8,128)(2,1)} %get-tuple-element.247), channel_id=1, source_target_pairs={{0,6},{1,7},{2,4},{3,5},{4,2},{5,3},{6,0},{7,1},{8,14},{9,15},{10,... | collective-permute-start | bytes 1769480 | tf_op jit(solution)/shard_map/ppermute | solution.py:254
  404.7 15.7 %collective-permute-start.43 = (bf16[192,256]{1,0:T(8,128)(2,1)S(1)}, bf16[192,256]{1,0:T(8,128)(2,1)S(1)}, u32[]{:S(2)}, u32[]{:S(2)}) collective-permute-start(bf16[192,256]{1,0:T(8,128)(2,1)S(1)} %get-tuple-element.267), channel_id=1, source_target_pairs={{0,2},{1,3},{2,0},{3,1},{4,6},{5,7},{6,4},{7,5},{8,10},{9,11},{10,... | collective-permute-start | bytes 294920 | tf_op jit(solution)/shard_map/ppermute | solution.py:254
  405.3 25.8 %collective-permute-start.44 = (bf16[192,256]{1,0:T(8,128)(2,1)S(1)}, bf16[192,256]{1,0:T(8,128)(2,1)S(1)}, u32[]{:S(2)}, u32[]{:S(2)}) collective-permute-start(bf16[192,256]{1,0:T(8,128)(2,1)S(1)} %get-tuple-element.266), channel_id=1, source_target_pairs={{0,4},{1,5},{2,6},{3,7},{4,0},{5,1},{6,2},{7,3},{8,12},{9,13},{10,... | collective-permute-start | bytes 294920 | tf_op jit(solution)/shard_map/ppermute | solution.py:254
  431.8 17.4 %collective-permute-start.42 = (bf16[192,512]{1,0:T(8,128)(2,1)S(1)}, bf16[192,512]{1,0:T(8,128)(2,1)S(1)}, u32[]{:S(2)}, u32[]{:S(2)}) collective-permute-start(bf16[192,512]{1,0:T(8,128)(2,1)S(1)} %select_select_fusion), channel_id=1, source_target_pairs={{0,24},{8,0},{16,8},{24,16},{1,25},{9,1},{17,9},{25,17},{2,26},{10... | collective-permute-start | bytes 589832 | tf_op jit(solution)/shard_map/ppermute | solution.py:236
  432.3 18.5 %collective-permute-start.41 = (bf16[192,512]{1,0:T(8,128)(2,1)S(1)}, bf16[192,512]{1,0:T(8,128)(2,1)S(1)}, u32[]{:S(2)}, u32[]{:S(2)}) collective-permute-start(bf16[192,512]{1,0:T(8,128)(2,1)S(1)} %select_select_fusion), channel_id=1, source_target_pairs={{0,16},{8,24},{16,0},{24,8},{1,17},{9,25},{17,1},{25,9},{2,18},{10... | collective-permute-start | bytes 589832 | tf_op jit(solution)/shard_map/ppermute | solution.py:236
  450.8 50.7 %collective-permute-start.46 = (bf16[192,256]{1,0:T(8,128)(2,1)}, bf16[192,256]{1,0:T(8,128)(2,1)}, u32[]{:S(2)}, u32[]{:S(2)}) collective-permute-start(bf16[192,256]{1,0:T(8,128)(2,1)} %add_convert_fusion.18), channel_id=1, source_target_pairs={{0,8},{8,16},{16,24},{24,0},{1,9},{9,17},{17,25},{25,1},{2,10},{10... | collective-permute-start | bytes 294920 | tf_op jit(solution)/shard_map/ppermute | solution.py:236
  454.8 46.7 %collective-permute-start.47 = (bf16[192,256]{1,0:T(8,128)(2,1)}, bf16[192,256]{1,0:T(8,128)(2,1)}, u32[]{:S(2)}, u32[]{:S(2)}) collective-permute-start(bf16[192,256]{1,0:T(8,128)(2,1)} %add_convert_fusion.18), channel_id=1, source_target_pairs={{0,16},{8,24},{16,0},{24,8},{1,17},{9,25},{17,1},{25,9},{2,18},{10... | collective-permute-start | bytes 294920 | tf_op jit(solution)/shard_map/ppermute | solution.py:236
  473.3 28.2 %collective-permute-start.48 = (bf16[192,256]{1,0:T(8,128)(2,1)}, bf16[192,256]{1,0:T(8,128)(2,1)}, u32[]{:S(2)}, u32[]{:S(2)}) collective-permute-start(bf16[192,256]{1,0:T(8,128)(2,1)} %add_convert_fusion.18), channel_id=1, source_target_pairs={{0,24},{8,0},{16,8},{24,16},{1,25},{9,1},{17,9},{25,17},{2,26},{10... | collective-permute-start | bytes 294920 | tf_op jit(solution)/shard_map/ppermute | solution.py:236
  (128 other events, 1213.6 us)
Sparse Core Ops, SparseCore 0:
  10.8 28.4 all-gather.8
  41.2 47.8 all-gather.10
  91.5 58.2 all-gather.12
  152.1 52.2 all-gather.14
  304.2 37.2 all-gather.18
  368.1 65.4 all-gather.16

commit v7 on v6

--- a/solution.py
+++ b/solution.py
@@ -1,4 +1,5 @@
 import functools
+import math
 
 import jax
 import jax.numpy as jnp
@@ -260,7 +261,7 @@
 
 
 def send_chips(parts, count):
-    return list(parts[0]) + [hop(parts[m], count, 2 * m) for m in range(1, count // 2)]
+    return [parts[0]] + [hop(parts[m], count, 2 * m) for m in range(1, count // 2)]
 
 
 def total_of(blocks):
@@ -274,24 +275,74 @@
     return lax.dynamic_index_in_dim(array, index, axis, keepdims=False)
 
 
-def pair_halves(product, shard, count):
-    width, cols = product.shape
-    cut = product.reshape(count // 2, 2, width // count, cols)
-    there = hop(take(cut, 1 - shard % 2, 1), count, 1)
-    return product.reshape(count, width // count, cols), there
-
-
-def pair_sums(halves, shard):
-    here, there = halves
-    sums = [(take(here, shard, 0), take(there, shard // 2, 0))]
-    for m in range(1, there.shape[0]):
-        each = take(here, shard ^ (2 * m), 0).astype(F32)
-        sums.append((each + take(there, (shard // 2) ^ m, 0).astype(F32)).astype(BF))
-    return sums
-
-
-def sum_rows(product, shard, count):
-    return total_of(send_chips(pair_sums(pair_halves(product, shard, count), shard), count))
+def product_kernel(core_ref, lhs_ref, rhs_ref, far_ref, near_ref):
+    part = lhs_ref.shape[1] // 2
+    rhs = rhs_ref[...]
+    first = dot_tn(lhs_ref[:, :part], rhs).astype(BF)
+    second = dot_tn(lhs_ref[:, part:], rhs).astype(BF)
+    core = core_ref[0]
+
+    @pl.when(core == 0)
+    def _():
+        near_ref[0] = first
+        far_ref[0] = second
+
+    @pl.when(core != 0)
+    def _():
+        near_ref[0] = second
+        far_ref[0] = first
+
+
+def split_product(lhs, rhs, shard, count):
+    tokens, width = lhs.shape
+    cols = rhs.shape[1]
+    part = width // count
+    if 2 * part % LANES:
+        cut = dot_tn(lhs, rhs).astype(BF).reshape(count // 2, 2, part, cols)
+        return take(cut, 1 - shard % 2, 1), take(cut, shard % 2, 1)
+    out = jax.ShapeDtypeStruct((count // 2, part, cols), BF)
+    out_spec = pl.BlockSpec((1, part, cols), lambda i: (i, 0, 0))
+    return pl.pallas_call(
+        product_kernel,
+        grid=(count // 2,),
+        in_specs=[
+            pl.BlockSpec(memory_space=pltpu.SMEM),
+            pl.BlockSpec((tokens, 2 * part), lambda i: (0, i)),
+            pl.BlockSpec((tokens, cols), lambda i: (0, 0)),
+        ],
+        out_specs=[out_spec, out_spec],
+        out_shape=[out, out],
+        compiler_params=pltpu.CompilerParams(vmem_limit_bytes=24 * 1024 * 1024),
+        cost_estimate=pl.CostEstimate(flops=0, bytes_accessed=0, transcendentals=0),
+    )((shard % 2).astype(jnp.int32).reshape(1), lhs, rhs)
+
+
+def pair_kernel(chip_ref, near_ref, there_ref, own_ref, *part_refs):
+    chip = chip_ref[0]
+    own_ref[...] = near_ref[chip].astype(F32) + there_ref[chip].astype(F32)
+    for m, part_ref in enumerate(part_refs):
+        which = chip ^ (m + 1)
+        part_ref[...] = (near_ref[which].astype(F32) + there_ref[which].astype(F32)).astype(BF)
+
+
+def pair_sums(near, far, shard, count):
+    there = hop(far, count, 1)
+    chips, part, cols = near.shape
+    tile = math.gcd(cols, 512)
+    if tile % LANES:
+        tile = cols
+    block = pl.BlockSpec((chips, part, tile), lambda i: (0, 0, i))
+    out_spec = pl.BlockSpec((part, tile), lambda i: (0, i))
+    out = jax.ShapeDtypeStruct((part, cols), BF)
+    return pl.pallas_call(
+        pair_kernel,
+        grid=(cols // tile,),
+        in_specs=[pl.BlockSpec(memory_space=pltpu.SMEM), block, block],
+        out_specs=[out_spec] * chips,
+        out_shape=[jax.ShapeDtypeStruct((part, cols), F32)] + [out] * (chips - 1),
+        compiler_params=pltpu.CompilerParams(vmem_limit_bytes=24 * 1024 * 1024),
+        cost_estimate=pl.CostEstimate(flops=0, bytes_accessed=0, transcendentals=0),
+    )((shard // 2).astype(jnp.int32).reshape(1), near, there)
 
 
 def two_parts(value):
@@ -449,7 +500,17 @@
     gate_up_full = expert_full[:, : 2 * piece]
     down_full = expert_full[:, 2 * piece : 3 * piece]
     router_full = expert_full[:, 3 * piece :]
-    attn_shard = jnp.concatenate([late_query, late_keyval], axis=1)
+    attn_shard = jnp.concatenate(
+        [
+            each
+            for s in range(seqs)
+            for each in (
+                late_query[:, s * q_cols : (s + 1) * q_cols],
+                late_keyval[:, s * kv_cols : (s + 1) * kv_cols],
+            )
+        ],
+        axis=1,
+    )
     attn_full = lax.all_gather(
         (attn_shard.astype(F32) * gain_one).astype(BF), "fsdp", axis=0, tiled=True
     )
@@ -531,22 +592,19 @@
     grad_returned = send_back([grad_rows[s] for s in range(seqs)], seqs)
     grad_returned = jnp.concatenate(grad_returned)
     held_out, held_hidden = after((grad_expert_out, hidden), returned_mark)
-    grad_down_sums = pair_sums(
-        pair_halves(dot_tn(held_out, held_hidden).astype(BF), shard, shards), shard
-    )
+    down_far, down_near = split_product(held_out, held_hidden, shard, shards)
     held_rows, held_gate_up = after((expert_rows, grad_gate_up_rows), returned_mark)
-    grad_gate_up_halves = pair_halves(
-        dot_tn(held_rows, held_gate_up).astype(BF), shard, shards
-    )
+    gate_up_far, gate_up_near = split_product(held_rows, held_gate_up, shard, shards)
+    grad_down_sums = pair_sums(down_near, down_far, shard, shards)
     kv_all = jnp.stack(after(kv_blocks, returned_mark))
     tokens_local = from_relative(after(token_blocks, returned_mark), z).reshape(local_rows, width)
     factor_local = root(tokens_local.astype(F32))
     ride_rows = jnp.concatenate([normed_two, jnp.ones((16, width), BF)], axis=0)
     product_rows = jnp.concatenate([tokens_local, ride_rows], axis=0)
 
-    grad_gate_up_sums = pair_sums(grad_gate_up_halves, shard)
+    grad_gate_up_sums = pair_sums(gate_up_near, gate_up_far, shard, shards)
     grad_down_shard = total_of(send_chips(grad_down_sums, shards)).astype(BF)
-    grad_returned = after(grad_returned, grad_down_shard)
+    grad_returned = after(grad_returned, grad_down_shard, product_rows)
     grad_normed_two = dot(dispatch, grad_returned) + dot_nt(grad_logits, router_full)
     grad_residual = grad_mixed + root_back(residual, factor_two, grad_normed_two)
     grad_branch = grad_residual.astype(BF)
@@ -565,23 +623,28 @@
         near.append(near_kv)
         far.append(far_kv)
         held = after(head_grad, part_q)
-    grad_gate_up_shard = total_of(after(grad_gate_up_blocks, part_q)).astype(BF)
+    grad_gate_up_blocks = after(grad_gate_up_blocks, grad_down, part_q)
+    grad_gate_up_shard = total_of(grad_gate_up_blocks).astype(BF)
     grad_gate_up_all = lax.all_gather(grad_gate_up_shard, "seq", axis=0, tiled=False)
     grad_q, near, far = after((grad_q, near, far), grad_gate_up_shard)
     grad_down = after(grad_down, part_q)
+    grad_q = jnp.concatenate(grad_q, axis=1)
     near = jnp.concatenate(near, axis=2)
     far = jnp.concatenate(far, axis=2)
     there = hop(far, shards, 1)
     pairs = [near[m].astype(F32) + there[m].astype(F32) for m in range(shards // 2)]
-    pairs = [(near[0], there[0])] + [each.astype(BF) for each in pairs[1:]]
-    grad_out_halves = pair_halves(
-        dot_tn(after(grad_branch, grad_gate_up_shard), attended).astype(BF), shard, shards
-    )
-    grad_q = jnp.concatenate(grad_q, axis=1)
-    token_grad_q = lax.all_to_all(
-        grad_q.astype(BF), "seq", split_axis=0, concat_axis=1, tiled=True
-    )
-    query_rhs = (grad_q * factor_local).astype(BF)
+    pairs = [pairs[0]] + [each.astype(BF) for each in pairs[1:]]
+    out_far, out_near = split_product(
+        after(grad_branch, grad_gate_up_shard), attended, shard, shards
+    )
+    out_sums = pair_sums(out_near, after(out_far, pairs), shard, shards)
+    out_blocks = send_chips(out_sums, shards)
+    grad_kv = total_of(after(send_chips(pairs, shards), out_sums))
+    grad_heads = jnp.concatenate([grad_q, grad_kv], axis=1)
+    token_grads = lax.all_to_all(
+        grad_heads.astype(BF), "seq", split_axis=0, concat_axis=1, tiled=True
+    )
+
     high, low = two_parts(squares)
     lane = jnp.arange(LANES, dtype=jnp.int32)[None, :]
     marks = jnp.where(lane == experts + 2 * (shard % 2), high, 0) + jnp.where(
@@ -590,70 +653,41 @@
     ride_columns = jnp.concatenate(
         [grad_logits, marks.astype(BF), jnp.zeros((15, LANES), BF)], axis=0
     )
+    head_cols = q_cols + kv_cols
     product_columns = jnp.concatenate(
         [
-            jnp.pad(query_rhs, ((0, 0), (0, LANES))),
-            jnp.pad(ride_columns, ((0, 0), (q_cols, 0))),
+            jnp.pad((grad_heads * factor_local).astype(BF), ((0, 0), (0, LANES))),
+            jnp.pad(ride_columns, ((0, 0), (head_cols, 0))),
         ],
         axis=0,
     )
-    query_product = dot_tn(product_rows, product_columns).astype(BF)
-    grad_query_sums = pair_sums(pair_halves(after(query_product, pairs), shard, shards), shard)
-    grad_query_sums = [
-        tuple(by_rows(part) for part in each) if isinstance(each, tuple) else by_rows(each)
-        for each in grad_query_sums
-    ]
-    grad_out_sums = pair_sums(after(grad_out_halves, pairs), shard)
-    grad_kv = total_of(after(send_chips(pairs, shards), grad_out_sums))
-    grad_out_blocks = send_chips(grad_out_sums, shards)
-    token_grad_kv = lax.all_to_all(
-        grad_kv.astype(BF), "seq", split_axis=0, concat_axis=1, tiled=True
-    )
-    keyval_rhs = (grad_kv * factor_local).astype(BF)
-    grad_keyval_sums = pair_sums(
-        pair_halves(dot_tn(tokens_local, keyval_rhs).astype(BF), shard, shards), shard
-    )
-    grad_query_part = total_of(after(send_chips(grad_query_sums, shards), grad_keyval_sums))
-    base_cols = q_cols + experts
+    head_far, head_near = split_product(product_rows, product_columns, shard, shards)
+    head_sums = pair_sums(head_near, head_far, shard, shards)
+    out_part = total_of(after(out_blocks, head_sums)).astype(BF)
+    out_parts = lax.all_to_all(
+        out_part.reshape(part, seqs, q_cols), "seq", split_axis=1, concat_axis=1, tiled=True
+    )
+    grad_normed = dot_nt(token_grads, attn_full)
+    grad_tokens = grad_residual + root_back(inputs, root(inputs), grad_normed)
+    head_part = total_of(send_chips(head_sums, shards))
+    base_cols = head_cols + experts
     plane_high, plane_low = two_parts(
-        jnp.sum(grad_query_part[:1, base_cols : base_cols + 4], axis=1, keepdims=True)
-    )
-    lanes = lax.broadcasted_iota(jnp.int32, grad_query_part.shape, 1)
-    grad_query_part = jnp.where(
+        jnp.sum(head_part[:1, base_cols : base_cols + 4], axis=1, keepdims=True)
+    )
+    lanes = lax.broadcasted_iota(jnp.int32, head_part.shape, 1)
+    head_part = jnp.where(
         lanes == base_cols,
         plane_high.astype(F32),
-        jnp.where(lanes == base_cols + 1, plane_low.astype(F32), grad_query_part),
-    )
-    grad_query_blocks = send_out([by_rows(grad_query_part.astype(BF))] * seqs, seqs)
-    grad_query_blocks = [by_rows(each) for each in grad_query_blocks]
-    grad_out_part = total_of(after(grad_out_blocks, grad_keyval_sums))
-    cut = grad_out_part.astype(BF)
-    grad_out_own = jnp.zeros((part, q_cols), F32)
-    out_parts = send_out(
-        [
-            lax.dynamic_slice_in_dim(cut, (z + s) % seqs * q_cols, q_cols, 1)
-            for s in range(seqs)
-        ],
-        seqs,
-    )
-    for each in out_parts:
-        grad_out_own = grad_out_own + each.astype(F32)
-    grad_out = place_columns(
-        send_out([grad_out_own.astype(BF)] * seqs, seqs), z, lambda block, column: block
-    ).T
-    grad_normed = dot_nt(after(token_grad_q, grad_kv), attn_full[:, : HEADS * HD]) + dot_nt(
-        token_grad_kv, attn_full[:, HEADS * HD :]
-    )
-    grad_tokens = grad_residual + root_back(inputs, root(inputs), grad_normed)
-
-    grad_keyval_part = total_of(after(send_chips(grad_keyval_sums, shards), grad_query_part))
-    grad_keyval_blocks = send_out([grad_keyval_part.astype(BF)] * seqs, seqs)
-    grad_gate_up, grad_gain_ffn = place_gate_up(grad_gate_up_all, w_gate_up, gain_two)
-    grad_keyval_blocks = after(grad_keyval_blocks, grad_gate_up)
-    sums = sum(
-        jnp.sum(each[:, q_cols : q_cols + LANES].astype(F32).reshape(part, 1, LANES), axis=1)
-        for each in grad_query_blocks
-    )
+        jnp.where(lanes == base_cols + 1, plane_low.astype(F32), head_part),
+    )
+    out_own = jnp.sum(out_parts.astype(F32), axis=1)
+    final_part = by_rows(jnp.concatenate([head_part, out_own], axis=1).astype(BF))
+    final_blocks = [by_rows(each) for each in send_out([final_part] * seqs, seqs)]
+    grad_gate_up, grad_gain_ffn = place_gate_up(
+        after(grad_gate_up_all, final_part), w_gate_up, gain_two
+    )
+    final_blocks = after(final_blocks, grad_gate_up)
+    sums = sum(each[:, head_cols : head_cols + LANES].astype(F32) for each in final_blocks)
     loss_value = jnp.sum(sums[0, experts : experts + 2]) / (width * valid_count)
     grad_router_base = sums[:, :experts]
 
@@ -667,11 +701,14 @@
         gain_parts.append(jnp.sum(columns_of(w_keyval, column, kv_cols) * block, axis=1))
         return block * gain_one
 
-    grad_query = place_columns([each[:, :q_cols] for each in grad_query_blocks], z, end_query)
-    grad_keyval = place_columns(grad_keyval_blocks, z, end_keyval)
+    grad_query = place_columns([each[:, :q_cols] for each in final_blocks], z, end_query)
+    grad_keyval = place_columns([each[:, q_cols:head_cols] for each in final_blocks], z, end_keyval)
+    grad_out = place_columns(
+        [each[:, head_cols + LANES :] for each in final_blocks], z, lambda block, column: block
+    ).T
     grad_gain_attn = sum(gain_parts)
     grad_down = (
-        after(grad_down, grad_kv).reshape(experts, split, part, piece)
+        after(grad_down, final_part).reshape(experts, split, part, piece)
         .transpose(0, 1, 3, 2)
         .reshape(experts, units, part)
         .astype(F32)

time: 526 us -> 529 us (level)
  Pallas kernels: 43.8 us -> 70.1 us
  waiting for transfers between devices: 189 us -> 204 us
  other arithmetic: 66.2 us -> 51.5 us
  matrix products: 53.5 us -> 45 us
  starting transfers between devices: 92.3 us -> 84.6 us
  local copies, waits for them, and re-layouts: 49.5 us -> 42.1 us
    all_to_all x2, waiting for transfers between devices: 0.01 us -> 29 us  [the longest x1 22.4 us: local(): lax.all_to_all(grad_heads.astype(BF), 'seq', split_axis=0, concat_axis=1,...]
    pallas_call x0 -> x8, Pallas kernels: none -> 25.8 us  [the longest x4 15.9 us: split_product(): pl.pallas_call(product_kernel, grid=(count // 2,), in_specs=[pl.BlockSpec...]
    convert_element_type x12 -> x5, other arithmetic: 23.7 us -> 8.92 us  [the longest x1 3.53 us: local(): grad_gate_up_shard = total_of(grad_gate_up_blocks).astype(BF)]
    squeeze x15 -> x0, local copies, waits for them, and re-layouts: 13.3 us -> none  [the longest x13 13.3 us: take(): return lax.dynamic_index_in_dim(array, index, axis, keepdims=False)]
    ppermute x27 -> x18, waiting for transfers between devices: 129 us -> 117 us  [shift(): lax.ppermute(block, 'seq', [(i, (i + step) % count) for i in range(count)])]
    ppermute x27 -> x18, starting transfers between devices: 42.5 us -> 32.9 us  [shift(): lax.ppermute(block, 'seq', [(i, (i + step) % count) for i in range(count)])]
    ppermute x31 -> x27, waiting for transfers between devices: 41.8 us -> 32.6 us  [hop(): return lax.ppermute(block, 'fsdp', [(i, i ^ mask) for i in range(count)])]
    dot_general x7 -> x2, matrix products: 10.1 us -> 0.92 us  [dot_tn(): lax.dot_general(a, b, (((0,), (0,)), ((), ())), preferred_element_type=F32)]
  transfers between devices with their start and end apart: 68 -> 55, of which waited for: 28 -> 27; matrix products, arithmetic and copies ran while one was open for 24% -> 17% of each run, Pallas kernels for 8% -> 14%
where the time goes in v7:
time: 529 us; the launch traced here: 519 us
  waiting for transfers between devices  204 us (39%)
  starting transfers between devices  84.6 us (16%)
  Pallas kernels  70.1 us (13%)
  other arithmetic  51.5 us (10%)
  matrix products  45 us (9%)
  local copies, waits for them, and re-layouts  42.1 us (8%)
  between operations  21.5 us (4%)
    ppermute x18, waiting for transfers between devices, shift(): lax.ppermute(block, 'seq', [(i, (i + step) % count) for i in range(count)])  117 us
    ppermute x18, starting transfers between devices, shift(): lax.ppermute(block, 'seq', [(i, (i + step) % count) for i in range(count)])  32.9 us
    ppermute x27, waiting for transfers between devices, hop(): return lax.ppermute(block, 'fsdp', [(i, i ^ mask) for i in range(count)])  32.6 us
    ppermute x27, starting transfers between devices, hop(): return lax.ppermute(block, 'fsdp', [(i, i ^ mask) for i in range(count)])  27 us
    pallas_call x2, Pallas kernels, flash_backward(): pl.pallas_call(functools.partial(backward_kernel, shards, seqs, rows, g,...  25.5 us
    dot_general x10, matrix products, dot(): return jnp.dot(a, b, preferred_element_type=F32)  23.8 us
    unnamed x219, local copies, waits for them, and re-layouts  22.8 us
    all_to_all x1, waiting for transfers between devices, local(): lax.all_to_all(grad_heads.astype(BF), 'seq', split_axis=0, concat_axis=1,...  22.4 us
  transfers between devices with their start and end apart: 55, of which 27 were waited for; matrix products, arithmetic and copies ran while one was open for 17% of the time, Pallas kernels for 14%

profile of v7, /device:TPU:12, one launch (start us, length us, event | category | flops | bytes accessed | tf_op | source)
XLA Modules:
  0.0 518.9 jit_solution(6851936749947222459)
XLA Ops:
  21.3 23.4 %collective-permute-done = bf16[136,1536]{1,0:T(8,128)(2,1)S(1)} collective-permute-done((bf16[136,1536]{1,0:T(8,128)(2,1)S(1)}, bf16[136,1536]{1,0:T(8,128)(2,1)S(1)}, u32[]{:S(2)}, u32[]{:S(2)}) %collective-permute-start) | collective-permute-done | bytes 417824 | tf_op jit(solution)/shard_map/ppermute | solution.py:237
  44.7 7.8 %collective-permute-done.1 = bf16[136,1536]{1,0:T(8,128)(2,1)S(1)} collective-permute-done((bf16[136,1536]{1,0:T(8,128)(2,1)S(1)}, bf16[136,1536]{1,0:T(8,128)(2,1)S(1)}, u32[]{:S(2)}, u32[]{:S(2)}) %collective-permute-start.1) | collective-permute-done | bytes 417824 | tf_op jit(solution)/shard_map/ppermute | solution.py:237
  62.7 7.4 %collective-permute-done.3.refs_1_ = bf16[528,256]{1,0:T(8,128)(2,1)S(1)} collective-permute-done((bf16[528,256]{1,0:T(8,128)(2,1)S(1)}, bf16[528,256]{1,0:T(8,128)(2,1)S(1)}, u32[]{:S(2)}, u32[]{:S(2)}) %collective-permute-start.3) | collective-permute-done | bytes 270368 | tf_op jit(solution)/shard_map/ppermute | solution.py:255
  70.1 7.4 %collective-permute-done.4.refs_2_ = bf16[528,256]{1,0:T(8,128)(2,1)S(1)} collective-permute-done((bf16[528,256]{1,0:T(8,128)(2,1)S(1)}, bf16[528,256]{1,0:T(8,128)(2,1)S(1)}, u32[]{:S(2)}, u32[]{:S(2)}) %collective-permute-start.4) | collective-permute-done | bytes 270368 | tf_op jit(solution)/shard_map/ppermute | solution.py:255
  77.5 3.3 collective-permute-done.5.refs_3_
  83.1 18.9 %shard_map.221 = (bf16[512,384]{1,0:T(8,128)(2,1)}, f32[512,384]{1,0:T(8,128)S(1)}, f32[512,384]{1,0:T(8,128)S(1)}) custom-call(bf16[528,256]{1,0:T(8,128)(2,1)S(1)} %maximum_maximum_fusion.1.refs_0_, bf16[528,256]{1,0:T(8,128)(2,1)S(1)} %collective-permute-done.3.refs_1_, bf16[528,256]{1,0:T(8,128)(2,1)S(1)} %collective-permute-done.4.refs_2_, ...), custom_call_target="tpu_custom_call" | custom-call | tf_op jit(solution)/shard_map/pallas_call | solution.py:114
  103.8 3.5 all-to-all-start
  107.5 9.1 %all-to-all-done = bf16[4,128,384]{2,1,0:T(8,128)(2,1)S(1)} async-done(((bf16[4,128,384]{2,1,0:T(8,128)(2,1)}), bf16[4,128,384]{2,1,0:T(8,128)(2,1)S(1)}, u32[]{:S(2)}, u32[]{:S(2)}) %all-to-all-start) | async-done | bytes 393248 | tf_op jit(solution)/shard_map/all_to_all | solution.py:535
  118.4 4.8 multiply_reduce_fusion.5
  129.2 3.0 collective-permute-start.10
  138.1 10.8 %collective-permute-done.11 = bf16[96,1536]{1,0:T(8,128)(2,1)S(1)} collective-permute-done((bf16[96,1536]{1,0:T(8,128)(2,1)}, bf16[96,1536]{1,0:T(8,128)(2,1)S(1)}, u32[]{:S(2)}, u32[]{:S(2)}) %collective-permute-start.11) | collective-permute-done | bytes 294944 | tf_op jit(solution)/shard_map/ppermute | solution.py:237
  149.0 5.3 %collective-permute-done.10 = bf16[96,1536]{1,0:T(8,128)(2,1)S(1)} collective-permute-done((bf16[96,1536]{1,0:T(8,128)(2,1)}, bf16[96,1536]{1,0:T(8,128)(2,1)S(1)}, u32[]{:S(2)}, u32[]{:S(2)}) %collective-permute-start.10) | collective-permute-done | bytes 294944 | tf_op jit(solution)/shard_map/ppermute | solution.py:237
  156.3 5.5 %fusion.3 = f32[384,2048]{1,0:T(8,128)S(1)} fusion(bf16[1536,3200]{1,0:T(8,128)(2,1)} %all-gather.13.cloned.1.call-done, bf16[96,1536]{1,0:T(8,128)(2,1)S(1)} %copy-done.81, bf16[96,1536]{1,0:T(8,128)(2,1)S(1)} %copy-done.83, bf16[96,1536]{1,0:T(8,128)(2,1)} %copy-done.84, bf16[96,1536]{1,0:T(8,128)(2,1)S(1)} %copy-done.73), kind=kOutput, calls=%fused_computation.5 | convolution fusion | flops 2420637696 | bytes 10616832 | tf_op jit(solution)/shard_map/dot_general | solution.py:24
  163.5 3.3 convolution_convert_fusion.2
  173.3 17.6 %collective-permute-done.15 = bf16[96,1536]{1,0:T(8,128)(2,1)} collective-permute-done((bf16[96,1536]{1,0:T(8,128)(2,1)}, bf16[96,1536]{1,0:T(8,128)(2,1)}, u32[]{:S(2)}, u32[]{:S(2)}) %collective-permute-start.15) | collective-permute-done | bytes 294944 | tf_op jit(solution)/shard_map/ppermute | solution.py:237
  190.9 4.2 collective-permute-done.14
  201.0 3.0 collective-permute-start.17
  203.9 2.9 collective-permute-start.16
  207.1 16.7 %collective-permute-done.18 = bf16[96,1536]{1,0:T(8,128)(2,1)} collective-permute-done((bf16[96,1536]{1,0:T(8,128)(2,1)}, bf16[96,1536]{1,0:T(8,128)(2,1)}, u32[]{:S(2)}, u32[]{:S(2)}) %collective-permute-start.18) | collective-permute-done | bytes 294944 | tf_op jit(solution)/shard_map/ppermute | solution.py:237
  223.8 3.9 collective-permute-done.16
  230.0 5.0 multiply_convert_fusion.2
  235.0 5.5 %fusion.5 = bf16[384,1536]{1,0:T(8,128)(2,1)S(1)} fusion(bf16[1536,3200]{1,0:T(8,128)(2,1)} %all-gather.13.cloned.1.call-done, bf16[384,1024]{1,0:T(8,128)(2,1)S(1)} %get-tuple-element.261, bf16[384,1024]{1,0:T(8,128)(2,1)S(1)} %get-tuple-element.260), kind=kOutput, calls=%fused_computation.10 | convolution fusion | flops 2419654656 | bytes 9043968 | tf_op jit(solution)/shard_map/dot_general | solution.py:28
  246.4 2.9 shard_map.222
  249.7 5.7 %shard_map.224 = (bf16[4,192,2048]{2,1,0:T(8,128)(2,1)}, bf16[4,192,2048]{2,1,0:T(8,128)(2,1)S(1)}) custom-call(s32[1]{0:T(128)} %bitcast.26.core_ref, bf16[384,1536]{1,0:T(8,128)(2,1)S(1)} %pad_maximum_fusion.1.lhs_ref, bf16[384,2048]{1,0:T(8,128)(2,1)S(1)} %pad_maximum_fusion.rhs_ref), custom_call_target="tpu_custom_call" | custom-call | tf_op jit(solution)/shard_map/pallas_call | solution.py:305
  259.7 3.4 collective-permute-start.25
  267.7 3.1 collective-permute-start.23
  273.1 8.1 %collective-permute-done.24 = bf16[192,1024]{1,0:T(8,128)(2,1)S(1)} collective-permute-done((bf16[192,1024]{1,0:T(8,128)(2,1)S(1)}, bf16[192,1024]{1,0:T(8,128)(2,1)S(1)}, u32[]{:S(2)}, u32[]{:S(2)}) %collective-permute-start.24) | collective-permute-done | bytes 393248 | tf_op jit(solution)/shard_map/ppermute | solution.py:255
  288.0 4.5 shard_map.225
  295.9 3.2 convolution_convert_fusion.3
  299.9 4.8 all-to-all-start.1
  307.9 15.9 %all-to-all-done.1 = bf16[128,4,384]{2,0,1:T(8,128)(2,1)S(1)} async-done(((bf16[128,4,384]{2,0,1:T(8,128)(2,1)}), bf16[128,4,384]{2,0,1:T(8,128)(2,1)S(1)}, u32[]{:S(2)}, u32[]{:S(2)}) %all-to-all-start.1) | async-done | bytes 393248 | tf_op jit(solution)/shard_map/all_to_all | solution.py:612
  326.1 12.7 %shard_map.226 = (f32[512,192]{1,0:T(8,128)S(1)}, bf16[4,512,128]{2,1,0:T(8,128)(2,1)S(1)}, bf16[4,512,128]{2,1,0:T(8,128)(2,1)S(1)}) custom-call(bf16[8,528,256]{2,1,0:T(8,128)(2,1)S(1)} %bitcast_dynamic-update-slice_fusion.8.refs_0_, bf16[512,384]{1,0:T(8,128)(2,1)S(1)} %slice_multiply_fusion.refs_8_.refs_1_, ...), custom_call_target="tpu_custom_call" | custom-call | tf_op jit(solution)/shard_map/pallas_call | solution.py:212
  340.5 12.8 %shard_map.227 = (f32[512,192]{1,0:T(8,128)S(1)}, bf16[4,512,128]{2,1,0:T(8,128)(2,1)S(1)}, bf16[4,512,128]{2,1,0:T(8,128)(2,1)S(1)}) custom-call(bf16[8,528,256]{2,1,0:T(8,128)(2,1)S(1)} %bitcast_dynamic-update-slice_fusion.8.refs_0_, bf16[512,384]{1,0:T(8,128)(2,1)S(1)} %slice_multiply_fusion.refs_8_.refs_1_, ...), custom_call_target="tpu_custom_call" | custom-call | tf_op jit(solution)/shard_map/pallas_call | solution.py:212
  355.7 3.5 add_convert_fusion
  360.3 3.5 shard_map.228
  373.5 3.0 shard_map.229
  380.0 3.8 collective-permute-done.32
  386.1 7.7 %all-to-all-start.3 = ((bf16[4,128,640]{1,2,0:T(8,128)(2,1)}), bf16[4,128,640]{1,2,0:T(8,128)(2,1)}, u32[]{:S(2)}, u32[]{:S(2)}) async-start(bf16[4,128,640]{1,2,0:T(8,128)(2,1)} %pad_maximum_fusion.5), calls=%async_computation.3 | async-start | bytes 1310720 | tf_op jit(solution)/shard_map/all_to_all | solution.py:644
  395.4 3.7 shard_map.230
  403.6 22.4 %all-to-all-done.3 = bf16[4,128,640]{1,2,0:T(8,128)(2,1)} async-done(((bf16[4,128,640]{1,2,0:T(8,128)(2,1)}), bf16[4,128,640]{1,2,0:T(8,128)(2,1)}, u32[]{:S(2)}, u32[]{:S(2)}) %all-to-all-start.3) | async-done | bytes 655392 | tf_op jit(solution)/shard_map/all_to_all | solution.py:644
  426.0 7.0 %fusion.34 = (f32[128]{0:T(128)S(1)}, f32[128]{0:T(128)S(1)}, f32[128,1536]{1,0:T(8,128)}) fusion(bf16[128,1536]{1,0:T(8,128)(2,1)} %param.14, bf16[128,2560]{0,1:T(8,128)(2,1)} %bitcast.59, bf16[1536,2560]{1,0:T(8,128)(2,1)} %all-gather.15.cloned.1.call-done), kind=kOutput, calls=%fused_computation.67 | convolution fusion | flops 1007615744 | bytes 9700352 | tf_op jit(solution)/shard_map/dot_general | solution.py:28
  441.3 8.2 %all-to-all-start.2 = ((bf16[192,4,384]{2,0,1:T(8,128)(2,1)}), bf16[192,4,384]{2,0,1:T(8,128)(2,1)}, u32[]{:S(2)}, u32[]{:S(2)}) async-start(bf16[192,4,384]{2,0,1:T(8,128)(2,1)} %bitcast.159), calls=%async_computation.2 | async-start | bytes 1179648 | tf_op jit(solution)/shard_map/all_to_all | solution.py:667
  453.9 6.6 %all-to-all-done.2 = bf16[192,4,384]{2,0,1:T(8,128)(2,1)} async-done(((bf16[192,4,384]{2,0,1:T(8,128)(2,1)}), bf16[192,4,384]{2,0,1:T(8,128)(2,1)}, u32[]{:S(2)}, u32[]{:S(2)}) %all-to-all-start.2) | async-done | bytes 589856 | tf_op jit(solution)/shard_map/all_to_all | solution.py:667
  461.7 3.5 collective-permute-start.43
  467.2 7.3 %fusion = (f32[192]{0:T(256)S(1)}, f32[4,192,2048]{2,1,0:T(8,128)}) fusion(bf16[4,192,2048]{2,1,0:T(8,128)(2,1)} %bitcast.155, bf16[4,192,2048]{2,1,0:T(8,128)(2,1)} %param.25, f32[192]{0:T(256)S(1)} %convert_element_type.398), kind=kLoop, calls=%fused_computation.2 | loop fusion | flops 7864128 | bytes 12584448 | tf_op jit(solution)/shard_map/reduce_sum | solution.py:393
  476.6 14.4 %collective-permute-done.42 = bf16[192,1152]{1,0:T(8,128)(2,1)S(1)} collective-permute-done((bf16[192,1152]{1,0:T(8,128)(2,1)S(1)}, bf16[192,1152]{1,0:T(8,128)(2,1)S(1)}, u32[]{:S(2)}, u32[]{:S(2)}) %collective-permute-start.42) | collective-permute-done | bytes 442400 | tf_op jit(solution)/shard_map/ppermute | solution.py:237
  490.9 4.7 collective-permute-done.43
  495.7 3.2 collective-permute-done.44
  (456 shorter events, 145.5 us)
Async XLA Ops:
  7.2 47.7 %all-gather.9.cloned.1.call-start = ((), (), s32[]{:S(2)}) async-start(), calls=%async_computation.4 | async-start | bytes 2211840 | tf_op jit(solution)/shard_map/all_gather | solution.py:456
  10.7 107.7 %all-gather.11.cloned.1.call-start = ((), (), s32[]{:S(2)}) async-start(), calls=%async_computation.5 | async-start | bytes 5308416 | tf_op jit(solution)/shard_map/all_gather | solution.py:484
  11.5 144.8 %all-gather.13.cloned.1.call-start = ((), (), s32[]{:S(2)}) async-start(), calls=%async_computation.6 | async-start | bytes 11059200 | tf_op jit(solution)/shard_map/all_gather | solution.py:499
  15.0 215.0 %all-gather.15.cloned.1.call-start = ((), (), s32[]{:S(2)}) async-start(), calls=%async_computation.7 | async-start | bytes 8847360 | tf_op jit(solution)/shard_map/all_gather | solution.py:514
  15.1 29.6 %collective-permute-start = (bf16[136,1536]{1,0:T(8,128)(2,1)S(1)}, bf16[136,1536]{1,0:T(8,128)(2,1)S(1)}, u32[]{:S(2)}, u32[]{:S(2)}) collective-permute-start(bf16[136,1536]{1,0:T(8,128)(2,1)S(1)} %fusion.43), channel_id=1, source_target_pairs={{0,8},{8,16},{16,24},{24,0},{1,9},{9,17},{17,25},{25,1},{2,10},{10... | collective-permute-start | bytes 1253384 | tf_op jit(solution)/shard_map/ppermute | solution.py:237
  16.7 35.8 %collective-permute-start.1 = (bf16[136,1536]{1,0:T(8,128)(2,1)S(1)}, bf16[136,1536]{1,0:T(8,128)(2,1)S(1)}, u32[]{:S(2)}, u32[]{:S(2)}) collective-permute-start(bf16[136,1536]{1,0:T(8,128)(2,1)S(1)} %fusion.43), channel_id=1, source_target_pairs={{0,16},{8,24},{16,0},{24,8},{1,17},{9,25},{17,1},{25,9},{2,18},{10... | collective-permute-start | bytes 1253384 | tf_op jit(solution)/shard_map/ppermute | solution.py:237
  18.0 36.3 %collective-permute-start.2 = (bf16[136,1536]{1,0:T(8,128)(2,1)S(1)}, bf16[136,1536]{1,0:T(8,128)(2,1)S(1)}, u32[]{:S(2)}, u32[]{:S(2)}) collective-permute-start(bf16[136,1536]{1,0:T(8,128)(2,1)S(1)} %fusion.43), channel_id=1, source_target_pairs={{0,24},{8,0},{16,8},{24,16},{1,25},{9,1},{17,9},{25,17},{2,26},{10... | collective-permute-start | bytes 1253384 | tf_op jit(solution)/shard_map/ppermute | solution.py:237
  60.6 16.9 %collective-permute-start.4 = (bf16[528,256]{1,0:T(8,128)(2,1)S(1)}, bf16[528,256]{1,0:T(8,128)(2,1)S(1)}, u32[]{:S(2)}, u32[]{:S(2)}) collective-permute-start(bf16[528,256]{1,0:T(8,128)(2,1)S(1)} %maximum_maximum_fusion.1.refs_0_), channel_id=1, source_target_pairs={{0,4},{1,5},{2,6},{3,7},{4,0},{5,1},{6,2},{7,3},{8,12},{9,13},{10,... | collective-permute-start | bytes 811016 | tf_op jit(solution)/shard_map/ppermute | solution.py:255
  61.1 19.7 %collective-permute-start.5 = (bf16[528,256]{1,0:T(8,128)(2,1)S(1)}, bf16[528,256]{1,0:T(8,128)(2,1)S(1)}, u32[]{:S(2)}, u32[]{:S(2)}) collective-permute-start(bf16[528,256]{1,0:T(8,128)(2,1)S(1)} %maximum_maximum_fusion.1.refs_0_), channel_id=1, source_target_pairs={{0,6},{1,7},{2,4},{3,5},{4,2},{5,3},{6,0},{7,1},{8,14},{9,15},{10,... | collective-permute-start | bytes 811016 | tf_op jit(solution)/shard_map/ppermute | solution.py:255
  62.7 18.3 %collective-permute-start.6 = (bf16[528,256]{1,0:T(8,128)(2,1)S(1)}, bf16[528,256]{1,0:T(8,128)(2,1)S(1)}, u32[]{:S(2)}, u32[]{:S(2)}) collective-permute-start(bf16[528,256]{1,0:T(8,128)(2,1)S(1)} %maximum_maximum_fusion.1.refs_0_), channel_id=1, source_target_pairs={{0,1},{1,0},{2,3},{3,2},{4,5},{5,4},{6,7},{7,6},{8,9},{9,8},{10,11... | collective-permute-start | bytes 811016 | tf_op jit(solution)/shard_map/ppermute | solution.py:255
  103.8 12.7 %all-to-all-start = ((bf16[4,128,384]{2,1,0:T(8,128)(2,1)}), bf16[4,128,384]{2,1,0:T(8,128)(2,1)S(1)}, u32[]{:S(2)}, u32[]{:S(2)}) async-start(bf16[4,128,384]{2,1,0:T(8,128)(2,1)} %bitcast.12), calls=%async_computation | async-start | bytes 786432 | tf_op jit(solution)/shard_map/all_to_all | solution.py:535
  107.3 248.4 %all-gather.17.cloned.1.call-start = ((), (), s32[]{:S(2)}) async-start(), calls=%async_computation.8 | async-start | bytes 1966080 | tf_op jit(solution)/shard_map/all_gather | solution.py:614
  125.0 13.1 %collective-permute-start.12 = (bf16[96,1536]{1,0:T(8,128)(2,1)}, bf16[96,1536]{1,0:T(8,128)(2,1)S(1)}, u32[]{:S(2)}, u32[]{:S(2)}) collective-permute-start(bf16[96,1536]{1,0:T(8,128)(2,1)} %get-tuple-element.283), channel_id=1, source_target_pairs={{0,24},{8,0},{16,8},{24,16},{1,25},{9,1},{17,9},{25,17},{2,26},{10... | collective-permute-start | bytes 884744 | tf_op jit(solution)/shard_map/ppermute | solution.py:237
  127.5 21.4 %collective-permute-start.11 = (bf16[96,1536]{1,0:T(8,128)(2,1)}, bf16[96,1536]{1,0:T(8,128)(2,1)S(1)}, u32[]{:S(2)}, u32[]{:S(2)}) collective-permute-start(bf16[96,1536]{1,0:T(8,128)(2,1)} %get-tuple-element.284), channel_id=1, source_target_pairs={{0,16},{8,24},{16,0},{24,8},{1,17},{9,25},{17,1},{25,9},{2,18},{10... | collective-permute-start | bytes 884744 | tf_op jit(solution)/shard_map/ppermute | solution.py:237
  129.2 25.0 %collective-permute-start.10 = (bf16[96,1536]{1,0:T(8,128)(2,1)}, bf16[96,1536]{1,0:T(8,128)(2,1)S(1)}, u32[]{:S(2)}, u32[]{:S(2)}) collective-permute-start(bf16[96,1536]{1,0:T(8,128)(2,1)} %get-tuple-element.285), channel_id=1, source_target_pairs={{0,8},{8,16},{16,24},{24,0},{1,9},{9,17},{17,25},{25,1},{2,10},{10... | collective-permute-start | bytes 884744 | tf_op jit(solution)/shard_map/ppermute | solution.py:237
  167.9 23.1 %collective-permute-start.15 = (bf16[96,1536]{1,0:T(8,128)(2,1)}, bf16[96,1536]{1,0:T(8,128)(2,1)}, u32[]{:S(2)}, u32[]{:S(2)}) collective-permute-start(bf16[96,1536]{1,0:T(8,128)(2,1)} %get-tuple-element.279), channel_id=1, source_target_pairs={{0,8},{8,16},{16,24},{24,0},{1,9},{9,17},{17,25},{25,1},{2,10},{10... | collective-permute-start | bytes 884744 | tf_op jit(solution)/shard_map/ppermute | solution.py:237
  170.5 24.6 %collective-permute-start.14 = (bf16[96,1536]{1,0:T(8,128)(2,1)}, bf16[96,1536]{1,0:T(8,128)(2,1)}, u32[]{:S(2)}, u32[]{:S(2)}) collective-permute-start(bf16[96,1536]{1,0:T(8,128)(2,1)} %get-tuple-element.280), channel_id=1, source_target_pairs={{0,16},{8,24},{16,0},{24,8},{1,17},{9,25},{17,1},{25,9},{2,18},{10... | collective-permute-start | bytes 884744 | tf_op jit(solution)/shard_map/ppermute | solution.py:237
  170.5 25.0 %collective-permute-start.13 = (bf16[96,1536]{1,0:T(8,128)(2,1)}, bf16[96,1536]{1,0:T(8,128)(2,1)}, u32[]{:S(2)}, u32[]{:S(2)}) collective-permute-start(bf16[96,1536]{1,0:T(8,128)(2,1)} %get-tuple-element.281), channel_id=1, source_target_pairs={{0,24},{8,0},{16,8},{24,16},{1,25},{9,1},{17,9},{25,17},{2,26},{10... | collective-permute-start | bytes 884744 | tf_op jit(solution)/shard_map/ppermute | solution.py:237
  201.0 22.8 %collective-permute-start.18 = (bf16[96,1536]{1,0:T(8,128)(2,1)}, bf16[96,1536]{1,0:T(8,128)(2,1)}, u32[]{:S(2)}, u32[]{:S(2)}) collective-permute-start(bf16[96,1536]{1,0:T(8,128)(2,1)} %get-tuple-element.275), channel_id=1, source_target_pairs={{0,24},{8,0},{16,8},{24,16},{1,25},{9,1},{17,9},{25,17},{2,26},{10... | collective-permute-start | bytes 884744 | tf_op jit(solution)/shard_map/ppermute | solution.py:237
  201.0 22.8 %collective-permute-start.17 = (bf16[96,1536]{1,0:T(8,128)(2,1)}, bf16[96,1536]{1,0:T(8,128)(2,1)}, u32[]{:S(2)}, u32[]{:S(2)}) collective-permute-start(bf16[96,1536]{1,0:T(8,128)(2,1)} %get-tuple-element.276), channel_id=1, source_target_pairs={{0,16},{8,24},{16,0},{24,8},{1,17},{9,25},{17,1},{25,9},{2,18},{10... | collective-permute-start | bytes 884744 | tf_op jit(solution)/shard_map/ppermute | solution.py:237
  203.9 23.7 %collective-permute-start.16 = (bf16[96,1536]{1,0:T(8,128)(2,1)}, bf16[96,1536]{1,0:T(8,128)(2,1)}, u32[]{:S(2)}, u32[]{:S(2)}) collective-permute-start(bf16[96,1536]{1,0:T(8,128)(2,1)} %get-tuple-element.277), channel_id=1, source_target_pairs={{0,8},{8,16},{16,24},{24,0},{1,9},{9,17},{17,25},{25,1},{2,10},{10... | collective-permute-start | bytes 884744 | tf_op jit(solution)/shard_map/ppermute | solution.py:237
  240.8 22.6 %collective-permute-start.21 = (bf16[96,1536]{1,0:T(8,128)(2,1)S(1)}, bf16[96,1536]{1,0:T(8,128)(2,1)S(1)}, u32[]{:S(2)}, u32[]{:S(2)}) collective-permute-start(bf16[96,1536]{1,0:T(8,128)(2,1)S(1)} %get-tuple-element.271), channel_id=1, source_target_pairs={{0,8},{8,16},{16,24},{24,0},{1,9},{9,17},{17,25},{25,1},{2,10},{10... | collective-permute-start | bytes 884744 | tf_op jit(solution)/shard_map/ppermute | solution.py:237
  243.3 24.4 %collective-permute-start.20 = (bf16[96,1536]{1,0:T(8,128)(2,1)S(1)}, bf16[96,1536]{1,0:T(8,128)(2,1)S(1)}, u32[]{:S(2)}, u32[]{:S(2)}) collective-permute-start(bf16[96,1536]{1,0:T(8,128)(2,1)S(1)} %get-tuple-element.272), channel_id=1, source_target_pairs={{0,16},{8,24},{16,0},{24,8},{1,17},{9,25},{17,1},{25,9},{2,18},{10... | collective-permute-start | bytes 884744 | tf_op jit(solution)/shard_map/ppermute | solution.py:237
  246.1 24.7 %collective-permute-start.19 = (bf16[96,1536]{1,0:T(8,128)(2,1)S(1)}, bf16[96,1536]{1,0:T(8,128)(2,1)S(1)}, u32[]{:S(2)}, u32[]{:S(2)}) collective-permute-start(bf16[96,1536]{1,0:T(8,128)(2,1)S(1)} %get-tuple-element.273), channel_id=1, source_target_pairs={{0,24},{8,0},{16,8},{24,16},{1,25},{9,1},{17,9},{25,17},{2,26},{10... | collective-permute-start | bytes 884744 | tf_op jit(solution)/shard_map/ppermute | solution.py:237
  255.4 31.4 %collective-permute-start.26 = (bf16[4,192,2048]{2,1,0:T(8,128)(2,1)}, bf16[4,192,2048]{2,1,0:T(8,128)(2,1)}, u32[]{:S(2)}, u32[]{:S(2)}) collective-permute-start(bf16[4,192,2048]{2,1,0:T(8,128)(2,1)} %get-tuple-element.138), channel_id=1, source_target_pairs={{0,1},{1,0},{2,3},{3,2},{4,5},{5,4},{6,7},{7,6},{8,9},{9,8},{10,11... | collective-permute-start | bytes 9437192 | tf_op jit(solution)/shard_map/ppermute | solution.py:255
  259.7 13.3 %collective-permute-start.25 = (bf16[192,1024]{1,0:T(8,128)(2,1)S(1)}, bf16[192,1024]{1,0:T(8,128)(2,1)S(1)}, u32[]{:S(2)}, u32[]{:S(2)}) collective-permute-start(bf16[192,1024]{1,0:T(8,128)(2,1)S(1)} %get-tuple-element.133), channel_id=1, source_target_pairs={{0,6},{1,7},{2,4},{3,5},{4,2},{5,3},{6,0},{7,1},{8,14},{9,15},{10,... | collective-permute-start | bytes 1179656 | tf_op jit(solution)/shard_map/ppermute | solution.py:255
  263.4 17.8 %collective-permute-start.24 = (bf16[192,1024]{1,0:T(8,128)(2,1)S(1)}, bf16[192,1024]{1,0:T(8,128)(2,1)S(1)}, u32[]{:S(2)}, u32[]{:S(2)}) collective-permute-start(bf16[192,1024]{1,0:T(8,128)(2,1)S(1)} %get-tuple-element.132), channel_id=1, source_target_pairs={{0,4},{1,5},{2,6},{3,7},{4,0},{5,1},{6,2},{7,3},{8,12},{9,13},{10,... | collective-permute-start | bytes 1179656 | tf_op jit(solution)/shard_map/ppermute | solution.py:255
  267.7 13.7 %collective-permute-start.23 = (bf16[192,1024]{1,0:T(8,128)(2,1)S(1)}, bf16[192,1024]{1,0:T(8,128)(2,1)S(1)}, u32[]{:S(2)}, u32[]{:S(2)}) collective-permute-start(bf16[192,1024]{1,0:T(8,128)(2,1)S(1)} %get-tuple-element.131), channel_id=1, source_target_pairs={{0,2},{1,3},{2,0},{3,1},{4,6},{5,7},{6,4},{7,5},{8,10},{9,11},{10,... | collective-permute-start | bytes 1179656 | tf_op jit(solution)/shard_map/ppermute | solution.py:255
  292.5 62.4 %collective-permute-start.27 = (bf16[192,2048]{1,0:T(8,128)(2,1)}, bf16[192,2048]{1,0:T(8,128)(2,1)}, u32[]{:S(2)}, u32[]{:S(2)}) collective-permute-start(bf16[192,2048]{1,0:T(8,128)(2,1)} %get-tuple-element.140), channel_id=1, source_target_pairs={{0,2},{1,3},{2,0},{3,1},{4,6},{5,7},{6,4},{7,5},{8,10},{9,11},{10,... | collective-permute-start | bytes 2359304 | tf_op jit(solution)/shard_map/ppermute | solution.py:255
  294.2 61.5 %collective-permute-start.28 = (bf16[192,2048]{1,0:T(8,128)(2,1)}, bf16[192,2048]{1,0:T(8,128)(2,1)}, u32[]{:S(2)}, u32[]{:S(2)}) collective-permute-start(bf16[192,2048]{1,0:T(8,128)(2,1)} %get-tuple-element.141), channel_id=1, source_target_pairs={{0,4},{1,5},{2,6},{3,7},{4,0},{5,1},{6,2},{7,3},{8,12},{9,13},{10,... | collective-permute-start | bytes 2359304 | tf_op jit(solution)/shard_map/ppermute | solution.py:255
  295.1 60.6 %collective-permute-start.29 = (bf16[192,2048]{1,0:T(8,128)(2,1)}, bf16[192,2048]{1,0:T(8,128)(2,1)}, u32[]{:S(2)}, u32[]{:S(2)}) collective-permute-start(bf16[192,2048]{1,0:T(8,128)(2,1)} %get-tuple-element.142), channel_id=1, source_target_pairs={{0,6},{1,7},{2,4},{3,5},{4,2},{5,3},{6,0},{7,1},{8,14},{9,15},{10,... | collective-permute-start | bytes 2359304 | tf_op jit(solution)/shard_map/ppermute | solution.py:255
  299.9 23.9 %all-to-all-start.1 = ((bf16[128,4,384]{2,0,1:T(8,128)(2,1)}), bf16[128,4,384]{2,0,1:T(8,128)(2,1)S(1)}, u32[]{:S(2)}, u32[]{:S(2)}) async-start(bf16[128,4,384]{2,0,1:T(8,128)(2,1)} %bitcast.164), calls=%async_computation.1 | async-start | bytes 786432 | tf_op jit(solution)/shard_map/all_to_all | solution.py:612
  304.7 162.4 %all-gather.19.cloned.1.call-start = ((), (), s32[]{:S(2)}) async-start(), calls=%async_computation.9 | async-start | bytes 3932160 | tf_op jit(solution)/shard_map/all_gather | solution.py:628
  367.7 12.2 %collective-permute-start.31 = (bf16[512,256]{1,0:T(8,128)(2,1)}, bf16[512,256]{1,0:T(8,128)(2,1)}, u32[]{:S(2)}, u32[]{:S(2)}) collective-permute-start(bf16[512,256]{1,0:T(8,128)(2,1)} %get-tuple-element.268), channel_id=1, source_target_pairs={{0,2},{1,3},{2,0},{3,1},{4,6},{5,7},{6,4},{7,5},{8,10},{9,11},{10,... | collective-permute-start | bytes 786440 | tf_op jit(solution)/shard_map/ppermute | solution.py:255
  369.4 14.4 %collective-permute-start.32 = (bf16[512,256]{1,0:T(8,128)(2,1)}, bf16[512,256]{1,0:T(8,128)(2,1)}, u32[]{:S(2)}, u32[]{:S(2)}) collective-permute-start(bf16[512,256]{1,0:T(8,128)(2,1)} %get-tuple-element.267), channel_id=1, source_target_pairs={{0,4},{1,5},{2,6},{3,7},{4,0},{5,1},{6,2},{7,3},{8,12},{9,13},{10,... | collective-permute-start | bytes 786440 | tf_op jit(solution)/shard_map/ppermute | solution.py:255
  370.4 13.4 %collective-permute-start.33 = (bf16[512,256]{1,0:T(8,128)(2,1)}, bf16[512,256]{1,0:T(8,128)(2,1)}, u32[]{:S(2)}, u32[]{:S(2)}) collective-permute-start(bf16[512,256]{1,0:T(8,128)(2,1)} %get-tuple-element.266), channel_id=1, source_target_pairs={{0,6},{1,7},{2,4},{3,5},{4,2},{5,3},{6,0},{7,1},{8,14},{9,15},{10,... | collective-permute-start | bytes 786440 | tf_op jit(solution)/shard_map/ppermute | solution.py:255
  386.1 39.9 %all-to-all-start.3 = ((bf16[4,128,640]{1,2,0:T(8,128)(2,1)}), bf16[4,128,640]{1,2,0:T(8,128)(2,1)}, u32[]{:S(2)}, u32[]{:S(2)}) async-start(bf16[4,128,640]{1,2,0:T(8,128)(2,1)} %pad_maximum_fusion.5), calls=%async_computation.3 | async-start | bytes 1310720 | tf_op jit(solution)/shard_map/all_to_all | solution.py:644
  399.2 34.3 %collective-permute-start.35 = (bf16[4,192,768]{2,1,0:T(8,128)(2,1)S(1)}, bf16[4,192,768]{2,1,0:T(8,128)(2,1)S(1)}, u32[]{:S(2)}, u32[]{:S(2)}) collective-permute-start(bf16[4,192,768]{2,1,0:T(8,128)(2,1)S(1)} %get-tuple-element.177), channel_id=1, source_target_pairs={{0,1},{1,0},{2,3},{3,2},{4,5},{5,4},{6,7},{7,6},{8,9},{9,8},{10,11... | collective-permute-start | bytes 3538952 | tf_op jit(solution)/shard_map/ppermute | solution.py:255
  400.1 37.5 %collective-permute-start.39 = (bf16[192,1536]{1,0:T(8,128)(2,1)}, bf16[192,1536]{1,0:T(8,128)(2,1)}, u32[]{:S(2)}, u32[]{:S(2)}) collective-permute-start(bf16[192,1536]{1,0:T(8,128)(2,1)} %copy-done.39), channel_id=1, source_target_pairs={{0,2},{1,3},{2,0},{3,1},{4,6},{5,7},{6,4},{7,5},{8,10},{9,11},{10,... | collective-permute-start | bytes 1769480 | tf_op jit(solution)/shard_map/ppermute | solution.py:255
  400.7 38.0 %collective-permute-start.40 = (bf16[192,1536]{1,0:T(8,128)(2,1)}, bf16[192,1536]{1,0:T(8,128)(2,1)}, u32[]{:S(2)}, u32[]{:S(2)}) collective-permute-start(bf16[192,1536]{1,0:T(8,128)(2,1)} %copy-done.38), channel_id=1, source_target_pairs={{0,4},{1,5},{2,6},{3,7},{4,0},{5,1},{6,2},{7,3},{8,12},{9,13},{10,... | collective-permute-start | bytes 1769480 | tf_op jit(solution)/shard_map/ppermute | solution.py:255
  401.9 36.8 %collective-permute-start.41 = (bf16[192,1536]{1,0:T(8,128)(2,1)}, bf16[192,1536]{1,0:T(8,128)(2,1)}, u32[]{:S(2)}, u32[]{:S(2)}) collective-permute-start(bf16[192,1536]{1,0:T(8,128)(2,1)} %copy-done.37), channel_id=1, source_target_pairs={{0,6},{1,7},{2,4},{3,5},{4,2},{5,3},{6,0},{7,1},{8,14},{9,15},{10,... | collective-permute-start | bytes 1769480 | tf_op jit(solution)/shard_map/ppermute | solution.py:255
  435.2 15.5 %collective-permute-start.38 = (bf16[192,768]{1,0:T(8,128)(2,1)}, bf16[192,768]{1,0:T(8,128)(2,1)S(1)}, u32[]{:S(2)}, u32[]{:S(2)}) collective-permute-start(bf16[192,768]{1,0:T(8,128)(2,1)} %get-tuple-element.181), channel_id=1, source_target_pairs={{0,6},{1,7},{2,4},{3,5},{4,2},{5,3},{6,0},{7,1},{8,14},{9,15},{10,... | collective-permute-start | bytes 884744 | tf_op jit(solution)/shard_map/ppermute | solution.py:255
  436.7 14.0 %collective-permute-start.37 = (bf16[192,768]{1,0:T(8,128)(2,1)S(1)}, bf16[192,768]{1,0:T(8,128)(2,1)}, u32[]{:S(2)}, u32[]{:S(2)}) collective-permute-start(bf16[192,768]{1,0:T(8,128)(2,1)S(1)} %get-tuple-element.180), channel_id=1, source_target_pairs={{0,4},{1,5},{2,6},{3,7},{4,0},{5,1},{6,2},{7,3},{8,12},{9,13},{10,... | collective-permute-start | bytes 884744 | tf_op jit(solution)/shard_map/ppermute | solution.py:255
  437.7 13.0 %collective-permute-start.36 = (bf16[192,768]{1,0:T(8,128)(2,1)S(1)}, bf16[192,768]{1,0:T(8,128)(2,1)}, u32[]{:S(2)}, u32[]{:S(2)}) collective-permute-start(bf16[192,768]{1,0:T(8,128)(2,1)S(1)} %get-tuple-element.179), channel_id=1, source_target_pairs={{0,2},{1,3},{2,0},{3,1},{4,6},{5,7},{6,4},{7,5},{8,10},{9,11},{10,... | collective-permute-start | bytes 884744 | tf_op jit(solution)/shard_map/ppermute | solution.py:255
  441.3 19.1 %all-to-all-start.2 = ((bf16[192,4,384]{2,0,1:T(8,128)(2,1)}), bf16[192,4,384]{2,0,1:T(8,128)(2,1)}, u32[]{:S(2)}, u32[]{:S(2)}) async-start(bf16[192,4,384]{2,0,1:T(8,128)(2,1)} %bitcast.159), calls=%async_computation.2 | async-start | bytes 1179648 | tf_op jit(solution)/shard_map/all_to_all | solution.py:667
  461.7 29.3 %collective-permute-start.42 = (bf16[192,1152]{1,0:T(8,128)(2,1)S(1)}, bf16[192,1152]{1,0:T(8,128)(2,1)S(1)}, u32[]{:S(2)}, u32[]{:S(2)}) collective-permute-start(bf16[192,1152]{1,0:T(8,128)(2,1)S(1)} %pad_maximum_fusion.6), channel_id=1, source_target_pairs={{0,8},{8,16},{16,24},{24,0},{1,9},{9,17},{17,25},{25,1},{2,10},{10... | collective-permute-start | bytes 1327112 | tf_op jit(solution)/shard_map/ppermute | solution.py:237
  461.7 33.9 %collective-permute-start.43 = (bf16[192,1152]{1,0:T(8,128)(2,1)S(1)}, bf16[192,1152]{1,0:T(8,128)(2,1)S(1)}, u32[]{:S(2)}, u32[]{:S(2)}) collective-permute-start(bf16[192,1152]{1,0:T(8,128)(2,1)S(1)} %pad_maximum_fusion.6), channel_id=1, source_target_pairs={{0,16},{8,24},{16,0},{24,8},{1,17},{9,25},{17,1},{25,9},{2,18},{10... | collective-permute-start | bytes 1327112 | tf_op jit(solution)/shard_map/ppermute | solution.py:237
  465.2 33.6 %collective-permute-start.44 = (bf16[192,1152]{1,0:T(8,128)(2,1)S(1)}, bf16[192,1152]{1,0:T(8,128)(2,1)S(1)}, u32[]{:S(2)}, u32[]{:S(2)}) collective-permute-start(bf16[192,1152]{1,0:T(8,128)(2,1)S(1)} %pad_maximum_fusion.6), channel_id=1, source_target_pairs={{0,24},{8,0},{16,8},{24,16},{1,25},{9,1},{17,9},{25,17},{2,26},{10... | collective-permute-start | bytes 1327112 | tf_op jit(solution)/shard_map/ppermute | solution.py:237
  (100 other events, 832.7 us)
Sparse Core Ops, SparseCore 0:
  10.8 28.3 all-gather.8
  41.2 47.8 all-gather.10
  91.5 58.2 all-gather.12
  152.1 52.3 all-gather.14
  282.6 43.0 all-gather.16
  366.5 75.8 all-gather.18

commit v8 on v7

--- a/solution.py
+++ b/solution.py
@@ -393,20 +393,61 @@
     return base * gain, jnp.sum(weight.astype(F32) * base, axis=(0, 2))
 
 
-def place_columns(blocks, place, finish):
+def place_kernel(count, q_cols, kv_cols, place_ref, *refs):
+    blocks = refs[:count]
+    w_query_ref, w_keyval_ref, gain_ref, query_ref, keyval_ref, out_ref, base_ref, sums_ref = refs[
+        count:
+    ]
+    gain = gain_ref[...]
+    base = jnp.zeros_like(gain)
+    sums = jnp.zeros(sums_ref.shape, F32)
+    for s in range(count):
+        owner = lax.rem(place_ref[0] + (count - s), count)
+        q_at = pl.ds(pl.multiple_of(owner * q_cols, LANES), q_cols)
+        kv_at = pl.ds(pl.multiple_of(owner * kv_cols, LANES), kv_cols)
+        query = blocks[s][:, :q_cols].astype(F32)
+        keyval = blocks[s][:, q_cols : q_cols + kv_cols].astype(F32)
+        start = q_cols + kv_cols
+        sums = sums + blocks[s][:, start : start + LANES].astype(F32)
+        out_ref[:, q_at] = blocks[s][:, start + LANES :].astype(F32)
+        base = base + jnp.sum(w_query_ref[:, q_at].astype(F32) * query, axis=1, keepdims=True)
+        base = base + jnp.sum(w_keyval_ref[:, kv_at].astype(F32) * keyval, axis=1, keepdims=True)
+        query_ref[:, q_at] = query * gain
+        keyval_ref[:, kv_at] = keyval * gain
+    base_ref[...] = jnp.broadcast_to(base, base_ref.shape)
+    sums_ref[...] = sums
+
+
+def place_heads(blocks, place, w_query, w_keyval, gain, q_cols, kv_cols):
     count = len(blocks)
-    rows, cols = blocks[0].shape
-    result = jnp.zeros((rows, count * cols), F32)
-    for s in range(count):
-        column = (place - s) % count * cols
-        result = lax.dynamic_update_slice(
-            result, finish(blocks[s].astype(F32), column), (0, column)
-        )
-    return result
-
-
-def columns_of(array, column, cols):
-    return lax.dynamic_slice_in_dim(array, column, cols, 1).astype(F32)
+    part = w_query.shape[0]
+    start = q_cols + kv_cols
+    if q_cols % LANES == 0 and kv_cols % LANES == 0:
+        wide = jax.ShapeDtypeStruct((part, count * q_cols), F32)
+        narrow = jax.ShapeDtypeStruct((part, count * kv_cols), F32)
+        lanes = jax.ShapeDtypeStruct((part, LANES), F32)
+        in_vmem = pl.BlockSpec(memory_space=pltpu.VMEM)
+        query, keyval, out, base, sums = pl.pallas_call(
+            functools.partial(place_kernel, count, q_cols, kv_cols),
+            in_specs=[pl.BlockSpec(memory_space=pltpu.SMEM)] + [in_vmem] * (count + 3),
+            out_specs=[in_vmem] * 5,
+            out_shape=[wide, narrow, wide, lanes, lanes],
+            compiler_params=pltpu.CompilerParams(vmem_limit_bytes=24 * 1024 * 1024),
+            cost_estimate=pl.CostEstimate(flops=0, bytes_accessed=0, transcendentals=0),
+        )(place.astype(jnp.int32).reshape(1), *blocks, w_query, w_keyval, gain)
+        return query, keyval, out, base[:, 0], sums
+    blocks = from_relative(blocks, place).astype(F32)
+
+    def columns(begin, end):
+        return blocks[:, :, begin:end].transpose(1, 0, 2).reshape(part, count * (end - begin))
+
+    query, keyval = columns(0, q_cols), columns(q_cols, start)
+    base = jnp.sum(w_query.astype(F32) * query, axis=1) + jnp.sum(
+        w_keyval.astype(F32) * keyval, axis=1
+    )
+    sums = jnp.sum(blocks[:, :, start : start + LANES], axis=0)
+    out = columns(start + LANES, start + LANES + q_cols)
+    return query * gain, keyval * gain, out, base, sums
 
 
 def local(
@@ -603,14 +644,15 @@
     product_rows = jnp.concatenate([tokens_local, ride_rows], axis=0)
 
     grad_gate_up_sums = pair_sums(gate_up_near, gate_up_far, shard, shards)
-    grad_down_shard = total_of(send_chips(grad_down_sums, shards)).astype(BF)
-    grad_returned = after(grad_returned, grad_down_shard, product_rows)
+    grad_down_blocks = send_chips(grad_down_sums, shards)
+    grad_returned = after(grad_returned, grad_down_sums, product_rows)
     grad_normed_two = dot(dispatch, grad_returned) + dot_nt(grad_logits, router_full)
     grad_residual = grad_mixed + root_back(residual, factor_two, grad_normed_two)
     grad_branch = grad_residual.astype(BF)
     grad_attended = dot_nt(after(grad_branch, grad_gate_up_sums), out_full).astype(BF)
     head_grad = lax.all_to_all(grad_attended, "seq", split_axis=1, concat_axis=0, tiled=True)
     grad_gate_up_blocks = send_chips(grad_gate_up_sums, shards)
+    grad_down_shard = total_of(after(grad_down_blocks, head_grad)).astype(BF)
     grad_down = lax.all_gather(grad_down_shard, "seq", axis=0, tiled=False)
 
     grad_q, near, far = [], [], []
@@ -667,9 +709,9 @@
     out_parts = lax.all_to_all(
         out_part.reshape(part, seqs, q_cols), "seq", split_axis=1, concat_axis=1, tiled=True
     )
-    grad_normed = dot_nt(token_grads, attn_full)
+    head_part = total_of(send_chips(head_sums, shards))
+    grad_normed = dot_nt(after(token_grads, head_part), attn_full)
     grad_tokens = grad_residual + root_back(inputs, root(inputs), grad_normed)
-    head_part = total_of(send_chips(head_sums, shards))
     base_cols = head_cols + experts
     plane_high, plane_low = two_parts(
         jnp.sum(head_part[:1, base_cols : base_cols + 4], axis=1, keepdims=True)
@@ -687,26 +729,11 @@
         after(grad_gate_up_all, final_part), w_gate_up, gain_two
     )
     final_blocks = after(final_blocks, grad_gate_up)
-    sums = sum(each[:, head_cols : head_cols + LANES].astype(F32) for each in final_blocks)
+    grad_query, grad_keyval, grad_out, grad_gain_attn, sums = place_heads(
+        final_blocks, z, w_query, w_keyval, gain_one, q_cols, kv_cols
+    )
     loss_value = jnp.sum(sums[0, experts : experts + 2]) / (width * valid_count)
     grad_router_base = sums[:, :experts]
-
-    gain_parts = []
-
-    def end_query(block, column):
-        gain_parts.append(jnp.sum(columns_of(w_query, column, q_cols) * block, axis=1))
-        return block * gain_one
-
-    def end_keyval(block, column):
-        gain_parts.append(jnp.sum(columns_of(w_keyval, column, kv_cols) * block, axis=1))
-        return block * gain_one
-
-    grad_query = place_columns([each[:, :q_cols] for each in final_blocks], z, end_query)
-    grad_keyval = place_columns([each[:, q_cols:head_cols] for each in final_blocks], z, end_keyval)
-    grad_out = place_columns(
-        [each[:, head_cols + LANES :] for each in final_blocks], z, lambda block, column: block
-    ).T
-    grad_gain_attn = sum(gain_parts)
     grad_down = (
         after(grad_down, final_part).reshape(experts, split, part, piece)
         .transpose(0, 1, 3, 2)
@@ -721,7 +748,7 @@
         grad_gain_attn,
         grad_query,
         grad_keyval,
-        grad_out,
+        grad_out.T,
         grad_gain_ffn,
         grad_router_base * gain_two,
         grad_gate_up,

time: 529 us -> 520 us (0.983); the launches traced: 519 us -> 515 us
  waiting for transfers between devices: 204 us -> 220 us
  other arithmetic: 51.5 us -> 43.3 us
  local copies, waits for them, and re-layouts: 42.1 us -> 35.7 us
    ppermute x27, waiting for transfers between devices: 32.6 us -> 65.7 us  [hop(): return lax.ppermute(block, 'fsdp', [(i, i ^ mask) for i in range(count)])]
    all_to_all x1, waiting for transfers between devices: 22.4 us -> 0.01 us  [local(): lax.all_to_all(grad_heads.astype(BF), 'seq', split_axis=0, concat_axis=1,...]
    ppermute x18, waiting for transfers between devices: 117 us -> 135 us  [shift(): lax.ppermute(block, 'seq', [(i, (i + step) % count) for i in range(count)])]
    all_to_all x1, waiting for transfers between devices: 15.9 us -> 0.01 us  [local(): lax.all_to_all(grad_attended, 'seq', split_axis=1, concat_axis=0, tiled=T...]
    all_gather x1, starting transfers between devices: 0.25 us -> 8.29 us  [local(): lax.all_gather(grad_gate_up_shard, 'seq', axis=0, tiled=False)]
  transfers between devices with their start and end apart: 55 -> 55, of which waited for: 27 -> 29; matrix products, arithmetic and copies ran while one was open for 17% -> 16% of each run, Pallas kernels for 14% -> 13%
where the time goes in v8:
time: 520 us; the launch traced here: 515 us
  waiting for transfers between devices  220 us (42%)
  starting transfers between devices  83.1 us (16%)
  Pallas kernels  70.9 us (14%)
  other arithmetic  43.3 us (8%)
  matrix products  41.5 us (8%)
  local copies, waits for them, and re-layouts  35.7 us (7%)
  between operations  21.3 us (4%)
    ppermute x18, waiting for transfers between devices, shift(): lax.ppermute(block, 'seq', [(i, (i + step) % count) for i in range(count)])  135 us
    ppermute x27, waiting for transfers between devices, hop(): return lax.ppermute(block, 'fsdp', [(i, i ^ mask) for i in range(count)])  65.7 us
    ppermute x18, starting transfers between devices, shift(): lax.ppermute(block, 'seq', [(i, (i + step) % count) for i in range(count)])  33.2 us
    pallas_call x2, Pallas kernels, flash_backward(): pl.pallas_call(functools.partial(backward_kernel, shards, seqs, rows, g,...  25.5 us
    ppermute x27, starting transfers between devices, hop(): return lax.ppermute(block, 'fsdp', [(i, i ^ mask) for i in range(count)])  22.7 us
    dot_general x10, matrix products, dot(): return jnp.dot(a, b, preferred_element_type=F32)  22.3 us
    pallas_call x1, Pallas kernels, flash_forward(): pl.pallas_call(functools.partial(forward_kernel, shards, seqs, rows, loca...  19 us
    dot_general x5, matrix products, dot_nt(): lax.dot_general(a, b, (((1,), (1,)), ((), ())), preferred_element_type=F32)  18.3 us
  transfers between devices with their start and end apart: 55, of which 29 were waited for; matrix products, arithmetic and copies ran while one was open for 16% of the time, Pallas kernels for 13%

profile of v8, /device:TPU:12, one launch (start us, length us, event | category | flops | bytes accessed | tf_op | source)
XLA Modules:
  0.0 515.3 jit_solution(10403267444038590590)
XLA Ops:
  21.3 23.4 %collective-permute-done = bf16[136,1536]{1,0:T(8,128)(2,1)S(1)} collective-permute-done((bf16[136,1536]{1,0:T(8,128)(2,1)S(1)}, bf16[136,1536]{1,0:T(8,128)(2,1)S(1)}, u32[]{:S(2)}, u32[]{:S(2)}) %collective-permute-start) | collective-permute-done | bytes 417824 | tf_op jit(solution)/shard_map/ppermute | solution.py:237
  44.7 7.8 %collective-permute-done.1 = bf16[136,1536]{1,0:T(8,128)(2,1)S(1)} collective-permute-done((bf16[136,1536]{1,0:T(8,128)(2,1)S(1)}, bf16[136,1536]{1,0:T(8,128)(2,1)S(1)}, u32[]{:S(2)}, u32[]{:S(2)}) %collective-permute-start.1) | collective-permute-done | bytes 417824 | tf_op jit(solution)/shard_map/ppermute | solution.py:237
  62.7 7.4 %collective-permute-done.3.refs_1_ = bf16[528,256]{1,0:T(8,128)(2,1)S(1)} collective-permute-done((bf16[528,256]{1,0:T(8,128)(2,1)S(1)}, bf16[528,256]{1,0:T(8,128)(2,1)S(1)}, u32[]{:S(2)}, u32[]{:S(2)}) %collective-permute-start.3) | collective-permute-done | bytes 270368 | tf_op jit(solution)/shard_map/ppermute | solution.py:255
  70.1 7.4 %collective-permute-done.4.refs_2_ = bf16[528,256]{1,0:T(8,128)(2,1)S(1)} collective-permute-done((bf16[528,256]{1,0:T(8,128)(2,1)S(1)}, bf16[528,256]{1,0:T(8,128)(2,1)S(1)}, u32[]{:S(2)}, u32[]{:S(2)}) %collective-permute-start.4) | collective-permute-done | bytes 270368 | tf_op jit(solution)/shard_map/ppermute | solution.py:255
  77.5 3.3 collective-permute-done.5.refs_3_
  83.1 19.0 %shard_map.221 = (bf16[512,384]{1,0:T(8,128)(2,1)}, f32[512,384]{1,0:T(8,128)S(1)}, f32[512,384]{1,0:T(8,128)S(1)}) custom-call(bf16[528,256]{1,0:T(8,128)(2,1)S(1)} %maximum_maximum_fusion.1.refs_0_, bf16[528,256]{1,0:T(8,128)(2,1)S(1)} %collective-permute-done.3.refs_1_, bf16[528,256]{1,0:T(8,128)(2,1)S(1)} %collective-permute-done.4.refs_2_, ...), custom_call_target="tpu_custom_call" | custom-call | tf_op jit(solution)/shard_map/pallas_call | solution.py:114
  103.9 4.1 all-to-all-start
  108.2 8.9 %all-to-all-done = bf16[4,128,384]{2,1,0:T(8,128)(2,1)} async-done(((bf16[4,128,384]{2,1,0:T(8,128)(2,1)}), bf16[4,128,384]{2,1,0:T(8,128)(2,1)}, u32[]{:S(2)}, u32[]{:S(2)}) %all-to-all-start) | async-done | bytes 393248 | tf_op jit(solution)/shard_map/all_to_all | solution.py:576
  118.2 4.4 multiply_reduce_fusion.5
  124.3 2.9 collective-permute-start.12
  128.7 3.1 collective-permute-start.10
  138.4 10.2 %collective-permute-done.11 = bf16[96,1536]{1,0:T(8,128)(2,1)S(1)} collective-permute-done((bf16[96,1536]{1,0:T(8,128)(2,1)}, bf16[96,1536]{1,0:T(8,128)(2,1)S(1)}, u32[]{:S(2)}, u32[]{:S(2)}) %collective-permute-start.11) | collective-permute-done | bytes 294944 | tf_op jit(solution)/shard_map/ppermute | solution.py:237
  148.6 5.3 %collective-permute-done.10 = bf16[96,1536]{1,0:T(8,128)(2,1)} collective-permute-done((bf16[96,1536]{1,0:T(8,128)(2,1)}, bf16[96,1536]{1,0:T(8,128)(2,1)}, u32[]{:S(2)}, u32[]{:S(2)}) %collective-permute-start.10) | collective-permute-done | bytes 294944 | tf_op jit(solution)/shard_map/ppermute | solution.py:237
  155.4 5.6 %fusion.3 = f32[384,2048]{1,0:T(8,128)S(1)} fusion(bf16[1536,3200]{1,0:T(8,128)(2,1)} %all-gather.13.cloned.1.call-done, bf16[96,1536]{1,0:T(8,128)(2,1)S(1)} %copy-done.79, bf16[96,1536]{1,0:T(8,128)(2,1)} %copy-done.80, bf16[96,1536]{1,0:T(8,128)(2,1)} %collective-permute-done.10, bf16[96,1536]{1,0:T(8,128)(2,1)S(1)} %copy-done.71), kind=kOutput, calls=%fused_computation.5 | convolution fusion | flops 2420637696 | bytes 10616832 | tf_op jit(solution)/shard_map/dot_general | solution.py:24
  161.5 4.0 convolution_convert_fusion.2
  171.8 17.6 %collective-permute-done.15 = bf16[96,1536]{1,0:T(8,128)(2,1)} collective-permute-done((bf16[96,1536]{1,0:T(8,128)(2,1)}, bf16[96,1536]{1,0:T(8,128)(2,1)}, u32[]{:S(2)}, u32[]{:S(2)}) %collective-permute-start.15) | collective-permute-done | bytes 294944 | tf_op jit(solution)/shard_map/ppermute | solution.py:237
  189.4 4.5 collective-permute-done.14
  200.0 2.9 collective-permute-start.17
  202.9 2.9 collective-permute-start.16
  206.0 16.8 %collective-permute-done.18 = bf16[96,1536]{1,0:T(8,128)(2,1)} collective-permute-done((bf16[96,1536]{1,0:T(8,128)(2,1)}, bf16[96,1536]{1,0:T(8,128)(2,1)}, u32[]{:S(2)}, u32[]{:S(2)}) %collective-permute-start.18) | collective-permute-done | bytes 294944 | tf_op jit(solution)/shard_map/ppermute | solution.py:237
  222.8 4.1 collective-permute-done.16
  229.2 4.9 multiply_convert_fusion.2
  234.2 5.5 %fusion.5 = bf16[384,1536]{1,0:T(8,128)(2,1)S(1)} fusion(bf16[1536,3200]{1,0:T(8,128)(2,1)} %all-gather.13.cloned.1.call-done, bf16[384,1024]{1,0:T(8,128)(2,1)S(1)} %get-tuple-element.273, bf16[384,1024]{1,0:T(8,128)(2,1)S(1)} %get-tuple-element.272), kind=kOutput, calls=%fused_computation.10 | convolution fusion | flops 2419654656 | bytes 9043968 | tf_op jit(solution)/shard_map/dot_general | solution.py:28
  245.1 2.9 shard_map.222
  248.4 4.8 shard_map.224
  254.6 8.0 %collective-permute-done.21 = bf16[96,1536]{1,0:T(8,128)(2,1)S(1)} collective-permute-done((bf16[96,1536]{1,0:T(8,128)(2,1)S(1)}, bf16[96,1536]{1,0:T(8,128)(2,1)S(1)}, u32[]{:S(2)}, u32[]{:S(2)}) %collective-permute-start.21) | collective-permute-done | bytes 294944 | tf_op jit(solution)/shard_map/ppermute | solution.py:237
  262.6 4.3 collective-permute-done.20
  277.9 3.8 all-to-all-start.1
  285.9 8.7 %collective-permute-done.27 = bf16[192,1024]{1,0:T(8,128)(2,1)S(1)} collective-permute-done((bf16[192,1024]{1,0:T(8,128)(2,1)}, bf16[192,1024]{1,0:T(8,128)(2,1)S(1)}, u32[]{:S(2)}, u32[]{:S(2)}) %collective-permute-start.27) | collective-permute-done | bytes 393248 | tf_op jit(solution)/shard_map/ppermute | solution.py:255
  294.6 8.2 %collective-permute-done.28 = bf16[192,1024]{1,0:T(8,128)(2,1)S(1)} collective-permute-done((bf16[192,1024]{1,0:T(8,128)(2,1)}, bf16[192,1024]{1,0:T(8,128)(2,1)S(1)}, u32[]{:S(2)}, u32[]{:S(2)}) %collective-permute-start.28) | collective-permute-done | bytes 393248 | tf_op jit(solution)/shard_map/ppermute | solution.py:255
  306.1 8.3 %all-gather.19.cloned.1.call-start = ((), (), s32[]{:S(2)}) async-start(), calls=%async_computation.9 | async-start | bytes 3932160 | tf_op jit(solution)/shard_map/all_gather | solution.py:670
  321.3 12.7 %shard_map.226 = (f32[512,192]{1,0:T(8,128)S(1)}, bf16[4,512,128]{2,1,0:T(8,128)(2,1)S(1)}, bf16[4,512,128]{2,1,0:T(8,128)(2,1)S(1)}) custom-call(bf16[8,528,256]{2,1,0:T(8,128)(2,1)S(1)} %bitcast_dynamic-update-slice_fusion.8.refs_0_, bf16[512,384]{1,0:T(8,128)(2,1)S(1)} %slice_multiply_fusion.refs_8_.refs_1_, ...), custom_call_target="tpu_custom_call" | custom-call | tf_op jit(solution)/shard_map/pallas_call | solution.py:212
  335.7 12.7 %shard_map.227 = (f32[512,192]{1,0:T(8,128)S(1)}, bf16[4,512,128]{2,1,0:T(8,128)(2,1)S(1)}, bf16[4,512,128]{2,1,0:T(8,128)(2,1)S(1)}) custom-call(bf16[8,528,256]{2,1,0:T(8,128)(2,1)S(1)} %bitcast_dynamic-update-slice_fusion.8.refs_0_, bf16[512,384]{1,0:T(8,128)(2,1)S(1)} %slice_multiply_fusion.refs_8_.refs_1_, ...), custom_call_target="tpu_custom_call" | custom-call | tf_op jit(solution)/shard_map/pallas_call | solution.py:212
  352.6 3.4 add_convert_fusion
  357.5 3.5 shard_map.228
  372.1 4.0 shard_map.229
  376.3 4.2 collective-permute-done.32
  383.8 4.4 shard_map.230
  393.2 4.2 all-to-all-start.3
  405.4 18.5 %collective-permute-done.40 = bf16[192,1536]{1,0:T(8,128)(2,1)} collective-permute-done((bf16[192,1536]{1,0:T(8,128)(2,1)}, bf16[192,1536]{1,0:T(8,128)(2,1)}, u32[]{:S(2)}, u32[]{:S(2)}) %collective-permute-start.40) | collective-permute-done | bytes 589856 | tf_op jit(solution)/shard_map/ppermute | solution.py:255
  426.4 3.5 collective-permute-done.37
  430.0 6.7 %all-to-all-start.2 = ((bf16[192,4,384]{2,0,1:T(8,128)(2,1)}), bf16[192,4,384]{2,0,1:T(8,128)(2,1)S(1)}, u32[]{:S(2)}, u32[]{:S(2)}) async-start(bf16[192,4,384]{2,0,1:T(8,128)(2,1)} %bitcast.150), calls=%async_computation.2 | async-start | bytes 1179648 | tf_op jit(solution)/shard_map/all_to_all | solution.py:709
  436.8 6.3 %fusion.34 = (f32[128]{0:T(128)S(1)}, f32[128]{0:T(128)S(1)}, f32[128,1536]{1,0:T(8,128)S(1)}) fusion(bf16[128,1536]{1,0:T(8,128)(2,1)S(1)} %copy-done.53, bf16[128,2560]{0,1:T(8,128)(2,1)} %bitcast.61, bf16[1536,2560]{1,0:T(8,128)(2,1)} %all-gather.15.cloned.1.call-done), kind=kOutput, calls=%fused_computation.67 | convolution fusion | flops 1007615744 | bytes 9700352 | tf_op jit(solution)/shard_map/dot_general | solution.py:28
  446.9 9.3 %all-to-all-done.2 = bf16[192,4,384]{2,0,1:T(8,128)(2,1)S(1)} async-done(((bf16[192,4,384]{2,0,1:T(8,128)(2,1)}), bf16[192,4,384]{2,0,1:T(8,128)(2,1)S(1)}, u32[]{:S(2)}, u32[]{:S(2)}) %all-to-all-start.2) | async-done | bytes 589856 | tf_op jit(solution)/shard_map/all_to_all | solution.py:709
  458.3 4.2 collective-permute-start.43
  462.5 7.3 %fusion = (f32[192]{0:T(256)S(1)}, f32[4,192,2048]{2,1,0:T(8,128)}) fusion(bf16[4,192,2048]{2,1,0:T(8,128)(2,1)} %bitcast.159, bf16[4,192,2048]{2,1,0:T(8,128)(2,1)} %param.25, f32[192]{0:T(256)S(1)} %convert_element_type.326), kind=kLoop, calls=%fused_computation.2 | loop fusion | flops 7864128 | bytes 12584448 | tf_op jit(solution)/shard_map/reduce_sum | solution.py:393
  471.9 24.4 %collective-permute-done.43.refs_2_ = bf16[192,1152]{1,0:T(8,128)(2,1)S(1)} collective-permute-done((bf16[192,1152]{1,0:T(8,128)(2,1)S(1)}, bf16[192,1152]{1,0:T(8,128)(2,1)S(1)}, u32[]{:S(2)}, u32[]{:S(2)}) %collective-permute-start.43) | collective-permute-done | bytes 442400 | tf_op jit(solution)/shard_map/ppermute | solution.py:237
  496.2 3.9 collective-permute-done.44.refs_3_
  (446 shorter events, 135.8 us)
Async XLA Ops:
  7.2 47.7 %all-gather.9.cloned.1.call-start = ((), (), s32[]{:S(2)}) async-start(), calls=%async_computation.4 | async-start | bytes 2211840 | tf_op jit(solution)/shard_map/all_gather | solution.py:497
  10.7 107.5 %all-gather.11.cloned.1.call-start = ((), (), s32[]{:S(2)}) async-start(), calls=%async_computation.5 | async-start | bytes 5308416 | tf_op jit(solution)/shard_map/all_gather | solution.py:525
  11.5 143.9 %all-gather.13.cloned.1.call-start = ((), (), s32[]{:S(2)}) async-start(), calls=%async_computation.6 | async-start | bytes 11059200 | tf_op jit(solution)/shard_map/all_gather | solution.py:540
  15.0 214.2 %all-gather.15.cloned.1.call-start = ((), (), s32[]{:S(2)}) async-start(), calls=%async_computation.7 | async-start | bytes 8847360 | tf_op jit(solution)/shard_map/all_gather | solution.py:555
  15.1 29.6 %collective-permute-start = (bf16[136,1536]{1,0:T(8,128)(2,1)S(1)}, bf16[136,1536]{1,0:T(8,128)(2,1)S(1)}, u32[]{:S(2)}, u32[]{:S(2)}) collective-permute-start(bf16[136,1536]{1,0:T(8,128)(2,1)S(1)} %fusion.43), channel_id=1, source_target_pairs={{0,8},{8,16},{16,24},{24,0},{1,9},{9,17},{17,25},{25,1},{2,10},{10... | collective-permute-start | bytes 1253384 | tf_op jit(solution)/shard_map/ppermute | solution.py:237
  16.7 35.8 %collective-permute-start.1 = (bf16[136,1536]{1,0:T(8,128)(2,1)S(1)}, bf16[136,1536]{1,0:T(8,128)(2,1)S(1)}, u32[]{:S(2)}, u32[]{:S(2)}) collective-permute-start(bf16[136,1536]{1,0:T(8,128)(2,1)S(1)} %fusion.43), channel_id=1, source_target_pairs={{0,16},{8,24},{16,0},{24,8},{1,17},{9,25},{17,1},{25,9},{2,18},{10... | collective-permute-start | bytes 1253384 | tf_op jit(solution)/shard_map/ppermute | solution.py:237
  18.0 36.3 %collective-permute-start.2 = (bf16[136,1536]{1,0:T(8,128)(2,1)S(1)}, bf16[136,1536]{1,0:T(8,128)(2,1)S(1)}, u32[]{:S(2)}, u32[]{:S(2)}) collective-permute-start(bf16[136,1536]{1,0:T(8,128)(2,1)S(1)} %fusion.43), channel_id=1, source_target_pairs={{0,24},{8,0},{16,8},{24,16},{1,25},{9,1},{17,9},{25,17},{2,26},{10... | collective-permute-start | bytes 1253384 | tf_op jit(solution)/shard_map/ppermute | solution.py:237
  59.1 11.0 %collective-permute-start.3 = (bf16[528,256]{1,0:T(8,128)(2,1)S(1)}, bf16[528,256]{1,0:T(8,128)(2,1)S(1)}, u32[]{:S(2)}, u32[]{:S(2)}) collective-permute-start(bf16[528,256]{1,0:T(8,128)(2,1)S(1)} %maximum_maximum_fusion.1.refs_0_), channel_id=1, source_target_pairs={{0,2},{1,3},{2,0},{3,1},{4,6},{5,7},{6,4},{7,5},{8,10},{9,11},{10,... | collective-permute-start | bytes 811016 | tf_op jit(solution)/shard_map/ppermute | solution.py:255
  60.6 16.9 %collective-permute-start.4 = (bf16[528,256]{1,0:T(8,128)(2,1)S(1)}, bf16[528,256]{1,0:T(8,128)(2,1)S(1)}, u32[]{:S(2)}, u32[]{:S(2)}) collective-permute-start(bf16[528,256]{1,0:T(8,128)(2,1)S(1)} %maximum_maximum_fusion.1.refs_0_), channel_id=1, source_target_pairs={{0,4},{1,5},{2,6},{3,7},{4,0},{5,1},{6,2},{7,3},{8,12},{9,13},{10,... | collective-permute-start | bytes 811016 | tf_op jit(solution)/shard_map/ppermute | solution.py:255
  61.2 19.7 %collective-permute-start.5 = (bf16[528,256]{1,0:T(8,128)(2,1)S(1)}, bf16[528,256]{1,0:T(8,128)(2,1)S(1)}, u32[]{:S(2)}, u32[]{:S(2)}) collective-permute-start(bf16[528,256]{1,0:T(8,128)(2,1)S(1)} %maximum_maximum_fusion.1.refs_0_), channel_id=1, source_target_pairs={{0,6},{1,7},{2,4},{3,5},{4,2},{5,3},{6,0},{7,1},{8,14},{9,15},{10,... | collective-permute-start | bytes 811016 | tf_op jit(solution)/shard_map/ppermute | solution.py:255
  62.7 18.3 %collective-permute-start.6 = (bf16[528,256]{1,0:T(8,128)(2,1)S(1)}, bf16[528,256]{1,0:T(8,128)(2,1)S(1)}, u32[]{:S(2)}, u32[]{:S(2)}) collective-permute-start(bf16[528,256]{1,0:T(8,128)(2,1)S(1)} %maximum_maximum_fusion.1.refs_0_), channel_id=1, source_target_pairs={{0,1},{1,0},{2,3},{3,2},{4,5},{5,4},{6,7},{7,6},{8,9},{9,8},{10,11... | collective-permute-start | bytes 811016 | tf_op jit(solution)/shard_map/ppermute | solution.py:255
  103.9 13.2 %all-to-all-start = ((bf16[4,128,384]{2,1,0:T(8,128)(2,1)}), bf16[4,128,384]{2,1,0:T(8,128)(2,1)}, u32[]{:S(2)}, u32[]{:S(2)}) async-start(bf16[4,128,384]{2,1,0:T(8,128)(2,1)} %bitcast.12), calls=%async_computation | async-start | bytes 786432 | tf_op jit(solution)/shard_map/all_to_all | solution.py:576
  124.3 14.1 %collective-permute-start.12 = (bf16[96,1536]{1,0:T(8,128)(2,1)}, bf16[96,1536]{1,0:T(8,128)(2,1)S(1)}, u32[]{:S(2)}, u32[]{:S(2)}) collective-permute-start(bf16[96,1536]{1,0:T(8,128)(2,1)} %get-tuple-element.295), channel_id=1, source_target_pairs={{0,24},{8,0},{16,8},{24,16},{1,25},{9,1},{17,9},{25,17},{2,26},{10... | collective-permute-start | bytes 884744 | tf_op jit(solution)/shard_map/ppermute | solution.py:237
  127.2 21.4 %collective-permute-start.11 = (bf16[96,1536]{1,0:T(8,128)(2,1)}, bf16[96,1536]{1,0:T(8,128)(2,1)S(1)}, u32[]{:S(2)}, u32[]{:S(2)}) collective-permute-start(bf16[96,1536]{1,0:T(8,128)(2,1)} %get-tuple-element.296), channel_id=1, source_target_pairs={{0,16},{8,24},{16,0},{24,8},{1,17},{9,25},{17,1},{25,9},{2,18},{10... | collective-permute-start | bytes 884744 | tf_op jit(solution)/shard_map/ppermute | solution.py:237
  128.7 25.2 %collective-permute-start.10 = (bf16[96,1536]{1,0:T(8,128)(2,1)}, bf16[96,1536]{1,0:T(8,128)(2,1)}, u32[]{:S(2)}, u32[]{:S(2)}) collective-permute-start(bf16[96,1536]{1,0:T(8,128)(2,1)} %get-tuple-element.297), channel_id=1, source_target_pairs={{0,8},{8,16},{16,24},{24,0},{1,9},{9,17},{17,25},{25,1},{2,10},{10... | collective-permute-start | bytes 884744 | tf_op jit(solution)/shard_map/ppermute | solution.py:237
  166.5 22.8 %collective-permute-start.15 = (bf16[96,1536]{1,0:T(8,128)(2,1)}, bf16[96,1536]{1,0:T(8,128)(2,1)}, u32[]{:S(2)}, u32[]{:S(2)}) collective-permute-start(bf16[96,1536]{1,0:T(8,128)(2,1)} %get-tuple-element.291), channel_id=1, source_target_pairs={{0,8},{8,16},{16,24},{24,0},{1,9},{9,17},{17,25},{25,1},{2,10},{10... | collective-permute-start | bytes 884744 | tf_op jit(solution)/shard_map/ppermute | solution.py:237
  169.0 24.9 %collective-permute-start.14 = (bf16[96,1536]{1,0:T(8,128)(2,1)}, bf16[96,1536]{1,0:T(8,128)(2,1)}, u32[]{:S(2)}, u32[]{:S(2)}) collective-permute-start(bf16[96,1536]{1,0:T(8,128)(2,1)} %get-tuple-element.292), channel_id=1, source_target_pairs={{0,16},{8,24},{16,0},{24,8},{1,17},{9,25},{17,1},{25,9},{2,18},{10... | collective-permute-start | bytes 884744 | tf_op jit(solution)/shard_map/ppermute | solution.py:237
  169.0 25.2 %collective-permute-start.13 = (bf16[96,1536]{1,0:T(8,128)(2,1)}, bf16[96,1536]{1,0:T(8,128)(2,1)}, u32[]{:S(2)}, u32[]{:S(2)}) collective-permute-start(bf16[96,1536]{1,0:T(8,128)(2,1)} %get-tuple-element.293), channel_id=1, source_target_pairs={{0,24},{8,0},{16,8},{24,16},{1,25},{9,1},{17,9},{25,17},{2,26},{10... | collective-permute-start | bytes 884744 | tf_op jit(solution)/shard_map/ppermute | solution.py:237
  200.0 22.8 %collective-permute-start.18 = (bf16[96,1536]{1,0:T(8,128)(2,1)}, bf16[96,1536]{1,0:T(8,128)(2,1)}, u32[]{:S(2)}, u32[]{:S(2)}) collective-permute-start(bf16[96,1536]{1,0:T(8,128)(2,1)} %get-tuple-element.287), channel_id=1, source_target_pairs={{0,24},{8,0},{16,8},{24,16},{1,25},{9,1},{17,9},{25,17},{2,26},{10... | collective-permute-start | bytes 884744 | tf_op jit(solution)/shard_map/ppermute | solution.py:237
  200.0 22.8 %collective-permute-start.17 = (bf16[96,1536]{1,0:T(8,128)(2,1)}, bf16[96,1536]{1,0:T(8,128)(2,1)}, u32[]{:S(2)}, u32[]{:S(2)}) collective-permute-start(bf16[96,1536]{1,0:T(8,128)(2,1)} %get-tuple-element.288), channel_id=1, source_target_pairs={{0,16},{8,24},{16,0},{24,8},{1,17},{9,25},{17,1},{25,9},{2,18},{10... | collective-permute-start | bytes 884744 | tf_op jit(solution)/shard_map/ppermute | solution.py:237
  202.9 24.0 %collective-permute-start.16 = (bf16[96,1536]{1,0:T(8,128)(2,1)}, bf16[96,1536]{1,0:T(8,128)(2,1)}, u32[]{:S(2)}, u32[]{:S(2)}) collective-permute-start(bf16[96,1536]{1,0:T(8,128)(2,1)} %get-tuple-element.289), channel_id=1, source_target_pairs={{0,8},{8,16},{16,24},{24,0},{1,9},{9,17},{17,25},{25,1},{2,10},{10... | collective-permute-start | bytes 884744 | tf_op jit(solution)/shard_map/ppermute | solution.py:237
  240.0 22.6 %collective-permute-start.21 = (bf16[96,1536]{1,0:T(8,128)(2,1)S(1)}, bf16[96,1536]{1,0:T(8,128)(2,1)S(1)}, u32[]{:S(2)}, u32[]{:S(2)}) collective-permute-start(bf16[96,1536]{1,0:T(8,128)(2,1)S(1)} %get-tuple-element.283), channel_id=1, source_target_pairs={{0,8},{8,16},{16,24},{24,0},{1,9},{9,17},{17,25},{25,1},{2,10},{10... | collective-permute-start | bytes 884744 | tf_op jit(solution)/shard_map/ppermute | solution.py:237
  242.5 24.4 %collective-permute-start.20 = (bf16[96,1536]{1,0:T(8,128)(2,1)S(1)}, bf16[96,1536]{1,0:T(8,128)(2,1)S(1)}, u32[]{:S(2)}, u32[]{:S(2)}) collective-permute-start(bf16[96,1536]{1,0:T(8,128)(2,1)S(1)} %get-tuple-element.284), channel_id=1, source_target_pairs={{0,16},{8,24},{16,0},{24,8},{1,17},{9,25},{17,1},{25,9},{2,18},{10... | collective-permute-start | bytes 884744 | tf_op jit(solution)/shard_map/ppermute | solution.py:237
  245.1 24.2 %collective-permute-start.19 = (bf16[96,1536]{1,0:T(8,128)(2,1)S(1)}, bf16[96,1536]{1,0:T(8,128)(2,1)S(1)}, u32[]{:S(2)}, u32[]{:S(2)}) collective-permute-start(bf16[96,1536]{1,0:T(8,128)(2,1)S(1)} %get-tuple-element.285), channel_id=1, source_target_pairs={{0,24},{8,0},{16,8},{24,16},{1,25},{9,1},{17,9},{25,17},{2,26},{10... | collective-permute-start | bytes 884744 | tf_op jit(solution)/shard_map/ppermute | solution.py:237
  248.0 21.3 %collective-permute-start.22 = (bf16[4,192,1024]{2,1,0:T(8,128)(2,1)S(1)}, bf16[4,192,1024]{2,1,0:T(8,128)(2,1)S(1)}, u32[]{:S(2)}, u32[]{:S(2)}) collective-permute-start(bf16[4,192,1024]{2,1,0:T(8,128)(2,1)S(1)} %get-tuple-element.139), channel_id=1, source_target_pairs={{0,1},{1,0},{2,3},{3,2},{4,5},{5,4},{6,7},{7,6},{8,9},{9,8},{10,11... | collective-permute-start | bytes 4718600 | tf_op jit(solution)/shard_map/ppermute | solution.py:255
  253.2 20.5 %collective-permute-start.23 = (bf16[4,192,2048]{2,1,0:T(8,128)(2,1)S(1)}, bf16[4,192,2048]{2,1,0:T(8,128)(2,1)S(1)}, u32[]{:S(2)}, u32[]{:S(2)}) collective-permute-start(bf16[4,192,2048]{2,1,0:T(8,128)(2,1)S(1)} %get-tuple-element.148), channel_id=1, source_target_pairs={{0,1},{1,0},{2,3},{3,2},{4,5},{5,4},{6,7},{7,6},{8,9},{9,8},{10,11... | collective-permute-start | bytes 9437192 | tf_op jit(solution)/shard_map/ppermute | solution.py:255
  277.9 25.7 %all-to-all-start.1 = ((bf16[128,4,384]{2,0,1:T(8,128)(2,1)}), bf16[128,4,384]{2,0,1:T(8,128)(2,1)S(1)}, u32[]{:S(2)}, u32[]{:S(2)}) async-start(bf16[128,4,384]{2,0,1:T(8,128)(2,1)} %bitcast.166), calls=%async_computation.1 | async-start | bytes 786432 | tf_op jit(solution)/shard_map/all_to_all | solution.py:653
  281.7 70.9 %all-gather.17.cloned.1.call-start = ((), (), s32[]{:S(2)}) async-start(), calls=%async_computation.8 | async-start | bytes 1966080 | tf_op jit(solution)/shard_map/all_gather | solution.py:656
  281.7 13.0 %collective-permute-start.27 = (bf16[192,1024]{1,0:T(8,128)(2,1)}, bf16[192,1024]{1,0:T(8,128)(2,1)S(1)}, u32[]{:S(2)}, u32[]{:S(2)}) collective-permute-start(bf16[192,1024]{1,0:T(8,128)(2,1)} %copy-done.45), channel_id=1, source_target_pairs={{0,2},{1,3},{2,0},{3,1},{4,6},{5,7},{6,4},{7,5},{8,10},{9,11},{10,... | collective-permute-start | bytes 1179656 | tf_op jit(solution)/shard_map/ppermute | solution.py:255
  284.4 18.5 %collective-permute-start.28 = (bf16[192,1024]{1,0:T(8,128)(2,1)}, bf16[192,1024]{1,0:T(8,128)(2,1)S(1)}, u32[]{:S(2)}, u32[]{:S(2)}) collective-permute-start(bf16[192,1024]{1,0:T(8,128)(2,1)} %copy-done.44), channel_id=1, source_target_pairs={{0,4},{1,5},{2,6},{3,7},{4,0},{5,1},{6,2},{7,3},{8,12},{9,13},{10,... | collective-permute-start | bytes 1179656 | tf_op jit(solution)/shard_map/ppermute | solution.py:255
  285.1 18.5 %collective-permute-start.29 = (bf16[192,1024]{1,0:T(8,128)(2,1)}, bf16[192,1024]{1,0:T(8,128)(2,1)}, u32[]{:S(2)}, u32[]{:S(2)}) collective-permute-start(bf16[192,1024]{1,0:T(8,128)(2,1)} %copy-done.43), channel_id=1, source_target_pairs={{0,6},{1,7},{2,4},{3,5},{4,2},{5,3},{6,0},{7,1},{8,14},{9,15},{10,... | collective-permute-start | bytes 1179656 | tf_op jit(solution)/shard_map/ppermute | solution.py:255
  306.1 156.3 %all-gather.19.cloned.1.call-start = ((), (), s32[]{:S(2)}) async-start(), calls=%async_computation.9 | async-start | bytes 3932160 | tf_op jit(solution)/shard_map/all_gather | solution.py:670
  317.6 33.2 %collective-permute-start.24 = (bf16[192,2048]{1,0:T(8,128)(2,1)}, bf16[192,2048]{1,0:T(8,128)(2,1)S(1)}, u32[]{:S(2)}, u32[]{:S(2)}) collective-permute-start(bf16[192,2048]{1,0:T(8,128)(2,1)} %copy-done.42), channel_id=1, source_target_pairs={{0,2},{1,3},{2,0},{3,1},{4,6},{5,7},{6,4},{7,5},{8,10},{9,11},{10,... | collective-permute-start | bytes 2359304 | tf_op jit(solution)/shard_map/ppermute | solution.py:255
  318.1 33.7 %collective-permute-start.25 = (bf16[192,2048]{1,0:T(8,128)(2,1)}, bf16[192,2048]{1,0:T(8,128)(2,1)S(1)}, u32[]{:S(2)}, u32[]{:S(2)}) collective-permute-start(bf16[192,2048]{1,0:T(8,128)(2,1)} %copy-done.41), channel_id=1, source_target_pairs={{0,4},{1,5},{2,6},{3,7},{4,0},{5,1},{6,2},{7,3},{8,12},{9,13},{10,... | collective-permute-start | bytes 2359304 | tf_op jit(solution)/shard_map/ppermute | solution.py:255
  318.8 33.8 %collective-permute-start.26 = (bf16[192,2048]{1,0:T(8,128)(2,1)S(1)}, bf16[192,2048]{1,0:T(8,128)(2,1)}, u32[]{:S(2)}, u32[]{:S(2)}) collective-permute-start(bf16[192,2048]{1,0:T(8,128)(2,1)S(1)} %copy-done.40), channel_id=1, source_target_pairs={{0,6},{1,7},{2,4},{3,5},{4,2},{5,3},{6,0},{7,1},{8,14},{9,15},{10,... | collective-permute-start | bytes 2359304 | tf_op jit(solution)/shard_map/ppermute | solution.py:255
  367.3 13.1 %collective-permute-start.32 = (bf16[512,256]{1,0:T(8,128)(2,1)}, bf16[512,256]{1,0:T(8,128)(2,1)}, u32[]{:S(2)}, u32[]{:S(2)}) collective-permute-start(bf16[512,256]{1,0:T(8,128)(2,1)} %get-tuple-element.279), channel_id=1, source_target_pairs={{0,4},{1,5},{2,6},{3,7},{4,0},{5,1},{6,2},{7,3},{8,12},{9,13},{10,... | collective-permute-start | bytes 786440 | tf_op jit(solution)/shard_map/ppermute | solution.py:255
  369.0 13.0 %collective-permute-start.33 = (bf16[512,256]{1,0:T(8,128)(2,1)S(1)}, bf16[512,256]{1,0:T(8,128)(2,1)}, u32[]{:S(2)}, u32[]{:S(2)}) collective-permute-start(bf16[512,256]{1,0:T(8,128)(2,1)S(1)} %get-tuple-element.278), channel_id=1, source_target_pairs={{0,6},{1,7},{2,4},{3,5},{4,2},{5,3},{6,0},{7,1},{8,14},{9,15},{10,... | collective-permute-start | bytes 786440 | tf_op jit(solution)/shard_map/ppermute | solution.py:255
  388.2 16.4 %collective-permute-start.39 = (bf16[192,1536]{1,0:T(8,128)(2,1)}, bf16[192,1536]{1,0:T(8,128)(2,1)}, u32[]{:S(2)}, u32[]{:S(2)}) collective-permute-start(bf16[192,1536]{1,0:T(8,128)(2,1)} %get-tuple-element.183), channel_id=1, source_target_pairs={{0,2},{1,3},{2,0},{3,1},{4,6},{5,7},{6,4},{7,5},{8,10},{9,11},{10,... | collective-permute-start | bytes 1769480 | tf_op jit(solution)/shard_map/ppermute | solution.py:255
  388.9 34.9 %collective-permute-start.40 = (bf16[192,1536]{1,0:T(8,128)(2,1)}, bf16[192,1536]{1,0:T(8,128)(2,1)}, u32[]{:S(2)}, u32[]{:S(2)}) collective-permute-start(bf16[192,1536]{1,0:T(8,128)(2,1)} %get-tuple-element.184), channel_id=1, source_target_pairs={{0,4},{1,5},{2,6},{3,7},{4,0},{5,1},{6,2},{7,3},{8,12},{9,13},{10,... | collective-permute-start | bytes 1769480 | tf_op jit(solution)/shard_map/ppermute | solution.py:255
  390.5 33.3 %collective-permute-start.41 = (bf16[192,1536]{1,0:T(8,128)(2,1)}, bf16[192,1536]{1,0:T(8,128)(2,1)}, u32[]{:S(2)}, u32[]{:S(2)}) collective-permute-start(bf16[192,1536]{1,0:T(8,128)(2,1)} %get-tuple-element.185), channel_id=1, source_target_pairs={{0,6},{1,7},{2,4},{3,5},{4,2},{5,3},{6,0},{7,1},{8,14},{9,15},{10,... | collective-permute-start | bytes 1769480 | tf_op jit(solution)/shard_map/ppermute | solution.py:255
  393.2 36.9 %all-to-all-start.3 = ((bf16[4,128,640]{1,2,0:T(8,128)(2,1)}), bf16[4,128,640]{1,2,0:T(8,128)(2,1)}, u32[]{:S(2)}, u32[]{:S(2)}) async-start(bf16[4,128,640]{1,2,0:T(8,128)(2,1)} %pad_maximum_fusion.5), calls=%async_computation.3 | async-start | bytes 1310720 | tf_op jit(solution)/shard_map/all_to_all | solution.py:686
  400.6 25.8 %collective-permute-start.38 = (bf16[192,768]{1,0:T(8,128)(2,1)S(1)}, bf16[192,768]{1,0:T(8,128)(2,1)S(1)}, u32[]{:S(2)}, u32[]{:S(2)}) collective-permute-start(bf16[192,768]{1,0:T(8,128)(2,1)S(1)} %get-tuple-element.195), channel_id=1, source_target_pairs={{0,6},{1,7},{2,4},{3,5},{4,2},{5,3},{6,0},{7,1},{8,14},{9,15},{10,... | collective-permute-start | bytes 884744 | tf_op jit(solution)/shard_map/ppermute | solution.py:255
  402.4 27.5 %collective-permute-start.37 = (bf16[192,768]{1,0:T(8,128)(2,1)S(1)}, bf16[192,768]{1,0:T(8,128)(2,1)S(1)}, u32[]{:S(2)}, u32[]{:S(2)}) collective-permute-start(bf16[192,768]{1,0:T(8,128)(2,1)S(1)} %get-tuple-element.194), channel_id=1, source_target_pairs={{0,4},{1,5},{2,6},{3,7},{4,0},{5,1},{6,2},{7,3},{8,12},{9,13},{10,... | collective-permute-start | bytes 884744 | tf_op jit(solution)/shard_map/ppermute | solution.py:255
  404.6 25.2 %collective-permute-start.36 = (bf16[192,768]{1,0:T(8,128)(2,1)S(1)}, bf16[192,768]{1,0:T(8,128)(2,1)S(1)}, u32[]{:S(2)}, u32[]{:S(2)}) collective-permute-start(bf16[192,768]{1,0:T(8,128)(2,1)S(1)} %get-tuple-element.193), channel_id=1, source_target_pairs={{0,2},{1,3},{2,0},{3,1},{4,6},{5,7},{6,4},{7,5},{8,10},{9,11},{10,... | collective-permute-start | bytes 884744 | tf_op jit(solution)/shard_map/ppermute | solution.py:255
  430.0 26.1 %all-to-all-start.2 = ((bf16[192,4,384]{2,0,1:T(8,128)(2,1)}), bf16[192,4,384]{2,0,1:T(8,128)(2,1)S(1)}, u32[]{:S(2)}, u32[]{:S(2)}) async-start(bf16[192,4,384]{2,0,1:T(8,128)(2,1)} %bitcast.150), calls=%async_computation.2 | async-start | bytes 1179648 | tf_op jit(solution)/shard_map/all_to_all | solution.py:709
  456.3 15.6 %collective-permute-start.42 = (bf16[192,1152]{1,0:T(8,128)(2,1)S(1)}, bf16[192,1152]{1,0:T(8,128)(2,1)S(1)}, u32[]{:S(2)}, u32[]{:S(2)}) collective-permute-start(bf16[192,1152]{1,0:T(8,128)(2,1)S(1)} %pad_maximum_fusion.6.refs_0_), channel_id=1, source_target_pairs={{0,8},{8,16},{16,24},{24,0},{1,9},{9,17},{17,25},{25,1},{2,10},{10... | collective-permute-start | bytes 1327112 | tf_op jit(solution)/shard_map/ppermute | solution.py:237
  458.3 38.0 %collective-permute-start.43 = (bf16[192,1152]{1,0:T(8,128)(2,1)S(1)}, bf16[192,1152]{1,0:T(8,128)(2,1)S(1)}, u32[]{:S(2)}, u32[]{:S(2)}) collective-permute-start(bf16[192,1152]{1,0:T(8,128)(2,1)S(1)} %pad_maximum_fusion.6.refs_0_), channel_id=1, source_target_pairs={{0,16},{8,24},{16,0},{24,8},{1,17},{9,25},{17,1},{25,9},{2,18},{10... | collective-permute-start | bytes 1327112 | tf_op jit(solution)/shard_map/ppermute | solution.py:237
  462.5 37.6 %collective-permute-start.44 = (bf16[192,1152]{1,0:T(8,128)(2,1)S(1)}, bf16[192,1152]{1,0:T(8,128)(2,1)S(1)}, u32[]{:S(2)}, u32[]{:S(2)}) collective-permute-start(bf16[192,1152]{1,0:T(8,128)(2,1)S(1)} %pad_maximum_fusion.6.refs_0_), channel_id=1, source_target_pairs={{0,24},{8,0},{16,8},{24,16},{1,25},{9,1},{17,9},{25,17},{2,26},{10... | collective-permute-start | bytes 1327112 | tf_op jit(solution)/shard_map/ppermute | solution.py:237
  (100 other events, 891.5 us)
Sparse Core Ops, SparseCore 0:
  10.8 28.3 all-gather.8
  41.2 47.8 all-gather.10
  91.5 58.2 all-gather.12
  152.1 52.2 all-gather.14
  306.2 35.1 all-gather.16
  370.5 84.5 all-gather.18

commit v9 on v8

--- a/solution.py
+++ b/solution.py
@@ -46,7 +46,7 @@
 
 def forward_kernel(shards, seqs, rows, local_kv, groups, *refs):
     kv_refs = refs[:shards]
-    q_ref, bias_ref, low_ref, exact_ref, lse_ref, acc_ref, max_ref = refs[shards:]
+    q_ref, bias_ref, low_ref, exact_ref, lse_ref, all_ref, acc_ref, max_ref = refs[shards:]
     zq = pl.program_id(0)
     stack = groups * rows
     zeros = jnp.zeros((rows, HD), BF)
@@ -81,6 +81,11 @@
             acc_ref[g] = acc_ref[g] * jnp.exp(max_ref[g][:, :1] - new_max) + part
         max_ref[g] = jnp.broadcast_to(new_max, (stack, 2 * HD))
 
+    @pl.when(zq == 0)
+    def _():
+        for p in range(shards):
+            all_ref[p] = kv_refs[p][...]
+
     for g in range(local_kv):
         chunk(g, zq, None)
 
@@ -110,13 +115,19 @@
     kv_spec = pl.BlockSpec(kv_blocks[0].shape, lambda i: (0, 0))
     q_spec = pl.BlockSpec((rows, q_cols), lambda i: (i, 0))
     stack = groups * rows
+    all_shape = (shards,) + kv_blocks[0].shape
     out = jax.ShapeDtypeStruct((seqs * rows, q_cols), F32)
     return pl.pallas_call(
         functools.partial(forward_kernel, shards, seqs, rows, local_kv, groups),
         grid=(seqs,),
         in_specs=[kv_spec] * shards + [q_spec, pl.BlockSpec(bias.shape, lambda i: (0, 0, 0))],
-        out_specs=[q_spec] * 3,
-        out_shape=[jax.ShapeDtypeStruct((seqs * rows, q_cols), BF), out, out],
+        out_specs=[q_spec] * 3 + [pl.BlockSpec(all_shape, lambda i: (0, 0, 0))],
+        out_shape=[
+            jax.ShapeDtypeStruct((seqs * rows, q_cols), BF),
+            out,
+            out,
+            jax.ShapeDtypeStruct(all_shape, BF),
+        ],
         scratch_shapes=[
             pltpu.VMEM((local_kv, stack, 2 * HD), F32),
             pltpu.VMEM((local_kv, stack, 2 * HD), F32),
@@ -343,6 +354,138 @@
         compiler_params=pltpu.CompilerParams(vmem_limit_bytes=24 * 1024 * 1024),
         cost_estimate=pl.CostEstimate(flops=0, bytes_accessed=0, transcendentals=0),
     )((shard // 2).astype(jnp.int32).reshape(1), near, there)
+
+
+def experts_forward_kernel(count, tile, *refs):
+    rows_in = refs[:count]
+    gate_w, up_w, down_w, rows_ref, gate_up_ref, hidden_ref = refs[count : count + 6]
+    out_refs, total = refs[count + 6 : -1], refs[-1]
+    step = pl.program_id(0)
+    piece = hidden_ref.shape[1]
+    cap = rows_in[0].shape[0]
+
+    @pl.when(step == 0)
+    def _():
+        for s in range(count):
+            rows_ref[s * cap : (s + 1) * cap, :] = rows_in[s][...]
+
+    rows = rows_ref[...]
+    gate = dot(rows, gate_w[...])
+    up = dot(rows, up_w[...])
+    gate_up_ref[:, pl.ds(pl.multiple_of(step * tile, tile), tile)] = gate
+    gate_up_ref[:, pl.ds(pl.multiple_of(piece + step * tile, tile), tile)] = up
+    hidden = (gate / (1.0 + jnp.exp(-gate)) * up).astype(BF)
+    hidden_ref[:, pl.ds(pl.multiple_of(step * tile, tile), tile)] = hidden
+    part = dot_nt(hidden, down_w[...])
+
+    @pl.when(step == 0)
+    def _():
+        total[...] = part
+
+    @pl.when(step > 0)
+    def _():
+        total[...] += part
+
+    @pl.when(step == pl.num_programs(0) - 1)
+    def _():
+        for s in range(count):
+            out_refs[s][...] = total[s * cap : (s + 1) * cap, :].astype(BF)
+
+
+def weight_specs(width, piece, tile):
+    steps = piece // tile
+    return [
+        pl.BlockSpec((width, tile), lambda i, part=part: (0, part * steps + i)) for part in range(3)
+    ]
+
+
+def experts_forward(blocks, weights, piece):
+    count = len(blocks)
+    cap, width = blocks[0].shape
+    rows = count * cap
+    tile = math.gcd(piece, 1024)
+    whole = lambda shape: pl.BlockSpec(shape, lambda i: (0,) * len(shape))
+    block = jax.ShapeDtypeStruct((cap, width), BF)
+    return pl.pallas_call(
+        functools.partial(experts_forward_kernel, count, tile),
+        grid=(piece // tile,),
+        in_specs=[whole((cap, width))] * count + weight_specs(width, piece, tile),
+        out_specs=[whole((rows, width)), whole((rows, 2 * piece)), whole((rows, piece))]
+        + [whole((cap, width))] * count,
+        out_shape=[
+            jax.ShapeDtypeStruct((rows, width), BF),
+            jax.ShapeDtypeStruct((rows, 2 * piece), F32),
+            jax.ShapeDtypeStruct((rows, piece), BF),
+        ]
+        + [block] * count,
+        scratch_shapes=[pltpu.VMEM((rows, width), F32)],
+        compiler_params=pltpu.CompilerParams(vmem_limit_bytes=32 * 1024 * 1024),
+        cost_estimate=pl.CostEstimate(flops=0, bytes_accessed=0, transcendentals=0),
+    )(*blocks, weights, weights, weights)
+
+
+def experts_backward_kernel(count, tile, *refs):
+    grads_in = refs[:count]
+    gate_up_ref, gate_w, up_w, down_w, grads_ref, rows_ref = refs[count : count + 6]
+    out_refs, total = refs[count + 6 : -1], refs[-1]
+    step = pl.program_id(0)
+    piece = rows_ref.shape[1] // 2
+    cap = grads_in[0].shape[0]
+    gate_at = pl.ds(pl.multiple_of(step * tile, tile), tile)
+    up_at = pl.ds(pl.multiple_of(piece + step * tile, tile), tile)
+
+    @pl.when(step == 0)
+    def _():
+        for s in range(count):
+            grads_ref[s * cap : (s + 1) * cap, :] = grads_in[s][...]
+
+    grad_hidden = dot(grads_ref[...], down_w[...])
+    gate = gate_up_ref[:, gate_at]
+    up = gate_up_ref[:, up_at]
+    slope = 1.0 / (1.0 + jnp.exp(-gate))
+    grad_gate = (grad_hidden * up * slope * (1.0 + gate * (1.0 - slope))).astype(BF)
+    grad_up = (grad_hidden * gate * slope).astype(BF)
+    rows_ref[:, gate_at] = grad_gate
+    rows_ref[:, up_at] = grad_up
+    part = dot_nt(grad_gate, gate_w[...]) + dot_nt(grad_up, up_w[...])
+
+    @pl.when(step == 0)
+    def _():
+        total[...] = part
+
+    @pl.when(step > 0)
+    def _():
+        total[...] += part
+
+    @pl.when(step == pl.num_programs(0) - 1)
+    def _():
+        for s in range(count):
+            out_refs[s][...] = total[s * cap : (s + 1) * cap, :].astype(BF)
+
+
+def experts_backward(blocks, gate_up, weights, piece):
+    count = len(blocks)
+    cap, width = blocks[0].shape
+    rows = count * cap
+    tile = math.gcd(piece, 1024)
+    whole = lambda shape: pl.BlockSpec(shape, lambda i: (0,) * len(shape))
+    block = jax.ShapeDtypeStruct((cap, width), BF)
+    return pl.pallas_call(
+        functools.partial(experts_backward_kernel, count, tile),
+        grid=(piece // tile,),
+        in_specs=[whole((cap, width))] * count
+        + [whole((rows, 2 * piece))]
+        + weight_specs(width, piece, tile),
+        out_specs=[whole((rows, width)), whole((rows, 2 * piece))] + [whole((cap, width))] * count,
+        out_shape=[
+            jax.ShapeDtypeStruct((rows, width), BF),
+            jax.ShapeDtypeStruct((rows, 2 * piece), BF),
+        ]
+        + [block] * count,
+        scratch_shapes=[pltpu.VMEM((rows, width), F32)],
+        compiler_params=pltpu.CompilerParams(vmem_limit_bytes=36 * 1024 * 1024),
+        cost_estimate=pl.CostEstimate(flops=0, bytes_accessed=0, transcendentals=0),
+    )(*blocks, gate_up, weights, weights, weights)
 
 
 def two_parts(value):
@@ -501,10 +644,9 @@
     token_blocks = after(send_out([token_rows] * seqs, seqs), token_mark)
 
     valid_local = from_relative([each[rows : rows + 1, :rows] for each in token_blocks], z)
-    token_blocks = [each[:rows] for each in token_blocks]
     projected = []
     for block in token_blocks:
-        projected.append(dot(block, heads_full) * root(block.astype(F32)))
+        projected.append(dot(block[:rows], heads_full) * root(block[:rows].astype(F32)))
     projected = from_relative([each.astype(BF) for each in projected], z)
     projected = projected.reshape(local_rows, q_cols + kv_cols)
     head_queries = projected[:, :q_cols] * jnp.asarray(scale, BF)
@@ -538,8 +680,6 @@
         axis=1,
     )
     expert_full = lax.all_gather(expert_shard, "fsdp", axis=0, tiled=True)
-    gate_up_full = expert_full[:, : 2 * piece]
-    down_full = expert_full[:, 2 * piece : 3 * piece]
     router_full = expert_full[:, 3 * piece :]
     attn_shard = jnp.concatenate(
         [
@@ -570,7 +710,7 @@
     earlier = ((order ^ shard) < shard) | (order == 0)
     bias_same = jnp.where(earlier[None, :, None], bias, FLOOR_SCORE)
     bias = jnp.concatenate([bias, bias_same]).reshape(2 * seqs, 1, shards * rows)
-    attended_low, exact, lse = flash_forward(
+    attended_low, exact, lse, kv_all = flash_forward(
         head_queries, kv_blocks, bias, seqs, rows, local_kv, groups
     )
     attended = lax.all_to_all(attended_low, "seq", split_axis=0, concat_axis=1, tiled=True)
@@ -593,15 +733,10 @@
     placed_pairs = jnp.concatenate([placed[:, 0], placed[:, 1]], axis=0)
     sent_rows = dot_tn(dispatch, normed_two).astype(BF)
     sent_rows = sent_rows.reshape(seqs, CAP, width)
-    expert_rows = jnp.concatenate(send_out([sent_rows[s] for s in range(seqs)], seqs))
-    gate_up = dot(expert_rows, gate_up_full)
-    gate_part = gate_up[:, :piece]
-    up_part = gate_up[:, piece:]
-    sigmoid_gate = jax.nn.sigmoid(gate_part)
-    hidden = (gate_part * sigmoid_gate * up_part).astype(BF)
-    expert_out = dot_nt(hidden, down_full).astype(BF)
-    expert_out = expert_out.reshape(seqs, CAP, width)
-    returned = jnp.concatenate(send_back([expert_out[s] for s in range(seqs)], seqs))
+    expert_rows, gate_up, hidden, *expert_out = experts_forward(
+        send_out([sent_rows[s] for s in range(seqs)], seqs), expert_full, piece
+    )
+    returned = jnp.concatenate(send_back(expert_out, seqs))
     selected = dot(placed_pairs, returned).reshape(2, rows, width)
     mixed_exact = residual + gating[:, :1] * selected[0] + gating[:, 1:] * selected[1]
     valid_rows = valid.astype(F32)
@@ -621,38 +756,33 @@
         [(gating[:, :1] * grad_mixed).astype(BF), (gating[:, 1:] * grad_mixed).astype(BF)], axis=0
     )
     sent_grads = dot_tn(placed_pairs, weighted).astype(BF).reshape(seqs, CAP, width)
-    grad_expert_out = jnp.concatenate(send_out([sent_grads[s] for s in range(seqs)], seqs))
-    grad_expert_out = after(grad_expert_out, attn_full)
-    grad_hidden = dot(grad_expert_out, down_full)
-    grad_gate = grad_hidden * up_part * sigmoid_gate * (1.0 + gate_part * (1.0 - sigmoid_gate))
-    grad_up = grad_hidden * gate_part * sigmoid_gate
-    grad_gate_up_rows = jnp.concatenate([grad_gate, grad_up], axis=-1).astype(BF)
-    grad_rows = dot_nt(grad_gate_up_rows, gate_up_full).astype(BF)
-    returned_mark = grad_rows
-    grad_rows = grad_rows.reshape(seqs, CAP, width)
-    grad_returned = send_back([grad_rows[s] for s in range(seqs)], seqs)
-    grad_returned = jnp.concatenate(grad_returned)
-    held_out, held_hidden = after((grad_expert_out, hidden), returned_mark)
-    down_far, down_near = split_product(held_out, held_hidden, shard, shards)
-    held_rows, held_gate_up = after((expert_rows, grad_gate_up_rows), returned_mark)
-    gate_up_far, gate_up_near = split_product(held_rows, held_gate_up, shard, shards)
-    grad_down_sums = pair_sums(down_near, down_far, shard, shards)
-    kv_all = jnp.stack(after(kv_blocks, returned_mark))
-    tokens_local = from_relative(after(token_blocks, returned_mark), z).reshape(local_rows, width)
+    grad_out_rows = send_out([sent_grads[s] for s in range(seqs)], seqs)
+    grad_out_rows = after(grad_out_rows, attn_full, grad_logits)
+    grad_expert_out, grad_gate_up_rows, *grad_rows = experts_backward(
+        grad_out_rows, gate_up, expert_full, piece
+    )
+    grad_returned = send_back(grad_rows, seqs)
+    tokens_local = from_relative(
+        [each[:rows] for each in after(token_blocks, grad_rows)], z
+    ).reshape(local_rows, width)
     factor_local = root(tokens_local.astype(F32))
     ride_rows = jnp.concatenate([normed_two, jnp.ones((16, width), BF)], axis=0)
     product_rows = jnp.concatenate([tokens_local, ride_rows], axis=0)
-
+    held_out, held_hidden = after((grad_expert_out, hidden), grad_rows)
+    down_far, down_near = split_product(held_out, held_hidden, shard, shards)
+    grad_down_sums = pair_sums(down_near, down_far, shard, shards)
+    held_rows, held_gate_up = after((expert_rows, grad_gate_up_rows), grad_rows)
+    gate_up_far, gate_up_near = split_product(held_rows, held_gate_up, shard, shards)
     grad_gate_up_sums = pair_sums(gate_up_near, gate_up_far, shard, shards)
     grad_down_blocks = send_chips(grad_down_sums, shards)
-    grad_returned = after(grad_returned, grad_down_sums, product_rows)
+    grad_returned = jnp.concatenate(after(grad_returned, grad_down_sums, product_rows))
     grad_normed_two = dot(dispatch, grad_returned) + dot_nt(grad_logits, router_full)
     grad_residual = grad_mixed + root_back(residual, factor_two, grad_normed_two)
     grad_branch = grad_residual.astype(BF)
     grad_attended = dot_nt(after(grad_branch, grad_gate_up_sums), out_full).astype(BF)
     head_grad = lax.all_to_all(grad_attended, "seq", split_axis=1, concat_axis=0, tiled=True)
     grad_gate_up_blocks = send_chips(grad_gate_up_sums, shards)
-    grad_down_shard = total_of(after(grad_down_blocks, head_grad)).astype(BF)
+    grad_down_shard = total_of(after(grad_down_blocks, grad_attended)).astype(BF)
     grad_down = lax.all_gather(grad_down_shard, "seq", axis=0, tiled=False)
 
     grad_q, near, far = [], [], []
@@ -705,7 +835,7 @@
     )
     head_far, head_near = split_product(product_rows, product_columns, shard, shards)
     head_sums = pair_sums(head_near, head_far, shard, shards)
-    out_part = total_of(after(out_blocks, head_sums)).astype(BF)
+    out_part = total_of(after(out_blocks, head_sums, grad_gate_up_all)).astype(BF)
     out_parts = lax.all_to_all(
         out_part.reshape(part, seqs, q_cols), "seq", split_axis=1, concat_axis=1, tiled=True
     )

time: 520 us -> 526 us (1.012)
  blocking collectives: 0 us -> 31.2 us
  waiting for transfers between devices: 220 us -> 194 us
  matrix products: 41.5 us -> 19.4 us
  local copies, waits for them, and re-layouts: 35.7 us -> 57.8 us
  Pallas kernels: 70.9 us -> 81.6 us
  starting transfers between devices: 83.1 us -> 72.5 us
    all_to_all x0 -> x1, blocking collectives: none -> 31.2 us  [local(): lax.all_to_all(grad_attended, 'seq', split_axis=1, concat_axis=0, tiled=T...]
    ppermute x27, waiting for transfers between devices: 65.7 us -> 34.8 us  [hop(): return lax.ppermute(block, 'fsdp', [(i, i ^ mask) for i in range(count)])]
    unnamed x219 -> x206, local copies, waits for them, and re-layouts: 17.8 us -> 39.8 us
    all_gather x1, waiting for transfers between devices: 0.01 us -> 12 us  [local(): lax.all_gather(grad_gate_up_shard, 'seq', axis=0, tiled=False)]
    dot_general x10 -> x8, matrix products: 22.3 us -> 10.4 us  [dot(): return jnp.dot(a, b, preferred_element_type=F32)]
    pallas_call x0 -> x2, Pallas kernels: none -> 11.1 us  [the longest x1 5.94 us: experts_forward(): pl.pallas_call(functools.partial(experts_forward_kernel, count, tile), gr...]
    dot_general x5 -> x3, matrix products: 18.3 us -> 8.17 us  [dot_nt(): lax.dot_general(a, b, (((1,), (1,)), ((), ())), preferred_element_type=F32)]
    all_gather x1, starting transfers between devices: 8.29 us -> 0.04 us  [local(): lax.all_gather(grad_gate_up_shard, 'seq', axis=0, tiled=False)]
  transfers between devices with their start and end apart: 55 -> 54, of which waited for: 29 -> 25; matrix products, arithmetic and copies ran while one was open for 16% -> 13% of each run, Pallas kernels for 13% -> 14%
where the time goes in v9:
time: 526 us; the launch traced here: 520 us
  waiting for transfers between devices  194 us (37%)
  Pallas kernels  81.6 us (16%)
  starting transfers between devices  72.5 us (14%)
  local copies, waits for them, and re-layouts  57.8 us (11%)
  other arithmetic  42.7 us (8%)
  blocking collectives  31.2 us (6%)
  between operations  20.7 us (4%)
  matrix products  19.4 us (4%)
    ppermute x18, waiting for transfers between devices, shift(): lax.ppermute(block, 'seq', [(i, (i + step) % count) for i in range(count)])  136 us
    unnamed x206, local copies, waits for them, and re-layouts  39.8 us
    ppermute x27, waiting for transfers between devices, hop(): return lax.ppermute(block, 'fsdp', [(i, i ^ mask) for i in range(count)])  34.8 us
    all_to_all x1, blocking collectives, local(): lax.all_to_all(grad_attended, 'seq', split_axis=1, concat_axis=0, tiled=T...  31.2 us
    ppermute x18, starting transfers between devices, shift(): lax.ppermute(block, 'seq', [(i, (i + step) % count) for i in range(count)])  26.4 us
    pallas_call x2, Pallas kernels, flash_backward(): pl.pallas_call(functools.partial(backward_kernel, shards, seqs, rows, g,...  25.5 us
    ppermute x27, starting transfers between devices, hop(): return lax.ppermute(block, 'fsdp', [(i, i ^ mask) for i in range(count)])  25.3 us
    pallas_call x1, Pallas kernels, flash_forward(): pl.pallas_call(functools.partial(forward_kernel, shards, seqs, rows, loca...  19.1 us
  transfers between devices with their start and end apart: 54, of which 25 were waited for; matrix products, arithmetic and copies ran while one was open for 13% of the time, Pallas kernels for 14%

profile of v9, /device:TPU:12, one launch (start us, length us, event | category | flops | bytes accessed | tf_op | source)
XLA Modules:
  0.0 520.3 jit_solution(3087810823471624196)
XLA Ops:
  21.6 24.8 %collective-permute-done = bf16[136,1536]{1,0:T(8,128)(2,1)S(1)} collective-permute-done((bf16[136,1536]{1,0:T(8,128)(2,1)S(1)}, bf16[136,1536]{1,0:T(8,128)(2,1)S(1)}, u32[]{:S(2)}, u32[]{:S(2)}) %collective-permute-start) | collective-permute-done | bytes 417824 | tf_op jit(solution)/shard_map/ppermute | solution.py:248
  46.4 7.8 %collective-permute-done.1 = bf16[136,1536]{1,0:T(8,128)(2,1)S(1)} collective-permute-done((bf16[136,1536]{1,0:T(8,128)(2,1)S(1)}, bf16[136,1536]{1,0:T(8,128)(2,1)S(1)}, u32[]{:S(2)}, u32[]{:S(2)}) %collective-permute-start.1) | collective-permute-done | bytes 417824 | tf_op jit(solution)/shard_map/ppermute | solution.py:248
  64.5 10.1 %collective-permute-done.3.refs_1_ = bf16[528,256]{1,0:T(8,128)(2,1)S(1)} collective-permute-done((bf16[528,256]{1,0:T(8,128)(2,1)S(1)}, bf16[528,256]{1,0:T(8,128)(2,1)S(1)}, u32[]{:S(2)}, u32[]{:S(2)}) %collective-permute-start.3) | collective-permute-done | bytes 270368 | tf_op jit(solution)/shard_map/ppermute | solution.py:266
  74.7 6.2 %collective-permute-done.4.refs_2_ = bf16[528,256]{1,0:T(8,128)(2,1)S(1)} collective-permute-done((bf16[528,256]{1,0:T(8,128)(2,1)S(1)}, bf16[528,256]{1,0:T(8,128)(2,1)S(1)}, u32[]{:S(2)}, u32[]{:S(2)}) %collective-permute-start.4) | collective-permute-done | bytes 270368 | tf_op jit(solution)/shard_map/ppermute | solution.py:266
  80.9 4.5 collective-permute-done.5.refs_3_
  95.0 19.1 %shard_map.221 = (bf16[512,384]{1,0:T(8,128)(2,1)}, f32[512,384]{1,0:T(8,128)S(1)}, f32[512,384]{1,0:T(8,128)S(1)}, bf16[8,528,256]{2,1,0:T(8,128)(2,1)S(1)}) custom-call(bf16[528,256]{1,0:T(8,128)(2,1)S(1)} %maximum_maximum_fusion.1.refs_0_, bf16[528,256]{1,0:T(8,128)(2,1)S(1)} %collective-permute-done.3.refs_1_, bf16[528,256]{1,0:T(8,128)(2,1)S(1)} %copy-done.34, ...), custom_call_target="tpu_custom_call" | custom-call | tf_op jit(solution)/shard_map/pallas_call | solution.py:120
  115.9 3.6 all-to-all-start
  120.4 8.8 %all-to-all-done = bf16[4,128,384]{2,1,0:T(8,128)(2,1)S(1)} async-done(((bf16[4,128,384]{2,1,0:T(8,128)(2,1)}), bf16[4,128,384]{2,1,0:T(8,128)(2,1)S(1)}, u32[]{:S(2)}, u32[]{:S(2)}) %all-to-all-start) | async-done | bytes 393248 | tf_op jit(solution)/shard_map/all_to_all | solution.py:716
  131.1 4.1 multiply_reduce_fusion.5
  138.3 4.1 collective-permute-start.11
  145.5 2.8 collective-permute-done.10.refs_1_
  148.3 15.3 %collective-permute-done.11.refs_2_ = bf16[96,1536]{1,0:T(8,128)(2,1)} collective-permute-done((bf16[96,1536]{1,0:T(8,128)(2,1)}, bf16[96,1536]{1,0:T(8,128)(2,1)}, u32[]{:S(2)}, u32[]{:S(2)}) %collective-permute-start.11) | collective-permute-done | bytes 294944 | tf_op jit(solution)/shard_map/ppermute | solution.py:248
  163.5 4.0 collective-permute-done.12.refs_3_
  167.5 3.8 copy-done.2
  171.3 5.9 %shard_map.222 = (bf16[384,1536]{1,0:T(8,128)(2,1)S(1)}, f32[384,2048]{1,0:T(8,128)S(1)}, bf16[384,1024]{1,0:T(8,128)(2,1)S(1)}, bf16[96,1536]{1,0:T(8,128)(2,1)...) custom-call(bf16[96,1536]{1,0:T(8,128)(2,1)S(1)} %get-tuple-element.311.refs_0_, ...), custom_call_target="tpu_custom_call" | custom-call | tf_op jit(solution)/shard_map/pallas_call | solution.py:409
  183.1 7.8 %collective-permute-done.15 = bf16[96,1536]{1,0:T(8,128)(2,1)S(1)} collective-permute-done((bf16[96,1536]{1,0:T(8,128)(2,1)}, bf16[96,1536]{1,0:T(8,128)(2,1)S(1)}, u32[]{:S(2)}, u32[]{:S(2)}) %collective-permute-start.15) | collective-permute-done | bytes 294944 | tf_op jit(solution)/shard_map/ppermute | solution.py:248
  190.8 15.3 %collective-permute-done.14 = bf16[96,1536]{1,0:T(8,128)(2,1)} collective-permute-done((bf16[96,1536]{1,0:T(8,128)(2,1)}, bf16[96,1536]{1,0:T(8,128)(2,1)}, u32[]{:S(2)}, u32[]{:S(2)}) %collective-permute-start.14) | collective-permute-done | bytes 294944 | tf_op jit(solution)/shard_map/ppermute | solution.py:248
  211.6 3.4 collective-permute-start.17
  217.2 4.6 collective-permute-done.16.refs_1_
  221.8 15.0 %collective-permute-done.17.refs_2_ = bf16[96,1536]{1,0:T(8,128)(2,1)} collective-permute-done((bf16[96,1536]{1,0:T(8,128)(2,1)}, bf16[96,1536]{1,0:T(8,128)(2,1)}, u32[]{:S(2)}, u32[]{:S(2)}) %collective-permute-start.17) | collective-permute-done | bytes 294944 | tf_op jit(solution)/shard_map/ppermute | solution.py:248
  236.9 3.4 collective-permute-done.18.refs_3_
  240.3 3.8 copy-done.3
  246.0 5.2 shard_map.223
  254.2 2.9 shard_map.224
  258.4 4.8 shard_map.226
  266.8 2.4 collective-permute-start.27
  269.2 4.6 collective-permute-done.19
  275.3 2.5 collective-permute-start.29
  285.5 4.5 collective-permute-done.28
  291.1 2.6 collective-permute-start.24
  296.2 31.2 %all_to_all.59 = bf16[128,4,384]{2,0,1:T(8,128)(2,1)S(1)} all-to-all(bf16[128,4,384]{2,0,1:T(8,128)(2,1)S(1)} %bitcast.145), channel_id=1, replica_groups=mesh['seq'=4,'fsdp'=8] {'seq'}, dimensions={1} | all-to-all | bytes 786432 | tf_op jit(solution)/shard_map/all_to_all | solution.py:783
  327.5 12.7 %shard_map.228 = (f32[512,192]{1,0:T(8,128)S(1)}, bf16[4,512,128]{2,1,0:T(8,128)(2,1)S(1)}, bf16[4,512,128]{2,1,0:T(8,128)(2,1)S(1)}) custom-call(bf16[8,528,256]{2,1,0:T(8,128)(2,1)S(1)} %get-tuple-element.152.refs_0_, bf16[512,384]{1,0:T(8,128)(2,1)S(1)} %slice_multiply_fusion.refs_8_.refs_1_, f32[8,1,1024]{2,1,0:T(1,128)S(1)} %pad_maximum_fusion.6.refs_9_.refs_2_, ...), custom_call_target="tpu_custom_call" | custom-call | tf_op jit(solution)/shard_map/pallas_call | solution.py:223
  341.8 12.8 %shard_map.229 = (f32[512,192]{1,0:T(8,128)S(1)}, bf16[4,512,128]{2,1,0:T(8,128)(2,1)S(1)}, bf16[4,512,128]{2,1,0:T(8,128)(2,1)S(1)}) custom-call(bf16[8,528,256]{2,1,0:T(8,128)(2,1)S(1)} %get-tuple-element.152.refs_0_, bf16[512,384]{1,0:T(8,128)(2,1)S(1)} %slice_multiply_fusion.refs_8_.refs_1_, f32[8,1,1024]{2,1,0:T(1,128)S(1)} %pad_maximum_fusion.6.refs_9_.refs_2_, ...), custom_call_target="tpu_custom_call" | custom-call | tf_op jit(solution)/shard_map/pallas_call | solution.py:223
  358.8 3.5 add_convert_fusion
  363.5 3.5 shard_map.230
  369.3 2.4 fusion.51
  377.3 4.0 shard_map.231
  383.1 6.0 %collective-permute-done.32 = bf16[512,256]{1,0:T(8,128)(2,1)S(1)} collective-permute-done((bf16[512,256]{1,0:T(8,128)(2,1)}, bf16[512,256]{1,0:T(8,128)(2,1)S(1)}, u32[]{:S(2)}, u32[]{:S(2)}) %collective-permute-start.32) | collective-permute-done | bytes 262176 | tf_op jit(solution)/shard_map/ppermute | solution.py:266
  391.5 4.4 shard_map.232
  408.2 7.8 %all-to-all-start.3 = ((bf16[4,128,640]{1,2,0:T(8,128)(2,1)}), bf16[4,128,640]{1,2,0:T(8,128)(2,1)}, u32[]{:S(2)}, u32[]{:S(2)}) async-start(bf16[4,128,640]{1,2,0:T(8,128)(2,1)} %pad_maximum_fusion.1), calls=%async_computation.3 | async-start | bytes 1310720 | tf_op jit(solution)/shard_map/all_to_all | solution.py:816
  425.4 12.0 %all-gather.19.cloned.1.call-done = bf16[768,2048]{1,0:T(8,128)(2,1)} async-done(((bf16[192,2048]{1,0:T(8,128)(2,1)}), bf16[768,2048]{1,0:T(8,128)(2,1)}) %all-gather.19.cloned.1.call-update) | async-done | bytes 3145744 | tf_op jit(solution)/shard_map/all_gather | solution.py:800
  440.2 9.2 %all-to-all-start.2 = ((bf16[192,4,384]{2,0,1:T(8,128)(2,1)}), bf16[192,4,384]{2,0,1:T(8,128)(2,1)}, u32[]{:S(2)}, u32[]{:S(2)}) async-start(bf16[192,4,384]{2,0,1:T(8,128)(2,1)} %bitcast.131), calls=%async_computation.2 | async-start | bytes 1179648 | tf_op jit(solution)/shard_map/all_to_all | solution.py:839
  449.5 6.3 %fusion.32 = (f32[128]{0:T(128)S(1)}, f32[128]{0:T(128)S(1)}, f32[128,1536]{1,0:T(8,128)S(1)}) fusion(bf16[128,1536]{1,0:T(8,128)(2,1)S(1)} %copy-done.59, bf16[128,2560]{0,1:T(8,128)(2,1)} %bitcast.53, bf16[1536,2560]{1,0:T(8,128)(2,1)} %all-gather.15.cloned.1.call-done), kind=kOutput, calls=%fused_computation.58 | convolution fusion | flops 1007615744 | bytes 9700352 | tf_op jit(solution)/shard_map/dot_general | solution.py:28
  459.6 2.2 all-to-all-done.2
  465.5 4.3 collective-permute-start.43
  469.8 6.3 %fusion = (f32[192]{0:T(256)S(1)}, f32[4,192,2048]{2,1,0:T(8,128)}) fusion(bf16[4,192,2048]{2,1,0:T(8,128)(2,1)} %bitcast.140, bf16[4,192,2048]{2,1,0:T(8,128)(2,1)S(1)} %copy-done.69, f32[192]{0:T(256)S(1)} %convert_element_type.316), kind=kLoop, calls=%fused_computation.2 | loop fusion | flops 7864128 | bytes 12584448 | tf_op jit(solution)/shard_map/reduce_sum | solution.py:536
  478.5 24.1 %collective-permute-done.43.refs_2_ = bf16[192,1152]{1,0:T(8,128)(2,1)S(1)} collective-permute-done((bf16[192,1152]{1,0:T(8,128)(2,1)S(1)}, bf16[192,1152]{1,0:T(8,128)(2,1)S(1)}, u32[]{:S(2)}, u32[]{:S(2)}) %collective-permute-start.43) | collective-permute-done | bytes 442400 | tf_op jit(solution)/shard_map/ppermute | solution.py:248
  502.6 4.0 collective-permute-done.44.refs_3_
  (418 shorter events, 135.1 us)
Async XLA Ops:
  7.2 49.5 %all-gather.9.cloned.1.call-start = ((), (), s32[]{:S(2)}) async-start(), calls=%async_computation.4 | async-start | bytes 2211840 | tf_op jit(solution)/shard_map/all_gather | solution.py:640
  10.7 120.3 %all-gather.11.cloned.1.call-start = ((), (), s32[]{:S(2)}) async-start(), calls=%async_computation.5 | async-start | bytes 5308416 | tf_op jit(solution)/shard_map/all_gather | solution.py:667
  11.5 156.0 %all-gather.13.cloned.1.call-start = ((), (), s32[]{:S(2)}) async-start(), calls=%async_computation.6 | async-start | bytes 11059200 | tf_op jit(solution)/shard_map/all_gather | solution.py:682
  15.0 202.2 %all-gather.15.cloned.1.call-start = ((), (), s32[]{:S(2)}) async-start(), calls=%async_computation.7 | async-start | bytes 8847360 | tf_op jit(solution)/shard_map/all_gather | solution.py:695
  16.9 29.6 %collective-permute-start = (bf16[136,1536]{1,0:T(8,128)(2,1)S(1)}, bf16[136,1536]{1,0:T(8,128)(2,1)S(1)}, u32[]{:S(2)}, u32[]{:S(2)}) collective-permute-start(bf16[136,1536]{1,0:T(8,128)(2,1)S(1)} %fusion.41), channel_id=1, source_target_pairs={{0,8},{8,16},{16,24},{24,0},{1,9},{9,17},{17,25},{25,1},{2,10},{10... | collective-permute-start | bytes 1253384 | tf_op jit(solution)/shard_map/ppermute | solution.py:248
  18.5 35.8 %collective-permute-start.1 = (bf16[136,1536]{1,0:T(8,128)(2,1)S(1)}, bf16[136,1536]{1,0:T(8,128)(2,1)S(1)}, u32[]{:S(2)}, u32[]{:S(2)}) collective-permute-start(bf16[136,1536]{1,0:T(8,128)(2,1)S(1)} %fusion.41), channel_id=1, source_target_pairs={{0,16},{8,24},{16,0},{24,8},{1,17},{9,25},{17,1},{25,9},{2,18},{10... | collective-permute-start | bytes 1253384 | tf_op jit(solution)/shard_map/ppermute | solution.py:248
  19.7 36.3 %collective-permute-start.2 = (bf16[136,1536]{1,0:T(8,128)(2,1)S(1)}, bf16[136,1536]{1,0:T(8,128)(2,1)S(1)}, u32[]{:S(2)}, u32[]{:S(2)}) collective-permute-start(bf16[136,1536]{1,0:T(8,128)(2,1)S(1)} %fusion.41), channel_id=1, source_target_pairs={{0,24},{8,0},{16,8},{24,16},{1,25},{9,1},{17,9},{25,17},{2,26},{10... | collective-permute-start | bytes 1253384 | tf_op jit(solution)/shard_map/ppermute | solution.py:248
  60.9 13.8 %collective-permute-start.3 = (bf16[528,256]{1,0:T(8,128)(2,1)S(1)}, bf16[528,256]{1,0:T(8,128)(2,1)S(1)}, u32[]{:S(2)}, u32[]{:S(2)}) collective-permute-start(bf16[528,256]{1,0:T(8,128)(2,1)S(1)} %maximum_maximum_fusion.1.refs_0_), channel_id=1, source_target_pairs={{0,2},{1,3},{2,0},{3,1},{4,6},{5,7},{6,4},{7,5},{8,10},{9,11},{10,... | collective-permute-start | bytes 811016 | tf_op jit(solution)/shard_map/ppermute | solution.py:266
  62.4 18.5 %collective-permute-start.4 = (bf16[528,256]{1,0:T(8,128)(2,1)S(1)}, bf16[528,256]{1,0:T(8,128)(2,1)S(1)}, u32[]{:S(2)}, u32[]{:S(2)}) collective-permute-start(bf16[528,256]{1,0:T(8,128)(2,1)S(1)} %maximum_maximum_fusion.1.refs_0_), channel_id=1, source_target_pairs={{0,4},{1,5},{2,6},{3,7},{4,0},{5,1},{6,2},{7,3},{8,12},{9,13},{10,... | collective-permute-start | bytes 811016 | tf_op jit(solution)/shard_map/ppermute | solution.py:266
  62.9 22.5 %collective-permute-start.5 = (bf16[528,256]{1,0:T(8,128)(2,1)S(1)}, bf16[528,256]{1,0:T(8,128)(2,1)S(1)}, u32[]{:S(2)}, u32[]{:S(2)}) collective-permute-start(bf16[528,256]{1,0:T(8,128)(2,1)S(1)} %maximum_maximum_fusion.1.refs_0_), channel_id=1, source_target_pairs={{0,6},{1,7},{2,4},{3,5},{4,2},{5,3},{6,0},{7,1},{8,14},{9,15},{10,... | collective-permute-start | bytes 811016 | tf_op jit(solution)/shard_map/ppermute | solution.py:266
  64.5 21.1 %collective-permute-start.6 = (bf16[528,256]{1,0:T(8,128)(2,1)S(1)}, bf16[528,256]{1,0:T(8,128)(2,1)S(1)}, u32[]{:S(2)}, u32[]{:S(2)}) collective-permute-start(bf16[528,256]{1,0:T(8,128)(2,1)S(1)} %maximum_maximum_fusion.1.refs_0_), channel_id=1, source_target_pairs={{0,1},{1,0},{2,3},{3,2},{4,5},{5,4},{6,7},{7,6},{8,9},{9,8},{10,11... | collective-permute-start | bytes 811016 | tf_op jit(solution)/shard_map/ppermute | solution.py:266
  74.7 11.7 %collective-permute-start.7 = (bf16[528,256]{1,0:T(8,128)(2,1)S(1)}, bf16[528,256]{1,0:T(8,128)(2,1)S(1)}, u32[]{:S(2)}, u32[]{:S(2)}) collective-permute-start(bf16[528,256]{1,0:T(8,128)(2,1)S(1)} %collective-permute-done.3.refs_1_), channel_id=1, source_target_pairs={{0,1},{1,0},{2,3},{3,2},{4,5},{5,4},{6,7},{7,6},{8,9},{9,8},{10,11... | collective-permute-start | bytes 811016 | tf_op jit(solution)/shard_map/ppermute | solution.py:266
  115.9 13.2 %all-to-all-start = ((bf16[4,128,384]{2,1,0:T(8,128)(2,1)}), bf16[4,128,384]{2,1,0:T(8,128)(2,1)S(1)}, u32[]{:S(2)}, u32[]{:S(2)}) async-start(bf16[4,128,384]{2,1,0:T(8,128)(2,1)} %bitcast.12), calls=%async_computation | async-start | bytes 786432 | tf_op jit(solution)/shard_map/all_to_all | solution.py:716
  119.5 239.3 %all-gather.17.cloned.1.call-start = ((), (), s32[]{:S(2)}) async-start(), calls=%async_computation.8 | async-start | bytes 1966080 | tf_op jit(solution)/shard_map/all_gather | solution.py:786
  137.6 10.7 %collective-permute-start.10 = (bf16[96,1536]{1,0:T(8,128)(2,1)}, bf16[96,1536]{1,0:T(8,128)(2,1)}, u32[]{:S(2)}, u32[]{:S(2)}) collective-permute-start(bf16[96,1536]{1,0:T(8,128)(2,1)} %get-tuple-element.310), channel_id=1, source_target_pairs={{0,8},{8,16},{16,24},{24,0},{1,9},{9,17},{17,25},{25,1},{2,10},{10... | collective-permute-start | bytes 884744 | tf_op jit(solution)/shard_map/ppermute | solution.py:248
  138.3 25.2 %collective-permute-start.11 = (bf16[96,1536]{1,0:T(8,128)(2,1)}, bf16[96,1536]{1,0:T(8,128)(2,1)}, u32[]{:S(2)}, u32[]{:S(2)}) collective-permute-start(bf16[96,1536]{1,0:T(8,128)(2,1)} %get-tuple-element.309), channel_id=1, source_target_pairs={{0,16},{8,24},{16,0},{24,8},{1,17},{9,25},{17,1},{25,9},{2,18},{10... | collective-permute-start | bytes 884744 | tf_op jit(solution)/shard_map/ppermute | solution.py:248
  142.4 25.1 %collective-permute-start.12 = (bf16[96,1536]{1,0:T(8,128)(2,1)}, bf16[96,1536]{1,0:T(8,128)(2,1)}, u32[]{:S(2)}, u32[]{:S(2)}) collective-permute-start(bf16[96,1536]{1,0:T(8,128)(2,1)} %get-tuple-element.308), channel_id=1, source_target_pairs={{0,24},{8,0},{16,8},{24,16},{1,25},{9,1},{17,9},{25,17},{2,26},{10... | collective-permute-start | bytes 884744 | tf_op jit(solution)/shard_map/ppermute | solution.py:248
  180.7 10.2 %collective-permute-start.15 = (bf16[96,1536]{1,0:T(8,128)(2,1)}, bf16[96,1536]{1,0:T(8,128)(2,1)S(1)}, u32[]{:S(2)}, u32[]{:S(2)}) collective-permute-start(bf16[96,1536]{1,0:T(8,128)(2,1)} %get-tuple-element.136), channel_id=1, source_target_pairs={{0,8},{8,16},{16,24},{24,0},{1,9},{9,17},{17,25},{25,1},{2,10},{10... | collective-permute-start | bytes 884744 | tf_op jit(solution)/shard_map/ppermute | solution.py:248
  180.7 25.4 %collective-permute-start.14 = (bf16[96,1536]{1,0:T(8,128)(2,1)}, bf16[96,1536]{1,0:T(8,128)(2,1)}, u32[]{:S(2)}, u32[]{:S(2)}) collective-permute-start(bf16[96,1536]{1,0:T(8,128)(2,1)} %get-tuple-element.135), channel_id=1, source_target_pairs={{0,16},{8,24},{16,0},{24,8},{1,17},{9,25},{17,1},{25,9},{2,18},{10... | collective-permute-start | bytes 884744 | tf_op jit(solution)/shard_map/ppermute | solution.py:248
  180.7 25.4 %collective-permute-start.13 = (bf16[96,1536]{1,0:T(8,128)(2,1)}, bf16[96,1536]{1,0:T(8,128)(2,1)}, u32[]{:S(2)}, u32[]{:S(2)}) collective-permute-start(bf16[96,1536]{1,0:T(8,128)(2,1)} %get-tuple-element.134), channel_id=1, source_target_pairs={{0,24},{8,0},{16,8},{24,16},{1,25},{9,1},{17,9},{25,17},{2,26},{10... | collective-permute-start | bytes 884744 | tf_op jit(solution)/shard_map/ppermute | solution.py:248
  211.6 10.3 %collective-permute-start.16 = (bf16[96,1536]{1,0:T(8,128)(2,1)}, bf16[96,1536]{1,0:T(8,128)(2,1)}, u32[]{:S(2)}, u32[]{:S(2)}) collective-permute-start(bf16[96,1536]{1,0:T(8,128)(2,1)} %get-tuple-element.306), channel_id=1, source_target_pairs={{0,8},{8,16},{16,24},{24,0},{1,9},{9,17},{17,25},{25,1},{2,10},{10... | collective-permute-start | bytes 884744 | tf_op jit(solution)/shard_map/ppermute | solution.py:248
  211.6 25.3 %collective-permute-start.17 = (bf16[96,1536]{1,0:T(8,128)(2,1)}, bf16[96,1536]{1,0:T(8,128)(2,1)}, u32[]{:S(2)}, u32[]{:S(2)}) collective-permute-start(bf16[96,1536]{1,0:T(8,128)(2,1)} %get-tuple-element.305), channel_id=1, source_target_pairs={{0,16},{8,24},{16,0},{24,8},{1,17},{9,25},{17,1},{25,9},{2,18},{10... | collective-permute-start | bytes 884744 | tf_op jit(solution)/shard_map/ppermute | solution.py:248
  215.0 25.3 %collective-permute-start.18 = (bf16[96,1536]{1,0:T(8,128)(2,1)}, bf16[96,1536]{1,0:T(8,128)(2,1)}, u32[]{:S(2)}, u32[]{:S(2)}) collective-permute-start(bf16[96,1536]{1,0:T(8,128)(2,1)} %get-tuple-element.304), channel_id=1, source_target_pairs={{0,24},{8,0},{16,8},{24,16},{1,25},{9,1},{17,9},{25,17},{2,26},{10... | collective-permute-start | bytes 884744 | tf_op jit(solution)/shard_map/ppermute | solution.py:248
  251.2 22.6 %collective-permute-start.19 = (bf16[96,1536]{1,0:T(8,128)(2,1)S(1)}, bf16[96,1536]{1,0:T(8,128)(2,1)S(1)}, u32[]{:S(2)}, u32[]{:S(2)}) collective-permute-start(bf16[96,1536]{1,0:T(8,128)(2,1)S(1)} %get-tuple-element.145), channel_id=1, source_target_pairs={{0,24},{8,0},{16,8},{24,16},{1,25},{9,1},{17,9},{25,17},{2,26},{10... | collective-permute-start | bytes 884744 | tf_op jit(solution)/shard_map/ppermute | solution.py:248
  251.3 24.0 %collective-permute-start.20 = (bf16[96,1536]{1,0:T(8,128)(2,1)S(1)}, bf16[96,1536]{1,0:T(8,128)(2,1)S(1)}, u32[]{:S(2)}, u32[]{:S(2)}) collective-permute-start(bf16[96,1536]{1,0:T(8,128)(2,1)S(1)} %get-tuple-element.146), channel_id=1, source_target_pairs={{0,16},{8,24},{16,0},{24,8},{1,17},{9,25},{17,1},{25,9},{2,18},{10... | collective-permute-start | bytes 884744 | tf_op jit(solution)/shard_map/ppermute | solution.py:248
  252.3 25.5 %collective-permute-start.21 = (bf16[96,1536]{1,0:T(8,128)(2,1)S(1)}, bf16[96,1536]{1,0:T(8,128)(2,1)S(1)}, u32[]{:S(2)}, u32[]{:S(2)}) collective-permute-start(bf16[96,1536]{1,0:T(8,128)(2,1)S(1)} %get-tuple-element.147), channel_id=1, source_target_pairs={{0,8},{8,16},{16,24},{24,0},{1,9},{9,17},{17,25},{25,1},{2,10},{10... | collective-permute-start | bytes 884744 | tf_op jit(solution)/shard_map/ppermute | solution.py:248
  263.2 17.2 %collective-permute-start.23 = (bf16[4,192,2048]{2,1,0:T(8,128)(2,1)S(1)}, bf16[4,192,2048]{2,1,0:T(8,128)(2,1)S(1)}, u32[]{:S(2)}, u32[]{:S(2)}) collective-permute-start(bf16[4,192,2048]{2,1,0:T(8,128)(2,1)S(1)} %get-tuple-element.172), channel_id=1, source_target_pairs={{0,1},{1,0},{2,3},{3,2},{4,5},{5,4},{6,7},{7,6},{8,9},{9,8},{10,11... | collective-permute-start | bytes 9437192 | tf_op jit(solution)/shard_map/ppermute | solution.py:266
  266.8 18.7 %collective-permute-start.27 = (bf16[192,1024]{1,0:T(8,128)(2,1)S(1)}, bf16[192,1024]{1,0:T(8,128)(2,1)S(1)}, u32[]{:S(2)}, u32[]{:S(2)}) collective-permute-start(bf16[192,1024]{1,0:T(8,128)(2,1)S(1)} %get-tuple-element.160), channel_id=1, source_target_pairs={{0,2},{1,3},{2,0},{3,1},{4,6},{5,7},{6,4},{7,5},{8,10},{9,11},{10,... | collective-permute-start | bytes 1179656 | tf_op jit(solution)/shard_map/ppermute | solution.py:266
  273.8 16.2 %collective-permute-start.28 = (bf16[192,1024]{1,0:T(8,128)(2,1)S(1)}, bf16[192,1024]{1,0:T(8,128)(2,1)S(1)}, u32[]{:S(2)}, u32[]{:S(2)}) collective-permute-start(bf16[192,1024]{1,0:T(8,128)(2,1)S(1)} %get-tuple-element.161), channel_id=1, source_target_pairs={{0,4},{1,5},{2,6},{3,7},{4,0},{5,1},{6,2},{7,3},{8,12},{9,13},{10,... | collective-permute-start | bytes 1179656 | tf_op jit(solution)/shard_map/ppermute | solution.py:266
  275.3 14.7 %collective-permute-start.29 = (bf16[192,1024]{1,0:T(8,128)(2,1)S(1)}, bf16[192,1024]{1,0:T(8,128)(2,1)S(1)}, u32[]{:S(2)}, u32[]{:S(2)}) collective-permute-start(bf16[192,1024]{1,0:T(8,128)(2,1)S(1)} %get-tuple-element.162), channel_id=1, source_target_pairs={{0,6},{1,7},{2,4},{3,5},{4,2},{5,3},{6,0},{7,1},{8,14},{9,15},{10,... | collective-permute-start | bytes 1179656 | tf_op jit(solution)/shard_map/ppermute | solution.py:266
  291.0 146.4 %all-gather.19.cloned.1.call-start = ((), (), s32[]{:S(2)}) async-start(), calls=%async_computation.9 | async-start | bytes 3932160 | tf_op jit(solution)/shard_map/all_gather | solution.py:800
  291.1 65.1 %collective-permute-start.24 = (bf16[192,2048]{1,0:T(8,128)(2,1)}, bf16[192,2048]{1,0:T(8,128)(2,1)S(1)}, u32[]{:S(2)}, u32[]{:S(2)}) collective-permute-start(bf16[192,2048]{1,0:T(8,128)(2,1)} %copy-done.47), channel_id=1, source_target_pairs={{0,2},{1,3},{2,0},{3,1},{4,6},{5,7},{6,4},{7,5},{8,10},{9,11},{10,... | collective-permute-start | bytes 2359304 | tf_op jit(solution)/shard_map/ppermute | solution.py:266
  293.7 63.4 %collective-permute-start.25 = (bf16[192,2048]{1,0:T(8,128)(2,1)}, bf16[192,2048]{1,0:T(8,128)(2,1)S(1)}, u32[]{:S(2)}, u32[]{:S(2)}) collective-permute-start(bf16[192,2048]{1,0:T(8,128)(2,1)} %copy-done.46), channel_id=1, source_target_pairs={{0,4},{1,5},{2,6},{3,7},{4,0},{5,1},{6,2},{7,3},{8,12},{9,13},{10,... | collective-permute-start | bytes 2359304 | tf_op jit(solution)/shard_map/ppermute | solution.py:266
  295.2 63.6 %collective-permute-start.26 = (bf16[192,2048]{1,0:T(8,128)(2,1)}, bf16[192,2048]{1,0:T(8,128)(2,1)}, u32[]{:S(2)}, u32[]{:S(2)}) collective-permute-start(bf16[192,2048]{1,0:T(8,128)(2,1)} %copy-done.45), channel_id=1, source_target_pairs={{0,6},{1,7},{2,4},{3,5},{4,2},{5,3},{6,0},{7,1},{8,14},{9,15},{10,... | collective-permute-start | bytes 2359304 | tf_op jit(solution)/shard_map/ppermute | solution.py:266
  375.3 13.8 %collective-permute-start.32 = (bf16[512,256]{1,0:T(8,128)(2,1)}, bf16[512,256]{1,0:T(8,128)(2,1)S(1)}, u32[]{:S(2)}, u32[]{:S(2)}) collective-permute-start(bf16[512,256]{1,0:T(8,128)(2,1)} %get-tuple-element.301), channel_id=1, source_target_pairs={{0,4},{1,5},{2,6},{3,7},{4,0},{5,1},{6,2},{7,3},{8,12},{9,13},{10,... | collective-permute-start | bytes 786440 | tf_op jit(solution)/shard_map/ppermute | solution.py:266
  376.2 12.8 %collective-permute-start.33 = (bf16[512,256]{1,0:T(8,128)(2,1)}, bf16[512,256]{1,0:T(8,128)(2,1)S(1)}, u32[]{:S(2)}, u32[]{:S(2)}) collective-permute-start(bf16[512,256]{1,0:T(8,128)(2,1)} %get-tuple-element.300), channel_id=1, source_target_pairs={{0,6},{1,7},{2,4},{3,5},{4,2},{5,3},{6,0},{7,1},{8,14},{9,15},{10,... | collective-permute-start | bytes 786440 | tf_op jit(solution)/shard_map/ppermute | solution.py:266
  395.9 21.6 %collective-permute-start.35 = (bf16[4,192,768]{2,1,0:T(8,128)(2,1)}, bf16[4,192,768]{2,1,0:T(8,128)(2,1)S(1)}, u32[]{:S(2)}, u32[]{:S(2)}) collective-permute-start(bf16[4,192,768]{2,1,0:T(8,128)(2,1)} %get-tuple-element.215), channel_id=1, source_target_pairs={{0,1},{1,0},{2,3},{3,2},{4,5},{5,4},{6,7},{7,6},{8,9},{9,8},{10,11... | collective-permute-start | bytes 3538952 | tf_op jit(solution)/shard_map/ppermute | solution.py:266
  395.9 26.4 %collective-permute-start.39 = (bf16[192,1536]{1,0:T(8,128)(2,1)}, bf16[192,1536]{1,0:T(8,128)(2,1)}, u32[]{:S(2)}, u32[]{:S(2)}) collective-permute-start(bf16[192,1536]{1,0:T(8,128)(2,1)} %get-tuple-element.207), channel_id=1, source_target_pairs={{0,2},{1,3},{2,0},{3,1},{4,6},{5,7},{6,4},{7,5},{8,10},{9,11},{10,... | collective-permute-start | bytes 1769480 | tf_op jit(solution)/shard_map/ppermute | solution.py:266
  396.6 27.2 %collective-permute-start.40 = (bf16[192,1536]{1,0:T(8,128)(2,1)}, bf16[192,1536]{1,0:T(8,128)(2,1)}, u32[]{:S(2)}, u32[]{:S(2)}) collective-permute-start(bf16[192,1536]{1,0:T(8,128)(2,1)} %get-tuple-element.208), channel_id=1, source_target_pairs={{0,4},{1,5},{2,6},{3,7},{4,0},{5,1},{6,2},{7,3},{8,12},{9,13},{10,... | collective-permute-start | bytes 1769480 | tf_op jit(solution)/shard_map/ppermute | solution.py:266
  397.7 27.8 %collective-permute-start.41 = (bf16[192,1536]{1,0:T(8,128)(2,1)}, bf16[192,1536]{1,0:T(8,128)(2,1)}, u32[]{:S(2)}, u32[]{:S(2)}) collective-permute-start(bf16[192,1536]{1,0:T(8,128)(2,1)} %get-tuple-element.209), channel_id=1, source_target_pairs={{0,6},{1,7},{2,4},{3,5},{4,2},{5,3},{6,0},{7,1},{8,14},{9,15},{10,... | collective-permute-start | bytes 1769480 | tf_op jit(solution)/shard_map/ppermute | solution.py:266
  408.2 32.0 %all-to-all-start.3 = ((bf16[4,128,640]{1,2,0:T(8,128)(2,1)}), bf16[4,128,640]{1,2,0:T(8,128)(2,1)}, u32[]{:S(2)}, u32[]{:S(2)}) async-start(bf16[4,128,640]{1,2,0:T(8,128)(2,1)} %pad_maximum_fusion.1), calls=%async_computation.3 | async-start | bytes 1310720 | tf_op jit(solution)/shard_map/all_to_all | solution.py:816
  420.2 19.8 %collective-permute-start.38 = (bf16[192,768]{1,0:T(8,128)(2,1)}, bf16[192,768]{1,0:T(8,128)(2,1)S(1)}, u32[]{:S(2)}, u32[]{:S(2)}) collective-permute-start(bf16[192,768]{1,0:T(8,128)(2,1)} %get-tuple-element.219), channel_id=1, source_target_pairs={{0,6},{1,7},{2,4},{3,5},{4,2},{5,3},{6,0},{7,1},{8,14},{9,15},{10,... | collective-permute-start | bytes 884744 | tf_op jit(solution)/shard_map/ppermute | solution.py:266
  421.4 18.6 %collective-permute-start.37 = (bf16[192,768]{1,0:T(8,128)(2,1)}, bf16[192,768]{1,0:T(8,128)(2,1)S(1)}, u32[]{:S(2)}, u32[]{:S(2)}) collective-permute-start(bf16[192,768]{1,0:T(8,128)(2,1)} %get-tuple-element.218), channel_id=1, source_target_pairs={{0,4},{1,5},{2,6},{3,7},{4,0},{5,1},{6,2},{7,3},{8,12},{9,13},{10,... | collective-permute-start | bytes 884744 | tf_op jit(solution)/shard_map/ppermute | solution.py:266
  422.3 17.7 %collective-permute-start.36 = (bf16[192,768]{1,0:T(8,128)(2,1)}, bf16[192,768]{1,0:T(8,128)(2,1)S(1)}, u32[]{:S(2)}, u32[]{:S(2)}) collective-permute-start(bf16[192,768]{1,0:T(8,128)(2,1)} %get-tuple-element.217), channel_id=1, source_target_pairs={{0,2},{1,3},{2,0},{3,1},{4,6},{5,7},{6,4},{7,5},{8,10},{9,11},{10,... | collective-permute-start | bytes 884744 | tf_op jit(solution)/shard_map/ppermute | solution.py:266
  440.2 21.6 %all-to-all-start.2 = ((bf16[192,4,384]{2,0,1:T(8,128)(2,1)}), bf16[192,4,384]{2,0,1:T(8,128)(2,1)}, u32[]{:S(2)}, u32[]{:S(2)}) async-start(bf16[192,4,384]{2,0,1:T(8,128)(2,1)} %bitcast.131), calls=%async_computation.2 | async-start | bytes 1179648 | tf_op jit(solution)/shard_map/all_to_all | solution.py:839
  464.0 14.5 %collective-permute-start.42 = (bf16[192,1152]{1,0:T(8,128)(2,1)S(1)}, bf16[192,1152]{1,0:T(8,128)(2,1)S(1)}, u32[]{:S(2)}, u32[]{:S(2)}) collective-permute-start(bf16[192,1152]{1,0:T(8,128)(2,1)S(1)} %pad_maximum_fusion.2.refs_0_), channel_id=1, source_target_pairs={{0,8},{8,16},{16,24},{24,0},{1,9},{9,17},{17,25},{25,1},{2,10},{10... | collective-permute-start | bytes 1327112 | tf_op jit(solution)/shard_map/ppermute | solution.py:248
  465.5 37.1 %collective-permute-start.43 = (bf16[192,1152]{1,0:T(8,128)(2,1)S(1)}, bf16[192,1152]{1,0:T(8,128)(2,1)S(1)}, u32[]{:S(2)}, u32[]{:S(2)}) collective-permute-start(bf16[192,1152]{1,0:T(8,128)(2,1)S(1)} %pad_maximum_fusion.2.refs_0_), channel_id=1, source_target_pairs={{0,16},{8,24},{16,0},{24,8},{1,17},{9,25},{17,1},{25,9},{2,18},{10... | collective-permute-start | bytes 1327112 | tf_op jit(solution)/shard_map/ppermute | solution.py:248
  469.8 36.8 %collective-permute-start.44 = (bf16[192,1152]{1,0:T(8,128)(2,1)S(1)}, bf16[192,1152]{1,0:T(8,128)(2,1)S(1)}, u32[]{:S(2)}, u32[]{:S(2)}) collective-permute-start(bf16[192,1152]{1,0:T(8,128)(2,1)S(1)} %pad_maximum_fusion.2.refs_0_), channel_id=1, source_target_pairs={{0,24},{8,0},{16,8},{24,16},{1,25},{9,1},{17,9},{25,17},{2,26},{10... | collective-permute-start | bytes 1327112 | tf_op jit(solution)/shard_map/ppermute | solution.py:248
  (96 other events, 700.2 us)
Sparse Core Ops, SparseCore 0:
  10.8 28.3 all-gather.8
  41.2 49.6 all-gather.10
  93.3 58.2 all-gather.12
  153.9 52.2 all-gather.14
  291.1 42.8 all-gather.16
  363.6 73.7 all-gather.18

commit v10 on v8

--- a/solution.py
+++ b/solution.py
@@ -226,7 +226,7 @@
         ],
         compiler_params=pltpu.CompilerParams(vmem_limit_bytes=28 * 1024 * 1024),
         cost_estimate=pl.CostEstimate(
-            flops=0,
+            flops=10**12 if g else 0,
             bytes_accessed=0,
             transcendentals=0,
         ),
@@ -343,6 +343,170 @@
         compiler_params=pltpu.CompilerParams(vmem_limit_bytes=24 * 1024 * 1024),
         cost_estimate=pl.CostEstimate(flops=0, bytes_accessed=0, transcendentals=0),
     )((shard // 2).astype(jnp.int32).reshape(1), near, there)
+
+
+def fetch_weights(weights_ref, held, sems, piece):
+    copies = [
+        pltpu.make_async_copy(
+            weights_ref.at[:, pl.ds(part * piece, piece)], held.at[part], sems.at[part]
+        )
+        for part in range(3)
+    ]
+    return copies
+
+
+def experts_forward_kernel(count, *refs):
+    rows_in, weights_ref = refs[:count], refs[count]
+    rows_ref, gate_up_ref, hidden_ref = refs[count + 1 : count + 4]
+    out_refs, (held, sems) = refs[count + 4 : -2], refs[-2:]
+    piece = hidden_ref.shape[1]
+    cap = rows_in[0].shape[0]
+    copies = fetch_weights(weights_ref, held, sems, piece)
+    for copy in copies:
+        copy.start()
+    for s in range(count):
+        rows_ref[s * cap : (s + 1) * cap, :] = rows_in[s][...]
+    rows = rows_ref[...]
+    copies[0].wait()
+    gate = dot(rows, held[0])
+    gate_up_ref[:, :piece] = gate
+    copies[1].wait()
+    up = dot(rows, held[1])
+    gate_up_ref[:, piece:] = up
+    hidden = (gate / (1.0 + jnp.exp(-gate)) * up).astype(BF)
+    hidden_ref[...] = hidden
+    copies[2].wait()
+    out = dot_nt(hidden, held[2]).astype(BF)
+    for s in range(count):
+        out_refs[s][...] = out[s * cap : (s + 1) * cap, :]
+
+
+def experts_forward(blocks, weights, piece):
+    count = len(blocks)
+    cap, width = blocks[0].shape
+    rows = count * cap
+    in_vmem = pl.BlockSpec(memory_space=pltpu.VMEM)
+    return pl.pallas_call(
+        functools.partial(experts_forward_kernel, count),
+        in_specs=[in_vmem] * count + [pl.BlockSpec(memory_space=pltpu.HBM)],
+        out_specs=[in_vmem] * (3 + count),
+        out_shape=[
+            jax.ShapeDtypeStruct((rows, width), BF),
+            jax.ShapeDtypeStruct((rows, 2 * piece), F32),
+            jax.ShapeDtypeStruct((rows, piece), BF),
+        ]
+        + [jax.ShapeDtypeStruct((cap, width), BF)] * count,
+        scratch_shapes=[pltpu.VMEM((3, width, piece), BF), pltpu.SemaphoreType.DMA((3,))],
+        compiler_params=pltpu.CompilerParams(vmem_limit_bytes=56 * 1024 * 1024),
+        cost_estimate=pl.CostEstimate(flops=0, bytes_accessed=0, transcendentals=0),
+    )(*blocks, weights)
+
+
+def experts_backward_kernel(count, *refs):
+    grads_in, gate_up_ref, weights_ref = refs[:count], refs[count], refs[count + 1]
+    grads_ref, rows_ref = refs[count + 2 : count + 4]
+    out_refs, (held, sems) = refs[count + 4 : -2], refs[-2:]
+    piece = rows_ref.shape[1] // 2
+    cap = grads_in[0].shape[0]
+    copies = fetch_weights(weights_ref, held, sems, piece)
+    for copy in (copies[2], copies[0], copies[1]):
+        copy.start()
+    for s in range(count):
+        grads_ref[s * cap : (s + 1) * cap, :] = grads_in[s][...]
+    copies[2].wait()
+    grad_hidden = dot(grads_ref[...], held[2])
+    gate = gate_up_ref[:, :piece]
+    up = gate_up_ref[:, piece:]
+    slope = 1.0 / (1.0 + jnp.exp(-gate))
+    grad_gate = (grad_hidden * up * slope * (1.0 + gate * (1.0 - slope))).astype(BF)
+    grad_up = (grad_hidden * gate * slope).astype(BF)
+    rows_ref[:, :piece] = grad_gate
+    rows_ref[:, piece:] = grad_up
+    copies[0].wait()
+    total = dot_nt(grad_gate, held[0])
+    copies[1].wait()
+    total = (total + dot_nt(grad_up, held[1])).astype(BF)
+    for s in range(count):
+        out_refs[s][...] = total[s * cap : (s + 1) * cap, :]
+
+
+def experts_backward(blocks, gate_up, weights, piece):
+    count = len(blocks)
+    cap, width = blocks[0].shape
+    rows = count * cap
+    in_vmem = pl.BlockSpec(memory_space=pltpu.VMEM)
+    return pl.pallas_call(
+        functools.partial(experts_backward_kernel, count),
+        in_specs=[in_vmem] * (count + 1) + [pl.BlockSpec(memory_space=pltpu.HBM)],
+        out_specs=[in_vmem] * (2 + count),
+        out_shape=[
+            jax.ShapeDtypeStruct((rows, width), BF),
+            jax.ShapeDtypeStruct((rows, 2 * piece), BF),
+        ]
+        + [jax.ShapeDtypeStruct((cap, width), BF)] * count,
+        scratch_shapes=[pltpu.VMEM((3, width, piece), BF), pltpu.SemaphoreType.DMA((3,))],
+        compiler_params=pltpu.CompilerParams(vmem_limit_bytes=56 * 1024 * 1024),
+        cost_estimate=pl.CostEstimate(flops=0, bytes_accessed=0, transcendentals=0),
+    )(*blocks, gate_up, weights)
+
+
+def kv_pair_kernel(heads, chips, *refs):
+    near, there, outs = refs[:heads], refs[heads : 2 * heads], refs[2 * heads :]
+    for m in range(chips):
+        for g in range(heads):
+            total = near[g][m].astype(F32) + there[g][m].astype(F32)
+            outs[m][:, g * 2 * HD : (g + 1) * 2 * HD] = total.astype(outs[m].dtype)
+
+
+def kv_pair_sums(near, there):
+    heads, (chips, rows, cols) = len(near), near[0].shape
+    in_vmem = pl.BlockSpec(memory_space=pltpu.VMEM)
+    out = jax.ShapeDtypeStruct((rows, heads * cols), BF)
+    return pl.pallas_call(
+        functools.partial(kv_pair_kernel, heads, chips),
+        in_specs=[in_vmem] * (2 * heads),
+        out_specs=[in_vmem] * chips,
+        out_shape=[jax.ShapeDtypeStruct((rows, heads * cols), F32)] + [out] * (chips - 1),
+        compiler_params=pltpu.CompilerParams(vmem_limit_bytes=20 * 1024 * 1024),
+        cost_estimate=pl.CostEstimate(flops=0, bytes_accessed=0, transcendentals=0),
+    )(*near, *there)
+
+
+def head_columns_kernel(heads, chips, *refs):
+    queries, sums = refs[:heads], refs[heads : heads + chips]
+    factor_ref, ride_ref, sent_ref, columns_ref = refs[heads + chips :]
+    query = jnp.concatenate([each[...] for each in queries], axis=1)
+    keyval = sums[0][...]
+    for each in sums[1:]:
+        keyval = keyval + each[...].astype(F32)
+    both = jnp.concatenate([query, keyval], axis=1)
+    rows, cols = both.shape
+    sent_ref[...] = both.astype(BF)
+    columns_ref[:rows, :cols] = (both * factor_ref[...]).astype(BF)
+    columns_ref[:rows, cols:] = jnp.zeros((rows, LANES), BF)
+    columns_ref[rows:, :cols] = jnp.zeros((ride_ref.shape[0], cols), BF)
+    columns_ref[rows:, cols:] = ride_ref[...]
+
+
+def head_columns(queries, sums, factor, ride):
+    rows = sums[0].shape[0]
+    cols = sum(each.shape[1] for each in queries) + sums[0].shape[1]
+    if cols % LANES:
+        both = jnp.concatenate(list(queries) + [total_of(sums)], axis=1)
+        scaled = jnp.pad((both * factor).astype(BF), ((0, 0), (0, LANES)))
+        return both.astype(BF), jnp.concatenate([scaled, jnp.pad(ride, ((0, 0), (cols, 0)))])
+    in_vmem = pl.BlockSpec(memory_space=pltpu.VMEM)
+    return pl.pallas_call(
+        functools.partial(head_columns_kernel, len(queries), len(sums)),
+        in_specs=[in_vmem] * (len(queries) + len(sums) + 2),
+        out_specs=[in_vmem] * 2,
+        out_shape=[
+            jax.ShapeDtypeStruct((rows, cols), BF),
+            jax.ShapeDtypeStruct((rows + ride.shape[0], cols + LANES), BF),
+        ],
+        compiler_params=pltpu.CompilerParams(vmem_limit_bytes=20 * 1024 * 1024),
+        cost_estimate=pl.CostEstimate(flops=0, bytes_accessed=0, transcendentals=0),
+    )(*queries, *sums, factor, ride)
 
 
 def two_parts(value):
@@ -501,10 +665,9 @@
     token_blocks = after(send_out([token_rows] * seqs, seqs), token_mark)
 
     valid_local = from_relative([each[rows : rows + 1, :rows] for each in token_blocks], z)
-    token_blocks = [each[:rows] for each in token_blocks]
     projected = []
     for block in token_blocks:
-        projected.append(dot(block, heads_full) * root(block.astype(F32)))
+        projected.append(dot(block[:rows], heads_full) * root(block[:rows].astype(F32)))
     projected = from_relative([each.astype(BF) for each in projected], z)
     projected = projected.reshape(local_rows, q_cols + kv_cols)
     head_queries = projected[:, :q_cols] * jnp.asarray(scale, BF)
@@ -538,8 +701,6 @@
         axis=1,
     )
     expert_full = lax.all_gather(expert_shard, "fsdp", axis=0, tiled=True)
-    gate_up_full = expert_full[:, : 2 * piece]
-    down_full = expert_full[:, 2 * piece : 3 * piece]
     router_full = expert_full[:, 3 * piece :]
     attn_shard = jnp.concatenate(
         [
@@ -592,16 +753,12 @@
     dispatch = placed[:, 0] + placed[:, 1]
     placed_pairs = jnp.concatenate([placed[:, 0], placed[:, 1]], axis=0)
     sent_rows = dot_tn(dispatch, normed_two).astype(BF)
+    kv_all = jnp.stack(after(kv_blocks, sent_rows))
     sent_rows = sent_rows.reshape(seqs, CAP, width)
-    expert_rows = jnp.concatenate(send_out([sent_rows[s] for s in range(seqs)], seqs))
-    gate_up = dot(expert_rows, gate_up_full)
-    gate_part = gate_up[:, :piece]
-    up_part = gate_up[:, piece:]
-    sigmoid_gate = jax.nn.sigmoid(gate_part)
-    hidden = (gate_part * sigmoid_gate * up_part).astype(BF)
-    expert_out = dot_nt(hidden, down_full).astype(BF)
-    expert_out = expert_out.reshape(seqs, CAP, width)
-    returned = jnp.concatenate(send_back([expert_out[s] for s in range(seqs)], seqs))
+    expert_rows, gate_up, hidden, *expert_out = experts_forward(
+        send_out([sent_rows[s] for s in range(seqs)], seqs), expert_full, piece
+    )
+    returned = jnp.concatenate(send_back(expert_out, seqs))
     selected = dot(placed_pairs, returned).reshape(2, rows, width)
     mixed_exact = residual + gating[:, :1] * selected[0] + gating[:, 1:] * selected[1]
     valid_rows = valid.astype(F32)
@@ -621,38 +778,41 @@
         [(gating[:, :1] * grad_mixed).astype(BF), (gating[:, 1:] * grad_mixed).astype(BF)], axis=0
     )
     sent_grads = dot_tn(placed_pairs, weighted).astype(BF).reshape(seqs, CAP, width)
-    grad_expert_out = jnp.concatenate(send_out([sent_grads[s] for s in range(seqs)], seqs))
-    grad_expert_out = after(grad_expert_out, attn_full)
-    grad_hidden = dot(grad_expert_out, down_full)
-    grad_gate = grad_hidden * up_part * sigmoid_gate * (1.0 + gate_part * (1.0 - sigmoid_gate))
-    grad_up = grad_hidden * gate_part * sigmoid_gate
-    grad_gate_up_rows = jnp.concatenate([grad_gate, grad_up], axis=-1).astype(BF)
-    grad_rows = dot_nt(grad_gate_up_rows, gate_up_full).astype(BF)
-    returned_mark = grad_rows
-    grad_rows = grad_rows.reshape(seqs, CAP, width)
-    grad_returned = send_back([grad_rows[s] for s in range(seqs)], seqs)
-    grad_returned = jnp.concatenate(grad_returned)
-    held_out, held_hidden = after((grad_expert_out, hidden), returned_mark)
-    down_far, down_near = split_product(held_out, held_hidden, shard, shards)
-    held_rows, held_gate_up = after((expert_rows, grad_gate_up_rows), returned_mark)
-    gate_up_far, gate_up_near = split_product(held_rows, held_gate_up, shard, shards)
-    grad_down_sums = pair_sums(down_near, down_far, shard, shards)
-    kv_all = jnp.stack(after(kv_blocks, returned_mark))
-    tokens_local = from_relative(after(token_blocks, returned_mark), z).reshape(local_rows, width)
+    grad_out_rows = send_out([sent_grads[s] for s in range(seqs)], seqs)
+    grad_out_rows = after(grad_out_rows, attn_full, grad_logits)
+    grad_expert_out, grad_gate_up_rows, *grad_rows = experts_backward(
+        grad_out_rows, gate_up, expert_full, piece
+    )
+    grad_returned = send_back(grad_rows, seqs)
+    tokens_local = from_relative(
+        [each[:rows] for each in after(token_blocks, grad_rows)], z
+    ).reshape(local_rows, width)
     factor_local = root(tokens_local.astype(F32))
     ride_rows = jnp.concatenate([normed_two, jnp.ones((16, width), BF)], axis=0)
     product_rows = jnp.concatenate([tokens_local, ride_rows], axis=0)
-
+    high, low = two_parts(squares)
+    lane = jnp.arange(LANES, dtype=jnp.int32)[None, :]
+    marks = jnp.where(lane == experts + 2 * (shard % 2), high, 0) + jnp.where(
+        lane == experts + 1 + 2 * (shard % 2), low, 0
+    )
+    ride_columns = jnp.concatenate(
+        [grad_logits, marks.astype(BF), jnp.zeros((15, LANES), BF)], axis=0
+    )
+    held_out, held_hidden = after((grad_expert_out, hidden), grad_rows)
+    down_far, down_near = split_product(held_out, held_hidden, shard, shards)
+    grad_down_sums = pair_sums(down_near, down_far, shard, shards)
+    held_rows, held_gate_up = after((expert_rows, grad_gate_up_rows), grad_rows)
+    gate_up_far, gate_up_near = split_product(held_rows, held_gate_up, shard, shards)
     grad_gate_up_sums = pair_sums(gate_up_near, gate_up_far, shard, shards)
     grad_down_blocks = send_chips(grad_down_sums, shards)
-    grad_returned = after(grad_returned, grad_down_sums, product_rows)
+    grad_returned = jnp.concatenate(after(grad_returned, grad_down_sums, product_rows, ride_columns, factor_local))
     grad_normed_two = dot(dispatch, grad_returned) + dot_nt(grad_logits, router_full)
     grad_residual = grad_mixed + root_back(residual, factor_two, grad_normed_two)
     grad_branch = grad_residual.astype(BF)
     grad_attended = dot_nt(after(grad_branch, grad_gate_up_sums), out_full).astype(BF)
     head_grad = lax.all_to_all(grad_attended, "seq", split_axis=1, concat_axis=0, tiled=True)
     grad_gate_up_blocks = send_chips(grad_gate_up_sums, shards)
-    grad_down_shard = total_of(after(grad_down_blocks, head_grad)).astype(BF)
+    grad_down_shard = total_of(after(grad_down_blocks, grad_attended)).astype(BF)
     grad_down = lax.all_gather(grad_down_shard, "seq", axis=0, tiled=False)
 
     grad_q, near, far = [], [], []
@@ -661,48 +821,27 @@
         part_q, near_kv, far_kv = flash_backward(
             head_queries, kv_all, bias, held, exact, lse, seqs, rows, g, groups
         )
+        if g == 0:
+            grad_gate_up_blocks = after(grad_gate_up_blocks, grad_down, part_q)
+            grad_gate_up_shard = total_of(grad_gate_up_blocks).astype(BF)
+            grad_gate_up_all = lax.all_gather(grad_gate_up_shard, "seq", axis=0, tiled=False)
         grad_q.append(part_q)
         near.append(near_kv)
         far.append(far_kv)
-        held = after(head_grad, part_q)
-    grad_gate_up_blocks = after(grad_gate_up_blocks, grad_down, part_q)
-    grad_gate_up_shard = total_of(grad_gate_up_blocks).astype(BF)
-    grad_gate_up_all = lax.all_gather(grad_gate_up_shard, "seq", axis=0, tiled=False)
-    grad_q, near, far = after((grad_q, near, far), grad_gate_up_shard)
-    grad_down = after(grad_down, part_q)
-    grad_q = jnp.concatenate(grad_q, axis=1)
-    near = jnp.concatenate(near, axis=2)
-    far = jnp.concatenate(far, axis=2)
-    there = hop(far, shards, 1)
-    pairs = [near[m].astype(F32) + there[m].astype(F32) for m in range(shards // 2)]
-    pairs = [pairs[0]] + [each.astype(BF) for each in pairs[1:]]
+        held = after(head_grad, grad_gate_up_shard)
+    grad_gate_up_all = after(grad_gate_up_all, part_q)
+    pairs = kv_pair_sums(near, [hop(each, shards, 1) for each in far])
     out_far, out_near = split_product(
-        after(grad_branch, grad_gate_up_shard), attended, shard, shards
+        after(grad_branch, part_q), attended, shard, shards
     )
     out_sums = pair_sums(out_near, after(out_far, pairs), shard, shards)
     out_blocks = send_chips(out_sums, shards)
-    grad_kv = total_of(after(send_chips(pairs, shards), out_sums))
-    grad_heads = jnp.concatenate([grad_q, grad_kv], axis=1)
-    token_grads = lax.all_to_all(
-        grad_heads.astype(BF), "seq", split_axis=0, concat_axis=1, tiled=True
-    )
-
-    high, low = two_parts(squares)
-    lane = jnp.arange(LANES, dtype=jnp.int32)[None, :]
-    marks = jnp.where(lane == experts + 2 * (shard % 2), high, 0) + jnp.where(
-        lane == experts + 1 + 2 * (shard % 2), low, 0
-    )
-    ride_columns = jnp.concatenate(
-        [grad_logits, marks.astype(BF), jnp.zeros((15, LANES), BF)], axis=0
-    )
+    sent_grads, product_columns = head_columns(
+        grad_q, after(send_chips(pairs, shards), out_sums), factor_local, ride_columns
+    )
+    token_grads = lax.all_to_all(sent_grads, "seq", split_axis=0, concat_axis=1, tiled=True)
+
     head_cols = q_cols + kv_cols
-    product_columns = jnp.concatenate(
-        [
-            jnp.pad((grad_heads * factor_local).astype(BF), ((0, 0), (0, LANES))),
-            jnp.pad(ride_columns, ((0, 0), (head_cols, 0))),
-        ],
-        axis=0,
-    )
     head_far, head_near = split_product(product_rows, product_columns, shard, shards)
     head_sums = pair_sums(head_near, head_far, shard, shards)
     out_part = total_of(after(out_blocks, head_sums)).astype(BF)
@@ -723,7 +862,8 @@
         jnp.where(lanes == base_cols + 1, plane_low.astype(F32), head_part),
     )
     out_own = jnp.sum(out_parts.astype(F32), axis=1)
-    final_part = by_rows(jnp.concatenate([head_part, out_own], axis=1).astype(BF))
+    final_part = jnp.concatenate([head_part, out_own], axis=1).astype(BF)
+    final_part = by_rows(after(final_part, grad_gate_up_all))
     final_blocks = [by_rows(each) for each in send_out([final_part] * seqs, seqs)]
     grad_gate_up, grad_gain_ffn = place_gate_up(
         after(grad_gate_up_all, final_part), w_gate_up, gain_two

time: 520 us -> 515 us (level); the launches traced: 515 us -> 505 us
  Pallas kernels: 70.9 us -> 98 us
  matrix products: 41.5 us -> 21.6 us
  waiting for transfers between devices: 220 us -> 209 us
  other arithmetic: 43.3 us -> 32.9 us
  local copies, waits for them, and re-layouts: 35.7 us -> 41 us
    pallas_call x0 -> x4, Pallas kernels: none -> 22.1 us  [the longest x1 9.93 us: experts_backward(): pl.pallas_call(functools.partial(experts_backward_kernel, count), in_spec...]
    ppermute x27 -> x28, waiting for transfers between devices: 65.7 us -> 46.8 us  [hop(): return lax.ppermute(block, 'fsdp', [(i, i ^ mask) for i in range(count)])]
    all_to_all x1, waiting for transfers between devices: 0.01 us -> 15 us  [local(): lax.all_to_all(grad_attended, 'seq', split_axis=1, concat_axis=0, tiled=T...]
    dot_general x10 -> x8, matrix products: 22.3 us -> 11.3 us  [dot(): return jnp.dot(a, b, preferred_element_type=F32)]
    unnamed x219 -> x184, local copies, waits for them, and re-layouts: 17.8 us -> 28.5 us
    ppermute x18, waiting for transfers between devices: 135 us -> 124 us  [shift(): lax.ppermute(block, 'seq', [(i, (i + step) % count) for i in range(count)])]
    dot_general x5 -> x3, matrix products: 18.3 us -> 9.28 us  [dot_nt(): lax.dot_general(a, b, (((1,), (1,)), ((), ())), preferred_element_type=F32)]
    all_gather x1, starting transfers between devices: 8.29 us -> 0.25 us  [local(): lax.all_gather(grad_gate_up_shard, 'seq', axis=0, tiled=False)]
  transfers between devices with their start and end apart: 55 -> 56, of which waited for: 29 -> 31; matrix products, arithmetic and copies ran while one was open for 16% -> 14% of each run, Pallas kernels for 13% -> 17%
where the time goes in v10:
time: 515 us; the launch traced here: 505 us
  waiting for transfers between devices  209 us (41%)
  Pallas kernels  98 us (19%)
  starting transfers between devices  81.7 us (16%)
  local copies, waits for them, and re-layouts  41 us (8%)
  other arithmetic  32.9 us (6%)
  matrix products  21.6 us (4%)
  between operations  21 us (4%)
    ppermute x18, waiting for transfers between devices, shift(): lax.ppermute(block, 'seq', [(i, (i + step) % count) for i in range(count)])  124 us
    ppermute x28, waiting for transfers between devices, hop(): return lax.ppermute(block, 'fsdp', [(i, i ^ mask) for i in range(count)])  46.8 us
    ppermute x18, starting transfers between devices, shift(): lax.ppermute(block, 'seq', [(i, (i + step) % count) for i in range(count)])  30.8 us
    pallas_call x2, Pallas kernels, flash_backward(): pl.pallas_call(functools.partial(backward_kernel, shards, seqs, rows, g,...  29.4 us
    unnamed x184, local copies, waits for them, and re-layouts  28.5 us
    ppermute x28, starting transfers between devices, hop(): return lax.ppermute(block, 'fsdp', [(i, i ^ mask) for i in range(count)])  24 us
    pallas_call x1, Pallas kernels, flash_forward(): pl.pallas_call(functools.partial(forward_kernel, shards, seqs, rows, loca...  18.9 us
    pallas_call x4, Pallas kernels, split_product(): pl.pallas_call(product_kernel, grid=(count // 2,), in_specs=[pl.BlockSpec...  15.6 us
  transfers between devices with their start and end apart: 56, of which 31 were waited for; matrix products, arithmetic and copies ran while one was open for 14% of the time, Pallas kernels for 17%

profile of v10, /device:TPU:12, one launch (start us, length us, event | category | flops | bytes accessed | tf_op | source)
XLA Modules:
  0.0 504.9 jit_solution(8137282057721097590)
XLA Ops:
  18.3 2.6 collective-permute-start.1
  20.9 2.5 collective-permute-start
  23.5 24.8 %collective-permute-done.2 = bf16[136,1536]{1,0:T(8,128)(2,1)S(1)} collective-permute-done((bf16[136,1536]{1,0:T(8,128)(2,1)S(1)}, bf16[136,1536]{1,0:T(8,128)(2,1)S(1)}, u32[]{:S(2)}, u32[]{:S(2)}) %collective-permute-start.2) | collective-permute-done | bytes 417824 | tf_op jit(solution)/shard_map/ppermute | solution.py:237
  48.4 8.1 %collective-permute-done = bf16[136,1536]{1,0:T(8,128)(2,1)S(1)} collective-permute-done((bf16[136,1536]{1,0:T(8,128)(2,1)S(1)}, bf16[136,1536]{1,0:T(8,128)(2,1)S(1)}, u32[]{:S(2)}, u32[]{:S(2)}) %collective-permute-start) | collective-permute-done | bytes 417824 | tf_op jit(solution)/shard_map/ppermute | solution.py:237
  64.9 6.8 %collective-permute-done.5.refs_3_ = bf16[528,256]{1,0:T(8,128)(2,1)S(1)} collective-permute-done((bf16[528,256]{1,0:T(8,128)(2,1)S(1)}, bf16[528,256]{1,0:T(8,128)(2,1)S(1)}, u32[]{:S(2)}, u32[]{:S(2)}) %collective-permute-start.5) | collective-permute-done | bytes 270368 | tf_op jit(solution)/shard_map/ppermute | solution.py:255
  71.7 7.5 %collective-permute-done.4.refs_2_ = bf16[528,256]{1,0:T(8,128)(2,1)S(1)} collective-permute-done((bf16[528,256]{1,0:T(8,128)(2,1)S(1)}, bf16[528,256]{1,0:T(8,128)(2,1)S(1)}, u32[]{:S(2)}, u32[]{:S(2)}) %collective-permute-start.4) | collective-permute-done | bytes 270368 | tf_op jit(solution)/shard_map/ppermute | solution.py:255
  81.9 18.9 %shard_map.221 = (bf16[512,384]{1,0:T(8,128)(2,1)}, f32[512,384]{1,0:T(8,128)S(1)}, f32[512,384]{1,0:T(8,128)S(1)}) custom-call(bf16[528,256]{1,0:T(8,128)(2,1)S(1)} %maximum_maximum_fusion.1.refs_0_, bf16[528,256]{1,0:T(8,128)(2,1)S(1)} %collective-permute-done.3.refs_1_, bf16[528,256]{1,0:T(8,128)(2,1)S(1)} %collective-permute-done.4.refs_2_, ...), custom_call_target="tpu_custom_call" | custom-call | tf_op jit(solution)/shard_map/pallas_call | solution.py:114
  102.7 6.2 %all-to-all-start = ((bf16[4,128,384]{2,1,0:T(8,128)(2,1)}), bf16[4,128,384]{2,1,0:T(8,128)(2,1)}, u32[]{:S(2)}, u32[]{:S(2)}) async-start(bf16[4,128,384]{2,1,0:T(8,128)(2,1)} %bitcast.12), calls=%async_computation | async-start | bytes 786432 | tf_op jit(solution)/shard_map/all_to_all | solution.py:737
  109.7 8.6 %all-to-all-done = bf16[4,128,384]{2,1,0:T(8,128)(2,1)} async-done(((bf16[4,128,384]{2,1,0:T(8,128)(2,1)}), bf16[4,128,384]{2,1,0:T(8,128)(2,1)}, u32[]{:S(2)}, u32[]{:S(2)}) %all-to-all-start) | async-done | bytes 393248 | tf_op jit(solution)/shard_map/all_to_all | solution.py:737
  119.4 4.3 multiply_reduce_fusion.5
  125.5 4.3 collective-permute-start.12
  133.1 15.1 %collective-permute-done.12.refs_3_ = bf16[96,1536]{1,0:T(8,128)(2,1)S(1)} collective-permute-done((bf16[96,1536]{1,0:T(8,128)(2,1)}, bf16[96,1536]{1,0:T(8,128)(2,1)S(1)}, u32[]{:S(2)}, u32[]{:S(2)}) %collective-permute-start.12) | collective-permute-done | bytes 294944 | tf_op jit(solution)/shard_map/ppermute | solution.py:237
  148.3 6.0 %collective-permute-done.10.refs_1_ = bf16[96,1536]{1,0:T(8,128)(2,1)} collective-permute-done((bf16[96,1536]{1,0:T(8,128)(2,1)}, bf16[96,1536]{1,0:T(8,128)(2,1)}, u32[]{:S(2)}, u32[]{:S(2)}) %collective-permute-start.10) | collective-permute-done | bytes 294944 | tf_op jit(solution)/shard_map/ppermute | solution.py:237
  154.3 8.7 %shard_map.222 = (bf16[384,1536]{1,0:T(8,128)(2,1)}, f32[384,2048]{1,0:T(8,128)}, bf16[384,1024]{1,0:T(8,128)(2,1)}, bf16[96,1536]{1,0:T(8,128)(2,1)}, bf16[96,1...) custom-call(bf16[96,1536]{1,0:T(8,128)(2,1)} %get-tuple-element.321.refs_0_, ...), custom_call_target="tpu_custom_call" | custom-call | tf_op jit(solution)/shard_map/pallas_call | solution.py:389
  163.0 4.0 collective-permute-start.14
  168.4 5.7 %collective-permute-done.13 = bf16[96,1536]{1,0:T(8,128)(2,1)S(1)} collective-permute-done((bf16[96,1536]{1,0:T(8,128)(2,1)}, bf16[96,1536]{1,0:T(8,128)(2,1)S(1)}, u32[]{:S(2)}, u32[]{:S(2)}) %collective-permute-start.13) | collective-permute-done | bytes 294944 | tf_op jit(solution)/shard_map/ppermute | solution.py:237
  174.1 10.7 %collective-permute-done.14 = bf16[96,1536]{1,0:T(8,128)(2,1)} collective-permute-done((bf16[96,1536]{1,0:T(8,128)(2,1)}, bf16[96,1536]{1,0:T(8,128)(2,1)}, u32[]{:S(2)}, u32[]{:S(2)}) %collective-permute-start.14) | collective-permute-done | bytes 294944 | tf_op jit(solution)/shard_map/ppermute | solution.py:237
  184.8 6.2 %collective-permute-done.15 = bf16[96,1536]{1,0:T(8,128)(2,1)} collective-permute-done((bf16[96,1536]{1,0:T(8,128)(2,1)}, bf16[96,1536]{1,0:T(8,128)(2,1)}, u32[]{:S(2)}, u32[]{:S(2)}) %collective-permute-start.15) | collective-permute-done | bytes 294944 | tf_op jit(solution)/shard_map/ppermute | solution.py:237
  201.8 5.8 %all-gather.15.cloned.1.call-done = bf16[1536,2560]{1,0:T(8,128)(2,1)} async-done(((bf16[192,2560]{1,0:T(8,128)(2,1)}), bf16[1536,2560]{1,0:T(8,128)(2,1)}) %all-gather.15.cloned.1.call-update) | async-done | bytes 7864336 | tf_op jit(solution)/shard_map/all_gather | solution.py:716
  208.5 10.2 %collective-permute-done.17.refs_2_ = bf16[96,1536]{1,0:T(8,128)(2,1)S(1)} collective-permute-done((bf16[96,1536]{1,0:T(8,128)(2,1)S(1)}, bf16[96,1536]{1,0:T(8,128)(2,1)S(1)}, u32[]{:S(2)}, u32[]{:S(2)}) %collective-permute-start.17) | collective-permute-done | bytes 294944 | tf_op jit(solution)/shard_map/ppermute | solution.py:237
  218.7 6.2 %collective-permute-done.16.refs_1_ = bf16[96,1536]{1,0:T(8,128)(2,1)S(1)} collective-permute-done((bf16[96,1536]{1,0:T(8,128)(2,1)S(1)}, bf16[96,1536]{1,0:T(8,128)(2,1)S(1)}, u32[]{:S(2)}, u32[]{:S(2)}) %collective-permute-start.16) | collective-permute-done | bytes 294944 | tf_op jit(solution)/shard_map/ppermute | solution.py:237
  225.7 9.9 %shard_map.223 = (bf16[384,1536]{1,0:T(8,128)(2,1)}, bf16[384,2048]{1,0:T(8,128)(2,1)}, bf16[96,1536]{1,0:T(8,128)(2,1)}, bf16[96,1536]{1,0:T(8,128)(2,1)}, bf16...) custom-call(bf16[96,1536]{1,0:T(8,128)(2,1)} %get-tuple-element.147.refs_0_, bf16[96,1536]{1,0:T(8,128)(2,1)} %copy-done.59, ...), custom_call_target="tpu_custom_call" | custom-call | tf_op jit(solution)/shard_map/pallas_call | solution.py:438
  235.6 3.3 collective-permute-start.19
  241.9 2.9 shard_map.224
  246.7 4.8 shard_map.226
  259.5 4.5 collective-permute-done.21
  267.0 2.6 shard_map.227
  271.2 4.4 collective-permute-done.28
  287.5 6.0 %all-to-all-start.1 = ((bf16[128,4,384]{2,0,1:T(8,128)(2,1)}), bf16[128,4,384]{2,0,1:T(8,128)(2,1)S(1)}, u32[]{:S(2)}, u32[]{:S(2)}) async-start(bf16[128,4,384]{2,0,1:T(8,128)(2,1)} %bitcast.150), calls=%async_computation.1 | async-start | bytes 786432 | tf_op jit(solution)/shard_map/all_to_all | solution.py:813
  297.8 15.0 %all-to-all-done.1 = bf16[128,4,384]{2,0,1:T(8,128)(2,1)S(1)} async-done(((bf16[128,4,384]{2,0,1:T(8,128)(2,1)}), bf16[128,4,384]{2,0,1:T(8,128)(2,1)S(1)}, u32[]{:S(2)}, u32[]{:S(2)}) %all-to-all-start.1) | async-done | bytes 393248 | tf_op jit(solution)/shard_map/all_to_all | solution.py:813
  315.1 15.0 %shard_map.228 = (f32[512,192]{1,0:T(8,128)S(1)}, bf16[4,512,128]{2,1,0:T(8,128)(2,1)S(1)}, bf16[4,512,128]{2,1,0:T(8,128)(2,1)}) custom-call(bf16[8,528,256]{2,1,0:T(8,128)(2,1)} %bitcast_dynamic-update-slice_fusion.8.refs_0_, bf16[512,384]{1,0:T(8,128)(2,1)S(1)} %slice_multiply_fusion.refs_8_.refs_1_, f32[8,1,1024]{2,1,0:T(1,128)S(1)} %pad_maximum_fusion.4.refs_9_.refs_2_, ...), custom_call_target="tpu_custom_call" | custom-call | tf_op jit(solution)/shard_map/pallas_call | solution.py:212
  330.9 3.5 add_convert_fusion
  336.6 14.5 %shard_map.229 = (f32[512,192]{1,0:T(8,128)S(1)}, bf16[4,512,128]{2,1,0:T(8,128)(2,1)S(1)}, bf16[4,512,128]{2,1,0:T(8,128)(2,1)S(1)}) custom-call(bf16[8,528,256]{2,1,0:T(8,128)(2,1)} %bitcast_dynamic-update-slice_fusion.8.refs_0_, bf16[512,384]{1,0:T(8,128)(2,1)S(1)} %slice_multiply_fusion.refs_8_.refs_1_, ...), custom_call_target="tpu_custom_call" | custom-call | flops 999999995904 | tf_op jit(solution)/shard_map/pallas_call | solution.py:212
  351.7 3.5 shard_map.231
  366.0 4.1 shard_map.232
  370.1 5.1 %collective-permute-done.33.refs_4_ = bf16[512,256]{1,0:T(8,128)(2,1)} collective-permute-done((bf16[512,256]{1,0:T(8,128)(2,1)}, bf16[512,256]{1,0:T(8,128)(2,1)}, u32[]{:S(2)}, u32[]{:S(2)}) %collective-permute-start.33) | collective-permute-done | bytes 262176 | tf_op jit(solution)/shard_map/ppermute | solution.py:255
  377.6 4.4 shard_map.234
  388.7 7.3 %all-to-all-start.3 = ((bf16[4,128,640]{1,2,0:T(8,128)(2,1)}), bf16[4,128,640]{1,2,0:T(8,128)(2,1)}, u32[]{:S(2)}, u32[]{:S(2)}) async-start(bf16[4,128,640]{1,2,0:T(8,128)(2,1)} %copy.101), calls=%async_computation.3 | async-start | bytes 1310720 | tf_op jit(solution)/shard_map/all_to_all | solution.py:842
  402.2 8.7 %collective-permute-done.41 = bf16[192,1536]{1,0:T(8,128)(2,1)} collective-permute-done((bf16[192,1536]{1,0:T(8,128)(2,1)}, bf16[192,1536]{1,0:T(8,128)(2,1)}, u32[]{:S(2)}, u32[]{:S(2)}) %collective-permute-start.41) | collective-permute-done | bytes 589856 | tf_op jit(solution)/shard_map/ppermute | solution.py:255
  418.3 5.3 %collective-permute-done.38 = bf16[192,768]{1,0:T(8,128)(2,1)S(1)} collective-permute-done((bf16[192,768]{1,0:T(8,128)(2,1)S(1)}, bf16[192,768]{1,0:T(8,128)(2,1)S(1)}, u32[]{:S(2)}, u32[]{:S(2)}) %collective-permute-start.38) | collective-permute-done | bytes 294944 | tf_op jit(solution)/shard_map/ppermute | solution.py:255
  425.6 3.0 all-to-all-done.3
  428.6 7.0 %all-to-all-start.2 = ((bf16[192,4,384]{2,0,1:T(8,128)(2,1)}), bf16[192,4,384]{2,0,1:T(8,128)(2,1)S(1)}, u32[]{:S(2)}, u32[]{:S(2)}) async-start(bf16[192,4,384]{2,0,1:T(8,128)(2,1)} %bitcast.136), calls=%async_computation.2 | async-start | bytes 1179648 | tf_op jit(solution)/shard_map/all_to_all | solution.py:848
  435.7 6.3 %fusion.28 = (f32[128]{0:T(128)S(1)}, f32[128]{0:T(128)S(1)}, f32[128,1536]{1,0:T(8,128)S(1)}) fusion(bf16[128,1536]{1,0:T(8,128)(2,1)S(1)} %copy-done.42, bf16[128,2560]{0,1:T(8,128)(2,1)} %bitcast.55, bf16[1536,2560]{1,0:T(8,128)(2,1)} %all-gather.15.cloned.1.call-done), kind=kOutput, calls=%fused_computation.50 | convolution fusion | flops 1007615744 | bytes 9700352 | tf_op jit(solution)/shard_map/dot_general | solution.py:28
  445.2 4.1 all-to-all-done.2
  449.4 3.8 collective-permute-start.45
  455.7 7.2 %fusion = (f32[192]{0:T(256)S(1)}, f32[4,192,2048]{2,1,0:T(8,128)}) fusion(bf16[4,192,2048]{2,1,0:T(8,128)(2,1)} %bitcast.146, bf16[4,192,2048]{2,1,0:T(8,128)(2,1)} %param.25, f32[192]{0:T(256)S(1)} %copy-done.62), kind=kLoop, calls=%fused_computation.2 | loop fusion | flops 7864128 | bytes 12584448 | tf_op jit(solution)/shard_map/reduce_sum | solution.py:557
  465.0 17.0 %collective-permute-done.44.refs_2_ = bf16[192,1152]{1,0:T(8,128)(2,1)S(1)} collective-permute-done((bf16[192,1152]{1,0:T(8,128)(2,1)S(1)}, bf16[192,1152]{1,0:T(8,128)(2,1)S(1)}, u32[]{:S(2)}, u32[]{:S(2)}) %collective-permute-start.44) | collective-permute-done | bytes 442400 | tf_op jit(solution)/shard_map/ppermute | solution.py:237
  482.0 9.0 %collective-permute-done.43.refs_1_ = bf16[192,1152]{1,0:T(8,128)(2,1)S(1)} collective-permute-done((bf16[192,1152]{1,0:T(8,128)(2,1)S(1)}, bf16[192,1152]{1,0:T(8,128)(2,1)S(1)}, u32[]{:S(2)}, u32[]{:S(2)}) %collective-permute-start.43) | collective-permute-done | bytes 442400 | tf_op jit(solution)/shard_map/ppermute | solution.py:237
  (392 shorter events, 128.5 us)
Async XLA Ops:
  7.2 49.9 %all-gather.9.cloned.1.call-start = ((), (), s32[]{:S(2)}) async-start(), calls=%async_computation.4 | async-start | bytes 2211840 | tf_op jit(solution)/shard_map/all_gather | solution.py:661
  10.7 108.7 %all-gather.11.cloned.1.call-start = ((), (), s32[]{:S(2)}) async-start(), calls=%async_computation.5 | async-start | bytes 5308416 | tf_op jit(solution)/shard_map/all_gather | solution.py:688
  11.4 142.9 %all-gather.13.cloned.1.call-start = ((), (), s32[]{:S(2)}) async-start(), calls=%async_computation.6 | async-start | bytes 11059200 | tf_op jit(solution)/shard_map/all_gather | solution.py:703
  16.0 191.6 %all-gather.15.cloned.1.call-start = ((), (), s32[]{:S(2)}) async-start(), calls=%async_computation.7 | async-start | bytes 8847360 | tf_op jit(solution)/shard_map/all_gather | solution.py:716
  17.8 30.5 %collective-permute-start.2 = (bf16[136,1536]{1,0:T(8,128)(2,1)S(1)}, bf16[136,1536]{1,0:T(8,128)(2,1)S(1)}, u32[]{:S(2)}, u32[]{:S(2)}) collective-permute-start(bf16[136,1536]{1,0:T(8,128)(2,1)S(1)} %fusion.37), channel_id=1, source_target_pairs={{0,24},{8,0},{16,8},{24,16},{1,25},{9,1},{17,9},{25,17},{2,26},{10... | collective-permute-start | bytes 1253384 | tf_op jit(solution)/shard_map/ppermute | solution.py:237
  18.3 30.0 %collective-permute-start.1 = (bf16[136,1536]{1,0:T(8,128)(2,1)S(1)}, bf16[136,1536]{1,0:T(8,128)(2,1)S(1)}, u32[]{:S(2)}, u32[]{:S(2)}) collective-permute-start(bf16[136,1536]{1,0:T(8,128)(2,1)S(1)} %fusion.37), channel_id=1, source_target_pairs={{0,16},{8,24},{16,0},{24,8},{1,17},{9,25},{17,1},{25,9},{2,18},{10... | collective-permute-start | bytes 1253384 | tf_op jit(solution)/shard_map/ppermute | solution.py:237
  20.9 35.5 %collective-permute-start = (bf16[136,1536]{1,0:T(8,128)(2,1)S(1)}, bf16[136,1536]{1,0:T(8,128)(2,1)S(1)}, u32[]{:S(2)}, u32[]{:S(2)}) collective-permute-start(bf16[136,1536]{1,0:T(8,128)(2,1)S(1)} %fusion.37), channel_id=1, source_target_pairs={{0,8},{8,16},{16,24},{24,0},{1,9},{9,17},{17,25},{25,1},{2,10},{10... | collective-permute-start | bytes 1253384 | tf_op jit(solution)/shard_map/ppermute | solution.py:237
  62.8 16.5 %collective-permute-start.4 = (bf16[528,256]{1,0:T(8,128)(2,1)S(1)}, bf16[528,256]{1,0:T(8,128)(2,1)S(1)}, u32[]{:S(2)}, u32[]{:S(2)}) collective-permute-start(bf16[528,256]{1,0:T(8,128)(2,1)S(1)} %maximum_maximum_fusion.1.refs_0_), channel_id=1, source_target_pairs={{0,4},{1,5},{2,6},{3,7},{4,0},{5,1},{6,2},{7,3},{8,12},{9,13},{10,... | collective-permute-start | bytes 811016 | tf_op jit(solution)/shard_map/ppermute | solution.py:255
  64.3 15.0 %collective-permute-start.3 = (bf16[528,256]{1,0:T(8,128)(2,1)S(1)}, bf16[528,256]{1,0:T(8,128)(2,1)S(1)}, u32[]{:S(2)}, u32[]{:S(2)}) collective-permute-start(bf16[528,256]{1,0:T(8,128)(2,1)S(1)} %maximum_maximum_fusion.1.refs_0_), channel_id=1, source_target_pairs={{0,2},{1,3},{2,0},{3,1},{4,6},{5,7},{6,4},{7,5},{8,10},{9,11},{10,... | collective-permute-start | bytes 811016 | tf_op jit(solution)/shard_map/ppermute | solution.py:255
  64.9 14.9 %collective-permute-start.6 = (bf16[528,256]{1,0:T(8,128)(2,1)S(1)}, bf16[528,256]{1,0:T(8,128)(2,1)S(1)}, u32[]{:S(2)}, u32[]{:S(2)}) collective-permute-start(bf16[528,256]{1,0:T(8,128)(2,1)S(1)} %maximum_maximum_fusion.1.refs_0_), channel_id=1, source_target_pairs={{0,1},{1,0},{2,3},{3,2},{4,5},{5,4},{6,7},{7,6},{8,9},{9,8},{10,11... | collective-permute-start | bytes 811016 | tf_op jit(solution)/shard_map/ppermute | solution.py:255
  102.7 15.7 %all-to-all-start = ((bf16[4,128,384]{2,1,0:T(8,128)(2,1)}), bf16[4,128,384]{2,1,0:T(8,128)(2,1)}, u32[]{:S(2)}, u32[]{:S(2)}) async-start(bf16[4,128,384]{2,1,0:T(8,128)(2,1)} %bitcast.12), calls=%async_computation | async-start | bytes 786432 | tf_op jit(solution)/shard_map/all_to_all | solution.py:737
  108.9 222.0 %all-gather.17.cloned.1.call-start = ((), (), s32[]{:S(2)}) async-start(), calls=%async_computation.8 | async-start | bytes 1966080 | tf_op jit(solution)/shard_map/all_gather | solution.py:816
  125.5 22.8 %collective-permute-start.12 = (bf16[96,1536]{1,0:T(8,128)(2,1)}, bf16[96,1536]{1,0:T(8,128)(2,1)S(1)}, u32[]{:S(2)}, u32[]{:S(2)}) collective-permute-start(bf16[96,1536]{1,0:T(8,128)(2,1)} %get-tuple-element.318), channel_id=1, source_target_pairs={{0,24},{8,0},{16,8},{24,16},{1,25},{9,1},{17,9},{25,17},{2,26},{10... | collective-permute-start | bytes 884744 | tf_op jit(solution)/shard_map/ppermute | solution.py:237
  129.8 18.5 %collective-permute-start.11 = (bf16[96,1536]{1,0:T(8,128)(2,1)}, bf16[96,1536]{1,0:T(8,128)(2,1)}, u32[]{:S(2)}, u32[]{:S(2)}) collective-permute-start(bf16[96,1536]{1,0:T(8,128)(2,1)} %get-tuple-element.319), channel_id=1, source_target_pairs={{0,16},{8,24},{16,0},{24,8},{1,17},{9,25},{17,1},{25,9},{2,18},{10... | collective-permute-start | bytes 884744 | tf_op jit(solution)/shard_map/ppermute | solution.py:237
  129.8 24.5 %collective-permute-start.10 = (bf16[96,1536]{1,0:T(8,128)(2,1)}, bf16[96,1536]{1,0:T(8,128)(2,1)}, u32[]{:S(2)}, u32[]{:S(2)}) collective-permute-start(bf16[96,1536]{1,0:T(8,128)(2,1)} %get-tuple-element.320), channel_id=1, source_target_pairs={{0,8},{8,16},{16,24},{24,0},{1,9},{9,17},{17,25},{25,1},{2,10},{10... | collective-permute-start | bytes 884744 | tf_op jit(solution)/shard_map/ppermute | solution.py:237
  163.0 11.1 %collective-permute-start.13 = (bf16[96,1536]{1,0:T(8,128)(2,1)}, bf16[96,1536]{1,0:T(8,128)(2,1)S(1)}, u32[]{:S(2)}, u32[]{:S(2)}) collective-permute-start(bf16[96,1536]{1,0:T(8,128)(2,1)} %get-tuple-element.142), channel_id=1, source_target_pairs={{0,24},{8,0},{16,8},{24,16},{1,25},{9,1},{17,9},{25,17},{2,26},{10... | collective-permute-start | bytes 884744 | tf_op jit(solution)/shard_map/ppermute | solution.py:237
  163.0 21.8 %collective-permute-start.14 = (bf16[96,1536]{1,0:T(8,128)(2,1)}, bf16[96,1536]{1,0:T(8,128)(2,1)}, u32[]{:S(2)}, u32[]{:S(2)}) collective-permute-start(bf16[96,1536]{1,0:T(8,128)(2,1)} %get-tuple-element.143), channel_id=1, source_target_pairs={{0,16},{8,24},{16,0},{24,8},{1,17},{9,25},{17,1},{25,9},{2,18},{10... | collective-permute-start | bytes 884744 | tf_op jit(solution)/shard_map/ppermute | solution.py:237
  167.0 24.0 %collective-permute-start.15 = (bf16[96,1536]{1,0:T(8,128)(2,1)}, bf16[96,1536]{1,0:T(8,128)(2,1)}, u32[]{:S(2)}, u32[]{:S(2)}) collective-permute-start(bf16[96,1536]{1,0:T(8,128)(2,1)} %get-tuple-element.144), channel_id=1, source_target_pairs={{0,8},{8,16},{16,24},{24,0},{1,9},{9,17},{17,25},{25,1},{2,10},{10... | collective-permute-start | bytes 884744 | tf_op jit(solution)/shard_map/ppermute | solution.py:237
  197.8 10.8 %collective-permute-start.18 = (bf16[96,1536]{1,0:T(8,128)(2,1)}, bf16[96,1536]{1,0:T(8,128)(2,1)S(1)}, u32[]{:S(2)}, u32[]{:S(2)}) collective-permute-start(bf16[96,1536]{1,0:T(8,128)(2,1)} %get-tuple-element.314), channel_id=1, source_target_pairs={{0,24},{8,0},{16,8},{24,16},{1,25},{9,1},{17,9},{25,17},{2,26},{10... | collective-permute-start | bytes 884744 | tf_op jit(solution)/shard_map/ppermute | solution.py:237
  200.2 18.6 %collective-permute-start.17 = (bf16[96,1536]{1,0:T(8,128)(2,1)S(1)}, bf16[96,1536]{1,0:T(8,128)(2,1)S(1)}, u32[]{:S(2)}, u32[]{:S(2)}) collective-permute-start(bf16[96,1536]{1,0:T(8,128)(2,1)S(1)} %get-tuple-element.315), channel_id=1, source_target_pairs={{0,16},{8,24},{16,0},{24,8},{1,17},{9,25},{17,1},{25,9},{2,18},{10... | collective-permute-start | bytes 884744 | tf_op jit(solution)/shard_map/ppermute | solution.py:237
  201.7 23.3 %collective-permute-start.16 = (bf16[96,1536]{1,0:T(8,128)(2,1)S(1)}, bf16[96,1536]{1,0:T(8,128)(2,1)S(1)}, u32[]{:S(2)}, u32[]{:S(2)}) collective-permute-start(bf16[96,1536]{1,0:T(8,128)(2,1)S(1)} %get-tuple-element.316), channel_id=1, source_target_pairs={{0,8},{8,16},{16,24},{24,0},{1,9},{9,17},{17,25},{25,1},{2,10},{10... | collective-permute-start | bytes 884744 | tf_op jit(solution)/shard_map/ppermute | solution.py:237
  235.6 20.2 %collective-permute-start.19 = (bf16[96,1536]{1,0:T(8,128)(2,1)}, bf16[96,1536]{1,0:T(8,128)(2,1)S(1)}, u32[]{:S(2)}, u32[]{:S(2)}) collective-permute-start(bf16[96,1536]{1,0:T(8,128)(2,1)} %get-tuple-element.153), channel_id=1, source_target_pairs={{0,24},{8,0},{16,8},{24,16},{1,25},{9,1},{17,9},{25,17},{2,26},{10... | collective-permute-start | bytes 884744 | tf_op jit(solution)/shard_map/ppermute | solution.py:237
  238.9 19.3 %collective-permute-start.20 = (bf16[96,1536]{1,0:T(8,128)(2,1)}, bf16[96,1536]{1,0:T(8,128)(2,1)S(1)}, u32[]{:S(2)}, u32[]{:S(2)}) collective-permute-start(bf16[96,1536]{1,0:T(8,128)(2,1)} %get-tuple-element.154), channel_id=1, source_target_pairs={{0,16},{8,24},{16,0},{24,8},{1,17},{9,25},{17,1},{25,9},{2,18},{10... | collective-permute-start | bytes 884744 | tf_op jit(solution)/shard_map/ppermute | solution.py:237
  239.6 24.3 %collective-permute-start.21 = (bf16[96,1536]{1,0:T(8,128)(2,1)}, bf16[96,1536]{1,0:T(8,128)(2,1)S(1)}, u32[]{:S(2)}, u32[]{:S(2)}) collective-permute-start(bf16[96,1536]{1,0:T(8,128)(2,1)} %get-tuple-element.155), channel_id=1, source_target_pairs={{0,8},{8,16},{16,24},{24,0},{1,9},{9,17},{17,25},{25,1},{2,10},{10... | collective-permute-start | bytes 884744 | tf_op jit(solution)/shard_map/ppermute | solution.py:237
  251.5 15.5 %collective-permute-start.23 = (bf16[4,192,2048]{2,1,0:T(8,128)(2,1)S(1)}, bf16[4,192,2048]{2,1,0:T(8,128)(2,1)S(1)}, u32[]{:S(2)}, u32[]{:S(2)}) collective-permute-start(bf16[4,192,2048]{2,1,0:T(8,128)(2,1)S(1)} %get-tuple-element.187), channel_id=1, source_target_pairs={{0,1},{1,0},{2,3},{3,2},{4,5},{5,4},{6,7},{7,6},{8,9},{9,8},{10,11... | collective-permute-start | bytes 9437192 | tf_op jit(solution)/shard_map/ppermute | solution.py:255
  254.9 16.4 %collective-permute-start.27 = (bf16[192,1024]{1,0:T(8,128)(2,1)S(1)}, bf16[192,1024]{1,0:T(8,128)(2,1)S(1)}, u32[]{:S(2)}, u32[]{:S(2)}) collective-permute-start(bf16[192,1024]{1,0:T(8,128)(2,1)S(1)} %get-tuple-element.175), channel_id=1, source_target_pairs={{0,2},{1,3},{2,0},{3,1},{4,6},{5,7},{6,4},{7,5},{8,10},{9,11},{10,... | collective-permute-start | bytes 1179656 | tf_op jit(solution)/shard_map/ppermute | solution.py:255
  255.9 19.8 %collective-permute-start.28 = (bf16[192,1024]{1,0:T(8,128)(2,1)S(1)}, bf16[192,1024]{1,0:T(8,128)(2,1)S(1)}, u32[]{:S(2)}, u32[]{:S(2)}) collective-permute-start(bf16[192,1024]{1,0:T(8,128)(2,1)S(1)} %get-tuple-element.176), channel_id=1, source_target_pairs={{0,4},{1,5},{2,6},{3,7},{4,0},{5,1},{6,2},{7,3},{8,12},{9,13},{10,... | collective-permute-start | bytes 1179656 | tf_op jit(solution)/shard_map/ppermute | solution.py:255
  258.2 17.4 %collective-permute-start.29 = (bf16[192,1024]{1,0:T(8,128)(2,1)S(1)}, bf16[192,1024]{1,0:T(8,128)(2,1)S(1)}, u32[]{:S(2)}, u32[]{:S(2)}) collective-permute-start(bf16[192,1024]{1,0:T(8,128)(2,1)S(1)} %get-tuple-element.177), channel_id=1, source_target_pairs={{0,6},{1,7},{2,4},{3,5},{4,2},{5,3},{6,0},{7,1},{8,14},{9,15},{10,... | collective-permute-start | bytes 1179656 | tf_op jit(solution)/shard_map/ppermute | solution.py:255
  281.5 49.4 %collective-permute-start.24 = (bf16[192,2048]{1,0:T(8,128)(2,1)}, bf16[192,2048]{1,0:T(8,128)(2,1)}, u32[]{:S(2)}, u32[]{:S(2)}) collective-permute-start(bf16[192,2048]{1,0:T(8,128)(2,1)} %get-tuple-element.189), channel_id=1, source_target_pairs={{0,2},{1,3},{2,0},{3,1},{4,6},{5,7},{6,4},{7,5},{8,10},{9,11},{10,... | collective-permute-start | bytes 2359304 | tf_op jit(solution)/shard_map/ppermute | solution.py:255
  282.9 47.9 %collective-permute-start.25 = (bf16[192,2048]{1,0:T(8,128)(2,1)}, bf16[192,2048]{1,0:T(8,128)(2,1)}, u32[]{:S(2)}, u32[]{:S(2)}) collective-permute-start(bf16[192,2048]{1,0:T(8,128)(2,1)} %get-tuple-element.190), channel_id=1, source_target_pairs={{0,4},{1,5},{2,6},{3,7},{4,0},{5,1},{6,2},{7,3},{8,12},{9,13},{10,... | collective-permute-start | bytes 2359304 | tf_op jit(solution)/shard_map/ppermute | solution.py:255
  283.6 47.3 %collective-permute-start.26 = (bf16[192,2048]{1,0:T(8,128)(2,1)}, bf16[192,2048]{1,0:T(8,128)(2,1)}, u32[]{:S(2)}, u32[]{:S(2)}) collective-permute-start(bf16[192,2048]{1,0:T(8,128)(2,1)} %get-tuple-element.191), channel_id=1, source_target_pairs={{0,6},{1,7},{2,4},{3,5},{4,2},{5,3},{6,0},{7,1},{8,14},{9,15},{10,... | collective-permute-start | bytes 2359304 | tf_op jit(solution)/shard_map/ppermute | solution.py:255
  287.5 25.4 %all-to-all-start.1 = ((bf16[128,4,384]{2,0,1:T(8,128)(2,1)}), bf16[128,4,384]{2,0,1:T(8,128)(2,1)S(1)}, u32[]{:S(2)}, u32[]{:S(2)}) async-start(bf16[128,4,384]{2,0,1:T(8,128)(2,1)} %bitcast.150), calls=%async_computation.1 | async-start | bytes 786432 | tf_op jit(solution)/shard_map/all_to_all | solution.py:813
  293.5 151.7 %all-gather.19.cloned.1.call-start = ((), (), s32[]{:S(2)}) async-start(), calls=%async_computation.9 | async-start | bytes 3932160 | tf_op jit(solution)/shard_map/all_gather | solution.py:827
  330.9 25.8 %collective-permute-start.30 = (bf16[4,512,128]{2,1,0:T(8,128)(2,1)}, bf16[4,512,128]{2,1,0:T(8,128)(2,1)}, u32[]{:S(2)}, u32[]{:S(2)}) collective-permute-start(bf16[4,512,128]{2,1,0:T(8,128)(2,1)} %get-tuple-element.209), channel_id=1, source_target_pairs={{0,1},{1,0},{2,3},{3,2},{4,5},{5,4},{6,7},{7,6},{8,9},{9,8},{10,11... | collective-permute-start | bytes 1572872 | tf_op jit(solution)/shard_map/ppermute | solution.py:255
  360.2 15.0 %collective-permute-start.33 = (bf16[512,256]{1,0:T(8,128)(2,1)}, bf16[512,256]{1,0:T(8,128)(2,1)}, u32[]{:S(2)}, u32[]{:S(2)}) collective-permute-start(bf16[512,256]{1,0:T(8,128)(2,1)} %get-tuple-element.213), channel_id=1, source_target_pairs={{0,4},{1,5},{2,6},{3,7},{4,0},{5,1},{6,2},{7,3},{8,12},{9,13},{10,... | collective-permute-start | bytes 786440 | tf_op jit(solution)/shard_map/ppermute | solution.py:255
  362.6 12.6 %collective-permute-start.34 = (bf16[512,256]{1,0:T(8,128)(2,1)}, bf16[512,256]{1,0:T(8,128)(2,1)}, u32[]{:S(2)}, u32[]{:S(2)}) collective-permute-start(bf16[512,256]{1,0:T(8,128)(2,1)} %get-tuple-element.214), channel_id=1, source_target_pairs={{0,6},{1,7},{2,4},{3,5},{4,2},{5,3},{6,0},{7,1},{8,14},{9,15},{10,... | collective-permute-start | bytes 786440 | tf_op jit(solution)/shard_map/ppermute | solution.py:255
  383.0 13.3 %collective-permute-start.36 = (bf16[4,192,768]{2,1,0:T(8,128)(2,1)}, bf16[4,192,768]{2,1,0:T(8,128)(2,1)}, u32[]{:S(2)}, u32[]{:S(2)}) collective-permute-start(bf16[4,192,768]{2,1,0:T(8,128)(2,1)} %get-tuple-element.229), channel_id=1, source_target_pairs={{0,1},{1,0},{2,3},{3,2},{4,5},{5,4},{6,7},{7,6},{8,9},{9,8},{10,11... | collective-permute-start | bytes 3538952 | tf_op jit(solution)/shard_map/ppermute | solution.py:255
  383.0 17.8 %collective-permute-start.40 = (bf16[192,1536]{1,0:T(8,128)(2,1)}, bf16[192,1536]{1,0:T(8,128)(2,1)}, u32[]{:S(2)}, u32[]{:S(2)}) collective-permute-start(bf16[192,1536]{1,0:T(8,128)(2,1)} %get-tuple-element.220), channel_id=1, source_target_pairs={{0,2},{1,3},{2,0},{3,1},{4,6},{5,7},{6,4},{7,5},{8,10},{9,11},{10,... | collective-permute-start | bytes 1769480 | tf_op jit(solution)/shard_map/ppermute | solution.py:255
  384.5 26.4 %collective-permute-start.41 = (bf16[192,1536]{1,0:T(8,128)(2,1)}, bf16[192,1536]{1,0:T(8,128)(2,1)}, u32[]{:S(2)}, u32[]{:S(2)}) collective-permute-start(bf16[192,1536]{1,0:T(8,128)(2,1)} %get-tuple-element.221), channel_id=1, source_target_pairs={{0,4},{1,5},{2,6},{3,7},{4,0},{5,1},{6,2},{7,3},{8,12},{9,13},{10,... | collective-permute-start | bytes 1769480 | tf_op jit(solution)/shard_map/ppermute | solution.py:255
  385.1 28.2 %collective-permute-start.42 = (bf16[192,1536]{1,0:T(8,128)(2,1)}, bf16[192,1536]{1,0:T(8,128)(2,1)}, u32[]{:S(2)}, u32[]{:S(2)}) collective-permute-start(bf16[192,1536]{1,0:T(8,128)(2,1)} %get-tuple-element.222), channel_id=1, source_target_pairs={{0,6},{1,7},{2,4},{3,5},{4,2},{5,3},{6,0},{7,1},{8,14},{9,15},{10,... | collective-permute-start | bytes 1769480 | tf_op jit(solution)/shard_map/ppermute | solution.py:255
  388.7 39.9 %all-to-all-start.3 = ((bf16[4,128,640]{1,2,0:T(8,128)(2,1)}), bf16[4,128,640]{1,2,0:T(8,128)(2,1)}, u32[]{:S(2)}, u32[]{:S(2)}) async-start(bf16[4,128,640]{1,2,0:T(8,128)(2,1)} %copy.101), calls=%async_computation.3 | async-start | bytes 1310720 | tf_op jit(solution)/shard_map/all_to_all | solution.py:842
  398.6 19.7 %collective-permute-start.37 = (bf16[192,768]{1,0:T(8,128)(2,1)S(1)}, bf16[192,768]{1,0:T(8,128)(2,1)S(1)}, u32[]{:S(2)}, u32[]{:S(2)}) collective-permute-start(bf16[192,768]{1,0:T(8,128)(2,1)S(1)} %get-tuple-element.231), channel_id=1, source_target_pairs={{0,2},{1,3},{2,0},{3,1},{4,6},{5,7},{6,4},{7,5},{8,10},{9,11},{10,... | collective-permute-start | bytes 884744 | tf_op jit(solution)/shard_map/ppermute | solution.py:255
  400.2 23.4 %collective-permute-start.38 = (bf16[192,768]{1,0:T(8,128)(2,1)S(1)}, bf16[192,768]{1,0:T(8,128)(2,1)S(1)}, u32[]{:S(2)}, u32[]{:S(2)}) collective-permute-start(bf16[192,768]{1,0:T(8,128)(2,1)S(1)} %get-tuple-element.232), channel_id=1, source_target_pairs={{0,4},{1,5},{2,6},{3,7},{4,0},{5,1},{6,2},{7,3},{8,12},{9,13},{10,... | collective-permute-start | bytes 884744 | tf_op jit(solution)/shard_map/ppermute | solution.py:255
  400.8 24.7 %collective-permute-start.39 = (bf16[192,768]{1,0:T(8,128)(2,1)S(1)}, bf16[192,768]{1,0:T(8,128)(2,1)S(1)}, u32[]{:S(2)}, u32[]{:S(2)}) collective-permute-start(bf16[192,768]{1,0:T(8,128)(2,1)S(1)} %get-tuple-element.233), channel_id=1, source_target_pairs={{0,6},{1,7},{2,4},{3,5},{4,2},{5,3},{6,0},{7,1},{8,14},{9,15},{10,... | collective-permute-start | bytes 884744 | tf_op jit(solution)/shard_map/ppermute | solution.py:255
  428.6 20.7 %all-to-all-start.2 = ((bf16[192,4,384]{2,0,1:T(8,128)(2,1)}), bf16[192,4,384]{2,0,1:T(8,128)(2,1)S(1)}, u32[]{:S(2)}, u32[]{:S(2)}) async-start(bf16[192,4,384]{2,0,1:T(8,128)(2,1)} %bitcast.136), calls=%async_computation.2 | async-start | bytes 1179648 | tf_op jit(solution)/shard_map/all_to_all | solution.py:848
  449.4 15.6 %collective-permute-start.45 = (bf16[192,1152]{1,0:T(8,128)(2,1)S(1)}, bf16[192,1152]{1,0:T(8,128)(2,1)S(1)}, u32[]{:S(2)}, u32[]{:S(2)}) collective-permute-start(bf16[192,1152]{1,0:T(8,128)(2,1)S(1)} %pad_maximum_fusion.refs_0_), channel_id=1, source_target_pairs={{0,24},{8,0},{16,8},{24,16},{1,25},{9,1},{17,9},{25,17},{2,26},{10... | collective-permute-start | bytes 1327112 | tf_op jit(solution)/shard_map/ppermute | solution.py:237
  453.2 28.8 %collective-permute-start.44 = (bf16[192,1152]{1,0:T(8,128)(2,1)S(1)}, bf16[192,1152]{1,0:T(8,128)(2,1)S(1)}, u32[]{:S(2)}, u32[]{:S(2)}) collective-permute-start(bf16[192,1152]{1,0:T(8,128)(2,1)S(1)} %pad_maximum_fusion.refs_0_), channel_id=1, source_target_pairs={{0,16},{8,24},{16,0},{24,8},{1,17},{9,25},{17,1},{25,9},{2,18},{10... | collective-permute-start | bytes 1327112 | tf_op jit(solution)/shard_map/ppermute | solution.py:237
  453.2 37.7 %collective-permute-start.43 = (bf16[192,1152]{1,0:T(8,128)(2,1)S(1)}, bf16[192,1152]{1,0:T(8,128)(2,1)S(1)}, u32[]{:S(2)}, u32[]{:S(2)}) collective-permute-start(bf16[192,1152]{1,0:T(8,128)(2,1)S(1)} %pad_maximum_fusion.refs_0_), channel_id=1, source_target_pairs={{0,8},{8,16},{16,24},{24,0},{1,9},{9,17},{17,25},{25,1},{2,10},{10... | collective-permute-start | bytes 1327112 | tf_op jit(solution)/shard_map/ppermute | solution.py:237
  (84 other events, 916.9 us)
Sparse Core Ops, SparseCore 0:
  10.8 28.3 all-gather.8
  41.1 48.8 all-gather.10
  92.5 60.4 all-gather.12
  155.3 52.2 all-gather.14
  276.8 43.3 all-gather.16
  359.6 85.5 all-gather.18

commit v11 on v10

--- a/solution.py
+++ b/solution.py
@@ -226,7 +226,7 @@
         ],
         compiler_params=pltpu.CompilerParams(vmem_limit_bytes=28 * 1024 * 1024),
         cost_estimate=pl.CostEstimate(
-            flops=10**12 if g else 0,
+            flops=10**12,
             bytes_accessed=0,
             transcendentals=0,
         ),
@@ -243,6 +243,14 @@
 
 def send_back(blocks, count):
     return [blocks[0]] + [shift(blocks[s], count, count - s) for s in range(1, count)]
+
+
+def relay_step(blocks, count):
+    up, down = blocks
+    return (
+        lax.ppermute(up, "seq", [(i, i + 1) for i in range(count - 1)]),
+        lax.ppermute(down, "seq", [(i + 1, i) for i in range(count - 1)]),
+    )
 
 
 def from_relative(blocks, place):
@@ -325,8 +333,7 @@
         part_ref[...] = (near_ref[which].astype(F32) + there_ref[which].astype(F32)).astype(BF)
 
 
-def pair_sums(near, far, shard, count):
-    there = hop(far, count, 1)
+def pair_sums(near, there, shard):
     chips, part, cols = near.shape
     tile = math.gcd(cols, 512)
     if tile % LANES:
@@ -544,23 +551,74 @@
     return factor * grad_scaled - values * (factor * factor * factor * inner)
 
 
-def place_gate_up(base, weight, gain):
+def place_gate_up_kernel(count, place_ref, *refs):
+    blocks = refs[: 2 * count - 1]
+    weight_ref, gain_ref, out_ref, sums_ref, base = refs[2 * count - 1 :]
+    offset = place_ref[0] - pl.program_id(1)
+
+    for s in range(2 * count - 1):
+
+        @pl.when(offset == (s if s < count else count - 1 - s))
+        def _(s=s):
+            base[...] = blocks[s][...].astype(F32)
+
+    @pl.when((pl.program_id(0) == 0) & (pl.program_id(1) == 0))
+    def _():
+        sums_ref[...] = jnp.zeros_like(sums_ref)
+
+    values = base[...]
+    out_ref[0] = values * gain_ref[...]
+    product = jnp.sum(weight_ref[0].astype(F32) * values, axis=1, keepdims=True)
+    sums_ref[...] += jnp.broadcast_to(product, sums_ref.shape)
+
+
+def place_gate_up(steps, weight, gain, place):
     experts, part, both = weight.shape
-    split = base.shape[0] // experts
-    base = base.astype(F32)
-    if split > 1:
-        base = (
-            base.reshape(experts, split, part, 2, both // (2 * split))
-            .transpose(0, 2, 3, 1, 4)
-            .reshape(experts, part, both)
-        )
+    count = len(steps)
+    split = count // experts
+    if split == 1:
+        tile = math.gcd(both, 1024)
+        blocks = [steps[0][0]] + [each[0] for each in steps[1:]] + [each[1] for each in steps[1:]]
+        block = pl.BlockSpec((part, tile), lambda t, e: (0, t))
+        out, sums = pl.pallas_call(
+            functools.partial(place_gate_up_kernel, count),
+            grid=(both // tile, experts),
+            in_specs=[pl.BlockSpec(memory_space=pltpu.SMEM)]
+            + [block] * len(blocks)
+            + [
+                pl.BlockSpec((1, part, tile), lambda t, e: (e, 0, t)),
+                pl.BlockSpec((part, 1), lambda t, e: (0, 0)),
+            ],
+            out_specs=[
+                pl.BlockSpec((1, part, tile), lambda t, e: (e, 0, t)),
+                pl.BlockSpec((part, LANES), lambda t, e: (0, 0)),
+            ],
+            out_shape=[
+                jax.ShapeDtypeStruct(weight.shape, F32),
+                jax.ShapeDtypeStruct((part, LANES), F32),
+            ],
+            scratch_shapes=[pltpu.VMEM((part, tile), F32)],
+            compiler_params=pltpu.CompilerParams(vmem_limit_bytes=28 * 1024 * 1024),
+            cost_estimate=pl.CostEstimate(flops=0, bytes_accessed=0, transcendentals=0),
+        )(place.astype(jnp.int32).reshape(1), *blocks, weight, gain)
+        return out, sums[:, 0]
+    blocks = [steps[0][0]] + [
+        jnp.where(place >= s, steps[s][0], steps[count - s][1]) for s in range(1, count)
+    ]
+    base = (
+        from_relative(blocks, place)
+        .reshape(experts, split, part, 2, both // (2 * split))
+        .transpose(0, 2, 3, 1, 4)
+        .reshape(experts, part, both)
+        .astype(F32)
+    )
     return base * gain, jnp.sum(weight.astype(F32) * base, axis=(0, 2))
 
 
 def place_kernel(count, q_cols, kv_cols, place_ref, *refs):
-    blocks = refs[:count]
+    blocks, outs = refs[:count], refs[count : 2 * count]
     w_query_ref, w_keyval_ref, gain_ref, query_ref, keyval_ref, out_ref, base_ref, sums_ref = refs[
-        count:
+        2 * count :
     ]
     gain = gain_ref[...]
     base = jnp.zeros_like(gain)
@@ -573,7 +631,7 @@
         keyval = blocks[s][:, q_cols : q_cols + kv_cols].astype(F32)
         start = q_cols + kv_cols
         sums = sums + blocks[s][:, start : start + LANES].astype(F32)
-        out_ref[:, q_at] = blocks[s][:, start + LANES :].astype(F32)
+        out_ref[:, q_at] = outs[s][...].astype(F32)
         base = base + jnp.sum(w_query_ref[:, q_at].astype(F32) * query, axis=1, keepdims=True)
         base = base + jnp.sum(w_keyval_ref[:, kv_at].astype(F32) * keyval, axis=1, keepdims=True)
         query_ref[:, q_at] = query * gain
@@ -582,7 +640,7 @@
     sums_ref[...] = sums
 
 
-def place_heads(blocks, place, w_query, w_keyval, gain, q_cols, kv_cols):
+def place_heads(blocks, outs, place, w_query, w_keyval, gain, q_cols, kv_cols):
     count = len(blocks)
     part = w_query.shape[0]
     start = q_cols + kv_cols
@@ -593,14 +651,15 @@
         in_vmem = pl.BlockSpec(memory_space=pltpu.VMEM)
         query, keyval, out, base, sums = pl.pallas_call(
             functools.partial(place_kernel, count, q_cols, kv_cols),
-            in_specs=[pl.BlockSpec(memory_space=pltpu.SMEM)] + [in_vmem] * (count + 3),
+            in_specs=[pl.BlockSpec(memory_space=pltpu.SMEM)] + [in_vmem] * (2 * count + 3),
             out_specs=[in_vmem] * 5,
             out_shape=[wide, narrow, wide, lanes, lanes],
             compiler_params=pltpu.CompilerParams(vmem_limit_bytes=24 * 1024 * 1024),
             cost_estimate=pl.CostEstimate(flops=0, bytes_accessed=0, transcendentals=0),
-        )(place.astype(jnp.int32).reshape(1), *blocks, w_query, w_keyval, gain)
+        )(place.astype(jnp.int32).reshape(1), *blocks, *outs, w_query, w_keyval, gain)
         return query, keyval, out, base[:, 0], sums
     blocks = from_relative(blocks, place).astype(F32)
+    outs = from_relative(outs, place).astype(F32)
 
     def columns(begin, end):
         return blocks[:, :, begin:end].transpose(1, 0, 2).reshape(part, count * (end - begin))
@@ -610,7 +669,7 @@
         w_keyval.astype(F32) * keyval, axis=1
     )
     sums = jnp.sum(blocks[:, :, start : start + LANES], axis=0)
-    out = columns(start + LANES, start + LANES + q_cols)
+    out = outs.transpose(1, 0, 2).reshape(part, count * q_cols)
     return query * gain, keyval * gain, out, base, sums
 
 
@@ -758,7 +817,7 @@
     expert_rows, gate_up, hidden, *expert_out = experts_forward(
         send_out([sent_rows[s] for s in range(seqs)], seqs), expert_full, piece
     )
-    returned = jnp.concatenate(send_back(expert_out, seqs))
+    returned = jnp.concatenate(after(send_back(expert_out, seqs), kv_all))
     selected = dot(placed_pairs, returned).reshape(2, rows, width)
     mixed_exact = residual + gating[:, :1] * selected[0] + gating[:, 1:] * selected[1]
     valid_rows = valid.astype(F32)
@@ -800,10 +859,10 @@
     )
     held_out, held_hidden = after((grad_expert_out, hidden), grad_rows)
     down_far, down_near = split_product(held_out, held_hidden, shard, shards)
-    grad_down_sums = pair_sums(down_near, down_far, shard, shards)
+    grad_down_sums = pair_sums(down_near, hop(down_far, shards, 1), shard)
     held_rows, held_gate_up = after((expert_rows, grad_gate_up_rows), grad_rows)
     gate_up_far, gate_up_near = split_product(held_rows, held_gate_up, shard, shards)
-    grad_gate_up_sums = pair_sums(gate_up_near, gate_up_far, shard, shards)
+    grad_gate_up_sums = pair_sums(gate_up_near, hop(gate_up_far, shards, 1), shard)
     grad_down_blocks = send_chips(grad_down_sums, shards)
     grad_returned = jnp.concatenate(after(grad_returned, grad_down_sums, product_rows, ride_columns, factor_local))
     grad_normed_two = dot(dispatch, grad_returned) + dot_nt(grad_logits, router_full)
@@ -815,8 +874,11 @@
     grad_down_shard = total_of(after(grad_down_blocks, grad_attended)).astype(BF)
     grad_down = lax.all_gather(grad_down_shard, "seq", axis=0, tiled=False)
 
+    out_far, out_near = split_product(
+        after(grad_branch, grad_attended), attended, shard, shards
+    )
     grad_q, near, far = [], [], []
-    held = after(head_grad, grad_attended)
+    held = after(head_grad, grad_down_shard)
     for g in range(local_kv):
         part_q, near_kv, far_kv = flash_backward(
             head_queries, kv_all, bias, held, exact, lse, seqs, rows, g, groups
@@ -824,31 +886,38 @@
         if g == 0:
             grad_gate_up_blocks = after(grad_gate_up_blocks, grad_down, part_q)
             grad_gate_up_shard = total_of(grad_gate_up_blocks).astype(BF)
-            grad_gate_up_all = lax.all_gather(grad_gate_up_shard, "seq", axis=0, tiled=False)
+            steps = [(grad_gate_up_shard, grad_gate_up_shard)]
+            steps.append(relay_step(steps[0], seqs))
+            out_there = hop(after(out_far, head_grad), shards, 1)
         grad_q.append(part_q)
         near.append(near_kv)
         far.append(far_kv)
-        held = after(head_grad, grad_gate_up_shard)
-    grad_gate_up_all = after(grad_gate_up_all, part_q)
+        held = after(head_grad, grad_gate_up_shard, out_there)
+    steps[1] = after(steps[1], part_q)
+    steps.append(relay_step(steps[1], seqs))
+    far = after(far, steps[1])
     pairs = kv_pair_sums(near, [hop(each, shards, 1) for each in far])
-    out_far, out_near = split_product(
-        after(grad_branch, part_q), attended, shard, shards
-    )
-    out_sums = pair_sums(out_near, after(out_far, pairs), shard, shards)
-    out_blocks = send_chips(out_sums, shards)
+    out_sums = pair_sums(out_near, after(out_there, pairs), shard)
     sent_grads, product_columns = head_columns(
-        grad_q, after(send_chips(pairs, shards), out_sums), factor_local, ride_columns
-    )
+        grad_q, after(send_chips(pairs, shards), out_sums, steps[2]), factor_local, ride_columns
+    )
+    steps[2] = after(steps[2], product_columns)
+    while len(steps) < seqs:
+        steps.append(relay_step(steps[-1], seqs))
     token_grads = lax.all_to_all(sent_grads, "seq", split_axis=0, concat_axis=1, tiled=True)
 
     head_cols = q_cols + kv_cols
     head_far, head_near = split_product(product_rows, product_columns, shard, shards)
-    head_sums = pair_sums(head_near, head_far, shard, shards)
-    out_part = total_of(after(out_blocks, head_sums)).astype(BF)
+    head_sums = pair_sums(head_near, hop(head_far, shards, 1), shard)
+    out_part = total_of(
+        after(send_chips(after(out_sums, product_columns), shards), head_sums)
+    ).astype(BF)
     out_parts = lax.all_to_all(
         out_part.reshape(part, seqs, q_cols), "seq", split_axis=1, concat_axis=1, tiled=True
     )
-    head_part = total_of(send_chips(head_sums, shards))
+    out_own = by_rows(jnp.sum(out_parts.astype(F32), axis=1).astype(BF))
+    out_last = [by_rows(each) for each in send_out([out_own] * seqs, seqs)]
+    head_part = total_of(after(send_chips(head_sums, shards), steps[3]))
     grad_normed = dot_nt(after(token_grads, head_part), attn_full)
     grad_tokens = grad_residual + root_back(inputs, root(inputs), grad_normed)
     base_cols = head_cols + experts
@@ -861,21 +930,17 @@
         plane_high.astype(F32),
         jnp.where(lanes == base_cols + 1, plane_low.astype(F32), head_part),
     )
-    out_own = jnp.sum(out_parts.astype(F32), axis=1)
-    final_part = jnp.concatenate([head_part, out_own], axis=1).astype(BF)
-    final_part = by_rows(after(final_part, grad_gate_up_all))
-    final_blocks = [by_rows(each) for each in send_out([final_part] * seqs, seqs)]
-    grad_gate_up, grad_gain_ffn = place_gate_up(
-        after(grad_gate_up_all, final_part), w_gate_up, gain_two
-    )
-    final_blocks = after(final_blocks, grad_gate_up)
+    head_part = by_rows(head_part.astype(BF))
+    head_last = [by_rows(each) for each in send_out([head_part] * seqs, seqs)]
+    grad_gate_up, grad_gain_ffn = place_gate_up(after(steps, head_part), w_gate_up, gain_two, z)
+    head_last, out_last = after((head_last, out_last), grad_gate_up)
     grad_query, grad_keyval, grad_out, grad_gain_attn, sums = place_heads(
-        final_blocks, z, w_query, w_keyval, gain_one, q_cols, kv_cols
+        head_last, out_last, z, w_query, w_keyval, gain_one, q_cols, kv_cols
     )
     loss_value = jnp.sum(sums[0, experts : experts + 2]) / (width * valid_count)
     grad_router_base = sums[:, :experts]
     grad_down = (
-        after(grad_down, final_part).reshape(experts, split, part, piece)
+        after(grad_down, head_part).reshape(experts, split, part, piece)
         .transpose(0, 1, 3, 2)
         .reshape(experts, units, part)
         .astype(F32)

time: 515 us -> 512 us (level)
  the two profiles are of different devices: /device:TPU:12 before, /device:TPU:0 now
where the time goes in v11:
time: 512 us; the launch traced here: 503 us
  waiting for transfers between devices  194 us (38%)
  Pallas kernels  99.8 us (19%)
  starting transfers between devices  99.7 us (19%)
  local copies, waits for them, and re-layouts  38.1 us (7%)
  other arithmetic  29.9 us (6%)
  between operations  21 us (4%)
  matrix products  20.7 us (4%)
    ppermute x21, waiting for transfers between devices, shift(): lax.ppermute(block, 'seq', [(i, (i + step) % count) for i in range(count)])  92.1 us
    ppermute x28, waiting for transfers between devices, hop(): return lax.ppermute(block, 'fsdp', [(i, i ^ mask) for i in range(count)])  48.7 us
    ppermute x21, starting transfers between devices, shift(): lax.ppermute(block, 'seq', [(i, (i + step) % count) for i in range(count)])  38.3 us
    pallas_call x2, Pallas kernels, flash_backward(): pl.pallas_call(functools.partial(backward_kernel, shards, seqs, rows, g,...  27.6 us
    unnamed x200, local copies, waits for them, and re-layouts  26.1 us
    ppermute x28, starting transfers between devices, hop(): return lax.ppermute(block, 'fsdp', [(i, i ^ mask) for i in range(count)])  24.9 us
    all_to_all x1, waiting for transfers between devices, local(): lax.all_to_all(out_part.reshape(part, seqs, q_cols), 'seq', split_axis=1,...  24.7 us
    pallas_call x1, Pallas kernels, flash_forward(): pl.pallas_call(functools.partial(forward_kernel, shards, seqs, rows, loca...  19 us
  transfers between devices with their start and end apart: 64, of which 25 were waited for; matrix products, arithmetic and copies ran while one was open for 11% of the time, Pallas kernels for 16%

profile of v11, /device:TPU:0, one launch (start us, length us, event | category | flops | bytes accessed | tf_op | source)
XLA Modules:
  0.0 503.1 jit_solution(4723594904469941030)
XLA Ops:
  15.1 3.1 collective-permute-start
  18.2 2.6 collective-permute-start.1
  23.7 7.1 %collective-permute-done = bf16[136,1536]{1,0:T(8,128)(2,1)S(1)} collective-permute-done((bf16[136,1536]{1,0:T(8,128)(2,1)S(1)}, bf16[136,1536]{1,0:T(8,128)(2,1)S(1)}, u32[]{:S(2)}, u32[]{:S(2)}) %collective-permute-start) | collective-permute-done | bytes 417824 | tf_op jit(solution)/shard_map/ppermute | solution.py:237
  30.8 17.1 %collective-permute-done.1 = bf16[136,1536]{1,0:T(8,128)(2,1)S(1)} collective-permute-done((bf16[136,1536]{1,0:T(8,128)(2,1)S(1)}, bf16[136,1536]{1,0:T(8,128)(2,1)S(1)}, u32[]{:S(2)}, u32[]{:S(2)}) %collective-permute-start.1) | collective-permute-done | bytes 417824 | tf_op jit(solution)/shard_map/ppermute | solution.py:237
  56.7 8.8 %collective-permute-done.3.refs_1_ = bf16[528,256]{1,0:T(8,128)(2,1)S(1)} collective-permute-done((bf16[528,256]{1,0:T(8,128)(2,1)S(1)}, bf16[528,256]{1,0:T(8,128)(2,1)S(1)}, u32[]{:S(2)}, u32[]{:S(2)}) %collective-permute-start.3) | collective-permute-done | bytes 270368 | tf_op jit(solution)/shard_map/ppermute | solution.py:263
  66.0 8.7 %collective-permute-done.5.refs_3_ = bf16[528,256]{1,0:T(8,128)(2,1)S(1)} collective-permute-done((bf16[528,256]{1,0:T(8,128)(2,1)S(1)}, bf16[528,256]{1,0:T(8,128)(2,1)S(1)}, u32[]{:S(2)}, u32[]{:S(2)}) %collective-permute-start.5) | collective-permute-done | bytes 270368 | tf_op jit(solution)/shard_map/ppermute | solution.py:263
  77.1 19.0 %shard_map.221 = (bf16[512,384]{1,0:T(8,128)(2,1)}, f32[512,384]{1,0:T(8,128)S(1)}, f32[512,384]{1,0:T(8,128)S(1)}) custom-call(bf16[528,256]{1,0:T(8,128)(2,1)S(1)} %maximum_maximum_fusion.1.refs_0_, bf16[528,256]{1,0:T(8,128)(2,1)S(1)} %collective-permute-done.3.refs_1_, bf16[528,256]{1,0:T(8,128)(2,1)S(1)} %collective-permute-done.4.refs_2_, ...), custom_call_target="tpu_custom_call" | custom-call | tf_op jit(solution)/shard_map/pallas_call | solution.py:114
  97.8 11.3 %all-to-all-start = ((bf16[4,128,384]{2,1,0:T(8,128)(2,1)}), bf16[4,128,384]{2,1,0:T(8,128)(2,1)S(1)}, u32[]{:S(2)}, u32[]{:S(2)}) async-start(bf16[4,128,384]{2,1,0:T(8,128)(2,1)} %bitcast.12), calls=%async_computation | async-start | bytes 786432 | tf_op jit(solution)/shard_map/all_to_all | solution.py:796
  110.6 10.7 %all-to-all-done = bf16[4,128,384]{2,1,0:T(8,128)(2,1)S(1)} async-done(((bf16[4,128,384]{2,1,0:T(8,128)(2,1)}), bf16[4,128,384]{2,1,0:T(8,128)(2,1)S(1)}, u32[]{:S(2)}, u32[]{:S(2)}) %all-to-all-start) | async-done | bytes 393248 | tf_op jit(solution)/shard_map/all_to_all | solution.py:796
  123.3 4.1 multiply_reduce_fusion.5
  135.4 6.3 %collective-permute-done.10.refs_1_ = bf16[96,1536]{1,0:T(8,128)(2,1)} collective-permute-done((bf16[96,1536]{1,0:T(8,128)(2,1)S(1)}, bf16[96,1536]{1,0:T(8,128)(2,1)}, u32[]{:S(2)}, u32[]{:S(2)}) %collective-permute-start.10) | collective-permute-done | bytes 294944 | tf_op jit(solution)/shard_map/ppermute | solution.py:237
  141.8 10.9 %collective-permute-done.11.refs_2_ = bf16[96,1536]{1,0:T(8,128)(2,1)} collective-permute-done((bf16[96,1536]{1,0:T(8,128)(2,1)S(1)}, bf16[96,1536]{1,0:T(8,128)(2,1)}, u32[]{:S(2)}, u32[]{:S(2)}) %collective-permute-start.11) | collective-permute-done | bytes 294944 | tf_op jit(solution)/shard_map/ppermute | solution.py:237
  152.7 8.7 %shard_map.222 = (bf16[384,1536]{1,0:T(8,128)(2,1)}, f32[384,2048]{1,0:T(8,128)}, bf16[384,1024]{1,0:T(8,128)(2,1)}, bf16[96,1536]{1,0:T(8,128)(2,1)}, bf16[96,1...) custom-call(bf16[96,1536]{1,0:T(8,128)(2,1)} %get-tuple-element.377.refs_0_, ...), custom_call_target="tpu_custom_call" | custom-call | tf_op jit(solution)/shard_map/pallas_call | solution.py:396
  161.4 6.4 %collective-permute-start.13 = (bf16[96,1536]{1,0:T(8,128)(2,1)}, bf16[96,1536]{1,0:T(8,128)(2,1)S(1)}, u32[]{:S(2)}, u32[]{:S(2)}) collective-permute-start(bf16[96,1536]{1,0:T(8,128)(2,1)} %get-tuple-element.171), channel_id=1, source_target_pairs={{0,24},{8,0},{16,8},{24,16},{1,25},{9,1},{17,9},{25,17},{2,26},{10... | collective-permute-start | bytes 884744 | tf_op jit(solution)/shard_map/ppermute | solution.py:237
  171.1 4.5 collective-permute-done.13
  175.7 20.1 %collective-permute-done.14 = bf16[96,1536]{1,0:T(8,128)(2,1)S(1)} collective-permute-done((bf16[96,1536]{1,0:T(8,128)(2,1)}, bf16[96,1536]{1,0:T(8,128)(2,1)S(1)}, u32[]{:S(2)}, u32[]{:S(2)}) %collective-permute-start.14) | collective-permute-done | bytes 294944 | tf_op jit(solution)/shard_map/ppermute | solution.py:237
  200.8 3.8 collective-permute-start.18
  206.4 6.2 %collective-permute-done.16.refs_1_ = bf16[96,1536]{1,0:T(8,128)(2,1)S(1)} collective-permute-done((bf16[96,1536]{1,0:T(8,128)(2,1)S(1)}, bf16[96,1536]{1,0:T(8,128)(2,1)S(1)}, u32[]{:S(2)}, u32[]{:S(2)}) %collective-permute-start.16) | collective-permute-done | bytes 294944 | tf_op jit(solution)/shard_map/ppermute | solution.py:237
  212.6 10.8 %collective-permute-done.17.refs_2_ = bf16[96,1536]{1,0:T(8,128)(2,1)S(1)} collective-permute-done((bf16[96,1536]{1,0:T(8,128)(2,1)S(1)}, bf16[96,1536]{1,0:T(8,128)(2,1)S(1)}, u32[]{:S(2)}, u32[]{:S(2)}) %collective-permute-start.17) | collective-permute-done | bytes 294944 | tf_op jit(solution)/shard_map/ppermute | solution.py:237
  224.3 9.9 %shard_map.223 = (bf16[384,1536]{1,0:T(8,128)(2,1)}, bf16[384,2048]{1,0:T(8,128)(2,1)}, bf16[96,1536]{1,0:T(8,128)(2,1)}, bf16[96,1536]{1,0:T(8,128)(2,1)}, bf16...) custom-call(bf16[96,1536]{1,0:T(8,128)(2,1)} %get-tuple-element.188.refs_0_, bf16[96,1536]{1,0:T(8,128)(2,1)} %copy-done.65, ...), custom_call_target="tpu_custom_call" | custom-call | tf_op jit(solution)/shard_map/pallas_call | solution.py:445
  234.2 6.2 %collective-permute-start.19 = (bf16[96,1536]{1,0:T(8,128)(2,1)}, bf16[96,1536]{1,0:T(8,128)(2,1)S(1)}, u32[]{:S(2)}, u32[]{:S(2)}) collective-permute-start(bf16[96,1536]{1,0:T(8,128)(2,1)} %get-tuple-element.194), channel_id=1, source_target_pairs={{0,24},{8,0},{16,8},{24,16},{1,25},{9,1},{17,9},{25,17},{2,26},{10... | collective-permute-start | bytes 884744 | tf_op jit(solution)/shard_map/ppermute | solution.py:237
  243.2 2.9 shard_map.224
  246.2 4.8 shard_map.226
  257.6 9.0 %collective-permute-done.20 = bf16[96,1536]{1,0:T(8,128)(2,1)S(1)} collective-permute-done((bf16[96,1536]{1,0:T(8,128)(2,1)}, bf16[96,1536]{1,0:T(8,128)(2,1)S(1)}, u32[]{:S(2)}, u32[]{:S(2)}) %collective-permute-start.20) | collective-permute-done | bytes 294944 | tf_op jit(solution)/shard_map/ppermute | solution.py:237
  277.7 4.1 all-to-all-start.1
  288.0 2.6 shard_map.229
  297.4 13.7 %shard_map.228 = (f32[512,192]{1,0:T(8,128)S(1)}, bf16[4,512,128]{2,1,0:T(8,128)(2,1)S(1)}, bf16[4,512,128]{2,1,0:T(8,128)(2,1)S(1)}) custom-call(bf16[8,528,256]{2,1,0:T(8,128)(2,1)S(1)} %copy-done.29, bf16[512,384]{1,0:T(8,128)(2,1)S(1)} %slice_multiply_fusion.refs_8_.refs_1_, f32[8,1,1024]{2,1,0:T(1,128)S(1)} %pad_maximum_fusion.3.refs_9_.refs_2_, ...), custom_call_target="tpu_custom_call" | custom-call | flops 999999995904 | tf_op jit(solution)/shard_map/pallas_call | solution.py:212
  312.7 3.8 collective-permute-done.28
  316.5 8.1 %all-gather.15.cloned.1.call-done = bf16[768,1024]{1,0:T(8,128)(2,1)} async-done(((bf16[192,1024]{1,0:T(8,128)(2,1)}), bf16[768,1024]{1,0:T(8,128)(2,1)}) %all-gather.15.cloned.1.call-update) | async-done | bytes 1572880 | tf_op jit(solution)/shard_map/all_gather | solution.py:875
  324.6 3.6 add_convert_fusion.refs_0_
  328.3 3.3 collective-permute-start.31
  333.1 13.8 %shard_map.230 = (f32[512,192]{1,0:T(8,128)S(1)}, bf16[4,512,128]{2,1,0:T(8,128)(2,1)S(1)}, bf16[4,512,128]{2,1,0:T(8,128)(2,1)S(1)}) custom-call(bf16[8,528,256]{2,1,0:T(8,128)(2,1)S(1)} %copy-done.30, bf16[512,384]{1,0:T(8,128)(2,1)S(1)} %slice_multiply_fusion.refs_8_.refs_1_, f32[8,1,1024]{2,1,0:T(1,128)S(1)} %pad_maximum_fusion.3.refs_9_.refs_2_, ...), custom_call_target="tpu_custom_call" | custom-call | flops 999999995904 | tf_op jit(solution)/shard_map/pallas_call | solution.py:212
  347.5 5.0 collective-permute-done.32.refs_4_
  353.0 3.5 collective-permute-start.38
  365.0 4.1 shard_map.232
  369.2 5.5 %collective-permute-done.36.refs_4_ = bf16[512,256]{1,0:T(8,128)(2,1)} collective-permute-done((bf16[512,256]{1,0:T(8,128)(2,1)}, bf16[512,256]{1,0:T(8,128)(2,1)}, u32[]{:S(2)}, u32[]{:S(2)}) %collective-permute-start.36) | collective-permute-done | bytes 262176 | tf_op jit(solution)/shard_map/ppermute | solution.py:263
  374.7 3.2 collective-permute-done.39.refs_5_
  380.3 3.7 shard_map.234
  395.6 4.2 all-to-all-start.3
  403.4 11.3 %collective-permute-done.50 = bf16[192,1536]{1,0:T(8,128)(2,1)} collective-permute-done((bf16[192,1536]{1,0:T(8,128)(2,1)}, bf16[192,1536]{1,0:T(8,128)(2,1)}, u32[]{:S(2)}, u32[]{:S(2)}) %collective-permute-start.50) | collective-permute-done | bytes 589856 | tf_op jit(solution)/shard_map/ppermute | solution.py:263
  420.3 8.9 %collective-permute-done.42 = bf16[192,768]{1,0:T(8,128)(2,1)S(1)} collective-permute-done((bf16[192,768]{1,0:T(8,128)(2,1)S(1)}, bf16[192,768]{1,0:T(8,128)(2,1)S(1)}, u32[]{:S(2)}, u32[]{:S(2)}) %collective-permute-start.42) | collective-permute-done | bytes 294944 | tf_op jit(solution)/shard_map/ppermute | solution.py:263
  431.6 3.7 collective-permute-start.48
  435.3 4.2 all-to-all-start.2
  439.5 6.3 %fusion.27 = (f32[128]{0:T(128)S(1)}, f32[128]{0:T(128)S(1)}, f32[128,1536]{1,0:T(8,128)S(1)}) fusion(bf16[128,1536]{1,0:T(8,128)(2,1)S(1)} %copy-done.52, bf16[128,2560]{0,1:T(8,128)(2,1)} %bitcast.55, bf16[1536,2560]{1,0:T(8,128)(2,1)} %all-gather.13.cloned.1.call-done), kind=kOutput, calls=%fused_computation.47 | convolution fusion | flops 1007615744 | bytes 9700352 | tf_op jit(solution)/shard_map/dot_general | solution.py:28
  446.9 24.7 %all-to-all-done.2 = bf16[192,4,384]{2,0,1:T(8,128)(2,1)} async-done(((bf16[192,4,384]{2,0,1:T(8,128)(2,1)}), bf16[192,4,384]{2,0,1:T(8,128)(2,1)}, u32[]{:S(2)}, u32[]{:S(2)}) %all-to-all-start.2) | async-done | bytes 589856 | tf_op jit(solution)/shard_map/all_to_all | solution.py:915
  472.9 3.7 collective-permute-start.54
  476.6 3.5 convert_bitcast_fusion
  480.1 8.3 %shard_map.236 = (f32[4,192,2048]{2,1,0:T(8,128)}, f32[192,128]{1,0:T(8,128)S(1)}) custom-call(s32[1]{0:T(128)} %bitcast.33.place_ref, bf16[192,2048]{1,0:T(8,128)(2,1)} %add_convert_fusion.refs_0_, bf16[192,2048]{1,0:T(8,128)(2,1)} %collective-permute-done.31.refs_1_, bf16[192,2048]{1,0:T(8,128)(2,1)} %collective-permute-done.38.refs_2_, ...), custom_call_target="tpu_custom_call" | custom-call | tf_op jit(solution)/shard_map/pallas_call | solution.py:583
  (424 shorter events, 122.0 us)
Async XLA Ops:
  7.2 41.4 %all-gather.7.cloned.1.call-start = ((), (), s32[]{:S(2)}) async-start(), calls=%async_computation.4 | async-start | bytes 2211840 | tf_op jit(solution)/shard_map/all_gather | solution.py:720
  10.7 112.6 %all-gather.9.cloned.1.call-start = ((), (), s32[]{:S(2)}) async-start(), calls=%async_computation.5 | async-start | bytes 5308416 | tf_op jit(solution)/shard_map/all_gather | solution.py:747
  11.5 141.2 %all-gather.11.cloned.1.call-start = ((), (), s32[]{:S(2)}) async-start(), calls=%async_computation.6 | async-start | bytes 11059200 | tf_op jit(solution)/shard_map/all_gather | solution.py:762
  15.1 191.3 %all-gather.13.cloned.1.call-start = ((), (), s32[]{:S(2)}) async-start(), calls=%async_computation.7 | async-start | bytes 8847360 | tf_op jit(solution)/shard_map/all_gather | solution.py:775
  15.1 15.7 %collective-permute-start = (bf16[136,1536]{1,0:T(8,128)(2,1)S(1)}, bf16[136,1536]{1,0:T(8,128)(2,1)S(1)}, u32[]{:S(2)}, u32[]{:S(2)}) collective-permute-start(bf16[136,1536]{1,0:T(8,128)(2,1)S(1)} %fusion.36), channel_id=1, source_target_pairs={{0,8},{8,16},{16,24},{24,0},{1,9},{9,17},{17,25},{25,1},{2,10},{10... | collective-permute-start | bytes 1253384 | tf_op jit(solution)/shard_map/ppermute | solution.py:237
  18.2 29.7 %collective-permute-start.1 = (bf16[136,1536]{1,0:T(8,128)(2,1)S(1)}, bf16[136,1536]{1,0:T(8,128)(2,1)S(1)}, u32[]{:S(2)}, u32[]{:S(2)}) collective-permute-start(bf16[136,1536]{1,0:T(8,128)(2,1)S(1)} %fusion.36), channel_id=1, source_target_pairs={{0,16},{8,24},{16,0},{24,8},{1,17},{9,25},{17,1},{25,9},{2,18},{10... | collective-permute-start | bytes 1253384 | tf_op jit(solution)/shard_map/ppermute | solution.py:237
  20.8 27.1 %collective-permute-start.2 = (bf16[136,1536]{1,0:T(8,128)(2,1)S(1)}, bf16[136,1536]{1,0:T(8,128)(2,1)S(1)}, u32[]{:S(2)}, u32[]{:S(2)}) collective-permute-start(bf16[136,1536]{1,0:T(8,128)(2,1)S(1)} %fusion.36), channel_id=1, source_target_pairs={{0,24},{8,0},{16,8},{24,16},{1,25},{9,1},{17,9},{25,17},{2,26},{10... | collective-permute-start | bytes 1253384 | tf_op jit(solution)/shard_map/ppermute | solution.py:237
  56.0 18.8 %collective-permute-start.5 = (bf16[528,256]{1,0:T(8,128)(2,1)S(1)}, bf16[528,256]{1,0:T(8,128)(2,1)S(1)}, u32[]{:S(2)}, u32[]{:S(2)}) collective-permute-start(bf16[528,256]{1,0:T(8,128)(2,1)S(1)} %maximum_maximum_fusion.1.refs_0_), channel_id=1, source_target_pairs={{0,6},{1,7},{2,4},{3,5},{4,2},{5,3},{6,0},{7,1},{8,14},{9,15},{10,... | collective-permute-start | bytes 811016 | tf_op jit(solution)/shard_map/ppermute | solution.py:263
  56.6 19.5 %collective-permute-start.6 = (bf16[528,256]{1,0:T(8,128)(2,1)S(1)}, bf16[528,256]{1,0:T(8,128)(2,1)S(1)}, u32[]{:S(2)}, u32[]{:S(2)}) collective-permute-start(bf16[528,256]{1,0:T(8,128)(2,1)S(1)} %maximum_maximum_fusion.1.refs_0_), channel_id=1, source_target_pairs={{0,1},{1,0},{2,3},{3,2},{4,5},{5,4},{6,7},{7,6},{8,9},{9,8},{10,11... | collective-permute-start | bytes 811016 | tf_op jit(solution)/shard_map/ppermute | solution.py:263
  97.8 23.5 %all-to-all-start = ((bf16[4,128,384]{2,1,0:T(8,128)(2,1)}), bf16[4,128,384]{2,1,0:T(8,128)(2,1)S(1)}, u32[]{:S(2)}, u32[]{:S(2)}) async-start(bf16[4,128,384]{2,1,0:T(8,128)(2,1)} %bitcast.12), calls=%async_computation | async-start | bytes 786432 | tf_op jit(solution)/shard_map/all_to_all | solution.py:796
  130.5 22.2 %collective-permute-start.11 = (bf16[96,1536]{1,0:T(8,128)(2,1)S(1)}, bf16[96,1536]{1,0:T(8,128)(2,1)}, u32[]{:S(2)}, u32[]{:S(2)}) collective-permute-start(bf16[96,1536]{1,0:T(8,128)(2,1)S(1)} %get-tuple-element.375), channel_id=1, source_target_pairs={{0,16},{8,24},{16,0},{24,8},{1,17},{9,25},{17,1},{25,9},{2,18},{10... | collective-permute-start | bytes 884744 | tf_op jit(solution)/shard_map/ppermute | solution.py:237
  133.0 19.7 %collective-permute-start.12 = (bf16[96,1536]{1,0:T(8,128)(2,1)S(1)}, bf16[96,1536]{1,0:T(8,128)(2,1)}, u32[]{:S(2)}, u32[]{:S(2)}) collective-permute-start(bf16[96,1536]{1,0:T(8,128)(2,1)S(1)} %get-tuple-element.374), channel_id=1, source_target_pairs={{0,24},{8,0},{16,8},{24,16},{1,25},{9,1},{17,9},{25,17},{2,26},{10... | collective-permute-start | bytes 884744 | tf_op jit(solution)/shard_map/ppermute | solution.py:237
  167.8 28.0 %collective-permute-start.14 = (bf16[96,1536]{1,0:T(8,128)(2,1)}, bf16[96,1536]{1,0:T(8,128)(2,1)S(1)}, u32[]{:S(2)}, u32[]{:S(2)}) collective-permute-start(bf16[96,1536]{1,0:T(8,128)(2,1)} %get-tuple-element.172), channel_id=1, source_target_pairs={{0,16},{8,24},{16,0},{24,8},{1,17},{9,25},{17,1},{25,9},{2,18},{10... | collective-permute-start | bytes 884744 | tf_op jit(solution)/shard_map/ppermute | solution.py:237
  169.8 26.0 %collective-permute-start.15 = (bf16[96,1536]{1,0:T(8,128)(2,1)}, bf16[96,1536]{1,0:T(8,128)(2,1)S(1)}, u32[]{:S(2)}, u32[]{:S(2)}) collective-permute-start(bf16[96,1536]{1,0:T(8,128)(2,1)} %get-tuple-element.173), channel_id=1, source_target_pairs={{0,8},{8,16},{16,24},{24,0},{1,9},{9,17},{17,25},{25,1},{2,10},{10... | collective-permute-start | bytes 884744 | tf_op jit(solution)/shard_map/ppermute | solution.py:237
  200.8 22.7 %collective-permute-start.17 = (bf16[96,1536]{1,0:T(8,128)(2,1)S(1)}, bf16[96,1536]{1,0:T(8,128)(2,1)S(1)}, u32[]{:S(2)}, u32[]{:S(2)}) collective-permute-start(bf16[96,1536]{1,0:T(8,128)(2,1)S(1)} %get-tuple-element.371), channel_id=1, source_target_pairs={{0,16},{8,24},{16,0},{24,8},{1,17},{9,25},{17,1},{25,9},{2,18},{10... | collective-permute-start | bytes 884744 | tf_op jit(solution)/shard_map/ppermute | solution.py:237
  200.8 22.7 %collective-permute-start.18 = (bf16[96,1536]{1,0:T(8,128)(2,1)S(1)}, bf16[96,1536]{1,0:T(8,128)(2,1)S(1)}, u32[]{:S(2)}, u32[]{:S(2)}) collective-permute-start(bf16[96,1536]{1,0:T(8,128)(2,1)S(1)} %get-tuple-element.370), channel_id=1, source_target_pairs={{0,24},{8,0},{16,8},{24,16},{1,25},{9,1},{17,9},{25,17},{2,26},{10... | collective-permute-start | bytes 884744 | tf_op jit(solution)/shard_map/ppermute | solution.py:237
  234.2 21.7 %collective-permute-start.19 = (bf16[96,1536]{1,0:T(8,128)(2,1)}, bf16[96,1536]{1,0:T(8,128)(2,1)S(1)}, u32[]{:S(2)}, u32[]{:S(2)}) collective-permute-start(bf16[96,1536]{1,0:T(8,128)(2,1)} %get-tuple-element.194), channel_id=1, source_target_pairs={{0,24},{8,0},{16,8},{24,16},{1,25},{9,1},{17,9},{25,17},{2,26},{10... | collective-permute-start | bytes 884744 | tf_op jit(solution)/shard_map/ppermute | solution.py:237
  240.5 26.1 %collective-permute-start.20 = (bf16[96,1536]{1,0:T(8,128)(2,1)}, bf16[96,1536]{1,0:T(8,128)(2,1)S(1)}, u32[]{:S(2)}, u32[]{:S(2)}) collective-permute-start(bf16[96,1536]{1,0:T(8,128)(2,1)} %get-tuple-element.195), channel_id=1, source_target_pairs={{0,16},{8,24},{16,0},{24,8},{1,17},{9,25},{17,1},{25,9},{2,18},{10... | collective-permute-start | bytes 884744 | tf_op jit(solution)/shard_map/ppermute | solution.py:237
  241.5 27.6 %collective-permute-start.21 = (bf16[96,1536]{1,0:T(8,128)(2,1)}, bf16[96,1536]{1,0:T(8,128)(2,1)S(1)}, u32[]{:S(2)}, u32[]{:S(2)}) collective-permute-start(bf16[96,1536]{1,0:T(8,128)(2,1)} %get-tuple-element.196), channel_id=1, source_target_pairs={{0,8},{8,16},{16,24},{24,0},{1,9},{9,17},{17,25},{25,1},{2,10},{10... | collective-permute-start | bytes 884744 | tf_op jit(solution)/shard_map/ppermute | solution.py:237
  251.0 21.8 %collective-permute-start.23 = (bf16[4,192,2048]{2,1,0:T(8,128)(2,1)S(1)}, bf16[4,192,2048]{2,1,0:T(8,128)(2,1)S(1)}, u32[]{:S(2)}, u32[]{:S(2)}) collective-permute-start(bf16[4,192,2048]{2,1,0:T(8,128)(2,1)S(1)} %get-tuple-element.220), channel_id=1, source_target_pairs={{0,1},{1,0},{2,3},{3,2},{4,5},{5,4},{6,7},{7,6},{8,9},{9,8},{10,11... | collective-permute-start | bytes 9437192 | tf_op jit(solution)/shard_map/ppermute | solution.py:263
  254.5 28.4 %collective-permute-start.24 = (bf16[192,1024]{1,0:T(8,128)(2,1)}, bf16[192,1024]{1,0:T(8,128)(2,1)}, u32[]{:S(2)}, u32[]{:S(2)}) collective-permute-start(bf16[192,1024]{1,0:T(8,128)(2,1)} %get-tuple-element.208), channel_id=1, source_target_pairs={{0,2},{1,3},{2,0},{3,1},{4,6},{5,7},{6,4},{7,5},{8,10},{9,11},{10,... | collective-permute-start | bytes 1179656 | tf_op jit(solution)/shard_map/ppermute | solution.py:263
  256.0 29.5 %collective-permute-start.25 = (bf16[192,1024]{1,0:T(8,128)(2,1)}, bf16[192,1024]{1,0:T(8,128)(2,1)}, u32[]{:S(2)}, u32[]{:S(2)}) collective-permute-start(bf16[192,1024]{1,0:T(8,128)(2,1)} %get-tuple-element.209), channel_id=1, source_target_pairs={{0,4},{1,5},{2,6},{3,7},{4,0},{5,1},{6,2},{7,3},{8,12},{9,13},{10,... | collective-permute-start | bytes 1179656 | tf_op jit(solution)/shard_map/ppermute | solution.py:263
  266.6 18.9 %collective-permute-start.26 = (bf16[192,1024]{1,0:T(8,128)(2,1)}, bf16[192,1024]{1,0:T(8,128)(2,1)}, u32[]{:S(2)}, u32[]{:S(2)}) collective-permute-start(bf16[192,1024]{1,0:T(8,128)(2,1)} %get-tuple-element.210), channel_id=1, source_target_pairs={{0,6},{1,7},{2,4},{3,5},{4,2},{5,3},{6,0},{7,1},{8,14},{9,15},{10,... | collective-permute-start | bytes 1179656 | tf_op jit(solution)/shard_map/ppermute | solution.py:263
  277.7 15.6 %all-to-all-start.1 = ((bf16[128,4,384]{2,0,1:T(8,128)(2,1)}), bf16[128,4,384]{2,0,1:T(8,128)(2,1)}, u32[]{:S(2)}, u32[]{:S(2)}) async-start(bf16[128,4,384]{2,0,1:T(8,128)(2,1)} %bitcast.147), calls=%async_computation.1 | async-start | bytes 786432 | tf_op jit(solution)/shard_map/all_to_all | solution.py:872
  281.8 42.8 %all-gather.15.cloned.1.call-start = ((), (), s32[]{:S(2)}) async-start(), calls=%async_computation.8 | async-start | bytes 1966080 | tf_op jit(solution)/shard_map/all_gather | solution.py:875
  281.9 30.8 %collective-permute-start.27 = (bf16[192,2048]{1,0:T(8,128)(2,1)}, bf16[192,2048]{1,0:T(8,128)(2,1)}, u32[]{:S(2)}, u32[]{:S(2)}) collective-permute-start(bf16[192,2048]{1,0:T(8,128)(2,1)} %copy-done.40), channel_id=1, source_target_pairs={{0,2},{1,3},{2,0},{3,1},{4,6},{5,7},{6,4},{7,5},{8,10},{9,11},{10,... | collective-permute-start | bytes 2359304 | tf_op jit(solution)/shard_map/ppermute | solution.py:263
  282.0 34.5 %collective-permute-start.28 = (bf16[192,2048]{1,0:T(8,128)(2,1)}, bf16[192,2048]{1,0:T(8,128)(2,1)}, u32[]{:S(2)}, u32[]{:S(2)}) collective-permute-start(bf16[192,2048]{1,0:T(8,128)(2,1)} %copy-done.39), channel_id=1, source_target_pairs={{0,4},{1,5},{2,6},{3,7},{4,0},{5,1},{6,2},{7,3},{8,12},{9,13},{10,... | collective-permute-start | bytes 2359304 | tf_op jit(solution)/shard_map/ppermute | solution.py:263
  282.9 33.6 %collective-permute-start.29 = (bf16[192,2048]{1,0:T(8,128)(2,1)}, bf16[192,2048]{1,0:T(8,128)(2,1)}, u32[]{:S(2)}, u32[]{:S(2)}) collective-permute-start(bf16[192,2048]{1,0:T(8,128)(2,1)} %copy-done.38), channel_id=1, source_target_pairs={{0,6},{1,7},{2,4},{3,5},{4,2},{5,3},{6,0},{7,1},{8,14},{9,15},{10,... | collective-permute-start | bytes 2359304 | tf_op jit(solution)/shard_map/ppermute | solution.py:263
  293.4 39.7 %collective-permute-start.30 = (bf16[4,192,1536]{2,1,0:T(8,128)(2,1)}, bf16[4,192,1536]{2,1,0:T(8,128)(2,1)}, u32[]{:S(2)}, u32[]{:S(2)}) collective-permute-start(bf16[4,192,1536]{2,1,0:T(8,128)(2,1)} %copy-done.31), channel_id=1, source_target_pairs={{0,1},{1,0},{2,3},{3,2},{4,5},{5,4},{6,7},{7,6},{8,9},{9,8},{10,11... | collective-permute-start | bytes 7077896 | tf_op jit(solution)/shard_map/ppermute | solution.py:263
  328.3 19.2 %collective-permute-start.31 = (bf16[192,2048]{1,0:T(8,128)(2,1)}, bf16[192,2048]{1,0:T(8,128)(2,1)}, u32[]{:S(2)}, u32[]{:S(2)}) collective-permute-start(bf16[192,2048]{1,0:T(8,128)(2,1)} %add_convert_fusion.refs_0_), channel_id=1, source_target_pairs={{0,8},{8,16},{16,24},{1,9},{9,17},{17,25},{2,10},{10,18},{18,26},{... | collective-permute-start | bytes 2359304 | tf_op jit(solution)/shard_map/ppermute | solution.py:251
  331.5 21.0 %collective-permute-start.32 = (bf16[192,2048]{1,0:T(8,128)(2,1)}, bf16[192,2048]{1,0:T(8,128)(2,1)}, u32[]{:S(2)}, u32[]{:S(2)}) collective-permute-start(bf16[192,2048]{1,0:T(8,128)(2,1)} %add_convert_fusion.refs_0_), channel_id=1, source_target_pairs={{8,0},{16,8},{24,16},{9,1},{17,9},{25,17},{10,2},{18,10},{26,18},{... | collective-permute-start | bytes 2359304 | tf_op jit(solution)/shard_map/ppermute | solution.py:252
  353.0 21.7 %collective-permute-start.38 = (bf16[192,2048]{1,0:T(8,128)(2,1)}, bf16[192,2048]{1,0:T(8,128)(2,1)}, u32[]{:S(2)}, u32[]{:S(2)}) collective-permute-start(bf16[192,2048]{1,0:T(8,128)(2,1)} %collective-permute-done.31.refs_1_), channel_id=1, source_target_pairs={{0,8},{8,16},{16,24},{1,9},{9,17},{17,25},{2,10},{10,18},{18,26},{... | collective-permute-start | bytes 2359304 | tf_op jit(solution)/shard_map/ppermute | solution.py:251
  356.5 21.4 %collective-permute-start.39 = (bf16[192,2048]{1,0:T(8,128)(2,1)}, bf16[192,2048]{1,0:T(8,128)(2,1)}, u32[]{:S(2)}, u32[]{:S(2)}) collective-permute-start(bf16[192,2048]{1,0:T(8,128)(2,1)} %collective-permute-done.32.refs_4_), channel_id=1, source_target_pairs={{8,0},{16,8},{24,16},{9,1},{17,9},{25,17},{10,2},{18,10},{26,18},{... | collective-permute-start | bytes 2359304 | tf_op jit(solution)/shard_map/ppermute | solution.py:252
  385.0 16.7 %collective-permute-start.49 = (bf16[192,1536]{1,0:T(8,128)(2,1)}, bf16[192,1536]{1,0:T(8,128)(2,1)}, u32[]{:S(2)}, u32[]{:S(2)}) collective-permute-start(bf16[192,1536]{1,0:T(8,128)(2,1)} %get-tuple-element.279), channel_id=1, source_target_pairs={{0,2},{1,3},{2,0},{3,1},{4,6},{5,7},{6,4},{7,5},{8,10},{9,11},{10,... | collective-permute-start | bytes 1769480 | tf_op jit(solution)/shard_map/ppermute | solution.py:263
  386.5 28.3 %collective-permute-start.50 = (bf16[192,1536]{1,0:T(8,128)(2,1)}, bf16[192,1536]{1,0:T(8,128)(2,1)}, u32[]{:S(2)}, u32[]{:S(2)}) collective-permute-start(bf16[192,1536]{1,0:T(8,128)(2,1)} %get-tuple-element.280), channel_id=1, source_target_pairs={{0,4},{1,5},{2,6},{3,7},{4,0},{5,1},{6,2},{7,3},{8,12},{9,13},{10,... | collective-permute-start | bytes 1769480 | tf_op jit(solution)/shard_map/ppermute | solution.py:263
  387.9 28.4 %collective-permute-start.51 = (bf16[192,1536]{1,0:T(8,128)(2,1)}, bf16[192,1536]{1,0:T(8,128)(2,1)}, u32[]{:S(2)}, u32[]{:S(2)}) collective-permute-start(bf16[192,1536]{1,0:T(8,128)(2,1)} %get-tuple-element.281), channel_id=1, source_target_pairs={{0,6},{1,7},{2,4},{3,5},{4,2},{5,3},{6,0},{7,1},{8,14},{9,15},{10,... | collective-permute-start | bytes 1769480 | tf_op jit(solution)/shard_map/ppermute | solution.py:263
  388.5 30.6 %collective-permute-start.44 = (bf16[192,2048]{1,0:T(8,128)(2,1)}, bf16[192,2048]{1,0:T(8,128)(2,1)S(1)}, u32[]{:S(2)}, u32[]{:S(2)}) collective-permute-start(bf16[192,2048]{1,0:T(8,128)(2,1)} %collective-permute-done.38.refs_2_), channel_id=1, source_target_pairs={{0,8},{8,16},{16,24},{1,9},{9,17},{17,25},{2,10},{10,18},{18,26},{... | collective-permute-start | bytes 2359304 | tf_op jit(solution)/shard_map/ppermute | solution.py:251
  391.1 28.0 %collective-permute-start.45 = (bf16[192,2048]{1,0:T(8,128)(2,1)}, bf16[192,2048]{1,0:T(8,128)(2,1)}, u32[]{:S(2)}, u32[]{:S(2)}) collective-permute-start(bf16[192,2048]{1,0:T(8,128)(2,1)} %collective-permute-done.39.refs_5_), channel_id=1, source_target_pairs={{8,0},{16,8},{24,16},{9,1},{17,9},{25,17},{10,2},{18,10},{26,18},{... | collective-permute-start | bytes 2359304 | tf_op jit(solution)/shard_map/ppermute | solution.py:252
  395.6 39.8 %all-to-all-start.3 = ((bf16[4,128,640]{1,2,0:T(8,128)(2,1)}), bf16[4,128,640]{1,2,0:T(8,128)(2,1)}, u32[]{:S(2)}, u32[]{:S(2)}) async-start(bf16[4,128,640]{1,2,0:T(8,128)(2,1)} %copy.104), calls=%async_computation.3 | async-start | bytes 1310720 | tf_op jit(solution)/shard_map/all_to_all | solution.py:907
  401.7 18.7 %collective-permute-start.41 = (bf16[192,768]{1,0:T(8,128)(2,1)S(1)}, bf16[192,768]{1,0:T(8,128)(2,1)S(1)}, u32[]{:S(2)}, u32[]{:S(2)}) collective-permute-start(bf16[192,768]{1,0:T(8,128)(2,1)S(1)} %get-tuple-element.269), channel_id=1, source_target_pairs={{0,2},{1,3},{2,0},{3,1},{4,6},{5,7},{6,4},{7,5},{8,10},{9,11},{10,... | collective-permute-start | bytes 884744 | tf_op jit(solution)/shard_map/ppermute | solution.py:263
  414.7 14.5 %collective-permute-start.42 = (bf16[192,768]{1,0:T(8,128)(2,1)S(1)}, bf16[192,768]{1,0:T(8,128)(2,1)S(1)}, u32[]{:S(2)}, u32[]{:S(2)}) collective-permute-start(bf16[192,768]{1,0:T(8,128)(2,1)S(1)} %get-tuple-element.270), channel_id=1, source_target_pairs={{0,4},{1,5},{2,6},{3,7},{4,0},{5,1},{6,2},{7,3},{8,12},{9,13},{10,... | collective-permute-start | bytes 884744 | tf_op jit(solution)/shard_map/ppermute | solution.py:263
  431.5 41.4 %collective-permute-start.46 = (bf16[192,768]{1,0:T(8,128)(2,1)S(1)}, bf16[192,768]{1,0:T(8,128)(2,1)S(1)}, u32[]{:S(2)}, u32[]{:S(2)}) collective-permute-start(bf16[192,768]{1,0:T(8,128)(2,1)S(1)} %select_convert_fusion.refs_0_), channel_id=1, source_target_pairs={{0,8},{8,16},{16,24},{24,0},{1,9},{9,17},{17,25},{25,1},{2,10},{10... | collective-permute-start | bytes 884744 | tf_op jit(solution)/shard_map/ppermute | solution.py:237
  431.5 57.0 %collective-permute-start.47 = (bf16[192,768]{1,0:T(8,128)(2,1)S(1)}, bf16[192,768]{1,0:T(8,128)(2,1)S(1)}, u32[]{:S(2)}, u32[]{:S(2)}) collective-permute-start(bf16[192,768]{1,0:T(8,128)(2,1)S(1)} %select_convert_fusion.refs_0_), channel_id=1, source_target_pairs={{0,16},{8,24},{16,0},{24,8},{1,17},{9,25},{17,1},{25,9},{2,18},{10... | collective-permute-start | bytes 884744 | tf_op jit(solution)/shard_map/ppermute | solution.py:237
  431.6 57.0 %collective-permute-start.48 = (bf16[192,768]{1,0:T(8,128)(2,1)S(1)}, bf16[192,768]{1,0:T(8,128)(2,1)S(1)}, u32[]{:S(2)}, u32[]{:S(2)}) collective-permute-start(bf16[192,768]{1,0:T(8,128)(2,1)S(1)} %select_convert_fusion.refs_0_), channel_id=1, source_target_pairs={{0,24},{8,0},{16,8},{24,16},{1,25},{9,1},{17,9},{25,17},{2,26},{10... | collective-permute-start | bytes 884744 | tf_op jit(solution)/shard_map/ppermute | solution.py:237
  435.3 36.2 %all-to-all-start.2 = ((bf16[192,4,384]{2,0,1:T(8,128)(2,1)}), bf16[192,4,384]{2,0,1:T(8,128)(2,1)}, u32[]{:S(2)}, u32[]{:S(2)}) async-start(bf16[192,4,384]{2,0,1:T(8,128)(2,1)} %bitcast.136), calls=%async_computation.2 | async-start | bytes 1179648 | tf_op jit(solution)/shard_map/all_to_all | solution.py:915
  472.7 15.8 %collective-permute-start.52 = (bf16[192,384]{1,0:T(8,128)(2,1)S(1)}, bf16[192,384]{1,0:T(8,128)(2,1)S(1)}, u32[]{:S(2)}, u32[]{:S(2)}) collective-permute-start(bf16[192,384]{1,0:T(8,128)(2,1)S(1)} %reduce_sum.208.refs_4_), channel_id=1, source_target_pairs={{0,8},{8,16},{16,24},{24,0},{1,9},{9,17},{17,25},{25,1},{2,10},{10... | collective-permute-start | bytes 442376 | tf_op jit(solution)/shard_map/ppermute | solution.py:237
  472.8 15.8 %collective-permute-start.53 = (bf16[192,384]{1,0:T(8,128)(2,1)S(1)}, bf16[192,384]{1,0:T(8,128)(2,1)S(1)}, u32[]{:S(2)}, u32[]{:S(2)}) collective-permute-start(bf16[192,384]{1,0:T(8,128)(2,1)S(1)} %reduce_sum.208.refs_4_), channel_id=1, source_target_pairs={{0,16},{8,24},{16,0},{24,8},{1,17},{9,25},{17,1},{25,9},{2,18},{10... | collective-permute-start | bytes 442376 | tf_op jit(solution)/shard_map/ppermute | solution.py:237
  472.9 15.7 %collective-permute-start.54 = (bf16[192,384]{1,0:T(8,128)(2,1)S(1)}, bf16[192,384]{1,0:T(8,128)(2,1)S(1)}, u32[]{:S(2)}, u32[]{:S(2)}) collective-permute-start(bf16[192,384]{1,0:T(8,128)(2,1)S(1)} %reduce_sum.208.refs_4_), channel_id=1, source_target_pairs={{0,24},{8,0},{16,8},{24,16},{1,25},{9,1},{17,9},{25,17},{2,26},{10... | collective-permute-start | bytes 442376 | tf_op jit(solution)/shard_map/ppermute | solution.py:237
  (100 other events, 816.4 us)
Sparse Core Ops, SparseCore 0:
  10.8 30.0 all-gather.6
  42.8 43.4 all-gather.8
  88.8 63.0 all-gather.10
  154.2 52.1 all-gather.12
  288.1 36.5 all-gather.14

commit v12 on v11

--- a/solution.py
+++ b/solution.py
@@ -226,7 +226,7 @@
         ],
         compiler_params=pltpu.CompilerParams(vmem_limit_bytes=28 * 1024 * 1024),
         cost_estimate=pl.CostEstimate(
-            flops=10**12,
+            flops=0 if g else 10**12,
             bytes_accessed=0,
             transcendentals=0,
         ),
@@ -616,9 +616,9 @@
 
 
 def place_kernel(count, q_cols, kv_cols, place_ref, *refs):
-    blocks, outs = refs[:count], refs[count : 2 * count]
+    blocks = refs[:count]
     w_query_ref, w_keyval_ref, gain_ref, query_ref, keyval_ref, out_ref, base_ref, sums_ref = refs[
-        2 * count :
+        count:
     ]
     gain = gain_ref[...]
     base = jnp.zeros_like(gain)
@@ -631,7 +631,7 @@
         keyval = blocks[s][:, q_cols : q_cols + kv_cols].astype(F32)
         start = q_cols + kv_cols
         sums = sums + blocks[s][:, start : start + LANES].astype(F32)
-        out_ref[:, q_at] = outs[s][...].astype(F32)
+        out_ref[:, q_at] = blocks[s][:, start + LANES :].astype(F32)
         base = base + jnp.sum(w_query_ref[:, q_at].astype(F32) * query, axis=1, keepdims=True)
         base = base + jnp.sum(w_keyval_ref[:, kv_at].astype(F32) * keyval, axis=1, keepdims=True)
         query_ref[:, q_at] = query * gain
@@ -640,7 +640,7 @@
     sums_ref[...] = sums
 
 
-def place_heads(blocks, outs, place, w_query, w_keyval, gain, q_cols, kv_cols):
+def place_heads(blocks, place, w_query, w_keyval, gain, q_cols, kv_cols):
     count = len(blocks)
     part = w_query.shape[0]
     start = q_cols + kv_cols
@@ -651,15 +651,14 @@
         in_vmem = pl.BlockSpec(memory_space=pltpu.VMEM)
         query, keyval, out, base, sums = pl.pallas_call(
             functools.partial(place_kernel, count, q_cols, kv_cols),
-            in_specs=[pl.BlockSpec(memory_space=pltpu.SMEM)] + [in_vmem] * (2 * count + 3),
+            in_specs=[pl.BlockSpec(memory_space=pltpu.SMEM)] + [in_vmem] * (count + 3),
             out_specs=[in_vmem] * 5,
             out_shape=[wide, narrow, wide, lanes, lanes],
             compiler_params=pltpu.CompilerParams(vmem_limit_bytes=24 * 1024 * 1024),
             cost_estimate=pl.CostEstimate(flops=0, bytes_accessed=0, transcendentals=0),
-        )(place.astype(jnp.int32).reshape(1), *blocks, *outs, w_query, w_keyval, gain)
+        )(place.astype(jnp.int32).reshape(1), *blocks, w_query, w_keyval, gain)
         return query, keyval, out, base[:, 0], sums
     blocks = from_relative(blocks, place).astype(F32)
-    outs = from_relative(outs, place).astype(F32)
 
     def columns(begin, end):
         return blocks[:, :, begin:end].transpose(1, 0, 2).reshape(part, count * (end - begin))
@@ -669,7 +668,7 @@
         w_keyval.astype(F32) * keyval, axis=1
     )
     sums = jnp.sum(blocks[:, :, start : start + LANES], axis=0)
-    out = outs.transpose(1, 0, 2).reshape(part, count * q_cols)
+    out = columns(start + LANES, start + LANES + q_cols)
     return query * gain, keyval * gain, out, base, sums
 
 
@@ -884,7 +883,7 @@
             head_queries, kv_all, bias, held, exact, lse, seqs, rows, g, groups
         )
         if g == 0:
-            grad_gate_up_blocks = after(grad_gate_up_blocks, grad_down, part_q)
+            grad_gate_up_blocks = after(grad_gate_up_blocks, part_q)
             grad_gate_up_shard = total_of(grad_gate_up_blocks).astype(BF)
             steps = [(grad_gate_up_shard, grad_gate_up_shard)]
             steps.append(relay_step(steps[0], seqs))
@@ -895,7 +894,7 @@
         held = after(head_grad, grad_gate_up_shard, out_there)
     steps[1] = after(steps[1], part_q)
     steps.append(relay_step(steps[1], seqs))
-    far = after(far, steps[1])
+    far = after(far, steps[1], grad_down)
     pairs = kv_pair_sums(near, [hop(each, shards, 1) for each in far])
     out_sums = pair_sums(out_near, after(out_there, pairs), shard)
     sent_grads, product_columns = head_columns(
@@ -915,9 +914,8 @@
     out_parts = lax.all_to_all(
         out_part.reshape(part, seqs, q_cols), "seq", split_axis=1, concat_axis=1, tiled=True
     )
-    out_own = by_rows(jnp.sum(out_parts.astype(F32), axis=1).astype(BF))
-    out_last = [by_rows(each) for each in send_out([out_own] * seqs, seqs)]
-    head_part = total_of(after(send_chips(head_sums, shards), steps[3]))
+    head_blocks = send_chips(head_sums, shards)
+    head_part = total_of(after(head_blocks, steps[3]))
     grad_normed = dot_nt(after(token_grads, head_part), attn_full)
     grad_tokens = grad_residual + root_back(inputs, root(inputs), grad_normed)
     base_cols = head_cols + experts
@@ -930,12 +928,13 @@
         plane_high.astype(F32),
         jnp.where(lanes == base_cols + 1, plane_low.astype(F32), head_part),
     )
-    head_part = by_rows(head_part.astype(BF))
+    out_own = jnp.sum(out_parts.astype(F32), axis=1)
+    head_part = by_rows(jnp.concatenate([head_part, out_own], axis=1).astype(BF))
     head_last = [by_rows(each) for each in send_out([head_part] * seqs, seqs)]
     grad_gate_up, grad_gain_ffn = place_gate_up(after(steps, head_part), w_gate_up, gain_two, z)
-    head_last, out_last = after((head_last, out_last), grad_gate_up)
+    head_last = after(head_last, grad_gate_up)
     grad_query, grad_keyval, grad_out, grad_gain_attn, sums = place_heads(
-        head_last, out_last, z, w_query, w_keyval, gain_one, q_cols, kv_cols
+        head_last, z, w_query, w_keyval, gain_one, q_cols, kv_cols
     )
     loss_value = jnp.sum(sums[0, experts : experts + 2]) / (width * valid_count)
     grad_router_base = sums[:, :experts]

time: 512 us -> 504 us (0.984)
  the two profiles are of different devices: /device:TPU:0 before, /device:TPU:12 now
where the time goes in v12:
time: 504 us; the launch traced here: 496 us
  waiting for transfers between devices  187 us (37%)
  Pallas kernels  99.7 us (20%)
  starting transfers between devices  96.9 us (19%)
  local copies, waits for them, and re-layouts  41.8 us (8%)
  other arithmetic  27.9 us (6%)
  matrix products  21.6 us (4%)
  between operations  21 us (4%)
    ppermute x18, waiting for transfers between devices, shift(): lax.ppermute(block, 'seq', [(i, (i + step) % count) for i in range(count)])  125 us
    ppermute x28, waiting for transfers between devices, hop(): return lax.ppermute(block, 'fsdp', [(i, i ^ mask) for i in range(count)])  46.4 us
    unnamed x214, local copies, waits for them, and re-layouts  30.6 us
    ppermute x18, starting transfers between devices, shift(): lax.ppermute(block, 'seq', [(i, (i + step) % count) for i in range(count)])  29.1 us
    pallas_call x2, Pallas kernels, flash_backward(): pl.pallas_call(functools.partial(backward_kernel, shards, seqs, rows, g,...  27.6 us
    ppermute x28, starting transfers between devices, hop(): return lax.ppermute(block, 'fsdp', [(i, i ^ mask) for i in range(count)])  24.8 us
    pallas_call x1, Pallas kernels, flash_forward(): pl.pallas_call(functools.partial(forward_kernel, shards, seqs, rows, loca...  19 us
    pallas_call x4, Pallas kernels, split_product(): pl.pallas_call(product_kernel, grid=(count // 2,), in_specs=[pl.BlockSpec...  14 us
  transfers between devices with their start and end apart: 61, of which 30 were waited for; matrix products, arithmetic and copies ran while one was open for 11% of the time, Pallas kernels for 17%

profile of v12, /device:TPU:12, one launch (start us, length us, event | category | flops | bytes accessed | tf_op | source)
XLA Modules:
  0.0 495.6 jit_solution(986473521139569198)
XLA Ops:
  21.3 23.3 %collective-permute-done = bf16[136,1536]{1,0:T(8,128)(2,1)S(1)} collective-permute-done((bf16[136,1536]{1,0:T(8,128)(2,1)S(1)}, bf16[136,1536]{1,0:T(8,128)(2,1)S(1)}, u32[]{:S(2)}, u32[]{:S(2)}) %collective-permute-start) | collective-permute-done | bytes 417824 | tf_op jit(solution)/shard_map/ppermute | solution.py:237
  44.7 7.8 %collective-permute-done.1 = bf16[136,1536]{1,0:T(8,128)(2,1)S(1)} collective-permute-done((bf16[136,1536]{1,0:T(8,128)(2,1)S(1)}, bf16[136,1536]{1,0:T(8,128)(2,1)S(1)}, u32[]{:S(2)}, u32[]{:S(2)}) %collective-permute-start.1) | collective-permute-done | bytes 417824 | tf_op jit(solution)/shard_map/ppermute | solution.py:237
  62.8 7.3 %collective-permute-done.3.refs_1_ = bf16[528,256]{1,0:T(8,128)(2,1)S(1)} collective-permute-done((bf16[528,256]{1,0:T(8,128)(2,1)S(1)}, bf16[528,256]{1,0:T(8,128)(2,1)S(1)}, u32[]{:S(2)}, u32[]{:S(2)}) %collective-permute-start.3) | collective-permute-done | bytes 270368 | tf_op jit(solution)/shard_map/ppermute | solution.py:263
  70.1 7.5 %collective-permute-done.4.refs_2_ = bf16[528,256]{1,0:T(8,128)(2,1)S(1)} collective-permute-done((bf16[528,256]{1,0:T(8,128)(2,1)S(1)}, bf16[528,256]{1,0:T(8,128)(2,1)S(1)}, u32[]{:S(2)}, u32[]{:S(2)}) %collective-permute-start.4) | collective-permute-done | bytes 270368 | tf_op jit(solution)/shard_map/ppermute | solution.py:263
  77.6 3.2 collective-permute-done.5.refs_3_
  83.1 19.0 %shard_map.221 = (bf16[512,384]{1,0:T(8,128)(2,1)}, f32[512,384]{1,0:T(8,128)S(1)}, f32[512,384]{1,0:T(8,128)S(1)}) custom-call(bf16[528,256]{1,0:T(8,128)(2,1)S(1)} %maximum_maximum_fusion.1.refs_0_, bf16[528,256]{1,0:T(8,128)(2,1)S(1)} %collective-permute-done.3.refs_1_, bf16[528,256]{1,0:T(8,128)(2,1)S(1)} %collective-permute-done.4.refs_2_, ...), custom_call_target="tpu_custom_call" | custom-call | tf_op jit(solution)/shard_map/pallas_call | solution.py:114
  103.9 3.4 all-to-all-start
  108.2 8.8 %all-to-all-done = bf16[4,128,384]{2,1,0:T(8,128)(2,1)S(1)} async-done(((bf16[4,128,384]{2,1,0:T(8,128)(2,1)}), bf16[4,128,384]{2,1,0:T(8,128)(2,1)S(1)}, u32[]{:S(2)}, u32[]{:S(2)}) %all-to-all-start) | async-done | bytes 393248 | tf_op jit(solution)/shard_map/all_to_all | solution.py:795
  118.8 5.2 %multiply_reduce_fusion.5 = (f32[128]{0:T(128)S(1)}, f32[128,1536]{1,0:T(8,128)S(1)}) fusion(bf16[128,1536]{1,0:T(8,128)(2,1)S(1)} %bitcast.138, bf16[1536,1536]{0,1:T(8,128)(2,1)} %all-gather.9.cloned.1.call-done, bf16[128,1536]{1,0:T(8,128)(2,1)} %param.14), kind=kOutput, calls=%fused_computation.69 | convolution fusion | flops 604766080 | bytes 6291968 | tf_op jit(solution)/shard_map/dot_general | solution.py:24
  126.3 4.1 collective-permute-start.11
  133.7 2.6 collective-permute-done.10.refs_1_
  136.3 15.2 %collective-permute-done.11.refs_2_ = bf16[96,1536]{1,0:T(8,128)(2,1)} collective-permute-done((bf16[96,1536]{1,0:T(8,128)(2,1)S(1)}, bf16[96,1536]{1,0:T(8,128)(2,1)}, u32[]{:S(2)}, u32[]{:S(2)}) %collective-permute-start.11) | collective-permute-done | bytes 294944 | tf_op jit(solution)/shard_map/ppermute | solution.py:237
  151.5 5.0 %collective-permute-done.12.refs_3_ = bf16[96,1536]{1,0:T(8,128)(2,1)} collective-permute-done((bf16[96,1536]{1,0:T(8,128)(2,1)S(1)}, bf16[96,1536]{1,0:T(8,128)(2,1)}, u32[]{:S(2)}, u32[]{:S(2)}) %collective-permute-start.12) | collective-permute-done | bytes 294944 | tf_op jit(solution)/shard_map/ppermute | solution.py:237
  156.5 8.8 %shard_map.222 = (bf16[384,1536]{1,0:T(8,128)(2,1)}, f32[384,2048]{1,0:T(8,128)}, bf16[384,1024]{1,0:T(8,128)(2,1)}, bf16[96,1536]{1,0:T(8,128)(2,1)}, bf16[96,1...) custom-call(bf16[96,1536]{1,0:T(8,128)(2,1)} %get-tuple-element.369.refs_0_, ...), custom_call_target="tpu_custom_call" | custom-call | tf_op jit(solution)/shard_map/pallas_call | solution.py:396
  168.7 19.4 %collective-permute-done.13 = bf16[96,1536]{1,0:T(8,128)(2,1)S(1)} collective-permute-done((bf16[96,1536]{1,0:T(8,128)(2,1)}, bf16[96,1536]{1,0:T(8,128)(2,1)S(1)}, u32[]{:S(2)}, u32[]{:S(2)}) %collective-permute-start.13) | collective-permute-done | bytes 294944 | tf_op jit(solution)/shard_map/ppermute | solution.py:237
  194.1 3.9 collective-permute-start.16
  198.0 4.2 collective-permute-start.17
  204.4 3.3 collective-permute-done.16.refs_1_
  207.7 14.7 %collective-permute-done.17.refs_2_ = bf16[96,1536]{1,0:T(8,128)(2,1)S(1)} collective-permute-done((bf16[96,1536]{1,0:T(8,128)(2,1)S(1)}, bf16[96,1536]{1,0:T(8,128)(2,1)S(1)}, u32[]{:S(2)}, u32[]{:S(2)}) %collective-permute-start.17) | collective-permute-done | bytes 294944 | tf_op jit(solution)/shard_map/ppermute | solution.py:237
  222.5 3.8 collective-permute-done.18.refs_3_
  227.0 10.0 %shard_map.223 = (bf16[384,1536]{1,0:T(8,128)(2,1)}, bf16[384,2048]{1,0:T(8,128)(2,1)}, bf16[96,1536]{1,0:T(8,128)(2,1)}, bf16[96,1536]{1,0:T(8,128)(2,1)}, bf16...) custom-call(bf16[96,1536]{1,0:T(8,128)(2,1)} %get-tuple-element.184.refs_0_, bf16[96,1536]{1,0:T(8,128)(2,1)} %copy-done.73, ...), custom_call_target="tpu_custom_call" | custom-call | tf_op jit(solution)/shard_map/pallas_call | solution.py:445
  241.1 2.9 shard_map.224
  245.9 4.8 shard_map.226
  254.2 2.6 collective-permute-start.24
  256.8 2.9 collective-permute-done.19
  270.7 7.9 %all-to-all-start.1 = ((bf16[128,4,384]{2,0,1:T(8,128)(2,1)}), bf16[128,4,384]{2,0,1:T(8,128)(2,1)}, u32[]{:S(2)}, u32[]{:S(2)}) async-start(bf16[128,4,384]{2,0,1:T(8,128)(2,1)} %bitcast.147), calls=%async_computation.1 | async-start | bytes 786432 | tf_op jit(solution)/shard_map/all_to_all | solution.py:871
  292.8 13.8 %shard_map.228 = (f32[512,192]{1,0:T(8,128)S(1)}, bf16[4,512,128]{2,1,0:T(8,128)(2,1)S(1)}, bf16[4,512,128]{2,1,0:T(8,128)(2,1)S(1)}) custom-call(bf16[8,528,256]{2,1,0:T(8,128)(2,1)S(1)} %copy-done.8, bf16[512,384]{1,0:T(8,128)(2,1)S(1)} %slice_multiply_fusion.refs_8_.refs_1_, f32[8,1,1024]{2,1,0:T(1,128)S(1)} %pad_maximum_fusion.4.refs_9_.refs_2_, ...), custom_call_target="tpu_custom_call" | custom-call | flops 999999995904 | tf_op jit(solution)/shard_map/pallas_call | solution.py:212
  306.7 5.9 %collective-permute-done.28 = bf16[192,2048]{1,0:T(8,128)(2,1)} collective-permute-done((bf16[192,2048]{1,0:T(8,128)(2,1)}, bf16[192,2048]{1,0:T(8,128)(2,1)}, u32[]{:S(2)}, u32[]{:S(2)}) %collective-permute-start.28) | collective-permute-done | bytes 786464 | tf_op jit(solution)/shard_map/ppermute | solution.py:263
  316.5 3.4 collective-permute-start.31
  319.9 3.6 collective-permute-start.32
  323.5 13.8 %shard_map.230 = (f32[512,192]{1,0:T(8,128)S(1)}, bf16[4,512,128]{2,1,0:T(8,128)(2,1)S(1)}, bf16[4,512,128]{2,1,0:T(8,128)(2,1)S(1)}) custom-call(bf16[8,528,256]{2,1,0:T(8,128)(2,1)S(1)} %copy-done.8, bf16[512,384]{1,0:T(8,128)(2,1)S(1)} %slice_multiply_fusion.refs_8_.refs_1_, f32[8,1,1024]{2,1,0:T(1,128)S(1)} %pad_maximum_fusion.4.refs_9_.refs_2_, ...), custom_call_target="tpu_custom_call" | custom-call | tf_op jit(solution)/shard_map/pallas_call | solution.py:212
  339.7 2.6 collective-permute-done.31.refs_1_
  343.9 3.2 collective-permute-start.38
  347.1 3.5 collective-permute-start.39
  359.9 4.1 shard_map.232
  364.1 5.2 %collective-permute-done.36.refs_4_ = bf16[512,256]{1,0:T(8,128)(2,1)} collective-permute-done((bf16[512,256]{1,0:T(8,128)(2,1)}, bf16[512,256]{1,0:T(8,128)(2,1)}, u32[]{:S(2)}, u32[]{:S(2)}) %collective-permute-start.36) | collective-permute-done | bytes 262176 | tf_op jit(solution)/shard_map/ppermute | solution.py:263
  371.7 3.7 shard_map.234
  383.4 3.6 collective-permute-start.45
  389.2 4.9 all-to-all-start.3
  397.7 8.1 %collective-permute-done.47 = bf16[192,1536]{1,0:T(8,128)(2,1)} collective-permute-done((bf16[192,1536]{1,0:T(8,128)(2,1)}, bf16[192,1536]{1,0:T(8,128)(2,1)}, u32[]{:S(2)}, u32[]{:S(2)}) %collective-permute-start.47) | collective-permute-done | bytes 589856 | tf_op jit(solution)/shard_map/ppermute | solution.py:263
  405.7 3.1 collective-permute-start.43
  412.0 6.8 %collective-permute-done.42 = bf16[192,768]{1,0:T(8,128)(2,1)S(1)} collective-permute-done((bf16[192,768]{1,0:T(8,128)(2,1)S(1)}, bf16[192,768]{1,0:T(8,128)(2,1)S(1)}, u32[]{:S(2)}, u32[]{:S(2)}) %collective-permute-start.42) | collective-permute-done | bytes 294944 | tf_op jit(solution)/shard_map/ppermute | solution.py:263
  418.9 7.0 %all-to-all-start.2 = ((bf16[192,4,384]{2,0,1:T(8,128)(2,1)}), bf16[192,4,384]{2,0,1:T(8,128)(2,1)}, u32[]{:S(2)}, u32[]{:S(2)}) async-start(bf16[192,4,384]{2,0,1:T(8,128)(2,1)} %bitcast.136), calls=%async_computation.2 | async-start | bytes 1179648 | tf_op jit(solution)/shard_map/all_to_all | solution.py:914
  426.0 6.3 %fusion.27 = (f32[128]{0:T(128)S(1)}, f32[128]{0:T(128)S(1)}, f32[128,1536]{1,0:T(8,128)S(1)}) fusion(bf16[128,1536]{1,0:T(8,128)(2,1)S(1)} %copy-done.57, bf16[128,2560]{0,1:T(8,128)(2,1)} %bitcast.55, bf16[1536,2560]{1,0:T(8,128)(2,1)} %all-gather.13.cloned.1.call-done), kind=kOutput, calls=%fused_computation.47 | convolution fusion | flops 1007615744 | bytes 9700352 | tf_op jit(solution)/shard_map/dot_general | solution.py:28
  441.0 4.3 collective-permute-start.50
  447.6 8.0 %shard_map.236 = (f32[4,192,2048]{2,1,0:T(8,128)}, f32[192,128]{1,0:T(8,128)S(1)}) custom-call(s32[1]{0:T(128)} %bitcast.33.place_ref, bf16[192,2048]{1,0:T(8,128)(2,1)S(1)} %copy-done.4, bf16[192,2048]{1,0:T(8,128)(2,1)} %collective-permute-done.31.refs_1_, bf16[192,2048]{1,0:T(8,128)(2,1)} %collective-permute-done.38.refs_2_, ...), custom_call_target="tpu_custom_call" | custom-call | tf_op jit(solution)/shard_map/pallas_call | solution.py:583
  457.9 20.2 %collective-permute-done.50.refs_2_ = bf16[192,1152]{1,0:T(8,128)(2,1)S(1)} collective-permute-done((bf16[192,1152]{1,0:T(8,128)(2,1)S(1)}, bf16[192,1152]{1,0:T(8,128)(2,1)S(1)}, u32[]{:S(2)}, u32[]{:S(2)}) %collective-permute-start.50) | collective-permute-done | bytes 442400 | tf_op jit(solution)/shard_map/ppermute | solution.py:237
  478.1 4.0 collective-permute-done.51.refs_3_
  (433 shorter events, 133.9 us)
Async XLA Ops:
  7.2 47.7 %all-gather.7.cloned.1.call-start = ((), (), s32[]{:S(2)}) async-start(), calls=%async_computation.4 | async-start | bytes 2211840 | tf_op jit(solution)/shard_map/all_gather | solution.py:719
  10.7 108.1 %all-gather.9.cloned.1.call-start = ((), (), s32[]{:S(2)}) async-start(), calls=%async_computation.5 | async-start | bytes 5308416 | tf_op jit(solution)/shard_map/all_gather | solution.py:746
  11.5 145.0 %all-gather.11.cloned.1.call-start = ((), (), s32[]{:S(2)}) async-start(), calls=%async_computation.6 | async-start | bytes 11059200 | tf_op jit(solution)/shard_map/all_gather | solution.py:761
  15.1 189.4 %all-gather.13.cloned.1.call-start = ((), (), s32[]{:S(2)}) async-start(), calls=%async_computation.7 | async-start | bytes 8847360 | tf_op jit(solution)/shard_map/all_gather | solution.py:774
  15.1 29.6 %collective-permute-start = (bf16[136,1536]{1,0:T(8,128)(2,1)S(1)}, bf16[136,1536]{1,0:T(8,128)(2,1)S(1)}, u32[]{:S(2)}, u32[]{:S(2)}) collective-permute-start(bf16[136,1536]{1,0:T(8,128)(2,1)S(1)} %fusion.36), channel_id=1, source_target_pairs={{0,8},{8,16},{16,24},{24,0},{1,9},{9,17},{17,25},{25,1},{2,10},{10... | collective-permute-start | bytes 1253384 | tf_op jit(solution)/shard_map/ppermute | solution.py:237
  16.7 35.8 %collective-permute-start.1 = (bf16[136,1536]{1,0:T(8,128)(2,1)S(1)}, bf16[136,1536]{1,0:T(8,128)(2,1)S(1)}, u32[]{:S(2)}, u32[]{:S(2)}) collective-permute-start(bf16[136,1536]{1,0:T(8,128)(2,1)S(1)} %fusion.36), channel_id=1, source_target_pairs={{0,16},{8,24},{16,0},{24,8},{1,17},{9,25},{17,1},{25,9},{2,18},{10... | collective-permute-start | bytes 1253384 | tf_op jit(solution)/shard_map/ppermute | solution.py:237
  18.0 36.3 %collective-permute-start.2 = (bf16[136,1536]{1,0:T(8,128)(2,1)S(1)}, bf16[136,1536]{1,0:T(8,128)(2,1)S(1)}, u32[]{:S(2)}, u32[]{:S(2)}) collective-permute-start(bf16[136,1536]{1,0:T(8,128)(2,1)S(1)} %fusion.36), channel_id=1, source_target_pairs={{0,24},{8,0},{16,8},{24,16},{1,25},{9,1},{17,9},{25,17},{2,26},{10... | collective-permute-start | bytes 1253384 | tf_op jit(solution)/shard_map/ppermute | solution.py:237
  60.6 16.9 %collective-permute-start.4 = (bf16[528,256]{1,0:T(8,128)(2,1)S(1)}, bf16[528,256]{1,0:T(8,128)(2,1)S(1)}, u32[]{:S(2)}, u32[]{:S(2)}) collective-permute-start(bf16[528,256]{1,0:T(8,128)(2,1)S(1)} %maximum_maximum_fusion.1.refs_0_), channel_id=1, source_target_pairs={{0,4},{1,5},{2,6},{3,7},{4,0},{5,1},{6,2},{7,3},{8,12},{9,13},{10,... | collective-permute-start | bytes 811016 | tf_op jit(solution)/shard_map/ppermute | solution.py:263
  61.2 19.7 %collective-permute-start.5 = (bf16[528,256]{1,0:T(8,128)(2,1)S(1)}, bf16[528,256]{1,0:T(8,128)(2,1)S(1)}, u32[]{:S(2)}, u32[]{:S(2)}) collective-permute-start(bf16[528,256]{1,0:T(8,128)(2,1)S(1)} %maximum_maximum_fusion.1.refs_0_), channel_id=1, source_target_pairs={{0,6},{1,7},{2,4},{3,5},{4,2},{5,3},{6,0},{7,1},{8,14},{9,15},{10,... | collective-permute-start | bytes 811016 | tf_op jit(solution)/shard_map/ppermute | solution.py:263
  62.7 19.4 %collective-permute-start.6 = (bf16[528,256]{1,0:T(8,128)(2,1)S(1)}, bf16[528,256]{1,0:T(8,128)(2,1)S(1)}, u32[]{:S(2)}, u32[]{:S(2)}) collective-permute-start(bf16[528,256]{1,0:T(8,128)(2,1)S(1)} %maximum_maximum_fusion.1.refs_0_), channel_id=1, source_target_pairs={{0,1},{1,0},{2,3},{3,2},{4,5},{5,4},{6,7},{7,6},{8,9},{9,8},{10,11... | collective-permute-start | bytes 811016 | tf_op jit(solution)/shard_map/ppermute | solution.py:263
  103.9 13.1 %all-to-all-start = ((bf16[4,128,384]{2,1,0:T(8,128)(2,1)}), bf16[4,128,384]{2,1,0:T(8,128)(2,1)S(1)}, u32[]{:S(2)}, u32[]{:S(2)}) async-start(bf16[4,128,384]{2,1,0:T(8,128)(2,1)} %bitcast.12), calls=%async_computation | async-start | bytes 786432 | tf_op jit(solution)/shard_map/all_to_all | solution.py:795
  126.3 25.1 %collective-permute-start.11 = (bf16[96,1536]{1,0:T(8,128)(2,1)S(1)}, bf16[96,1536]{1,0:T(8,128)(2,1)}, u32[]{:S(2)}, u32[]{:S(2)}) collective-permute-start(bf16[96,1536]{1,0:T(8,128)(2,1)S(1)} %get-tuple-element.367), channel_id=1, source_target_pairs={{0,16},{8,24},{16,0},{24,8},{1,17},{9,25},{17,1},{25,9},{2,18},{10... | collective-permute-start | bytes 884744 | tf_op jit(solution)/shard_map/ppermute | solution.py:237
  130.4 26.1 %collective-permute-start.12 = (bf16[96,1536]{1,0:T(8,128)(2,1)S(1)}, bf16[96,1536]{1,0:T(8,128)(2,1)}, u32[]{:S(2)}, u32[]{:S(2)}) collective-permute-start(bf16[96,1536]{1,0:T(8,128)(2,1)S(1)} %get-tuple-element.366), channel_id=1, source_target_pairs={{0,24},{8,0},{16,8},{24,16},{1,25},{9,1},{17,9},{25,17},{2,26},{10... | collective-permute-start | bytes 884744 | tf_op jit(solution)/shard_map/ppermute | solution.py:237
  165.3 22.8 %collective-permute-start.13 = (bf16[96,1536]{1,0:T(8,128)(2,1)}, bf16[96,1536]{1,0:T(8,128)(2,1)S(1)}, u32[]{:S(2)}, u32[]{:S(2)}) collective-permute-start(bf16[96,1536]{1,0:T(8,128)(2,1)} %get-tuple-element.167), channel_id=1, source_target_pairs={{0,24},{8,0},{16,8},{24,16},{1,25},{9,1},{17,9},{25,17},{2,26},{10... | collective-permute-start | bytes 884744 | tf_op jit(solution)/shard_map/ppermute | solution.py:237
  165.4 22.7 %collective-permute-start.14 = (bf16[96,1536]{1,0:T(8,128)(2,1)}, bf16[96,1536]{1,0:T(8,128)(2,1)S(1)}, u32[]{:S(2)}, u32[]{:S(2)}) collective-permute-start(bf16[96,1536]{1,0:T(8,128)(2,1)} %get-tuple-element.168), channel_id=1, source_target_pairs={{0,16},{8,24},{16,0},{24,8},{1,17},{9,25},{17,1},{25,9},{2,18},{10... | collective-permute-start | bytes 884744 | tf_op jit(solution)/shard_map/ppermute | solution.py:237
  166.1 23.0 %collective-permute-start.15 = (bf16[96,1536]{1,0:T(8,128)(2,1)}, bf16[96,1536]{1,0:T(8,128)(2,1)S(1)}, u32[]{:S(2)}, u32[]{:S(2)}) collective-permute-start(bf16[96,1536]{1,0:T(8,128)(2,1)} %get-tuple-element.169), channel_id=1, source_target_pairs={{0,8},{8,16},{16,24},{24,0},{1,9},{9,17},{17,25},{25,1},{2,10},{10... | collective-permute-start | bytes 884744 | tf_op jit(solution)/shard_map/ppermute | solution.py:237
  194.1 13.6 %collective-permute-start.16 = (bf16[96,1536]{1,0:T(8,128)(2,1)S(1)}, bf16[96,1536]{1,0:T(8,128)(2,1)S(1)}, u32[]{:S(2)}, u32[]{:S(2)}) collective-permute-start(bf16[96,1536]{1,0:T(8,128)(2,1)S(1)} %get-tuple-element.364), channel_id=1, source_target_pairs={{0,8},{8,16},{16,24},{24,0},{1,9},{9,17},{17,25},{25,1},{2,10},{10... | collective-permute-start | bytes 884744 | tf_op jit(solution)/shard_map/ppermute | solution.py:237
  198.0 24.5 %collective-permute-start.17 = (bf16[96,1536]{1,0:T(8,128)(2,1)S(1)}, bf16[96,1536]{1,0:T(8,128)(2,1)S(1)}, u32[]{:S(2)}, u32[]{:S(2)}) collective-permute-start(bf16[96,1536]{1,0:T(8,128)(2,1)S(1)} %get-tuple-element.363), channel_id=1, source_target_pairs={{0,16},{8,24},{16,0},{24,8},{1,17},{9,25},{17,1},{25,9},{2,18},{10... | collective-permute-start | bytes 884744 | tf_op jit(solution)/shard_map/ppermute | solution.py:237
  202.2 24.1 %collective-permute-start.18 = (bf16[96,1536]{1,0:T(8,128)(2,1)S(1)}, bf16[96,1536]{1,0:T(8,128)(2,1)S(1)}, u32[]{:S(2)}, u32[]{:S(2)}) collective-permute-start(bf16[96,1536]{1,0:T(8,128)(2,1)S(1)} %get-tuple-element.362), channel_id=1, source_target_pairs={{0,24},{8,0},{16,8},{24,16},{1,25},{9,1},{17,9},{25,17},{2,26},{10... | collective-permute-start | bytes 884744 | tf_op jit(solution)/shard_map/ppermute | solution.py:237
  236.9 22.8 %collective-permute-start.19 = (bf16[96,1536]{1,0:T(8,128)(2,1)}, bf16[96,1536]{1,0:T(8,128)(2,1)S(1)}, u32[]{:S(2)}, u32[]{:S(2)}) collective-permute-start(bf16[96,1536]{1,0:T(8,128)(2,1)} %get-tuple-element.190), channel_id=1, source_target_pairs={{0,24},{8,0},{16,8},{24,16},{1,25},{9,1},{17,9},{25,17},{2,26},{10... | collective-permute-start | bytes 884744 | tf_op jit(solution)/shard_map/ppermute | solution.py:237
  237.0 23.2 %collective-permute-start.20 = (bf16[96,1536]{1,0:T(8,128)(2,1)}, bf16[96,1536]{1,0:T(8,128)(2,1)S(1)}, u32[]{:S(2)}, u32[]{:S(2)}) collective-permute-start(bf16[96,1536]{1,0:T(8,128)(2,1)} %get-tuple-element.191), channel_id=1, source_target_pairs={{0,16},{8,24},{16,0},{24,8},{1,17},{9,25},{17,1},{25,9},{2,18},{10... | collective-permute-start | bytes 884744 | tf_op jit(solution)/shard_map/ppermute | solution.py:237
  238.0 24.7 %collective-permute-start.21 = (bf16[96,1536]{1,0:T(8,128)(2,1)}, bf16[96,1536]{1,0:T(8,128)(2,1)S(1)}, u32[]{:S(2)}, u32[]{:S(2)}) collective-permute-start(bf16[96,1536]{1,0:T(8,128)(2,1)} %get-tuple-element.192), channel_id=1, source_target_pairs={{0,8},{8,16},{16,24},{24,0},{1,9},{9,17},{17,25},{25,1},{2,10},{10... | collective-permute-start | bytes 884744 | tf_op jit(solution)/shard_map/ppermute | solution.py:237
  250.7 15.8 %collective-permute-start.23 = (bf16[4,192,2048]{2,1,0:T(8,128)(2,1)S(1)}, bf16[4,192,2048]{2,1,0:T(8,128)(2,1)S(1)}, u32[]{:S(2)}, u32[]{:S(2)}) collective-permute-start(bf16[4,192,2048]{2,1,0:T(8,128)(2,1)S(1)} %get-tuple-element.216), channel_id=1, source_target_pairs={{0,1},{1,0},{2,3},{3,2},{4,5},{5,4},{6,7},{7,6},{8,9},{9,8},{10,11... | collective-permute-start | bytes 9437192 | tf_op jit(solution)/shard_map/ppermute | solution.py:263
  254.2 32.3 %collective-permute-start.24 = (bf16[192,1024]{1,0:T(8,128)(2,1)}, bf16[192,1024]{1,0:T(8,128)(2,1)}, u32[]{:S(2)}, u32[]{:S(2)}) collective-permute-start(bf16[192,1024]{1,0:T(8,128)(2,1)} %get-tuple-element.204), channel_id=1, source_target_pairs={{0,2},{1,3},{2,0},{3,1},{4,6},{5,7},{6,4},{7,5},{8,10},{9,11},{10,... | collective-permute-start | bytes 1179656 | tf_op jit(solution)/shard_map/ppermute | solution.py:263
  259.8 27.7 %collective-permute-start.25 = (bf16[192,1024]{1,0:T(8,128)(2,1)}, bf16[192,1024]{1,0:T(8,128)(2,1)}, u32[]{:S(2)}, u32[]{:S(2)}) collective-permute-start(bf16[192,1024]{1,0:T(8,128)(2,1)} %get-tuple-element.205), channel_id=1, source_target_pairs={{0,4},{1,5},{2,6},{3,7},{4,0},{5,1},{6,2},{7,3},{8,12},{9,13},{10,... | collective-permute-start | bytes 1179656 | tf_op jit(solution)/shard_map/ppermute | solution.py:263
  260.2 27.3 %collective-permute-start.26 = (bf16[192,1024]{1,0:T(8,128)(2,1)}, bf16[192,1024]{1,0:T(8,128)(2,1)}, u32[]{:S(2)}, u32[]{:S(2)}) collective-permute-start(bf16[192,1024]{1,0:T(8,128)(2,1)} %get-tuple-element.206), channel_id=1, source_target_pairs={{0,6},{1,7},{2,4},{3,5},{4,2},{5,3},{6,0},{7,1},{8,14},{9,15},{10,... | collective-permute-start | bytes 1179656 | tf_op jit(solution)/shard_map/ppermute | solution.py:263
  270.7 19.2 %all-to-all-start.1 = ((bf16[128,4,384]{2,0,1:T(8,128)(2,1)}), bf16[128,4,384]{2,0,1:T(8,128)(2,1)}, u32[]{:S(2)}, u32[]{:S(2)}) async-start(bf16[128,4,384]{2,0,1:T(8,128)(2,1)} %bitcast.147), calls=%async_computation.1 | async-start | bytes 786432 | tf_op jit(solution)/shard_map/all_to_all | solution.py:871
  278.6 64.8 %all-gather.15.cloned.1.call-start = ((), (), s32[]{:S(2)}) async-start(), calls=%async_computation.8 | async-start | bytes 1966080 | tf_op jit(solution)/shard_map/all_gather | solution.py:874
  278.6 28.1 %collective-permute-start.27 = (bf16[192,2048]{1,0:T(8,128)(2,1)}, bf16[192,2048]{1,0:T(8,128)(2,1)}, u32[]{:S(2)}, u32[]{:S(2)}) collective-permute-start(bf16[192,2048]{1,0:T(8,128)(2,1)} %copy-done.45), channel_id=1, source_target_pairs={{0,2},{1,3},{2,0},{3,1},{4,6},{5,7},{6,4},{7,5},{8,10},{9,11},{10,... | collective-permute-start | bytes 2359304 | tf_op jit(solution)/shard_map/ppermute | solution.py:263
  279.6 33.0 %collective-permute-start.28 = (bf16[192,2048]{1,0:T(8,128)(2,1)}, bf16[192,2048]{1,0:T(8,128)(2,1)}, u32[]{:S(2)}, u32[]{:S(2)}) collective-permute-start(bf16[192,2048]{1,0:T(8,128)(2,1)} %copy-done.44), channel_id=1, source_target_pairs={{0,4},{1,5},{2,6},{3,7},{4,0},{5,1},{6,2},{7,3},{8,12},{9,13},{10,... | collective-permute-start | bytes 2359304 | tf_op jit(solution)/shard_map/ppermute | solution.py:263
  286.6 27.7 %collective-permute-start.29 = (bf16[192,2048]{1,0:T(8,128)(2,1)}, bf16[192,2048]{1,0:T(8,128)(2,1)}, u32[]{:S(2)}, u32[]{:S(2)}) collective-permute-start(bf16[192,2048]{1,0:T(8,128)(2,1)} %copy-done.43), channel_id=1, source_target_pairs={{0,6},{1,7},{2,4},{3,5},{4,2},{5,3},{6,0},{7,1},{8,14},{9,15},{10,... | collective-permute-start | bytes 2359304 | tf_op jit(solution)/shard_map/ppermute | solution.py:263
  290.0 33.5 %collective-permute-start.30 = (bf16[4,192,1536]{2,1,0:T(8,128)(2,1)}, bf16[4,192,1536]{2,1,0:T(8,128)(2,1)}, u32[]{:S(2)}, u32[]{:S(2)}) collective-permute-start(bf16[4,192,1536]{2,1,0:T(8,128)(2,1)} %copy-done.42), channel_id=1, source_target_pairs={{0,1},{1,0},{2,3},{3,2},{4,5},{5,4},{6,7},{7,6},{8,9},{9,8},{10,11... | collective-permute-start | bytes 7077896 | tf_op jit(solution)/shard_map/ppermute | solution.py:263
  316.5 25.8 %collective-permute-start.31 = (bf16[192,2048]{1,0:T(8,128)(2,1)S(1)}, bf16[192,2048]{1,0:T(8,128)(2,1)}, u32[]{:S(2)}, u32[]{:S(2)}) collective-permute-start(bf16[192,2048]{1,0:T(8,128)(2,1)S(1)} %add_convert_fusion.refs_0_), channel_id=1, source_target_pairs={{0,8},{8,16},{16,24},{1,9},{9,17},{17,25},{2,10},{10,18},{18,26},{... | collective-permute-start | bytes 2359304 | tf_op jit(solution)/shard_map/ppermute | solution.py:251
  319.9 23.5 %collective-permute-start.32 = (bf16[192,2048]{1,0:T(8,128)(2,1)S(1)}, bf16[192,2048]{1,0:T(8,128)(2,1)}, u32[]{:S(2)}, u32[]{:S(2)}) collective-permute-start(bf16[192,2048]{1,0:T(8,128)(2,1)S(1)} %add_convert_fusion.refs_0_), channel_id=1, source_target_pairs={{8,0},{16,8},{24,16},{9,1},{17,9},{25,17},{10,2},{18,10},{26,18},{... | collective-permute-start | bytes 2359304 | tf_op jit(solution)/shard_map/ppermute | solution.py:252
  343.9 25.4 %collective-permute-start.38 = (bf16[192,2048]{1,0:T(8,128)(2,1)}, bf16[192,2048]{1,0:T(8,128)(2,1)}, u32[]{:S(2)}, u32[]{:S(2)}) collective-permute-start(bf16[192,2048]{1,0:T(8,128)(2,1)} %collective-permute-done.31.refs_1_), channel_id=1, source_target_pairs={{0,8},{8,16},{16,24},{1,9},{9,17},{17,25},{2,10},{10,18},{18,26},{... | collective-permute-start | bytes 2359304 | tf_op jit(solution)/shard_map/ppermute | solution.py:251
  347.1 22.2 %collective-permute-start.39 = (bf16[192,2048]{1,0:T(8,128)(2,1)}, bf16[192,2048]{1,0:T(8,128)(2,1)}, u32[]{:S(2)}, u32[]{:S(2)}) collective-permute-start(bf16[192,2048]{1,0:T(8,128)(2,1)} %collective-permute-done.32.refs_4_), channel_id=1, source_target_pairs={{8,0},{16,8},{24,16},{9,1},{17,9},{25,17},{10,2},{18,10},{26,18},{... | collective-permute-start | bytes 2359304 | tf_op jit(solution)/shard_map/ppermute | solution.py:252
  356.0 13.3 %collective-permute-start.36 = (bf16[512,256]{1,0:T(8,128)(2,1)}, bf16[512,256]{1,0:T(8,128)(2,1)}, u32[]{:S(2)}, u32[]{:S(2)}) collective-permute-start(bf16[512,256]{1,0:T(8,128)(2,1)} %get-tuple-element.249), channel_id=1, source_target_pairs={{0,4},{1,5},{2,6},{3,7},{4,0},{5,1},{6,2},{7,3},{8,12},{9,13},{10,... | collective-permute-start | bytes 786440 | tf_op jit(solution)/shard_map/ppermute | solution.py:263
  376.6 20.5 %collective-permute-start.46 = (bf16[192,1536]{1,0:T(8,128)(2,1)}, bf16[192,1536]{1,0:T(8,128)(2,1)}, u32[]{:S(2)}, u32[]{:S(2)}) collective-permute-start(bf16[192,1536]{1,0:T(8,128)(2,1)} %get-tuple-element.275), channel_id=1, source_target_pairs={{0,2},{1,3},{2,0},{3,1},{4,6},{5,7},{6,4},{7,5},{8,10},{9,11},{10,... | collective-permute-start | bytes 1769480 | tf_op jit(solution)/shard_map/ppermute | solution.py:263
  377.2 28.5 %collective-permute-start.47 = (bf16[192,1536]{1,0:T(8,128)(2,1)}, bf16[192,1536]{1,0:T(8,128)(2,1)}, u32[]{:S(2)}, u32[]{:S(2)}) collective-permute-start(bf16[192,1536]{1,0:T(8,128)(2,1)} %get-tuple-element.276), channel_id=1, source_target_pairs={{0,4},{1,5},{2,6},{3,7},{4,0},{5,1},{6,2},{7,3},{8,12},{9,13},{10,... | collective-permute-start | bytes 1769480 | tf_op jit(solution)/shard_map/ppermute | solution.py:263
  378.3 27.4 %collective-permute-start.48 = (bf16[192,1536]{1,0:T(8,128)(2,1)}, bf16[192,1536]{1,0:T(8,128)(2,1)}, u32[]{:S(2)}, u32[]{:S(2)}) collective-permute-start(bf16[192,1536]{1,0:T(8,128)(2,1)} %get-tuple-element.277), channel_id=1, source_target_pairs={{0,6},{1,7},{2,4},{3,5},{4,2},{5,3},{6,0},{7,1},{8,14},{9,15},{10,... | collective-permute-start | bytes 1769480 | tf_op jit(solution)/shard_map/ppermute | solution.py:263
  380.1 31.4 %collective-permute-start.44 = (bf16[192,2048]{1,0:T(8,128)(2,1)}, bf16[192,2048]{1,0:T(8,128)(2,1)S(1)}, u32[]{:S(2)}, u32[]{:S(2)}) collective-permute-start(bf16[192,2048]{1,0:T(8,128)(2,1)} %collective-permute-done.38.refs_2_), channel_id=1, source_target_pairs={{0,8},{8,16},{16,24},{1,9},{9,17},{17,25},{2,10},{10,18},{18,26},{... | collective-permute-start | bytes 2359304 | tf_op jit(solution)/shard_map/ppermute | solution.py:251
  383.4 28.0 %collective-permute-start.45 = (bf16[192,2048]{1,0:T(8,128)(2,1)}, bf16[192,2048]{1,0:T(8,128)(2,1)}, u32[]{:S(2)}, u32[]{:S(2)}) collective-permute-start(bf16[192,2048]{1,0:T(8,128)(2,1)} %collective-permute-done.39.refs_5_), channel_id=1, source_target_pairs={{8,0},{16,8},{24,16},{9,1},{17,9},{25,17},{10,2},{18,10},{26,18},{... | collective-permute-start | bytes 2359304 | tf_op jit(solution)/shard_map/ppermute | solution.py:252
  389.2 29.7 %all-to-all-start.3 = ((bf16[4,128,640]{1,2,0:T(8,128)(2,1)}), bf16[4,128,640]{1,2,0:T(8,128)(2,1)}, u32[]{:S(2)}, u32[]{:S(2)}) async-start(bf16[4,128,640]{1,2,0:T(8,128)(2,1)} %copy.104), calls=%async_computation.3 | async-start | bytes 1310720 | tf_op jit(solution)/shard_map/all_to_all | solution.py:906
  397.1 14.9 %collective-permute-start.41 = (bf16[192,768]{1,0:T(8,128)(2,1)S(1)}, bf16[192,768]{1,0:T(8,128)(2,1)S(1)}, u32[]{:S(2)}, u32[]{:S(2)}) collective-permute-start(bf16[192,768]{1,0:T(8,128)(2,1)S(1)} %get-tuple-element.265), channel_id=1, source_target_pairs={{0,2},{1,3},{2,0},{3,1},{4,6},{5,7},{6,4},{7,5},{8,10},{9,11},{10,... | collective-permute-start | bytes 884744 | tf_op jit(solution)/shard_map/ppermute | solution.py:263
  418.9 18.4 %all-to-all-start.2 = ((bf16[192,4,384]{2,0,1:T(8,128)(2,1)}), bf16[192,4,384]{2,0,1:T(8,128)(2,1)}, u32[]{:S(2)}, u32[]{:S(2)}) async-start(bf16[192,4,384]{2,0,1:T(8,128)(2,1)} %bitcast.136), calls=%async_computation.2 | async-start | bytes 1179648 | tf_op jit(solution)/shard_map/all_to_all | solution.py:914
  439.5 18.3 %collective-permute-start.49 = (bf16[192,1152]{1,0:T(8,128)(2,1)S(1)}, bf16[192,1152]{1,0:T(8,128)(2,1)S(1)}, u32[]{:S(2)}, u32[]{:S(2)}) collective-permute-start(bf16[192,1152]{1,0:T(8,128)(2,1)S(1)} %pad_maximum_fusion.refs_0_), channel_id=1, source_target_pairs={{0,8},{8,16},{16,24},{24,0},{1,9},{9,17},{17,25},{25,1},{2,10},{10... | collective-permute-start | bytes 1327112 | tf_op jit(solution)/shard_map/ppermute | solution.py:237
  441.0 37.0 %collective-permute-start.50 = (bf16[192,1152]{1,0:T(8,128)(2,1)S(1)}, bf16[192,1152]{1,0:T(8,128)(2,1)S(1)}, u32[]{:S(2)}, u32[]{:S(2)}) collective-permute-start(bf16[192,1152]{1,0:T(8,128)(2,1)S(1)} %pad_maximum_fusion.refs_0_), channel_id=1, source_target_pairs={{0,16},{8,24},{16,0},{24,8},{1,17},{9,25},{17,1},{25,9},{2,18},{10... | collective-permute-start | bytes 1327112 | tf_op jit(solution)/shard_map/ppermute | solution.py:237
  445.3 36.7 %collective-permute-start.51 = (bf16[192,1152]{1,0:T(8,128)(2,1)S(1)}, bf16[192,1152]{1,0:T(8,128)(2,1)S(1)}, u32[]{:S(2)}, u32[]{:S(2)}) collective-permute-start(bf16[192,1152]{1,0:T(8,128)(2,1)S(1)} %pad_maximum_fusion.refs_0_), channel_id=1, source_target_pairs={{0,24},{8,0},{16,8},{24,16},{1,25},{9,1},{17,9},{25,17},{2,26},{10... | collective-permute-start | bytes 1327112 | tf_op jit(solution)/shard_map/ppermute | solution.py:237
  (104 other events, 853.1 us)
Sparse Core Ops, SparseCore 0:
  10.8 28.3 all-gather.6
  41.2 47.8 all-gather.8
  91.5 58.2 all-gather.10
  152.1 52.2 all-gather.12
  290.1 42.0 all-gather.14

commit v13 on v11

--- a/solution.py
+++ b/solution.py
@@ -226,7 +226,7 @@
         ],
         compiler_params=pltpu.CompilerParams(vmem_limit_bytes=28 * 1024 * 1024),
         cost_estimate=pl.CostEstimate(
-            flops=10**12,
+            flops=0 if g else 10**12,
             bytes_accessed=0,
             transcendentals=0,
         ),
@@ -884,7 +884,7 @@
             head_queries, kv_all, bias, held, exact, lse, seqs, rows, g, groups
         )
         if g == 0:
-            grad_gate_up_blocks = after(grad_gate_up_blocks, grad_down, part_q)
+            grad_gate_up_blocks = after(grad_gate_up_blocks, part_q)
             grad_gate_up_shard = total_of(grad_gate_up_blocks).astype(BF)
             steps = [(grad_gate_up_shard, grad_gate_up_shard)]
             steps.append(relay_step(steps[0], seqs))
@@ -895,7 +895,7 @@
         held = after(head_grad, grad_gate_up_shard, out_there)
     steps[1] = after(steps[1], part_q)
     steps.append(relay_step(steps[1], seqs))
-    far = after(far, steps[1])
+    far = after(far, steps[1], grad_down)
     pairs = kv_pair_sums(near, [hop(each, shards, 1) for each in far])
     out_sums = pair_sums(out_near, after(out_there, pairs), shard)
     sent_grads, product_columns = head_columns(
@@ -915,10 +915,9 @@
     out_parts = lax.all_to_all(
         out_part.reshape(part, seqs, q_cols), "seq", split_axis=1, concat_axis=1, tiled=True
     )
-    out_own = by_rows(jnp.sum(out_parts.astype(F32), axis=1).astype(BF))
-    out_last = [by_rows(each) for each in send_out([out_own] * seqs, seqs)]
-    head_part = total_of(after(send_chips(head_sums, shards), steps[3]))
-    grad_normed = dot_nt(after(token_grads, head_part), attn_full)
+    head_blocks = send_chips(head_sums, shards)
+    head_part = total_of(after(head_blocks, steps[3]))
+    grad_normed = dot_nt(after(token_grads, head_part, out_parts), attn_full)
     grad_tokens = grad_residual + root_back(inputs, root(inputs), grad_normed)
     base_cols = head_cols + experts
     plane_high, plane_low = two_parts(
@@ -932,6 +931,8 @@
     )
     head_part = by_rows(head_part.astype(BF))
     head_last = [by_rows(each) for each in send_out([head_part] * seqs, seqs)]
+    out_own = by_rows(jnp.sum(out_parts.astype(F32), axis=1).astype(BF))
+    out_last = [by_rows(each) for each in send_out([out_own] * seqs, seqs)]
     grad_gate_up, grad_gain_ffn = place_gate_up(after(steps, head_part), w_gate_up, gain_two, z)
     head_last, out_last = after((head_last, out_last), grad_gate_up)
     grad_query, grad_keyval, grad_out, grad_gain_attn, sums = place_heads(

time: 512 us -> 521 us (1.018)
  the two profiles are of different devices: /device:TPU:0 before, /device:TPU:12 now
where the time goes in v13:
time: 521 us; the launch traced here: 512 us
  waiting for transfers between devices  211 us (40%)
  Pallas kernels  101 us (19%)
  starting transfers between devices  97.3 us (19%)
  local copies, waits for them, and re-layouts  34.5 us (7%)
  other arithmetic  26.3 us (5%)
  matrix products  21.5 us (4%)
  between operations  21 us (4%)
    ppermute x21, waiting for transfers between devices, shift(): lax.ppermute(block, 'seq', [(i, (i + step) % count) for i in range(count)])  122 us
    ppermute x28, waiting for transfers between devices, hop(): return lax.ppermute(block, 'fsdp', [(i, i ^ mask) for i in range(count)])  55.5 us
    ppermute x21, starting transfers between devices, shift(): lax.ppermute(block, 'seq', [(i, (i + step) % count) for i in range(count)])  30.8 us
    pallas_call x2, Pallas kernels, flash_backward(): pl.pallas_call(functools.partial(backward_kernel, shards, seqs, rows, g,...  27.6 us
    ppermute x28, starting transfers between devices, hop(): return lax.ppermute(block, 'fsdp', [(i, i ^ mask) for i in range(count)])  25.9 us
    unnamed x208, local copies, waits for them, and re-layouts  23.7 us
    ppermute x3, waiting for transfers between devices, relay_step(): lax.ppermute(up, 'seq', [(i, i + 1) for i in range(count - 1)])  19.5 us
    pallas_call x1, Pallas kernels, flash_forward(): pl.pallas_call(functools.partial(forward_kernel, shards, seqs, rows, loca...  19 us
  transfers between devices with their start and end apart: 64, of which 34 were waited for; matrix products, arithmetic and copies ran while one was open for 10% of the time, Pallas kernels for 16%

profile of v13, /device:TPU:12, one launch (start us, length us, event | category | flops | bytes accessed | tf_op | source)
XLA Modules:
  0.0 512.4 jit_solution(5992296238926959842)
XLA Ops:
  21.3 23.3 %collective-permute-done = bf16[136,1536]{1,0:T(8,128)(2,1)S(1)} collective-permute-done((bf16[136,1536]{1,0:T(8,128)(2,1)S(1)}, bf16[136,1536]{1,0:T(8,128)(2,1)S(1)}, u32[]{:S(2)}, u32[]{:S(2)}) %collective-permute-start) | collective-permute-done | bytes 417824 | tf_op jit(solution)/shard_map/ppermute | solution.py:237
  44.7 7.8 %collective-permute-done.1 = bf16[136,1536]{1,0:T(8,128)(2,1)S(1)} collective-permute-done((bf16[136,1536]{1,0:T(8,128)(2,1)S(1)}, bf16[136,1536]{1,0:T(8,128)(2,1)S(1)}, u32[]{:S(2)}, u32[]{:S(2)}) %collective-permute-start.1) | collective-permute-done | bytes 417824 | tf_op jit(solution)/shard_map/ppermute | solution.py:237
  62.8 7.3 %collective-permute-done.3.refs_1_ = bf16[528,256]{1,0:T(8,128)(2,1)S(1)} collective-permute-done((bf16[528,256]{1,0:T(8,128)(2,1)S(1)}, bf16[528,256]{1,0:T(8,128)(2,1)S(1)}, u32[]{:S(2)}, u32[]{:S(2)}) %collective-permute-start.3) | collective-permute-done | bytes 270368 | tf_op jit(solution)/shard_map/ppermute | solution.py:263
  70.1 7.5 %collective-permute-done.4.refs_2_ = bf16[528,256]{1,0:T(8,128)(2,1)S(1)} collective-permute-done((bf16[528,256]{1,0:T(8,128)(2,1)S(1)}, bf16[528,256]{1,0:T(8,128)(2,1)S(1)}, u32[]{:S(2)}, u32[]{:S(2)}) %collective-permute-start.4) | collective-permute-done | bytes 270368 | tf_op jit(solution)/shard_map/ppermute | solution.py:263
  77.6 3.2 collective-permute-done.5.refs_3_
  83.1 19.0 %shard_map.221 = (bf16[512,384]{1,0:T(8,128)(2,1)}, f32[512,384]{1,0:T(8,128)S(1)}, f32[512,384]{1,0:T(8,128)S(1)}) custom-call(bf16[528,256]{1,0:T(8,128)(2,1)S(1)} %maximum_maximum_fusion.1.refs_0_, bf16[528,256]{1,0:T(8,128)(2,1)S(1)} %collective-permute-done.3.refs_1_, bf16[528,256]{1,0:T(8,128)(2,1)S(1)} %collective-permute-done.4.refs_2_, ...), custom_call_target="tpu_custom_call" | custom-call | tf_op jit(solution)/shard_map/pallas_call | solution.py:114
  103.9 3.4 all-to-all-start
  108.2 8.7 %all-to-all-done = bf16[4,128,384]{2,1,0:T(8,128)(2,1)S(1)} async-done(((bf16[4,128,384]{2,1,0:T(8,128)(2,1)}), bf16[4,128,384]{2,1,0:T(8,128)(2,1)S(1)}, u32[]{:S(2)}, u32[]{:S(2)}) %all-to-all-start) | async-done | bytes 393248 | tf_op jit(solution)/shard_map/all_to_all | solution.py:796
  118.8 5.1 %multiply_reduce_fusion.5 = (f32[128]{0:T(128)S(1)}, f32[128,1536]{1,0:T(8,128)S(1)}) fusion(bf16[128,1536]{1,0:T(8,128)(2,1)S(1)} %bitcast.138, bf16[1536,1536]{0,1:T(8,128)(2,1)} %all-gather.9.cloned.1.call-done, bf16[128,1536]{1,0:T(8,128)(2,1)} %param.14), kind=kOutput, calls=%fused_computation.69 | convolution fusion | flops 604766080 | bytes 6291968 | tf_op jit(solution)/shard_map/dot_general | solution.py:24
  126.3 4.2 collective-permute-start.11
  136.2 15.1 %collective-permute-done.11.refs_2_ = bf16[96,1536]{1,0:T(8,128)(2,1)} collective-permute-done((bf16[96,1536]{1,0:T(8,128)(2,1)S(1)}, bf16[96,1536]{1,0:T(8,128)(2,1)}, u32[]{:S(2)}, u32[]{:S(2)}) %collective-permute-start.11) | collective-permute-done | bytes 294944 | tf_op jit(solution)/shard_map/ppermute | solution.py:237
  151.3 5.0 collective-permute-done.12.refs_3_
  156.3 8.8 %shard_map.222 = (bf16[384,1536]{1,0:T(8,128)(2,1)}, f32[384,2048]{1,0:T(8,128)}, bf16[384,1024]{1,0:T(8,128)(2,1)}, bf16[96,1536]{1,0:T(8,128)(2,1)}, bf16[96,1...) custom-call(bf16[96,1536]{1,0:T(8,128)(2,1)} %get-tuple-element.377.refs_0_, ...), custom_call_target="tpu_custom_call" | custom-call | tf_op jit(solution)/shard_map/pallas_call | solution.py:396
  168.5 19.4 %collective-permute-done.13 = bf16[96,1536]{1,0:T(8,128)(2,1)S(1)} collective-permute-done((bf16[96,1536]{1,0:T(8,128)(2,1)}, bf16[96,1536]{1,0:T(8,128)(2,1)S(1)}, u32[]{:S(2)}, u32[]{:S(2)}) %collective-permute-start.13) | collective-permute-done | bytes 294944 | tf_op jit(solution)/shard_map/ppermute | solution.py:237
  193.9 3.8 collective-permute-start.16
  197.6 4.2 collective-permute-start.17
  204.5 13.1 %collective-permute-done.16.refs_1_ = bf16[96,1536]{1,0:T(8,128)(2,1)S(1)} collective-permute-done((bf16[96,1536]{1,0:T(8,128)(2,1)S(1)}, bf16[96,1536]{1,0:T(8,128)(2,1)S(1)}, u32[]{:S(2)}, u32[]{:S(2)}) %collective-permute-start.16) | collective-permute-done | bytes 294944 | tf_op jit(solution)/shard_map/ppermute | solution.py:237
  217.6 4.3 collective-permute-done.17.refs_2_
  221.9 3.8 collective-permute-done.18.refs_3_
  226.4 9.9 %shard_map.223 = (bf16[384,1536]{1,0:T(8,128)(2,1)}, bf16[384,2048]{1,0:T(8,128)(2,1)}, bf16[96,1536]{1,0:T(8,128)(2,1)}, bf16[96,1536]{1,0:T(8,128)(2,1)}, bf16...) custom-call(bf16[96,1536]{1,0:T(8,128)(2,1)} %get-tuple-element.188.refs_0_, bf16[96,1536]{1,0:T(8,128)(2,1)} %copy-done.70, ...), custom_call_target="tpu_custom_call" | custom-call | tf_op jit(solution)/shard_map/pallas_call | solution.py:445
  240.7 2.9 shard_map.224
  243.7 4.8 shard_map.226
  252.0 3.1 collective-permute-start.24
  255.1 4.0 collective-permute-done.19
  270.7 7.6 %all-to-all-start.1 = ((bf16[128,4,384]{2,0,1:T(8,128)(2,1)}), bf16[128,4,384]{2,0,1:T(8,128)(2,1)}, u32[]{:S(2)}, u32[]{:S(2)}) async-start(bf16[128,4,384]{2,0,1:T(8,128)(2,1)} %bitcast.147), calls=%async_computation.1 | async-start | bytes 786432 | tf_op jit(solution)/shard_map/all_to_all | solution.py:872
  292.8 13.8 %shard_map.228 = (f32[512,192]{1,0:T(8,128)S(1)}, bf16[4,512,128]{2,1,0:T(8,128)(2,1)S(1)}, bf16[4,512,128]{2,1,0:T(8,128)(2,1)S(1)}) custom-call(bf16[8,528,256]{2,1,0:T(8,128)(2,1)S(1)} %copy-done.8, bf16[512,384]{1,0:T(8,128)(2,1)S(1)} %slice_multiply_fusion.refs_8_.refs_1_, f32[8,1,1024]{2,1,0:T(1,128)S(1)} %pad_maximum_fusion.3.refs_9_.refs_2_, ...), custom_call_target="tpu_custom_call" | custom-call | flops 999999995904 | tf_op jit(solution)/shard_map/pallas_call | solution.py:212
  306.7 5.6 %collective-permute-done.28 = bf16[192,2048]{1,0:T(8,128)(2,1)} collective-permute-done((bf16[192,2048]{1,0:T(8,128)(2,1)}, bf16[192,2048]{1,0:T(8,128)(2,1)}, u32[]{:S(2)}, u32[]{:S(2)}) %collective-permute-start.28) | collective-permute-done | bytes 786464 | tf_op jit(solution)/shard_map/ppermute | solution.py:263
  316.5 3.4 collective-permute-start.31
  322.6 13.8 %shard_map.230 = (f32[512,192]{1,0:T(8,128)S(1)}, bf16[4,512,128]{2,1,0:T(8,128)(2,1)S(1)}, bf16[4,512,128]{2,1,0:T(8,128)(2,1)S(1)}) custom-call(bf16[8,528,256]{2,1,0:T(8,128)(2,1)S(1)} %copy-done.8, bf16[512,384]{1,0:T(8,128)(2,1)S(1)} %slice_multiply_fusion.refs_8_.refs_1_, f32[8,1,1024]{2,1,0:T(1,128)S(1)} %pad_maximum_fusion.3.refs_9_.refs_2_, ...), custom_call_target="tpu_custom_call" | custom-call | tf_op jit(solution)/shard_map/pallas_call | solution.py:212
  338.8 3.3 collective-permute-done.31.refs_1_
  343.9 3.2 collective-permute-start.38
  347.1 3.5 collective-permute-start.39
  359.9 3.0 shard_map.232
  364.0 5.3 %collective-permute-done.36.refs_4_ = bf16[512,256]{1,0:T(8,128)(2,1)} collective-permute-done((bf16[512,256]{1,0:T(8,128)(2,1)}, bf16[512,256]{1,0:T(8,128)(2,1)}, u32[]{:S(2)}, u32[]{:S(2)}) %collective-permute-start.36) | collective-permute-done | bytes 262176 | tf_op jit(solution)/shard_map/ppermute | solution.py:263
  370.8 3.7 shard_map.234
  379.9 10.9 %collective-permute-done.49 = bf16[192,1536]{1,0:T(8,128)(2,1)S(1)} collective-permute-done((bf16[192,1536]{1,0:T(8,128)(2,1)S(1)}, bf16[192,1536]{1,0:T(8,128)(2,1)S(1)}, u32[]{:S(2)}, u32[]{:S(2)}) %collective-permute-start.49) | collective-permute-done | bytes 589856 | tf_op jit(solution)/shard_map/ppermute | solution.py:263
  390.8 12.5 %collective-permute-done.50 = bf16[192,1536]{1,0:T(8,128)(2,1)S(1)} collective-permute-done((bf16[192,1536]{1,0:T(8,128)(2,1)S(1)}, bf16[192,1536]{1,0:T(8,128)(2,1)S(1)}, u32[]{:S(2)}, u32[]{:S(2)}) %collective-permute-start.50) | collective-permute-done | bytes 589856 | tf_op jit(solution)/shard_map/ppermute | solution.py:263
  404.5 5.7 %all-to-all-start.2 = ((bf16[192,4,384]{2,0,1:T(8,128)(2,1)}), bf16[192,4,384]{2,0,1:T(8,128)(2,1)}, u32[]{:S(2)}, u32[]{:S(2)}) async-start(bf16[192,4,384]{2,0,1:T(8,128)(2,1)} %bitcast.136), calls=%async_computation.2 | async-start | bytes 1179648 | tf_op jit(solution)/shard_map/all_to_all | solution.py:915
  410.2 3.4 collective-permute-start.44
  413.6 3.3 collective-permute-start.45
  423.2 16.2 %collective-permute-done.44.refs_3_ = bf16[192,2048]{1,0:T(8,128)(2,1)} collective-permute-done((bf16[192,2048]{1,0:T(8,128)(2,1)}, bf16[192,2048]{1,0:T(8,128)(2,1)}, u32[]{:S(2)}, u32[]{:S(2)}) %collective-permute-start.44) | collective-permute-done | bytes 786464 | tf_op jit(solution)/shard_map/ppermute | solution.py:251
  441.4 4.2 all-to-all-start.3
  453.9 8.1 %shard_map.236 = (f32[4,192,2048]{2,1,0:T(8,128)}, f32[192,128]{1,0:T(8,128)S(1)}) custom-call(s32[1]{0:T(128)} %bitcast.33.place_ref, bf16[192,2048]{1,0:T(8,128)(2,1)S(1)} %copy-done.4, bf16[192,2048]{1,0:T(8,128)(2,1)S(1)} %copy-done.19, bf16[192,2048]{1,0:T(8,128)(2,1)} %collective-permute-done.38.refs_2_, ...), custom_call_target="tpu_custom_call" | custom-call | tf_op jit(solution)/shard_map/pallas_call | solution.py:583
  465.4 3.8 collective-permute-start.53
  469.2 6.3 %fusion.27 = (f32[128]{0:T(128)S(1)}, f32[128]{0:T(128)S(1)}, f32[128,1536]{1,0:T(8,128)S(1)}) fusion(bf16[128,1536]{1,0:T(8,128)(2,1)S(1)} %copy-done.55, bf16[128,2560]{0,1:T(8,128)(2,1)} %bitcast.55, bf16[1536,2560]{1,0:T(8,128)(2,1)} %all-gather.13.cloned.1.call-done), kind=kOutput, calls=%fused_computation.47 | convolution fusion | flops 1007615744 | bytes 9700352 | tf_op jit(solution)/shard_map/dot_general | solution.py:28
  475.5 9.9 %collective-permute-done.46.refs_1_ = bf16[192,768]{1,0:T(8,128)(2,1)} collective-permute-done((bf16[192,768]{1,0:T(8,128)(2,1)S(1)}, bf16[192,768]{1,0:T(8,128)(2,1)}, u32[]{:S(2)}, u32[]{:S(2)}) %collective-permute-start.46) | collective-permute-done | bytes 294944 | tf_op jit(solution)/shard_map/ppermute | solution.py:237
  486.5 5.2 %collective-permute-done.47.refs_2_ = bf16[192,768]{1,0:T(8,128)(2,1)} collective-permute-done((bf16[192,768]{1,0:T(8,128)(2,1)S(1)}, bf16[192,768]{1,0:T(8,128)(2,1)}, u32[]{:S(2)}, u32[]{:S(2)}) %collective-permute-start.47) | collective-permute-done | bytes 294944 | tf_op jit(solution)/shard_map/ppermute | solution.py:237
  497.7 3.3 shard_map.237
  (432 shorter events, 140.8 us)
Async XLA Ops:
  7.2 47.7 %all-gather.7.cloned.1.call-start = ((), (), s32[]{:S(2)}) async-start(), calls=%async_computation.4 | async-start | bytes 2211840 | tf_op jit(solution)/shard_map/all_gather | solution.py:720
  10.7 108.0 %all-gather.9.cloned.1.call-start = ((), (), s32[]{:S(2)}) async-start(), calls=%async_computation.5 | async-start | bytes 5308416 | tf_op jit(solution)/shard_map/all_gather | solution.py:747
  11.5 144.9 %all-gather.11.cloned.1.call-start = ((), (), s32[]{:S(2)}) async-start(), calls=%async_computation.6 | async-start | bytes 11059200 | tf_op jit(solution)/shard_map/all_gather | solution.py:762
  15.1 189.4 %all-gather.13.cloned.1.call-start = ((), (), s32[]{:S(2)}) async-start(), calls=%async_computation.7 | async-start | bytes 8847360 | tf_op jit(solution)/shard_map/all_gather | solution.py:775
  15.1 29.6 %collective-permute-start = (bf16[136,1536]{1,0:T(8,128)(2,1)S(1)}, bf16[136,1536]{1,0:T(8,128)(2,1)S(1)}, u32[]{:S(2)}, u32[]{:S(2)}) collective-permute-start(bf16[136,1536]{1,0:T(8,128)(2,1)S(1)} %fusion.36), channel_id=1, source_target_pairs={{0,8},{8,16},{16,24},{24,0},{1,9},{9,17},{17,25},{25,1},{2,10},{10... | collective-permute-start | bytes 1253384 | tf_op jit(solution)/shard_map/ppermute | solution.py:237
  16.7 35.8 %collective-permute-start.1 = (bf16[136,1536]{1,0:T(8,128)(2,1)S(1)}, bf16[136,1536]{1,0:T(8,128)(2,1)S(1)}, u32[]{:S(2)}, u32[]{:S(2)}) collective-permute-start(bf16[136,1536]{1,0:T(8,128)(2,1)S(1)} %fusion.36), channel_id=1, source_target_pairs={{0,16},{8,24},{16,0},{24,8},{1,17},{9,25},{17,1},{25,9},{2,18},{10... | collective-permute-start | bytes 1253384 | tf_op jit(solution)/shard_map/ppermute | solution.py:237
  18.0 36.3 %collective-permute-start.2 = (bf16[136,1536]{1,0:T(8,128)(2,1)S(1)}, bf16[136,1536]{1,0:T(8,128)(2,1)S(1)}, u32[]{:S(2)}, u32[]{:S(2)}) collective-permute-start(bf16[136,1536]{1,0:T(8,128)(2,1)S(1)} %fusion.36), channel_id=1, source_target_pairs={{0,24},{8,0},{16,8},{24,16},{1,25},{9,1},{17,9},{25,17},{2,26},{10... | collective-permute-start | bytes 1253384 | tf_op jit(solution)/shard_map/ppermute | solution.py:237
  61.1 19.7 %collective-permute-start.5 = (bf16[528,256]{1,0:T(8,128)(2,1)S(1)}, bf16[528,256]{1,0:T(8,128)(2,1)S(1)}, u32[]{:S(2)}, u32[]{:S(2)}) collective-permute-start(bf16[528,256]{1,0:T(8,128)(2,1)S(1)} %maximum_maximum_fusion.1.refs_0_), channel_id=1, source_target_pairs={{0,6},{1,7},{2,4},{3,5},{4,2},{5,3},{6,0},{7,1},{8,14},{9,15},{10,... | collective-permute-start | bytes 811016 | tf_op jit(solution)/shard_map/ppermute | solution.py:263
  62.7 19.4 %collective-permute-start.6 = (bf16[528,256]{1,0:T(8,128)(2,1)S(1)}, bf16[528,256]{1,0:T(8,128)(2,1)S(1)}, u32[]{:S(2)}, u32[]{:S(2)}) collective-permute-start(bf16[528,256]{1,0:T(8,128)(2,1)S(1)} %maximum_maximum_fusion.1.refs_0_), channel_id=1, source_target_pairs={{0,1},{1,0},{2,3},{3,2},{4,5},{5,4},{6,7},{7,6},{8,9},{9,8},{10,11... | collective-permute-start | bytes 811016 | tf_op jit(solution)/shard_map/ppermute | solution.py:263
  126.3 25.0 %collective-permute-start.11 = (bf16[96,1536]{1,0:T(8,128)(2,1)S(1)}, bf16[96,1536]{1,0:T(8,128)(2,1)}, u32[]{:S(2)}, u32[]{:S(2)}) collective-permute-start(bf16[96,1536]{1,0:T(8,128)(2,1)S(1)} %get-tuple-element.375), channel_id=1, source_target_pairs={{0,16},{8,24},{16,0},{24,8},{1,17},{9,25},{17,1},{25,9},{2,18},{10... | collective-permute-start | bytes 884744 | tf_op jit(solution)/shard_map/ppermute | solution.py:237
  130.4 25.9 %collective-permute-start.12 = (bf16[96,1536]{1,0:T(8,128)(2,1)S(1)}, bf16[96,1536]{1,0:T(8,128)(2,1)}, u32[]{:S(2)}, u32[]{:S(2)}) collective-permute-start(bf16[96,1536]{1,0:T(8,128)(2,1)S(1)} %get-tuple-element.374), channel_id=1, source_target_pairs={{0,24},{8,0},{16,8},{24,16},{1,25},{9,1},{17,9},{25,17},{2,26},{10... | collective-permute-start | bytes 884744 | tf_op jit(solution)/shard_map/ppermute | solution.py:237
  165.1 22.8 %collective-permute-start.13 = (bf16[96,1536]{1,0:T(8,128)(2,1)}, bf16[96,1536]{1,0:T(8,128)(2,1)S(1)}, u32[]{:S(2)}, u32[]{:S(2)}) collective-permute-start(bf16[96,1536]{1,0:T(8,128)(2,1)} %get-tuple-element.171), channel_id=1, source_target_pairs={{0,24},{8,0},{16,8},{24,16},{1,25},{9,1},{17,9},{25,17},{2,26},{10... | collective-permute-start | bytes 884744 | tf_op jit(solution)/shard_map/ppermute | solution.py:237
  165.2 22.7 %collective-permute-start.14 = (bf16[96,1536]{1,0:T(8,128)(2,1)}, bf16[96,1536]{1,0:T(8,128)(2,1)S(1)}, u32[]{:S(2)}, u32[]{:S(2)}) collective-permute-start(bf16[96,1536]{1,0:T(8,128)(2,1)} %get-tuple-element.172), channel_id=1, source_target_pairs={{0,16},{8,24},{16,0},{24,8},{1,17},{9,25},{17,1},{25,9},{2,18},{10... | collective-permute-start | bytes 884744 | tf_op jit(solution)/shard_map/ppermute | solution.py:237
  166.0 22.9 %collective-permute-start.15 = (bf16[96,1536]{1,0:T(8,128)(2,1)}, bf16[96,1536]{1,0:T(8,128)(2,1)S(1)}, u32[]{:S(2)}, u32[]{:S(2)}) collective-permute-start(bf16[96,1536]{1,0:T(8,128)(2,1)} %get-tuple-element.173), channel_id=1, source_target_pairs={{0,8},{8,16},{16,24},{24,0},{1,9},{9,17},{17,25},{25,1},{2,10},{10... | collective-permute-start | bytes 884744 | tf_op jit(solution)/shard_map/ppermute | solution.py:237
  193.9 23.7 %collective-permute-start.16 = (bf16[96,1536]{1,0:T(8,128)(2,1)S(1)}, bf16[96,1536]{1,0:T(8,128)(2,1)S(1)}, u32[]{:S(2)}, u32[]{:S(2)}) collective-permute-start(bf16[96,1536]{1,0:T(8,128)(2,1)S(1)} %get-tuple-element.372), channel_id=1, source_target_pairs={{0,8},{8,16},{16,24},{24,0},{1,9},{9,17},{17,25},{25,1},{2,10},{10... | collective-permute-start | bytes 884744 | tf_op jit(solution)/shard_map/ppermute | solution.py:237
  197.6 24.3 %collective-permute-start.17 = (bf16[96,1536]{1,0:T(8,128)(2,1)S(1)}, bf16[96,1536]{1,0:T(8,128)(2,1)S(1)}, u32[]{:S(2)}, u32[]{:S(2)}) collective-permute-start(bf16[96,1536]{1,0:T(8,128)(2,1)S(1)} %get-tuple-element.371), channel_id=1, source_target_pairs={{0,16},{8,24},{16,0},{24,8},{1,17},{9,25},{17,1},{25,9},{2,18},{10... | collective-permute-start | bytes 884744 | tf_op jit(solution)/shard_map/ppermute | solution.py:237
  201.8 23.9 %collective-permute-start.18 = (bf16[96,1536]{1,0:T(8,128)(2,1)S(1)}, bf16[96,1536]{1,0:T(8,128)(2,1)S(1)}, u32[]{:S(2)}, u32[]{:S(2)}) collective-permute-start(bf16[96,1536]{1,0:T(8,128)(2,1)S(1)} %get-tuple-element.370), channel_id=1, source_target_pairs={{0,24},{8,0},{16,8},{24,16},{1,25},{9,1},{17,9},{25,17},{2,26},{10... | collective-permute-start | bytes 884744 | tf_op jit(solution)/shard_map/ppermute | solution.py:237
  236.3 22.9 %collective-permute-start.19 = (bf16[96,1536]{1,0:T(8,128)(2,1)}, bf16[96,1536]{1,0:T(8,128)(2,1)S(1)}, u32[]{:S(2)}, u32[]{:S(2)}) collective-permute-start(bf16[96,1536]{1,0:T(8,128)(2,1)} %get-tuple-element.194), channel_id=1, source_target_pairs={{0,24},{8,0},{16,8},{24,16},{1,25},{9,1},{17,9},{25,17},{2,26},{10... | collective-permute-start | bytes 884744 | tf_op jit(solution)/shard_map/ppermute | solution.py:237
  236.4 23.8 %collective-permute-start.20 = (bf16[96,1536]{1,0:T(8,128)(2,1)}, bf16[96,1536]{1,0:T(8,128)(2,1)S(1)}, u32[]{:S(2)}, u32[]{:S(2)}) collective-permute-start(bf16[96,1536]{1,0:T(8,128)(2,1)} %get-tuple-element.195), channel_id=1, source_target_pairs={{0,16},{8,24},{16,0},{24,8},{1,17},{9,25},{17,1},{25,9},{2,18},{10... | collective-permute-start | bytes 884744 | tf_op jit(solution)/shard_map/ppermute | solution.py:237
  237.4 25.3 %collective-permute-start.21 = (bf16[96,1536]{1,0:T(8,128)(2,1)}, bf16[96,1536]{1,0:T(8,128)(2,1)S(1)}, u32[]{:S(2)}, u32[]{:S(2)}) collective-permute-start(bf16[96,1536]{1,0:T(8,128)(2,1)} %get-tuple-element.196), channel_id=1, source_target_pairs={{0,8},{8,16},{16,24},{24,0},{1,9},{9,17},{17,25},{25,1},{2,10},{10... | collective-permute-start | bytes 884744 | tf_op jit(solution)/shard_map/ppermute | solution.py:237
  248.6 17.9 %collective-permute-start.23 = (bf16[4,192,2048]{2,1,0:T(8,128)(2,1)S(1)}, bf16[4,192,2048]{2,1,0:T(8,128)(2,1)S(1)}, u32[]{:S(2)}, u32[]{:S(2)}) collective-permute-start(bf16[4,192,2048]{2,1,0:T(8,128)(2,1)S(1)} %get-tuple-element.220), channel_id=1, source_target_pairs={{0,1},{1,0},{2,3},{3,2},{4,5},{5,4},{6,7},{7,6},{8,9},{9,8},{10,11... | collective-permute-start | bytes 9437192 | tf_op jit(solution)/shard_map/ppermute | solution.py:263
  252.0 28.5 %collective-permute-start.24 = (bf16[192,1024]{1,0:T(8,128)(2,1)}, bf16[192,1024]{1,0:T(8,128)(2,1)}, u32[]{:S(2)}, u32[]{:S(2)}) collective-permute-start(bf16[192,1024]{1,0:T(8,128)(2,1)} %get-tuple-element.208), channel_id=1, source_target_pairs={{0,2},{1,3},{2,0},{3,1},{4,6},{5,7},{6,4},{7,5},{8,10},{9,11},{10,... | collective-permute-start | bytes 1179656 | tf_op jit(solution)/shard_map/ppermute | solution.py:263
  259.1 22.9 %collective-permute-start.25 = (bf16[192,1024]{1,0:T(8,128)(2,1)}, bf16[192,1024]{1,0:T(8,128)(2,1)}, u32[]{:S(2)}, u32[]{:S(2)}) collective-permute-start(bf16[192,1024]{1,0:T(8,128)(2,1)} %get-tuple-element.209), channel_id=1, source_target_pairs={{0,4},{1,5},{2,6},{3,7},{4,0},{5,1},{6,2},{7,3},{8,12},{9,13},{10,... | collective-permute-start | bytes 1179656 | tf_op jit(solution)/shard_map/ppermute | solution.py:263
  260.2 21.8 %collective-permute-start.26 = (bf16[192,1024]{1,0:T(8,128)(2,1)}, bf16[192,1024]{1,0:T(8,128)(2,1)}, u32[]{:S(2)}, u32[]{:S(2)}) collective-permute-start(bf16[192,1024]{1,0:T(8,128)(2,1)} %get-tuple-element.210), channel_id=1, source_target_pairs={{0,6},{1,7},{2,4},{3,5},{4,2},{5,3},{6,0},{7,1},{8,14},{9,15},{10,... | collective-permute-start | bytes 1179656 | tf_op jit(solution)/shard_map/ppermute | solution.py:263
  270.7 19.3 %all-to-all-start.1 = ((bf16[128,4,384]{2,0,1:T(8,128)(2,1)}), bf16[128,4,384]{2,0,1:T(8,128)(2,1)}, u32[]{:S(2)}, u32[]{:S(2)}) async-start(bf16[128,4,384]{2,0,1:T(8,128)(2,1)} %bitcast.147), calls=%async_computation.1 | async-start | bytes 786432 | tf_op jit(solution)/shard_map/all_to_all | solution.py:872
  278.3 65.1 %all-gather.15.cloned.1.call-start = ((), (), s32[]{:S(2)}) async-start(), calls=%async_computation.8 | async-start | bytes 1966080 | tf_op jit(solution)/shard_map/all_gather | solution.py:875
  278.3 28.4 %collective-permute-start.27 = (bf16[192,2048]{1,0:T(8,128)(2,1)}, bf16[192,2048]{1,0:T(8,128)(2,1)}, u32[]{:S(2)}, u32[]{:S(2)}) collective-permute-start(bf16[192,2048]{1,0:T(8,128)(2,1)} %copy-done.43), channel_id=1, source_target_pairs={{0,2},{1,3},{2,0},{3,1},{4,6},{5,7},{6,4},{7,5},{8,10},{9,11},{10,... | collective-permute-start | bytes 2359304 | tf_op jit(solution)/shard_map/ppermute | solution.py:263
  279.5 32.7 %collective-permute-start.28 = (bf16[192,2048]{1,0:T(8,128)(2,1)}, bf16[192,2048]{1,0:T(8,128)(2,1)}, u32[]{:S(2)}, u32[]{:S(2)}) collective-permute-start(bf16[192,2048]{1,0:T(8,128)(2,1)} %copy-done.42), channel_id=1, source_target_pairs={{0,4},{1,5},{2,6},{3,7},{4,0},{5,1},{6,2},{7,3},{8,12},{9,13},{10,... | collective-permute-start | bytes 2359304 | tf_op jit(solution)/shard_map/ppermute | solution.py:263
  280.6 33.6 %collective-permute-start.29 = (bf16[192,2048]{1,0:T(8,128)(2,1)}, bf16[192,2048]{1,0:T(8,128)(2,1)}, u32[]{:S(2)}, u32[]{:S(2)}) collective-permute-start(bf16[192,2048]{1,0:T(8,128)(2,1)} %copy-done.41), channel_id=1, source_target_pairs={{0,6},{1,7},{2,4},{3,5},{4,2},{5,3},{6,0},{7,1},{8,14},{9,15},{10,... | collective-permute-start | bytes 2359304 | tf_op jit(solution)/shard_map/ppermute | solution.py:263
  290.0 32.7 %collective-permute-start.30 = (bf16[4,192,1536]{2,1,0:T(8,128)(2,1)}, bf16[4,192,1536]{2,1,0:T(8,128)(2,1)}, u32[]{:S(2)}, u32[]{:S(2)}) collective-permute-start(bf16[4,192,1536]{2,1,0:T(8,128)(2,1)} %copy-done.40), channel_id=1, source_target_pairs={{0,1},{1,0},{2,3},{3,2},{4,5},{5,4},{6,7},{7,6},{8,9},{9,8},{10,11... | collective-permute-start | bytes 7077896 | tf_op jit(solution)/shard_map/ppermute | solution.py:263
  316.5 25.7 %collective-permute-start.31 = (bf16[192,2048]{1,0:T(8,128)(2,1)S(1)}, bf16[192,2048]{1,0:T(8,128)(2,1)S(1)}, u32[]{:S(2)}, u32[]{:S(2)}) collective-permute-start(bf16[192,2048]{1,0:T(8,128)(2,1)S(1)} %add_convert_fusion.refs_0_), channel_id=1, source_target_pairs={{0,8},{8,16},{16,24},{1,9},{9,17},{17,25},{2,10},{10,18},{18,26},{... | collective-permute-start | bytes 2359304 | tf_op jit(solution)/shard_map/ppermute | solution.py:251
  319.8 23.5 %collective-permute-start.32 = (bf16[192,2048]{1,0:T(8,128)(2,1)S(1)}, bf16[192,2048]{1,0:T(8,128)(2,1)}, u32[]{:S(2)}, u32[]{:S(2)}) collective-permute-start(bf16[192,2048]{1,0:T(8,128)(2,1)S(1)} %add_convert_fusion.refs_0_), channel_id=1, source_target_pairs={{8,0},{16,8},{24,16},{9,1},{17,9},{25,17},{10,2},{18,10},{26,18},{... | collective-permute-start | bytes 2359304 | tf_op jit(solution)/shard_map/ppermute | solution.py:252
  343.9 25.5 %collective-permute-start.38 = (bf16[192,2048]{1,0:T(8,128)(2,1)S(1)}, bf16[192,2048]{1,0:T(8,128)(2,1)}, u32[]{:S(2)}, u32[]{:S(2)}) collective-permute-start(bf16[192,2048]{1,0:T(8,128)(2,1)S(1)} %collective-permute-done.31.refs_1_), channel_id=1, source_target_pairs={{0,8},{8,16},{16,24},{1,9},{9,17},{17,25},{2,10},{10,18},{18,26},{... | collective-permute-start | bytes 2359304 | tf_op jit(solution)/shard_map/ppermute | solution.py:251
  347.1 22.3 %collective-permute-start.39 = (bf16[192,2048]{1,0:T(8,128)(2,1)}, bf16[192,2048]{1,0:T(8,128)(2,1)}, u32[]{:S(2)}, u32[]{:S(2)}) collective-permute-start(bf16[192,2048]{1,0:T(8,128)(2,1)} %collective-permute-done.32.refs_4_), channel_id=1, source_target_pairs={{8,0},{16,8},{24,16},{9,1},{17,9},{25,17},{10,2},{18,10},{26,18},{... | collective-permute-start | bytes 2359304 | tf_op jit(solution)/shard_map/ppermute | solution.py:252
  375.2 28.0 %collective-permute-start.50 = (bf16[192,1536]{1,0:T(8,128)(2,1)S(1)}, bf16[192,1536]{1,0:T(8,128)(2,1)S(1)}, u32[]{:S(2)}, u32[]{:S(2)}) collective-permute-start(bf16[192,1536]{1,0:T(8,128)(2,1)S(1)} %get-tuple-element.280), channel_id=1, source_target_pairs={{0,4},{1,5},{2,6},{3,7},{4,0},{5,1},{6,2},{7,3},{8,12},{9,13},{10,... | collective-permute-start | bytes 1769480 | tf_op jit(solution)/shard_map/ppermute | solution.py:263
  376.4 26.9 %collective-permute-start.51 = (bf16[192,1536]{1,0:T(8,128)(2,1)S(1)}, bf16[192,1536]{1,0:T(8,128)(2,1)S(1)}, u32[]{:S(2)}, u32[]{:S(2)}) collective-permute-start(bf16[192,1536]{1,0:T(8,128)(2,1)S(1)} %get-tuple-element.281), channel_id=1, source_target_pairs={{0,6},{1,7},{2,4},{3,5},{4,2},{5,3},{6,0},{7,1},{8,14},{9,15},{10,... | collective-permute-start | bytes 1769480 | tf_op jit(solution)/shard_map/ppermute | solution.py:263
  404.5 36.9 %all-to-all-start.2 = ((bf16[192,4,384]{2,0,1:T(8,128)(2,1)}), bf16[192,4,384]{2,0,1:T(8,128)(2,1)}, u32[]{:S(2)}, u32[]{:S(2)}) async-start(bf16[192,4,384]{2,0,1:T(8,128)(2,1)} %bitcast.136), calls=%async_computation.2 | async-start | bytes 1179648 | tf_op jit(solution)/shard_map/all_to_all | solution.py:915
  410.2 29.3 %collective-permute-start.44 = (bf16[192,2048]{1,0:T(8,128)(2,1)}, bf16[192,2048]{1,0:T(8,128)(2,1)}, u32[]{:S(2)}, u32[]{:S(2)}) collective-permute-start(bf16[192,2048]{1,0:T(8,128)(2,1)} %collective-permute-done.38.refs_2_), channel_id=1, source_target_pairs={{0,8},{8,16},{16,24},{1,9},{9,17},{17,25},{2,10},{10,18},{18,26},{... | collective-permute-start | bytes 2359304 | tf_op jit(solution)/shard_map/ppermute | solution.py:251
  413.6 27.8 %collective-permute-start.45 = (bf16[192,2048]{1,0:T(8,128)(2,1)}, bf16[192,2048]{1,0:T(8,128)(2,1)}, u32[]{:S(2)}, u32[]{:S(2)}) collective-permute-start(bf16[192,2048]{1,0:T(8,128)(2,1)} %collective-permute-done.39.refs_5_), channel_id=1, source_target_pairs={{8,0},{16,8},{24,16},{9,1},{17,9},{25,17},{10,2},{18,10},{26,18},{... | collective-permute-start | bytes 2359304 | tf_op jit(solution)/shard_map/ppermute | solution.py:252
  416.9 24.5 %collective-permute-start.41 = (bf16[192,768]{1,0:T(8,128)(2,1)}, bf16[192,768]{1,0:T(8,128)(2,1)}, u32[]{:S(2)}, u32[]{:S(2)}) collective-permute-start(bf16[192,768]{1,0:T(8,128)(2,1)} %get-tuple-element.269), channel_id=1, source_target_pairs={{0,2},{1,3},{2,0},{3,1},{4,6},{5,7},{6,4},{7,5},{8,10},{9,11},{10,... | collective-permute-start | bytes 884744 | tf_op jit(solution)/shard_map/ppermute | solution.py:263
  417.6 23.8 %collective-permute-start.42 = (bf16[192,768]{1,0:T(8,128)(2,1)}, bf16[192,768]{1,0:T(8,128)(2,1)}, u32[]{:S(2)}, u32[]{:S(2)}) collective-permute-start(bf16[192,768]{1,0:T(8,128)(2,1)} %get-tuple-element.270), channel_id=1, source_target_pairs={{0,4},{1,5},{2,6},{3,7},{4,0},{5,1},{6,2},{7,3},{8,12},{9,13},{10,... | collective-permute-start | bytes 884744 | tf_op jit(solution)/shard_map/ppermute | solution.py:263
  418.7 22.7 %collective-permute-start.43 = (bf16[192,768]{1,0:T(8,128)(2,1)S(1)}, bf16[192,768]{1,0:T(8,128)(2,1)}, u32[]{:S(2)}, u32[]{:S(2)}) collective-permute-start(bf16[192,768]{1,0:T(8,128)(2,1)S(1)} %get-tuple-element.271), channel_id=1, source_target_pairs={{0,6},{1,7},{2,4},{3,5},{4,2},{5,3},{6,0},{7,1},{8,14},{9,15},{10,... | collective-permute-start | bytes 884744 | tf_op jit(solution)/shard_map/ppermute | solution.py:263
  441.4 27.8 %all-to-all-start.3 = ((bf16[4,128,640]{1,2,0:T(8,128)(2,1)}), bf16[4,128,640]{1,2,0:T(8,128)(2,1)}, u32[]{:S(2)}, u32[]{:S(2)}) async-start(bf16[4,128,640]{1,2,0:T(8,128)(2,1)} %copy.104), calls=%async_computation.3 | async-start | bytes 1310720 | tf_op jit(solution)/shard_map/all_to_all | solution.py:907
  449.2 36.2 %collective-permute-start.46 = (bf16[192,768]{1,0:T(8,128)(2,1)S(1)}, bf16[192,768]{1,0:T(8,128)(2,1)}, u32[]{:S(2)}, u32[]{:S(2)}) collective-permute-start(bf16[192,768]{1,0:T(8,128)(2,1)S(1)} %select_convert_fusion.refs_0_), channel_id=1, source_target_pairs={{0,8},{8,16},{16,24},{24,0},{1,9},{9,17},{17,25},{25,1},{2,10},{10... | collective-permute-start | bytes 884744 | tf_op jit(solution)/shard_map/ppermute | solution.py:237
  449.8 41.9 %collective-permute-start.47 = (bf16[192,768]{1,0:T(8,128)(2,1)S(1)}, bf16[192,768]{1,0:T(8,128)(2,1)}, u32[]{:S(2)}, u32[]{:S(2)}) collective-permute-start(bf16[192,768]{1,0:T(8,128)(2,1)S(1)} %select_convert_fusion.refs_0_), channel_id=1, source_target_pairs={{0,16},{8,24},{16,0},{24,8},{1,17},{9,25},{17,1},{25,9},{2,18},{10... | collective-permute-start | bytes 884744 | tf_op jit(solution)/shard_map/ppermute | solution.py:237
  450.8 41.8 %collective-permute-start.48 = (bf16[192,768]{1,0:T(8,128)(2,1)S(1)}, bf16[192,768]{1,0:T(8,128)(2,1)}, u32[]{:S(2)}, u32[]{:S(2)}) collective-permute-start(bf16[192,768]{1,0:T(8,128)(2,1)S(1)} %select_convert_fusion.refs_0_), channel_id=1, source_target_pairs={{0,24},{8,0},{16,8},{24,16},{1,25},{9,1},{17,9},{25,17},{2,26},{10... | collective-permute-start | bytes 884744 | tf_op jit(solution)/shard_map/ppermute | solution.py:237
  465.3 29.6 %collective-permute-start.52 = (bf16[192,384]{1,0:T(8,128)(2,1)S(1)}, bf16[192,384]{1,0:T(8,128)(2,1)S(1)}, u32[]{:S(2)}, u32[]{:S(2)}) collective-permute-start(bf16[192,384]{1,0:T(8,128)(2,1)S(1)} %reduce_sum.208.refs_4_), channel_id=1, source_target_pairs={{0,8},{8,16},{16,24},{24,0},{1,9},{9,17},{17,25},{25,1},{2,10},{10... | collective-permute-start | bytes 442376 | tf_op jit(solution)/shard_map/ppermute | solution.py:237
  465.4 31.8 %collective-permute-start.53 = (bf16[192,384]{1,0:T(8,128)(2,1)S(1)}, bf16[192,384]{1,0:T(8,128)(2,1)S(1)}, u32[]{:S(2)}, u32[]{:S(2)}) collective-permute-start(bf16[192,384]{1,0:T(8,128)(2,1)S(1)} %reduce_sum.208.refs_4_), channel_id=1, source_target_pairs={{0,16},{8,24},{16,0},{24,8},{1,17},{9,25},{17,1},{25,9},{2,18},{10... | collective-permute-start | bytes 442376 | tf_op jit(solution)/shard_map/ppermute | solution.py:237
  (104 other events, 878.0 us)
Sparse Core Ops, SparseCore 0:
  10.8 28.3 all-gather.6
  41.2 47.8 all-gather.8
  91.5 58.2 all-gather.10
  152.2 52.2 all-gather.12
  290.1 42.0 all-gather.14

commit v14 on v13

--- a/solution.py
+++ b/solution.py
@@ -909,15 +909,9 @@
     head_cols = q_cols + kv_cols
     head_far, head_near = split_product(product_rows, product_columns, shard, shards)
     head_sums = pair_sums(head_near, hop(head_far, shards, 1), shard)
-    out_part = total_of(
-        after(send_chips(after(out_sums, product_columns), shards), head_sums)
-    ).astype(BF)
-    out_parts = lax.all_to_all(
-        out_part.reshape(part, seqs, q_cols), "seq", split_axis=1, concat_axis=1, tiled=True
-    )
     head_blocks = send_chips(head_sums, shards)
     head_part = total_of(after(head_blocks, steps[3]))
-    grad_normed = dot_nt(after(token_grads, head_part, out_parts), attn_full)
+    grad_normed = dot_nt(after(token_grads, head_part), attn_full)
     grad_tokens = grad_residual + root_back(inputs, root(inputs), grad_normed)
     base_cols = head_cols + experts
     plane_high, plane_low = two_parts(
@@ -931,10 +925,15 @@
     )
     head_part = by_rows(head_part.astype(BF))
     head_last = [by_rows(each) for each in send_out([head_part] * seqs, seqs)]
+    out_blocks = send_chips(after(out_sums, head_part), shards)
+    out_part = total_of(out_blocks).astype(BF)
+    out_parts = lax.all_to_all(
+        out_part.reshape(part, seqs, q_cols), "seq", split_axis=1, concat_axis=1, tiled=True
+    )
     out_own = by_rows(jnp.sum(out_parts.astype(F32), axis=1).astype(BF))
+    grad_gate_up, grad_gain_ffn = place_gate_up(after(steps, head_part), w_gate_up, gain_two, z)
+    out_own = after(out_own, grad_gate_up)
     out_last = [by_rows(each) for each in send_out([out_own] * seqs, seqs)]
-    grad_gate_up, grad_gain_ffn = place_gate_up(after(steps, head_part), w_gate_up, gain_two, z)
-    head_last, out_last = after((head_last, out_last), grad_gate_up)
     grad_query, grad_keyval, grad_out, grad_gain_attn, sums = place_heads(
         head_last, out_last, z, w_query, w_keyval, gain_one, q_cols, kv_cols
     )

time: 521 us -> 496 us (0.952)
  waiting for transfers between devices: 211 us -> 171 us
  starting transfers between devices: 97.3 us -> 108 us
    ppermute x28, waiting for transfers between devices: 55.5 us -> 39.8 us  [hop(): return lax.ppermute(block, 'fsdp', [(i, i ^ mask) for i in range(count)])]
    ppermute x21, waiting for transfers between devices: 122 us -> 109 us  [shift(): lax.ppermute(block, 'seq', [(i, (i + step) % count) for i in range(count)])]
    ppermute x3, waiting for transfers between devices: 19.5 us -> 7.13 us  [relay_step(): lax.ppermute(up, 'seq', [(i, i + 1) for i in range(count - 1)])]
    ppermute x21, starting transfers between devices: 30.8 us -> 39.4 us  [shift(): lax.ppermute(block, 'seq', [(i, (i + step) % count) for i in range(count)])]
    unnamed x208 -> x212, local copies, waits for them, and re-layouts: 23.7 us -> 25.2 us
  transfers between devices with their start and end apart: 64 -> 64, of which waited for: 34 -> 30; matrix products, arithmetic and copies ran while one was open for 10% -> 12% of each run, Pallas kernels for 16% -> 17%
where the time goes in v14:
time: 496 us; the launch traced here: 487 us
  waiting for transfers between devices  171 us (34%)
  starting transfers between devices  108 us (22%)
  Pallas kernels  101 us (20%)
  local copies, waits for them, and re-layouts  35.4 us (7%)
  other arithmetic  29.1 us (6%)
  matrix products  21.6 us (4%)
  between operations  21 us (4%)
    ppermute x21, waiting for transfers between devices, shift(): lax.ppermute(block, 'seq', [(i, (i + step) % count) for i in range(count)])  109 us
    ppermute x28, waiting for transfers between devices, hop(): return lax.ppermute(block, 'fsdp', [(i, i ^ mask) for i in range(count)])  39.8 us
    ppermute x21, starting transfers between devices, shift(): lax.ppermute(block, 'seq', [(i, (i + step) % count) for i in range(count)])  39.4 us
    pallas_call x2, Pallas kernels, flash_backward(): pl.pallas_call(functools.partial(backward_kernel, shards, seqs, rows, g,...  27.6 us
    ppermute x28, starting transfers between devices, hop(): return lax.ppermute(block, 'fsdp', [(i, i ^ mask) for i in range(count)])  26.5 us
    unnamed x212, local copies, waits for them, and re-layouts  25.2 us
    pallas_call x1, Pallas kernels, flash_forward(): pl.pallas_call(functools.partial(forward_kernel, shards, seqs, rows, loca...  19 us
    pallas_call x4, Pallas kernels, split_product(): pl.pallas_call(product_kernel, grid=(count // 2,), in_specs=[pl.BlockSpec...  14 us
  transfers between devices with their start and end apart: 64, of which 30 were waited for; matrix products, arithmetic and copies ran while one was open for 12% of the time, Pallas kernels for 17%

profile of v14, /device:TPU:12, one launch (start us, length us, event | category | flops | bytes accessed | tf_op | source)
XLA Modules:
  0.0 486.9 jit_solution(17796972398406850983)
XLA Ops:
  21.3 23.3 %collective-permute-done = bf16[136,1536]{1,0:T(8,128)(2,1)S(1)} collective-permute-done((bf16[136,1536]{1,0:T(8,128)(2,1)S(1)}, bf16[136,1536]{1,0:T(8,128)(2,1)S(1)}, u32[]{:S(2)}, u32[]{:S(2)}) %collective-permute-start) | collective-permute-done | bytes 417824 | tf_op jit(solution)/shard_map/ppermute | solution.py:237
  44.7 7.8 %collective-permute-done.1 = bf16[136,1536]{1,0:T(8,128)(2,1)S(1)} collective-permute-done((bf16[136,1536]{1,0:T(8,128)(2,1)S(1)}, bf16[136,1536]{1,0:T(8,128)(2,1)S(1)}, u32[]{:S(2)}, u32[]{:S(2)}) %collective-permute-start.1) | collective-permute-done | bytes 417824 | tf_op jit(solution)/shard_map/ppermute | solution.py:237
  62.8 7.3 %collective-permute-done.3.refs_1_ = bf16[528,256]{1,0:T(8,128)(2,1)S(1)} collective-permute-done((bf16[528,256]{1,0:T(8,128)(2,1)S(1)}, bf16[528,256]{1,0:T(8,128)(2,1)S(1)}, u32[]{:S(2)}, u32[]{:S(2)}) %collective-permute-start.3) | collective-permute-done | bytes 270368 | tf_op jit(solution)/shard_map/ppermute | solution.py:263
  70.1 7.5 %collective-permute-done.4.refs_2_ = bf16[528,256]{1,0:T(8,128)(2,1)S(1)} collective-permute-done((bf16[528,256]{1,0:T(8,128)(2,1)S(1)}, bf16[528,256]{1,0:T(8,128)(2,1)S(1)}, u32[]{:S(2)}, u32[]{:S(2)}) %collective-permute-start.4) | collective-permute-done | bytes 270368 | tf_op jit(solution)/shard_map/ppermute | solution.py:263
  77.6 3.2 collective-permute-done.5.refs_3_
  83.1 19.0 %shard_map.221 = (bf16[512,384]{1,0:T(8,128)(2,1)}, f32[512,384]{1,0:T(8,128)S(1)}, f32[512,384]{1,0:T(8,128)S(1)}) custom-call(bf16[528,256]{1,0:T(8,128)(2,1)S(1)} %maximum_maximum_fusion.1.refs_0_, bf16[528,256]{1,0:T(8,128)(2,1)S(1)} %collective-permute-done.3.refs_1_, bf16[528,256]{1,0:T(8,128)(2,1)S(1)} %collective-permute-done.4.refs_2_, ...), custom_call_target="tpu_custom_call" | custom-call | tf_op jit(solution)/shard_map/pallas_call | solution.py:114
  103.9 3.4 all-to-all-start
  108.2 8.7 %all-to-all-done = bf16[4,128,384]{2,1,0:T(8,128)(2,1)S(1)} async-done(((bf16[4,128,384]{2,1,0:T(8,128)(2,1)}), bf16[4,128,384]{2,1,0:T(8,128)(2,1)S(1)}, u32[]{:S(2)}, u32[]{:S(2)}) %all-to-all-start) | async-done | bytes 393248 | tf_op jit(solution)/shard_map/all_to_all | solution.py:796
  118.8 5.1 %multiply_reduce_fusion.5 = (f32[128]{0:T(128)S(1)}, f32[128,1536]{1,0:T(8,128)S(1)}) fusion(bf16[128,1536]{1,0:T(8,128)(2,1)S(1)} %bitcast.138, bf16[1536,1536]{0,1:T(8,128)(2,1)} %all-gather.9.cloned.1.call-done, bf16[128,1536]{1,0:T(8,128)(2,1)} %param.14), kind=kOutput, calls=%fused_computation.69 | convolution fusion | flops 604766080 | bytes 6291968 | tf_op jit(solution)/shard_map/dot_general | solution.py:24
  126.3 4.2 collective-permute-start.11
  136.2 15.1 %collective-permute-done.11.refs_2_ = bf16[96,1536]{1,0:T(8,128)(2,1)} collective-permute-done((bf16[96,1536]{1,0:T(8,128)(2,1)S(1)}, bf16[96,1536]{1,0:T(8,128)(2,1)}, u32[]{:S(2)}, u32[]{:S(2)}) %collective-permute-start.11) | collective-permute-done | bytes 294944 | tf_op jit(solution)/shard_map/ppermute | solution.py:237
  151.3 5.0 %collective-permute-done.12.refs_3_ = bf16[96,1536]{1,0:T(8,128)(2,1)} collective-permute-done((bf16[96,1536]{1,0:T(8,128)(2,1)S(1)}, bf16[96,1536]{1,0:T(8,128)(2,1)}, u32[]{:S(2)}, u32[]{:S(2)}) %collective-permute-start.12) | collective-permute-done | bytes 294944 | tf_op jit(solution)/shard_map/ppermute | solution.py:237
  156.3 8.8 %shard_map.222 = (bf16[384,1536]{1,0:T(8,128)(2,1)}, f32[384,2048]{1,0:T(8,128)}, bf16[384,1024]{1,0:T(8,128)(2,1)}, bf16[96,1536]{1,0:T(8,128)(2,1)}, bf16[96,1...) custom-call(bf16[96,1536]{1,0:T(8,128)(2,1)} %get-tuple-element.355.refs_0_, ...), custom_call_target="tpu_custom_call" | custom-call | tf_op jit(solution)/shard_map/pallas_call | solution.py:396
  168.5 19.4 %collective-permute-done.13 = bf16[96,1536]{1,0:T(8,128)(2,1)S(1)} collective-permute-done((bf16[96,1536]{1,0:T(8,128)(2,1)}, bf16[96,1536]{1,0:T(8,128)(2,1)S(1)}, u32[]{:S(2)}, u32[]{:S(2)}) %collective-permute-start.13) | collective-permute-done | bytes 294944 | tf_op jit(solution)/shard_map/ppermute | solution.py:237
  193.8 3.8 collective-permute-start.16
  197.6 4.2 collective-permute-start.17
  204.5 13.1 %collective-permute-done.16.refs_1_ = bf16[96,1536]{1,0:T(8,128)(2,1)S(1)} collective-permute-done((bf16[96,1536]{1,0:T(8,128)(2,1)S(1)}, bf16[96,1536]{1,0:T(8,128)(2,1)S(1)}, u32[]{:S(2)}, u32[]{:S(2)}) %collective-permute-start.16) | collective-permute-done | bytes 294944 | tf_op jit(solution)/shard_map/ppermute | solution.py:237
  217.6 4.3 collective-permute-done.17.refs_2_
  221.9 3.8 collective-permute-done.18.refs_3_
  226.4 9.9 %shard_map.223 = (bf16[384,1536]{1,0:T(8,128)(2,1)}, bf16[384,2048]{1,0:T(8,128)(2,1)}, bf16[96,1536]{1,0:T(8,128)(2,1)}, bf16[96,1536]{1,0:T(8,128)(2,1)}, bf16...) custom-call(bf16[96,1536]{1,0:T(8,128)(2,1)} %get-tuple-element.177.refs_0_, bf16[96,1536]{1,0:T(8,128)(2,1)} %copy-done.72, ...), custom_call_target="tpu_custom_call" | custom-call | tf_op jit(solution)/shard_map/pallas_call | solution.py:445
  243.8 4.8 shard_map.226
  252.1 3.1 collective-permute-start.24
  255.2 4.0 collective-permute-done.19
  270.7 7.6 %all-to-all-start.1 = ((bf16[128,4,384]{2,0,1:T(8,128)(2,1)}), bf16[128,4,384]{2,0,1:T(8,128)(2,1)}, u32[]{:S(2)}, u32[]{:S(2)}) async-start(bf16[128,4,384]{2,0,1:T(8,128)(2,1)} %bitcast.147), calls=%async_computation.1 | async-start | bytes 786432 | tf_op jit(solution)/shard_map/all_to_all | solution.py:872
  292.8 13.8 %shard_map.228 = (f32[512,192]{1,0:T(8,128)S(1)}, bf16[4,512,128]{2,1,0:T(8,128)(2,1)S(1)}, bf16[4,512,128]{2,1,0:T(8,128)(2,1)S(1)}) custom-call(bf16[8,528,256]{2,1,0:T(8,128)(2,1)S(1)} %copy-done.6, bf16[512,384]{1,0:T(8,128)(2,1)S(1)} %slice_multiply_fusion.refs_8_.refs_1_, f32[8,1,1024]{2,1,0:T(1,128)S(1)} %pad_maximum_fusion.3.refs_9_.refs_2_, ...), custom_call_target="tpu_custom_call" | custom-call | flops 999999995904 | tf_op jit(solution)/shard_map/pallas_call | solution.py:212
  306.7 5.6 %collective-permute-done.28 = bf16[192,2048]{1,0:T(8,128)(2,1)} collective-permute-done((bf16[192,2048]{1,0:T(8,128)(2,1)}, bf16[192,2048]{1,0:T(8,128)(2,1)}, u32[]{:S(2)}, u32[]{:S(2)}) %collective-permute-start.28) | collective-permute-done | bytes 786464 | tf_op jit(solution)/shard_map/ppermute | solution.py:263
  316.4 3.4 collective-permute-start.31
  319.8 3.6 collective-permute-start.32
  323.5 13.8 %shard_map.230 = (f32[512,192]{1,0:T(8,128)S(1)}, bf16[4,512,128]{2,1,0:T(8,128)(2,1)S(1)}, bf16[4,512,128]{2,1,0:T(8,128)(2,1)S(1)}) custom-call(bf16[8,528,256]{2,1,0:T(8,128)(2,1)S(1)} %copy-done.6, bf16[512,384]{1,0:T(8,128)(2,1)S(1)} %slice_multiply_fusion.refs_8_.refs_1_, f32[8,1,1024]{2,1,0:T(1,128)S(1)} %pad_maximum_fusion.3.refs_9_.refs_2_, ...), custom_call_target="tpu_custom_call" | custom-call | tf_op jit(solution)/shard_map/pallas_call | solution.py:212
  343.9 3.2 collective-permute-start.38
  347.1 3.5 collective-permute-start.39
  359.9 4.1 shard_map.232
  365.0 4.4 collective-permute-done.36.refs_4_
  371.7 3.7 shard_map.234
  377.9 3.6 collective-permute-start.45
  388.6 5.0 %all-to-all-start.3 = ((bf16[4,128,640]{1,2,0:T(8,128)(2,1)}), bf16[4,128,640]{1,2,0:T(8,128)(2,1)}, u32[]{:S(2)}, u32[]{:S(2)}) async-start(bf16[4,128,640]{1,2,0:T(8,128)(2,1)} %copy.104), calls=%async_computation.3 | async-start | bytes 1310720 | tf_op jit(solution)/shard_map/all_to_all | solution.py:907
  393.6 4.5 collective-permute-done.44.refs_3_
  398.0 3.2 collective-permute-done.45.refs_6_
  406.1 3.0 collective-permute-start.50
  410.2 5.3 %collective-permute-start.47 = (bf16[192,768]{1,0:T(8,128)(2,1)S(1)}, bf16[192,768]{1,0:T(8,128)(2,1)S(1)}, u32[]{:S(2)}, u32[]{:S(2)}) collective-permute-start(bf16[192,768]{1,0:T(8,128)(2,1)S(1)} %select_convert_fusion.refs_0_), channel_id=1, source_target_pairs={{0,16},{8,24},{16,0},{24,8},{1,17},{9,25},{17,1},{25,9},{2,18},{10... | collective-permute-start | bytes 884744 | tf_op jit(solution)/shard_map/ppermute | solution.py:237
  415.4 6.9 %collective-permute-done.51 = bf16[192,1536]{1,0:T(8,128)(2,1)} collective-permute-done((bf16[192,1536]{1,0:T(8,128)(2,1)}, bf16[192,1536]{1,0:T(8,128)(2,1)}, u32[]{:S(2)}, u32[]{:S(2)}) %collective-permute-start.51) | collective-permute-done | bytes 589856 | tf_op jit(solution)/shard_map/ppermute | solution.py:263
  422.4 6.3 %collective-permute-start.48 = (bf16[192,768]{1,0:T(8,128)(2,1)S(1)}, bf16[192,768]{1,0:T(8,128)(2,1)}, u32[]{:S(2)}, u32[]{:S(2)}) collective-permute-start(bf16[192,768]{1,0:T(8,128)(2,1)S(1)} %select_convert_fusion.refs_0_), channel_id=1, source_target_pairs={{0,24},{8,0},{16,8},{24,16},{1,25},{9,1},{17,9},{25,17},{2,26},{10... | collective-permute-start | bytes 884744 | tf_op jit(solution)/shard_map/ppermute | solution.py:237
  434.1 5.8 %all-to-all-start.2 = ((bf16[192,4,384]{2,0,1:T(8,128)(2,1)}), bf16[192,4,384]{2,0,1:T(8,128)(2,1)}, u32[]{:S(2)}, u32[]{:S(2)}) async-start(bf16[192,4,384]{2,0,1:T(8,128)(2,1)} %bitcast.136), calls=%async_computation.2 | async-start | bytes 1179648 | tf_op jit(solution)/shard_map/all_to_all | solution.py:930
  439.9 6.3 %fusion.27 = (f32[128]{0:T(128)S(1)}, f32[128]{0:T(128)S(1)}, f32[128,1536]{1,0:T(8,128)S(1)}) fusion(bf16[128,1536]{1,0:T(8,128)(2,1)S(1)} %copy-done.58, bf16[128,2560]{0,1:T(8,128)(2,1)} %bitcast.55, bf16[1536,2560]{1,0:T(8,128)(2,1)} %all-gather.13.cloned.1.call-done), kind=kOutput, calls=%fused_computation.47 | convolution fusion | flops 1007615744 | bytes 9700352 | tf_op jit(solution)/shard_map/dot_general | solution.py:28
  446.2 8.0 %shard_map.236 = (f32[4,192,2048]{2,1,0:T(8,128)}, f32[192,128]{1,0:T(8,128)S(1)}) custom-call(s32[1]{0:T(128)} %bitcast.33.place_ref, bf16[192,2048]{1,0:T(8,128)(2,1)S(1)} %add_convert_fusion.refs_0_, bf16[192,2048]{1,0:T(8,128)(2,1)} %collective-permute-done.31.refs_1_, bf16[192,2048]{1,0:T(8,128)(2,1)} %collective-permute-done.38.refs_2_, ...), custom_call_target="tpu_custom_call" | custom-call | tf_op jit(solution)/shard_map/pallas_call | solution.py:583
  461.0 3.6 convert_bitcast_fusion
  464.7 3.9 collective-permute-done.52.refs_5_
  472.3 3.1 shard_map.237
  (436 shorter events, 141.9 us)
Async XLA Ops:
  7.2 47.7 %all-gather.7.cloned.1.call-start = ((), (), s32[]{:S(2)}) async-start(), calls=%async_computation.4 | async-start | bytes 2211840 | tf_op jit(solution)/shard_map/all_gather | solution.py:720
  10.7 108.0 %all-gather.9.cloned.1.call-start = ((), (), s32[]{:S(2)}) async-start(), calls=%async_computation.5 | async-start | bytes 5308416 | tf_op jit(solution)/shard_map/all_gather | solution.py:747
  11.5 144.9 %all-gather.11.cloned.1.call-start = ((), (), s32[]{:S(2)}) async-start(), calls=%async_computation.6 | async-start | bytes 11059200 | tf_op jit(solution)/shard_map/all_gather | solution.py:762
  15.1 189.4 %all-gather.13.cloned.1.call-start = ((), (), s32[]{:S(2)}) async-start(), calls=%async_computation.7 | async-start | bytes 8847360 | tf_op jit(solution)/shard_map/all_gather | solution.py:775
  15.1 29.6 %collective-permute-start = (bf16[136,1536]{1,0:T(8,128)(2,1)S(1)}, bf16[136,1536]{1,0:T(8,128)(2,1)S(1)}, u32[]{:S(2)}, u32[]{:S(2)}) collective-permute-start(bf16[136,1536]{1,0:T(8,128)(2,1)S(1)} %fusion.36), channel_id=1, source_target_pairs={{0,8},{8,16},{16,24},{24,0},{1,9},{9,17},{17,25},{25,1},{2,10},{10... | collective-permute-start | bytes 1253384 | tf_op jit(solution)/shard_map/ppermute | solution.py:237
  16.7 35.8 %collective-permute-start.1 = (bf16[136,1536]{1,0:T(8,128)(2,1)S(1)}, bf16[136,1536]{1,0:T(8,128)(2,1)S(1)}, u32[]{:S(2)}, u32[]{:S(2)}) collective-permute-start(bf16[136,1536]{1,0:T(8,128)(2,1)S(1)} %fusion.36), channel_id=1, source_target_pairs={{0,16},{8,24},{16,0},{24,8},{1,17},{9,25},{17,1},{25,9},{2,18},{10... | collective-permute-start | bytes 1253384 | tf_op jit(solution)/shard_map/ppermute | solution.py:237
  18.0 36.3 %collective-permute-start.2 = (bf16[136,1536]{1,0:T(8,128)(2,1)S(1)}, bf16[136,1536]{1,0:T(8,128)(2,1)S(1)}, u32[]{:S(2)}, u32[]{:S(2)}) collective-permute-start(bf16[136,1536]{1,0:T(8,128)(2,1)S(1)} %fusion.36), channel_id=1, source_target_pairs={{0,24},{8,0},{16,8},{24,16},{1,25},{9,1},{17,9},{25,17},{2,26},{10... | collective-permute-start | bytes 1253384 | tf_op jit(solution)/shard_map/ppermute | solution.py:237
  60.6 16.9 %collective-permute-start.4 = (bf16[528,256]{1,0:T(8,128)(2,1)S(1)}, bf16[528,256]{1,0:T(8,128)(2,1)S(1)}, u32[]{:S(2)}, u32[]{:S(2)}) collective-permute-start(bf16[528,256]{1,0:T(8,128)(2,1)S(1)} %maximum_maximum_fusion.1.refs_0_), channel_id=1, source_target_pairs={{0,4},{1,5},{2,6},{3,7},{4,0},{5,1},{6,2},{7,3},{8,12},{9,13},{10,... | collective-permute-start | bytes 811016 | tf_op jit(solution)/shard_map/ppermute | solution.py:263
  61.1 19.7 %collective-permute-start.5 = (bf16[528,256]{1,0:T(8,128)(2,1)S(1)}, bf16[528,256]{1,0:T(8,128)(2,1)S(1)}, u32[]{:S(2)}, u32[]{:S(2)}) collective-permute-start(bf16[528,256]{1,0:T(8,128)(2,1)S(1)} %maximum_maximum_fusion.1.refs_0_), channel_id=1, source_target_pairs={{0,6},{1,7},{2,4},{3,5},{4,2},{5,3},{6,0},{7,1},{8,14},{9,15},{10,... | collective-permute-start | bytes 811016 | tf_op jit(solution)/shard_map/ppermute | solution.py:263
  62.7 19.4 %collective-permute-start.6 = (bf16[528,256]{1,0:T(8,128)(2,1)S(1)}, bf16[528,256]{1,0:T(8,128)(2,1)S(1)}, u32[]{:S(2)}, u32[]{:S(2)}) collective-permute-start(bf16[528,256]{1,0:T(8,128)(2,1)S(1)} %maximum_maximum_fusion.1.refs_0_), channel_id=1, source_target_pairs={{0,1},{1,0},{2,3},{3,2},{4,5},{5,4},{6,7},{7,6},{8,9},{9,8},{10,11... | collective-permute-start | bytes 811016 | tf_op jit(solution)/shard_map/ppermute | solution.py:263
  126.3 25.0 %collective-permute-start.11 = (bf16[96,1536]{1,0:T(8,128)(2,1)S(1)}, bf16[96,1536]{1,0:T(8,128)(2,1)}, u32[]{:S(2)}, u32[]{:S(2)}) collective-permute-start(bf16[96,1536]{1,0:T(8,128)(2,1)S(1)} %get-tuple-element.353), channel_id=1, source_target_pairs={{0,16},{8,24},{16,0},{24,8},{1,17},{9,25},{17,1},{25,9},{2,18},{10... | collective-permute-start | bytes 884744 | tf_op jit(solution)/shard_map/ppermute | solution.py:237
  130.4 25.9 %collective-permute-start.12 = (bf16[96,1536]{1,0:T(8,128)(2,1)S(1)}, bf16[96,1536]{1,0:T(8,128)(2,1)}, u32[]{:S(2)}, u32[]{:S(2)}) collective-permute-start(bf16[96,1536]{1,0:T(8,128)(2,1)S(1)} %get-tuple-element.352), channel_id=1, source_target_pairs={{0,24},{8,0},{16,8},{24,16},{1,25},{9,1},{17,9},{25,17},{2,26},{10... | collective-permute-start | bytes 884744 | tf_op jit(solution)/shard_map/ppermute | solution.py:237
  165.1 22.8 %collective-permute-start.13 = (bf16[96,1536]{1,0:T(8,128)(2,1)}, bf16[96,1536]{1,0:T(8,128)(2,1)S(1)}, u32[]{:S(2)}, u32[]{:S(2)}) collective-permute-start(bf16[96,1536]{1,0:T(8,128)(2,1)} %get-tuple-element.160), channel_id=1, source_target_pairs={{0,24},{8,0},{16,8},{24,16},{1,25},{9,1},{17,9},{25,17},{2,26},{10... | collective-permute-start | bytes 884744 | tf_op jit(solution)/shard_map/ppermute | solution.py:237
  165.2 22.7 %collective-permute-start.14 = (bf16[96,1536]{1,0:T(8,128)(2,1)}, bf16[96,1536]{1,0:T(8,128)(2,1)S(1)}, u32[]{:S(2)}, u32[]{:S(2)}) collective-permute-start(bf16[96,1536]{1,0:T(8,128)(2,1)} %get-tuple-element.161), channel_id=1, source_target_pairs={{0,16},{8,24},{16,0},{24,8},{1,17},{9,25},{17,1},{25,9},{2,18},{10... | collective-permute-start | bytes 884744 | tf_op jit(solution)/shard_map/ppermute | solution.py:237
  166.0 22.9 %collective-permute-start.15 = (bf16[96,1536]{1,0:T(8,128)(2,1)}, bf16[96,1536]{1,0:T(8,128)(2,1)S(1)}, u32[]{:S(2)}, u32[]{:S(2)}) collective-permute-start(bf16[96,1536]{1,0:T(8,128)(2,1)} %get-tuple-element.162), channel_id=1, source_target_pairs={{0,8},{8,16},{16,24},{24,0},{1,9},{9,17},{17,25},{25,1},{2,10},{10... | collective-permute-start | bytes 884744 | tf_op jit(solution)/shard_map/ppermute | solution.py:237
  193.8 23.7 %collective-permute-start.16 = (bf16[96,1536]{1,0:T(8,128)(2,1)S(1)}, bf16[96,1536]{1,0:T(8,128)(2,1)S(1)}, u32[]{:S(2)}, u32[]{:S(2)}) collective-permute-start(bf16[96,1536]{1,0:T(8,128)(2,1)S(1)} %get-tuple-element.350), channel_id=1, source_target_pairs={{0,8},{8,16},{16,24},{24,0},{1,9},{9,17},{17,25},{25,1},{2,10},{10... | collective-permute-start | bytes 884744 | tf_op jit(solution)/shard_map/ppermute | solution.py:237
  197.6 24.3 %collective-permute-start.17 = (bf16[96,1536]{1,0:T(8,128)(2,1)S(1)}, bf16[96,1536]{1,0:T(8,128)(2,1)S(1)}, u32[]{:S(2)}, u32[]{:S(2)}) collective-permute-start(bf16[96,1536]{1,0:T(8,128)(2,1)S(1)} %get-tuple-element.349), channel_id=1, source_target_pairs={{0,16},{8,24},{16,0},{24,8},{1,17},{9,25},{17,1},{25,9},{2,18},{10... | collective-permute-start | bytes 884744 | tf_op jit(solution)/shard_map/ppermute | solution.py:237
  201.8 23.9 %collective-permute-start.18 = (bf16[96,1536]{1,0:T(8,128)(2,1)S(1)}, bf16[96,1536]{1,0:T(8,128)(2,1)S(1)}, u32[]{:S(2)}, u32[]{:S(2)}) collective-permute-start(bf16[96,1536]{1,0:T(8,128)(2,1)S(1)} %get-tuple-element.348), channel_id=1, source_target_pairs={{0,24},{8,0},{16,8},{24,16},{1,25},{9,1},{17,9},{25,17},{2,26},{10... | collective-permute-start | bytes 884744 | tf_op jit(solution)/shard_map/ppermute | solution.py:237
  236.3 22.8 %collective-permute-start.19 = (bf16[96,1536]{1,0:T(8,128)(2,1)}, bf16[96,1536]{1,0:T(8,128)(2,1)S(1)}, u32[]{:S(2)}, u32[]{:S(2)}) collective-permute-start(bf16[96,1536]{1,0:T(8,128)(2,1)} %get-tuple-element.183), channel_id=1, source_target_pairs={{0,24},{8,0},{16,8},{24,16},{1,25},{9,1},{17,9},{25,17},{2,26},{10... | collective-permute-start | bytes 884744 | tf_op jit(solution)/shard_map/ppermute | solution.py:237
  236.4 23.8 %collective-permute-start.20 = (bf16[96,1536]{1,0:T(8,128)(2,1)}, bf16[96,1536]{1,0:T(8,128)(2,1)S(1)}, u32[]{:S(2)}, u32[]{:S(2)}) collective-permute-start(bf16[96,1536]{1,0:T(8,128)(2,1)} %get-tuple-element.184), channel_id=1, source_target_pairs={{0,16},{8,24},{16,0},{24,8},{1,17},{9,25},{17,1},{25,9},{2,18},{10... | collective-permute-start | bytes 884744 | tf_op jit(solution)/shard_map/ppermute | solution.py:237
  237.4 25.3 %collective-permute-start.21 = (bf16[96,1536]{1,0:T(8,128)(2,1)}, bf16[96,1536]{1,0:T(8,128)(2,1)S(1)}, u32[]{:S(2)}, u32[]{:S(2)}) collective-permute-start(bf16[96,1536]{1,0:T(8,128)(2,1)} %get-tuple-element.185), channel_id=1, source_target_pairs={{0,8},{8,16},{16,24},{24,0},{1,9},{9,17},{17,25},{25,1},{2,10},{10... | collective-permute-start | bytes 884744 | tf_op jit(solution)/shard_map/ppermute | solution.py:237
  248.6 17.8 %collective-permute-start.23 = (bf16[4,192,2048]{2,1,0:T(8,128)(2,1)S(1)}, bf16[4,192,2048]{2,1,0:T(8,128)(2,1)S(1)}, u32[]{:S(2)}, u32[]{:S(2)}) collective-permute-start(bf16[4,192,2048]{2,1,0:T(8,128)(2,1)S(1)} %get-tuple-element.209), channel_id=1, source_target_pairs={{0,1},{1,0},{2,3},{3,2},{4,5},{5,4},{6,7},{7,6},{8,9},{9,8},{10,11... | collective-permute-start | bytes 9437192 | tf_op jit(solution)/shard_map/ppermute | solution.py:263
  252.1 28.5 %collective-permute-start.24 = (bf16[192,1024]{1,0:T(8,128)(2,1)}, bf16[192,1024]{1,0:T(8,128)(2,1)}, u32[]{:S(2)}, u32[]{:S(2)}) collective-permute-start(bf16[192,1024]{1,0:T(8,128)(2,1)} %get-tuple-element.197), channel_id=1, source_target_pairs={{0,2},{1,3},{2,0},{3,1},{4,6},{5,7},{6,4},{7,5},{8,10},{9,11},{10,... | collective-permute-start | bytes 1179656 | tf_op jit(solution)/shard_map/ppermute | solution.py:263
  259.2 22.9 %collective-permute-start.25 = (bf16[192,1024]{1,0:T(8,128)(2,1)}, bf16[192,1024]{1,0:T(8,128)(2,1)}, u32[]{:S(2)}, u32[]{:S(2)}) collective-permute-start(bf16[192,1024]{1,0:T(8,128)(2,1)} %get-tuple-element.198), channel_id=1, source_target_pairs={{0,4},{1,5},{2,6},{3,7},{4,0},{5,1},{6,2},{7,3},{8,12},{9,13},{10,... | collective-permute-start | bytes 1179656 | tf_op jit(solution)/shard_map/ppermute | solution.py:263
  260.2 21.9 %collective-permute-start.26 = (bf16[192,1024]{1,0:T(8,128)(2,1)}, bf16[192,1024]{1,0:T(8,128)(2,1)}, u32[]{:S(2)}, u32[]{:S(2)}) collective-permute-start(bf16[192,1024]{1,0:T(8,128)(2,1)} %get-tuple-element.199), channel_id=1, source_target_pairs={{0,6},{1,7},{2,4},{3,5},{4,2},{5,3},{6,0},{7,1},{8,14},{9,15},{10,... | collective-permute-start | bytes 1179656 | tf_op jit(solution)/shard_map/ppermute | solution.py:263
  270.7 19.3 %all-to-all-start.1 = ((bf16[128,4,384]{2,0,1:T(8,128)(2,1)}), bf16[128,4,384]{2,0,1:T(8,128)(2,1)}, u32[]{:S(2)}, u32[]{:S(2)}) async-start(bf16[128,4,384]{2,0,1:T(8,128)(2,1)} %bitcast.147), calls=%async_computation.1 | async-start | bytes 786432 | tf_op jit(solution)/shard_map/all_to_all | solution.py:872
  278.3 65.1 %all-gather.15.cloned.1.call-start = ((), (), s32[]{:S(2)}) async-start(), calls=%async_computation.8 | async-start | bytes 1966080 | tf_op jit(solution)/shard_map/all_gather | solution.py:875
  278.3 28.4 %collective-permute-start.27 = (bf16[192,2048]{1,0:T(8,128)(2,1)}, bf16[192,2048]{1,0:T(8,128)(2,1)}, u32[]{:S(2)}, u32[]{:S(2)}) collective-permute-start(bf16[192,2048]{1,0:T(8,128)(2,1)} %copy-done.46), channel_id=1, source_target_pairs={{0,2},{1,3},{2,0},{3,1},{4,6},{5,7},{6,4},{7,5},{8,10},{9,11},{10,... | collective-permute-start | bytes 2359304 | tf_op jit(solution)/shard_map/ppermute | solution.py:263
  279.5 32.7 %collective-permute-start.28 = (bf16[192,2048]{1,0:T(8,128)(2,1)}, bf16[192,2048]{1,0:T(8,128)(2,1)}, u32[]{:S(2)}, u32[]{:S(2)}) collective-permute-start(bf16[192,2048]{1,0:T(8,128)(2,1)} %copy-done.45), channel_id=1, source_target_pairs={{0,4},{1,5},{2,6},{3,7},{4,0},{5,1},{6,2},{7,3},{8,12},{9,13},{10,... | collective-permute-start | bytes 2359304 | tf_op jit(solution)/shard_map/ppermute | solution.py:263
  280.6 33.6 %collective-permute-start.29 = (bf16[192,2048]{1,0:T(8,128)(2,1)}, bf16[192,2048]{1,0:T(8,128)(2,1)}, u32[]{:S(2)}, u32[]{:S(2)}) collective-permute-start(bf16[192,2048]{1,0:T(8,128)(2,1)} %copy-done.44), channel_id=1, source_target_pairs={{0,6},{1,7},{2,4},{3,5},{4,2},{5,3},{6,0},{7,1},{8,14},{9,15},{10,... | collective-permute-start | bytes 2359304 | tf_op jit(solution)/shard_map/ppermute | solution.py:263
  290.0 33.5 %collective-permute-start.30 = (bf16[4,192,1536]{2,1,0:T(8,128)(2,1)}, bf16[4,192,1536]{2,1,0:T(8,128)(2,1)}, u32[]{:S(2)}, u32[]{:S(2)}) collective-permute-start(bf16[4,192,1536]{2,1,0:T(8,128)(2,1)} %copy-done.43), channel_id=1, source_target_pairs={{0,1},{1,0},{2,3},{3,2},{4,5},{5,4},{6,7},{7,6},{8,9},{9,8},{10,11... | collective-permute-start | bytes 7077896 | tf_op jit(solution)/shard_map/ppermute | solution.py:263
  316.4 25.8 %collective-permute-start.31 = (bf16[192,2048]{1,0:T(8,128)(2,1)S(1)}, bf16[192,2048]{1,0:T(8,128)(2,1)}, u32[]{:S(2)}, u32[]{:S(2)}) collective-permute-start(bf16[192,2048]{1,0:T(8,128)(2,1)S(1)} %add_convert_fusion.refs_0_), channel_id=1, source_target_pairs={{0,8},{8,16},{16,24},{1,9},{9,17},{17,25},{2,10},{10,18},{18,26},{... | collective-permute-start | bytes 2359304 | tf_op jit(solution)/shard_map/ppermute | solution.py:251
  319.8 23.6 %collective-permute-start.32 = (bf16[192,2048]{1,0:T(8,128)(2,1)S(1)}, bf16[192,2048]{1,0:T(8,128)(2,1)}, u32[]{:S(2)}, u32[]{:S(2)}) collective-permute-start(bf16[192,2048]{1,0:T(8,128)(2,1)S(1)} %add_convert_fusion.refs_0_), channel_id=1, source_target_pairs={{8,0},{16,8},{24,16},{9,1},{17,9},{25,17},{10,2},{18,10},{26,18},{... | collective-permute-start | bytes 2359304 | tf_op jit(solution)/shard_map/ppermute | solution.py:252
  343.9 25.5 %collective-permute-start.38 = (bf16[192,2048]{1,0:T(8,128)(2,1)}, bf16[192,2048]{1,0:T(8,128)(2,1)}, u32[]{:S(2)}, u32[]{:S(2)}) collective-permute-start(bf16[192,2048]{1,0:T(8,128)(2,1)} %collective-permute-done.31.refs_1_), channel_id=1, source_target_pairs={{0,8},{8,16},{16,24},{1,9},{9,17},{17,25},{2,10},{10,18},{18,26},{... | collective-permute-start | bytes 2359304 | tf_op jit(solution)/shard_map/ppermute | solution.py:251
  347.1 22.3 %collective-permute-start.39 = (bf16[192,2048]{1,0:T(8,128)(2,1)}, bf16[192,2048]{1,0:T(8,128)(2,1)}, u32[]{:S(2)}, u32[]{:S(2)}) collective-permute-start(bf16[192,2048]{1,0:T(8,128)(2,1)} %collective-permute-done.32.refs_4_), channel_id=1, source_target_pairs={{8,0},{16,8},{24,16},{9,1},{17,9},{25,17},{10,2},{18,10},{26,18},{... | collective-permute-start | bytes 2359304 | tf_op jit(solution)/shard_map/ppermute | solution.py:252
  375.5 22.6 %collective-permute-start.44 = (bf16[192,2048]{1,0:T(8,128)(2,1)}, bf16[192,2048]{1,0:T(8,128)(2,1)S(1)}, u32[]{:S(2)}, u32[]{:S(2)}) collective-permute-start(bf16[192,2048]{1,0:T(8,128)(2,1)} %collective-permute-done.38.refs_2_), channel_id=1, source_target_pairs={{0,8},{8,16},{16,24},{1,9},{9,17},{17,25},{2,10},{10,18},{18,26},{... | collective-permute-start | bytes 2359304 | tf_op jit(solution)/shard_map/ppermute | solution.py:251
  377.9 23.4 %collective-permute-start.45 = (bf16[192,2048]{1,0:T(8,128)(2,1)}, bf16[192,2048]{1,0:T(8,128)(2,1)}, u32[]{:S(2)}, u32[]{:S(2)}) collective-permute-start(bf16[192,2048]{1,0:T(8,128)(2,1)} %collective-permute-done.39.refs_5_), channel_id=1, source_target_pairs={{8,0},{16,8},{24,16},{9,1},{17,9},{25,17},{10,2},{18,10},{26,18},{... | collective-permute-start | bytes 2359304 | tf_op jit(solution)/shard_map/ppermute | solution.py:252
  384.0 17.3 %collective-permute-start.41 = (bf16[192,768]{1,0:T(8,128)(2,1)}, bf16[192,768]{1,0:T(8,128)(2,1)}, u32[]{:S(2)}, u32[]{:S(2)}) collective-permute-start(bf16[192,768]{1,0:T(8,128)(2,1)} %get-tuple-element.258), channel_id=1, source_target_pairs={{0,2},{1,3},{2,0},{3,1},{4,6},{5,7},{6,4},{7,5},{8,10},{9,11},{10,... | collective-permute-start | bytes 884744 | tf_op jit(solution)/shard_map/ppermute | solution.py:263
  384.5 16.8 %collective-permute-start.42 = (bf16[192,768]{1,0:T(8,128)(2,1)S(1)}, bf16[192,768]{1,0:T(8,128)(2,1)}, u32[]{:S(2)}, u32[]{:S(2)}) collective-permute-start(bf16[192,768]{1,0:T(8,128)(2,1)S(1)} %get-tuple-element.259), channel_id=1, source_target_pairs={{0,4},{1,5},{2,6},{3,7},{4,0},{5,1},{6,2},{7,3},{8,12},{9,13},{10,... | collective-permute-start | bytes 884744 | tf_op jit(solution)/shard_map/ppermute | solution.py:263
  385.7 15.6 %collective-permute-start.43 = (bf16[192,768]{1,0:T(8,128)(2,1)S(1)}, bf16[192,768]{1,0:T(8,128)(2,1)}, u32[]{:S(2)}, u32[]{:S(2)}) collective-permute-start(bf16[192,768]{1,0:T(8,128)(2,1)S(1)} %get-tuple-element.260), channel_id=1, source_target_pairs={{0,6},{1,7},{2,4},{3,5},{4,2},{5,3},{6,0},{7,1},{8,14},{9,15},{10,... | collective-permute-start | bytes 884744 | tf_op jit(solution)/shard_map/ppermute | solution.py:263
  388.6 26.9 %all-to-all-start.3 = ((bf16[4,128,640]{1,2,0:T(8,128)(2,1)}), bf16[4,128,640]{1,2,0:T(8,128)(2,1)}, u32[]{:S(2)}, u32[]{:S(2)}) async-start(bf16[4,128,640]{1,2,0:T(8,128)(2,1)} %copy.104), calls=%async_computation.3 | async-start | bytes 1310720 | tf_op jit(solution)/shard_map/all_to_all | solution.py:907
  404.8 17.5 %collective-permute-start.51 = (bf16[192,1536]{1,0:T(8,128)(2,1)}, bf16[192,1536]{1,0:T(8,128)(2,1)}, u32[]{:S(2)}, u32[]{:S(2)}) collective-permute-start(bf16[192,1536]{1,0:T(8,128)(2,1)} %get-tuple-element.270), channel_id=1, source_target_pairs={{0,6},{1,7},{2,4},{3,5},{4,2},{5,3},{6,0},{7,1},{8,14},{9,15},{10,... | collective-permute-start | bytes 1769480 | tf_op jit(solution)/shard_map/ppermute | solution.py:263
  406.1 25.4 %collective-permute-start.50 = (bf16[192,1536]{1,0:T(8,128)(2,1)}, bf16[192,1536]{1,0:T(8,128)(2,1)}, u32[]{:S(2)}, u32[]{:S(2)}) collective-permute-start(bf16[192,1536]{1,0:T(8,128)(2,1)} %get-tuple-element.269), channel_id=1, source_target_pairs={{0,4},{1,5},{2,6},{3,7},{4,0},{5,1},{6,2},{7,3},{8,12},{9,13},{10,... | collective-permute-start | bytes 1769480 | tf_op jit(solution)/shard_map/ppermute | solution.py:263
  409.1 22.4 %collective-permute-start.49 = (bf16[192,1536]{1,0:T(8,128)(2,1)}, bf16[192,1536]{1,0:T(8,128)(2,1)}, u32[]{:S(2)}, u32[]{:S(2)}) collective-permute-start(bf16[192,1536]{1,0:T(8,128)(2,1)} %get-tuple-element.268), channel_id=1, source_target_pairs={{0,2},{1,3},{2,0},{3,1},{4,6},{5,7},{6,4},{7,5},{8,10},{9,11},{10,... | collective-permute-start | bytes 1769480 | tf_op jit(solution)/shard_map/ppermute | solution.py:263
  410.1 49.8 %collective-permute-start.46 = (bf16[192,768]{1,0:T(8,128)(2,1)S(1)}, bf16[192,768]{1,0:T(8,128)(2,1)S(1)}, u32[]{:S(2)}, u32[]{:S(2)}) collective-permute-start(bf16[192,768]{1,0:T(8,128)(2,1)S(1)} %select_convert_fusion.refs_0_), channel_id=1, source_target_pairs={{0,8},{8,16},{16,24},{24,0},{1,9},{9,17},{17,25},{25,1},{2,10},{10... | collective-permute-start | bytes 884744 | tf_op jit(solution)/shard_map/ppermute | solution.py:237
  410.2 54.5 %collective-permute-start.47 = (bf16[192,768]{1,0:T(8,128)(2,1)S(1)}, bf16[192,768]{1,0:T(8,128)(2,1)S(1)}, u32[]{:S(2)}, u32[]{:S(2)}) collective-permute-start(bf16[192,768]{1,0:T(8,128)(2,1)S(1)} %select_convert_fusion.refs_0_), channel_id=1, source_target_pairs={{0,16},{8,24},{16,0},{24,8},{1,17},{9,25},{17,1},{25,9},{2,18},{10... | collective-permute-start | bytes 884744 | tf_op jit(solution)/shard_map/ppermute | solution.py:237
  422.4 42.3 %collective-permute-start.48 = (bf16[192,768]{1,0:T(8,128)(2,1)S(1)}, bf16[192,768]{1,0:T(8,128)(2,1)}, u32[]{:S(2)}, u32[]{:S(2)}) collective-permute-start(bf16[192,768]{1,0:T(8,128)(2,1)S(1)} %select_convert_fusion.refs_0_), channel_id=1, source_target_pairs={{0,24},{8,0},{16,8},{24,16},{1,25},{9,1},{17,9},{25,17},{2,26},{10... | collective-permute-start | bytes 884744 | tf_op jit(solution)/shard_map/ppermute | solution.py:237
  434.1 21.3 %all-to-all-start.2 = ((bf16[192,4,384]{2,0,1:T(8,128)(2,1)}), bf16[192,4,384]{2,0,1:T(8,128)(2,1)}, u32[]{:S(2)}, u32[]{:S(2)}) async-start(bf16[192,4,384]{2,0,1:T(8,128)(2,1)} %bitcast.136), calls=%async_computation.2 | async-start | bytes 1179648 | tf_op jit(solution)/shard_map/all_to_all | solution.py:930
  (106 other events, 811.7 us)
Sparse Core Ops, SparseCore 0:
  10.8 28.3 all-gather.6
  41.2 47.8 all-gather.8
  91.5 58.2 all-gather.10
  152.2 52.2 all-gather.12
  290.1 42.1 all-gather.14

commit v15 on v12

--- a/solution.py
+++ b/solution.py
@@ -891,14 +891,20 @@
         grad_q.append(part_q)
         near.append(near_kv)
         far.append(far_kv)
-        held = after(head_grad, grad_gate_up_shard, out_there)
+        if g == 0:
+            out_sums = pair_sums(out_near, out_there, shard)
+        held = after(head_grad, grad_gate_up_shard, out_sums)
     steps[1] = after(steps[1], part_q)
     steps.append(relay_step(steps[1], seqs))
-    far = after(far, steps[1], grad_down)
+    out_blocks = after(send_chips(out_sums, shards), part_q)
+    far = after(far, steps[1], grad_down, out_blocks)
     pairs = kv_pair_sums(near, [hop(each, shards, 1) for each in far])
-    out_sums = pair_sums(out_near, after(out_there, pairs), shard)
+    out_part = total_of(after(out_blocks, pairs)).astype(BF)
+    out_parts = lax.all_to_all(
+        out_part.reshape(part, seqs, q_cols), "seq", split_axis=1, concat_axis=1, tiled=True
+    )
     sent_grads, product_columns = head_columns(
-        grad_q, after(send_chips(pairs, shards), out_sums, steps[2]), factor_local, ride_columns
+        grad_q, after(send_chips(pairs, shards), out_part, steps[2]), factor_local, ride_columns
     )
     steps[2] = after(steps[2], product_columns)
     while len(steps) < seqs:
@@ -908,12 +914,6 @@
     head_cols = q_cols + kv_cols
     head_far, head_near = split_product(product_rows, product_columns, shard, shards)
     head_sums = pair_sums(head_near, hop(head_far, shards, 1), shard)
-    out_part = total_of(
-        after(send_chips(after(out_sums, product_columns), shards), head_sums)
-    ).astype(BF)
-    out_parts = lax.all_to_all(
-        out_part.reshape(part, seqs, q_cols), "seq", split_axis=1, concat_axis=1, tiled=True
-    )
     head_blocks = send_chips(head_sums, shards)
     head_part = total_of(after(head_blocks, steps[3]))
     grad_normed = dot_nt(after(token_grads, head_part), attn_full)

time: 504 us -> 501 us (level)
  the two profiles are of different devices: /device:TPU:12 before, /device:TPU:0 now
where the time goes in v15:
time: 501 us; the launch traced here: 492 us
  waiting for transfers between devices  170 us (34%)
  starting transfers between devices  113 us (23%)
  Pallas kernels  101 us (20%)
  local copies, waits for them, and re-layouts  40 us (8%)
  other arithmetic  27.2 us (5%)
  between operations  21 us (4%)
  matrix products  20.7 us (4%)
    ppermute x18, waiting for transfers between devices, shift(): lax.ppermute(block, 'seq', [(i, (i + step) % count) for i in range(count)])  90.5 us
    ppermute x18, starting transfers between devices, shift(): lax.ppermute(block, 'seq', [(i, (i + step) % count) for i in range(count)])  45 us
    ppermute x28, waiting for transfers between devices, hop(): return lax.ppermute(block, 'fsdp', [(i, i ^ mask) for i in range(count)])  28.9 us
    unnamed x220, local copies, waits for them, and re-layouts  28 us
    pallas_call x2, Pallas kernels, flash_backward(): pl.pallas_call(functools.partial(backward_kernel, shards, seqs, rows, g,...  27.6 us
    ppermute x28, starting transfers between devices, hop(): return lax.ppermute(block, 'fsdp', [(i, i ^ mask) for i in range(count)])  25 us
    pallas_call x1, Pallas kernels, flash_forward(): pl.pallas_call(functools.partial(forward_kernel, shards, seqs, rows, loca...  19 us
    all_to_all x1, waiting for transfers between devices, local(): lax.all_to_all(sent_grads, 'seq', split_axis=0, concat_axis=1, tiled=True)  17.7 us
  transfers between devices with their start and end apart: 61, of which 23 were waited for; matrix products, arithmetic and copies ran while one was open for 11% of the time, Pallas kernels for 17%

profile of v15, /device:TPU:0, one launch (start us, length us, event | category | flops | bytes accessed | tf_op | source)
XLA Modules:
  0.0 492.3 jit_solution(11364872217678704015)
XLA Ops:
  15.1 3.1 collective-permute-start
  18.2 2.6 collective-permute-start.1
  23.7 7.1 %collective-permute-done = bf16[136,1536]{1,0:T(8,128)(2,1)S(1)} collective-permute-done((bf16[136,1536]{1,0:T(8,128)(2,1)S(1)}, bf16[136,1536]{1,0:T(8,128)(2,1)S(1)}, u32[]{:S(2)}, u32[]{:S(2)}) %collective-permute-start) | collective-permute-done | bytes 417824 | tf_op jit(solution)/shard_map/ppermute | solution.py:237
  30.8 17.1 %collective-permute-done.1 = bf16[136,1536]{1,0:T(8,128)(2,1)S(1)} collective-permute-done((bf16[136,1536]{1,0:T(8,128)(2,1)S(1)}, bf16[136,1536]{1,0:T(8,128)(2,1)S(1)}, u32[]{:S(2)}, u32[]{:S(2)}) %collective-permute-start.1) | collective-permute-done | bytes 417824 | tf_op jit(solution)/shard_map/ppermute | solution.py:237
  56.7 8.8 %collective-permute-done.3.refs_1_ = bf16[528,256]{1,0:T(8,128)(2,1)S(1)} collective-permute-done((bf16[528,256]{1,0:T(8,128)(2,1)S(1)}, bf16[528,256]{1,0:T(8,128)(2,1)S(1)}, u32[]{:S(2)}, u32[]{:S(2)}) %collective-permute-start.3) | collective-permute-done | bytes 270368 | tf_op jit(solution)/shard_map/ppermute | solution.py:263
  66.0 8.7 %collective-permute-done.5.refs_3_ = bf16[528,256]{1,0:T(8,128)(2,1)S(1)} collective-permute-done((bf16[528,256]{1,0:T(8,128)(2,1)S(1)}, bf16[528,256]{1,0:T(8,128)(2,1)S(1)}, u32[]{:S(2)}, u32[]{:S(2)}) %collective-permute-start.5) | collective-permute-done | bytes 270368 | tf_op jit(solution)/shard_map/ppermute | solution.py:263
  77.1 19.0 %shard_map.221 = (bf16[512,384]{1,0:T(8,128)(2,1)}, f32[512,384]{1,0:T(8,128)S(1)}, f32[512,384]{1,0:T(8,128)S(1)}) custom-call(bf16[528,256]{1,0:T(8,128)(2,1)S(1)} %maximum_maximum_fusion.1.refs_0_, bf16[528,256]{1,0:T(8,128)(2,1)S(1)} %collective-permute-done.3.refs_1_, bf16[528,256]{1,0:T(8,128)(2,1)S(1)} %collective-permute-done.4.refs_2_, ...), custom_call_target="tpu_custom_call" | custom-call | tf_op jit(solution)/shard_map/pallas_call | solution.py:114
  97.9 11.3 %all-to-all-start = ((bf16[4,128,384]{2,1,0:T(8,128)(2,1)}), bf16[4,128,384]{2,1,0:T(8,128)(2,1)S(1)}, u32[]{:S(2)}, u32[]{:S(2)}) async-start(bf16[4,128,384]{2,1,0:T(8,128)(2,1)} %bitcast.12), calls=%async_computation | async-start | bytes 786432 | tf_op jit(solution)/shard_map/all_to_all | solution.py:795
  110.7 10.7 %all-to-all-done = bf16[4,128,384]{2,1,0:T(8,128)(2,1)S(1)} async-done(((bf16[4,128,384]{2,1,0:T(8,128)(2,1)}), bf16[4,128,384]{2,1,0:T(8,128)(2,1)S(1)}, u32[]{:S(2)}, u32[]{:S(2)}) %all-to-all-start) | async-done | bytes 393248 | tf_op jit(solution)/shard_map/all_to_all | solution.py:795
  123.3 4.1 multiply_reduce_fusion.5
  135.5 6.3 %collective-permute-done.10.refs_1_ = bf16[96,1536]{1,0:T(8,128)(2,1)} collective-permute-done((bf16[96,1536]{1,0:T(8,128)(2,1)S(1)}, bf16[96,1536]{1,0:T(8,128)(2,1)}, u32[]{:S(2)}, u32[]{:S(2)}) %collective-permute-start.10) | collective-permute-done | bytes 294944 | tf_op jit(solution)/shard_map/ppermute | solution.py:237
  141.8 10.9 %collective-permute-done.11.refs_2_ = bf16[96,1536]{1,0:T(8,128)(2,1)} collective-permute-done((bf16[96,1536]{1,0:T(8,128)(2,1)S(1)}, bf16[96,1536]{1,0:T(8,128)(2,1)}, u32[]{:S(2)}, u32[]{:S(2)}) %collective-permute-start.11) | collective-permute-done | bytes 294944 | tf_op jit(solution)/shard_map/ppermute | solution.py:237
  152.7 8.7 %shard_map.222 = (bf16[384,1536]{1,0:T(8,128)(2,1)}, f32[384,2048]{1,0:T(8,128)}, bf16[384,1024]{1,0:T(8,128)(2,1)}, bf16[96,1536]{1,0:T(8,128)(2,1)}, bf16[96,1...) custom-call(bf16[96,1536]{1,0:T(8,128)(2,1)} %get-tuple-element.367.refs_0_, ...), custom_call_target="tpu_custom_call" | custom-call | tf_op jit(solution)/shard_map/pallas_call | solution.py:396
  161.4 6.4 %collective-permute-start.13 = (bf16[96,1536]{1,0:T(8,128)(2,1)}, bf16[96,1536]{1,0:T(8,128)(2,1)S(1)}, u32[]{:S(2)}, u32[]{:S(2)}) collective-permute-start(bf16[96,1536]{1,0:T(8,128)(2,1)} %get-tuple-element.166), channel_id=1, source_target_pairs={{0,24},{8,0},{16,8},{24,16},{1,25},{9,1},{17,9},{25,17},{2,26},{10... | collective-permute-start | bytes 884744 | tf_op jit(solution)/shard_map/ppermute | solution.py:237
  171.1 4.6 collective-permute-done.13
  175.7 20.1 %collective-permute-done.14 = bf16[96,1536]{1,0:T(8,128)(2,1)S(1)} collective-permute-done((bf16[96,1536]{1,0:T(8,128)(2,1)}, bf16[96,1536]{1,0:T(8,128)(2,1)S(1)}, u32[]{:S(2)}, u32[]{:S(2)}) %collective-permute-start.14) | collective-permute-done | bytes 294944 | tf_op jit(solution)/shard_map/ppermute | solution.py:237
  200.8 3.8 collective-permute-start.18
  206.3 6.2 %collective-permute-done.16.refs_1_ = bf16[96,1536]{1,0:T(8,128)(2,1)S(1)} collective-permute-done((bf16[96,1536]{1,0:T(8,128)(2,1)S(1)}, bf16[96,1536]{1,0:T(8,128)(2,1)S(1)}, u32[]{:S(2)}, u32[]{:S(2)}) %collective-permute-start.16) | collective-permute-done | bytes 294944 | tf_op jit(solution)/shard_map/ppermute | solution.py:237
  212.6 10.8 %collective-permute-done.17.refs_2_ = bf16[96,1536]{1,0:T(8,128)(2,1)S(1)} collective-permute-done((bf16[96,1536]{1,0:T(8,128)(2,1)S(1)}, bf16[96,1536]{1,0:T(8,128)(2,1)S(1)}, u32[]{:S(2)}, u32[]{:S(2)}) %collective-permute-start.17) | collective-permute-done | bytes 294944 | tf_op jit(solution)/shard_map/ppermute | solution.py:237
  224.2 9.9 %shard_map.223 = (bf16[384,1536]{1,0:T(8,128)(2,1)}, bf16[384,2048]{1,0:T(8,128)(2,1)}, bf16[96,1536]{1,0:T(8,128)(2,1)}, bf16[96,1536]{1,0:T(8,128)(2,1)}, bf16...) custom-call(bf16[96,1536]{1,0:T(8,128)(2,1)} %get-tuple-element.183.refs_0_, bf16[96,1536]{1,0:T(8,128)(2,1)} %copy-done.73, ...), custom_call_target="tpu_custom_call" | custom-call | tf_op jit(solution)/shard_map/pallas_call | solution.py:445
  234.2 6.2 %collective-permute-start.19 = (bf16[96,1536]{1,0:T(8,128)(2,1)}, bf16[96,1536]{1,0:T(8,128)(2,1)S(1)}, u32[]{:S(2)}, u32[]{:S(2)}) collective-permute-start(bf16[96,1536]{1,0:T(8,128)(2,1)} %get-tuple-element.189), channel_id=1, source_target_pairs={{0,24},{8,0},{16,8},{24,16},{1,25},{9,1},{17,9},{25,17},{2,26},{10... | collective-permute-start | bytes 884744 | tf_op jit(solution)/shard_map/ppermute | solution.py:237
  242.9 2.9 shard_map.224
  247.7 4.8 shard_map.226
  259.1 7.4 %collective-permute-done.20 = bf16[96,1536]{1,0:T(8,128)(2,1)S(1)} collective-permute-done((bf16[96,1536]{1,0:T(8,128)(2,1)}, bf16[96,1536]{1,0:T(8,128)(2,1)S(1)}, u32[]{:S(2)}, u32[]{:S(2)}) %collective-permute-start.20) | collective-permute-done | bytes 294944 | tf_op jit(solution)/shard_map/ppermute | solution.py:237
  277.1 4.1 all-to-all-start.1
  282.3 2.6 shard_map.229
  295.5 13.8 %shard_map.228 = (f32[512,192]{1,0:T(8,128)S(1)}, bf16[4,512,128]{2,1,0:T(8,128)(2,1)S(1)}, bf16[4,512,128]{2,1,0:T(8,128)(2,1)S(1)}) custom-call(bf16[8,528,256]{2,1,0:T(8,128)(2,1)S(1)} %copy-done.6, bf16[512,384]{1,0:T(8,128)(2,1)S(1)} %slice_multiply_fusion.refs_8_.refs_1_, f32[8,1,1024]{2,1,0:T(1,128)S(1)} %pad_maximum_fusion.4.refs_9_.refs_2_, ...), custom_call_target="tpu_custom_call" | custom-call | flops 999999995904 | tf_op jit(solution)/shard_map/pallas_call | solution.py:212
  309.4 6.6 %collective-permute-done.28 = bf16[192,2048]{1,0:T(8,128)(2,1)} collective-permute-done((bf16[192,2048]{1,0:T(8,128)(2,1)}, bf16[192,2048]{1,0:T(8,128)(2,1)}, u32[]{:S(2)}, u32[]{:S(2)}) %collective-permute-start.28) | collective-permute-done | bytes 786464 | tf_op jit(solution)/shard_map/ppermute | solution.py:263
  318.3 4.4 collective-permute-start.31
  324.3 3.0 shard_map.230
  331.8 13.8 %shard_map.231 = (f32[512,192]{1,0:T(8,128)S(1)}, bf16[4,512,128]{2,1,0:T(8,128)(2,1)S(1)}, bf16[4,512,128]{2,1,0:T(8,128)(2,1)S(1)}) custom-call(bf16[8,528,256]{2,1,0:T(8,128)(2,1)S(1)} %copy-done.7, bf16[512,384]{1,0:T(8,128)(2,1)S(1)} %slice_multiply_fusion.refs_8_.refs_1_, f32[8,1,1024]{2,1,0:T(1,128)S(1)} %pad_maximum_fusion.4.refs_9_.refs_2_, ...), custom_call_target="tpu_custom_call" | custom-call | tf_op jit(solution)/shard_map/pallas_call | solution.py:212
  348.1 3.5 collective-permute-done.34
  353.9 5.2 %collective-permute-start.41 = (bf16[192,2048]{1,0:T(8,128)(2,1)}, bf16[192,2048]{1,0:T(8,128)(2,1)}, u32[]{:S(2)}, u32[]{:S(2)}) collective-permute-start(bf16[192,2048]{1,0:T(8,128)(2,1)} %collective-permute-done.31.refs_1_), channel_id=1, source_target_pairs={{0,8},{8,16},{16,24},{1,9},{9,17},{17,25},{2,10},{10,18},{18,26},{... | collective-permute-start | bytes 2359304 | tf_op jit(solution)/shard_map/ppermute | solution.py:251
  369.3 6.1 %collective-permute-done.41.refs_2_ = bf16[192,2048]{1,0:T(8,128)(2,1)} collective-permute-done((bf16[192,2048]{1,0:T(8,128)(2,1)}, bf16[192,2048]{1,0:T(8,128)(2,1)}, u32[]{:S(2)}, u32[]{:S(2)}) %collective-permute-start.41) | collective-permute-done | bytes 786464 | tf_op jit(solution)/shard_map/ppermute | solution.py:251
  375.4 5.0 %collective-permute-done.42.refs_5_ = bf16[192,2048]{1,0:T(8,128)(2,1)} collective-permute-done((bf16[192,2048]{1,0:T(8,128)(2,1)}, bf16[192,2048]{1,0:T(8,128)(2,1)}, u32[]{:S(2)}, u32[]{:S(2)}) %collective-permute-start.42) | collective-permute-done | bytes 786464 | tf_op jit(solution)/shard_map/ppermute | solution.py:252
  381.6 4.4 shard_map.234
  388.0 4.3 all-to-all-start.2
  392.3 4.8 collective-permute-start.47
  409.6 4.2 all-to-all-start.3
  415.0 5.0 %collective-permute-done.47.refs_3_ = bf16[192,2048]{1,0:T(8,128)(2,1)} collective-permute-done((bf16[192,2048]{1,0:T(8,128)(2,1)}, bf16[192,2048]{1,0:T(8,128)(2,1)}, u32[]{:S(2)}, u32[]{:S(2)}) %collective-permute-start.47) | collective-permute-done | bytes 786464 | tf_op jit(solution)/shard_map/ppermute | solution.py:251
  420.0 2.6 collective-permute-done.48.refs_6_
  427.3 7.9 %collective-permute-start.49 = (bf16[192,1152]{1,0:T(8,128)(2,1)S(1)}, bf16[192,1152]{1,0:T(8,128)(2,1)}, u32[]{:S(2)}, u32[]{:S(2)}) collective-permute-start(bf16[192,1152]{1,0:T(8,128)(2,1)S(1)} %pad_maximum_fusion.refs_0_), channel_id=1, source_target_pairs={{0,8},{8,16},{16,24},{24,0},{1,9},{9,17},{17,25},{25,1},{2,10},{10... | collective-permute-start | bytes 1327112 | tf_op jit(solution)/shard_map/ppermute | solution.py:237
  435.3 3.6 collective-permute-start.50
  438.9 2.8 collective-permute-start.51
  441.7 17.7 %all-to-all-done.3 = bf16[4,128,640]{1,2,0:T(8,128)(2,1)} async-done(((bf16[4,128,640]{1,2,0:T(8,128)(2,1)}), bf16[4,128,640]{1,2,0:T(8,128)(2,1)}, u32[]{:S(2)}, u32[]{:S(2)}) %all-to-all-start.3) | async-done | bytes 655392 | tf_op jit(solution)/shard_map/all_to_all | solution.py:912
  459.5 6.3 %fusion.27 = (f32[128]{0:T(128)S(1)}, f32[128]{0:T(128)S(1)}, f32[128,1536]{1,0:T(8,128)S(1)}) fusion(bf16[128,1536]{1,0:T(8,128)(2,1)S(1)} %copy-done.55, bf16[128,2560]{0,1:T(8,128)(2,1)} %bitcast.55, bf16[1536,2560]{1,0:T(8,128)(2,1)} %all-gather.13.cloned.1.call-done), kind=kOutput, calls=%fused_computation.47 | convolution fusion | flops 1007615744 | bytes 9700352 | tf_op jit(solution)/shard_map/dot_general | solution.py:28
  466.9 8.3 %shard_map.236 = (f32[4,192,2048]{2,1,0:T(8,128)}, f32[192,128]{1,0:T(8,128)S(1)}) custom-call(s32[1]{0:T(128)} %bitcast.33.place_ref, bf16[192,2048]{1,0:T(8,128)(2,1)S(1)} %add_convert_fusion.refs_0_, bf16[192,2048]{1,0:T(8,128)(2,1)} %collective-permute-done.31.refs_1_, bf16[192,2048]{1,0:T(8,128)(2,1)} %collective-permute-done.41.refs_2_, ...), custom_call_target="tpu_custom_call" | custom-call | tf_op jit(solution)/shard_map/pallas_call | solution.py:583
  477.5 3.4 shard_map.237
  (439 shorter events, 126.1 us)
Async XLA Ops:
  7.2 41.4 %all-gather.7.cloned.1.call-start = ((), (), s32[]{:S(2)}) async-start(), calls=%async_computation.4 | async-start | bytes 2211840 | tf_op jit(solution)/shard_map/all_gather | solution.py:719
  10.7 112.6 %all-gather.9.cloned.1.call-start = ((), (), s32[]{:S(2)}) async-start(), calls=%async_computation.5 | async-start | bytes 5308416 | tf_op jit(solution)/shard_map/all_gather | solution.py:746
  11.5 141.2 %all-gather.11.cloned.1.call-start = ((), (), s32[]{:S(2)}) async-start(), calls=%async_computation.6 | async-start | bytes 11059200 | tf_op jit(solution)/shard_map/all_gather | solution.py:761
  15.1 191.3 %all-gather.13.cloned.1.call-start = ((), (), s32[]{:S(2)}) async-start(), calls=%async_computation.7 | async-start | bytes 8847360 | tf_op jit(solution)/shard_map/all_gather | solution.py:774
  15.1 15.7 %collective-permute-start = (bf16[136,1536]{1,0:T(8,128)(2,1)S(1)}, bf16[136,1536]{1,0:T(8,128)(2,1)S(1)}, u32[]{:S(2)}, u32[]{:S(2)}) collective-permute-start(bf16[136,1536]{1,0:T(8,128)(2,1)S(1)} %fusion.36), channel_id=1, source_target_pairs={{0,8},{8,16},{16,24},{24,0},{1,9},{9,17},{17,25},{25,1},{2,10},{10... | collective-permute-start | bytes 1253384 | tf_op jit(solution)/shard_map/ppermute | solution.py:237
  18.2 29.7 %collective-permute-start.1 = (bf16[136,1536]{1,0:T(8,128)(2,1)S(1)}, bf16[136,1536]{1,0:T(8,128)(2,1)S(1)}, u32[]{:S(2)}, u32[]{:S(2)}) collective-permute-start(bf16[136,1536]{1,0:T(8,128)(2,1)S(1)} %fusion.36), channel_id=1, source_target_pairs={{0,16},{8,24},{16,0},{24,8},{1,17},{9,25},{17,1},{25,9},{2,18},{10... | collective-permute-start | bytes 1253384 | tf_op jit(solution)/shard_map/ppermute | solution.py:237
  20.8 27.1 %collective-permute-start.2 = (bf16[136,1536]{1,0:T(8,128)(2,1)S(1)}, bf16[136,1536]{1,0:T(8,128)(2,1)S(1)}, u32[]{:S(2)}, u32[]{:S(2)}) collective-permute-start(bf16[136,1536]{1,0:T(8,128)(2,1)S(1)} %fusion.36), channel_id=1, source_target_pairs={{0,24},{8,0},{16,8},{24,16},{1,25},{9,1},{17,9},{25,17},{2,26},{10... | collective-permute-start | bytes 1253384 | tf_op jit(solution)/shard_map/ppermute | solution.py:237
  56.0 18.8 %collective-permute-start.5 = (bf16[528,256]{1,0:T(8,128)(2,1)S(1)}, bf16[528,256]{1,0:T(8,128)(2,1)S(1)}, u32[]{:S(2)}, u32[]{:S(2)}) collective-permute-start(bf16[528,256]{1,0:T(8,128)(2,1)S(1)} %maximum_maximum_fusion.1.refs_0_), channel_id=1, source_target_pairs={{0,6},{1,7},{2,4},{3,5},{4,2},{5,3},{6,0},{7,1},{8,14},{9,15},{10,... | collective-permute-start | bytes 811016 | tf_op jit(solution)/shard_map/ppermute | solution.py:263
  56.6 19.5 %collective-permute-start.6 = (bf16[528,256]{1,0:T(8,128)(2,1)S(1)}, bf16[528,256]{1,0:T(8,128)(2,1)S(1)}, u32[]{:S(2)}, u32[]{:S(2)}) collective-permute-start(bf16[528,256]{1,0:T(8,128)(2,1)S(1)} %maximum_maximum_fusion.1.refs_0_), channel_id=1, source_target_pairs={{0,1},{1,0},{2,3},{3,2},{4,5},{5,4},{6,7},{7,6},{8,9},{9,8},{10,11... | collective-permute-start | bytes 811016 | tf_op jit(solution)/shard_map/ppermute | solution.py:263
  97.9 23.5 %all-to-all-start = ((bf16[4,128,384]{2,1,0:T(8,128)(2,1)}), bf16[4,128,384]{2,1,0:T(8,128)(2,1)S(1)}, u32[]{:S(2)}, u32[]{:S(2)}) async-start(bf16[4,128,384]{2,1,0:T(8,128)(2,1)} %bitcast.12), calls=%async_computation | async-start | bytes 786432 | tf_op jit(solution)/shard_map/all_to_all | solution.py:795
  130.5 22.2 %collective-permute-start.11 = (bf16[96,1536]{1,0:T(8,128)(2,1)S(1)}, bf16[96,1536]{1,0:T(8,128)(2,1)}, u32[]{:S(2)}, u32[]{:S(2)}) collective-permute-start(bf16[96,1536]{1,0:T(8,128)(2,1)S(1)} %get-tuple-element.365), channel_id=1, source_target_pairs={{0,16},{8,24},{16,0},{24,8},{1,17},{9,25},{17,1},{25,9},{2,18},{10... | collective-permute-start | bytes 884744 | tf_op jit(solution)/shard_map/ppermute | solution.py:237
  133.0 19.6 %collective-permute-start.12 = (bf16[96,1536]{1,0:T(8,128)(2,1)S(1)}, bf16[96,1536]{1,0:T(8,128)(2,1)}, u32[]{:S(2)}, u32[]{:S(2)}) collective-permute-start(bf16[96,1536]{1,0:T(8,128)(2,1)S(1)} %get-tuple-element.364), channel_id=1, source_target_pairs={{0,24},{8,0},{16,8},{24,16},{1,25},{9,1},{17,9},{25,17},{2,26},{10... | collective-permute-start | bytes 884744 | tf_op jit(solution)/shard_map/ppermute | solution.py:237
  167.8 28.0 %collective-permute-start.14 = (bf16[96,1536]{1,0:T(8,128)(2,1)}, bf16[96,1536]{1,0:T(8,128)(2,1)S(1)}, u32[]{:S(2)}, u32[]{:S(2)}) collective-permute-start(bf16[96,1536]{1,0:T(8,128)(2,1)} %get-tuple-element.167), channel_id=1, source_target_pairs={{0,16},{8,24},{16,0},{24,8},{1,17},{9,25},{17,1},{25,9},{2,18},{10... | collective-permute-start | bytes 884744 | tf_op jit(solution)/shard_map/ppermute | solution.py:237
  169.8 26.0 %collective-permute-start.15 = (bf16[96,1536]{1,0:T(8,128)(2,1)}, bf16[96,1536]{1,0:T(8,128)(2,1)S(1)}, u32[]{:S(2)}, u32[]{:S(2)}) collective-permute-start(bf16[96,1536]{1,0:T(8,128)(2,1)} %get-tuple-element.168), channel_id=1, source_target_pairs={{0,8},{8,16},{16,24},{24,0},{1,9},{9,17},{17,25},{25,1},{2,10},{10... | collective-permute-start | bytes 884744 | tf_op jit(solution)/shard_map/ppermute | solution.py:237
  200.7 22.7 %collective-permute-start.17 = (bf16[96,1536]{1,0:T(8,128)(2,1)S(1)}, bf16[96,1536]{1,0:T(8,128)(2,1)S(1)}, u32[]{:S(2)}, u32[]{:S(2)}) collective-permute-start(bf16[96,1536]{1,0:T(8,128)(2,1)S(1)} %get-tuple-element.361), channel_id=1, source_target_pairs={{0,16},{8,24},{16,0},{24,8},{1,17},{9,25},{17,1},{25,9},{2,18},{10... | collective-permute-start | bytes 884744 | tf_op jit(solution)/shard_map/ppermute | solution.py:237
  200.8 22.7 %collective-permute-start.18 = (bf16[96,1536]{1,0:T(8,128)(2,1)S(1)}, bf16[96,1536]{1,0:T(8,128)(2,1)S(1)}, u32[]{:S(2)}, u32[]{:S(2)}) collective-permute-start(bf16[96,1536]{1,0:T(8,128)(2,1)S(1)} %get-tuple-element.360), channel_id=1, source_target_pairs={{0,24},{8,0},{16,8},{24,16},{1,25},{9,1},{17,9},{25,17},{2,26},{10... | collective-permute-start | bytes 884744 | tf_op jit(solution)/shard_map/ppermute | solution.py:237
  234.2 23.7 %collective-permute-start.19 = (bf16[96,1536]{1,0:T(8,128)(2,1)}, bf16[96,1536]{1,0:T(8,128)(2,1)S(1)}, u32[]{:S(2)}, u32[]{:S(2)}) collective-permute-start(bf16[96,1536]{1,0:T(8,128)(2,1)} %get-tuple-element.189), channel_id=1, source_target_pairs={{0,24},{8,0},{16,8},{24,16},{1,25},{9,1},{17,9},{25,17},{2,26},{10... | collective-permute-start | bytes 884744 | tf_op jit(solution)/shard_map/ppermute | solution.py:237
  240.3 26.2 %collective-permute-start.20 = (bf16[96,1536]{1,0:T(8,128)(2,1)}, bf16[96,1536]{1,0:T(8,128)(2,1)S(1)}, u32[]{:S(2)}, u32[]{:S(2)}) collective-permute-start(bf16[96,1536]{1,0:T(8,128)(2,1)} %get-tuple-element.190), channel_id=1, source_target_pairs={{0,16},{8,24},{16,0},{24,8},{1,17},{9,25},{17,1},{25,9},{2,18},{10... | collective-permute-start | bytes 884744 | tf_op jit(solution)/shard_map/ppermute | solution.py:237
  241.4 27.6 %collective-permute-start.21 = (bf16[96,1536]{1,0:T(8,128)(2,1)}, bf16[96,1536]{1,0:T(8,128)(2,1)S(1)}, u32[]{:S(2)}, u32[]{:S(2)}) collective-permute-start(bf16[96,1536]{1,0:T(8,128)(2,1)} %get-tuple-element.191), channel_id=1, source_target_pairs={{0,8},{8,16},{16,24},{24,0},{1,9},{9,17},{17,25},{25,1},{2,10},{10... | collective-permute-start | bytes 884744 | tf_op jit(solution)/shard_map/ppermute | solution.py:237
  252.5 20.3 %collective-permute-start.23 = (bf16[4,192,2048]{2,1,0:T(8,128)(2,1)S(1)}, bf16[4,192,2048]{2,1,0:T(8,128)(2,1)S(1)}, u32[]{:S(2)}, u32[]{:S(2)}) collective-permute-start(bf16[4,192,2048]{2,1,0:T(8,128)(2,1)S(1)} %get-tuple-element.215), channel_id=1, source_target_pairs={{0,1},{1,0},{2,3},{3,2},{4,5},{5,4},{6,7},{7,6},{8,9},{9,8},{10,11... | collective-permute-start | bytes 9437192 | tf_op jit(solution)/shard_map/ppermute | solution.py:263
  256.0 31.6 %collective-permute-start.24 = (bf16[192,1024]{1,0:T(8,128)(2,1)}, bf16[192,1024]{1,0:T(8,128)(2,1)}, u32[]{:S(2)}, u32[]{:S(2)}) collective-permute-start(bf16[192,1024]{1,0:T(8,128)(2,1)} %get-tuple-element.203), channel_id=1, source_target_pairs={{0,2},{1,3},{2,0},{3,1},{4,6},{5,7},{6,4},{7,5},{8,10},{9,11},{10,... | collective-permute-start | bytes 1179656 | tf_op jit(solution)/shard_map/ppermute | solution.py:263
  257.8 32.3 %collective-permute-start.25 = (bf16[192,1024]{1,0:T(8,128)(2,1)}, bf16[192,1024]{1,0:T(8,128)(2,1)}, u32[]{:S(2)}, u32[]{:S(2)}) collective-permute-start(bf16[192,1024]{1,0:T(8,128)(2,1)} %get-tuple-element.204), channel_id=1, source_target_pairs={{0,4},{1,5},{2,6},{3,7},{4,0},{5,1},{6,2},{7,3},{8,12},{9,13},{10,... | collective-permute-start | bytes 1179656 | tf_op jit(solution)/shard_map/ppermute | solution.py:263
  266.5 23.6 %collective-permute-start.26 = (bf16[192,1024]{1,0:T(8,128)(2,1)}, bf16[192,1024]{1,0:T(8,128)(2,1)}, u32[]{:S(2)}, u32[]{:S(2)}) collective-permute-start(bf16[192,1024]{1,0:T(8,128)(2,1)} %get-tuple-element.205), channel_id=1, source_target_pairs={{0,6},{1,7},{2,4},{3,5},{4,2},{5,3},{6,0},{7,1},{8,14},{9,15},{10,... | collective-permute-start | bytes 1179656 | tf_op jit(solution)/shard_map/ppermute | solution.py:263
  277.1 15.6 %all-to-all-start.1 = ((bf16[128,4,384]{2,0,1:T(8,128)(2,1)}), bf16[128,4,384]{2,0,1:T(8,128)(2,1)}, u32[]{:S(2)}, u32[]{:S(2)}) async-start(bf16[128,4,384]{2,0,1:T(8,128)(2,1)} %bitcast.148), calls=%async_computation.1 | async-start | bytes 786432 | tf_op jit(solution)/shard_map/all_to_all | solution.py:871
  281.2 72.2 %all-gather.15.cloned.1.call-start = ((), (), s32[]{:S(2)}) async-start(), calls=%async_computation.8 | async-start | bytes 1966080 | tf_op jit(solution)/shard_map/all_gather | solution.py:874
  281.2 28.2 %collective-permute-start.27 = (bf16[192,2048]{1,0:T(8,128)(2,1)}, bf16[192,2048]{1,0:T(8,128)(2,1)}, u32[]{:S(2)}, u32[]{:S(2)}) collective-permute-start(bf16[192,2048]{1,0:T(8,128)(2,1)} %copy-done.43), channel_id=1, source_target_pairs={{0,2},{1,3},{2,0},{3,1},{4,6},{5,7},{6,4},{7,5},{8,10},{9,11},{10,... | collective-permute-start | bytes 2359304 | tf_op jit(solution)/shard_map/ppermute | solution.py:263
  281.8 34.2 %collective-permute-start.28 = (bf16[192,2048]{1,0:T(8,128)(2,1)}, bf16[192,2048]{1,0:T(8,128)(2,1)}, u32[]{:S(2)}, u32[]{:S(2)}) collective-permute-start(bf16[192,2048]{1,0:T(8,128)(2,1)} %copy-done.42), channel_id=1, source_target_pairs={{0,4},{1,5},{2,6},{3,7},{4,0},{5,1},{6,2},{7,3},{8,12},{9,13},{10,... | collective-permute-start | bytes 2359304 | tf_op jit(solution)/shard_map/ppermute | solution.py:263
  287.7 28.4 %collective-permute-start.29 = (bf16[192,2048]{1,0:T(8,128)(2,1)}, bf16[192,2048]{1,0:T(8,128)(2,1)}, u32[]{:S(2)}, u32[]{:S(2)}) collective-permute-start(bf16[192,2048]{1,0:T(8,128)(2,1)} %copy-done.41), channel_id=1, source_target_pairs={{0,6},{1,7},{2,4},{3,5},{4,2},{5,3},{6,0},{7,1},{8,14},{9,15},{10,... | collective-permute-start | bytes 2359304 | tf_op jit(solution)/shard_map/ppermute | solution.py:263
  292.7 31.5 %collective-permute-start.30 = (bf16[4,192,1536]{2,1,0:T(8,128)(2,1)}, bf16[4,192,1536]{2,1,0:T(8,128)(2,1)}, u32[]{:S(2)}, u32[]{:S(2)}) collective-permute-start(bf16[4,192,1536]{2,1,0:T(8,128)(2,1)} %copy-done.40), channel_id=1, source_target_pairs={{0,1},{1,0},{2,3},{3,2},{4,5},{5,4},{6,7},{7,6},{8,9},{9,8},{10,11... | collective-permute-start | bytes 7077896 | tf_op jit(solution)/shard_map/ppermute | solution.py:263
  318.3 29.7 %collective-permute-start.31 = (bf16[192,2048]{1,0:T(8,128)(2,1)S(1)}, bf16[192,2048]{1,0:T(8,128)(2,1)}, u32[]{:S(2)}, u32[]{:S(2)}) collective-permute-start(bf16[192,2048]{1,0:T(8,128)(2,1)S(1)} %add_convert_fusion.refs_0_), channel_id=1, source_target_pairs={{0,8},{8,16},{16,24},{1,9},{9,17},{17,25},{2,10},{10,18},{18,26},{... | collective-permute-start | bytes 2359304 | tf_op jit(solution)/shard_map/ppermute | solution.py:251
  322.7 25.3 %collective-permute-start.32 = (bf16[192,2048]{1,0:T(8,128)(2,1)S(1)}, bf16[192,2048]{1,0:T(8,128)(2,1)}, u32[]{:S(2)}, u32[]{:S(2)}) collective-permute-start(bf16[192,2048]{1,0:T(8,128)(2,1)S(1)} %add_convert_fusion.refs_0_), channel_id=1, source_target_pairs={{8,0},{16,8},{24,16},{9,1},{17,9},{25,17},{10,2},{18,10},{26,18},{... | collective-permute-start | bytes 2359304 | tf_op jit(solution)/shard_map/ppermute | solution.py:252
  328.3 19.7 %collective-permute-start.33 = (bf16[192,1536]{1,0:T(8,128)(2,1)S(1)}, bf16[192,1536]{1,0:T(8,128)(2,1)S(1)}, u32[]{:S(2)}, u32[]{:S(2)}) collective-permute-start(bf16[192,1536]{1,0:T(8,128)(2,1)S(1)} %get-tuple-element.238), channel_id=1, source_target_pairs={{0,2},{1,3},{2,0},{3,1},{4,6},{5,7},{6,4},{7,5},{8,10},{9,11},{10,... | collective-permute-start | bytes 1769480 | tf_op jit(solution)/shard_map/ppermute | solution.py:263
  329.8 21.8 %collective-permute-start.34 = (bf16[192,1536]{1,0:T(8,128)(2,1)S(1)}, bf16[192,1536]{1,0:T(8,128)(2,1)S(1)}, u32[]{:S(2)}, u32[]{:S(2)}) collective-permute-start(bf16[192,1536]{1,0:T(8,128)(2,1)S(1)} %get-tuple-element.239), channel_id=1, source_target_pairs={{0,4},{1,5},{2,6},{3,7},{4,0},{5,1},{6,2},{7,3},{8,12},{9,13},{10,... | collective-permute-start | bytes 1769480 | tf_op jit(solution)/shard_map/ppermute | solution.py:263
  330.1 23.2 %collective-permute-start.35 = (bf16[192,1536]{1,0:T(8,128)(2,1)S(1)}, bf16[192,1536]{1,0:T(8,128)(2,1)}, u32[]{:S(2)}, u32[]{:S(2)}) collective-permute-start(bf16[192,1536]{1,0:T(8,128)(2,1)S(1)} %get-tuple-element.240), channel_id=1, source_target_pairs={{0,6},{1,7},{2,4},{3,5},{4,2},{5,3},{6,0},{7,1},{8,14},{9,15},{10,... | collective-permute-start | bytes 1769480 | tf_op jit(solution)/shard_map/ppermute | solution.py:263
  353.9 21.5 %collective-permute-start.41 = (bf16[192,2048]{1,0:T(8,128)(2,1)}, bf16[192,2048]{1,0:T(8,128)(2,1)}, u32[]{:S(2)}, u32[]{:S(2)}) collective-permute-start(bf16[192,2048]{1,0:T(8,128)(2,1)} %collective-permute-done.31.refs_1_), channel_id=1, source_target_pairs={{0,8},{8,16},{16,24},{1,9},{9,17},{17,25},{2,10},{10,18},{18,26},{... | collective-permute-start | bytes 2359304 | tf_op jit(solution)/shard_map/ppermute | solution.py:251
  359.0 21.4 %collective-permute-start.42 = (bf16[192,2048]{1,0:T(8,128)(2,1)}, bf16[192,2048]{1,0:T(8,128)(2,1)}, u32[]{:S(2)}, u32[]{:S(2)}) collective-permute-start(bf16[192,2048]{1,0:T(8,128)(2,1)} %collective-permute-done.32.refs_4_), channel_id=1, source_target_pairs={{8,0},{16,8},{24,16},{9,1},{17,9},{25,17},{10,2},{18,10},{26,18},{... | collective-permute-start | bytes 2359304 | tf_op jit(solution)/shard_map/ppermute | solution.py:252
  364.2 16.2 %collective-permute-start.38 = (bf16[512,256]{1,0:T(8,128)(2,1)S(1)}, bf16[512,256]{1,0:T(8,128)(2,1)S(1)}, u32[]{:S(2)}, u32[]{:S(2)}) collective-permute-start(bf16[512,256]{1,0:T(8,128)(2,1)S(1)} %get-tuple-element.256), channel_id=1, source_target_pairs={{0,2},{1,3},{2,0},{3,1},{4,6},{5,7},{6,4},{7,5},{8,10},{9,11},{10,... | collective-permute-start | bytes 786440 | tf_op jit(solution)/shard_map/ppermute | solution.py:263
  364.9 15.5 %collective-permute-start.39 = (bf16[512,256]{1,0:T(8,128)(2,1)S(1)}, bf16[512,256]{1,0:T(8,128)(2,1)S(1)}, u32[]{:S(2)}, u32[]{:S(2)}) collective-permute-start(bf16[512,256]{1,0:T(8,128)(2,1)S(1)} %get-tuple-element.257), channel_id=1, source_target_pairs={{0,4},{1,5},{2,6},{3,7},{4,0},{5,1},{6,2},{7,3},{8,12},{9,13},{10,... | collective-permute-start | bytes 786440 | tf_op jit(solution)/shard_map/ppermute | solution.py:263
  388.0 21.6 %all-to-all-start.2 = ((bf16[192,4,384]{2,0,1:T(8,128)(2,1)}), bf16[192,4,384]{2,0,1:T(8,128)(2,1)}, u32[]{:S(2)}, u32[]{:S(2)}) async-start(bf16[192,4,384]{2,0,1:T(8,128)(2,1)} %bitcast.147), calls=%async_computation.2 | async-start | bytes 1179648 | tf_op jit(solution)/shard_map/all_to_all | solution.py:903
  392.3 27.7 %collective-permute-start.47 = (bf16[192,2048]{1,0:T(8,128)(2,1)}, bf16[192,2048]{1,0:T(8,128)(2,1)}, u32[]{:S(2)}, u32[]{:S(2)}) collective-permute-start(bf16[192,2048]{1,0:T(8,128)(2,1)} %collective-permute-done.41.refs_2_), channel_id=1, source_target_pairs={{0,8},{8,16},{16,24},{1,9},{9,17},{17,25},{2,10},{10,18},{18,26},{... | collective-permute-start | bytes 2359304 | tf_op jit(solution)/shard_map/ppermute | solution.py:251
  397.0 25.6 %collective-permute-start.48 = (bf16[192,2048]{1,0:T(8,128)(2,1)}, bf16[192,2048]{1,0:T(8,128)(2,1)}, u32[]{:S(2)}, u32[]{:S(2)}) collective-permute-start(bf16[192,2048]{1,0:T(8,128)(2,1)} %collective-permute-done.42.refs_5_), channel_id=1, source_target_pairs={{8,0},{16,8},{24,16},{9,1},{17,9},{25,17},{10,2},{18,10},{26,18},{... | collective-permute-start | bytes 2359304 | tf_op jit(solution)/shard_map/ppermute | solution.py:252
  400.9 21.7 %collective-permute-start.44 = (bf16[192,768]{1,0:T(8,128)(2,1)}, bf16[192,768]{1,0:T(8,128)(2,1)S(1)}, u32[]{:S(2)}, u32[]{:S(2)}) collective-permute-start(bf16[192,768]{1,0:T(8,128)(2,1)} %get-tuple-element.271), channel_id=1, source_target_pairs={{0,2},{1,3},{2,0},{3,1},{4,6},{5,7},{6,4},{7,5},{8,10},{9,11},{10,... | collective-permute-start | bytes 884744 | tf_op jit(solution)/shard_map/ppermute | solution.py:263
  402.2 20.5 %collective-permute-start.45 = (bf16[192,768]{1,0:T(8,128)(2,1)}, bf16[192,768]{1,0:T(8,128)(2,1)S(1)}, u32[]{:S(2)}, u32[]{:S(2)}) collective-permute-start(bf16[192,768]{1,0:T(8,128)(2,1)} %get-tuple-element.272), channel_id=1, source_target_pairs={{0,4},{1,5},{2,6},{3,7},{4,0},{5,1},{6,2},{7,3},{8,12},{9,13},{10,... | collective-permute-start | bytes 884744 | tf_op jit(solution)/shard_map/ppermute | solution.py:263
  404.0 18.7 %collective-permute-start.46 = (bf16[192,768]{1,0:T(8,128)(2,1)S(1)}, bf16[192,768]{1,0:T(8,128)(2,1)S(1)}, u32[]{:S(2)}, u32[]{:S(2)}) collective-permute-start(bf16[192,768]{1,0:T(8,128)(2,1)S(1)} %get-tuple-element.273), channel_id=1, source_target_pairs={{0,6},{1,7},{2,4},{3,5},{4,2},{5,3},{6,0},{7,1},{8,14},{9,15},{10,... | collective-permute-start | bytes 884744 | tf_op jit(solution)/shard_map/ppermute | solution.py:263
  409.6 49.9 %all-to-all-start.3 = ((bf16[4,128,640]{1,2,0:T(8,128)(2,1)}), bf16[4,128,640]{1,2,0:T(8,128)(2,1)}, u32[]{:S(2)}, u32[]{:S(2)}) async-start(bf16[4,128,640]{1,2,0:T(8,128)(2,1)} %copy.104), calls=%async_computation.3 | async-start | bytes 1310720 | tf_op jit(solution)/shard_map/all_to_all | solution.py:912
  427.3 50.1 %collective-permute-start.49 = (bf16[192,1152]{1,0:T(8,128)(2,1)S(1)}, bf16[192,1152]{1,0:T(8,128)(2,1)}, u32[]{:S(2)}, u32[]{:S(2)}) collective-permute-start(bf16[192,1152]{1,0:T(8,128)(2,1)S(1)} %pad_maximum_fusion.refs_0_), channel_id=1, source_target_pairs={{0,8},{8,16},{16,24},{24,0},{1,9},{9,17},{17,25},{25,1},{2,10},{10... | collective-permute-start | bytes 1327112 | tf_op jit(solution)/shard_map/ppermute | solution.py:237
  435.3 42.2 %collective-permute-start.50 = (bf16[192,1152]{1,0:T(8,128)(2,1)S(1)}, bf16[192,1152]{1,0:T(8,128)(2,1)}, u32[]{:S(2)}, u32[]{:S(2)}) collective-permute-start(bf16[192,1152]{1,0:T(8,128)(2,1)S(1)} %pad_maximum_fusion.refs_0_), channel_id=1, source_target_pairs={{0,16},{8,24},{16,0},{24,8},{1,17},{9,25},{17,1},{25,9},{2,18},{10... | collective-permute-start | bytes 1327112 | tf_op jit(solution)/shard_map/ppermute | solution.py:237
  438.9 38.6 %collective-permute-start.51 = (bf16[192,1152]{1,0:T(8,128)(2,1)S(1)}, bf16[192,1152]{1,0:T(8,128)(2,1)}, u32[]{:S(2)}, u32[]{:S(2)}) collective-permute-start(bf16[192,1152]{1,0:T(8,128)(2,1)S(1)} %pad_maximum_fusion.refs_0_), channel_id=1, source_target_pairs={{0,24},{8,0},{16,8},{24,16},{1,25},{9,1},{17,9},{25,17},{2,26},{10... | collective-permute-start | bytes 1327112 | tf_op jit(solution)/shard_map/ppermute | solution.py:237
  (107 other events, 887.7 us)
Sparse Core Ops, SparseCore 0:
  10.8 30.0 all-gather.6
  42.8 43.4 all-gather.8
  88.8 63.0 all-gather.10
  154.1 52.1 all-gather.12
  292.8 39.1 all-gather.14

commit v16 on v14

--- a/solution.py
+++ b/solution.py
@@ -121,7 +121,7 @@
             pltpu.VMEM((local_kv, stack, 2 * HD), F32),
             pltpu.VMEM((local_kv, stack, 2 * HD), F32),
         ],
-        compiler_params=pltpu.CompilerParams(vmem_limit_bytes=24 * 1024 * 1024),
+        compiler_params=pltpu.CompilerParams(vmem_limit_bytes=20 * 1024 * 1024),
         cost_estimate=pl.CostEstimate(
             flops=0,
             bytes_accessed=0,
@@ -224,7 +224,7 @@
             pltpu.VMEM((seqs, stack, 2 * HD), F32),
             pltpu.VMEM((2 * HD, shards * rows), F32),
         ],
-        compiler_params=pltpu.CompilerParams(vmem_limit_bytes=28 * 1024 * 1024),
+        compiler_params=pltpu.CompilerParams(vmem_limit_bytes=26 * 1024 * 1024),
         cost_estimate=pl.CostEstimate(
             flops=0 if g else 10**12,
             bytes_accessed=0,
@@ -320,7 +320,7 @@
         ],
         out_specs=[out_spec, out_spec],
         out_shape=[out, out],
-        compiler_params=pltpu.CompilerParams(vmem_limit_bytes=24 * 1024 * 1024),
+        compiler_params=pltpu.CompilerParams(vmem_limit_bytes=16 * 1024 * 1024),
         cost_estimate=pl.CostEstimate(flops=0, bytes_accessed=0, transcendentals=0),
     )((shard % 2).astype(jnp.int32).reshape(1), lhs, rhs)
 
@@ -347,7 +347,7 @@
         in_specs=[pl.BlockSpec(memory_space=pltpu.SMEM), block, block],
         out_specs=[out_spec] * chips,
         out_shape=[jax.ShapeDtypeStruct((part, cols), F32)] + [out] * (chips - 1),
-        compiler_params=pltpu.CompilerParams(vmem_limit_bytes=24 * 1024 * 1024),
+        compiler_params=pltpu.CompilerParams(vmem_limit_bytes=12 * 1024 * 1024),
         cost_estimate=pl.CostEstimate(flops=0, bytes_accessed=0, transcendentals=0),
     )((shard // 2).astype(jnp.int32).reshape(1), near, there)
 
@@ -474,7 +474,7 @@
         in_specs=[in_vmem] * (2 * heads),
         out_specs=[in_vmem] * chips,
         out_shape=[jax.ShapeDtypeStruct((rows, heads * cols), F32)] + [out] * (chips - 1),
-        compiler_params=pltpu.CompilerParams(vmem_limit_bytes=20 * 1024 * 1024),
+        compiler_params=pltpu.CompilerParams(vmem_limit_bytes=10 * 1024 * 1024),
         cost_estimate=pl.CostEstimate(flops=0, bytes_accessed=0, transcendentals=0),
     )(*near, *there)
 
@@ -511,7 +511,7 @@
             jax.ShapeDtypeStruct((rows, cols), BF),
             jax.ShapeDtypeStruct((rows + ride.shape[0], cols + LANES), BF),
         ],
-        compiler_params=pltpu.CompilerParams(vmem_limit_bytes=20 * 1024 * 1024),
+        compiler_params=pltpu.CompilerParams(vmem_limit_bytes=14 * 1024 * 1024),
         cost_estimate=pl.CostEstimate(flops=0, bytes_accessed=0, transcendentals=0),
     )(*queries, *sums, factor, ride)
 
@@ -598,7 +598,7 @@
                 jax.ShapeDtypeStruct((part, LANES), F32),
             ],
             scratch_shapes=[pltpu.VMEM((part, tile), F32)],
-            compiler_params=pltpu.CompilerParams(vmem_limit_bytes=28 * 1024 * 1024),
+            compiler_params=pltpu.CompilerParams(vmem_limit_bytes=18 * 1024 * 1024),
             cost_estimate=pl.CostEstimate(flops=0, bytes_accessed=0, transcendentals=0),
         )(place.astype(jnp.int32).reshape(1), *blocks, weight, gain)
         return out, sums[:, 0]
@@ -654,7 +654,7 @@
             in_specs=[pl.BlockSpec(memory_space=pltpu.SMEM)] + [in_vmem] * (2 * count + 3),
             out_specs=[in_vmem] * 5,
             out_shape=[wide, narrow, wide, lanes, lanes],
-            compiler_params=pltpu.CompilerParams(vmem_limit_bytes=24 * 1024 * 1024),
+            compiler_params=pltpu.CompilerParams(vmem_limit_bytes=16 * 1024 * 1024),
             cost_estimate=pl.CostEstimate(flops=0, bytes_accessed=0, transcendentals=0),
         )(place.astype(jnp.int32).reshape(1), *blocks, *outs, w_query, w_keyval, gain)
         return query, keyval, out, base[:, 0], sums
@@ -931,9 +931,10 @@
         out_part.reshape(part, seqs, q_cols), "seq", split_axis=1, concat_axis=1, tiled=True
     )
     out_own = by_rows(jnp.sum(out_parts.astype(F32), axis=1).astype(BF))
-    grad_gate_up, grad_gain_ffn = place_gate_up(after(steps, head_part), w_gate_up, gain_two, z)
-    out_own = after(out_own, grad_gate_up)
     out_last = [by_rows(each) for each in send_out([out_own] * seqs, seqs)]
+    grad_gate_up, grad_gain_ffn = place_gate_up(
+        after(steps, out_last[1]), w_gate_up, gain_two, z
+    )
     grad_query, grad_keyval, grad_out, grad_gain_attn, sums = place_heads(
         head_last, out_last, z, w_query, w_keyval, gain_one, q_cols, kv_cols
     )

time: 496 us -> 505 us (1.018)
  waiting for transfers between devices: 171 us -> 178 us
    all_to_all x1, waiting for transfers between devices: 0.01 us -> 5.7 us  [local(): lax.all_to_all(out_part.reshape(part, seqs, q_cols), 'seq', split_axis=1,...]
    unnamed x212 -> x202, local copies, waits for them, and re-layouts: 25.2 us -> 27.9 us
  transfers between devices with their start and end apart: 64 -> 64, of which waited for: 30 -> 30; matrix products, arithmetic and copies ran while one was open for 12% -> 11% of each run, Pallas kernels for 17% -> 15%
where the time goes in v16:
time: 505 us; the launch traced here: 496 us
  waiting for transfers between devices  178 us (35%)
  starting transfers between devices  108 us (21%)
  Pallas kernels  102 us (20%)
  local copies, waits for them, and re-layouts  37.5 us (7%)
  other arithmetic  29 us (6%)
  matrix products  21.6 us (4%)
  between operations  20.9 us (4%)
    ppermute x21, waiting for transfers between devices, shift(): lax.ppermute(block, 'seq', [(i, (i + step) % count) for i in range(count)])  110 us
    ppermute x21, starting transfers between devices, shift(): lax.ppermute(block, 'seq', [(i, (i + step) % count) for i in range(count)])  40.7 us
    ppermute x28, waiting for transfers between devices, hop(): return lax.ppermute(block, 'fsdp', [(i, i ^ mask) for i in range(count)])  40.4 us
    unnamed x202, local copies, waits for them, and re-layouts  27.9 us
    pallas_call x2, Pallas kernels, flash_backward(): pl.pallas_call(functools.partial(backward_kernel, shards, seqs, rows, g,...  27.6 us
    ppermute x28, starting transfers between devices, hop(): return lax.ppermute(block, 'fsdp', [(i, i ^ mask) for i in range(count)])  25.2 us
    pallas_call x1, Pallas kernels, flash_forward(): pl.pallas_call(functools.partial(forward_kernel, shards, seqs, rows, loca...  19 us
    pallas_call x4, Pallas kernels, split_product(): pl.pallas_call(product_kernel, grid=(count // 2,), in_specs=[pl.BlockSpec...  14.1 us
  transfers between devices with their start and end apart: 64, of which 30 were waited for; matrix products, arithmetic and copies ran while one was open for 11% of the time, Pallas kernels for 15%

profile of v16, /device:TPU:12, one launch (start us, length us, event | category | flops | bytes accessed | tf_op | source)
XLA Modules:
  0.0 496.3 jit_solution(7704975123346571959)
XLA Ops:
  21.3 23.3 %collective-permute-done = bf16[136,1536]{1,0:T(8,128)(2,1)S(1)} collective-permute-done((bf16[136,1536]{1,0:T(8,128)(2,1)S(1)}, bf16[136,1536]{1,0:T(8,128)(2,1)S(1)}, u32[]{:S(2)}, u32[]{:S(2)}) %collective-permute-start) | collective-permute-done | bytes 417824 | tf_op jit(solution)/shard_map/ppermute | solution.py:237
  44.7 7.8 %collective-permute-done.1 = bf16[136,1536]{1,0:T(8,128)(2,1)S(1)} collective-permute-done((bf16[136,1536]{1,0:T(8,128)(2,1)S(1)}, bf16[136,1536]{1,0:T(8,128)(2,1)S(1)}, u32[]{:S(2)}, u32[]{:S(2)}) %collective-permute-start.1) | collective-permute-done | bytes 417824 | tf_op jit(solution)/shard_map/ppermute | solution.py:237
  62.8 7.3 %collective-permute-done.3.refs_1_ = bf16[528,256]{1,0:T(8,128)(2,1)S(1)} collective-permute-done((bf16[528,256]{1,0:T(8,128)(2,1)S(1)}, bf16[528,256]{1,0:T(8,128)(2,1)S(1)}, u32[]{:S(2)}, u32[]{:S(2)}) %collective-permute-start.3) | collective-permute-done | bytes 270368 | tf_op jit(solution)/shard_map/ppermute | solution.py:263
  70.1 7.5 %collective-permute-done.4.refs_2_ = bf16[528,256]{1,0:T(8,128)(2,1)S(1)} collective-permute-done((bf16[528,256]{1,0:T(8,128)(2,1)S(1)}, bf16[528,256]{1,0:T(8,128)(2,1)S(1)}, u32[]{:S(2)}, u32[]{:S(2)}) %collective-permute-start.4) | collective-permute-done | bytes 270368 | tf_op jit(solution)/shard_map/ppermute | solution.py:263
  77.6 3.2 collective-permute-done.5.refs_3_
  83.1 19.0 %shard_map.221 = (bf16[512,384]{1,0:T(8,128)(2,1)}, f32[512,384]{1,0:T(8,128)S(1)}, f32[512,384]{1,0:T(8,128)S(1)}) custom-call(bf16[528,256]{1,0:T(8,128)(2,1)S(1)} %maximum_maximum_fusion.1.refs_0_, bf16[528,256]{1,0:T(8,128)(2,1)S(1)} %collective-permute-done.3.refs_1_, bf16[528,256]{1,0:T(8,128)(2,1)S(1)} %collective-permute-done.4.refs_2_, ...), custom_call_target="tpu_custom_call" | custom-call | tf_op jit(solution)/shard_map/pallas_call | solution.py:114
  103.9 3.4 all-to-all-start
  108.2 8.8 %all-to-all-done = bf16[4,128,384]{2,1,0:T(8,128)(2,1)S(1)} async-done(((bf16[4,128,384]{2,1,0:T(8,128)(2,1)}), bf16[4,128,384]{2,1,0:T(8,128)(2,1)S(1)}, u32[]{:S(2)}, u32[]{:S(2)}) %all-to-all-start) | async-done | bytes 393248 | tf_op jit(solution)/shard_map/all_to_all | solution.py:796
  118.8 5.2 %multiply_reduce_fusion.5 = (f32[128]{0:T(128)S(1)}, f32[128,1536]{1,0:T(8,128)S(1)}) fusion(bf16[128,1536]{1,0:T(8,128)(2,1)S(1)} %bitcast.138, bf16[1536,1536]{0,1:T(8,128)(2,1)} %all-gather.9.cloned.1.call-done, bf16[128,1536]{1,0:T(8,128)(2,1)} %param.14), kind=kOutput, calls=%fused_computation.69 | convolution fusion | flops 604766080 | bytes 6291968 | tf_op jit(solution)/shard_map/dot_general | solution.py:24
  126.3 4.1 collective-permute-start.11
  136.3 15.2 %collective-permute-done.11.refs_2_ = bf16[96,1536]{1,0:T(8,128)(2,1)} collective-permute-done((bf16[96,1536]{1,0:T(8,128)(2,1)S(1)}, bf16[96,1536]{1,0:T(8,128)(2,1)}, u32[]{:S(2)}, u32[]{:S(2)}) %collective-permute-start.11) | collective-permute-done | bytes 294944 | tf_op jit(solution)/shard_map/ppermute | solution.py:237
  151.5 5.0 %collective-permute-done.12.refs_3_ = bf16[96,1536]{1,0:T(8,128)(2,1)} collective-permute-done((bf16[96,1536]{1,0:T(8,128)(2,1)S(1)}, bf16[96,1536]{1,0:T(8,128)(2,1)}, u32[]{:S(2)}, u32[]{:S(2)}) %collective-permute-start.12) | collective-permute-done | bytes 294944 | tf_op jit(solution)/shard_map/ppermute | solution.py:237
  156.5 8.8 %shard_map.222 = (bf16[384,1536]{1,0:T(8,128)(2,1)}, f32[384,2048]{1,0:T(8,128)}, bf16[384,1024]{1,0:T(8,128)(2,1)}, bf16[96,1536]{1,0:T(8,128)(2,1)}, bf16[96,1...) custom-call(bf16[96,1536]{1,0:T(8,128)(2,1)} %get-tuple-element.353.refs_0_, ...), custom_call_target="tpu_custom_call" | custom-call | tf_op jit(solution)/shard_map/pallas_call | solution.py:396
  168.7 19.4 %collective-permute-done.13 = bf16[96,1536]{1,0:T(8,128)(2,1)S(1)} collective-permute-done((bf16[96,1536]{1,0:T(8,128)(2,1)}, bf16[96,1536]{1,0:T(8,128)(2,1)S(1)}, u32[]{:S(2)}, u32[]{:S(2)}) %collective-permute-start.13) | collective-permute-done | bytes 294944 | tf_op jit(solution)/shard_map/ppermute | solution.py:237
  194.1 3.8 collective-permute-start.16
  198.0 4.2 collective-permute-start.17
  204.4 3.3 collective-permute-done.16.refs_1_
  207.7 14.7 %collective-permute-done.17.refs_2_ = bf16[96,1536]{1,0:T(8,128)(2,1)S(1)} collective-permute-done((bf16[96,1536]{1,0:T(8,128)(2,1)S(1)}, bf16[96,1536]{1,0:T(8,128)(2,1)S(1)}, u32[]{:S(2)}, u32[]{:S(2)}) %collective-permute-start.17) | collective-permute-done | bytes 294944 | tf_op jit(solution)/shard_map/ppermute | solution.py:237
  222.5 3.8 collective-permute-done.18.refs_3_
  226.9 9.9 %shard_map.223 = (bf16[384,1536]{1,0:T(8,128)(2,1)}, bf16[384,2048]{1,0:T(8,128)(2,1)}, bf16[96,1536]{1,0:T(8,128)(2,1)}, bf16[96,1536]{1,0:T(8,128)(2,1)}, bf16...) custom-call(bf16[96,1536]{1,0:T(8,128)(2,1)} %get-tuple-element.176.refs_0_, bf16[96,1536]{1,0:T(8,128)(2,1)} %copy-done.67, ...), custom_call_target="tpu_custom_call" | custom-call | tf_op jit(solution)/shard_map/pallas_call | solution.py:445
  244.3 4.9 shard_map.226
  256.2 3.5 collective-permute-done.19
  270.7 7.8 %all-to-all-start.1 = ((bf16[128,4,384]{2,0,1:T(8,128)(2,1)}), bf16[128,4,384]{2,0,1:T(8,128)(2,1)}, u32[]{:S(2)}, u32[]{:S(2)}) async-start(bf16[128,4,384]{2,0,1:T(8,128)(2,1)} %bitcast.147), calls=%async_computation.1 | async-start | bytes 786432 | tf_op jit(solution)/shard_map/all_to_all | solution.py:872
  292.8 13.8 %shard_map.228 = (f32[512,192]{1,0:T(8,128)S(1)}, bf16[4,512,128]{2,1,0:T(8,128)(2,1)S(1)}, bf16[4,512,128]{2,1,0:T(8,128)(2,1)S(1)}) custom-call(bf16[8,528,256]{2,1,0:T(8,128)(2,1)S(1)} %copy-done.6, bf16[512,384]{1,0:T(8,128)(2,1)S(1)} %slice_multiply_fusion.refs_8_.refs_1_, f32[8,1,1024]{2,1,0:T(1,128)S(1)} %pad_maximum_fusion.3.refs_9_.refs_2_, ...), custom_call_target="tpu_custom_call" | custom-call | flops 999999995904 | tf_op jit(solution)/shard_map/pallas_call | solution.py:212
  306.7 5.9 %collective-permute-done.28 = bf16[192,2048]{1,0:T(8,128)(2,1)} collective-permute-done((bf16[192,2048]{1,0:T(8,128)(2,1)}, bf16[192,2048]{1,0:T(8,128)(2,1)}, u32[]{:S(2)}, u32[]{:S(2)}) %collective-permute-start.28) | collective-permute-done | bytes 786464 | tf_op jit(solution)/shard_map/ppermute | solution.py:263
  316.4 3.4 collective-permute-start.31
  319.8 3.6 collective-permute-start.32
  323.5 13.8 %shard_map.230 = (f32[512,192]{1,0:T(8,128)S(1)}, bf16[4,512,128]{2,1,0:T(8,128)(2,1)S(1)}, bf16[4,512,128]{2,1,0:T(8,128)(2,1)S(1)}) custom-call(bf16[8,528,256]{2,1,0:T(8,128)(2,1)S(1)} %copy-done.6, bf16[512,384]{1,0:T(8,128)(2,1)S(1)} %slice_multiply_fusion.refs_8_.refs_1_, f32[8,1,1024]{2,1,0:T(1,128)S(1)} %pad_maximum_fusion.3.refs_9_.refs_2_, ...), custom_call_target="tpu_custom_call" | custom-call | tf_op jit(solution)/shard_map/pallas_call | solution.py:212
  347.1 3.5 collective-permute-start.39
  359.9 4.1 shard_map.232
  365.0 4.4 collective-permute-done.36.refs_4_
  371.7 3.7 shard_map.234
  377.9 3.6 collective-permute-start.45
  388.6 5.0 %all-to-all-start.3 = ((bf16[4,128,640]{1,2,0:T(8,128)(2,1)}), bf16[4,128,640]{1,2,0:T(8,128)(2,1)}, u32[]{:S(2)}, u32[]{:S(2)}) async-start(bf16[4,128,640]{1,2,0:T(8,128)(2,1)} %copy.103), calls=%async_computation.3 | async-start | bytes 1310720 | tf_op jit(solution)/shard_map/all_to_all | solution.py:907
  393.6 4.5 collective-permute-done.44.refs_3_
  398.1 3.3 collective-permute-done.45.refs_6_
  409.6 5.3 %collective-permute-start.47 = (bf16[192,768]{1,0:T(8,128)(2,1)S(1)}, bf16[192,768]{1,0:T(8,128)(2,1)}, u32[]{:S(2)}, u32[]{:S(2)}) collective-permute-start(bf16[192,768]{1,0:T(8,128)(2,1)S(1)} %select_convert_fusion.refs_0_), channel_id=1, source_target_pairs={{0,16},{8,24},{16,0},{24,8},{1,17},{9,25},{17,1},{25,9},{2,18},{10... | collective-permute-start | bytes 884744 | tf_op jit(solution)/shard_map/ppermute | solution.py:237
  414.8 7.6 %collective-permute-done.51 = bf16[192,1536]{1,0:T(8,128)(2,1)} collective-permute-done((bf16[192,1536]{1,0:T(8,128)(2,1)}, bf16[192,1536]{1,0:T(8,128)(2,1)}, u32[]{:S(2)}, u32[]{:S(2)}) %collective-permute-start.51) | collective-permute-done | bytes 589856 | tf_op jit(solution)/shard_map/ppermute | solution.py:263
  422.4 6.3 %collective-permute-start.48 = (bf16[192,768]{1,0:T(8,128)(2,1)S(1)}, bf16[192,768]{1,0:T(8,128)(2,1)}, u32[]{:S(2)}, u32[]{:S(2)}) collective-permute-start(bf16[192,768]{1,0:T(8,128)(2,1)S(1)} %select_convert_fusion.refs_0_), channel_id=1, source_target_pairs={{0,24},{8,0},{16,8},{24,16},{1,25},{9,1},{17,9},{25,17},{2,26},{10... | collective-permute-start | bytes 884744 | tf_op jit(solution)/shard_map/ppermute | solution.py:237
  434.1 5.8 %all-to-all-start.2 = ((bf16[192,4,384]{2,0,1:T(8,128)(2,1)}), bf16[192,4,384]{2,0,1:T(8,128)(2,1)}, u32[]{:S(2)}, u32[]{:S(2)}) async-start(bf16[192,4,384]{2,0,1:T(8,128)(2,1)} %bitcast.136), calls=%async_computation.2 | async-start | bytes 1179648 | tf_op jit(solution)/shard_map/all_to_all | solution.py:930
  439.9 6.2 %fusion.27 = (f32[128]{0:T(128)S(1)}, f32[128]{0:T(128)S(1)}, f32[128,1536]{1,0:T(8,128)S(1)}) fusion(bf16[128,1536]{1,0:T(8,128)(2,1)S(1)} %copy-done.54, bf16[128,2560]{0,1:T(8,128)(2,1)} %bitcast.54, bf16[1536,2560]{1,0:T(8,128)(2,1)} %all-gather.13.cloned.1.call-done), kind=kOutput, calls=%fused_computation.47 | convolution fusion | flops 1007615744 | bytes 9700352 | tf_op jit(solution)/shard_map/dot_general | solution.py:28
  447.3 5.7 %all-to-all-done.2 = bf16[192,4,384]{2,0,1:T(8,128)(2,1)} async-done(((bf16[192,4,384]{2,0,1:T(8,128)(2,1)}), bf16[192,4,384]{2,0,1:T(8,128)(2,1)}, u32[]{:S(2)}, u32[]{:S(2)}) %all-to-all-start.2) | async-done | bytes 589856 | tf_op jit(solution)/shard_map/all_to_all | solution.py:930
  455.7 4.3 collective-permute-start.53
  459.9 3.5 convert_bitcast_fusion
  463.4 4.6 collective-permute-done.53.refs_6_
  468.0 3.5 collective-permute-done.54.refs_7_
  471.5 3.3 shard_map.236
  478.6 8.0 %shard_map.237 = (f32[4,192,2048]{2,1,0:T(8,128)}, f32[192,128]{1,0:T(8,128)S(1)}) custom-call(s32[1]{0:T(128)} %bitcast.33.place_ref, bf16[192,2048]{1,0:T(8,128)(2,1)S(1)} %add_convert_fusion.refs_0_, bf16[192,2048]{1,0:T(8,128)(2,1)} %collective-permute-done.31.refs_1_, bf16[192,2048]{1,0:T(8,128)(2,1)} %collective-permute-done.38.refs_2_, ...), custom_call_target="tpu_custom_call" | custom-call | tf_op jit(solution)/shard_map/pallas_call | solution.py:583
  (426 shorter events, 145.0 us)
Async XLA Ops:
  7.2 47.7 %all-gather.7.cloned.1.call-start = ((), (), s32[]{:S(2)}) async-start(), calls=%async_computation.4 | async-start | bytes 2211840 | tf_op jit(solution)/shard_map/all_gather | solution.py:720
  10.7 108.1 %all-gather.9.cloned.1.call-start = ((), (), s32[]{:S(2)}) async-start(), calls=%async_computation.5 | async-start | bytes 5308416 | tf_op jit(solution)/shard_map/all_gather | solution.py:747
  11.5 145.0 %all-gather.11.cloned.1.call-start = ((), (), s32[]{:S(2)}) async-start(), calls=%async_computation.6 | async-start | bytes 11059200 | tf_op jit(solution)/shard_map/all_gather | solution.py:762
  15.1 189.4 %all-gather.13.cloned.1.call-start = ((), (), s32[]{:S(2)}) async-start(), calls=%async_computation.7 | async-start | bytes 8847360 | tf_op jit(solution)/shard_map/all_gather | solution.py:775
  15.1 29.6 %collective-permute-start = (bf16[136,1536]{1,0:T(8,128)(2,1)S(1)}, bf16[136,1536]{1,0:T(8,128)(2,1)S(1)}, u32[]{:S(2)}, u32[]{:S(2)}) collective-permute-start(bf16[136,1536]{1,0:T(8,128)(2,1)S(1)} %fusion.36), channel_id=1, source_target_pairs={{0,8},{8,16},{16,24},{24,0},{1,9},{9,17},{17,25},{25,1},{2,10},{10... | collective-permute-start | bytes 1253384 | tf_op jit(solution)/shard_map/ppermute | solution.py:237
  16.7 35.8 %collective-permute-start.1 = (bf16[136,1536]{1,0:T(8,128)(2,1)S(1)}, bf16[136,1536]{1,0:T(8,128)(2,1)S(1)}, u32[]{:S(2)}, u32[]{:S(2)}) collective-permute-start(bf16[136,1536]{1,0:T(8,128)(2,1)S(1)} %fusion.36), channel_id=1, source_target_pairs={{0,16},{8,24},{16,0},{24,8},{1,17},{9,25},{17,1},{25,9},{2,18},{10... | collective-permute-start | bytes 1253384 | tf_op jit(solution)/shard_map/ppermute | solution.py:237
  18.0 36.3 %collective-permute-start.2 = (bf16[136,1536]{1,0:T(8,128)(2,1)S(1)}, bf16[136,1536]{1,0:T(8,128)(2,1)S(1)}, u32[]{:S(2)}, u32[]{:S(2)}) collective-permute-start(bf16[136,1536]{1,0:T(8,128)(2,1)S(1)} %fusion.36), channel_id=1, source_target_pairs={{0,24},{8,0},{16,8},{24,16},{1,25},{9,1},{17,9},{25,17},{2,26},{10... | collective-permute-start | bytes 1253384 | tf_op jit(solution)/shard_map/ppermute | solution.py:237
  60.6 16.9 %collective-permute-start.4 = (bf16[528,256]{1,0:T(8,128)(2,1)S(1)}, bf16[528,256]{1,0:T(8,128)(2,1)S(1)}, u32[]{:S(2)}, u32[]{:S(2)}) collective-permute-start(bf16[528,256]{1,0:T(8,128)(2,1)S(1)} %maximum_maximum_fusion.1.refs_0_), channel_id=1, source_target_pairs={{0,4},{1,5},{2,6},{3,7},{4,0},{5,1},{6,2},{7,3},{8,12},{9,13},{10,... | collective-permute-start | bytes 811016 | tf_op jit(solution)/shard_map/ppermute | solution.py:263
  61.2 19.7 %collective-permute-start.5 = (bf16[528,256]{1,0:T(8,128)(2,1)S(1)}, bf16[528,256]{1,0:T(8,128)(2,1)S(1)}, u32[]{:S(2)}, u32[]{:S(2)}) collective-permute-start(bf16[528,256]{1,0:T(8,128)(2,1)S(1)} %maximum_maximum_fusion.1.refs_0_), channel_id=1, source_target_pairs={{0,6},{1,7},{2,4},{3,5},{4,2},{5,3},{6,0},{7,1},{8,14},{9,15},{10,... | collective-permute-start | bytes 811016 | tf_op jit(solution)/shard_map/ppermute | solution.py:263
  62.7 19.4 %collective-permute-start.6 = (bf16[528,256]{1,0:T(8,128)(2,1)S(1)}, bf16[528,256]{1,0:T(8,128)(2,1)S(1)}, u32[]{:S(2)}, u32[]{:S(2)}) collective-permute-start(bf16[528,256]{1,0:T(8,128)(2,1)S(1)} %maximum_maximum_fusion.1.refs_0_), channel_id=1, source_target_pairs={{0,1},{1,0},{2,3},{3,2},{4,5},{5,4},{6,7},{7,6},{8,9},{9,8},{10,11... | collective-permute-start | bytes 811016 | tf_op jit(solution)/shard_map/ppermute | solution.py:263
  126.3 25.1 %collective-permute-start.11 = (bf16[96,1536]{1,0:T(8,128)(2,1)S(1)}, bf16[96,1536]{1,0:T(8,128)(2,1)}, u32[]{:S(2)}, u32[]{:S(2)}) collective-permute-start(bf16[96,1536]{1,0:T(8,128)(2,1)S(1)} %get-tuple-element.351), channel_id=1, source_target_pairs={{0,16},{8,24},{16,0},{24,8},{1,17},{9,25},{17,1},{25,9},{2,18},{10... | collective-permute-start | bytes 884744 | tf_op jit(solution)/shard_map/ppermute | solution.py:237
  130.4 26.1 %collective-permute-start.12 = (bf16[96,1536]{1,0:T(8,128)(2,1)S(1)}, bf16[96,1536]{1,0:T(8,128)(2,1)}, u32[]{:S(2)}, u32[]{:S(2)}) collective-permute-start(bf16[96,1536]{1,0:T(8,128)(2,1)S(1)} %get-tuple-element.350), channel_id=1, source_target_pairs={{0,24},{8,0},{16,8},{24,16},{1,25},{9,1},{17,9},{25,17},{2,26},{10... | collective-permute-start | bytes 884744 | tf_op jit(solution)/shard_map/ppermute | solution.py:237
  165.3 22.8 %collective-permute-start.13 = (bf16[96,1536]{1,0:T(8,128)(2,1)}, bf16[96,1536]{1,0:T(8,128)(2,1)S(1)}, u32[]{:S(2)}, u32[]{:S(2)}) collective-permute-start(bf16[96,1536]{1,0:T(8,128)(2,1)} %get-tuple-element.159), channel_id=1, source_target_pairs={{0,24},{8,0},{16,8},{24,16},{1,25},{9,1},{17,9},{25,17},{2,26},{10... | collective-permute-start | bytes 884744 | tf_op jit(solution)/shard_map/ppermute | solution.py:237
  165.4 22.7 %collective-permute-start.14 = (bf16[96,1536]{1,0:T(8,128)(2,1)}, bf16[96,1536]{1,0:T(8,128)(2,1)S(1)}, u32[]{:S(2)}, u32[]{:S(2)}) collective-permute-start(bf16[96,1536]{1,0:T(8,128)(2,1)} %get-tuple-element.160), channel_id=1, source_target_pairs={{0,16},{8,24},{16,0},{24,8},{1,17},{9,25},{17,1},{25,9},{2,18},{10... | collective-permute-start | bytes 884744 | tf_op jit(solution)/shard_map/ppermute | solution.py:237
  166.1 23.0 %collective-permute-start.15 = (bf16[96,1536]{1,0:T(8,128)(2,1)}, bf16[96,1536]{1,0:T(8,128)(2,1)S(1)}, u32[]{:S(2)}, u32[]{:S(2)}) collective-permute-start(bf16[96,1536]{1,0:T(8,128)(2,1)} %get-tuple-element.161), channel_id=1, source_target_pairs={{0,8},{8,16},{16,24},{24,0},{1,9},{9,17},{17,25},{25,1},{2,10},{10... | collective-permute-start | bytes 884744 | tf_op jit(solution)/shard_map/ppermute | solution.py:237
  194.1 13.6 %collective-permute-start.16 = (bf16[96,1536]{1,0:T(8,128)(2,1)S(1)}, bf16[96,1536]{1,0:T(8,128)(2,1)S(1)}, u32[]{:S(2)}, u32[]{:S(2)}) collective-permute-start(bf16[96,1536]{1,0:T(8,128)(2,1)S(1)} %get-tuple-element.348), channel_id=1, source_target_pairs={{0,8},{8,16},{16,24},{24,0},{1,9},{9,17},{17,25},{25,1},{2,10},{10... | collective-permute-start | bytes 884744 | tf_op jit(solution)/shard_map/ppermute | solution.py:237
  198.0 24.5 %collective-permute-start.17 = (bf16[96,1536]{1,0:T(8,128)(2,1)S(1)}, bf16[96,1536]{1,0:T(8,128)(2,1)S(1)}, u32[]{:S(2)}, u32[]{:S(2)}) collective-permute-start(bf16[96,1536]{1,0:T(8,128)(2,1)S(1)} %get-tuple-element.347), channel_id=1, source_target_pairs={{0,16},{8,24},{16,0},{24,8},{1,17},{9,25},{17,1},{25,9},{2,18},{10... | collective-permute-start | bytes 884744 | tf_op jit(solution)/shard_map/ppermute | solution.py:237
  202.2 24.1 %collective-permute-start.18 = (bf16[96,1536]{1,0:T(8,128)(2,1)S(1)}, bf16[96,1536]{1,0:T(8,128)(2,1)S(1)}, u32[]{:S(2)}, u32[]{:S(2)}) collective-permute-start(bf16[96,1536]{1,0:T(8,128)(2,1)S(1)} %get-tuple-element.346), channel_id=1, source_target_pairs={{0,24},{8,0},{16,8},{24,16},{1,25},{9,1},{17,9},{25,17},{2,26},{10... | collective-permute-start | bytes 884744 | tf_op jit(solution)/shard_map/ppermute | solution.py:237
  236.9 22.8 %collective-permute-start.19 = (bf16[96,1536]{1,0:T(8,128)(2,1)}, bf16[96,1536]{1,0:T(8,128)(2,1)S(1)}, u32[]{:S(2)}, u32[]{:S(2)}) collective-permute-start(bf16[96,1536]{1,0:T(8,128)(2,1)} %get-tuple-element.182), channel_id=1, source_target_pairs={{0,24},{8,0},{16,8},{24,16},{1,25},{9,1},{17,9},{25,17},{2,26},{10... | collective-permute-start | bytes 884744 | tf_op jit(solution)/shard_map/ppermute | solution.py:237
  236.9 23.2 %collective-permute-start.20 = (bf16[96,1536]{1,0:T(8,128)(2,1)}, bf16[96,1536]{1,0:T(8,128)(2,1)S(1)}, u32[]{:S(2)}, u32[]{:S(2)}) collective-permute-start(bf16[96,1536]{1,0:T(8,128)(2,1)} %get-tuple-element.183), channel_id=1, source_target_pairs={{0,16},{8,24},{16,0},{24,8},{1,17},{9,25},{17,1},{25,9},{2,18},{10... | collective-permute-start | bytes 884744 | tf_op jit(solution)/shard_map/ppermute | solution.py:237
  237.9 24.7 %collective-permute-start.21 = (bf16[96,1536]{1,0:T(8,128)(2,1)}, bf16[96,1536]{1,0:T(8,128)(2,1)S(1)}, u32[]{:S(2)}, u32[]{:S(2)}) collective-permute-start(bf16[96,1536]{1,0:T(8,128)(2,1)} %get-tuple-element.184), channel_id=1, source_target_pairs={{0,8},{8,16},{16,24},{24,0},{1,9},{9,17},{17,25},{25,1},{2,10},{10... | collective-permute-start | bytes 884744 | tf_op jit(solution)/shard_map/ppermute | solution.py:237
  249.2 17.2 %collective-permute-start.23 = (bf16[4,192,2048]{2,1,0:T(8,128)(2,1)S(1)}, bf16[4,192,2048]{2,1,0:T(8,128)(2,1)S(1)}, u32[]{:S(2)}, u32[]{:S(2)}) collective-permute-start(bf16[4,192,2048]{2,1,0:T(8,128)(2,1)S(1)} %get-tuple-element.208), channel_id=1, source_target_pairs={{0,1},{1,0},{2,3},{3,2},{4,5},{5,4},{6,7},{7,6},{8,9},{9,8},{10,11... | collective-permute-start | bytes 9437192 | tf_op jit(solution)/shard_map/ppermute | solution.py:263
  253.6 27.5 %collective-permute-start.24 = (bf16[192,1024]{1,0:T(8,128)(2,1)}, bf16[192,1024]{1,0:T(8,128)(2,1)}, u32[]{:S(2)}, u32[]{:S(2)}) collective-permute-start(bf16[192,1024]{1,0:T(8,128)(2,1)} %get-tuple-element.196), channel_id=1, source_target_pairs={{0,2},{1,3},{2,0},{3,1},{4,6},{5,7},{6,4},{7,5},{8,10},{9,11},{10,... | collective-permute-start | bytes 1179656 | tf_op jit(solution)/shard_map/ppermute | solution.py:263
  259.7 22.3 %collective-permute-start.25 = (bf16[192,1024]{1,0:T(8,128)(2,1)}, bf16[192,1024]{1,0:T(8,128)(2,1)}, u32[]{:S(2)}, u32[]{:S(2)}) collective-permute-start(bf16[192,1024]{1,0:T(8,128)(2,1)} %get-tuple-element.197), channel_id=1, source_target_pairs={{0,4},{1,5},{2,6},{3,7},{4,0},{5,1},{6,2},{7,3},{8,12},{9,13},{10,... | collective-permute-start | bytes 1179656 | tf_op jit(solution)/shard_map/ppermute | solution.py:263
  260.2 21.9 %collective-permute-start.26 = (bf16[192,1024]{1,0:T(8,128)(2,1)}, bf16[192,1024]{1,0:T(8,128)(2,1)}, u32[]{:S(2)}, u32[]{:S(2)}) collective-permute-start(bf16[192,1024]{1,0:T(8,128)(2,1)} %get-tuple-element.198), channel_id=1, source_target_pairs={{0,6},{1,7},{2,4},{3,5},{4,2},{5,3},{6,0},{7,1},{8,14},{9,15},{10,... | collective-permute-start | bytes 1179656 | tf_op jit(solution)/shard_map/ppermute | solution.py:263
  270.7 19.3 %all-to-all-start.1 = ((bf16[128,4,384]{2,0,1:T(8,128)(2,1)}), bf16[128,4,384]{2,0,1:T(8,128)(2,1)}, u32[]{:S(2)}, u32[]{:S(2)}) async-start(bf16[128,4,384]{2,0,1:T(8,128)(2,1)} %bitcast.147), calls=%async_computation.1 | async-start | bytes 786432 | tf_op jit(solution)/shard_map/all_to_all | solution.py:872
  278.5 64.9 %all-gather.15.cloned.1.call-start = ((), (), s32[]{:S(2)}) async-start(), calls=%async_computation.8 | async-start | bytes 1966080 | tf_op jit(solution)/shard_map/all_gather | solution.py:875
  278.5 28.2 %collective-permute-start.27 = (bf16[192,2048]{1,0:T(8,128)(2,1)}, bf16[192,2048]{1,0:T(8,128)(2,1)}, u32[]{:S(2)}, u32[]{:S(2)}) collective-permute-start(bf16[192,2048]{1,0:T(8,128)(2,1)} %copy-done.42), channel_id=1, source_target_pairs={{0,2},{1,3},{2,0},{3,1},{4,6},{5,7},{6,4},{7,5},{8,10},{9,11},{10,... | collective-permute-start | bytes 2359304 | tf_op jit(solution)/shard_map/ppermute | solution.py:263
  279.5 33.0 %collective-permute-start.28 = (bf16[192,2048]{1,0:T(8,128)(2,1)}, bf16[192,2048]{1,0:T(8,128)(2,1)}, u32[]{:S(2)}, u32[]{:S(2)}) collective-permute-start(bf16[192,2048]{1,0:T(8,128)(2,1)} %copy-done.41), channel_id=1, source_target_pairs={{0,4},{1,5},{2,6},{3,7},{4,0},{5,1},{6,2},{7,3},{8,12},{9,13},{10,... | collective-permute-start | bytes 2359304 | tf_op jit(solution)/shard_map/ppermute | solution.py:263
  281.1 33.1 %collective-permute-start.29 = (bf16[192,2048]{1,0:T(8,128)(2,1)}, bf16[192,2048]{1,0:T(8,128)(2,1)}, u32[]{:S(2)}, u32[]{:S(2)}) collective-permute-start(bf16[192,2048]{1,0:T(8,128)(2,1)} %copy-done.40), channel_id=1, source_target_pairs={{0,6},{1,7},{2,4},{3,5},{4,2},{5,3},{6,0},{7,1},{8,14},{9,15},{10,... | collective-permute-start | bytes 2359304 | tf_op jit(solution)/shard_map/ppermute | solution.py:263
  290.0 33.5 %collective-permute-start.30 = (bf16[4,192,1536]{2,1,0:T(8,128)(2,1)}, bf16[4,192,1536]{2,1,0:T(8,128)(2,1)}, u32[]{:S(2)}, u32[]{:S(2)}) collective-permute-start(bf16[4,192,1536]{2,1,0:T(8,128)(2,1)} %copy-done.39), channel_id=1, source_target_pairs={{0,1},{1,0},{2,3},{3,2},{4,5},{5,4},{6,7},{7,6},{8,9},{9,8},{10,11... | collective-permute-start | bytes 7077896 | tf_op jit(solution)/shard_map/ppermute | solution.py:263
  316.4 25.9 %collective-permute-start.31 = (bf16[192,2048]{1,0:T(8,128)(2,1)S(1)}, bf16[192,2048]{1,0:T(8,128)(2,1)}, u32[]{:S(2)}, u32[]{:S(2)}) collective-permute-start(bf16[192,2048]{1,0:T(8,128)(2,1)S(1)} %add_convert_fusion.refs_0_), channel_id=1, source_target_pairs={{0,8},{8,16},{16,24},{1,9},{9,17},{17,25},{2,10},{10,18},{18,26},{... | collective-permute-start | bytes 2359304 | tf_op jit(solution)/shard_map/ppermute | solution.py:251
  319.8 23.6 %collective-permute-start.32 = (bf16[192,2048]{1,0:T(8,128)(2,1)S(1)}, bf16[192,2048]{1,0:T(8,128)(2,1)}, u32[]{:S(2)}, u32[]{:S(2)}) collective-permute-start(bf16[192,2048]{1,0:T(8,128)(2,1)S(1)} %add_convert_fusion.refs_0_), channel_id=1, source_target_pairs={{8,0},{16,8},{24,16},{9,1},{17,9},{25,17},{10,2},{18,10},{26,18},{... | collective-permute-start | bytes 2359304 | tf_op jit(solution)/shard_map/ppermute | solution.py:252
  343.9 25.4 %collective-permute-start.38 = (bf16[192,2048]{1,0:T(8,128)(2,1)}, bf16[192,2048]{1,0:T(8,128)(2,1)}, u32[]{:S(2)}, u32[]{:S(2)}) collective-permute-start(bf16[192,2048]{1,0:T(8,128)(2,1)} %collective-permute-done.31.refs_1_), channel_id=1, source_target_pairs={{0,8},{8,16},{16,24},{1,9},{9,17},{17,25},{2,10},{10,18},{18,26},{... | collective-permute-start | bytes 2359304 | tf_op jit(solution)/shard_map/ppermute | solution.py:251
  347.1 22.3 %collective-permute-start.39 = (bf16[192,2048]{1,0:T(8,128)(2,1)}, bf16[192,2048]{1,0:T(8,128)(2,1)}, u32[]{:S(2)}, u32[]{:S(2)}) collective-permute-start(bf16[192,2048]{1,0:T(8,128)(2,1)} %collective-permute-done.32.refs_4_), channel_id=1, source_target_pairs={{8,0},{16,8},{24,16},{9,1},{17,9},{25,17},{10,2},{18,10},{26,18},{... | collective-permute-start | bytes 2359304 | tf_op jit(solution)/shard_map/ppermute | solution.py:252
  375.5 22.6 %collective-permute-start.44 = (bf16[192,2048]{1,0:T(8,128)(2,1)}, bf16[192,2048]{1,0:T(8,128)(2,1)S(1)}, u32[]{:S(2)}, u32[]{:S(2)}) collective-permute-start(bf16[192,2048]{1,0:T(8,128)(2,1)} %collective-permute-done.38.refs_2_), channel_id=1, source_target_pairs={{0,8},{8,16},{16,24},{1,9},{9,17},{17,25},{2,10},{10,18},{18,26},{... | collective-permute-start | bytes 2359304 | tf_op jit(solution)/shard_map/ppermute | solution.py:251
  377.9 23.4 %collective-permute-start.45 = (bf16[192,2048]{1,0:T(8,128)(2,1)}, bf16[192,2048]{1,0:T(8,128)(2,1)}, u32[]{:S(2)}, u32[]{:S(2)}) collective-permute-start(bf16[192,2048]{1,0:T(8,128)(2,1)} %collective-permute-done.39.refs_5_), channel_id=1, source_target_pairs={{8,0},{16,8},{24,16},{9,1},{17,9},{25,17},{10,2},{18,10},{26,18},{... | collective-permute-start | bytes 2359304 | tf_op jit(solution)/shard_map/ppermute | solution.py:252
  384.0 17.4 %collective-permute-start.41 = (bf16[192,768]{1,0:T(8,128)(2,1)}, bf16[192,768]{1,0:T(8,128)(2,1)}, u32[]{:S(2)}, u32[]{:S(2)}) collective-permute-start(bf16[192,768]{1,0:T(8,128)(2,1)} %get-tuple-element.257), channel_id=1, source_target_pairs={{0,2},{1,3},{2,0},{3,1},{4,6},{5,7},{6,4},{7,5},{8,10},{9,11},{10,... | collective-permute-start | bytes 884744 | tf_op jit(solution)/shard_map/ppermute | solution.py:263
  384.5 16.8 %collective-permute-start.42 = (bf16[192,768]{1,0:T(8,128)(2,1)S(1)}, bf16[192,768]{1,0:T(8,128)(2,1)}, u32[]{:S(2)}, u32[]{:S(2)}) collective-permute-start(bf16[192,768]{1,0:T(8,128)(2,1)S(1)} %get-tuple-element.258), channel_id=1, source_target_pairs={{0,4},{1,5},{2,6},{3,7},{4,0},{5,1},{6,2},{7,3},{8,12},{9,13},{10,... | collective-permute-start | bytes 884744 | tf_op jit(solution)/shard_map/ppermute | solution.py:263
  385.7 15.6 %collective-permute-start.43 = (bf16[192,768]{1,0:T(8,128)(2,1)S(1)}, bf16[192,768]{1,0:T(8,128)(2,1)}, u32[]{:S(2)}, u32[]{:S(2)}) collective-permute-start(bf16[192,768]{1,0:T(8,128)(2,1)S(1)} %get-tuple-element.259), channel_id=1, source_target_pairs={{0,6},{1,7},{2,4},{3,5},{4,2},{5,3},{6,0},{7,1},{8,14},{9,15},{10,... | collective-permute-start | bytes 884744 | tf_op jit(solution)/shard_map/ppermute | solution.py:263
  388.6 26.3 %all-to-all-start.3 = ((bf16[4,128,640]{1,2,0:T(8,128)(2,1)}), bf16[4,128,640]{1,2,0:T(8,128)(2,1)}, u32[]{:S(2)}, u32[]{:S(2)}) async-start(bf16[4,128,640]{1,2,0:T(8,128)(2,1)} %copy.103), calls=%async_computation.3 | async-start | bytes 1310720 | tf_op jit(solution)/shard_map/all_to_all | solution.py:907
  404.8 17.5 %collective-permute-start.51 = (bf16[192,1536]{1,0:T(8,128)(2,1)}, bf16[192,1536]{1,0:T(8,128)(2,1)}, u32[]{:S(2)}, u32[]{:S(2)}) collective-permute-start(bf16[192,1536]{1,0:T(8,128)(2,1)} %get-tuple-element.269), channel_id=1, source_target_pairs={{0,6},{1,7},{2,4},{3,5},{4,2},{5,3},{6,0},{7,1},{8,14},{9,15},{10,... | collective-permute-start | bytes 1769480 | tf_op jit(solution)/shard_map/ppermute | solution.py:263
  406.1 25.4 %collective-permute-start.50 = (bf16[192,1536]{1,0:T(8,128)(2,1)}, bf16[192,1536]{1,0:T(8,128)(2,1)}, u32[]{:S(2)}, u32[]{:S(2)}) collective-permute-start(bf16[192,1536]{1,0:T(8,128)(2,1)} %get-tuple-element.268), channel_id=1, source_target_pairs={{0,4},{1,5},{2,6},{3,7},{4,0},{5,1},{6,2},{7,3},{8,12},{9,13},{10,... | collective-permute-start | bytes 1769480 | tf_op jit(solution)/shard_map/ppermute | solution.py:263
  409.1 22.4 %collective-permute-start.49 = (bf16[192,1536]{1,0:T(8,128)(2,1)}, bf16[192,1536]{1,0:T(8,128)(2,1)}, u32[]{:S(2)}, u32[]{:S(2)}) collective-permute-start(bf16[192,1536]{1,0:T(8,128)(2,1)} %get-tuple-element.267), channel_id=1, source_target_pairs={{0,2},{1,3},{2,0},{3,1},{4,6},{5,7},{6,4},{7,5},{8,10},{9,11},{10,... | collective-permute-start | bytes 1769480 | tf_op jit(solution)/shard_map/ppermute | solution.py:263
  409.5 50.4 %collective-permute-start.46 = (bf16[192,768]{1,0:T(8,128)(2,1)S(1)}, bf16[192,768]{1,0:T(8,128)(2,1)}, u32[]{:S(2)}, u32[]{:S(2)}) collective-permute-start(bf16[192,768]{1,0:T(8,128)(2,1)S(1)} %select_convert_fusion.refs_0_), channel_id=1, source_target_pairs={{0,8},{8,16},{16,24},{24,0},{1,9},{9,17},{17,25},{25,1},{2,10},{10... | collective-permute-start | bytes 884744 | tf_op jit(solution)/shard_map/ppermute | solution.py:237
  409.6 53.9 %collective-permute-start.47 = (bf16[192,768]{1,0:T(8,128)(2,1)S(1)}, bf16[192,768]{1,0:T(8,128)(2,1)}, u32[]{:S(2)}, u32[]{:S(2)}) collective-permute-start(bf16[192,768]{1,0:T(8,128)(2,1)S(1)} %select_convert_fusion.refs_0_), channel_id=1, source_target_pairs={{0,16},{8,24},{16,0},{24,8},{1,17},{9,25},{17,1},{25,9},{2,18},{10... | collective-permute-start | bytes 884744 | tf_op jit(solution)/shard_map/ppermute | solution.py:237
  422.4 41.0 %collective-permute-start.48 = (bf16[192,768]{1,0:T(8,128)(2,1)S(1)}, bf16[192,768]{1,0:T(8,128)(2,1)}, u32[]{:S(2)}, u32[]{:S(2)}) collective-permute-start(bf16[192,768]{1,0:T(8,128)(2,1)S(1)} %select_convert_fusion.refs_0_), channel_id=1, source_target_pairs={{0,24},{8,0},{16,8},{24,16},{1,25},{9,1},{17,9},{25,17},{2,26},{10... | collective-permute-start | bytes 884744 | tf_op jit(solution)/shard_map/ppermute | solution.py:237
  434.1 18.9 %all-to-all-start.2 = ((bf16[192,4,384]{2,0,1:T(8,128)(2,1)}), bf16[192,4,384]{2,0,1:T(8,128)(2,1)}, u32[]{:S(2)}, u32[]{:S(2)}) async-start(bf16[192,4,384]{2,0,1:T(8,128)(2,1)} %bitcast.136), calls=%async_computation.2 | async-start | bytes 1179648 | tf_op jit(solution)/shard_map/all_to_all | solution.py:930
  (101 other events, 757.1 us)
Sparse Core Ops, SparseCore 0:
  10.8 28.3 all-gather.6
  41.2 47.8 all-gather.8
  91.5 58.2 all-gather.10
  152.1 52.2 all-gather.12
  290.1 42.1 all-gather.14

commit v17 on v15

--- a/solution.py
+++ b/solution.py
@@ -912,10 +912,12 @@
     token_grads = lax.all_to_all(sent_grads, "seq", split_axis=0, concat_axis=1, tiled=True)
 
     head_cols = q_cols + kv_cols
-    head_far, head_near = split_product(product_rows, product_columns, shard, shards)
+    head_far, head_near = split_product(
+        product_rows, after(product_columns, out_parts), shard, shards
+    )
     head_sums = pair_sums(head_near, hop(head_far, shards, 1), shard)
     head_blocks = send_chips(head_sums, shards)
-    head_part = total_of(after(head_blocks, steps[3]))
+    head_part = total_of(after(head_blocks, steps[3], token_grads))
     grad_normed = dot_nt(after(token_grads, head_part), attn_full)
     grad_tokens = grad_residual + root_back(inputs, root(inputs), grad_normed)
     base_cols = head_cols + experts

time: 501 us -> 517 us (1.032)
  the two profiles are of different devices: /device:TPU:0 before, /device:TPU:12 now
where the time goes in v17:
time: 517 us; the launch traced here: 507 us
  waiting for transfers between devices  201 us (39%)
  Pallas kernels  101 us (20%)
  starting transfers between devices  92.1 us (18%)
  local copies, waits for them, and re-layouts  43 us (8%)
  other arithmetic  27.3 us (5%)
  matrix products  21.6 us (4%)
  between operations  20.9 us (4%)
    ppermute x18, waiting for transfers between devices, shift(): lax.ppermute(block, 'seq', [(i, (i + step) % count) for i in range(count)])  119 us
    ppermute x3, waiting for transfers between devices, relay_step(): lax.ppermute(up, 'seq', [(i, i + 1) for i in range(count - 1)])  36.4 us
    ppermute x28, waiting for transfers between devices, hop(): return lax.ppermute(block, 'fsdp', [(i, i ^ mask) for i in range(count)])  32.6 us
    unnamed x220, local copies, waits for them, and re-layouts  31.6 us
    pallas_call x2, Pallas kernels, flash_backward(): pl.pallas_call(functools.partial(backward_kernel, shards, seqs, rows, g,...  27.6 us
    ppermute x18, starting transfers between devices, shift(): lax.ppermute(block, 'seq', [(i, (i + step) % count) for i in range(count)])  26.4 us
    ppermute x28, starting transfers between devices, hop(): return lax.ppermute(block, 'fsdp', [(i, i ^ mask) for i in range(count)])  24.5 us
    pallas_call x1, Pallas kernels, flash_forward(): pl.pallas_call(functools.partial(forward_kernel, shards, seqs, rows, loca...  19 us
  transfers between devices with their start and end apart: 61, of which 29 were waited for; matrix products, arithmetic and copies ran while one was open for 10% of the time, Pallas kernels for 16%

profile of v17, /device:TPU:12, one launch (start us, length us, event | category | flops | bytes accessed | tf_op | source)
XLA Modules:
  0.0 506.9 jit_solution(18283394165322407822)
XLA Ops:
  21.3 23.3 %collective-permute-done = bf16[136,1536]{1,0:T(8,128)(2,1)S(1)} collective-permute-done((bf16[136,1536]{1,0:T(8,128)(2,1)S(1)}, bf16[136,1536]{1,0:T(8,128)(2,1)S(1)}, u32[]{:S(2)}, u32[]{:S(2)}) %collective-permute-start) | collective-permute-done | bytes 417824 | tf_op jit(solution)/shard_map/ppermute | solution.py:237
  44.7 7.8 %collective-permute-done.1 = bf16[136,1536]{1,0:T(8,128)(2,1)S(1)} collective-permute-done((bf16[136,1536]{1,0:T(8,128)(2,1)S(1)}, bf16[136,1536]{1,0:T(8,128)(2,1)S(1)}, u32[]{:S(2)}, u32[]{:S(2)}) %collective-permute-start.1) | collective-permute-done | bytes 417824 | tf_op jit(solution)/shard_map/ppermute | solution.py:237
  62.8 7.3 %collective-permute-done.3.refs_1_ = bf16[528,256]{1,0:T(8,128)(2,1)S(1)} collective-permute-done((bf16[528,256]{1,0:T(8,128)(2,1)S(1)}, bf16[528,256]{1,0:T(8,128)(2,1)S(1)}, u32[]{:S(2)}, u32[]{:S(2)}) %collective-permute-start.3) | collective-permute-done | bytes 270368 | tf_op jit(solution)/shard_map/ppermute | solution.py:263
  70.1 7.5 %collective-permute-done.4.refs_2_ = bf16[528,256]{1,0:T(8,128)(2,1)S(1)} collective-permute-done((bf16[528,256]{1,0:T(8,128)(2,1)S(1)}, bf16[528,256]{1,0:T(8,128)(2,1)S(1)}, u32[]{:S(2)}, u32[]{:S(2)}) %collective-permute-start.4) | collective-permute-done | bytes 270368 | tf_op jit(solution)/shard_map/ppermute | solution.py:263
  77.6 3.2 collective-permute-done.5.refs_3_
  83.1 19.0 %shard_map.221 = (bf16[512,384]{1,0:T(8,128)(2,1)}, f32[512,384]{1,0:T(8,128)S(1)}, f32[512,384]{1,0:T(8,128)S(1)}) custom-call(bf16[528,256]{1,0:T(8,128)(2,1)S(1)} %maximum_maximum_fusion.1.refs_0_, bf16[528,256]{1,0:T(8,128)(2,1)S(1)} %collective-permute-done.3.refs_1_, bf16[528,256]{1,0:T(8,128)(2,1)S(1)} %collective-permute-done.4.refs_2_, ...), custom_call_target="tpu_custom_call" | custom-call | tf_op jit(solution)/shard_map/pallas_call | solution.py:114
  103.9 3.4 all-to-all-start
  108.2 8.8 %all-to-all-done = bf16[4,128,384]{2,1,0:T(8,128)(2,1)S(1)} async-done(((bf16[4,128,384]{2,1,0:T(8,128)(2,1)}), bf16[4,128,384]{2,1,0:T(8,128)(2,1)S(1)}, u32[]{:S(2)}, u32[]{:S(2)}) %all-to-all-start) | async-done | bytes 393248 | tf_op jit(solution)/shard_map/all_to_all | solution.py:795
  118.8 5.2 %multiply_reduce_fusion.5 = (f32[128]{0:T(128)S(1)}, f32[128,1536]{1,0:T(8,128)S(1)}) fusion(bf16[128,1536]{1,0:T(8,128)(2,1)S(1)} %bitcast.138, bf16[1536,1536]{0,1:T(8,128)(2,1)} %all-gather.9.cloned.1.call-done, bf16[128,1536]{1,0:T(8,128)(2,1)} %param.14), kind=kOutput, calls=%fused_computation.69 | convolution fusion | flops 604766080 | bytes 6291968 | tf_op jit(solution)/shard_map/dot_general | solution.py:24
  126.3 4.1 collective-permute-start.11
  133.7 2.6 collective-permute-done.10.refs_1_
  136.3 15.2 %collective-permute-done.11.refs_2_ = bf16[96,1536]{1,0:T(8,128)(2,1)} collective-permute-done((bf16[96,1536]{1,0:T(8,128)(2,1)S(1)}, bf16[96,1536]{1,0:T(8,128)(2,1)}, u32[]{:S(2)}, u32[]{:S(2)}) %collective-permute-start.11) | collective-permute-done | bytes 294944 | tf_op jit(solution)/shard_map/ppermute | solution.py:237
  151.4 5.0 collective-permute-done.12.refs_3_
  156.5 8.8 %shard_map.222 = (bf16[384,1536]{1,0:T(8,128)(2,1)}, f32[384,2048]{1,0:T(8,128)}, bf16[384,1024]{1,0:T(8,128)(2,1)}, bf16[96,1536]{1,0:T(8,128)(2,1)}, bf16[96,1...) custom-call(bf16[96,1536]{1,0:T(8,128)(2,1)} %get-tuple-element.369.refs_0_, ...), custom_call_target="tpu_custom_call" | custom-call | tf_op jit(solution)/shard_map/pallas_call | solution.py:396
  168.7 19.4 %collective-permute-done.13 = bf16[96,1536]{1,0:T(8,128)(2,1)S(1)} collective-permute-done((bf16[96,1536]{1,0:T(8,128)(2,1)}, bf16[96,1536]{1,0:T(8,128)(2,1)S(1)}, u32[]{:S(2)}, u32[]{:S(2)}) %collective-permute-start.13) | collective-permute-done | bytes 294944 | tf_op jit(solution)/shard_map/ppermute | solution.py:237
  194.1 3.9 collective-permute-start.16
  198.0 4.2 collective-permute-start.17
  204.4 3.3 collective-permute-done.16.refs_1_
  207.7 14.7 %collective-permute-done.17.refs_2_ = bf16[96,1536]{1,0:T(8,128)(2,1)S(1)} collective-permute-done((bf16[96,1536]{1,0:T(8,128)(2,1)S(1)}, bf16[96,1536]{1,0:T(8,128)(2,1)S(1)}, u32[]{:S(2)}, u32[]{:S(2)}) %collective-permute-start.17) | collective-permute-done | bytes 294944 | tf_op jit(solution)/shard_map/ppermute | solution.py:237
  222.4 3.8 collective-permute-done.18.refs_3_
  227.0 9.9 %shard_map.223 = (bf16[384,1536]{1,0:T(8,128)(2,1)}, bf16[384,2048]{1,0:T(8,128)(2,1)}, bf16[96,1536]{1,0:T(8,128)(2,1)}, bf16[96,1536]{1,0:T(8,128)(2,1)}, bf16...) custom-call(bf16[96,1536]{1,0:T(8,128)(2,1)} %get-tuple-element.184.refs_0_, bf16[96,1536]{1,0:T(8,128)(2,1)} %copy-done.76, ...), custom_call_target="tpu_custom_call" | custom-call | tf_op jit(solution)/shard_map/pallas_call | solution.py:445
  241.0 2.9 shard_map.224
  245.8 4.8 shard_map.226
  254.2 2.6 collective-permute-start.24
  256.8 2.9 collective-permute-done.19
  260.2 2.5 collective-permute-start.26
  270.7 7.8 %all-to-all-start.1 = ((bf16[128,4,384]{2,0,1:T(8,128)(2,1)}), bf16[128,4,384]{2,0,1:T(8,128)(2,1)}, u32[]{:S(2)}, u32[]{:S(2)}) async-start(bf16[128,4,384]{2,0,1:T(8,128)(2,1)} %bitcast.148), calls=%async_computation.1 | async-start | bytes 786432 | tf_op jit(solution)/shard_map/all_to_all | solution.py:871
  281.1 2.6 shard_map.229
  292.8 13.8 %shard_map.228 = (f32[512,192]{1,0:T(8,128)S(1)}, bf16[4,512,128]{2,1,0:T(8,128)(2,1)S(1)}, bf16[4,512,128]{2,1,0:T(8,128)(2,1)S(1)}) custom-call(bf16[8,528,256]{2,1,0:T(8,128)(2,1)S(1)} %copy-done.6, bf16[512,384]{1,0:T(8,128)(2,1)S(1)} %slice_multiply_fusion.refs_8_.refs_1_, f32[8,1,1024]{2,1,0:T(1,128)S(1)} %pad_maximum_fusion.4.refs_9_.refs_2_, ...), custom_call_target="tpu_custom_call" | custom-call | flops 999999995904 | tf_op jit(solution)/shard_map/pallas_call | solution.py:212
  306.7 5.9 %collective-permute-done.28 = bf16[192,2048]{1,0:T(8,128)(2,1)} collective-permute-done((bf16[192,2048]{1,0:T(8,128)(2,1)}, bf16[192,2048]{1,0:T(8,128)(2,1)}, u32[]{:S(2)}, u32[]{:S(2)}) %collective-permute-start.28) | collective-permute-done | bytes 786464 | tf_op jit(solution)/shard_map/ppermute | solution.py:263
  316.5 3.4 collective-permute-start.31
  319.9 3.6 collective-permute-start.32
  323.5 3.0 shard_map.230
  331.1 13.8 %shard_map.231 = (f32[512,192]{1,0:T(8,128)S(1)}, bf16[4,512,128]{2,1,0:T(8,128)(2,1)S(1)}, bf16[4,512,128]{2,1,0:T(8,128)(2,1)S(1)}) custom-call(bf16[8,528,256]{2,1,0:T(8,128)(2,1)S(1)} %copy-done.7, bf16[512,384]{1,0:T(8,128)(2,1)S(1)} %slice_multiply_fusion.refs_8_.refs_1_, f32[8,1,1024]{2,1,0:T(1,128)S(1)} %pad_maximum_fusion.4.refs_9_.refs_2_, ...), custom_call_target="tpu_custom_call" | custom-call | tf_op jit(solution)/shard_map/pallas_call | solution.py:212
  347.3 4.5 collective-permute-done.34
  361.2 5.1 %all-to-all-start.2 = ((bf16[192,4,384]{2,0,1:T(8,128)(2,1)}), bf16[192,4,384]{2,0,1:T(8,128)(2,1)}, u32[]{:S(2)}, u32[]{:S(2)}) async-start(bf16[192,4,384]{2,0,1:T(8,128)(2,1)} %bitcast.147), calls=%async_computation.2 | async-start | bytes 1179648 | tf_op jit(solution)/shard_map/all_to_all | solution.py:903
  366.3 3.4 collective-permute-start.41
  369.7 3.4 collective-permute-start.42
  376.8 19.3 %collective-permute-done.41.refs_2_ = bf16[192,2048]{1,0:T(8,128)(2,1)} collective-permute-done((bf16[192,2048]{1,0:T(8,128)(2,1)}, bf16[192,2048]{1,0:T(8,128)(2,1)}, u32[]{:S(2)}, u32[]{:S(2)}) %collective-permute-start.41) | collective-permute-done | bytes 786464 | tf_op jit(solution)/shard_map/ppermute | solution.py:251
  405.5 4.4 shard_map.234
  413.3 4.3 all-to-all-start.3
  417.6 2.5 collective-permute-start.47
  420.1 4.2 collective-permute-start.48
  432.6 17.0 %collective-permute-done.47.refs_3_ = bf16[192,2048]{1,0:T(8,128)(2,1)} collective-permute-done((bf16[192,2048]{1,0:T(8,128)(2,1)}, bf16[192,2048]{1,0:T(8,128)(2,1)}, u32[]{:S(2)}, u32[]{:S(2)}) %collective-permute-start.47) | collective-permute-done | bytes 786464 | tf_op jit(solution)/shard_map/ppermute | solution.py:251
  457.0 6.3 %fusion.27 = (f32[128]{0:T(128)S(1)}, f32[128]{0:T(128)S(1)}, f32[128,1536]{1,0:T(8,128)S(1)}) fusion(bf16[128,1536]{1,0:T(8,128)(2,1)S(1)} %copy-done.58, bf16[128,2560]{0,1:T(8,128)(2,1)} %bitcast.50, bf16[1536,2560]{1,0:T(8,128)(2,1)} %all-gather.13.cloned.1.call-done), kind=kOutput, calls=%fused_computation.47 | convolution fusion | flops 1007615744 | bytes 9700352 | tf_op jit(solution)/shard_map/dot_general | solution.py:28
  464.4 8.3 %shard_map.236 = (f32[4,192,2048]{2,1,0:T(8,128)}, f32[192,128]{1,0:T(8,128)S(1)}) custom-call(s32[1]{0:T(128)} %bitcast.33.place_ref, bf16[192,2048]{1,0:T(8,128)(2,1)S(1)} %add_convert_fusion.refs_0_, bf16[192,2048]{1,0:T(8,128)(2,1)} %collective-permute-done.31.refs_1_, bf16[192,2048]{1,0:T(8,128)(2,1)} %collective-permute-done.41.refs_2_, ...), custom_call_target="tpu_custom_call" | custom-call | tf_op jit(solution)/shard_map/pallas_call | solution.py:583
  475.0 10.0 %collective-permute-done.49.refs_1_ = bf16[192,1152]{1,0:T(8,128)(2,1)S(1)} collective-permute-done((bf16[192,1152]{1,0:T(8,128)(2,1)S(1)}, bf16[192,1152]{1,0:T(8,128)(2,1)S(1)}, u32[]{:S(2)}, u32[]{:S(2)}) %collective-permute-start.49) | collective-permute-done | bytes 442400 | tf_op jit(solution)/shard_map/ppermute | solution.py:237
  485.0 8.3 %collective-permute-done.50.refs_2_ = bf16[192,1152]{1,0:T(8,128)(2,1)S(1)} collective-permute-done((bf16[192,1152]{1,0:T(8,128)(2,1)S(1)}, bf16[192,1152]{1,0:T(8,128)(2,1)S(1)}, u32[]{:S(2)}, u32[]{:S(2)}) %collective-permute-start.50) | collective-permute-done | bytes 442400 | tf_op jit(solution)/shard_map/ppermute | solution.py:237
  (439 shorter events, 134.9 us)
Async XLA Ops:
  7.2 47.7 %all-gather.7.cloned.1.call-start = ((), (), s32[]{:S(2)}) async-start(), calls=%async_computation.4 | async-start | bytes 2211840 | tf_op jit(solution)/shard_map/all_gather | solution.py:719
  10.7 108.0 %all-gather.9.cloned.1.call-start = ((), (), s32[]{:S(2)}) async-start(), calls=%async_computation.5 | async-start | bytes 5308416 | tf_op jit(solution)/shard_map/all_gather | solution.py:746
  11.5 145.0 %all-gather.11.cloned.1.call-start = ((), (), s32[]{:S(2)}) async-start(), calls=%async_computation.6 | async-start | bytes 11059200 | tf_op jit(solution)/shard_map/all_gather | solution.py:761
  15.1 189.4 %all-gather.13.cloned.1.call-start = ((), (), s32[]{:S(2)}) async-start(), calls=%async_computation.7 | async-start | bytes 8847360 | tf_op jit(solution)/shard_map/all_gather | solution.py:774
  15.1 29.6 %collective-permute-start = (bf16[136,1536]{1,0:T(8,128)(2,1)S(1)}, bf16[136,1536]{1,0:T(8,128)(2,1)S(1)}, u32[]{:S(2)}, u32[]{:S(2)}) collective-permute-start(bf16[136,1536]{1,0:T(8,128)(2,1)S(1)} %fusion.36), channel_id=1, source_target_pairs={{0,8},{8,16},{16,24},{24,0},{1,9},{9,17},{17,25},{25,1},{2,10},{10... | collective-permute-start | bytes 1253384 | tf_op jit(solution)/shard_map/ppermute | solution.py:237
  16.7 35.8 %collective-permute-start.1 = (bf16[136,1536]{1,0:T(8,128)(2,1)S(1)}, bf16[136,1536]{1,0:T(8,128)(2,1)S(1)}, u32[]{:S(2)}, u32[]{:S(2)}) collective-permute-start(bf16[136,1536]{1,0:T(8,128)(2,1)S(1)} %fusion.36), channel_id=1, source_target_pairs={{0,16},{8,24},{16,0},{24,8},{1,17},{9,25},{17,1},{25,9},{2,18},{10... | collective-permute-start | bytes 1253384 | tf_op jit(solution)/shard_map/ppermute | solution.py:237
  18.0 36.3 %collective-permute-start.2 = (bf16[136,1536]{1,0:T(8,128)(2,1)S(1)}, bf16[136,1536]{1,0:T(8,128)(2,1)S(1)}, u32[]{:S(2)}, u32[]{:S(2)}) collective-permute-start(bf16[136,1536]{1,0:T(8,128)(2,1)S(1)} %fusion.36), channel_id=1, source_target_pairs={{0,24},{8,0},{16,8},{24,16},{1,25},{9,1},{17,9},{25,17},{2,26},{10... | collective-permute-start | bytes 1253384 | tf_op jit(solution)/shard_map/ppermute | solution.py:237
  61.2 19.7 %collective-permute-start.5 = (bf16[528,256]{1,0:T(8,128)(2,1)S(1)}, bf16[528,256]{1,0:T(8,128)(2,1)S(1)}, u32[]{:S(2)}, u32[]{:S(2)}) collective-permute-start(bf16[528,256]{1,0:T(8,128)(2,1)S(1)} %maximum_maximum_fusion.1.refs_0_), channel_id=1, source_target_pairs={{0,6},{1,7},{2,4},{3,5},{4,2},{5,3},{6,0},{7,1},{8,14},{9,15},{10,... | collective-permute-start | bytes 811016 | tf_op jit(solution)/shard_map/ppermute | solution.py:263
  62.7 19.4 %collective-permute-start.6 = (bf16[528,256]{1,0:T(8,128)(2,1)S(1)}, bf16[528,256]{1,0:T(8,128)(2,1)S(1)}, u32[]{:S(2)}, u32[]{:S(2)}) collective-permute-start(bf16[528,256]{1,0:T(8,128)(2,1)S(1)} %maximum_maximum_fusion.1.refs_0_), channel_id=1, source_target_pairs={{0,1},{1,0},{2,3},{3,2},{4,5},{5,4},{6,7},{7,6},{8,9},{9,8},{10,11... | collective-permute-start | bytes 811016 | tf_op jit(solution)/shard_map/ppermute | solution.py:263
  126.3 25.1 %collective-permute-start.11 = (bf16[96,1536]{1,0:T(8,128)(2,1)S(1)}, bf16[96,1536]{1,0:T(8,128)(2,1)}, u32[]{:S(2)}, u32[]{:S(2)}) collective-permute-start(bf16[96,1536]{1,0:T(8,128)(2,1)S(1)} %get-tuple-element.367), channel_id=1, source_target_pairs={{0,16},{8,24},{16,0},{24,8},{1,17},{9,25},{17,1},{25,9},{2,18},{10... | collective-permute-start | bytes 884744 | tf_op jit(solution)/shard_map/ppermute | solution.py:237
  130.4 26.1 %collective-permute-start.12 = (bf16[96,1536]{1,0:T(8,128)(2,1)S(1)}, bf16[96,1536]{1,0:T(8,128)(2,1)}, u32[]{:S(2)}, u32[]{:S(2)}) collective-permute-start(bf16[96,1536]{1,0:T(8,128)(2,1)S(1)} %get-tuple-element.366), channel_id=1, source_target_pairs={{0,24},{8,0},{16,8},{24,16},{1,25},{9,1},{17,9},{25,17},{2,26},{10... | collective-permute-start | bytes 884744 | tf_op jit(solution)/shard_map/ppermute | solution.py:237
  165.3 22.8 %collective-permute-start.13 = (bf16[96,1536]{1,0:T(8,128)(2,1)}, bf16[96,1536]{1,0:T(8,128)(2,1)S(1)}, u32[]{:S(2)}, u32[]{:S(2)}) collective-permute-start(bf16[96,1536]{1,0:T(8,128)(2,1)} %get-tuple-element.167), channel_id=1, source_target_pairs={{0,24},{8,0},{16,8},{24,16},{1,25},{9,1},{17,9},{25,17},{2,26},{10... | collective-permute-start | bytes 884744 | tf_op jit(solution)/shard_map/ppermute | solution.py:237
  165.4 22.7 %collective-permute-start.14 = (bf16[96,1536]{1,0:T(8,128)(2,1)}, bf16[96,1536]{1,0:T(8,128)(2,1)S(1)}, u32[]{:S(2)}, u32[]{:S(2)}) collective-permute-start(bf16[96,1536]{1,0:T(8,128)(2,1)} %get-tuple-element.168), channel_id=1, source_target_pairs={{0,16},{8,24},{16,0},{24,8},{1,17},{9,25},{17,1},{25,9},{2,18},{10... | collective-permute-start | bytes 884744 | tf_op jit(solution)/shard_map/ppermute | solution.py:237
  166.1 23.0 %collective-permute-start.15 = (bf16[96,1536]{1,0:T(8,128)(2,1)}, bf16[96,1536]{1,0:T(8,128)(2,1)S(1)}, u32[]{:S(2)}, u32[]{:S(2)}) collective-permute-start(bf16[96,1536]{1,0:T(8,128)(2,1)} %get-tuple-element.169), channel_id=1, source_target_pairs={{0,8},{8,16},{16,24},{24,0},{1,9},{9,17},{17,25},{25,1},{2,10},{10... | collective-permute-start | bytes 884744 | tf_op jit(solution)/shard_map/ppermute | solution.py:237
  198.0 24.5 %collective-permute-start.17 = (bf16[96,1536]{1,0:T(8,128)(2,1)S(1)}, bf16[96,1536]{1,0:T(8,128)(2,1)S(1)}, u32[]{:S(2)}, u32[]{:S(2)}) collective-permute-start(bf16[96,1536]{1,0:T(8,128)(2,1)S(1)} %get-tuple-element.363), channel_id=1, source_target_pairs={{0,16},{8,24},{16,0},{24,8},{1,17},{9,25},{17,1},{25,9},{2,18},{10... | collective-permute-start | bytes 884744 | tf_op jit(solution)/shard_map/ppermute | solution.py:237
  202.1 24.1 %collective-permute-start.18 = (bf16[96,1536]{1,0:T(8,128)(2,1)S(1)}, bf16[96,1536]{1,0:T(8,128)(2,1)S(1)}, u32[]{:S(2)}, u32[]{:S(2)}) collective-permute-start(bf16[96,1536]{1,0:T(8,128)(2,1)S(1)} %get-tuple-element.362), channel_id=1, source_target_pairs={{0,24},{8,0},{16,8},{24,16},{1,25},{9,1},{17,9},{25,17},{2,26},{10... | collective-permute-start | bytes 884744 | tf_op jit(solution)/shard_map/ppermute | solution.py:237
  236.9 22.8 %collective-permute-start.19 = (bf16[96,1536]{1,0:T(8,128)(2,1)}, bf16[96,1536]{1,0:T(8,128)(2,1)S(1)}, u32[]{:S(2)}, u32[]{:S(2)}) collective-permute-start(bf16[96,1536]{1,0:T(8,128)(2,1)} %get-tuple-element.190), channel_id=1, source_target_pairs={{0,24},{8,0},{16,8},{24,16},{1,25},{9,1},{17,9},{25,17},{2,26},{10... | collective-permute-start | bytes 884744 | tf_op jit(solution)/shard_map/ppermute | solution.py:237
  237.0 23.2 %collective-permute-start.20 = (bf16[96,1536]{1,0:T(8,128)(2,1)}, bf16[96,1536]{1,0:T(8,128)(2,1)S(1)}, u32[]{:S(2)}, u32[]{:S(2)}) collective-permute-start(bf16[96,1536]{1,0:T(8,128)(2,1)} %get-tuple-element.191), channel_id=1, source_target_pairs={{0,16},{8,24},{16,0},{24,8},{1,17},{9,25},{17,1},{25,9},{2,18},{10... | collective-permute-start | bytes 884744 | tf_op jit(solution)/shard_map/ppermute | solution.py:237
  237.9 24.8 %collective-permute-start.21 = (bf16[96,1536]{1,0:T(8,128)(2,1)}, bf16[96,1536]{1,0:T(8,128)(2,1)S(1)}, u32[]{:S(2)}, u32[]{:S(2)}) collective-permute-start(bf16[96,1536]{1,0:T(8,128)(2,1)} %get-tuple-element.192), channel_id=1, source_target_pairs={{0,8},{8,16},{16,24},{24,0},{1,9},{9,17},{17,25},{25,1},{2,10},{10... | collective-permute-start | bytes 884744 | tf_op jit(solution)/shard_map/ppermute | solution.py:237
  254.2 32.3 %collective-permute-start.24 = (bf16[192,1024]{1,0:T(8,128)(2,1)}, bf16[192,1024]{1,0:T(8,128)(2,1)}, u32[]{:S(2)}, u32[]{:S(2)}) collective-permute-start(bf16[192,1024]{1,0:T(8,128)(2,1)} %get-tuple-element.204), channel_id=1, source_target_pairs={{0,2},{1,3},{2,0},{3,1},{4,6},{5,7},{6,4},{7,5},{8,10},{9,11},{10,... | collective-permute-start | bytes 1179656 | tf_op jit(solution)/shard_map/ppermute | solution.py:263
  259.7 27.7 %collective-permute-start.25 = (bf16[192,1024]{1,0:T(8,128)(2,1)}, bf16[192,1024]{1,0:T(8,128)(2,1)}, u32[]{:S(2)}, u32[]{:S(2)}) collective-permute-start(bf16[192,1024]{1,0:T(8,128)(2,1)} %get-tuple-element.205), channel_id=1, source_target_pairs={{0,4},{1,5},{2,6},{3,7},{4,0},{5,1},{6,2},{7,3},{8,12},{9,13},{10,... | collective-permute-start | bytes 1179656 | tf_op jit(solution)/shard_map/ppermute | solution.py:263
  260.2 27.2 %collective-permute-start.26 = (bf16[192,1024]{1,0:T(8,128)(2,1)}, bf16[192,1024]{1,0:T(8,128)(2,1)}, u32[]{:S(2)}, u32[]{:S(2)}) collective-permute-start(bf16[192,1024]{1,0:T(8,128)(2,1)} %get-tuple-element.206), channel_id=1, source_target_pairs={{0,6},{1,7},{2,4},{3,5},{4,2},{5,3},{6,0},{7,1},{8,14},{9,15},{10,... | collective-permute-start | bytes 1179656 | tf_op jit(solution)/shard_map/ppermute | solution.py:263
  270.7 19.2 %all-to-all-start.1 = ((bf16[128,4,384]{2,0,1:T(8,128)(2,1)}), bf16[128,4,384]{2,0,1:T(8,128)(2,1)}, u32[]{:S(2)}, u32[]{:S(2)}) async-start(bf16[128,4,384]{2,0,1:T(8,128)(2,1)} %bitcast.148), calls=%async_computation.1 | async-start | bytes 786432 | tf_op jit(solution)/shard_map/all_to_all | solution.py:871
  278.5 74.1 %all-gather.15.cloned.1.call-start = ((), (), s32[]{:S(2)}) async-start(), calls=%async_computation.8 | async-start | bytes 1966080 | tf_op jit(solution)/shard_map/all_gather | solution.py:874
  278.5 28.1 %collective-permute-start.27 = (bf16[192,2048]{1,0:T(8,128)(2,1)}, bf16[192,2048]{1,0:T(8,128)(2,1)}, u32[]{:S(2)}, u32[]{:S(2)}) collective-permute-start(bf16[192,2048]{1,0:T(8,128)(2,1)} %copy-done.46), channel_id=1, source_target_pairs={{0,2},{1,3},{2,0},{3,1},{4,6},{5,7},{6,4},{7,5},{8,10},{9,11},{10,... | collective-permute-start | bytes 2359304 | tf_op jit(solution)/shard_map/ppermute | solution.py:263
  279.5 33.0 %collective-permute-start.28 = (bf16[192,2048]{1,0:T(8,128)(2,1)}, bf16[192,2048]{1,0:T(8,128)(2,1)}, u32[]{:S(2)}, u32[]{:S(2)}) collective-permute-start(bf16[192,2048]{1,0:T(8,128)(2,1)} %copy-done.45), channel_id=1, source_target_pairs={{0,4},{1,5},{2,6},{3,7},{4,0},{5,1},{6,2},{7,3},{8,12},{9,13},{10,... | collective-permute-start | bytes 2359304 | tf_op jit(solution)/shard_map/ppermute | solution.py:263
  286.5 27.7 %collective-permute-start.29 = (bf16[192,2048]{1,0:T(8,128)(2,1)}, bf16[192,2048]{1,0:T(8,128)(2,1)}, u32[]{:S(2)}, u32[]{:S(2)}) collective-permute-start(bf16[192,2048]{1,0:T(8,128)(2,1)} %copy-done.44), channel_id=1, source_target_pairs={{0,6},{1,7},{2,4},{3,5},{4,2},{5,3},{6,0},{7,1},{8,14},{9,15},{10,... | collective-permute-start | bytes 2359304 | tf_op jit(solution)/shard_map/ppermute | solution.py:263
  290.0 33.5 %collective-permute-start.30 = (bf16[4,192,1536]{2,1,0:T(8,128)(2,1)}, bf16[4,192,1536]{2,1,0:T(8,128)(2,1)}, u32[]{:S(2)}, u32[]{:S(2)}) collective-permute-start(bf16[4,192,1536]{2,1,0:T(8,128)(2,1)} %copy-done.43), channel_id=1, source_target_pairs={{0,1},{1,0},{2,3},{3,2},{4,5},{5,4},{6,7},{7,6},{8,9},{9,8},{10,11... | collective-permute-start | bytes 7077896 | tf_op jit(solution)/shard_map/ppermute | solution.py:263
  316.5 30.8 %collective-permute-start.31 = (bf16[192,2048]{1,0:T(8,128)(2,1)S(1)}, bf16[192,2048]{1,0:T(8,128)(2,1)}, u32[]{:S(2)}, u32[]{:S(2)}) collective-permute-start(bf16[192,2048]{1,0:T(8,128)(2,1)S(1)} %add_convert_fusion.refs_0_), channel_id=1, source_target_pairs={{0,8},{8,16},{16,24},{1,9},{9,17},{17,25},{2,10},{10,18},{18,26},{... | collective-permute-start | bytes 2359304 | tf_op jit(solution)/shard_map/ppermute | solution.py:251
  319.9 27.4 %collective-permute-start.32 = (bf16[192,2048]{1,0:T(8,128)(2,1)S(1)}, bf16[192,2048]{1,0:T(8,128)(2,1)}, u32[]{:S(2)}, u32[]{:S(2)}) collective-permute-start(bf16[192,2048]{1,0:T(8,128)(2,1)S(1)} %add_convert_fusion.refs_0_), channel_id=1, source_target_pairs={{8,0},{16,8},{24,16},{9,1},{17,9},{25,17},{10,2},{18,10},{26,18},{... | collective-permute-start | bytes 2359304 | tf_op jit(solution)/shard_map/ppermute | solution.py:252
  327.6 19.7 %collective-permute-start.33 = (bf16[192,1536]{1,0:T(8,128)(2,1)S(1)}, bf16[192,1536]{1,0:T(8,128)(2,1)S(1)}, u32[]{:S(2)}, u32[]{:S(2)}) collective-permute-start(bf16[192,1536]{1,0:T(8,128)(2,1)S(1)} %get-tuple-element.239), channel_id=1, source_target_pairs={{0,2},{1,3},{2,0},{3,1},{4,6},{5,7},{6,4},{7,5},{8,10},{9,11},{10,... | collective-permute-start | bytes 1769480 | tf_op jit(solution)/shard_map/ppermute | solution.py:263
  328.2 23.6 %collective-permute-start.34 = (bf16[192,1536]{1,0:T(8,128)(2,1)S(1)}, bf16[192,1536]{1,0:T(8,128)(2,1)S(1)}, u32[]{:S(2)}, u32[]{:S(2)}) collective-permute-start(bf16[192,1536]{1,0:T(8,128)(2,1)S(1)} %get-tuple-element.240), channel_id=1, source_target_pairs={{0,4},{1,5},{2,6},{3,7},{4,0},{5,1},{6,2},{7,3},{8,12},{9,13},{10,... | collective-permute-start | bytes 1769480 | tf_op jit(solution)/shard_map/ppermute | solution.py:263
  329.9 22.7 %collective-permute-start.35 = (bf16[192,1536]{1,0:T(8,128)(2,1)S(1)}, bf16[192,1536]{1,0:T(8,128)(2,1)}, u32[]{:S(2)}, u32[]{:S(2)}) collective-permute-start(bf16[192,1536]{1,0:T(8,128)(2,1)S(1)} %get-tuple-element.241), channel_id=1, source_target_pairs={{0,6},{1,7},{2,4},{3,5},{4,2},{5,3},{6,0},{7,1},{8,14},{9,15},{10,... | collective-permute-start | bytes 1769480 | tf_op jit(solution)/shard_map/ppermute | solution.py:263
  361.2 43.1 %all-to-all-start.2 = ((bf16[192,4,384]{2,0,1:T(8,128)(2,1)}), bf16[192,4,384]{2,0,1:T(8,128)(2,1)}, u32[]{:S(2)}, u32[]{:S(2)}) async-start(bf16[192,4,384]{2,0,1:T(8,128)(2,1)} %bitcast.147), calls=%async_computation.2 | async-start | bytes 1179648 | tf_op jit(solution)/shard_map/all_to_all | solution.py:903
  366.3 29.8 %collective-permute-start.41 = (bf16[192,2048]{1,0:T(8,128)(2,1)}, bf16[192,2048]{1,0:T(8,128)(2,1)}, u32[]{:S(2)}, u32[]{:S(2)}) collective-permute-start(bf16[192,2048]{1,0:T(8,128)(2,1)} %collective-permute-done.31.refs_1_), channel_id=1, source_target_pairs={{0,8},{8,16},{16,24},{1,9},{9,17},{17,25},{2,10},{10,18},{18,26},{... | collective-permute-start | bytes 2359304 | tf_op jit(solution)/shard_map/ppermute | solution.py:251
  369.7 28.3 %collective-permute-start.42 = (bf16[192,2048]{1,0:T(8,128)(2,1)}, bf16[192,2048]{1,0:T(8,128)(2,1)}, u32[]{:S(2)}, u32[]{:S(2)}) collective-permute-start(bf16[192,2048]{1,0:T(8,128)(2,1)} %collective-permute-done.32.refs_4_), channel_id=1, source_target_pairs={{8,0},{16,8},{24,16},{9,1},{17,9},{25,17},{10,2},{18,10},{26,18},{... | collective-permute-start | bytes 2359304 | tf_op jit(solution)/shard_map/ppermute | solution.py:252
  373.1 25.0 %collective-permute-start.38 = (bf16[512,256]{1,0:T(8,128)(2,1)}, bf16[512,256]{1,0:T(8,128)(2,1)S(1)}, u32[]{:S(2)}, u32[]{:S(2)}) collective-permute-start(bf16[512,256]{1,0:T(8,128)(2,1)} %get-tuple-element.257), channel_id=1, source_target_pairs={{0,2},{1,3},{2,0},{3,1},{4,6},{5,7},{6,4},{7,5},{8,10},{9,11},{10,... | collective-permute-start | bytes 786440 | tf_op jit(solution)/shard_map/ppermute | solution.py:263
  374.6 23.4 %collective-permute-start.39 = (bf16[512,256]{1,0:T(8,128)(2,1)}, bf16[512,256]{1,0:T(8,128)(2,1)}, u32[]{:S(2)}, u32[]{:S(2)}) collective-permute-start(bf16[512,256]{1,0:T(8,128)(2,1)} %get-tuple-element.258), channel_id=1, source_target_pairs={{0,4},{1,5},{2,6},{3,7},{4,0},{5,1},{6,2},{7,3},{8,12},{9,13},{10,... | collective-permute-start | bytes 786440 | tf_op jit(solution)/shard_map/ppermute | solution.py:263
  374.6 23.4 %collective-permute-start.40 = (bf16[512,256]{1,0:T(8,128)(2,1)}, bf16[512,256]{1,0:T(8,128)(2,1)}, u32[]{:S(2)}, u32[]{:S(2)}) collective-permute-start(bf16[512,256]{1,0:T(8,128)(2,1)} %get-tuple-element.259), channel_id=1, source_target_pairs={{0,6},{1,7},{2,4},{3,5},{4,2},{5,3},{6,0},{7,1},{8,14},{9,15},{10,... | collective-permute-start | bytes 786440 | tf_op jit(solution)/shard_map/ppermute | solution.py:263
  413.3 37.3 %all-to-all-start.3 = ((bf16[4,128,640]{1,2,0:T(8,128)(2,1)}), bf16[4,128,640]{1,2,0:T(8,128)(2,1)}, u32[]{:S(2)}, u32[]{:S(2)}) async-start(bf16[4,128,640]{1,2,0:T(8,128)(2,1)} %copy.102), calls=%async_computation.3 | async-start | bytes 1310720 | tf_op jit(solution)/shard_map/all_to_all | solution.py:912
  417.6 32.0 %collective-permute-start.47 = (bf16[192,2048]{1,0:T(8,128)(2,1)}, bf16[192,2048]{1,0:T(8,128)(2,1)}, u32[]{:S(2)}, u32[]{:S(2)}) collective-permute-start(bf16[192,2048]{1,0:T(8,128)(2,1)} %collective-permute-done.41.refs_2_), channel_id=1, source_target_pairs={{0,8},{8,16},{16,24},{1,9},{9,17},{17,25},{2,10},{10,18},{18,26},{... | collective-permute-start | bytes 2359304 | tf_op jit(solution)/shard_map/ppermute | solution.py:251
  420.1 30.5 %collective-permute-start.48 = (bf16[192,2048]{1,0:T(8,128)(2,1)}, bf16[192,2048]{1,0:T(8,128)(2,1)}, u32[]{:S(2)}, u32[]{:S(2)}) collective-permute-start(bf16[192,2048]{1,0:T(8,128)(2,1)} %collective-permute-done.42.refs_5_), channel_id=1, source_target_pairs={{8,0},{16,8},{24,16},{9,1},{17,9},{25,17},{10,2},{18,10},{26,18},{... | collective-permute-start | bytes 2359304 | tf_op jit(solution)/shard_map/ppermute | solution.py:252
  426.8 23.8 %collective-permute-start.44 = (bf16[192,768]{1,0:T(8,128)(2,1)}, bf16[192,768]{1,0:T(8,128)(2,1)S(1)}, u32[]{:S(2)}, u32[]{:S(2)}) collective-permute-start(bf16[192,768]{1,0:T(8,128)(2,1)} %get-tuple-element.273), channel_id=1, source_target_pairs={{0,2},{1,3},{2,0},{3,1},{4,6},{5,7},{6,4},{7,5},{8,10},{9,11},{10,... | collective-permute-start | bytes 884744 | tf_op jit(solution)/shard_map/ppermute | solution.py:263
  428.3 22.3 %collective-permute-start.45 = (bf16[192,768]{1,0:T(8,128)(2,1)}, bf16[192,768]{1,0:T(8,128)(2,1)S(1)}, u32[]{:S(2)}, u32[]{:S(2)}) collective-permute-start(bf16[192,768]{1,0:T(8,128)(2,1)} %get-tuple-element.274), channel_id=1, source_target_pairs={{0,4},{1,5},{2,6},{3,7},{4,0},{5,1},{6,2},{7,3},{8,12},{9,13},{10,... | collective-permute-start | bytes 884744 | tf_op jit(solution)/shard_map/ppermute | solution.py:263
  428.3 22.3 %collective-permute-start.46 = (bf16[192,768]{1,0:T(8,128)(2,1)S(1)}, bf16[192,768]{1,0:T(8,128)(2,1)S(1)}, u32[]{:S(2)}, u32[]{:S(2)}) collective-permute-start(bf16[192,768]{1,0:T(8,128)(2,1)S(1)} %get-tuple-element.275), channel_id=1, source_target_pairs={{0,6},{1,7},{2,4},{3,5},{4,2},{5,3},{6,0},{7,1},{8,14},{9,15},{10,... | collective-permute-start | bytes 884744 | tf_op jit(solution)/shard_map/ppermute | solution.py:263
  453.9 31.1 %collective-permute-start.49 = (bf16[192,1152]{1,0:T(8,128)(2,1)S(1)}, bf16[192,1152]{1,0:T(8,128)(2,1)S(1)}, u32[]{:S(2)}, u32[]{:S(2)}) collective-permute-start(bf16[192,1152]{1,0:T(8,128)(2,1)S(1)} %pad_maximum_fusion.refs_0_), channel_id=1, source_target_pairs={{0,8},{8,16},{16,24},{24,0},{1,9},{9,17},{17,25},{25,1},{2,10},{10... | collective-permute-start | bytes 1327112 | tf_op jit(solution)/shard_map/ppermute | solution.py:237
  455.4 37.9 %collective-permute-start.50 = (bf16[192,1152]{1,0:T(8,128)(2,1)S(1)}, bf16[192,1152]{1,0:T(8,128)(2,1)S(1)}, u32[]{:S(2)}, u32[]{:S(2)}) collective-permute-start(bf16[192,1152]{1,0:T(8,128)(2,1)S(1)} %pad_maximum_fusion.refs_0_), channel_id=1, source_target_pairs={{0,16},{8,24},{16,0},{24,8},{1,17},{9,25},{17,1},{25,9},{2,18},{10... | collective-permute-start | bytes 1327112 | tf_op jit(solution)/shard_map/ppermute | solution.py:237
  455.4 37.9 %collective-permute-start.51 = (bf16[192,1152]{1,0:T(8,128)(2,1)S(1)}, bf16[192,1152]{1,0:T(8,128)(2,1)S(1)}, u32[]{:S(2)}, u32[]{:S(2)}) collective-permute-start(bf16[192,1152]{1,0:T(8,128)(2,1)S(1)} %pad_maximum_fusion.refs_0_), channel_id=1, source_target_pairs={{0,24},{8,0},{16,8},{24,16},{1,25},{9,1},{17,9},{25,17},{2,26},{10... | collective-permute-start | bytes 1327112 | tf_op jit(solution)/shard_map/ppermute | solution.py:237
  (107 other events, 795.5 us)
Sparse Core Ops, SparseCore 0:
  10.8 28.3 all-gather.6
  41.2 47.8 all-gather.8
  91.5 58.2 all-gather.10
  152.1 52.2 all-gather.12
  290.1 42.0 all-gather.14

commit v18 on v14

--- a/solution.py
+++ b/solution.py
@@ -897,9 +897,17 @@
     steps.append(relay_step(steps[1], seqs))
     far = after(far, steps[1], grad_down)
     pairs = kv_pair_sums(near, [hop(each, shards, 1) for each in far])
-    out_sums = pair_sums(out_near, after(out_there, pairs), shard)
+    out_pair = out_near.astype(F32) + after(out_there, pairs).astype(F32)
+    out_sums = lax.all_to_all(
+        out_pair.astype(BF),
+        "fsdp",
+        split_axis=0,
+        concat_axis=0,
+        tiled=True,
+        axis_index_groups=[list(range(core, shards, 2)) for core in range(2)],
+    )
     sent_grads, product_columns = head_columns(
-        grad_q, after(send_chips(pairs, shards), out_sums, steps[2]), factor_local, ride_columns
+        grad_q, after(send_chips(pairs, shards), out_pair, steps[2]), factor_local, ride_columns
     )
     steps[2] = after(steps[2], product_columns)
     while len(steps) < seqs:
@@ -925,8 +933,7 @@
     )
     head_part = by_rows(head_part.astype(BF))
     head_last = [by_rows(each) for each in send_out([head_part] * seqs, seqs)]
-    out_blocks = send_chips(after(out_sums, head_part), shards)
-    out_part = total_of(out_blocks).astype(BF)
+    out_part = jnp.sum(after(out_sums, head_sums).astype(F32), axis=0).astype(BF)
     out_parts = lax.all_to_all(
         out_part.reshape(part, seqs, q_cols), "seq", split_axis=1, concat_axis=1, tiled=True
     )

time: 496 us -> 528 us (1.065)
  waiting for transfers between devices: 171 us -> 195 us
    ppermute x28 -> x25, waiting for transfers between devices: 39.8 us -> 52.1 us  [hop(): return lax.ppermute(block, 'fsdp', [(i, i ^ mask) for i in range(count)])]
    all_to_all x1, waiting for transfers between devices: 0.01 us -> 8.73 us  [local(): lax.all_to_all(out_part.reshape(part, seqs, q_cols), 'seq', split_axis=1,...]
    ppermute x28 -> x25, starting transfers between devices: 26.5 us -> 22 us  [hop(): return lax.ppermute(block, 'fsdp', [(i, i ^ mask) for i in range(count)])]
    unnamed x212 -> x208, local copies, waits for them, and re-layouts: 25.2 us -> 28.8 us
  transfers between devices with their start and end apart: 64 -> 62, of which waited for: 30 -> 32; matrix products, arithmetic and copies ran while one was open for 12% -> 11% of each run, Pallas kernels for 17% -> 16%
where the time goes in v18:
time: 528 us; the launch traced here: 518 us
  waiting for transfers between devices  195 us (37%)
  starting transfers between devices  108 us (20%)
  Pallas kernels  98.7 us (19%)
  local copies, waits for them, and re-layouts  40.2 us (8%)
  other arithmetic  34.2 us (6%)
  matrix products  20.9 us (4%)
  between operations  20.9 us (4%)
    ppermute x21, waiting for transfers between devices, shift(): lax.ppermute(block, 'seq', [(i, (i + step) % count) for i in range(count)])  108 us
    ppermute x25, waiting for transfers between devices, hop(): return lax.ppermute(block, 'fsdp', [(i, i ^ mask) for i in range(count)])  52.1 us
    ppermute x21, starting transfers between devices, shift(): lax.ppermute(block, 'seq', [(i, (i + step) % count) for i in range(count)])  36.6 us
    unnamed x208, local copies, waits for them, and re-layouts  28.8 us
    pallas_call x2, Pallas kernels, flash_backward(): pl.pallas_call(functools.partial(backward_kernel, shards, seqs, rows, g,...  27.7 us
    ppermute x25, starting transfers between devices, hop(): return lax.ppermute(block, 'fsdp', [(i, i ^ mask) for i in range(count)])  22 us
    pallas_call x1, Pallas kernels, flash_forward(): pl.pallas_call(functools.partial(forward_kernel, shards, seqs, rows, loca...  19 us
    pallas_call x4, Pallas kernels, split_product(): pl.pallas_call(product_kernel, grid=(count // 2,), in_specs=[pl.BlockSpec...  14.7 us
  transfers between devices with their start and end apart: 62, of which 32 were waited for; matrix products, arithmetic and copies ran while one was open for 11% of the time, Pallas kernels for 16%

profile of v18, /device:TPU:12, one launch (start us, length us, event | category | flops | bytes accessed | tf_op | source)
XLA Modules:
  0.0 518.0 jit_solution(10938115837485506256)
XLA Ops:
  22.3 23.3 %collective-permute-done = bf16[136,1536]{1,0:T(8,128)(2,1)S(1)} collective-permute-done((bf16[136,1536]{1,0:T(8,128)(2,1)S(1)}, bf16[136,1536]{1,0:T(8,128)(2,1)S(1)}, u32[]{:S(2)}, u32[]{:S(2)}) %collective-permute-start) | collective-permute-done | bytes 417824 | tf_op jit(solution)/shard_map/ppermute | solution.py:237
  45.6 7.8 %collective-permute-done.1 = bf16[136,1536]{1,0:T(8,128)(2,1)S(1)} collective-permute-done((bf16[136,1536]{1,0:T(8,128)(2,1)S(1)}, bf16[136,1536]{1,0:T(8,128)(2,1)S(1)}, u32[]{:S(2)}, u32[]{:S(2)}) %collective-permute-start.1) | collective-permute-done | bytes 417824 | tf_op jit(solution)/shard_map/ppermute | solution.py:237
  63.8 9.2 %collective-permute-done.3.refs_1_ = bf16[528,256]{1,0:T(8,128)(2,1)S(1)} collective-permute-done((bf16[528,256]{1,0:T(8,128)(2,1)S(1)}, bf16[528,256]{1,0:T(8,128)(2,1)S(1)}, u32[]{:S(2)}, u32[]{:S(2)}) %collective-permute-start.3) | collective-permute-done | bytes 270368 | tf_op jit(solution)/shard_map/ppermute | solution.py:263
  73.0 7.1 %collective-permute-done.4.refs_2_ = bf16[528,256]{1,0:T(8,128)(2,1)S(1)} collective-permute-done((bf16[528,256]{1,0:T(8,128)(2,1)S(1)}, bf16[528,256]{1,0:T(8,128)(2,1)S(1)}, u32[]{:S(2)}, u32[]{:S(2)}) %collective-permute-start.4) | collective-permute-done | bytes 270368 | tf_op jit(solution)/shard_map/ppermute | solution.py:263
  80.0 3.7 collective-permute-done.5.refs_3_
  86.0 19.0 %shard_map.221 = (bf16[512,384]{1,0:T(8,128)(2,1)}, f32[512,384]{1,0:T(8,128)S(1)}, f32[512,384]{1,0:T(8,128)S(1)}) custom-call(bf16[528,256]{1,0:T(8,128)(2,1)S(1)} %maximum_maximum_fusion.1.refs_0_, bf16[528,256]{1,0:T(8,128)(2,1)S(1)} %collective-permute-done.3.refs_1_, bf16[528,256]{1,0:T(8,128)(2,1)S(1)} %collective-permute-done.4.refs_2_, ...), custom_call_target="tpu_custom_call" | custom-call | tf_op jit(solution)/shard_map/pallas_call | solution.py:114
  106.8 3.4 all-to-all-start
  111.1 8.6 %all-to-all-done = bf16[4,128,384]{2,1,0:T(8,128)(2,1)S(1)} async-done(((bf16[4,128,384]{2,1,0:T(8,128)(2,1)}), bf16[4,128,384]{2,1,0:T(8,128)(2,1)S(1)}, u32[]{:S(2)}, u32[]{:S(2)}) %all-to-all-start) | async-done | bytes 393248 | tf_op jit(solution)/shard_map/all_to_all | solution.py:796
  121.7 4.4 multiply_reduce_fusion.5
  129.8 3.1 collective-permute-start.11
  135.2 14.6 %collective-permute-done.10.refs_1_ = bf16[96,1536]{1,0:T(8,128)(2,1)} collective-permute-done((bf16[96,1536]{1,0:T(8,128)(2,1)S(1)}, bf16[96,1536]{1,0:T(8,128)(2,1)}, u32[]{:S(2)}, u32[]{:S(2)}) %collective-permute-start.10) | collective-permute-done | bytes 294944 | tf_op jit(solution)/shard_map/ppermute | solution.py:237
  149.8 4.9 collective-permute-done.11.refs_2_
  157.8 8.9 %shard_map.222 = (bf16[384,1536]{1,0:T(8,128)(2,1)}, f32[384,2048]{1,0:T(8,128)}, bf16[384,1024]{1,0:T(8,128)(2,1)}, bf16[96,1536]{1,0:T(8,128)(2,1)}, bf16[96,1...) custom-call(bf16[96,1536]{1,0:T(8,128)(2,1)} %get-tuple-element.352.refs_0_, ...), custom_call_target="tpu_custom_call" | custom-call | tf_op jit(solution)/shard_map/pallas_call | solution.py:396
  171.3 18.3 %collective-permute-done.13 = bf16[96,1536]{1,0:T(8,128)(2,1)S(1)} collective-permute-done((bf16[96,1536]{1,0:T(8,128)(2,1)}, bf16[96,1536]{1,0:T(8,128)(2,1)S(1)}, u32[]{:S(2)}, u32[]{:S(2)}) %collective-permute-start.13) | collective-permute-done | bytes 294944 | tf_op jit(solution)/shard_map/ppermute | solution.py:237
  199.7 3.2 collective-permute-start.17
  205.4 14.3 %collective-permute-done.16.refs_1_ = bf16[96,1536]{1,0:T(8,128)(2,1)S(1)} collective-permute-done((bf16[96,1536]{1,0:T(8,128)(2,1)S(1)}, bf16[96,1536]{1,0:T(8,128)(2,1)S(1)}, u32[]{:S(2)}, u32[]{:S(2)}) %collective-permute-start.16) | collective-permute-done | bytes 294944 | tf_op jit(solution)/shard_map/ppermute | solution.py:237
  219.7 5.5 %collective-permute-done.17.refs_2_ = bf16[96,1536]{1,0:T(8,128)(2,1)S(1)} collective-permute-done((bf16[96,1536]{1,0:T(8,128)(2,1)S(1)}, bf16[96,1536]{1,0:T(8,128)(2,1)S(1)}, u32[]{:S(2)}, u32[]{:S(2)}) %collective-permute-start.17) | collective-permute-done | bytes 294944 | tf_op jit(solution)/shard_map/ppermute | solution.py:237
  227.1 9.9 %shard_map.223 = (bf16[384,1536]{1,0:T(8,128)(2,1)}, bf16[384,2048]{1,0:T(8,128)(2,1)}, bf16[96,1536]{1,0:T(8,128)(2,1)}, bf16[96,1536]{1,0:T(8,128)(2,1)}, bf16...) custom-call(bf16[96,1536]{1,0:T(8,128)(2,1)} %get-tuple-element.170.refs_0_, bf16[96,1536]{1,0:T(8,128)(2,1)} %copy-done.70, ...), custom_call_target="tpu_custom_call" | custom-call | tf_op jit(solution)/shard_map/pallas_call | solution.py:445
  247.1 4.9 shard_map.226
  271.8 8.9 %all-to-all-start.1 = ((bf16[128,4,384]{2,0,1:T(8,128)(2,1)}), bf16[128,4,384]{2,0,1:T(8,128)(2,1)}, u32[]{:S(2)}, u32[]{:S(2)}) async-start(bf16[128,4,384]{2,0,1:T(8,128)(2,1)} %bitcast.147), calls=%async_computation.1 | async-start | bytes 786432 | tf_op jit(solution)/shard_map/all_to_all | solution.py:872
  295.0 13.8 %shard_map.228 = (f32[512,192]{1,0:T(8,128)S(1)}, bf16[4,512,128]{2,1,0:T(8,128)(2,1)S(1)}, bf16[4,512,128]{2,1,0:T(8,128)(2,1)S(1)}) custom-call(bf16[8,528,256]{2,1,0:T(8,128)(2,1)S(1)} %copy-done.6, bf16[512,384]{1,0:T(8,128)(2,1)S(1)} %slice_multiply_fusion.refs_8_.refs_1_, f32[8,1,1024]{2,1,0:T(1,128)S(1)} %pad_maximum_fusion.3.refs_9_.refs_2_, ...), custom_call_target="tpu_custom_call" | custom-call | flops 999999995904 | tf_op jit(solution)/shard_map/pallas_call | solution.py:212
  308.9 6.0 %collective-permute-done.29 = bf16[192,2048]{1,0:T(8,128)(2,1)} collective-permute-done((bf16[192,2048]{1,0:T(8,128)(2,1)}, bf16[192,2048]{1,0:T(8,128)(2,1)}, u32[]{:S(2)}, u32[]{:S(2)}) %collective-permute-start.29) | collective-permute-done | bytes 786464 | tf_op jit(solution)/shard_map/ppermute | solution.py:263
  317.2 3.4 collective-permute-start.31
  320.6 3.6 collective-permute-start.32
  324.2 13.8 %shard_map.230 = (f32[512,192]{1,0:T(8,128)S(1)}, bf16[4,512,128]{2,1,0:T(8,128)(2,1)S(1)}, bf16[4,512,128]{2,1,0:T(8,128)(2,1)S(1)}) custom-call(bf16[8,528,256]{2,1,0:T(8,128)(2,1)S(1)} %copy-done.6, bf16[512,384]{1,0:T(8,128)(2,1)S(1)} %slice_multiply_fusion.refs_8_.refs_1_, f32[8,1,1024]{2,1,0:T(1,128)S(1)} %pad_maximum_fusion.3.refs_9_.refs_2_, ...), custom_call_target="tpu_custom_call" | custom-call | tf_op jit(solution)/shard_map/pallas_call | solution.py:212
  340.4 3.4 collective-permute-done.31.refs_1_
  345.5 3.2 collective-permute-start.38
  348.7 3.5 collective-permute-start.39
  359.8 5.8 %collective-permute-done.35.refs_3_ = bf16[512,256]{1,0:T(8,128)(2,1)S(1)} collective-permute-done((bf16[512,256]{1,0:T(8,128)(2,1)}, bf16[512,256]{1,0:T(8,128)(2,1)S(1)}, u32[]{:S(2)}, u32[]{:S(2)}) %collective-permute-start.35) | collective-permute-done | bytes 262176 | tf_op jit(solution)/shard_map/ppermute | solution.py:263
  365.6 5.3 %collective-permute-done.36.refs_4_ = bf16[512,256]{1,0:T(8,128)(2,1)} collective-permute-done((bf16[512,256]{1,0:T(8,128)(2,1)}, bf16[512,256]{1,0:T(8,128)(2,1)}, u32[]{:S(2)}, u32[]{:S(2)}) %collective-permute-start.36) | collective-permute-done | bytes 262176 | tf_op jit(solution)/shard_map/ppermute | solution.py:263
  379.4 4.9 all-to-all-start.4
  385.6 4.4 shard_map.233
  391.1 3.7 fusion.58
  397.6 5.0 all-to-all-start.2
  402.6 3.5 collective-permute-start.44
  406.1 4.1 collective-permute-start.45
  417.2 6.9 %collective-permute-done.44.refs_3_ = bf16[192,2048]{1,0:T(8,128)(2,1)} collective-permute-done((bf16[192,2048]{1,0:T(8,128)(2,1)}, bf16[192,2048]{1,0:T(8,128)(2,1)}, u32[]{:S(2)}, u32[]{:S(2)}) %collective-permute-start.44) | collective-permute-done | bytes 786464 | tf_op jit(solution)/shard_map/ppermute | solution.py:251
  426.2 11.2 %collective-permute-done.41 = bf16[192,768]{1,0:T(8,128)(2,1)S(1)} collective-permute-done((bf16[192,768]{1,0:T(8,128)(2,1)}, bf16[192,768]{1,0:T(8,128)(2,1)S(1)}, u32[]{:S(2)}, u32[]{:S(2)}) %collective-permute-start.41) | collective-permute-done | bytes 294944 | tf_op jit(solution)/shard_map/ppermute | solution.py:263
  437.5 3.6 collective-permute-done.43
  446.6 4.3 collective-permute-start.47
  454.1 5.6 %all-to-all-start.3 = ((bf16[192,4,384]{2,0,1:T(8,128)(2,1)}), bf16[192,4,384]{2,0,1:T(8,128)(2,1)}, u32[]{:S(2)}, u32[]{:S(2)}) async-start(bf16[192,4,384]{2,0,1:T(8,128)(2,1)} %bitcast.136), calls=%async_computation.3 | async-start | bytes 1179648 | tf_op jit(solution)/shard_map/all_to_all | solution.py:937
  459.6 6.3 %fusion.27 = (f32[128]{0:T(128)S(1)}, f32[128]{0:T(128)S(1)}, f32[128,1536]{1,0:T(8,128)S(1)}) fusion(bf16[128,1536]{1,0:T(8,128)(2,1)S(1)} %copy-done.56, bf16[128,2560]{0,1:T(8,128)(2,1)} %bitcast.55, bf16[1536,2560]{1,0:T(8,128)(2,1)} %all-gather.13.cloned.1.call-done), kind=kOutput, calls=%fused_computation.47 | convolution fusion | flops 1007615744 | bytes 9700352 | tf_op jit(solution)/shard_map/dot_general | solution.py:28
  466.0 8.2 %shard_map.235 = (f32[4,192,2048]{2,1,0:T(8,128)}, f32[192,128]{1,0:T(8,128)S(1)}) custom-call(s32[1]{0:T(128)} %bitcast.33.place_ref, bf16[192,2048]{1,0:T(8,128)(2,1)S(1)} %add_convert_fusion.refs_0_, bf16[192,2048]{1,0:T(8,128)(2,1)} %collective-permute-done.31.refs_1_, bf16[192,2048]{1,0:T(8,128)(2,1)} %collective-permute-done.38.refs_2_, ...), custom_call_target="tpu_custom_call" | custom-call | tf_op jit(solution)/shard_map/pallas_call | solution.py:583
  476.0 8.7 %all-to-all-done.3 = bf16[192,4,384]{2,0,1:T(8,128)(2,1)} async-done(((bf16[192,4,384]{2,0,1:T(8,128)(2,1)}), bf16[192,4,384]{2,0,1:T(8,128)(2,1)}, u32[]{:S(2)}, u32[]{:S(2)}) %all-to-all-start.3) | async-done | bytes 589856 | tf_op jit(solution)/shard_map/all_to_all | solution.py:937
  487.7 4.3 collective-permute-start.50
  492.0 3.6 convert_bitcast_fusion
  495.7 4.3 collective-permute-done.50.refs_6_
  500.0 3.5 collective-permute-done.51.refs_7_
  (428 shorter events, 155.8 us)
Async XLA Ops:
  7.2 48.7 %all-gather.7.cloned.1.call-start = ((), (), s32[]{:S(2)}) async-start(), calls=%async_computation.5 | async-start | bytes 2211840 | tf_op jit(solution)/shard_map/all_gather | solution.py:720
  10.7 111.0 %all-gather.9.cloned.1.call-start = ((), (), s32[]{:S(2)}) async-start(), calls=%async_computation.6 | async-start | bytes 5308416 | tf_op jit(solution)/shard_map/all_gather | solution.py:747
  11.4 146.3 %all-gather.11.cloned.1.call-start = ((), (), s32[]{:S(2)}) async-start(), calls=%async_computation.7 | async-start | bytes 11059200 | tf_op jit(solution)/shard_map/all_gather | solution.py:762
  16.0 189.4 %all-gather.13.cloned.1.call-start = ((), (), s32[]{:S(2)}) async-start(), calls=%async_computation.8 | async-start | bytes 8847360 | tf_op jit(solution)/shard_map/all_gather | solution.py:775
  16.1 29.6 %collective-permute-start = (bf16[136,1536]{1,0:T(8,128)(2,1)S(1)}, bf16[136,1536]{1,0:T(8,128)(2,1)S(1)}, u32[]{:S(2)}, u32[]{:S(2)}) collective-permute-start(bf16[136,1536]{1,0:T(8,128)(2,1)S(1)} %fusion.36), channel_id=1, source_target_pairs={{0,8},{8,16},{16,24},{24,0},{1,9},{9,17},{17,25},{25,1},{2,10},{10... | collective-permute-start | bytes 1253384 | tf_op jit(solution)/shard_map/ppermute | solution.py:237
  17.7 35.8 %collective-permute-start.1 = (bf16[136,1536]{1,0:T(8,128)(2,1)S(1)}, bf16[136,1536]{1,0:T(8,128)(2,1)S(1)}, u32[]{:S(2)}, u32[]{:S(2)}) collective-permute-start(bf16[136,1536]{1,0:T(8,128)(2,1)S(1)} %fusion.36), channel_id=1, source_target_pairs={{0,16},{8,24},{16,0},{24,8},{1,17},{9,25},{17,1},{25,9},{2,18},{10... | collective-permute-start | bytes 1253384 | tf_op jit(solution)/shard_map/ppermute | solution.py:237
  18.9 36.3 %collective-permute-start.2 = (bf16[136,1536]{1,0:T(8,128)(2,1)S(1)}, bf16[136,1536]{1,0:T(8,128)(2,1)S(1)}, u32[]{:S(2)}, u32[]{:S(2)}) collective-permute-start(bf16[136,1536]{1,0:T(8,128)(2,1)S(1)} %fusion.36), channel_id=1, source_target_pairs={{0,24},{8,0},{16,8},{24,16},{1,25},{9,1},{17,9},{25,17},{2,26},{10... | collective-permute-start | bytes 1253384 | tf_op jit(solution)/shard_map/ppermute | solution.py:237
  61.6 18.4 %collective-permute-start.4 = (bf16[528,256]{1,0:T(8,128)(2,1)S(1)}, bf16[528,256]{1,0:T(8,128)(2,1)S(1)}, u32[]{:S(2)}, u32[]{:S(2)}) collective-permute-start(bf16[528,256]{1,0:T(8,128)(2,1)S(1)} %maximum_maximum_fusion.1.refs_0_), channel_id=1, source_target_pairs={{0,4},{1,5},{2,6},{3,7},{4,0},{5,1},{6,2},{7,3},{8,12},{9,13},{10,... | collective-permute-start | bytes 811016 | tf_op jit(solution)/shard_map/ppermute | solution.py:263
  62.1 21.6 %collective-permute-start.5 = (bf16[528,256]{1,0:T(8,128)(2,1)S(1)}, bf16[528,256]{1,0:T(8,128)(2,1)S(1)}, u32[]{:S(2)}, u32[]{:S(2)}) collective-permute-start(bf16[528,256]{1,0:T(8,128)(2,1)S(1)} %maximum_maximum_fusion.1.refs_0_), channel_id=1, source_target_pairs={{0,6},{1,7},{2,4},{3,5},{4,2},{5,3},{6,0},{7,1},{8,14},{9,15},{10,... | collective-permute-start | bytes 811016 | tf_op jit(solution)/shard_map/ppermute | solution.py:263
  63.7 21.4 %collective-permute-start.6 = (bf16[528,256]{1,0:T(8,128)(2,1)S(1)}, bf16[528,256]{1,0:T(8,128)(2,1)S(1)}, u32[]{:S(2)}, u32[]{:S(2)}) collective-permute-start(bf16[528,256]{1,0:T(8,128)(2,1)S(1)} %maximum_maximum_fusion.1.refs_0_), channel_id=1, source_target_pairs={{0,1},{1,0},{2,3},{3,2},{4,5},{5,4},{6,7},{7,6},{8,9},{9,8},{10,11... | collective-permute-start | bytes 811016 | tf_op jit(solution)/shard_map/ppermute | solution.py:263
  128.5 21.3 %collective-permute-start.10 = (bf16[96,1536]{1,0:T(8,128)(2,1)S(1)}, bf16[96,1536]{1,0:T(8,128)(2,1)}, u32[]{:S(2)}, u32[]{:S(2)}) collective-permute-start(bf16[96,1536]{1,0:T(8,128)(2,1)S(1)} %get-tuple-element.351), channel_id=1, source_target_pairs={{0,8},{8,16},{16,24},{24,0},{1,9},{9,17},{17,25},{25,1},{2,10},{10... | collective-permute-start | bytes 884744 | tf_op jit(solution)/shard_map/ppermute | solution.py:237
  129.8 24.9 %collective-permute-start.11 = (bf16[96,1536]{1,0:T(8,128)(2,1)S(1)}, bf16[96,1536]{1,0:T(8,128)(2,1)}, u32[]{:S(2)}, u32[]{:S(2)}) collective-permute-start(bf16[96,1536]{1,0:T(8,128)(2,1)S(1)} %get-tuple-element.350), channel_id=1, source_target_pairs={{0,16},{8,24},{16,0},{24,8},{1,17},{9,25},{17,1},{25,9},{2,18},{10... | collective-permute-start | bytes 884744 | tf_op jit(solution)/shard_map/ppermute | solution.py:237
  133.0 24.8 %collective-permute-start.12 = (bf16[96,1536]{1,0:T(8,128)(2,1)S(1)}, bf16[96,1536]{1,0:T(8,128)(2,1)}, u32[]{:S(2)}, u32[]{:S(2)}) collective-permute-start(bf16[96,1536]{1,0:T(8,128)(2,1)S(1)} %get-tuple-element.349), channel_id=1, source_target_pairs={{0,24},{8,0},{16,8},{24,16},{1,25},{9,1},{17,9},{25,17},{2,26},{10... | collective-permute-start | bytes 884744 | tf_op jit(solution)/shard_map/ppermute | solution.py:237
  166.7 22.8 %collective-permute-start.13 = (bf16[96,1536]{1,0:T(8,128)(2,1)}, bf16[96,1536]{1,0:T(8,128)(2,1)S(1)}, u32[]{:S(2)}, u32[]{:S(2)}) collective-permute-start(bf16[96,1536]{1,0:T(8,128)(2,1)} %get-tuple-element.153), channel_id=1, source_target_pairs={{0,24},{8,0},{16,8},{24,16},{1,25},{9,1},{17,9},{25,17},{2,26},{10... | collective-permute-start | bytes 884744 | tf_op jit(solution)/shard_map/ppermute | solution.py:237
  166.8 22.8 %collective-permute-start.14 = (bf16[96,1536]{1,0:T(8,128)(2,1)}, bf16[96,1536]{1,0:T(8,128)(2,1)S(1)}, u32[]{:S(2)}, u32[]{:S(2)}) collective-permute-start(bf16[96,1536]{1,0:T(8,128)(2,1)} %get-tuple-element.154), channel_id=1, source_target_pairs={{0,16},{8,24},{16,0},{24,8},{1,17},{9,25},{17,1},{25,9},{2,18},{10... | collective-permute-start | bytes 884744 | tf_op jit(solution)/shard_map/ppermute | solution.py:237
  167.4 24.9 %collective-permute-start.15 = (bf16[96,1536]{1,0:T(8,128)(2,1)}, bf16[96,1536]{1,0:T(8,128)(2,1)S(1)}, u32[]{:S(2)}, u32[]{:S(2)}) collective-permute-start(bf16[96,1536]{1,0:T(8,128)(2,1)} %get-tuple-element.155), channel_id=1, source_target_pairs={{0,8},{8,16},{16,24},{24,0},{1,9},{9,17},{17,25},{25,1},{2,10},{10... | collective-permute-start | bytes 884744 | tf_op jit(solution)/shard_map/ppermute | solution.py:237
  197.3 22.4 %collective-permute-start.16 = (bf16[96,1536]{1,0:T(8,128)(2,1)S(1)}, bf16[96,1536]{1,0:T(8,128)(2,1)S(1)}, u32[]{:S(2)}, u32[]{:S(2)}) collective-permute-start(bf16[96,1536]{1,0:T(8,128)(2,1)S(1)} %get-tuple-element.347), channel_id=1, source_target_pairs={{0,8},{8,16},{16,24},{24,0},{1,9},{9,17},{17,25},{25,1},{2,10},{10... | collective-permute-start | bytes 884744 | tf_op jit(solution)/shard_map/ppermute | solution.py:237
  199.7 25.5 %collective-permute-start.17 = (bf16[96,1536]{1,0:T(8,128)(2,1)S(1)}, bf16[96,1536]{1,0:T(8,128)(2,1)S(1)}, u32[]{:S(2)}, u32[]{:S(2)}) collective-permute-start(bf16[96,1536]{1,0:T(8,128)(2,1)S(1)} %get-tuple-element.346), channel_id=1, source_target_pairs={{0,16},{8,24},{16,0},{24,8},{1,17},{9,25},{17,1},{25,9},{2,18},{10... | collective-permute-start | bytes 884744 | tf_op jit(solution)/shard_map/ppermute | solution.py:237
  202.9 23.6 %collective-permute-start.18 = (bf16[96,1536]{1,0:T(8,128)(2,1)S(1)}, bf16[96,1536]{1,0:T(8,128)(2,1)S(1)}, u32[]{:S(2)}, u32[]{:S(2)}) collective-permute-start(bf16[96,1536]{1,0:T(8,128)(2,1)S(1)} %get-tuple-element.345), channel_id=1, source_target_pairs={{0,24},{8,0},{16,8},{24,16},{1,25},{9,1},{17,9},{25,17},{2,26},{10... | collective-permute-start | bytes 884744 | tf_op jit(solution)/shard_map/ppermute | solution.py:237
  237.0 22.8 %collective-permute-start.19 = (bf16[96,1536]{1,0:T(8,128)(2,1)}, bf16[96,1536]{1,0:T(8,128)(2,1)S(1)}, u32[]{:S(2)}, u32[]{:S(2)}) collective-permute-start(bf16[96,1536]{1,0:T(8,128)(2,1)} %get-tuple-element.176), channel_id=1, source_target_pairs={{0,24},{8,0},{16,8},{24,16},{1,25},{9,1},{17,9},{25,17},{2,26},{10... | collective-permute-start | bytes 884744 | tf_op jit(solution)/shard_map/ppermute | solution.py:237
  237.1 24.9 %collective-permute-start.20 = (bf16[96,1536]{1,0:T(8,128)(2,1)}, bf16[96,1536]{1,0:T(8,128)(2,1)S(1)}, u32[]{:S(2)}, u32[]{:S(2)}) collective-permute-start(bf16[96,1536]{1,0:T(8,128)(2,1)} %get-tuple-element.177), channel_id=1, source_target_pairs={{0,16},{8,24},{16,0},{24,8},{1,17},{9,25},{17,1},{25,9},{2,18},{10... | collective-permute-start | bytes 884744 | tf_op jit(solution)/shard_map/ppermute | solution.py:237
  239.5 25.0 %collective-permute-start.21 = (bf16[96,1536]{1,0:T(8,128)(2,1)}, bf16[96,1536]{1,0:T(8,128)(2,1)S(1)}, u32[]{:S(2)}, u32[]{:S(2)}) collective-permute-start(bf16[96,1536]{1,0:T(8,128)(2,1)} %get-tuple-element.178), channel_id=1, source_target_pairs={{0,8},{8,16},{16,24},{24,0},{1,9},{9,17},{17,25},{25,1},{2,10},{10... | collective-permute-start | bytes 884744 | tf_op jit(solution)/shard_map/ppermute | solution.py:237
  251.9 15.6 %collective-permute-start.23 = (bf16[4,192,2048]{2,1,0:T(8,128)(2,1)S(1)}, bf16[4,192,2048]{2,1,0:T(8,128)(2,1)S(1)}, u32[]{:S(2)}, u32[]{:S(2)}) collective-permute-start(bf16[4,192,2048]{2,1,0:T(8,128)(2,1)S(1)} %get-tuple-element.202), channel_id=1, source_target_pairs={{0,1},{1,0},{2,3},{3,2},{4,5},{5,4},{6,7},{7,6},{8,9},{9,8},{10,11... | collective-permute-start | bytes 9437192 | tf_op jit(solution)/shard_map/ppermute | solution.py:263
  255.4 25.9 %collective-permute-start.24 = (bf16[192,1024]{1,0:T(8,128)(2,1)}, bf16[192,1024]{1,0:T(8,128)(2,1)}, u32[]{:S(2)}, u32[]{:S(2)}) collective-permute-start(bf16[192,1024]{1,0:T(8,128)(2,1)} %get-tuple-element.190), channel_id=1, source_target_pairs={{0,2},{1,3},{2,0},{3,1},{4,6},{5,7},{6,4},{7,5},{8,10},{9,11},{10,... | collective-permute-start | bytes 1179656 | tf_op jit(solution)/shard_map/ppermute | solution.py:263
  259.9 24.3 %collective-permute-start.25 = (bf16[192,1024]{1,0:T(8,128)(2,1)}, bf16[192,1024]{1,0:T(8,128)(2,1)}, u32[]{:S(2)}, u32[]{:S(2)}) collective-permute-start(bf16[192,1024]{1,0:T(8,128)(2,1)} %get-tuple-element.191), channel_id=1, source_target_pairs={{0,4},{1,5},{2,6},{3,7},{4,0},{5,1},{6,2},{7,3},{8,12},{9,13},{10,... | collective-permute-start | bytes 1179656 | tf_op jit(solution)/shard_map/ppermute | solution.py:263
  262.0 22.2 %collective-permute-start.26 = (bf16[192,1024]{1,0:T(8,128)(2,1)}, bf16[192,1024]{1,0:T(8,128)(2,1)}, u32[]{:S(2)}, u32[]{:S(2)}) collective-permute-start(bf16[192,1024]{1,0:T(8,128)(2,1)} %get-tuple-element.192), channel_id=1, source_target_pairs={{0,6},{1,7},{2,4},{3,5},{4,2},{5,3},{6,0},{7,1},{8,14},{9,15},{10,... | collective-permute-start | bytes 1179656 | tf_op jit(solution)/shard_map/ppermute | solution.py:263
  271.8 20.4 %all-to-all-start.1 = ((bf16[128,4,384]{2,0,1:T(8,128)(2,1)}), bf16[128,4,384]{2,0,1:T(8,128)(2,1)}, u32[]{:S(2)}, u32[]{:S(2)}) async-start(bf16[128,4,384]{2,0,1:T(8,128)(2,1)} %bitcast.147), calls=%async_computation.1 | async-start | bytes 786432 | tf_op jit(solution)/shard_map/all_to_all | solution.py:872
  280.7 64.3 %all-gather.15.cloned.1.call-start = ((), (), s32[]{:S(2)}) async-start(), calls=%async_computation.9 | async-start | bytes 1966080 | tf_op jit(solution)/shard_map/all_gather | solution.py:875
  280.7 28.2 %collective-permute-start.27 = (bf16[192,2048]{1,0:T(8,128)(2,1)}, bf16[192,2048]{1,0:T(8,128)(2,1)}, u32[]{:S(2)}, u32[]{:S(2)}) collective-permute-start(bf16[192,2048]{1,0:T(8,128)(2,1)} %copy-done.45), channel_id=1, source_target_pairs={{0,2},{1,3},{2,0},{3,1},{4,6},{5,7},{6,4},{7,5},{8,10},{9,11},{10,... | collective-permute-start | bytes 2359304 | tf_op jit(solution)/shard_map/ppermute | solution.py:263
  280.7 28.2 %collective-permute-start.28 = (bf16[192,2048]{1,0:T(8,128)(2,1)}, bf16[192,2048]{1,0:T(8,128)(2,1)}, u32[]{:S(2)}, u32[]{:S(2)}) collective-permute-start(bf16[192,2048]{1,0:T(8,128)(2,1)} %copy-done.44), channel_id=1, source_target_pairs={{0,4},{1,5},{2,6},{3,7},{4,0},{5,1},{6,2},{7,3},{8,12},{9,13},{10,... | collective-permute-start | bytes 2359304 | tf_op jit(solution)/shard_map/ppermute | solution.py:263
  281.3 33.6 %collective-permute-start.29 = (bf16[192,2048]{1,0:T(8,128)(2,1)}, bf16[192,2048]{1,0:T(8,128)(2,1)}, u32[]{:S(2)}, u32[]{:S(2)}) collective-permute-start(bf16[192,2048]{1,0:T(8,128)(2,1)} %copy-done.43), channel_id=1, source_target_pairs={{0,6},{1,7},{2,4},{3,5},{4,2},{5,3},{6,0},{7,1},{8,14},{9,15},{10,... | collective-permute-start | bytes 2359304 | tf_op jit(solution)/shard_map/ppermute | solution.py:263
  292.2 32.1 %collective-permute-start.30 = (bf16[4,192,1536]{2,1,0:T(8,128)(2,1)}, bf16[4,192,1536]{2,1,0:T(8,128)(2,1)}, u32[]{:S(2)}, u32[]{:S(2)}) collective-permute-start(bf16[4,192,1536]{2,1,0:T(8,128)(2,1)} %copy-done.42), channel_id=1, source_target_pairs={{0,1},{1,0},{2,3},{3,2},{4,5},{5,4},{6,7},{7,6},{8,9},{9,8},{10,11... | collective-permute-start | bytes 7077896 | tf_op jit(solution)/shard_map/ppermute | solution.py:263
  317.2 26.7 %collective-permute-start.31 = (bf16[192,2048]{1,0:T(8,128)(2,1)S(1)}, bf16[192,2048]{1,0:T(8,128)(2,1)}, u32[]{:S(2)}, u32[]{:S(2)}) collective-permute-start(bf16[192,2048]{1,0:T(8,128)(2,1)S(1)} %add_convert_fusion.refs_0_), channel_id=1, source_target_pairs={{0,8},{8,16},{16,24},{1,9},{9,17},{17,25},{2,10},{10,18},{18,26},{... | collective-permute-start | bytes 2359304 | tf_op jit(solution)/shard_map/ppermute | solution.py:251
  320.6 24.4 %collective-permute-start.32 = (bf16[192,2048]{1,0:T(8,128)(2,1)S(1)}, bf16[192,2048]{1,0:T(8,128)(2,1)}, u32[]{:S(2)}, u32[]{:S(2)}) collective-permute-start(bf16[192,2048]{1,0:T(8,128)(2,1)S(1)} %add_convert_fusion.refs_0_), channel_id=1, source_target_pairs={{8,0},{16,8},{24,16},{9,1},{17,9},{25,17},{10,2},{18,10},{26,18},{... | collective-permute-start | bytes 2359304 | tf_op jit(solution)/shard_map/ppermute | solution.py:252
  345.5 25.4 %collective-permute-start.38 = (bf16[192,2048]{1,0:T(8,128)(2,1)}, bf16[192,2048]{1,0:T(8,128)(2,1)}, u32[]{:S(2)}, u32[]{:S(2)}) collective-permute-start(bf16[192,2048]{1,0:T(8,128)(2,1)} %collective-permute-done.31.refs_1_), channel_id=1, source_target_pairs={{0,8},{8,16},{16,24},{1,9},{9,17},{17,25},{2,10},{10,18},{18,26},{... | collective-permute-start | bytes 2359304 | tf_op jit(solution)/shard_map/ppermute | solution.py:251
  348.7 22.2 %collective-permute-start.39 = (bf16[192,2048]{1,0:T(8,128)(2,1)}, bf16[192,2048]{1,0:T(8,128)(2,1)}, u32[]{:S(2)}, u32[]{:S(2)}) collective-permute-start(bf16[192,2048]{1,0:T(8,128)(2,1)} %collective-permute-done.32.refs_4_), channel_id=1, source_target_pairs={{8,0},{16,8},{24,16},{9,1},{17,9},{25,17},{10,2},{18,10},{26,18},{... | collective-permute-start | bytes 2359304 | tf_op jit(solution)/shard_map/ppermute | solution.py:252
  379.4 18.2 %all-to-all-start.4 = ((bf16[4,128,640]{1,2,0:T(8,128)(2,1)}), bf16[4,128,640]{1,2,0:T(8,128)(2,1)}, u32[]{:S(2)}, u32[]{:S(2)}) async-start(bf16[4,128,640]{1,2,0:T(8,128)(2,1)} %copy.125), calls=%async_computation.4 | async-start | bytes 1310720 | tf_op jit(solution)/shard_map/all_to_all | solution.py:915
  391.1 19.1 %collective-permute-start.40 = (bf16[4,192,768]{2,1,0:T(8,128)(2,1)}, bf16[4,192,768]{2,1,0:T(8,128)(2,1)S(1)}, u32[]{:S(2)}, u32[]{:S(2)}) collective-permute-start(bf16[4,192,768]{2,1,0:T(8,128)(2,1)} %get-tuple-element.245), channel_id=1, source_target_pairs={{0,1},{1,0},{2,3},{3,2},{4,5},{5,4},{6,7},{7,6},{8,9},{9,8},{10,11... | collective-permute-start | bytes 3538952 | tf_op jit(solution)/shard_map/ppermute | solution.py:263
  397.6 53.3 %all-to-all-start.2 = ((bf16[4,192,1536]{2,1,0:T(8,128)(2,1)}), bf16[4,192,1536]{2,1,0:T(8,128)(2,1)}, u32[]{:S(2)}, u32[]{:S(2)}) async-start(bf16[4,192,1536]{2,1,0:T(8,128)(2,1)} %fusion.58), calls=%async_computation.2 | async-start | bytes 4718592 | tf_op jit(solution)/shard_map/all_to_all | solution.py:901
  402.6 21.6 %collective-permute-start.44 = (bf16[192,2048]{1,0:T(8,128)(2,1)}, bf16[192,2048]{1,0:T(8,128)(2,1)}, u32[]{:S(2)}, u32[]{:S(2)}) collective-permute-start(bf16[192,2048]{1,0:T(8,128)(2,1)} %collective-permute-done.38.refs_2_), channel_id=1, source_target_pairs={{0,8},{8,16},{16,24},{1,9},{9,17},{17,25},{2,10},{10,18},{18,26},{... | collective-permute-start | bytes 2359304 | tf_op jit(solution)/shard_map/ppermute | solution.py:251
  406.1 20.1 %collective-permute-start.45 = (bf16[192,2048]{1,0:T(8,128)(2,1)}, bf16[192,2048]{1,0:T(8,128)(2,1)}, u32[]{:S(2)}, u32[]{:S(2)}) collective-permute-start(bf16[192,2048]{1,0:T(8,128)(2,1)} %collective-permute-done.39.refs_5_), channel_id=1, source_target_pairs={{8,0},{16,8},{24,16},{9,1},{17,9},{25,17},{10,2},{18,10},{26,18},{... | collective-permute-start | bytes 2359304 | tf_op jit(solution)/shard_map/ppermute | solution.py:252
  412.7 24.7 %collective-permute-start.41 = (bf16[192,768]{1,0:T(8,128)(2,1)}, bf16[192,768]{1,0:T(8,128)(2,1)S(1)}, u32[]{:S(2)}, u32[]{:S(2)}) collective-permute-start(bf16[192,768]{1,0:T(8,128)(2,1)} %get-tuple-element.247), channel_id=1, source_target_pairs={{0,2},{1,3},{2,0},{3,1},{4,6},{5,7},{6,4},{7,5},{8,10},{9,11},{10,... | collective-permute-start | bytes 884744 | tf_op jit(solution)/shard_map/ppermute | solution.py:263
  414.2 23.3 %collective-permute-start.42 = (bf16[192,768]{1,0:T(8,128)(2,1)}, bf16[192,768]{1,0:T(8,128)(2,1)S(1)}, u32[]{:S(2)}, u32[]{:S(2)}) collective-permute-start(bf16[192,768]{1,0:T(8,128)(2,1)} %get-tuple-element.248), channel_id=1, source_target_pairs={{0,4},{1,5},{2,6},{3,7},{4,0},{5,1},{6,2},{7,3},{8,12},{9,13},{10,... | collective-permute-start | bytes 884744 | tf_op jit(solution)/shard_map/ppermute | solution.py:263
  414.7 26.4 %collective-permute-start.43 = (bf16[192,768]{1,0:T(8,128)(2,1)S(1)}, bf16[192,768]{1,0:T(8,128)(2,1)S(1)}, u32[]{:S(2)}, u32[]{:S(2)}) collective-permute-start(bf16[192,768]{1,0:T(8,128)(2,1)S(1)} %get-tuple-element.249), channel_id=1, source_target_pairs={{0,6},{1,7},{2,4},{3,5},{4,2},{5,3},{6,0},{7,1},{8,14},{9,15},{10,... | collective-permute-start | bytes 884744 | tf_op jit(solution)/shard_map/ppermute | solution.py:263
  444.3 47.6 %collective-permute-start.46 = (bf16[192,768]{1,0:T(8,128)(2,1)S(1)}, bf16[192,768]{1,0:T(8,128)(2,1)S(1)}, u32[]{:S(2)}, u32[]{:S(2)}) collective-permute-start(bf16[192,768]{1,0:T(8,128)(2,1)S(1)} %select_convert_fusion.refs_0_), channel_id=1, source_target_pairs={{0,8},{8,16},{16,24},{24,0},{1,9},{9,17},{17,25},{25,1},{2,10},{10... | collective-permute-start | bytes 884744 | tf_op jit(solution)/shard_map/ppermute | solution.py:237
  446.6 49.1 %collective-permute-start.47 = (bf16[192,768]{1,0:T(8,128)(2,1)S(1)}, bf16[192,768]{1,0:T(8,128)(2,1)S(1)}, u32[]{:S(2)}, u32[]{:S(2)}) collective-permute-start(bf16[192,768]{1,0:T(8,128)(2,1)S(1)} %select_convert_fusion.refs_0_), channel_id=1, source_target_pairs={{0,16},{8,24},{16,0},{24,8},{1,17},{9,25},{17,1},{25,9},{2,18},{10... | collective-permute-start | bytes 884744 | tf_op jit(solution)/shard_map/ppermute | solution.py:237
  450.9 44.8 %collective-permute-start.48 = (bf16[192,768]{1,0:T(8,128)(2,1)S(1)}, bf16[192,768]{1,0:T(8,128)(2,1)}, u32[]{:S(2)}, u32[]{:S(2)}) collective-permute-start(bf16[192,768]{1,0:T(8,128)(2,1)S(1)} %select_convert_fusion.refs_0_), channel_id=1, source_target_pairs={{0,24},{8,0},{16,8},{24,16},{1,25},{9,1},{17,9},{25,17},{2,26},{10... | collective-permute-start | bytes 884744 | tf_op jit(solution)/shard_map/ppermute | solution.py:237
  454.1 30.6 %all-to-all-start.3 = ((bf16[192,4,384]{2,0,1:T(8,128)(2,1)}), bf16[192,4,384]{2,0,1:T(8,128)(2,1)}, u32[]{:S(2)}, u32[]{:S(2)}) async-start(bf16[192,4,384]{2,0,1:T(8,128)(2,1)} %bitcast.136), calls=%async_computation.3 | async-start | bytes 1179648 | tf_op jit(solution)/shard_map/all_to_all | solution.py:937
  (102 other events, 741.9 us)
Sparse Core Ops, SparseCore 0:
  10.8 28.3 all-gather.6
  41.1 48.8 all-gather.8
  92.5 58.2 all-gather.10
  153.1 52.2 all-gather.12
  292.3 42.3 all-gather.14

commit v19 on v14

--- a/solution.py
+++ b/solution.py
@@ -46,7 +46,7 @@
 
 def forward_kernel(shards, seqs, rows, local_kv, groups, *refs):
     kv_refs = refs[:shards]
-    q_ref, bias_ref, low_ref, exact_ref, lse_ref, acc_ref, max_ref = refs[shards:]
+    q_ref, bias_ref, low_ref, lse_ref, acc_ref, max_ref = refs[shards:]
     zq = pl.program_id(0)
     stack = groups * rows
     zeros = jnp.zeros((rows, HD), BF)
@@ -98,9 +98,7 @@
         for h in range(groups):
             exact_parts.append(exact[h * rows : (h + 1) * rows])
             lse_parts.append(lse[h * rows : (h + 1) * rows])
-    exact = jnp.concatenate(exact_parts, axis=1)
-    exact_ref[...] = exact
-    low_ref[...] = exact.astype(BF)
+    low_ref[...] = jnp.concatenate(exact_parts, axis=1).astype(BF)
     lse_ref[...] = jnp.concatenate(lse_parts, axis=1)
 
 
@@ -115,8 +113,8 @@
         functools.partial(forward_kernel, shards, seqs, rows, local_kv, groups),
         grid=(seqs,),
         in_specs=[kv_spec] * shards + [q_spec, pl.BlockSpec(bias.shape, lambda i: (0, 0, 0))],
-        out_specs=[q_spec] * 3,
-        out_shape=[jax.ShapeDtypeStruct((seqs * rows, q_cols), BF), out, out],
+        out_specs=[q_spec] * 2,
+        out_shape=[jax.ShapeDtypeStruct((seqs * rows, q_cols), BF), out],
         scratch_shapes=[
             pltpu.VMEM((local_kv, stack, 2 * HD), F32),
             pltpu.VMEM((local_kv, stack, 2 * HD), F32),
@@ -133,7 +131,7 @@
 def backward_kernel(shards, seqs, rows, g, groups, *refs):
     kv_refs = [refs[0].at[p] for p in range(shards)]
     (
-        q_ref, bias_ref, grad_ref, exact_ref, lse_ref, grad_q_ref, near_ref, far_ref,
+        q_ref, bias_ref, grad_ref, low_ref, lse_ref, grad_q_ref, near_ref, far_ref,
         pair_ref, pair_t_ref, lse_wide, delta_wide, acc_q, acc_kv,
     ) = refs[1:]
     zk = pl.program_id(0)
@@ -153,7 +151,7 @@
                 grad = grad_ref[here, cols]
                 tops.append(jnp.concatenate([q_ref[here, cols], zeros], axis=1))
                 bottoms.append(jnp.concatenate([zeros, grad], axis=1))
-                delta = jnp.sum(grad.astype(F32) * exact_ref[here, cols], axis=1, keepdims=True)
+                delta = jnp.sum(grad.astype(F32) * low_ref[here, cols].astype(F32), axis=1, keepdims=True)
                 part = slice(h * rows, (h + 1) * rows)
                 delta_wide[zq, part] = jnp.broadcast_to(delta, (rows, 2 * HD))
                 lse_wide[zq, part] = jnp.broadcast_to(lse_ref[here, cols][:, :1], (rows, 2 * HD))
@@ -200,7 +198,7 @@
             grad_q_ref[pl.ds(zq * rows, rows), :] = jnp.concatenate(parts, axis=1) * HD ** (-0.5)
 
 
-def flash_backward(q, kv_all, bias, grad, exact, lse, seqs, rows, g, groups):
+def flash_backward(q, kv_all, bias, grad, low, lse, seqs, rows, g, groups):
     shards = kv_all.shape[0]
     q_cols = q.shape[1]
     stack = groups * rows
@@ -230,7 +228,7 @@
             bytes_accessed=0,
             transcendentals=0,
         ),
-    )(kv_all, q, bias, grad, exact, lse)
+    )(kv_all, q, bias, grad, low, lse)
 
 
 def shift(block, count, step):
@@ -790,7 +788,7 @@
     earlier = ((order ^ shard) < shard) | (order == 0)
     bias_same = jnp.where(earlier[None, :, None], bias, FLOOR_SCORE)
     bias = jnp.concatenate([bias, bias_same]).reshape(2 * seqs, 1, shards * rows)
-    attended_low, exact, lse = flash_forward(
+    attended_low, lse = flash_forward(
         head_queries, kv_blocks, bias, seqs, rows, local_kv, groups
     )
     attended = lax.all_to_all(attended_low, "seq", split_axis=0, concat_axis=1, tiled=True)
@@ -881,7 +879,7 @@
     held = after(head_grad, grad_down_shard)
     for g in range(local_kv):
         part_q, near_kv, far_kv = flash_backward(
-            head_queries, kv_all, bias, held, exact, lse, seqs, rows, g, groups
+            head_queries, kv_all, bias, held, attended_low, lse, seqs, rows, g, groups
         )
         if g == 0:
             grad_gate_up_blocks = after(grad_gate_up_blocks, part_q)

time: 496 us -> 494 us (level)
  starting transfers between devices: 108 us -> 98.2 us
  waiting for transfers between devices: 171 us -> 180 us
    all_to_all x1, waiting for transfers between devices: 0.01 us -> 8.94 us  [local(): lax.all_to_all(sent_grads, 'seq', split_axis=0, concat_axis=1, tiled=True)]
    ppermute x28, waiting for transfers between devices: 39.8 us -> 34.5 us  [hop(): return lax.ppermute(block, 'fsdp', [(i, i ^ mask) for i in range(count)])]
    unnamed x212 -> x198, local copies, waits for them, and re-layouts: 25.2 us -> 22.8 us
  transfers between devices with their start and end apart: 64 -> 64, of which waited for: 30 -> 32; matrix products, arithmetic and copies ran while one was open for 12% -> 12% of each run, Pallas kernels for 17% -> 17%
where the time goes in v19:
time: 494 us; the launch traced here: 485 us
  waiting for transfers between devices  180 us (36%)
  Pallas kernels  102 us (21%)
  starting transfers between devices  98.2 us (20%)
  local copies, waits for them, and re-layouts  34 us (7%)
  other arithmetic  28.4 us (6%)
  matrix products  22.1 us (4%)
  between operations  21 us (4%)
    ppermute x21, waiting for transfers between devices, shift(): lax.ppermute(block, 'seq', [(i, (i + step) % count) for i in range(count)])  112 us
    ppermute x21, starting transfers between devices, shift(): lax.ppermute(block, 'seq', [(i, (i + step) % count) for i in range(count)])  35 us
    ppermute x28, waiting for transfers between devices, hop(): return lax.ppermute(block, 'fsdp', [(i, i ^ mask) for i in range(count)])  34.5 us
    pallas_call x2, Pallas kernels, flash_backward(): pl.pallas_call(functools.partial(backward_kernel, shards, seqs, rows, g,...  27.9 us
    unnamed x198, local copies, waits for them, and re-layouts  22.8 us
    ppermute x28, starting transfers between devices, hop(): return lax.ppermute(block, 'fsdp', [(i, i ^ mask) for i in range(count)])  22.5 us
    pallas_call x1, Pallas kernels, flash_forward(): pl.pallas_call(functools.partial(forward_kernel, shards, seqs, rows, loca...  19 us
    pallas_call x4, Pallas kernels, split_product(): pl.pallas_call(product_kernel, grid=(count // 2,), in_specs=[pl.BlockSpec...  14 us
  transfers between devices with their start and end apart: 64, of which 32 were waited for; matrix products, arithmetic and copies ran while one was open for 12% of the time, Pallas kernels for 17%

profile of v19, /device:TPU:12, one launch (start us, length us, event | category | flops | bytes accessed | tf_op | source)
XLA Modules:
  0.0 485.1 jit_solution(1614720457395350255)
XLA Ops:
  21.9 23.3 %collective-permute-done = bf16[136,1536]{1,0:T(8,128)(2,1)S(1)} collective-permute-done((bf16[136,1536]{1,0:T(8,128)(2,1)S(1)}, bf16[136,1536]{1,0:T(8,128)(2,1)S(1)}, u32[]{:S(2)}, u32[]{:S(2)}) %collective-permute-start) | collective-permute-done | bytes 417824 | tf_op jit(solution)/shard_map/ppermute | solution.py:235
  45.2 7.8 %collective-permute-done.1 = bf16[136,1536]{1,0:T(8,128)(2,1)S(1)} collective-permute-done((bf16[136,1536]{1,0:T(8,128)(2,1)S(1)}, bf16[136,1536]{1,0:T(8,128)(2,1)S(1)}, u32[]{:S(2)}, u32[]{:S(2)}) %collective-permute-start.1) | collective-permute-done | bytes 417824 | tf_op jit(solution)/shard_map/ppermute | solution.py:235
  63.3 8.3 %collective-permute-done.3.refs_1_ = bf16[528,256]{1,0:T(8,128)(2,1)S(1)} collective-permute-done((bf16[528,256]{1,0:T(8,128)(2,1)S(1)}, bf16[528,256]{1,0:T(8,128)(2,1)S(1)}, u32[]{:S(2)}, u32[]{:S(2)}) %collective-permute-start.3) | collective-permute-done | bytes 270368 | tf_op jit(solution)/shard_map/ppermute | solution.py:261
  71.6 7.7 %collective-permute-done.4.refs_2_ = bf16[528,256]{1,0:T(8,128)(2,1)S(1)} collective-permute-done((bf16[528,256]{1,0:T(8,128)(2,1)S(1)}, bf16[528,256]{1,0:T(8,128)(2,1)S(1)}, u32[]{:S(2)}, u32[]{:S(2)}) %collective-permute-start.4) | collective-permute-done | bytes 270368 | tf_op jit(solution)/shard_map/ppermute | solution.py:261
  79.4 3.0 collective-permute-done.5.refs_3_
  85.0 19.0 %shard_map.221 = (bf16[512,384]{1,0:T(8,128)(2,1)}, f32[512,384]{1,0:T(8,128)S(1)}) custom-call(bf16[528,256]{1,0:T(8,128)(2,1)S(1)} %maximum_maximum_fusion.1.refs_0_, bf16[528,256]{1,0:T(8,128)(2,1)S(1)} %collective-permute-done.3.refs_1_, bf16[528,256]{1,0:T(8,128)(2,1)S(1)} %collective-permute-done.4.refs_2_, ...), custom_call_target="tpu_custom_call" | custom-call | tf_op jit(solution)/shard_map/pallas_call | solution.py:112
  104.9 3.4 all-to-all-start
  109.3 8.8 %all-to-all-done = bf16[4,128,384]{2,1,0:T(8,128)(2,1)S(1)} async-done(((bf16[4,128,384]{2,1,0:T(8,128)(2,1)}), bf16[4,128,384]{2,1,0:T(8,128)(2,1)S(1)}, u32[]{:S(2)}, u32[]{:S(2)}) %all-to-all-start) | async-done | bytes 393248 | tf_op jit(solution)/shard_map/all_to_all | solution.py:794
  119.8 5.7 %multiply_reduce_fusion.5 = (f32[128]{0:T(128)S(1)}, f32[128,1536]{1,0:T(8,128)S(1)}) fusion(bf16[128,1536]{1,0:T(8,128)(2,1)S(1)} %bitcast.138, bf16[1536,1536]{0,1:T(8,128)(2,1)} %all-gather.9.cloned.1.call-done, bf16[128,1536]{1,0:T(8,128)(2,1)} %param.14), kind=kOutput, calls=%fused_computation.69 | convolution fusion | flops 604766080 | bytes 6291968 | tf_op jit(solution)/shard_map/dot_general | solution.py:24
  127.8 3.5 collective-permute-start.11
  134.1 3.8 collective-permute-done.10.refs_1_
  137.8 15.3 %collective-permute-done.11.refs_2_ = bf16[96,1536]{1,0:T(8,128)(2,1)} collective-permute-done((bf16[96,1536]{1,0:T(8,128)(2,1)S(1)}, bf16[96,1536]{1,0:T(8,128)(2,1)}, u32[]{:S(2)}, u32[]{:S(2)}) %collective-permute-start.11) | collective-permute-done | bytes 294944 | tf_op jit(solution)/shard_map/ppermute | solution.py:235
  153.1 3.9 collective-permute-done.12.refs_3_
  157.0 8.8 %shard_map.222 = (bf16[384,1536]{1,0:T(8,128)(2,1)}, f32[384,2048]{1,0:T(8,128)}, bf16[384,1024]{1,0:T(8,128)(2,1)}, bf16[96,1536]{1,0:T(8,128)(2,1)}, bf16[96,1...) custom-call(bf16[96,1536]{1,0:T(8,128)(2,1)} %get-tuple-element.353.refs_0_, ...), custom_call_target="tpu_custom_call" | custom-call | tf_op jit(solution)/shard_map/pallas_call | solution.py:394
  169.7 19.0 %collective-permute-done.13 = bf16[96,1536]{1,0:T(8,128)(2,1)S(1)} collective-permute-done((bf16[96,1536]{1,0:T(8,128)(2,1)}, bf16[96,1536]{1,0:T(8,128)(2,1)S(1)}, u32[]{:S(2)}, u32[]{:S(2)}) %collective-permute-start.13) | collective-permute-done | bytes 294944 | tf_op jit(solution)/shard_map/ppermute | solution.py:235
  198.5 4.2 collective-permute-start.17
  204.9 3.3 collective-permute-done.16.refs_1_
  208.3 15.8 %collective-permute-done.17.refs_2_ = bf16[96,1536]{1,0:T(8,128)(2,1)S(1)} collective-permute-done((bf16[96,1536]{1,0:T(8,128)(2,1)S(1)}, bf16[96,1536]{1,0:T(8,128)(2,1)S(1)}, u32[]{:S(2)}, u32[]{:S(2)}) %collective-permute-start.17) | collective-permute-done | bytes 294944 | tf_op jit(solution)/shard_map/ppermute | solution.py:235
  227.5 9.9 %shard_map.223 = (bf16[384,1536]{1,0:T(8,128)(2,1)}, bf16[384,2048]{1,0:T(8,128)(2,1)}, bf16[96,1536]{1,0:T(8,128)(2,1)}, bf16[96,1536]{1,0:T(8,128)(2,1)}, bf16...) custom-call(bf16[96,1536]{1,0:T(8,128)(2,1)} %get-tuple-element.176.refs_0_, bf16[96,1536]{1,0:T(8,128)(2,1)} %copy-done.63, ...), custom_call_target="tpu_custom_call" | custom-call | tf_op jit(solution)/shard_map/pallas_call | solution.py:443
  238.4 2.9 collective-permute-start.21
  245.9 4.8 shard_map.226
  255.8 4.4 collective-permute-done.19
  271.3 8.4 %all-to-all-start.1 = ((bf16[128,4,384]{2,0,1:T(8,128)(2,1)}), bf16[128,4,384]{2,0,1:T(8,128)(2,1)}, u32[]{:S(2)}, u32[]{:S(2)}) async-start(bf16[128,4,384]{2,0,1:T(8,128)(2,1)} %bitcast.148), calls=%async_computation.1 | async-start | bytes 786432 | tf_op jit(solution)/shard_map/all_to_all | solution.py:870
  293.9 14.0 %shard_map.228 = (f32[512,192]{1,0:T(8,128)S(1)}, bf16[4,512,128]{2,1,0:T(8,128)(2,1)S(1)}, bf16[4,512,128]{2,1,0:T(8,128)(2,1)S(1)}) custom-call(bf16[8,528,256]{2,1,0:T(8,128)(2,1)S(1)} %copy-done.8, bf16[512,384]{1,0:T(8,128)(2,1)S(1)} %slice_multiply_fusion.refs_8_.refs_1_, f32[8,1,1024]{2,1,0:T(1,128)S(1)} %pad_maximum_fusion.3.refs_9_.refs_2_, ...), custom_call_target="tpu_custom_call" | custom-call | flops 999999995904 | tf_op jit(solution)/shard_map/pallas_call | solution.py:210
  308.0 6.3 %collective-permute-done.29 = bf16[192,2048]{1,0:T(8,128)(2,1)} collective-permute-done((bf16[192,2048]{1,0:T(8,128)(2,1)}, bf16[192,2048]{1,0:T(8,128)(2,1)}, u32[]{:S(2)}, u32[]{:S(2)}) %collective-permute-start.29) | collective-permute-done | bytes 786464 | tf_op jit(solution)/shard_map/ppermute | solution.py:261
  316.4 3.4 collective-permute-start.31
  319.8 3.6 collective-permute-start.32
  323.4 13.9 %shard_map.230 = (f32[512,192]{1,0:T(8,128)S(1)}, bf16[4,512,128]{2,1,0:T(8,128)(2,1)S(1)}, bf16[4,512,128]{2,1,0:T(8,128)(2,1)S(1)}) custom-call(bf16[8,528,256]{2,1,0:T(8,128)(2,1)S(1)} %copy-done.8, bf16[512,384]{1,0:T(8,128)(2,1)S(1)} %slice_multiply_fusion.refs_8_.refs_1_, f32[8,1,1024]{2,1,0:T(1,128)S(1)} %pad_maximum_fusion.3.refs_9_.refs_2_, ...), custom_call_target="tpu_custom_call" | custom-call | tf_op jit(solution)/shard_map/pallas_call | solution.py:210
  339.7 3.1 collective-permute-done.31.refs_1_
  344.5 3.2 collective-permute-start.38
  347.7 3.5 collective-permute-start.39
  359.4 4.1 shard_map.232
  363.7 5.2 %collective-permute-done.36.refs_4_ = bf16[512,256]{1,0:T(8,128)(2,1)} collective-permute-done((bf16[512,256]{1,0:T(8,128)(2,1)}, bf16[512,256]{1,0:T(8,128)(2,1)}, u32[]{:S(2)}, u32[]{:S(2)}) %collective-permute-start.36) | collective-permute-done | bytes 262176 | tf_op jit(solution)/shard_map/ppermute | solution.py:261
  371.5 3.7 shard_map.234
  377.7 3.4 collective-permute-start.45
  389.3 4.3 all-to-all-start.3
  393.6 4.1 collective-permute-done.44.refs_3_
  397.7 5.4 %collective-permute-done.45.refs_6_ = bf16[192,2048]{1,0:T(8,128)(2,1)S(1)} collective-permute-done((bf16[192,2048]{1,0:T(8,128)(2,1)}, bf16[192,2048]{1,0:T(8,128)(2,1)S(1)}, u32[]{:S(2)}, u32[]{:S(2)}) %collective-permute-start.45) | collective-permute-done | bytes 786464 | tf_op jit(solution)/shard_map/ppermute | solution.py:250
  410.7 3.9 collective-permute-start.47
  414.6 8.9 %all-to-all-done.3 = bf16[4,128,640]{1,2,0:T(8,128)(2,1)} async-done(((bf16[4,128,640]{1,2,0:T(8,128)(2,1)}), bf16[4,128,640]{1,2,0:T(8,128)(2,1)}, u32[]{:S(2)}, u32[]{:S(2)}) %all-to-all-start.3) | async-done | bytes 655392 | tf_op jit(solution)/shard_map/all_to_all | solution.py:905
  424.2 4.3 collective-permute-start.48
  428.5 3.1 collective-permute-done.50
  434.2 4.9 %all-to-all-start.2 = ((bf16[192,4,384]{2,0,1:T(8,128)(2,1)}), bf16[192,4,384]{2,0,1:T(8,128)(2,1)S(1)}, u32[]{:S(2)}, u32[]{:S(2)}) async-start(bf16[192,4,384]{2,0,1:T(8,128)(2,1)} %bitcast.147), calls=%async_computation.2 | async-start | bytes 1179648 | tf_op jit(solution)/shard_map/all_to_all | solution.py:928
  439.1 6.3 %fusion.27 = (f32[128]{0:T(128)S(1)}, f32[128]{0:T(128)S(1)}, f32[128,1536]{1,0:T(8,128)S(1)}) fusion(bf16[128,1536]{1,0:T(8,128)(2,1)S(1)} %copy-done.47, bf16[128,2560]{0,1:T(8,128)(2,1)} %bitcast.55, bf16[1536,2560]{1,0:T(8,128)(2,1)} %all-gather.13.cloned.1.call-done), kind=kOutput, calls=%fused_computation.47 | convolution fusion | flops 1007615744 | bytes 9700352 | tf_op jit(solution)/shard_map/dot_general | solution.py:28
  445.4 7.8 %shard_map.236 = (f32[4,192,2048]{2,1,0:T(8,128)}, f32[192,128]{1,0:T(8,128)S(1)}) custom-call(s32[1]{0:T(128)} %bitcast.33.place_ref, bf16[192,2048]{1,0:T(8,128)(2,1)S(1)} %copy-done.4, bf16[192,2048]{1,0:T(8,128)(2,1)} %collective-permute-done.31.refs_1_, bf16[192,2048]{1,0:T(8,128)(2,1)} %collective-permute-done.38.refs_2_, ...), custom_call_target="tpu_custom_call" | custom-call | tf_op jit(solution)/shard_map/pallas_call | solution.py:581
  458.8 3.6 convert_bitcast_fusion
  462.6 4.0 collective-permute-done.52.refs_5_
  470.3 3.3 shard_map.237
  (422 shorter events, 137.9 us)
Async XLA Ops:
  7.2 48.2 %all-gather.7.cloned.1.call-start = ((), (), s32[]{:S(2)}) async-start(), calls=%async_computation.4 | async-start | bytes 2211840 | tf_op jit(solution)/shard_map/all_gather | solution.py:718
  10.7 109.1 %all-gather.9.cloned.1.call-start = ((), (), s32[]{:S(2)}) async-start(), calls=%async_computation.5 | async-start | bytes 5308416 | tf_op jit(solution)/shard_map/all_gather | solution.py:745
  11.5 145.5 %all-gather.11.cloned.1.call-start = ((), (), s32[]{:S(2)}) async-start(), calls=%async_computation.6 | async-start | bytes 11059200 | tf_op jit(solution)/shard_map/all_gather | solution.py:760
  15.6 189.4 %all-gather.13.cloned.1.call-start = ((), (), s32[]{:S(2)}) async-start(), calls=%async_computation.7 | async-start | bytes 8847360 | tf_op jit(solution)/shard_map/all_gather | solution.py:773
  15.6 29.6 %collective-permute-start = (bf16[136,1536]{1,0:T(8,128)(2,1)S(1)}, bf16[136,1536]{1,0:T(8,128)(2,1)S(1)}, u32[]{:S(2)}, u32[]{:S(2)}) collective-permute-start(bf16[136,1536]{1,0:T(8,128)(2,1)S(1)} %fusion.36), channel_id=1, source_target_pairs={{0,8},{8,16},{16,24},{24,0},{1,9},{9,17},{17,25},{25,1},{2,10},{10... | collective-permute-start | bytes 1253384 | tf_op jit(solution)/shard_map/ppermute | solution.py:235
  17.2 35.8 %collective-permute-start.1 = (bf16[136,1536]{1,0:T(8,128)(2,1)S(1)}, bf16[136,1536]{1,0:T(8,128)(2,1)S(1)}, u32[]{:S(2)}, u32[]{:S(2)}) collective-permute-start(bf16[136,1536]{1,0:T(8,128)(2,1)S(1)} %fusion.36), channel_id=1, source_target_pairs={{0,16},{8,24},{16,0},{24,8},{1,17},{9,25},{17,1},{25,9},{2,18},{10... | collective-permute-start | bytes 1253384 | tf_op jit(solution)/shard_map/ppermute | solution.py:235
  18.5 36.3 %collective-permute-start.2 = (bf16[136,1536]{1,0:T(8,128)(2,1)S(1)}, bf16[136,1536]{1,0:T(8,128)(2,1)S(1)}, u32[]{:S(2)}, u32[]{:S(2)}) collective-permute-start(bf16[136,1536]{1,0:T(8,128)(2,1)S(1)} %fusion.36), channel_id=1, source_target_pairs={{0,24},{8,0},{16,8},{24,16},{1,25},{9,1},{17,9},{25,17},{2,26},{10... | collective-permute-start | bytes 1253384 | tf_op jit(solution)/shard_map/ppermute | solution.py:235
  61.2 18.2 %collective-permute-start.4 = (bf16[528,256]{1,0:T(8,128)(2,1)S(1)}, bf16[528,256]{1,0:T(8,128)(2,1)S(1)}, u32[]{:S(2)}, u32[]{:S(2)}) collective-permute-start(bf16[528,256]{1,0:T(8,128)(2,1)S(1)} %maximum_maximum_fusion.1.refs_0_), channel_id=1, source_target_pairs={{0,4},{1,5},{2,6},{3,7},{4,0},{5,1},{6,2},{7,3},{8,12},{9,13},{10,... | collective-permute-start | bytes 811016 | tf_op jit(solution)/shard_map/ppermute | solution.py:261
  61.7 20.7 %collective-permute-start.5 = (bf16[528,256]{1,0:T(8,128)(2,1)S(1)}, bf16[528,256]{1,0:T(8,128)(2,1)S(1)}, u32[]{:S(2)}, u32[]{:S(2)}) collective-permute-start(bf16[528,256]{1,0:T(8,128)(2,1)S(1)} %maximum_maximum_fusion.1.refs_0_), channel_id=1, source_target_pairs={{0,6},{1,7},{2,4},{3,5},{4,2},{5,3},{6,0},{7,1},{8,14},{9,15},{10,... | collective-permute-start | bytes 811016 | tf_op jit(solution)/shard_map/ppermute | solution.py:261
  63.3 20.9 %collective-permute-start.6 = (bf16[528,256]{1,0:T(8,128)(2,1)S(1)}, bf16[528,256]{1,0:T(8,128)(2,1)S(1)}, u32[]{:S(2)}, u32[]{:S(2)}) collective-permute-start(bf16[528,256]{1,0:T(8,128)(2,1)S(1)} %maximum_maximum_fusion.1.refs_0_), channel_id=1, source_target_pairs={{0,1},{1,0},{2,3},{3,2},{4,5},{5,4},{6,7},{7,6},{8,9},{9,8},{10,11... | collective-permute-start | bytes 811016 | tf_op jit(solution)/shard_map/ppermute | solution.py:261
  127.8 25.3 %collective-permute-start.11 = (bf16[96,1536]{1,0:T(8,128)(2,1)S(1)}, bf16[96,1536]{1,0:T(8,128)(2,1)}, u32[]{:S(2)}, u32[]{:S(2)}) collective-permute-start(bf16[96,1536]{1,0:T(8,128)(2,1)S(1)} %get-tuple-element.351), channel_id=1, source_target_pairs={{0,16},{8,24},{16,0},{24,8},{1,17},{9,25},{17,1},{25,9},{2,18},{10... | collective-permute-start | bytes 884744 | tf_op jit(solution)/shard_map/ppermute | solution.py:235
  131.3 25.7 %collective-permute-start.12 = (bf16[96,1536]{1,0:T(8,128)(2,1)S(1)}, bf16[96,1536]{1,0:T(8,128)(2,1)}, u32[]{:S(2)}, u32[]{:S(2)}) collective-permute-start(bf16[96,1536]{1,0:T(8,128)(2,1)S(1)} %get-tuple-element.350), channel_id=1, source_target_pairs={{0,24},{8,0},{16,8},{24,16},{1,25},{9,1},{17,9},{25,17},{2,26},{10... | collective-permute-start | bytes 884744 | tf_op jit(solution)/shard_map/ppermute | solution.py:235
  165.8 22.8 %collective-permute-start.13 = (bf16[96,1536]{1,0:T(8,128)(2,1)}, bf16[96,1536]{1,0:T(8,128)(2,1)S(1)}, u32[]{:S(2)}, u32[]{:S(2)}) collective-permute-start(bf16[96,1536]{1,0:T(8,128)(2,1)} %get-tuple-element.159), channel_id=1, source_target_pairs={{0,24},{8,0},{16,8},{24,16},{1,25},{9,1},{17,9},{25,17},{2,26},{10... | collective-permute-start | bytes 884744 | tf_op jit(solution)/shard_map/ppermute | solution.py:235
  165.9 22.7 %collective-permute-start.14 = (bf16[96,1536]{1,0:T(8,128)(2,1)}, bf16[96,1536]{1,0:T(8,128)(2,1)S(1)}, u32[]{:S(2)}, u32[]{:S(2)}) collective-permute-start(bf16[96,1536]{1,0:T(8,128)(2,1)} %get-tuple-element.160), channel_id=1, source_target_pairs={{0,16},{8,24},{16,0},{24,8},{1,17},{9,25},{17,1},{25,9},{2,18},{10... | collective-permute-start | bytes 884744 | tf_op jit(solution)/shard_map/ppermute | solution.py:235
  166.7 24.5 %collective-permute-start.15 = (bf16[96,1536]{1,0:T(8,128)(2,1)}, bf16[96,1536]{1,0:T(8,128)(2,1)S(1)}, u32[]{:S(2)}, u32[]{:S(2)}) collective-permute-start(bf16[96,1536]{1,0:T(8,128)(2,1)} %get-tuple-element.161), channel_id=1, source_target_pairs={{0,8},{8,16},{16,24},{24,0},{1,9},{9,17},{17,25},{25,1},{2,10},{10... | collective-permute-start | bytes 884744 | tf_op jit(solution)/shard_map/ppermute | solution.py:235
  198.5 25.5 %collective-permute-start.17 = (bf16[96,1536]{1,0:T(8,128)(2,1)S(1)}, bf16[96,1536]{1,0:T(8,128)(2,1)S(1)}, u32[]{:S(2)}, u32[]{:S(2)}) collective-permute-start(bf16[96,1536]{1,0:T(8,128)(2,1)S(1)} %get-tuple-element.347), channel_id=1, source_target_pairs={{0,16},{8,24},{16,0},{24,8},{1,17},{9,25},{17,1},{25,9},{2,18},{10... | collective-permute-start | bytes 884744 | tf_op jit(solution)/shard_map/ppermute | solution.py:235
  202.7 24.0 %collective-permute-start.18 = (bf16[96,1536]{1,0:T(8,128)(2,1)S(1)}, bf16[96,1536]{1,0:T(8,128)(2,1)S(1)}, u32[]{:S(2)}, u32[]{:S(2)}) collective-permute-start(bf16[96,1536]{1,0:T(8,128)(2,1)S(1)} %get-tuple-element.346), channel_id=1, source_target_pairs={{0,24},{8,0},{16,8},{24,16},{1,25},{9,1},{17,9},{25,17},{2,26},{10... | collective-permute-start | bytes 884744 | tf_op jit(solution)/shard_map/ppermute | solution.py:235
  237.4 22.9 %collective-permute-start.19 = (bf16[96,1536]{1,0:T(8,128)(2,1)}, bf16[96,1536]{1,0:T(8,128)(2,1)S(1)}, u32[]{:S(2)}, u32[]{:S(2)}) collective-permute-start(bf16[96,1536]{1,0:T(8,128)(2,1)} %get-tuple-element.182), channel_id=1, source_target_pairs={{0,24},{8,0},{16,8},{24,16},{1,25},{9,1},{17,9},{25,17},{2,26},{10... | collective-permute-start | bytes 884744 | tf_op jit(solution)/shard_map/ppermute | solution.py:235
  237.4 22.8 %collective-permute-start.20 = (bf16[96,1536]{1,0:T(8,128)(2,1)}, bf16[96,1536]{1,0:T(8,128)(2,1)S(1)}, u32[]{:S(2)}, u32[]{:S(2)}) collective-permute-start(bf16[96,1536]{1,0:T(8,128)(2,1)} %get-tuple-element.183), channel_id=1, source_target_pairs={{0,16},{8,24},{16,0},{24,8},{1,17},{9,25},{17,1},{25,9},{2,18},{10... | collective-permute-start | bytes 884744 | tf_op jit(solution)/shard_map/ppermute | solution.py:235
  238.4 24.9 %collective-permute-start.21 = (bf16[96,1536]{1,0:T(8,128)(2,1)}, bf16[96,1536]{1,0:T(8,128)(2,1)S(1)}, u32[]{:S(2)}, u32[]{:S(2)}) collective-permute-start(bf16[96,1536]{1,0:T(8,128)(2,1)} %get-tuple-element.184), channel_id=1, source_target_pairs={{0,8},{8,16},{16,24},{24,0},{1,9},{9,17},{17,25},{25,1},{2,10},{10... | collective-permute-start | bytes 884744 | tf_op jit(solution)/shard_map/ppermute | solution.py:235
  250.7 16.4 %collective-permute-start.23 = (bf16[4,192,2048]{2,1,0:T(8,128)(2,1)S(1)}, bf16[4,192,2048]{2,1,0:T(8,128)(2,1)S(1)}, u32[]{:S(2)}, u32[]{:S(2)}) collective-permute-start(bf16[4,192,2048]{2,1,0:T(8,128)(2,1)S(1)} %get-tuple-element.208), channel_id=1, source_target_pairs={{0,1},{1,0},{2,3},{3,2},{4,5},{5,4},{6,7},{7,6},{8,9},{9,8},{10,11... | collective-permute-start | bytes 9437192 | tf_op jit(solution)/shard_map/ppermute | solution.py:261
  254.8 26.8 %collective-permute-start.24 = (bf16[192,1024]{1,0:T(8,128)(2,1)}, bf16[192,1024]{1,0:T(8,128)(2,1)}, u32[]{:S(2)}, u32[]{:S(2)}) collective-permute-start(bf16[192,1024]{1,0:T(8,128)(2,1)} %get-tuple-element.196), channel_id=1, source_target_pairs={{0,2},{1,3},{2,0},{3,1},{4,6},{5,7},{6,4},{7,5},{8,10},{9,11},{10,... | collective-permute-start | bytes 1179656 | tf_op jit(solution)/shard_map/ppermute | solution.py:261
  260.2 23.0 %collective-permute-start.25 = (bf16[192,1024]{1,0:T(8,128)(2,1)}, bf16[192,1024]{1,0:T(8,128)(2,1)}, u32[]{:S(2)}, u32[]{:S(2)}) collective-permute-start(bf16[192,1024]{1,0:T(8,128)(2,1)} %get-tuple-element.197), channel_id=1, source_target_pairs={{0,4},{1,5},{2,6},{3,7},{4,0},{5,1},{6,2},{7,3},{8,12},{9,13},{10,... | collective-permute-start | bytes 1179656 | tf_op jit(solution)/shard_map/ppermute | solution.py:261
  260.2 23.0 %collective-permute-start.26 = (bf16[192,1024]{1,0:T(8,128)(2,1)}, bf16[192,1024]{1,0:T(8,128)(2,1)}, u32[]{:S(2)}, u32[]{:S(2)}) collective-permute-start(bf16[192,1024]{1,0:T(8,128)(2,1)} %get-tuple-element.198), channel_id=1, source_target_pairs={{0,6},{1,7},{2,4},{3,5},{4,2},{5,3},{6,0},{7,1},{8,14},{9,15},{10,... | collective-permute-start | bytes 1179656 | tf_op jit(solution)/shard_map/ppermute | solution.py:261
  271.3 19.8 %all-to-all-start.1 = ((bf16[128,4,384]{2,0,1:T(8,128)(2,1)}), bf16[128,4,384]{2,0,1:T(8,128)(2,1)}, u32[]{:S(2)}, u32[]{:S(2)}) async-start(bf16[128,4,384]{2,0,1:T(8,128)(2,1)} %bitcast.148), calls=%async_computation.1 | async-start | bytes 786432 | tf_op jit(solution)/shard_map/all_to_all | solution.py:870
  279.7 64.2 %all-gather.15.cloned.1.call-start = ((), (), s32[]{:S(2)}) async-start(), calls=%async_computation.8 | async-start | bytes 1966080 | tf_op jit(solution)/shard_map/all_gather | solution.py:873
  279.7 28.2 %collective-permute-start.27 = (bf16[192,2048]{1,0:T(8,128)(2,1)}, bf16[192,2048]{1,0:T(8,128)(2,1)}, u32[]{:S(2)}, u32[]{:S(2)}) collective-permute-start(bf16[192,2048]{1,0:T(8,128)(2,1)} %copy-done.35), channel_id=1, source_target_pairs={{0,2},{1,3},{2,0},{3,1},{4,6},{5,7},{6,4},{7,5},{8,10},{9,11},{10,... | collective-permute-start | bytes 2359304 | tf_op jit(solution)/shard_map/ppermute | solution.py:261
  279.7 28.2 %collective-permute-start.28 = (bf16[192,2048]{1,0:T(8,128)(2,1)}, bf16[192,2048]{1,0:T(8,128)(2,1)}, u32[]{:S(2)}, u32[]{:S(2)}) collective-permute-start(bf16[192,2048]{1,0:T(8,128)(2,1)} %copy-done.34), channel_id=1, source_target_pairs={{0,4},{1,5},{2,6},{3,7},{4,0},{5,1},{6,2},{7,3},{8,12},{9,13},{10,... | collective-permute-start | bytes 2359304 | tf_op jit(solution)/shard_map/ppermute | solution.py:261
  281.6 32.7 %collective-permute-start.29 = (bf16[192,2048]{1,0:T(8,128)(2,1)}, bf16[192,2048]{1,0:T(8,128)(2,1)}, u32[]{:S(2)}, u32[]{:S(2)}) collective-permute-start(bf16[192,2048]{1,0:T(8,128)(2,1)} %copy-done.33), channel_id=1, source_target_pairs={{0,6},{1,7},{2,4},{3,5},{4,2},{5,3},{6,0},{7,1},{8,14},{9,15},{10,... | collective-permute-start | bytes 2359304 | tf_op jit(solution)/shard_map/ppermute | solution.py:261
  291.1 32.3 %collective-permute-start.30 = (bf16[4,192,1536]{2,1,0:T(8,128)(2,1)}, bf16[4,192,1536]{2,1,0:T(8,128)(2,1)}, u32[]{:S(2)}, u32[]{:S(2)}) collective-permute-start(bf16[4,192,1536]{2,1,0:T(8,128)(2,1)} %copy-done.32), channel_id=1, source_target_pairs={{0,1},{1,0},{2,3},{3,2},{4,5},{5,4},{6,7},{7,6},{8,9},{9,8},{10,11... | collective-permute-start | bytes 7077896 | tf_op jit(solution)/shard_map/ppermute | solution.py:261
  316.4 26.4 %collective-permute-start.31 = (bf16[192,2048]{1,0:T(8,128)(2,1)S(1)}, bf16[192,2048]{1,0:T(8,128)(2,1)}, u32[]{:S(2)}, u32[]{:S(2)}) collective-permute-start(bf16[192,2048]{1,0:T(8,128)(2,1)S(1)} %add_convert_fusion.refs_0_), channel_id=1, source_target_pairs={{0,8},{8,16},{16,24},{1,9},{9,17},{17,25},{2,10},{10,18},{18,26},{... | collective-permute-start | bytes 2359304 | tf_op jit(solution)/shard_map/ppermute | solution.py:249
  319.8 24.2 %collective-permute-start.32 = (bf16[192,2048]{1,0:T(8,128)(2,1)S(1)}, bf16[192,2048]{1,0:T(8,128)(2,1)}, u32[]{:S(2)}, u32[]{:S(2)}) collective-permute-start(bf16[192,2048]{1,0:T(8,128)(2,1)S(1)} %add_convert_fusion.refs_0_), channel_id=1, source_target_pairs={{8,0},{16,8},{24,16},{9,1},{17,9},{25,17},{10,2},{18,10},{26,18},{... | collective-permute-start | bytes 2359304 | tf_op jit(solution)/shard_map/ppermute | solution.py:250
  344.5 24.4 %collective-permute-start.38 = (bf16[192,2048]{1,0:T(8,128)(2,1)}, bf16[192,2048]{1,0:T(8,128)(2,1)}, u32[]{:S(2)}, u32[]{:S(2)}) collective-permute-start(bf16[192,2048]{1,0:T(8,128)(2,1)} %collective-permute-done.31.refs_1_), channel_id=1, source_target_pairs={{0,8},{8,16},{16,24},{1,9},{9,17},{17,25},{2,10},{10,18},{18,26},{... | collective-permute-start | bytes 2359304 | tf_op jit(solution)/shard_map/ppermute | solution.py:249
  347.7 21.4 %collective-permute-start.39 = (bf16[192,2048]{1,0:T(8,128)(2,1)}, bf16[192,2048]{1,0:T(8,128)(2,1)}, u32[]{:S(2)}, u32[]{:S(2)}) collective-permute-start(bf16[192,2048]{1,0:T(8,128)(2,1)} %collective-permute-done.32.refs_4_), channel_id=1, source_target_pairs={{8,0},{16,8},{24,16},{9,1},{17,9},{25,17},{10,2},{18,10},{26,18},{... | collective-permute-start | bytes 2359304 | tf_op jit(solution)/shard_map/ppermute | solution.py:250
  355.6 13.3 %collective-permute-start.36 = (bf16[512,256]{1,0:T(8,128)(2,1)}, bf16[512,256]{1,0:T(8,128)(2,1)}, u32[]{:S(2)}, u32[]{:S(2)}) collective-permute-start(bf16[512,256]{1,0:T(8,128)(2,1)} %get-tuple-element.240), channel_id=1, source_target_pairs={{0,4},{1,5},{2,6},{3,7},{4,0},{5,1},{6,2},{7,3},{8,12},{9,13},{10,... | collective-permute-start | bytes 786440 | tf_op jit(solution)/shard_map/ppermute | solution.py:261
  375.3 22.4 %collective-permute-start.44 = (bf16[192,2048]{1,0:T(8,128)(2,1)}, bf16[192,2048]{1,0:T(8,128)(2,1)S(1)}, u32[]{:S(2)}, u32[]{:S(2)}) collective-permute-start(bf16[192,2048]{1,0:T(8,128)(2,1)} %collective-permute-done.38.refs_2_), channel_id=1, source_target_pairs={{0,8},{8,16},{16,24},{1,9},{9,17},{17,25},{2,10},{10,18},{18,26},{... | collective-permute-start | bytes 2359304 | tf_op jit(solution)/shard_map/ppermute | solution.py:249
  377.7 25.4 %collective-permute-start.45 = (bf16[192,2048]{1,0:T(8,128)(2,1)}, bf16[192,2048]{1,0:T(8,128)(2,1)S(1)}, u32[]{:S(2)}, u32[]{:S(2)}) collective-permute-start(bf16[192,2048]{1,0:T(8,128)(2,1)} %collective-permute-done.39.refs_5_), channel_id=1, source_target_pairs={{8,0},{16,8},{24,16},{9,1},{17,9},{25,17},{10,2},{18,10},{26,18},{... | collective-permute-start | bytes 2359304 | tf_op jit(solution)/shard_map/ppermute | solution.py:250
  383.6 19.5 %collective-permute-start.41 = (bf16[192,768]{1,0:T(8,128)(2,1)}, bf16[192,768]{1,0:T(8,128)(2,1)}, u32[]{:S(2)}, u32[]{:S(2)}) collective-permute-start(bf16[192,768]{1,0:T(8,128)(2,1)} %get-tuple-element.256), channel_id=1, source_target_pairs={{0,2},{1,3},{2,0},{3,1},{4,6},{5,7},{6,4},{7,5},{8,10},{9,11},{10,... | collective-permute-start | bytes 884744 | tf_op jit(solution)/shard_map/ppermute | solution.py:261
  385.0 18.1 %collective-permute-start.42 = (bf16[192,768]{1,0:T(8,128)(2,1)S(1)}, bf16[192,768]{1,0:T(8,128)(2,1)}, u32[]{:S(2)}, u32[]{:S(2)}) collective-permute-start(bf16[192,768]{1,0:T(8,128)(2,1)S(1)} %get-tuple-element.257), channel_id=1, source_target_pairs={{0,4},{1,5},{2,6},{3,7},{4,0},{5,1},{6,2},{7,3},{8,12},{9,13},{10,... | collective-permute-start | bytes 884744 | tf_op jit(solution)/shard_map/ppermute | solution.py:261
  385.6 17.6 %collective-permute-start.43 = (bf16[192,768]{1,0:T(8,128)(2,1)S(1)}, bf16[192,768]{1,0:T(8,128)(2,1)}, u32[]{:S(2)}, u32[]{:S(2)}) collective-permute-start(bf16[192,768]{1,0:T(8,128)(2,1)S(1)} %get-tuple-element.258), channel_id=1, source_target_pairs={{0,6},{1,7},{2,4},{3,5},{4,2},{5,3},{6,0},{7,1},{8,14},{9,15},{10,... | collective-permute-start | bytes 884744 | tf_op jit(solution)/shard_map/ppermute | solution.py:261
  389.3 34.2 %all-to-all-start.3 = ((bf16[4,128,640]{1,2,0:T(8,128)(2,1)}), bf16[4,128,640]{1,2,0:T(8,128)(2,1)}, u32[]{:S(2)}, u32[]{:S(2)}) async-start(bf16[4,128,640]{1,2,0:T(8,128)(2,1)} %copy.104), calls=%async_computation.3 | async-start | bytes 1310720 | tf_op jit(solution)/shard_map/all_to_all | solution.py:905
  406.6 17.5 %collective-permute-start.51 = (bf16[192,1536]{1,0:T(8,128)(2,1)}, bf16[192,1536]{1,0:T(8,128)(2,1)}, u32[]{:S(2)}, u32[]{:S(2)}) collective-permute-start(bf16[192,1536]{1,0:T(8,128)(2,1)} %get-tuple-element.268), channel_id=1, source_target_pairs={{0,6},{1,7},{2,4},{3,5},{4,2},{5,3},{6,0},{7,1},{8,14},{9,15},{10,... | collective-permute-start | bytes 1769480 | tf_op jit(solution)/shard_map/ppermute | solution.py:261
  408.4 23.2 %collective-permute-start.50 = (bf16[192,1536]{1,0:T(8,128)(2,1)}, bf16[192,1536]{1,0:T(8,128)(2,1)}, u32[]{:S(2)}, u32[]{:S(2)}) collective-permute-start(bf16[192,1536]{1,0:T(8,128)(2,1)} %get-tuple-element.267), channel_id=1, source_target_pairs={{0,4},{1,5},{2,6},{3,7},{4,0},{5,1},{6,2},{7,3},{8,12},{9,13},{10,... | collective-permute-start | bytes 1769480 | tf_op jit(solution)/shard_map/ppermute | solution.py:261
  410.2 21.4 %collective-permute-start.49 = (bf16[192,1536]{1,0:T(8,128)(2,1)}, bf16[192,1536]{1,0:T(8,128)(2,1)}, u32[]{:S(2)}, u32[]{:S(2)}) collective-permute-start(bf16[192,1536]{1,0:T(8,128)(2,1)} %get-tuple-element.266), channel_id=1, source_target_pairs={{0,2},{1,3},{2,0},{3,1},{4,6},{5,7},{6,4},{7,5},{8,10},{9,11},{10,... | collective-permute-start | bytes 1769480 | tf_op jit(solution)/shard_map/ppermute | solution.py:261
  410.6 47.3 %collective-permute-start.46 = (bf16[192,768]{1,0:T(8,128)(2,1)S(1)}, bf16[192,768]{1,0:T(8,128)(2,1)}, u32[]{:S(2)}, u32[]{:S(2)}) collective-permute-start(bf16[192,768]{1,0:T(8,128)(2,1)S(1)} %select_convert_fusion.refs_0_), channel_id=1, source_target_pairs={{0,8},{8,16},{16,24},{24,0},{1,9},{9,17},{17,25},{25,1},{2,10},{10... | collective-permute-start | bytes 884744 | tf_op jit(solution)/shard_map/ppermute | solution.py:235
  410.7 51.9 %collective-permute-start.47 = (bf16[192,768]{1,0:T(8,128)(2,1)S(1)}, bf16[192,768]{1,0:T(8,128)(2,1)}, u32[]{:S(2)}, u32[]{:S(2)}) collective-permute-start(bf16[192,768]{1,0:T(8,128)(2,1)S(1)} %select_convert_fusion.refs_0_), channel_id=1, source_target_pairs={{0,16},{8,24},{16,0},{24,8},{1,17},{9,25},{17,1},{25,9},{2,18},{10... | collective-permute-start | bytes 884744 | tf_op jit(solution)/shard_map/ppermute | solution.py:235
  424.2 38.4 %collective-permute-start.48 = (bf16[192,768]{1,0:T(8,128)(2,1)S(1)}, bf16[192,768]{1,0:T(8,128)(2,1)}, u32[]{:S(2)}, u32[]{:S(2)}) collective-permute-start(bf16[192,768]{1,0:T(8,128)(2,1)S(1)} %select_convert_fusion.refs_0_), channel_id=1, source_target_pairs={{0,24},{8,0},{16,8},{24,16},{1,25},{9,1},{17,9},{25,17},{2,26},{10... | collective-permute-start | bytes 884744 | tf_op jit(solution)/shard_map/ppermute | solution.py:235
  434.2 20.1 %all-to-all-start.2 = ((bf16[192,4,384]{2,0,1:T(8,128)(2,1)}), bf16[192,4,384]{2,0,1:T(8,128)(2,1)S(1)}, u32[]{:S(2)}, u32[]{:S(2)}) async-start(bf16[192,4,384]{2,0,1:T(8,128)(2,1)} %bitcast.147), calls=%async_computation.2 | async-start | bytes 1179648 | tf_op jit(solution)/shard_map/all_to_all | solution.py:928
  (99 other events, 764.1 us)
Sparse Core Ops, SparseCore 0:
  10.8 28.3 all-gather.6
  41.2 48.3 all-gather.8
  92.1 58.2 all-gather.10
  152.6 52.2 all-gather.12
  291.2 42.1 all-gather.14

commit v20 on v19

--- a/solution.py
+++ b/solution.py
@@ -908,7 +908,7 @@
     head_far, head_near = split_product(product_rows, product_columns, shard, shards)
     head_sums = pair_sums(head_near, hop(head_far, shards, 1), shard)
     head_blocks = send_chips(head_sums, shards)
-    head_part = total_of(after(head_blocks, steps[3]))
+    head_part = total_of(head_blocks)
     grad_normed = dot_nt(after(token_grads, head_part), attn_full)
     grad_tokens = grad_residual + root_back(inputs, root(inputs), grad_normed)
     base_cols = head_cols + experts
@@ -923,7 +923,7 @@
     )
     head_part = by_rows(head_part.astype(BF))
     head_last = [by_rows(each) for each in send_out([head_part] * seqs, seqs)]
-    out_blocks = send_chips(after(out_sums, head_part), shards)
+    out_blocks = send_chips(after(out_sums, head_part, steps[3]), shards)
     out_part = total_of(out_blocks).astype(BF)
     out_parts = lax.all_to_all(
         out_part.reshape(part, seqs, q_cols), "seq", split_axis=1, concat_axis=1, tiled=True

time: 494 us -> 497 us (level)
  no operation moved by 1% of the time
where the time goes in v20:
time: 497 us; the launch traced here: 488 us
  waiting for transfers between devices  183 us (37%)
  Pallas kernels  102 us (21%)
  starting transfers between devices  97.6 us (20%)
  local copies, waits for them, and re-layouts  34 us (7%)
  other arithmetic  28.4 us (6%)
  matrix products  22.1 us (4%)
  between operations  21.1 us (4%)
    ppermute x21, waiting for transfers between devices, shift(): lax.ppermute(block, 'seq', [(i, (i + step) % count) for i in range(count)])  110 us
    ppermute x21, starting transfers between devices, shift(): lax.ppermute(block, 'seq', [(i, (i + step) % count) for i in range(count)])  35.1 us
    ppermute x28, waiting for transfers between devices, hop(): return lax.ppermute(block, 'fsdp', [(i, i ^ mask) for i in range(count)])  34.3 us
    pallas_call x2, Pallas kernels, flash_backward(): pl.pallas_call(functools.partial(backward_kernel, shards, seqs, rows, g,...  27.9 us
    ppermute x28, starting transfers between devices, hop(): return lax.ppermute(block, 'fsdp', [(i, i ^ mask) for i in range(count)])  23.1 us
    unnamed x198, local copies, waits for them, and re-layouts  22.8 us
    pallas_call x1, Pallas kernels, flash_forward(): pl.pallas_call(functools.partial(forward_kernel, shards, seqs, rows, loca...  19 us
    pallas_call x4, Pallas kernels, split_product(): pl.pallas_call(product_kernel, grid=(count // 2,), in_specs=[pl.BlockSpec...  14 us
  transfers between devices with their start and end apart: 64, of which 32 were waited for; matrix products, arithmetic and copies ran while one was open for 12% of the time, Pallas kernels for 17%

profile of v20, /device:TPU:12, one launch (start us, length us, event | category | flops | bytes accessed | tf_op | source)
XLA Modules:
  0.0 488.1 jit_solution(2165381565765463276)
XLA Ops:
  21.9 23.3 %collective-permute-done = bf16[136,1536]{1,0:T(8,128)(2,1)S(1)} collective-permute-done((bf16[136,1536]{1,0:T(8,128)(2,1)S(1)}, bf16[136,1536]{1,0:T(8,128)(2,1)S(1)}, u32[]{:S(2)}, u32[]{:S(2)}) %collective-permute-start) | collective-permute-done | bytes 417824 | tf_op jit(solution)/shard_map/ppermute | solution.py:235
  45.2 7.8 %collective-permute-done.1 = bf16[136,1536]{1,0:T(8,128)(2,1)S(1)} collective-permute-done((bf16[136,1536]{1,0:T(8,128)(2,1)S(1)}, bf16[136,1536]{1,0:T(8,128)(2,1)S(1)}, u32[]{:S(2)}, u32[]{:S(2)}) %collective-permute-start.1) | collective-permute-done | bytes 417824 | tf_op jit(solution)/shard_map/ppermute | solution.py:235
  63.3 8.3 %collective-permute-done.3.refs_1_ = bf16[528,256]{1,0:T(8,128)(2,1)S(1)} collective-permute-done((bf16[528,256]{1,0:T(8,128)(2,1)S(1)}, bf16[528,256]{1,0:T(8,128)(2,1)S(1)}, u32[]{:S(2)}, u32[]{:S(2)}) %collective-permute-start.3) | collective-permute-done | bytes 270368 | tf_op jit(solution)/shard_map/ppermute | solution.py:261
  71.6 7.7 %collective-permute-done.4.refs_2_ = bf16[528,256]{1,0:T(8,128)(2,1)S(1)} collective-permute-done((bf16[528,256]{1,0:T(8,128)(2,1)S(1)}, bf16[528,256]{1,0:T(8,128)(2,1)S(1)}, u32[]{:S(2)}, u32[]{:S(2)}) %collective-permute-start.4) | collective-permute-done | bytes 270368 | tf_op jit(solution)/shard_map/ppermute | solution.py:261
  79.4 3.0 collective-permute-done.5.refs_3_
  85.0 19.0 %shard_map.221 = (bf16[512,384]{1,0:T(8,128)(2,1)}, f32[512,384]{1,0:T(8,128)S(1)}) custom-call(bf16[528,256]{1,0:T(8,128)(2,1)S(1)} %maximum_maximum_fusion.1.refs_0_, bf16[528,256]{1,0:T(8,128)(2,1)S(1)} %collective-permute-done.3.refs_1_, bf16[528,256]{1,0:T(8,128)(2,1)S(1)} %collective-permute-done.4.refs_2_, ...), custom_call_target="tpu_custom_call" | custom-call | tf_op jit(solution)/shard_map/pallas_call | solution.py:112
  104.9 3.4 all-to-all-start
  109.3 8.8 %all-to-all-done = bf16[4,128,384]{2,1,0:T(8,128)(2,1)S(1)} async-done(((bf16[4,128,384]{2,1,0:T(8,128)(2,1)}), bf16[4,128,384]{2,1,0:T(8,128)(2,1)S(1)}, u32[]{:S(2)}, u32[]{:S(2)}) %all-to-all-start) | async-done | bytes 393248 | tf_op jit(solution)/shard_map/all_to_all | solution.py:794
  119.8 5.7 %multiply_reduce_fusion.5 = (f32[128]{0:T(128)S(1)}, f32[128,1536]{1,0:T(8,128)S(1)}) fusion(bf16[128,1536]{1,0:T(8,128)(2,1)S(1)} %bitcast.138, bf16[1536,1536]{0,1:T(8,128)(2,1)} %all-gather.9.cloned.1.call-done, bf16[128,1536]{1,0:T(8,128)(2,1)} %param.14), kind=kOutput, calls=%fused_computation.69 | convolution fusion | flops 604766080 | bytes 6291968 | tf_op jit(solution)/shard_map/dot_general | solution.py:24
  127.8 3.5 collective-permute-start.11
  134.1 3.8 collective-permute-done.10.refs_1_
  137.8 15.3 %collective-permute-done.11.refs_2_ = bf16[96,1536]{1,0:T(8,128)(2,1)} collective-permute-done((bf16[96,1536]{1,0:T(8,128)(2,1)S(1)}, bf16[96,1536]{1,0:T(8,128)(2,1)}, u32[]{:S(2)}, u32[]{:S(2)}) %collective-permute-start.11) | collective-permute-done | bytes 294944 | tf_op jit(solution)/shard_map/ppermute | solution.py:235
  153.1 3.9 collective-permute-done.12.refs_3_
  157.0 8.8 %shard_map.222 = (bf16[384,1536]{1,0:T(8,128)(2,1)}, f32[384,2048]{1,0:T(8,128)}, bf16[384,1024]{1,0:T(8,128)(2,1)}, bf16[96,1536]{1,0:T(8,128)(2,1)}, bf16[96,1...) custom-call(bf16[96,1536]{1,0:T(8,128)(2,1)} %get-tuple-element.345.refs_0_, ...), custom_call_target="tpu_custom_call" | custom-call | tf_op jit(solution)/shard_map/pallas_call | solution.py:394
  169.7 19.0 %collective-permute-done.13 = bf16[96,1536]{1,0:T(8,128)(2,1)S(1)} collective-permute-done((bf16[96,1536]{1,0:T(8,128)(2,1)}, bf16[96,1536]{1,0:T(8,128)(2,1)S(1)}, u32[]{:S(2)}, u32[]{:S(2)}) %collective-permute-start.13) | collective-permute-done | bytes 294944 | tf_op jit(solution)/shard_map/ppermute | solution.py:235
  198.5 4.2 collective-permute-start.17
  204.9 3.3 collective-permute-done.16.refs_1_
  208.3 15.8 %collective-permute-done.17.refs_2_ = bf16[96,1536]{1,0:T(8,128)(2,1)S(1)} collective-permute-done((bf16[96,1536]{1,0:T(8,128)(2,1)S(1)}, bf16[96,1536]{1,0:T(8,128)(2,1)S(1)}, u32[]{:S(2)}, u32[]{:S(2)}) %collective-permute-start.17) | collective-permute-done | bytes 294944 | tf_op jit(solution)/shard_map/ppermute | solution.py:235
  227.5 9.9 %shard_map.223 = (bf16[384,1536]{1,0:T(8,128)(2,1)}, bf16[384,2048]{1,0:T(8,128)(2,1)}, bf16[96,1536]{1,0:T(8,128)(2,1)}, bf16[96,1536]{1,0:T(8,128)(2,1)}, bf16...) custom-call(bf16[96,1536]{1,0:T(8,128)(2,1)} %get-tuple-element.172.refs_0_, bf16[96,1536]{1,0:T(8,128)(2,1)} %copy-done.63, ...), custom_call_target="tpu_custom_call" | custom-call | tf_op jit(solution)/shard_map/pallas_call | solution.py:443
  238.4 2.9 collective-permute-start.21
  242.9 2.9 shard_map.224
  245.9 4.8 shard_map.226
  255.8 4.4 collective-permute-done.19
  271.3 8.4 %all-to-all-start.1 = ((bf16[128,4,384]{2,0,1:T(8,128)(2,1)}), bf16[128,4,384]{2,0,1:T(8,128)(2,1)}, u32[]{:S(2)}, u32[]{:S(2)}) async-start(bf16[128,4,384]{2,0,1:T(8,128)(2,1)} %bitcast.148), calls=%async_computation.1 | async-start | bytes 786432 | tf_op jit(solution)/shard_map/all_to_all | solution.py:870
  293.9 14.0 %shard_map.228 = (f32[512,192]{1,0:T(8,128)S(1)}, bf16[4,512,128]{2,1,0:T(8,128)(2,1)S(1)}, bf16[4,512,128]{2,1,0:T(8,128)(2,1)S(1)}) custom-call(bf16[8,528,256]{2,1,0:T(8,128)(2,1)S(1)} %copy-done.8, bf16[512,384]{1,0:T(8,128)(2,1)S(1)} %slice_multiply_fusion.refs_8_.refs_1_, f32[8,1,1024]{2,1,0:T(1,128)S(1)} %pad_maximum_fusion.3.refs_9_.refs_2_, ...), custom_call_target="tpu_custom_call" | custom-call | flops 999999995904 | tf_op jit(solution)/shard_map/pallas_call | solution.py:210
  308.0 6.3 %collective-permute-done.29 = bf16[192,2048]{1,0:T(8,128)(2,1)} collective-permute-done((bf16[192,2048]{1,0:T(8,128)(2,1)}, bf16[192,2048]{1,0:T(8,128)(2,1)}, u32[]{:S(2)}, u32[]{:S(2)}) %collective-permute-start.29) | collective-permute-done | bytes 786464 | tf_op jit(solution)/shard_map/ppermute | solution.py:261
  316.4 3.4 collective-permute-start.31
  319.8 3.6 collective-permute-start.32
  323.4 13.9 %shard_map.230 = (f32[512,192]{1,0:T(8,128)S(1)}, bf16[4,512,128]{2,1,0:T(8,128)(2,1)S(1)}, bf16[4,512,128]{2,1,0:T(8,128)(2,1)S(1)}) custom-call(bf16[8,528,256]{2,1,0:T(8,128)(2,1)S(1)} %copy-done.8, bf16[512,384]{1,0:T(8,128)(2,1)S(1)} %slice_multiply_fusion.refs_8_.refs_1_, f32[8,1,1024]{2,1,0:T(1,128)S(1)} %pad_maximum_fusion.3.refs_9_.refs_2_, ...), custom_call_target="tpu_custom_call" | custom-call | tf_op jit(solution)/shard_map/pallas_call | solution.py:210
  339.7 3.1 collective-permute-done.31.refs_1_
  344.5 3.2 collective-permute-start.38
  347.7 3.5 collective-permute-start.39
  359.4 4.1 shard_map.232
  363.7 5.2 %collective-permute-done.36.refs_4_ = bf16[512,256]{1,0:T(8,128)(2,1)} collective-permute-done((bf16[512,256]{1,0:T(8,128)(2,1)}, bf16[512,256]{1,0:T(8,128)(2,1)}, u32[]{:S(2)}, u32[]{:S(2)}) %collective-permute-start.36) | collective-permute-done | bytes 262176 | tf_op jit(solution)/shard_map/ppermute | solution.py:261
  371.5 3.7 shard_map.234
  375.3 2.8 collective-permute-done.40.there_ref
  386.5 3.4 collective-permute-start.48
  392.1 4.3 all-to-all-start.3
  400.6 6.0 %collective-permute-done.47.refs_3_ = bf16[192,2048]{1,0:T(8,128)(2,1)S(1)} collective-permute-done((bf16[192,2048]{1,0:T(8,128)(2,1)}, bf16[192,2048]{1,0:T(8,128)(2,1)S(1)}, u32[]{:S(2)}, u32[]{:S(2)}) %collective-permute-start.47) | collective-permute-done | bytes 786464 | tf_op jit(solution)/shard_map/ppermute | solution.py:249
  406.6 5.4 %collective-permute-done.48.refs_6_ = bf16[192,2048]{1,0:T(8,128)(2,1)S(1)} collective-permute-done((bf16[192,2048]{1,0:T(8,128)(2,1)}, bf16[192,2048]{1,0:T(8,128)(2,1)S(1)}, u32[]{:S(2)}, u32[]{:S(2)}) %collective-permute-start.48) | collective-permute-done | bytes 786464 | tf_op jit(solution)/shard_map/ppermute | solution.py:250
  416.7 3.3 collective-permute-start.45
  420.0 12.4 %all-to-all-done.3 = bf16[4,128,640]{1,2,0:T(8,128)(2,1)} async-done(((bf16[4,128,640]{1,2,0:T(8,128)(2,1)}), bf16[4,128,640]{1,2,0:T(8,128)(2,1)}, u32[]{:S(2)}, u32[]{:S(2)}) %all-to-all-start.3) | async-done | bytes 655392 | tf_op jit(solution)/shard_map/all_to_all | solution.py:905
  432.4 5.1 %collective-permute-start.46 = (bf16[192,768]{1,0:T(8,128)(2,1)S(1)}, bf16[192,768]{1,0:T(8,128)(2,1)}, u32[]{:S(2)}, u32[]{:S(2)}) collective-permute-start(bf16[192,768]{1,0:T(8,128)(2,1)S(1)} %select_convert_fusion.refs_0_), channel_id=1, source_target_pairs={{0,24},{8,0},{16,8},{24,16},{1,25},{9,1},{17,9},{25,17},{2,26},{10... | collective-permute-start | bytes 884744 | tf_op jit(solution)/shard_map/ppermute | solution.py:235
  440.0 3.5 all-to-all-start.2
  443.5 6.3 %fusion.27 = (f32[128]{0:T(128)S(1)}, f32[128]{0:T(128)S(1)}, f32[128,1536]{1,0:T(8,128)S(1)}) fusion(bf16[128,1536]{1,0:T(8,128)(2,1)S(1)} %copy-done.47, bf16[128,2560]{0,1:T(8,128)(2,1)} %bitcast.55, bf16[1536,2560]{1,0:T(8,128)(2,1)} %all-gather.13.cloned.1.call-done), kind=kOutput, calls=%fused_computation.47 | convolution fusion | flops 1007615744 | bytes 9700352 | tf_op jit(solution)/shard_map/dot_general | solution.py:28
  449.9 7.8 %shard_map.236 = (f32[4,192,2048]{2,1,0:T(8,128)}, f32[192,128]{1,0:T(8,128)S(1)}) custom-call(s32[1]{0:T(128)} %bitcast.33.place_ref, bf16[192,2048]{1,0:T(8,128)(2,1)S(1)} %copy-done.4, bf16[192,2048]{1,0:T(8,128)(2,1)} %collective-permute-done.31.refs_1_, bf16[192,2048]{1,0:T(8,128)(2,1)} %collective-permute-done.38.refs_2_, ...), custom_call_target="tpu_custom_call" | custom-call | tf_op jit(solution)/shard_map/pallas_call | solution.py:581
  463.3 3.6 convert_bitcast_fusion
  473.3 3.3 shard_map.237
  (422 shorter events, 138.1 us)
Async XLA Ops:
  7.2 48.2 %all-gather.7.cloned.1.call-start = ((), (), s32[]{:S(2)}) async-start(), calls=%async_computation.4 | async-start | bytes 2211840 | tf_op jit(solution)/shard_map/all_gather | solution.py:718
  10.7 109.1 %all-gather.9.cloned.1.call-start = ((), (), s32[]{:S(2)}) async-start(), calls=%async_computation.5 | async-start | bytes 5308416 | tf_op jit(solution)/shard_map/all_gather | solution.py:745
  11.5 145.5 %all-gather.11.cloned.1.call-start = ((), (), s32[]{:S(2)}) async-start(), calls=%async_computation.6 | async-start | bytes 11059200 | tf_op jit(solution)/shard_map/all_gather | solution.py:760
  15.6 189.4 %all-gather.13.cloned.1.call-start = ((), (), s32[]{:S(2)}) async-start(), calls=%async_computation.7 | async-start | bytes 8847360 | tf_op jit(solution)/shard_map/all_gather | solution.py:773
  15.6 29.6 %collective-permute-start = (bf16[136,1536]{1,0:T(8,128)(2,1)S(1)}, bf16[136,1536]{1,0:T(8,128)(2,1)S(1)}, u32[]{:S(2)}, u32[]{:S(2)}) collective-permute-start(bf16[136,1536]{1,0:T(8,128)(2,1)S(1)} %fusion.36), channel_id=1, source_target_pairs={{0,8},{8,16},{16,24},{24,0},{1,9},{9,17},{17,25},{25,1},{2,10},{10... | collective-permute-start | bytes 1253384 | tf_op jit(solution)/shard_map/ppermute | solution.py:235
  17.2 35.8 %collective-permute-start.1 = (bf16[136,1536]{1,0:T(8,128)(2,1)S(1)}, bf16[136,1536]{1,0:T(8,128)(2,1)S(1)}, u32[]{:S(2)}, u32[]{:S(2)}) collective-permute-start(bf16[136,1536]{1,0:T(8,128)(2,1)S(1)} %fusion.36), channel_id=1, source_target_pairs={{0,16},{8,24},{16,0},{24,8},{1,17},{9,25},{17,1},{25,9},{2,18},{10... | collective-permute-start | bytes 1253384 | tf_op jit(solution)/shard_map/ppermute | solution.py:235
  18.5 36.3 %collective-permute-start.2 = (bf16[136,1536]{1,0:T(8,128)(2,1)S(1)}, bf16[136,1536]{1,0:T(8,128)(2,1)S(1)}, u32[]{:S(2)}, u32[]{:S(2)}) collective-permute-start(bf16[136,1536]{1,0:T(8,128)(2,1)S(1)} %fusion.36), channel_id=1, source_target_pairs={{0,24},{8,0},{16,8},{24,16},{1,25},{9,1},{17,9},{25,17},{2,26},{10... | collective-permute-start | bytes 1253384 | tf_op jit(solution)/shard_map/ppermute | solution.py:235
  61.2 18.2 %collective-permute-start.4 = (bf16[528,256]{1,0:T(8,128)(2,1)S(1)}, bf16[528,256]{1,0:T(8,128)(2,1)S(1)}, u32[]{:S(2)}, u32[]{:S(2)}) collective-permute-start(bf16[528,256]{1,0:T(8,128)(2,1)S(1)} %maximum_maximum_fusion.1.refs_0_), channel_id=1, source_target_pairs={{0,4},{1,5},{2,6},{3,7},{4,0},{5,1},{6,2},{7,3},{8,12},{9,13},{10,... | collective-permute-start | bytes 811016 | tf_op jit(solution)/shard_map/ppermute | solution.py:261
  61.7 20.7 %collective-permute-start.5 = (bf16[528,256]{1,0:T(8,128)(2,1)S(1)}, bf16[528,256]{1,0:T(8,128)(2,1)S(1)}, u32[]{:S(2)}, u32[]{:S(2)}) collective-permute-start(bf16[528,256]{1,0:T(8,128)(2,1)S(1)} %maximum_maximum_fusion.1.refs_0_), channel_id=1, source_target_pairs={{0,6},{1,7},{2,4},{3,5},{4,2},{5,3},{6,0},{7,1},{8,14},{9,15},{10,... | collective-permute-start | bytes 811016 | tf_op jit(solution)/shard_map/ppermute | solution.py:261
  63.3 20.9 %collective-permute-start.6 = (bf16[528,256]{1,0:T(8,128)(2,1)S(1)}, bf16[528,256]{1,0:T(8,128)(2,1)S(1)}, u32[]{:S(2)}, u32[]{:S(2)}) collective-permute-start(bf16[528,256]{1,0:T(8,128)(2,1)S(1)} %maximum_maximum_fusion.1.refs_0_), channel_id=1, source_target_pairs={{0,1},{1,0},{2,3},{3,2},{4,5},{5,4},{6,7},{7,6},{8,9},{9,8},{10,11... | collective-permute-start | bytes 811016 | tf_op jit(solution)/shard_map/ppermute | solution.py:261
  127.8 25.3 %collective-permute-start.11 = (bf16[96,1536]{1,0:T(8,128)(2,1)S(1)}, bf16[96,1536]{1,0:T(8,128)(2,1)}, u32[]{:S(2)}, u32[]{:S(2)}) collective-permute-start(bf16[96,1536]{1,0:T(8,128)(2,1)S(1)} %get-tuple-element.343), channel_id=1, source_target_pairs={{0,16},{8,24},{16,0},{24,8},{1,17},{9,25},{17,1},{25,9},{2,18},{10... | collective-permute-start | bytes 884744 | tf_op jit(solution)/shard_map/ppermute | solution.py:235
  131.3 25.7 %collective-permute-start.12 = (bf16[96,1536]{1,0:T(8,128)(2,1)S(1)}, bf16[96,1536]{1,0:T(8,128)(2,1)}, u32[]{:S(2)}, u32[]{:S(2)}) collective-permute-start(bf16[96,1536]{1,0:T(8,128)(2,1)S(1)} %get-tuple-element.342), channel_id=1, source_target_pairs={{0,24},{8,0},{16,8},{24,16},{1,25},{9,1},{17,9},{25,17},{2,26},{10... | collective-permute-start | bytes 884744 | tf_op jit(solution)/shard_map/ppermute | solution.py:235
  165.8 22.8 %collective-permute-start.13 = (bf16[96,1536]{1,0:T(8,128)(2,1)}, bf16[96,1536]{1,0:T(8,128)(2,1)S(1)}, u32[]{:S(2)}, u32[]{:S(2)}) collective-permute-start(bf16[96,1536]{1,0:T(8,128)(2,1)} %get-tuple-element.155), channel_id=1, source_target_pairs={{0,24},{8,0},{16,8},{24,16},{1,25},{9,1},{17,9},{25,17},{2,26},{10... | collective-permute-start | bytes 884744 | tf_op jit(solution)/shard_map/ppermute | solution.py:235
  165.9 22.7 %collective-permute-start.14 = (bf16[96,1536]{1,0:T(8,128)(2,1)}, bf16[96,1536]{1,0:T(8,128)(2,1)S(1)}, u32[]{:S(2)}, u32[]{:S(2)}) collective-permute-start(bf16[96,1536]{1,0:T(8,128)(2,1)} %get-tuple-element.156), channel_id=1, source_target_pairs={{0,16},{8,24},{16,0},{24,8},{1,17},{9,25},{17,1},{25,9},{2,18},{10... | collective-permute-start | bytes 884744 | tf_op jit(solution)/shard_map/ppermute | solution.py:235
  166.7 24.5 %collective-permute-start.15 = (bf16[96,1536]{1,0:T(8,128)(2,1)}, bf16[96,1536]{1,0:T(8,128)(2,1)S(1)}, u32[]{:S(2)}, u32[]{:S(2)}) collective-permute-start(bf16[96,1536]{1,0:T(8,128)(2,1)} %get-tuple-element.157), channel_id=1, source_target_pairs={{0,8},{8,16},{16,24},{24,0},{1,9},{9,17},{17,25},{25,1},{2,10},{10... | collective-permute-start | bytes 884744 | tf_op jit(solution)/shard_map/ppermute | solution.py:235
  198.5 25.5 %collective-permute-start.17 = (bf16[96,1536]{1,0:T(8,128)(2,1)S(1)}, bf16[96,1536]{1,0:T(8,128)(2,1)S(1)}, u32[]{:S(2)}, u32[]{:S(2)}) collective-permute-start(bf16[96,1536]{1,0:T(8,128)(2,1)S(1)} %get-tuple-element.339), channel_id=1, source_target_pairs={{0,16},{8,24},{16,0},{24,8},{1,17},{9,25},{17,1},{25,9},{2,18},{10... | collective-permute-start | bytes 884744 | tf_op jit(solution)/shard_map/ppermute | solution.py:235
  202.7 24.0 %collective-permute-start.18 = (bf16[96,1536]{1,0:T(8,128)(2,1)S(1)}, bf16[96,1536]{1,0:T(8,128)(2,1)S(1)}, u32[]{:S(2)}, u32[]{:S(2)}) collective-permute-start(bf16[96,1536]{1,0:T(8,128)(2,1)S(1)} %get-tuple-element.338), channel_id=1, source_target_pairs={{0,24},{8,0},{16,8},{24,16},{1,25},{9,1},{17,9},{25,17},{2,26},{10... | collective-permute-start | bytes 884744 | tf_op jit(solution)/shard_map/ppermute | solution.py:235
  237.4 22.9 %collective-permute-start.19 = (bf16[96,1536]{1,0:T(8,128)(2,1)}, bf16[96,1536]{1,0:T(8,128)(2,1)S(1)}, u32[]{:S(2)}, u32[]{:S(2)}) collective-permute-start(bf16[96,1536]{1,0:T(8,128)(2,1)} %get-tuple-element.178), channel_id=1, source_target_pairs={{0,24},{8,0},{16,8},{24,16},{1,25},{9,1},{17,9},{25,17},{2,26},{10... | collective-permute-start | bytes 884744 | tf_op jit(solution)/shard_map/ppermute | solution.py:235
  237.4 22.8 %collective-permute-start.20 = (bf16[96,1536]{1,0:T(8,128)(2,1)}, bf16[96,1536]{1,0:T(8,128)(2,1)S(1)}, u32[]{:S(2)}, u32[]{:S(2)}) collective-permute-start(bf16[96,1536]{1,0:T(8,128)(2,1)} %get-tuple-element.179), channel_id=1, source_target_pairs={{0,16},{8,24},{16,0},{24,8},{1,17},{9,25},{17,1},{25,9},{2,18},{10... | collective-permute-start | bytes 884744 | tf_op jit(solution)/shard_map/ppermute | solution.py:235
  238.4 24.9 %collective-permute-start.21 = (bf16[96,1536]{1,0:T(8,128)(2,1)}, bf16[96,1536]{1,0:T(8,128)(2,1)S(1)}, u32[]{:S(2)}, u32[]{:S(2)}) collective-permute-start(bf16[96,1536]{1,0:T(8,128)(2,1)} %get-tuple-element.180), channel_id=1, source_target_pairs={{0,8},{8,16},{16,24},{24,0},{1,9},{9,17},{17,25},{25,1},{2,10},{10... | collective-permute-start | bytes 884744 | tf_op jit(solution)/shard_map/ppermute | solution.py:235
  250.7 16.4 %collective-permute-start.23 = (bf16[4,192,2048]{2,1,0:T(8,128)(2,1)S(1)}, bf16[4,192,2048]{2,1,0:T(8,128)(2,1)S(1)}, u32[]{:S(2)}, u32[]{:S(2)}) collective-permute-start(bf16[4,192,2048]{2,1,0:T(8,128)(2,1)S(1)} %get-tuple-element.204), channel_id=1, source_target_pairs={{0,1},{1,0},{2,3},{3,2},{4,5},{5,4},{6,7},{7,6},{8,9},{9,8},{10,11... | collective-permute-start | bytes 9437192 | tf_op jit(solution)/shard_map/ppermute | solution.py:261
  254.8 26.8 %collective-permute-start.24 = (bf16[192,1024]{1,0:T(8,128)(2,1)}, bf16[192,1024]{1,0:T(8,128)(2,1)}, u32[]{:S(2)}, u32[]{:S(2)}) collective-permute-start(bf16[192,1024]{1,0:T(8,128)(2,1)} %get-tuple-element.192), channel_id=1, source_target_pairs={{0,2},{1,3},{2,0},{3,1},{4,6},{5,7},{6,4},{7,5},{8,10},{9,11},{10,... | collective-permute-start | bytes 1179656 | tf_op jit(solution)/shard_map/ppermute | solution.py:261
  260.2 23.0 %collective-permute-start.25 = (bf16[192,1024]{1,0:T(8,128)(2,1)}, bf16[192,1024]{1,0:T(8,128)(2,1)}, u32[]{:S(2)}, u32[]{:S(2)}) collective-permute-start(bf16[192,1024]{1,0:T(8,128)(2,1)} %get-tuple-element.193), channel_id=1, source_target_pairs={{0,4},{1,5},{2,6},{3,7},{4,0},{5,1},{6,2},{7,3},{8,12},{9,13},{10,... | collective-permute-start | bytes 1179656 | tf_op jit(solution)/shard_map/ppermute | solution.py:261
  260.2 23.0 %collective-permute-start.26 = (bf16[192,1024]{1,0:T(8,128)(2,1)}, bf16[192,1024]{1,0:T(8,128)(2,1)}, u32[]{:S(2)}, u32[]{:S(2)}) collective-permute-start(bf16[192,1024]{1,0:T(8,128)(2,1)} %get-tuple-element.194), channel_id=1, source_target_pairs={{0,6},{1,7},{2,4},{3,5},{4,2},{5,3},{6,0},{7,1},{8,14},{9,15},{10,... | collective-permute-start | bytes 1179656 | tf_op jit(solution)/shard_map/ppermute | solution.py:261
  271.3 19.8 %all-to-all-start.1 = ((bf16[128,4,384]{2,0,1:T(8,128)(2,1)}), bf16[128,4,384]{2,0,1:T(8,128)(2,1)}, u32[]{:S(2)}, u32[]{:S(2)}) async-start(bf16[128,4,384]{2,0,1:T(8,128)(2,1)} %bitcast.148), calls=%async_computation.1 | async-start | bytes 786432 | tf_op jit(solution)/shard_map/all_to_all | solution.py:870
  279.7 64.2 %all-gather.15.cloned.1.call-start = ((), (), s32[]{:S(2)}) async-start(), calls=%async_computation.8 | async-start | bytes 1966080 | tf_op jit(solution)/shard_map/all_gather | solution.py:873
  279.7 28.2 %collective-permute-start.27 = (bf16[192,2048]{1,0:T(8,128)(2,1)}, bf16[192,2048]{1,0:T(8,128)(2,1)}, u32[]{:S(2)}, u32[]{:S(2)}) collective-permute-start(bf16[192,2048]{1,0:T(8,128)(2,1)} %copy-done.35), channel_id=1, source_target_pairs={{0,2},{1,3},{2,0},{3,1},{4,6},{5,7},{6,4},{7,5},{8,10},{9,11},{10,... | collective-permute-start | bytes 2359304 | tf_op jit(solution)/shard_map/ppermute | solution.py:261
  279.7 28.2 %collective-permute-start.28 = (bf16[192,2048]{1,0:T(8,128)(2,1)}, bf16[192,2048]{1,0:T(8,128)(2,1)}, u32[]{:S(2)}, u32[]{:S(2)}) collective-permute-start(bf16[192,2048]{1,0:T(8,128)(2,1)} %copy-done.34), channel_id=1, source_target_pairs={{0,4},{1,5},{2,6},{3,7},{4,0},{5,1},{6,2},{7,3},{8,12},{9,13},{10,... | collective-permute-start | bytes 2359304 | tf_op jit(solution)/shard_map/ppermute | solution.py:261
  281.6 32.7 %collective-permute-start.29 = (bf16[192,2048]{1,0:T(8,128)(2,1)}, bf16[192,2048]{1,0:T(8,128)(2,1)}, u32[]{:S(2)}, u32[]{:S(2)}) collective-permute-start(bf16[192,2048]{1,0:T(8,128)(2,1)} %copy-done.33), channel_id=1, source_target_pairs={{0,6},{1,7},{2,4},{3,5},{4,2},{5,3},{6,0},{7,1},{8,14},{9,15},{10,... | collective-permute-start | bytes 2359304 | tf_op jit(solution)/shard_map/ppermute | solution.py:261
  291.1 32.3 %collective-permute-start.30 = (bf16[4,192,1536]{2,1,0:T(8,128)(2,1)}, bf16[4,192,1536]{2,1,0:T(8,128)(2,1)}, u32[]{:S(2)}, u32[]{:S(2)}) collective-permute-start(bf16[4,192,1536]{2,1,0:T(8,128)(2,1)} %copy-done.32), channel_id=1, source_target_pairs={{0,1},{1,0},{2,3},{3,2},{4,5},{5,4},{6,7},{7,6},{8,9},{9,8},{10,11... | collective-permute-start | bytes 7077896 | tf_op jit(solution)/shard_map/ppermute | solution.py:261
  316.4 26.4 %collective-permute-start.31 = (bf16[192,2048]{1,0:T(8,128)(2,1)S(1)}, bf16[192,2048]{1,0:T(8,128)(2,1)}, u32[]{:S(2)}, u32[]{:S(2)}) collective-permute-start(bf16[192,2048]{1,0:T(8,128)(2,1)S(1)} %add_convert_fusion.refs_0_), channel_id=1, source_target_pairs={{0,8},{8,16},{16,24},{1,9},{9,17},{17,25},{2,10},{10,18},{18,26},{... | collective-permute-start | bytes 2359304 | tf_op jit(solution)/shard_map/ppermute | solution.py:249
  319.8 24.2 %collective-permute-start.32 = (bf16[192,2048]{1,0:T(8,128)(2,1)S(1)}, bf16[192,2048]{1,0:T(8,128)(2,1)}, u32[]{:S(2)}, u32[]{:S(2)}) collective-permute-start(bf16[192,2048]{1,0:T(8,128)(2,1)S(1)} %add_convert_fusion.refs_0_), channel_id=1, source_target_pairs={{8,0},{16,8},{24,16},{9,1},{17,9},{25,17},{10,2},{18,10},{26,18},{... | collective-permute-start | bytes 2359304 | tf_op jit(solution)/shard_map/ppermute | solution.py:250
  344.5 24.4 %collective-permute-start.38 = (bf16[192,2048]{1,0:T(8,128)(2,1)}, bf16[192,2048]{1,0:T(8,128)(2,1)}, u32[]{:S(2)}, u32[]{:S(2)}) collective-permute-start(bf16[192,2048]{1,0:T(8,128)(2,1)} %collective-permute-done.31.refs_1_), channel_id=1, source_target_pairs={{0,8},{8,16},{16,24},{1,9},{9,17},{17,25},{2,10},{10,18},{18,26},{... | collective-permute-start | bytes 2359304 | tf_op jit(solution)/shard_map/ppermute | solution.py:249
  347.7 21.4 %collective-permute-start.39 = (bf16[192,2048]{1,0:T(8,128)(2,1)}, bf16[192,2048]{1,0:T(8,128)(2,1)}, u32[]{:S(2)}, u32[]{:S(2)}) collective-permute-start(bf16[192,2048]{1,0:T(8,128)(2,1)} %collective-permute-done.32.refs_4_), channel_id=1, source_target_pairs={{8,0},{16,8},{24,16},{9,1},{17,9},{25,17},{10,2},{18,10},{26,18},{... | collective-permute-start | bytes 2359304 | tf_op jit(solution)/shard_map/ppermute | solution.py:250
  355.6 13.3 %collective-permute-start.36 = (bf16[512,256]{1,0:T(8,128)(2,1)}, bf16[512,256]{1,0:T(8,128)(2,1)}, u32[]{:S(2)}, u32[]{:S(2)}) collective-permute-start(bf16[512,256]{1,0:T(8,128)(2,1)} %get-tuple-element.236), channel_id=1, source_target_pairs={{0,4},{1,5},{2,6},{3,7},{4,0},{5,1},{6,2},{7,3},{8,12},{9,13},{10,... | collective-permute-start | bytes 786440 | tf_op jit(solution)/shard_map/ppermute | solution.py:261
  380.6 15.9 %collective-permute-start.43 = (bf16[192,768]{1,0:T(8,128)(2,1)}, bf16[192,768]{1,0:T(8,128)(2,1)}, u32[]{:S(2)}, u32[]{:S(2)}) collective-permute-start(bf16[192,768]{1,0:T(8,128)(2,1)} %get-tuple-element.254), channel_id=1, source_target_pairs={{0,6},{1,7},{2,4},{3,5},{4,2},{5,3},{6,0},{7,1},{8,14},{9,15},{10,... | collective-permute-start | bytes 884744 | tf_op jit(solution)/shard_map/ppermute | solution.py:261
  381.9 15.2 %collective-permute-start.42 = (bf16[192,768]{1,0:T(8,128)(2,1)S(1)}, bf16[192,768]{1,0:T(8,128)(2,1)}, u32[]{:S(2)}, u32[]{:S(2)}) collective-permute-start(bf16[192,768]{1,0:T(8,128)(2,1)S(1)} %get-tuple-element.253), channel_id=1, source_target_pairs={{0,4},{1,5},{2,6},{3,7},{4,0},{5,1},{6,2},{7,3},{8,12},{9,13},{10,... | collective-permute-start | bytes 884744 | tf_op jit(solution)/shard_map/ppermute | solution.py:261
  383.4 13.7 %collective-permute-start.41 = (bf16[192,768]{1,0:T(8,128)(2,1)S(1)}, bf16[192,768]{1,0:T(8,128)(2,1)}, u32[]{:S(2)}, u32[]{:S(2)}) collective-permute-start(bf16[192,768]{1,0:T(8,128)(2,1)S(1)} %get-tuple-element.252), channel_id=1, source_target_pairs={{0,2},{1,3},{2,0},{3,1},{4,6},{5,7},{6,4},{7,5},{8,10},{9,11},{10,... | collective-permute-start | bytes 884744 | tf_op jit(solution)/shard_map/ppermute | solution.py:261
  384.0 22.6 %collective-permute-start.47 = (bf16[192,2048]{1,0:T(8,128)(2,1)}, bf16[192,2048]{1,0:T(8,128)(2,1)S(1)}, u32[]{:S(2)}, u32[]{:S(2)}) collective-permute-start(bf16[192,2048]{1,0:T(8,128)(2,1)} %collective-permute-done.38.refs_2_), channel_id=1, source_target_pairs={{0,8},{8,16},{16,24},{1,9},{9,17},{17,25},{2,10},{10,18},{18,26},{... | collective-permute-start | bytes 2359304 | tf_op jit(solution)/shard_map/ppermute | solution.py:249
  386.5 25.5 %collective-permute-start.48 = (bf16[192,2048]{1,0:T(8,128)(2,1)}, bf16[192,2048]{1,0:T(8,128)(2,1)S(1)}, u32[]{:S(2)}, u32[]{:S(2)}) collective-permute-start(bf16[192,2048]{1,0:T(8,128)(2,1)} %collective-permute-done.39.refs_5_), channel_id=1, source_target_pairs={{8,0},{16,8},{24,16},{9,1},{17,9},{25,17},{10,2},{18,10},{26,18},{... | collective-permute-start | bytes 2359304 | tf_op jit(solution)/shard_map/ppermute | solution.py:250
  392.1 40.3 %all-to-all-start.3 = ((bf16[4,128,640]{1,2,0:T(8,128)(2,1)}), bf16[4,128,640]{1,2,0:T(8,128)(2,1)}, u32[]{:S(2)}, u32[]{:S(2)}) async-start(bf16[4,128,640]{1,2,0:T(8,128)(2,1)} %copy.104), calls=%async_computation.3 | async-start | bytes 1310720 | tf_op jit(solution)/shard_map/all_to_all | solution.py:905
  412.0 20.3 %collective-permute-start.51 = (bf16[192,1536]{1,0:T(8,128)(2,1)}, bf16[192,1536]{1,0:T(8,128)(2,1)}, u32[]{:S(2)}, u32[]{:S(2)}) collective-permute-start(bf16[192,1536]{1,0:T(8,128)(2,1)} %get-tuple-element.260), channel_id=1, source_target_pairs={{0,6},{1,7},{2,4},{3,5},{4,2},{5,3},{6,0},{7,1},{8,14},{9,15},{10,... | collective-permute-start | bytes 1769480 | tf_op jit(solution)/shard_map/ppermute | solution.py:261
  413.8 23.7 %collective-permute-start.50 = (bf16[192,1536]{1,0:T(8,128)(2,1)}, bf16[192,1536]{1,0:T(8,128)(2,1)}, u32[]{:S(2)}, u32[]{:S(2)}) collective-permute-start(bf16[192,1536]{1,0:T(8,128)(2,1)} %get-tuple-element.259), channel_id=1, source_target_pairs={{0,4},{1,5},{2,6},{3,7},{4,0},{5,1},{6,2},{7,3},{8,12},{9,13},{10,... | collective-permute-start | bytes 1769480 | tf_op jit(solution)/shard_map/ppermute | solution.py:261
  416.2 21.2 %collective-permute-start.49 = (bf16[192,1536]{1,0:T(8,128)(2,1)}, bf16[192,1536]{1,0:T(8,128)(2,1)}, u32[]{:S(2)}, u32[]{:S(2)}) collective-permute-start(bf16[192,1536]{1,0:T(8,128)(2,1)} %get-tuple-element.258), channel_id=1, source_target_pairs={{0,2},{1,3},{2,0},{3,1},{4,6},{5,7},{6,4},{7,5},{8,10},{9,11},{10,... | collective-permute-start | bytes 1769480 | tf_op jit(solution)/shard_map/ppermute | solution.py:261
  416.6 46.4 %collective-permute-start.44 = (bf16[192,768]{1,0:T(8,128)(2,1)S(1)}, bf16[192,768]{1,0:T(8,128)(2,1)}, u32[]{:S(2)}, u32[]{:S(2)}) collective-permute-start(bf16[192,768]{1,0:T(8,128)(2,1)S(1)} %select_convert_fusion.refs_0_), channel_id=1, source_target_pairs={{0,8},{8,16},{16,24},{24,0},{1,9},{9,17},{17,25},{25,1},{2,10},{10... | collective-permute-start | bytes 884744 | tf_op jit(solution)/shard_map/ppermute | solution.py:235
  416.7 50.3 %collective-permute-start.45 = (bf16[192,768]{1,0:T(8,128)(2,1)S(1)}, bf16[192,768]{1,0:T(8,128)(2,1)}, u32[]{:S(2)}, u32[]{:S(2)}) collective-permute-start(bf16[192,768]{1,0:T(8,128)(2,1)S(1)} %select_convert_fusion.refs_0_), channel_id=1, source_target_pairs={{0,16},{8,24},{16,0},{24,8},{1,17},{9,25},{17,1},{25,9},{2,18},{10... | collective-permute-start | bytes 884744 | tf_op jit(solution)/shard_map/ppermute | solution.py:235
  432.4 34.6 %collective-permute-start.46 = (bf16[192,768]{1,0:T(8,128)(2,1)S(1)}, bf16[192,768]{1,0:T(8,128)(2,1)}, u32[]{:S(2)}, u32[]{:S(2)}) collective-permute-start(bf16[192,768]{1,0:T(8,128)(2,1)S(1)} %select_convert_fusion.refs_0_), channel_id=1, source_target_pairs={{0,24},{8,0},{16,8},{24,16},{1,25},{9,1},{17,9},{25,17},{2,26},{10... | collective-permute-start | bytes 884744 | tf_op jit(solution)/shard_map/ppermute | solution.py:235
  440.0 18.7 %all-to-all-start.2 = ((bf16[192,4,384]{2,0,1:T(8,128)(2,1)}), bf16[192,4,384]{2,0,1:T(8,128)(2,1)S(1)}, u32[]{:S(2)}, u32[]{:S(2)}) async-start(bf16[192,4,384]{2,0,1:T(8,128)(2,1)} %bitcast.147), calls=%async_computation.2 | async-start | bytes 1179648 | tf_op jit(solution)/shard_map/all_to_all | solution.py:928
  (99 other events, 759.2 us)
Sparse Core Ops, SparseCore 0:
  10.8 28.3 all-gather.6
  41.2 48.3 all-gather.8
  92.1 58.2 all-gather.10
  152.6 52.2 all-gather.12
  291.2 42.1 all-gather.14

commit v21 on v19

--- a/solution.py
+++ b/solution.py
@@ -893,7 +893,7 @@
         held = after(head_grad, grad_gate_up_shard, out_there)
     steps[1] = after(steps[1], part_q)
     steps.append(relay_step(steps[1], seqs))
-    far = after(far, steps[1], grad_down)
+    far = after(far, grad_down)
     pairs = kv_pair_sums(near, [hop(each, shards, 1) for each in far])
     out_sums = pair_sums(out_near, after(out_there, pairs), shard)
     sent_grads, product_columns = head_columns(

time: 494 us -> 492 us (level)
    unnamed x198 -> x194, local copies, waits for them, and re-layouts: 22.8 us -> 22.8 us
  transfers between devices with their start and end apart: 64 -> 64, of which waited for: 32 -> 31; matrix products, arithmetic and copies ran while one was open for 12% -> 12% of each run, Pallas kernels for 17% -> 17%
where the time goes in v21:
time: 492 us; the launch traced here: 484 us
  waiting for transfers between devices  179 us (36%)
  Pallas kernels  102 us (21%)
  starting transfers between devices  96.1 us (20%)
  local copies, waits for them, and re-layouts  33.9 us (7%)
  other arithmetic  29.3 us (6%)
  matrix products  22.1 us (4%)
  between operations  21 us (4%)
    ppermute x21, waiting for transfers between devices, shift(): lax.ppermute(block, 'seq', [(i, (i + step) % count) for i in range(count)])  112 us
    ppermute x28, waiting for transfers between devices, hop(): return lax.ppermute(block, 'fsdp', [(i, i ^ mask) for i in range(count)])  33.7 us
    ppermute x21, starting transfers between devices, shift(): lax.ppermute(block, 'seq', [(i, (i + step) % count) for i in range(count)])  33.3 us
    pallas_call x2, Pallas kernels, flash_backward(): pl.pallas_call(functools.partial(backward_kernel, shards, seqs, rows, g,...  27.9 us
    unnamed x194, local copies, waits for them, and re-layouts  22.8 us
    ppermute x28, starting transfers between devices, hop(): return lax.ppermute(block, 'fsdp', [(i, i ^ mask) for i in range(count)])  22.4 us
    pallas_call x1, Pallas kernels, flash_forward(): pl.pallas_call(functools.partial(forward_kernel, shards, seqs, rows, loca...  19 us
    pallas_call x4, Pallas kernels, split_product(): pl.pallas_call(product_kernel, grid=(count // 2,), in_specs=[pl.BlockSpec...  14 us
  transfers between devices with their start and end apart: 64, of which 31 were waited for; matrix products, arithmetic and copies ran while one was open for 12% of the time, Pallas kernels for 17%

profile of v21, /device:TPU:12, one launch (start us, length us, event | category | flops | bytes accessed | tf_op | source)
XLA Modules:
  0.0 483.5 jit_solution(4151264066609646110)
XLA Ops:
  21.9 23.3 %collective-permute-done = bf16[136,1536]{1,0:T(8,128)(2,1)S(1)} collective-permute-done((bf16[136,1536]{1,0:T(8,128)(2,1)S(1)}, bf16[136,1536]{1,0:T(8,128)(2,1)S(1)}, u32[]{:S(2)}, u32[]{:S(2)}) %collective-permute-start) | collective-permute-done | bytes 417824 | tf_op jit(solution)/shard_map/ppermute | solution.py:235
  45.2 7.8 %collective-permute-done.1 = bf16[136,1536]{1,0:T(8,128)(2,1)S(1)} collective-permute-done((bf16[136,1536]{1,0:T(8,128)(2,1)S(1)}, bf16[136,1536]{1,0:T(8,128)(2,1)S(1)}, u32[]{:S(2)}, u32[]{:S(2)}) %collective-permute-start.1) | collective-permute-done | bytes 417824 | tf_op jit(solution)/shard_map/ppermute | solution.py:235
  63.3 8.3 %collective-permute-done.3.refs_1_ = bf16[528,256]{1,0:T(8,128)(2,1)S(1)} collective-permute-done((bf16[528,256]{1,0:T(8,128)(2,1)S(1)}, bf16[528,256]{1,0:T(8,128)(2,1)S(1)}, u32[]{:S(2)}, u32[]{:S(2)}) %collective-permute-start.3) | collective-permute-done | bytes 270368 | tf_op jit(solution)/shard_map/ppermute | solution.py:261
  71.6 7.7 %collective-permute-done.4.refs_2_ = bf16[528,256]{1,0:T(8,128)(2,1)S(1)} collective-permute-done((bf16[528,256]{1,0:T(8,128)(2,1)S(1)}, bf16[528,256]{1,0:T(8,128)(2,1)S(1)}, u32[]{:S(2)}, u32[]{:S(2)}) %collective-permute-start.4) | collective-permute-done | bytes 270368 | tf_op jit(solution)/shard_map/ppermute | solution.py:261
  79.4 3.0 collective-permute-done.5.refs_3_
  85.0 19.0 %shard_map.221 = (bf16[512,384]{1,0:T(8,128)(2,1)}, f32[512,384]{1,0:T(8,128)S(1)}) custom-call(bf16[528,256]{1,0:T(8,128)(2,1)S(1)} %maximum_maximum_fusion.1.refs_0_, bf16[528,256]{1,0:T(8,128)(2,1)S(1)} %collective-permute-done.3.refs_1_, bf16[528,256]{1,0:T(8,128)(2,1)S(1)} %collective-permute-done.4.refs_2_, ...), custom_call_target="tpu_custom_call" | custom-call | tf_op jit(solution)/shard_map/pallas_call | solution.py:112
  104.9 3.4 all-to-all-start
  109.2 8.8 %all-to-all-done = bf16[4,128,384]{2,1,0:T(8,128)(2,1)S(1)} async-done(((bf16[4,128,384]{2,1,0:T(8,128)(2,1)}), bf16[4,128,384]{2,1,0:T(8,128)(2,1)S(1)}, u32[]{:S(2)}, u32[]{:S(2)}) %all-to-all-start) | async-done | bytes 393248 | tf_op jit(solution)/shard_map/all_to_all | solution.py:794
  119.8 5.7 %multiply_reduce_fusion.5 = (f32[128]{0:T(128)S(1)}, f32[128,1536]{1,0:T(8,128)S(1)}) fusion(bf16[128,1536]{1,0:T(8,128)(2,1)S(1)} %bitcast.138, bf16[1536,1536]{0,1:T(8,128)(2,1)} %all-gather.9.cloned.1.call-done, bf16[128,1536]{1,0:T(8,128)(2,1)} %param.14), kind=kOutput, calls=%fused_computation.69 | convolution fusion | flops 604766080 | bytes 6291968 | tf_op jit(solution)/shard_map/dot_general | solution.py:24
  127.8 3.5 collective-permute-start.11
  134.1 3.7 collective-permute-done.10.refs_1_
  137.8 15.3 %collective-permute-done.11.refs_2_ = bf16[96,1536]{1,0:T(8,128)(2,1)} collective-permute-done((bf16[96,1536]{1,0:T(8,128)(2,1)S(1)}, bf16[96,1536]{1,0:T(8,128)(2,1)}, u32[]{:S(2)}, u32[]{:S(2)}) %collective-permute-start.11) | collective-permute-done | bytes 294944 | tf_op jit(solution)/shard_map/ppermute | solution.py:235
  153.1 3.9 collective-permute-done.12.refs_3_
  157.0 8.8 %shard_map.222 = (bf16[384,1536]{1,0:T(8,128)(2,1)}, f32[384,2048]{1,0:T(8,128)}, bf16[384,1024]{1,0:T(8,128)(2,1)}, bf16[96,1536]{1,0:T(8,128)(2,1)}, bf16[96,1...) custom-call(bf16[96,1536]{1,0:T(8,128)(2,1)} %get-tuple-element.353.refs_0_, ...), custom_call_target="tpu_custom_call" | custom-call | tf_op jit(solution)/shard_map/pallas_call | solution.py:394
  169.7 18.9 %collective-permute-done.13 = bf16[96,1536]{1,0:T(8,128)(2,1)S(1)} collective-permute-done((bf16[96,1536]{1,0:T(8,128)(2,1)}, bf16[96,1536]{1,0:T(8,128)(2,1)S(1)}, u32[]{:S(2)}, u32[]{:S(2)}) %collective-permute-start.13) | collective-permute-done | bytes 294944 | tf_op jit(solution)/shard_map/ppermute | solution.py:235
  198.5 4.2 collective-permute-start.17
  204.9 3.3 collective-permute-done.16.refs_1_
  208.3 15.8 %collective-permute-done.17.refs_2_ = bf16[96,1536]{1,0:T(8,128)(2,1)S(1)} collective-permute-done((bf16[96,1536]{1,0:T(8,128)(2,1)S(1)}, bf16[96,1536]{1,0:T(8,128)(2,1)S(1)}, u32[]{:S(2)}, u32[]{:S(2)}) %collective-permute-start.17) | collective-permute-done | bytes 294944 | tf_op jit(solution)/shard_map/ppermute | solution.py:235
  227.4 9.9 %shard_map.223 = (bf16[384,1536]{1,0:T(8,128)(2,1)}, bf16[384,2048]{1,0:T(8,128)(2,1)}, bf16[96,1536]{1,0:T(8,128)(2,1)}, bf16[96,1536]{1,0:T(8,128)(2,1)}, bf16...) custom-call(bf16[96,1536]{1,0:T(8,128)(2,1)} %get-tuple-element.176.refs_0_, bf16[96,1536]{1,0:T(8,128)(2,1)} %copy-done.61, ...), custom_call_target="tpu_custom_call" | custom-call | tf_op jit(solution)/shard_map/pallas_call | solution.py:443
  238.4 2.9 collective-permute-start.21
  242.9 2.9 shard_map.224
  245.9 4.9 %shard_map.226 = (bf16[4,192,2048]{2,1,0:T(8,128)(2,1)S(1)}, bf16[4,192,2048]{2,1,0:T(8,128)(2,1)S(1)}) custom-call(s32[1]{0:T(128)} %bitcast.35.core_ref, bf16[384,1536]{1,0:T(8,128)(2,1)S(1)} %copy-done.14, bf16[384,2048]{1,0:T(8,128)(2,1)S(1)} %copy-done.11), custom_call_target="tpu_custom_call" | custom-call | tf_op jit(solution)/shard_map/pallas_call | solution.py:311
  255.8 4.4 collective-permute-done.19
  271.3 8.4 %all-to-all-start.1 = ((bf16[128,4,384]{2,0,1:T(8,128)(2,1)}), bf16[128,4,384]{2,0,1:T(8,128)(2,1)}, u32[]{:S(2)}, u32[]{:S(2)}) async-start(bf16[128,4,384]{2,0,1:T(8,128)(2,1)} %bitcast.148), calls=%async_computation.1 | async-start | bytes 786432 | tf_op jit(solution)/shard_map/all_to_all | solution.py:870
  293.9 13.9 %shard_map.228 = (f32[512,192]{1,0:T(8,128)S(1)}, bf16[4,512,128]{2,1,0:T(8,128)(2,1)S(1)}, bf16[4,512,128]{2,1,0:T(8,128)(2,1)S(1)}) custom-call(bf16[8,528,256]{2,1,0:T(8,128)(2,1)S(1)} %copy-done.6, bf16[512,384]{1,0:T(8,128)(2,1)S(1)} %slice_multiply_fusion.refs_8_.refs_1_, f32[8,1,1024]{2,1,0:T(1,128)S(1)} %pad_maximum_fusion.3.refs_9_.refs_2_, ...), custom_call_target="tpu_custom_call" | custom-call | flops 999999995904 | tf_op jit(solution)/shard_map/pallas_call | solution.py:210
  307.9 6.3 %collective-permute-done.29 = bf16[192,2048]{1,0:T(8,128)(2,1)} collective-permute-done((bf16[192,2048]{1,0:T(8,128)(2,1)}, bf16[192,2048]{1,0:T(8,128)(2,1)}, u32[]{:S(2)}, u32[]{:S(2)}) %collective-permute-start.29) | collective-permute-done | bytes 786464 | tf_op jit(solution)/shard_map/ppermute | solution.py:261
  314.2 3.0 add_convert_fusion.refs_0_
  317.2 3.4 collective-permute-start.36
  320.6 3.6 collective-permute-start.37
  324.2 13.9 %shard_map.230 = (f32[512,192]{1,0:T(8,128)S(1)}, bf16[4,512,128]{2,1,0:T(8,128)(2,1)S(1)}, bf16[4,512,128]{2,1,0:T(8,128)(2,1)S(1)}) custom-call(bf16[8,528,256]{2,1,0:T(8,128)(2,1)S(1)} %copy-done.6, bf16[512,384]{1,0:T(8,128)(2,1)S(1)} %slice_multiply_fusion.refs_8_.refs_1_, f32[8,1,1024]{2,1,0:T(1,128)S(1)} %pad_maximum_fusion.3.refs_9_.refs_2_, ...), custom_call_target="tpu_custom_call" | custom-call | tf_op jit(solution)/shard_map/pallas_call | solution.py:210
  344.0 3.2 collective-permute-start.38
  347.2 3.5 collective-permute-start.39
  358.9 4.1 shard_map.232
  363.2 4.4 collective-permute-done.34.refs_4_
  369.9 3.7 shard_map.234
  376.5 3.1 collective-permute-start.45
  387.8 4.3 all-to-all-start.3
  392.1 4.1 collective-permute-done.44.refs_3_
  396.1 5.9 %collective-permute-done.45.refs_6_ = bf16[192,2048]{1,0:T(8,128)(2,1)S(1)} collective-permute-done((bf16[192,2048]{1,0:T(8,128)(2,1)}, bf16[192,2048]{1,0:T(8,128)(2,1)S(1)}, u32[]{:S(2)}, u32[]{:S(2)}) %collective-permute-start.45) | collective-permute-done | bytes 786464 | tf_op jit(solution)/shard_map/ppermute | solution.py:250
  411.8 10.5 %all-to-all-done.3 = bf16[4,128,640]{1,2,0:T(8,128)(2,1)} async-done(((bf16[4,128,640]{1,2,0:T(8,128)(2,1)}), bf16[4,128,640]{1,2,0:T(8,128)(2,1)}, u32[]{:S(2)}, u32[]{:S(2)}) %all-to-all-start.3) | async-done | bytes 655392 | tf_op jit(solution)/shard_map/all_to_all | solution.py:905
  423.0 4.2 collective-permute-start.48
  427.2 3.1 collective-permute-done.50
  433.0 4.5 all-to-all-start.2
  437.5 6.3 %fusion.27 = (f32[128]{0:T(128)S(1)}, f32[128]{0:T(128)S(1)}, f32[128,1536]{1,0:T(8,128)S(1)}) fusion(bf16[128,1536]{1,0:T(8,128)(2,1)S(1)} %copy-done.45, bf16[128,2560]{0,1:T(8,128)(2,1)} %bitcast.55, bf16[1536,2560]{1,0:T(8,128)(2,1)} %all-gather.13.cloned.1.call-done), kind=kOutput, calls=%fused_computation.47 | convolution fusion | flops 1007615744 | bytes 9700352 | tf_op jit(solution)/shard_map/dot_general | solution.py:28
  443.8 8.0 %shard_map.236 = (f32[4,192,2048]{2,1,0:T(8,128)}, f32[192,128]{1,0:T(8,128)S(1)}) custom-call(s32[1]{0:T(128)} %bitcast.33.place_ref, bf16[192,2048]{1,0:T(8,128)(2,1)} %add_convert_fusion.refs_0_, bf16[192,2048]{1,0:T(8,128)(2,1)} %collective-permute-done.36.refs_1_, bf16[192,2048]{1,0:T(8,128)(2,1)} %collective-permute-done.38.refs_2_, ...), custom_call_target="tpu_custom_call" | custom-call | tf_op jit(solution)/shard_map/pallas_call | solution.py:581
  457.5 3.6 convert_bitcast_fusion
  461.2 4.0 collective-permute-done.52.refs_5_
  468.8 3.3 shard_map.237
  (418 shorter events, 136.9 us)
Async XLA Ops:
  7.2 48.2 %all-gather.7.cloned.1.call-start = ((), (), s32[]{:S(2)}) async-start(), calls=%async_computation.4 | async-start | bytes 2211840 | tf_op jit(solution)/shard_map/all_gather | solution.py:718
  10.7 109.1 %all-gather.9.cloned.1.call-start = ((), (), s32[]{:S(2)}) async-start(), calls=%async_computation.5 | async-start | bytes 5308416 | tf_op jit(solution)/shard_map/all_gather | solution.py:745
  11.5 145.5 %all-gather.11.cloned.1.call-start = ((), (), s32[]{:S(2)}) async-start(), calls=%async_computation.6 | async-start | bytes 11059200 | tf_op jit(solution)/shard_map/all_gather | solution.py:760
  15.6 189.4 %all-gather.13.cloned.1.call-start = ((), (), s32[]{:S(2)}) async-start(), calls=%async_computation.7 | async-start | bytes 8847360 | tf_op jit(solution)/shard_map/all_gather | solution.py:773
  15.6 29.6 %collective-permute-start = (bf16[136,1536]{1,0:T(8,128)(2,1)S(1)}, bf16[136,1536]{1,0:T(8,128)(2,1)S(1)}, u32[]{:S(2)}, u32[]{:S(2)}) collective-permute-start(bf16[136,1536]{1,0:T(8,128)(2,1)S(1)} %fusion.36), channel_id=1, source_target_pairs={{0,8},{8,16},{16,24},{24,0},{1,9},{9,17},{17,25},{25,1},{2,10},{10... | collective-permute-start | bytes 1253384 | tf_op jit(solution)/shard_map/ppermute | solution.py:235
  17.2 35.8 %collective-permute-start.1 = (bf16[136,1536]{1,0:T(8,128)(2,1)S(1)}, bf16[136,1536]{1,0:T(8,128)(2,1)S(1)}, u32[]{:S(2)}, u32[]{:S(2)}) collective-permute-start(bf16[136,1536]{1,0:T(8,128)(2,1)S(1)} %fusion.36), channel_id=1, source_target_pairs={{0,16},{8,24},{16,0},{24,8},{1,17},{9,25},{17,1},{25,9},{2,18},{10... | collective-permute-start | bytes 1253384 | tf_op jit(solution)/shard_map/ppermute | solution.py:235
  18.5 36.3 %collective-permute-start.2 = (bf16[136,1536]{1,0:T(8,128)(2,1)S(1)}, bf16[136,1536]{1,0:T(8,128)(2,1)S(1)}, u32[]{:S(2)}, u32[]{:S(2)}) collective-permute-start(bf16[136,1536]{1,0:T(8,128)(2,1)S(1)} %fusion.36), channel_id=1, source_target_pairs={{0,24},{8,0},{16,8},{24,16},{1,25},{9,1},{17,9},{25,17},{2,26},{10... | collective-permute-start | bytes 1253384 | tf_op jit(solution)/shard_map/ppermute | solution.py:235
  61.2 18.2 %collective-permute-start.4 = (bf16[528,256]{1,0:T(8,128)(2,1)S(1)}, bf16[528,256]{1,0:T(8,128)(2,1)S(1)}, u32[]{:S(2)}, u32[]{:S(2)}) collective-permute-start(bf16[528,256]{1,0:T(8,128)(2,1)S(1)} %maximum_maximum_fusion.1.refs_0_), channel_id=1, source_target_pairs={{0,4},{1,5},{2,6},{3,7},{4,0},{5,1},{6,2},{7,3},{8,12},{9,13},{10,... | collective-permute-start | bytes 811016 | tf_op jit(solution)/shard_map/ppermute | solution.py:261
  61.7 20.7 %collective-permute-start.5 = (bf16[528,256]{1,0:T(8,128)(2,1)S(1)}, bf16[528,256]{1,0:T(8,128)(2,1)S(1)}, u32[]{:S(2)}, u32[]{:S(2)}) collective-permute-start(bf16[528,256]{1,0:T(8,128)(2,1)S(1)} %maximum_maximum_fusion.1.refs_0_), channel_id=1, source_target_pairs={{0,6},{1,7},{2,4},{3,5},{4,2},{5,3},{6,0},{7,1},{8,14},{9,15},{10,... | collective-permute-start | bytes 811016 | tf_op jit(solution)/shard_map/ppermute | solution.py:261
  63.3 20.9 %collective-permute-start.6 = (bf16[528,256]{1,0:T(8,128)(2,1)S(1)}, bf16[528,256]{1,0:T(8,128)(2,1)S(1)}, u32[]{:S(2)}, u32[]{:S(2)}) collective-permute-start(bf16[528,256]{1,0:T(8,128)(2,1)S(1)} %maximum_maximum_fusion.1.refs_0_), channel_id=1, source_target_pairs={{0,1},{1,0},{2,3},{3,2},{4,5},{5,4},{6,7},{7,6},{8,9},{9,8},{10,11... | collective-permute-start | bytes 811016 | tf_op jit(solution)/shard_map/ppermute | solution.py:261
  104.9 13.1 %all-to-all-start = ((bf16[4,128,384]{2,1,0:T(8,128)(2,1)}), bf16[4,128,384]{2,1,0:T(8,128)(2,1)S(1)}, u32[]{:S(2)}, u32[]{:S(2)}) async-start(bf16[4,128,384]{2,1,0:T(8,128)(2,1)} %bitcast.12), calls=%async_computation | async-start | bytes 786432 | tf_op jit(solution)/shard_map/all_to_all | solution.py:794
  127.8 25.3 %collective-permute-start.11 = (bf16[96,1536]{1,0:T(8,128)(2,1)S(1)}, bf16[96,1536]{1,0:T(8,128)(2,1)}, u32[]{:S(2)}, u32[]{:S(2)}) collective-permute-start(bf16[96,1536]{1,0:T(8,128)(2,1)S(1)} %get-tuple-element.351), channel_id=1, source_target_pairs={{0,16},{8,24},{16,0},{24,8},{1,17},{9,25},{17,1},{25,9},{2,18},{10... | collective-permute-start | bytes 884744 | tf_op jit(solution)/shard_map/ppermute | solution.py:235
  131.3 25.7 %collective-permute-start.12 = (bf16[96,1536]{1,0:T(8,128)(2,1)S(1)}, bf16[96,1536]{1,0:T(8,128)(2,1)}, u32[]{:S(2)}, u32[]{:S(2)}) collective-permute-start(bf16[96,1536]{1,0:T(8,128)(2,1)S(1)} %get-tuple-element.350), channel_id=1, source_target_pairs={{0,24},{8,0},{16,8},{24,16},{1,25},{9,1},{17,9},{25,17},{2,26},{10... | collective-permute-start | bytes 884744 | tf_op jit(solution)/shard_map/ppermute | solution.py:235
  165.8 22.8 %collective-permute-start.13 = (bf16[96,1536]{1,0:T(8,128)(2,1)}, bf16[96,1536]{1,0:T(8,128)(2,1)S(1)}, u32[]{:S(2)}, u32[]{:S(2)}) collective-permute-start(bf16[96,1536]{1,0:T(8,128)(2,1)} %get-tuple-element.159), channel_id=1, source_target_pairs={{0,24},{8,0},{16,8},{24,16},{1,25},{9,1},{17,9},{25,17},{2,26},{10... | collective-permute-start | bytes 884744 | tf_op jit(solution)/shard_map/ppermute | solution.py:235
  165.9 22.7 %collective-permute-start.14 = (bf16[96,1536]{1,0:T(8,128)(2,1)}, bf16[96,1536]{1,0:T(8,128)(2,1)S(1)}, u32[]{:S(2)}, u32[]{:S(2)}) collective-permute-start(bf16[96,1536]{1,0:T(8,128)(2,1)} %get-tuple-element.160), channel_id=1, source_target_pairs={{0,16},{8,24},{16,0},{24,8},{1,17},{9,25},{17,1},{25,9},{2,18},{10... | collective-permute-start | bytes 884744 | tf_op jit(solution)/shard_map/ppermute | solution.py:235
  166.7 24.5 %collective-permute-start.15 = (bf16[96,1536]{1,0:T(8,128)(2,1)}, bf16[96,1536]{1,0:T(8,128)(2,1)S(1)}, u32[]{:S(2)}, u32[]{:S(2)}) collective-permute-start(bf16[96,1536]{1,0:T(8,128)(2,1)} %get-tuple-element.161), channel_id=1, source_target_pairs={{0,8},{8,16},{16,24},{24,0},{1,9},{9,17},{17,25},{25,1},{2,10},{10... | collective-permute-start | bytes 884744 | tf_op jit(solution)/shard_map/ppermute | solution.py:235
  198.5 25.5 %collective-permute-start.17 = (bf16[96,1536]{1,0:T(8,128)(2,1)S(1)}, bf16[96,1536]{1,0:T(8,128)(2,1)S(1)}, u32[]{:S(2)}, u32[]{:S(2)}) collective-permute-start(bf16[96,1536]{1,0:T(8,128)(2,1)S(1)} %get-tuple-element.347), channel_id=1, source_target_pairs={{0,16},{8,24},{16,0},{24,8},{1,17},{9,25},{17,1},{25,9},{2,18},{10... | collective-permute-start | bytes 884744 | tf_op jit(solution)/shard_map/ppermute | solution.py:235
  202.7 24.0 %collective-permute-start.18 = (bf16[96,1536]{1,0:T(8,128)(2,1)S(1)}, bf16[96,1536]{1,0:T(8,128)(2,1)S(1)}, u32[]{:S(2)}, u32[]{:S(2)}) collective-permute-start(bf16[96,1536]{1,0:T(8,128)(2,1)S(1)} %get-tuple-element.346), channel_id=1, source_target_pairs={{0,24},{8,0},{16,8},{24,16},{1,25},{9,1},{17,9},{25,17},{2,26},{10... | collective-permute-start | bytes 884744 | tf_op jit(solution)/shard_map/ppermute | solution.py:235
  237.4 22.8 %collective-permute-start.19 = (bf16[96,1536]{1,0:T(8,128)(2,1)}, bf16[96,1536]{1,0:T(8,128)(2,1)S(1)}, u32[]{:S(2)}, u32[]{:S(2)}) collective-permute-start(bf16[96,1536]{1,0:T(8,128)(2,1)} %get-tuple-element.182), channel_id=1, source_target_pairs={{0,24},{8,0},{16,8},{24,16},{1,25},{9,1},{17,9},{25,17},{2,26},{10... | collective-permute-start | bytes 884744 | tf_op jit(solution)/shard_map/ppermute | solution.py:235
  237.4 22.8 %collective-permute-start.20 = (bf16[96,1536]{1,0:T(8,128)(2,1)}, bf16[96,1536]{1,0:T(8,128)(2,1)S(1)}, u32[]{:S(2)}, u32[]{:S(2)}) collective-permute-start(bf16[96,1536]{1,0:T(8,128)(2,1)} %get-tuple-element.183), channel_id=1, source_target_pairs={{0,16},{8,24},{16,0},{24,8},{1,17},{9,25},{17,1},{25,9},{2,18},{10... | collective-permute-start | bytes 884744 | tf_op jit(solution)/shard_map/ppermute | solution.py:235
  238.4 24.9 %collective-permute-start.21 = (bf16[96,1536]{1,0:T(8,128)(2,1)}, bf16[96,1536]{1,0:T(8,128)(2,1)S(1)}, u32[]{:S(2)}, u32[]{:S(2)}) collective-permute-start(bf16[96,1536]{1,0:T(8,128)(2,1)} %get-tuple-element.184), channel_id=1, source_target_pairs={{0,8},{8,16},{16,24},{24,0},{1,9},{9,17},{17,25},{25,1},{2,10},{10... | collective-permute-start | bytes 884744 | tf_op jit(solution)/shard_map/ppermute | solution.py:235
  250.8 16.3 %collective-permute-start.23 = (bf16[4,192,2048]{2,1,0:T(8,128)(2,1)S(1)}, bf16[4,192,2048]{2,1,0:T(8,128)(2,1)S(1)}, u32[]{:S(2)}, u32[]{:S(2)}) collective-permute-start(bf16[4,192,2048]{2,1,0:T(8,128)(2,1)S(1)} %get-tuple-element.208), channel_id=1, source_target_pairs={{0,1},{1,0},{2,3},{3,2},{4,5},{5,4},{6,7},{7,6},{8,9},{9,8},{10,11... | collective-permute-start | bytes 9437192 | tf_op jit(solution)/shard_map/ppermute | solution.py:261
  254.8 26.8 %collective-permute-start.24 = (bf16[192,1024]{1,0:T(8,128)(2,1)}, bf16[192,1024]{1,0:T(8,128)(2,1)}, u32[]{:S(2)}, u32[]{:S(2)}) collective-permute-start(bf16[192,1024]{1,0:T(8,128)(2,1)} %get-tuple-element.196), channel_id=1, source_target_pairs={{0,2},{1,3},{2,0},{3,1},{4,6},{5,7},{6,4},{7,5},{8,10},{9,11},{10,... | collective-permute-start | bytes 1179656 | tf_op jit(solution)/shard_map/ppermute | solution.py:261
  260.2 23.0 %collective-permute-start.25 = (bf16[192,1024]{1,0:T(8,128)(2,1)}, bf16[192,1024]{1,0:T(8,128)(2,1)}, u32[]{:S(2)}, u32[]{:S(2)}) collective-permute-start(bf16[192,1024]{1,0:T(8,128)(2,1)} %get-tuple-element.197), channel_id=1, source_target_pairs={{0,4},{1,5},{2,6},{3,7},{4,0},{5,1},{6,2},{7,3},{8,12},{9,13},{10,... | collective-permute-start | bytes 1179656 | tf_op jit(solution)/shard_map/ppermute | solution.py:261
  260.2 23.0 %collective-permute-start.26 = (bf16[192,1024]{1,0:T(8,128)(2,1)}, bf16[192,1024]{1,0:T(8,128)(2,1)}, u32[]{:S(2)}, u32[]{:S(2)}) collective-permute-start(bf16[192,1024]{1,0:T(8,128)(2,1)} %get-tuple-element.198), channel_id=1, source_target_pairs={{0,6},{1,7},{2,4},{3,5},{4,2},{5,3},{6,0},{7,1},{8,14},{9,15},{10,... | collective-permute-start | bytes 1179656 | tf_op jit(solution)/shard_map/ppermute | solution.py:261
  271.3 19.8 %all-to-all-start.1 = ((bf16[128,4,384]{2,0,1:T(8,128)(2,1)}), bf16[128,4,384]{2,0,1:T(8,128)(2,1)}, u32[]{:S(2)}, u32[]{:S(2)}) async-start(bf16[128,4,384]{2,0,1:T(8,128)(2,1)} %bitcast.148), calls=%async_computation.1 | async-start | bytes 786432 | tf_op jit(solution)/shard_map/all_to_all | solution.py:870
  279.7 60.8 %all-gather.15.cloned.1.call-start = ((), (), s32[]{:S(2)}) async-start(), calls=%async_computation.8 | async-start | bytes 1966080 | tf_op jit(solution)/shard_map/all_gather | solution.py:873
  279.7 28.2 %collective-permute-start.27 = (bf16[192,2048]{1,0:T(8,128)(2,1)}, bf16[192,2048]{1,0:T(8,128)(2,1)}, u32[]{:S(2)}, u32[]{:S(2)}) collective-permute-start(bf16[192,2048]{1,0:T(8,128)(2,1)} %copy-done.33), channel_id=1, source_target_pairs={{0,2},{1,3},{2,0},{3,1},{4,6},{5,7},{6,4},{7,5},{8,10},{9,11},{10,... | collective-permute-start | bytes 2359304 | tf_op jit(solution)/shard_map/ppermute | solution.py:261
  279.7 28.2 %collective-permute-start.28 = (bf16[192,2048]{1,0:T(8,128)(2,1)}, bf16[192,2048]{1,0:T(8,128)(2,1)}, u32[]{:S(2)}, u32[]{:S(2)}) collective-permute-start(bf16[192,2048]{1,0:T(8,128)(2,1)} %copy-done.32), channel_id=1, source_target_pairs={{0,4},{1,5},{2,6},{3,7},{4,0},{5,1},{6,2},{7,3},{8,12},{9,13},{10,... | collective-permute-start | bytes 2359304 | tf_op jit(solution)/shard_map/ppermute | solution.py:261
  281.6 32.6 %collective-permute-start.29 = (bf16[192,2048]{1,0:T(8,128)(2,1)}, bf16[192,2048]{1,0:T(8,128)(2,1)}, u32[]{:S(2)}, u32[]{:S(2)}) collective-permute-start(bf16[192,2048]{1,0:T(8,128)(2,1)} %copy-done.31), channel_id=1, source_target_pairs={{0,6},{1,7},{2,4},{3,5},{4,2},{5,3},{6,0},{7,1},{8,14},{9,15},{10,... | collective-permute-start | bytes 2359304 | tf_op jit(solution)/shard_map/ppermute | solution.py:261
  291.1 33.1 %collective-permute-start.30 = (bf16[4,192,1536]{2,1,0:T(8,128)(2,1)}, bf16[4,192,1536]{2,1,0:T(8,128)(2,1)}, u32[]{:S(2)}, u32[]{:S(2)}) collective-permute-start(bf16[4,192,1536]{2,1,0:T(8,128)(2,1)} %copy-done.30), channel_id=1, source_target_pairs={{0,1},{1,0},{2,3},{3,2},{4,5},{5,4},{6,7},{7,6},{8,9},{9,8},{10,11... | collective-permute-start | bytes 7077896 | tf_op jit(solution)/shard_map/ppermute | solution.py:261
  317.2 25.6 %collective-permute-start.36 = (bf16[192,2048]{1,0:T(8,128)(2,1)}, bf16[192,2048]{1,0:T(8,128)(2,1)}, u32[]{:S(2)}, u32[]{:S(2)}) collective-permute-start(bf16[192,2048]{1,0:T(8,128)(2,1)} %add_convert_fusion.refs_0_), channel_id=1, source_target_pairs={{0,8},{8,16},{16,24},{1,9},{9,17},{17,25},{2,10},{10,18},{18,26},{... | collective-permute-start | bytes 2359304 | tf_op jit(solution)/shard_map/ppermute | solution.py:249
  320.6 23.4 %collective-permute-start.37 = (bf16[192,2048]{1,0:T(8,128)(2,1)}, bf16[192,2048]{1,0:T(8,128)(2,1)}, u32[]{:S(2)}, u32[]{:S(2)}) collective-permute-start(bf16[192,2048]{1,0:T(8,128)(2,1)} %add_convert_fusion.refs_0_), channel_id=1, source_target_pairs={{8,0},{16,8},{24,16},{9,1},{17,9},{25,17},{10,2},{18,10},{26,18},{... | collective-permute-start | bytes 2359304 | tf_op jit(solution)/shard_map/ppermute | solution.py:250
  344.0 23.6 %collective-permute-start.38 = (bf16[192,2048]{1,0:T(8,128)(2,1)}, bf16[192,2048]{1,0:T(8,128)(2,1)}, u32[]{:S(2)}, u32[]{:S(2)}) collective-permute-start(bf16[192,2048]{1,0:T(8,128)(2,1)} %collective-permute-done.36.refs_1_), channel_id=1, source_target_pairs={{0,8},{8,16},{16,24},{1,9},{9,17},{17,25},{2,10},{10,18},{18,26},{... | collective-permute-start | bytes 2359304 | tf_op jit(solution)/shard_map/ppermute | solution.py:249
  347.2 20.3 %collective-permute-start.39 = (bf16[192,2048]{1,0:T(8,128)(2,1)}, bf16[192,2048]{1,0:T(8,128)(2,1)}, u32[]{:S(2)}, u32[]{:S(2)}) collective-permute-start(bf16[192,2048]{1,0:T(8,128)(2,1)} %collective-permute-done.37.refs_4_), channel_id=1, source_target_pairs={{8,0},{16,8},{24,16},{9,1},{17,9},{25,17},{10,2},{18,10},{26,18},{... | collective-permute-start | bytes 2359304 | tf_op jit(solution)/shard_map/ppermute | solution.py:250
  373.7 22.4 %collective-permute-start.44 = (bf16[192,2048]{1,0:T(8,128)(2,1)}, bf16[192,2048]{1,0:T(8,128)(2,1)S(1)}, u32[]{:S(2)}, u32[]{:S(2)}) collective-permute-start(bf16[192,2048]{1,0:T(8,128)(2,1)} %collective-permute-done.38.refs_2_), channel_id=1, source_target_pairs={{0,8},{8,16},{16,24},{1,9},{9,17},{17,25},{2,10},{10,18},{18,26},{... | collective-permute-start | bytes 2359304 | tf_op jit(solution)/shard_map/ppermute | solution.py:249
  376.5 25.5 %collective-permute-start.45 = (bf16[192,2048]{1,0:T(8,128)(2,1)}, bf16[192,2048]{1,0:T(8,128)(2,1)S(1)}, u32[]{:S(2)}, u32[]{:S(2)}) collective-permute-start(bf16[192,2048]{1,0:T(8,128)(2,1)} %collective-permute-done.39.refs_5_), channel_id=1, source_target_pairs={{8,0},{16,8},{24,16},{9,1},{17,9},{25,17},{10,2},{18,10},{26,18},{... | collective-permute-start | bytes 2359304 | tf_op jit(solution)/shard_map/ppermute | solution.py:250
  382.1 19.9 %collective-permute-start.41 = (bf16[192,768]{1,0:T(8,128)(2,1)}, bf16[192,768]{1,0:T(8,128)(2,1)}, u32[]{:S(2)}, u32[]{:S(2)}) collective-permute-start(bf16[192,768]{1,0:T(8,128)(2,1)} %get-tuple-element.256), channel_id=1, source_target_pairs={{0,2},{1,3},{2,0},{3,1},{4,6},{5,7},{6,4},{7,5},{8,10},{9,11},{10,... | collective-permute-start | bytes 884744 | tf_op jit(solution)/shard_map/ppermute | solution.py:261
  383.0 19.0 %collective-permute-start.42 = (bf16[192,768]{1,0:T(8,128)(2,1)S(1)}, bf16[192,768]{1,0:T(8,128)(2,1)}, u32[]{:S(2)}, u32[]{:S(2)}) collective-permute-start(bf16[192,768]{1,0:T(8,128)(2,1)S(1)} %get-tuple-element.257), channel_id=1, source_target_pairs={{0,4},{1,5},{2,6},{3,7},{4,0},{5,1},{6,2},{7,3},{8,12},{9,13},{10,... | collective-permute-start | bytes 884744 | tf_op jit(solution)/shard_map/ppermute | solution.py:261
  383.8 18.2 %collective-permute-start.43 = (bf16[192,768]{1,0:T(8,128)(2,1)S(1)}, bf16[192,768]{1,0:T(8,128)(2,1)}, u32[]{:S(2)}, u32[]{:S(2)}) collective-permute-start(bf16[192,768]{1,0:T(8,128)(2,1)S(1)} %get-tuple-element.258), channel_id=1, source_target_pairs={{0,6},{1,7},{2,4},{3,5},{4,2},{5,3},{6,0},{7,1},{8,14},{9,15},{10,... | collective-permute-start | bytes 884744 | tf_op jit(solution)/shard_map/ppermute | solution.py:261
  387.8 34.5 %all-to-all-start.3 = ((bf16[4,128,640]{1,2,0:T(8,128)(2,1)}), bf16[4,128,640]{1,2,0:T(8,128)(2,1)}, u32[]{:S(2)}, u32[]{:S(2)}) async-start(bf16[4,128,640]{1,2,0:T(8,128)(2,1)} %copy.104), calls=%async_computation.3 | async-start | bytes 1310720 | tf_op jit(solution)/shard_map/all_to_all | solution.py:905
  405.5 17.5 %collective-permute-start.51 = (bf16[192,1536]{1,0:T(8,128)(2,1)}, bf16[192,1536]{1,0:T(8,128)(2,1)}, u32[]{:S(2)}, u32[]{:S(2)}) collective-permute-start(bf16[192,1536]{1,0:T(8,128)(2,1)} %get-tuple-element.268), channel_id=1, source_target_pairs={{0,6},{1,7},{2,4},{3,5},{4,2},{5,3},{6,0},{7,1},{8,14},{9,15},{10,... | collective-permute-start | bytes 1769480 | tf_op jit(solution)/shard_map/ppermute | solution.py:261
  407.1 23.3 %collective-permute-start.50 = (bf16[192,1536]{1,0:T(8,128)(2,1)}, bf16[192,1536]{1,0:T(8,128)(2,1)}, u32[]{:S(2)}, u32[]{:S(2)}) collective-permute-start(bf16[192,1536]{1,0:T(8,128)(2,1)} %get-tuple-element.267), channel_id=1, source_target_pairs={{0,4},{1,5},{2,6},{3,7},{4,0},{5,1},{6,2},{7,3},{8,12},{9,13},{10,... | collective-permute-start | bytes 1769480 | tf_op jit(solution)/shard_map/ppermute | solution.py:261
  408.9 21.5 %collective-permute-start.49 = (bf16[192,1536]{1,0:T(8,128)(2,1)}, bf16[192,1536]{1,0:T(8,128)(2,1)}, u32[]{:S(2)}, u32[]{:S(2)}) collective-permute-start(bf16[192,1536]{1,0:T(8,128)(2,1)} %get-tuple-element.266), channel_id=1, source_target_pairs={{0,2},{1,3},{2,0},{3,1},{4,6},{5,7},{6,4},{7,5},{8,10},{9,11},{10,... | collective-permute-start | bytes 1769480 | tf_op jit(solution)/shard_map/ppermute | solution.py:261
  409.4 46.9 %collective-permute-start.46 = (bf16[192,768]{1,0:T(8,128)(2,1)S(1)}, bf16[192,768]{1,0:T(8,128)(2,1)}, u32[]{:S(2)}, u32[]{:S(2)}) collective-permute-start(bf16[192,768]{1,0:T(8,128)(2,1)S(1)} %select_convert_fusion.refs_0_), channel_id=1, source_target_pairs={{0,8},{8,16},{16,24},{24,0},{1,9},{9,17},{17,25},{25,1},{2,10},{10... | collective-permute-start | bytes 884744 | tf_op jit(solution)/shard_map/ppermute | solution.py:235
  409.5 51.7 %collective-permute-start.47 = (bf16[192,768]{1,0:T(8,128)(2,1)S(1)}, bf16[192,768]{1,0:T(8,128)(2,1)}, u32[]{:S(2)}, u32[]{:S(2)}) collective-permute-start(bf16[192,768]{1,0:T(8,128)(2,1)S(1)} %select_convert_fusion.refs_0_), channel_id=1, source_target_pairs={{0,16},{8,24},{16,0},{24,8},{1,17},{9,25},{17,1},{25,9},{2,18},{10... | collective-permute-start | bytes 884744 | tf_op jit(solution)/shard_map/ppermute | solution.py:235
  423.0 38.2 %collective-permute-start.48 = (bf16[192,768]{1,0:T(8,128)(2,1)S(1)}, bf16[192,768]{1,0:T(8,128)(2,1)}, u32[]{:S(2)}, u32[]{:S(2)}) collective-permute-start(bf16[192,768]{1,0:T(8,128)(2,1)S(1)} %select_convert_fusion.refs_0_), channel_id=1, source_target_pairs={{0,24},{8,0},{16,8},{24,16},{1,25},{9,1},{17,9},{25,17},{2,26},{10... | collective-permute-start | bytes 884744 | tf_op jit(solution)/shard_map/ppermute | solution.py:235
  433.0 20.0 %all-to-all-start.2 = ((bf16[192,4,384]{2,0,1:T(8,128)(2,1)}), bf16[192,4,384]{2,0,1:T(8,128)(2,1)S(1)}, u32[]{:S(2)}, u32[]{:S(2)}) async-start(bf16[192,4,384]{2,0,1:T(8,128)(2,1)} %bitcast.147), calls=%async_computation.2 | async-start | bytes 1179648 | tf_op jit(solution)/shard_map/all_to_all | solution.py:928
  (97 other events, 738.7 us)
Sparse Core Ops, SparseCore 0:
  10.8 28.3 all-gather.6
  41.2 48.3 all-gather.8
  92.1 58.2 all-gather.10
  152.6 52.2 all-gather.12
  291.2 41.0 all-gather.14
